TPU v7x, 32 devices: a whole 2x2x4 slice. The times are simulated.
32 devices in a mesh: group: 2 (over core), tok: 4 (over y, x), head: 4 (over z).
Axes of the slice: x: 2, y: 2, z: 4, core: 2. Of those that a mesh axis runs over, the one named last changes fastest.
Arguments:
- streams: bfloat16 [2, 4096, 2240], P(None, ('group', 'tok'), 'head'), may hold values from -6 to 6
- w_query: bfloat16 [2240, 2240], P(None, 'head'), may hold values from -0.125 to 0.125
- w_key: bfloat16 [2240, 2240], P(None, 'head'), may hold values from -0.125 to 0.125
- w_value: bfloat16 [2240, 2240], P(None, 'head'), may hold values from -0.125 to 0.125
- gain: float32 [2240], P('head'), may hold values from 0.25 to 1.75
Outputs:
- attended: bfloat16 [2, 4096, 2240], P(None, ('group', 'tok'), 'head')
All inputs are finite; a program needn't handle non-finite values.
Results may differ from a plain program's by a relative error of at most 0.0053.
Values may be sent and summed in bfloat16 or wider, within the bound.
No kernel may reach another device: no remote copies, remote signals or barrier semaphores. Data moves between devices by JAX's collectives and lax.ppermute only.
A program may use at most 64 MiB of HBM per device.

v0:
```python
import jax
import jax.numpy as jnp
from jax import lax
from jax.sharding import PartitionSpec as P

HEAD_DIM = 112


def entering(value, axis, join, neutral):
    count, mine = (lax.axis_size(axis), lax.axis_index(axis))
    pieces = lax.all_gather(value, axis)
    total = jnp.full_like(value, 0) + jnp.asarray(neutral, value.dtype)

    def lap(position, total):
        longer = join(total, pieces[position])
        return jnp.where(position < mine, longer, total)

    return lax.fori_loop(0, count - 1, lap, total)


def add_states(earlier, later):
    return earlier + later


def local(streams, w_query, w_key, w_value, gain):
    width_dev = w_query.shape[1]
    heads_dev = width_dev // HEAD_DIM
    token_count = streams.shape[1]
    blank_sums = jnp.zeros((2, token_count, width_dev), jnp.float32)
    running = (blank_sums, blank_sums, blank_sums)
    pieces = lax.all_gather(streams, "head", axis=2, tiled=True)
    results = []
    for total, matrix in zip(running, (w_query, w_key, w_value)):
        results.append(
            jnp.einsum("std,dw->stw", pieces, matrix, preferred_element_type=jnp.float32)
        )
    query_sum, key_sum, value_sum = tuple(results)
    query = query_sum.astype(jnp.bfloat16)
    key_relu = jnp.maximum(key_sum.astype(jnp.bfloat16), 0).reshape(
        2, token_count, heads_dev, HEAD_DIM
    )
    value_heads = value_sum.astype(jnp.bfloat16).reshape(2, token_count, heads_dev, HEAD_DIM)
    states = jnp.einsum(
        "stha,sthb->sahb", key_relu, value_heads, preferred_element_type=jnp.float32
    )
    states = states.reshape(2, HEAD_DIM, width_dev)
    clean_part = states[0:1]
    noisy_part = states[1:2]
    empty_state = jnp.zeros_like(clean_part)
    clean_total, noisy_total = lax.psum((clean_part, noisy_part), "tok")
    prefix = entering(clean_total, "group", add_states, empty_state)
    totals = jnp.concatenate([prefix + clean_total, prefix + noisy_total], axis=0)
    totals = totals.reshape(2, HEAD_DIM, heads_dev, HEAD_DIM)
    query_relu = (
        jnp.maximum(query, 0).astype(jnp.float32).reshape(2, token_count, heads_dev, HEAD_DIM)
    )
    reading = jnp.einsum("stha,sahb->sthb", query_relu, totals, precision=lax.Precision.HIGHEST)
    scale = lax.rsqrt(jnp.mean(reading * reading, axis=-1, keepdims=True) + 1e-06)
    normed = reading * scale * gain.reshape(heads_dev, HEAD_DIM)
    return normed.reshape(2, token_count, width_dev).astype(jnp.bfloat16)


def solution(mesh):
    return jax.shard_map(
        local,
        mesh=mesh,
        in_specs=(
            P(None, ("group", "tok"), "head"),
            P(None, "head"),
            P(None, "head"),
            P(None, "head"),
            P("head"),
        ),
        out_specs=P(None, ("group", "tok"), "head"),
        check_vma=False,
    )
```

profile of v0, /device:TPU:0, one launch (start us, length us, event | category | flops | bytes accessed | tf_op | source)
XLA Modules:
  0.0 169.4 jit_solution(6220214093094115534)
XLA Ops:
  6.5 0.0 copy-start
  6.5 0.0 all-gather.3.cloned.1.call-start
  6.5 0.7 all-gather.3.cloned.1.call-update
  7.3 0.0 all-reduce.3.cloned.1.call-start
  7.3 0.8 mul.24
  8.1 90.8 %all-gather.3.cloned.1.call-done = bf16[2,512,2240]{1,2,0:T(8,128)(2,1)} async-done(((bf16[2,512,560]{1,2,0:T(8,128)(2,1)}), bf16[2,512,2240]{1,2,0:T(8,128)(2,1)}) %all-gather.3.cloned.1.call-update) | async-done | bytes 4587536 | tf_op jit(solution)/shard_map/all_gather | solution.py:31
  98.9 0.0 copy-done
  98.9 0.0 copy-start.1
  98.9 0.0 copy-start.2
  98.9 5.3 %fusion.9 = bf16[2,512,560]{1,2,0:T(8,128)(2,1)S(1)} fusion(bf16[2,512,2240]{1,2,0:T(8,128)(2,1)} %all-gather.3.cloned.1.call-done, bf16[2240,560]{0,1:T(8,128)(2,1)S(1)} %copy-done), kind=kOutput, calls=%fused_computation.11 | convolution fusion | flops 2569584640 | bytes 8243200 | tf_op jit(solution)/shard_map/std,dw->stw/dot_general | solution.py:35
  104.2 0.0 copy-done.1
  104.2 0.0 copy-done.2
  104.2 2.8 %fusion.21 = bf16[2,512,560]{1,2,0:T(8,128)(2,1)S(1)} fusion(bf16[2,512,2240]{1,2,0:T(8,128)(2,1)S(1)} %copy-done.1, bf16[2240,560]{0,1:T(8,128)(2,1)S(1)} %copy-done.2), kind=kOutput, calls=%fused_computation.15 | convolution fusion | flops 2570158080 | bytes 8243200 | tf_op jit(solution)/shard_map/std,dw->stw/dot_general | solution.py:35
  107.0 0.5 convolution_bitcast_fusion
  107.5 0.9 copy.6
  108.4 0.9 copy.7
  109.3 0.0 all-reduce.3.cloned.1.call-update
  109.3 6.9 %fusion.18 = bf16[2,512,560]{1,2,0:T(8,128)(2,1)} fusion(bf16[2,512,2240]{1,2,0:T(8,128)(2,1)} %all-gather.3.cloned.1.call-done, bf16[2240,560]{0,1:T(8,128)(2,1)} %param.6), kind=kOutput, calls=%fused_computation.14 | convolution fusion | flops 2570158080 | bytes 8243200 | tf_op jit(solution)/shard_map/std,dw->stw/dot_general | solution.py:35
  116.2 37.8 %all-reduce.3.cloned.1.call-done = (f32[1,112,560]{2,1,0:T(8,128)}, f32[1,112,560]{2,1,0:T(8,128)}) async-done(((f32[1,112,560]{2,1,0:T(8,128)}, f32[1,112,560]{2,1,0:T(8,128)}), (f32[1,112,560]{2,1,0:T(8,128)}, f32[1,112,560]{2,1,0:T(8,128)})) %all-reduce.3.cloned.1.call-update) | async-done | bytes 501776 | tf_op jit(solution)/shard_map/psum | solution.py:50
  154.0 2.4 %all-gather = f32[2,112,560]{2,1,0:T(8,128)S(1)} all-gather(f32[1,112,560]{2,1,0:T(8,128)} %get-tuple-element.14), channel_id=2, replica_groups=mesh['group'=2,'tok'=4,'head'=4] {'group'}, dimensions={0}, use_global_device_ids=true | all-gather | bytes 752640 | tf_op jit(solution)/shard_map/all_gather | solution.py:11
  156.5 1.1 fusion.24
  157.6 1.0 copy.8
  158.6 2.6 %fusion.6 = (f32[2,512,5]{1,2,0:T(8,128)S(1)}, f32[2,5,112,512]{3,2,1,0:T(8,128)S(1)}) fusion(f32[2,112,5,112]{1,3,2,0:T(8,128)} %bitcast.44, bf16[2,512,5,112]{1,3,2,0:T(8,128)(2,1)} %bitcast.49), kind=kOutput, calls=%fused_computation.8 | convolution fusion | flops 771845120 | bytes 3962880 | tf_op jit(solution)/shard_map/stha,sahb->sthb/dot_general | solution.py:57
  161.3 1.3 fusion.8
  (3 shorter events, 0.1 us)
Async XLA Ops:
  6.5 92.4 %copy-start = (bf16[2240,560]{0,1:T(8,128)(2,1)S(1)}, bf16[2240,560]{0,1:T(8,128)(2,1)}, u32[]{:S(2)}) copy-start(bf16[2240,560]{0,1:T(8,128)(2,1)} %param.8) | copy-start | bytes 7526404
  6.5 92.4 %all-gather.3.cloned.1.call-start = ((), (), s32[]{:S(2)}) async-start(), calls=%async_computation | async-start | bytes 5734400 | tf_op jit(solution)/shard_map/all_gather | solution.py:31
  7.3 146.8 %all-reduce.3.cloned.1.call-start = ((), (), s32[]{:S(2)}) async-start(), calls=%async_computation.1 | async-start | bytes 1146880 | tf_op jit(solution)/shard_map/psum | solution.py:50
  98.9 5.3 %copy-start.1 = (bf16[2,512,2240]{1,2,0:T(8,128)(2,1)S(1)}, bf16[2,512,2240]{1,2,0:T(8,128)(2,1)}, u32[]{:S(2)}) copy-start(bf16[2,512,2240]{1,2,0:T(8,128)(2,1)} %all-gather.3.cloned.1.call-done) | copy-start | bytes 13762564
  98.9 5.3 %copy-start.2 = (bf16[2240,560]{0,1:T(8,128)(2,1)S(1)}, bf16[2240,560]{0,1:T(8,128)(2,1)}, u32[]{:S(2)}) copy-start(bf16[2240,560]{0,1:T(8,128)(2,1)} %param.7) | copy-start | bytes 7526404
Sparse Core Ops, SparseCore 0:
  8.9 89.9 all-gather.2
  109.5 44.5 all-reduce.2
where the time goes:
time: 170 us; the launch traced here: 169 us
  waiting for transfers between devices  129 us (76%)
  matrix products  18.1 us (11%)
  between operations  13.5 us (8%)
  local copies, waits for them, and re-layouts  3.64 us (2%)
  blocking collectives  2.42 us (1%)
  other arithmetic  2.42 us (1%)
    all_gather x1, waiting for transfers between devices, local(): pieces = lax.all_gather(streams, 'head', axis=2, tiled=True)  90.8 us
    psum x1, waiting for transfers between devices, local(): clean_total, noisy_total = lax.psum((clean_part, noisy_part), 'tok')  37.8 us
    dot_general x3, matrix products, local(): jnp.einsum('std,dw->stw', pieces, matrix, preferred_element_type=jnp.floa...  15 us
  transfers between devices with their start and end apart: 2, of which 2 were waited for; matrix products, arithmetic and copies ran while one was open for 5% of the time, Pallas kernels for 0%

commit v1 on v0

v1 whole, which is shorter than its diff:
```python
import jax
import jax.numpy as jnp
from jax import lax
from jax.sharding import PartitionSpec as P

HEAD_DIM = 112


def gather_blocks(block, axis):
    count, mine = lax.axis_size(axis), lax.axis_index(axis)
    up = [(i, i + 1) for i in range(count - 1)]
    down = [(i + 1, i) for i in range(count - 1)]
    rising, falling = [block], [block]
    for _ in range(count - 1):
        rising.append(lax.ppermute(rising[-1], axis, up))
        falling.append(lax.ppermute(falling[-1], axis, down))
    rows = block.shape[0]
    whole = jnp.zeros((rows * count,) + block.shape[1:], block.dtype)
    whole = lax.dynamic_update_slice_in_dim(whole, block, mine * rows, 0)
    for back in range(1, count):
        piece = jnp.where(mine >= back, rising[back], falling[count - back])
        place = lax.rem(mine - back + count, count)
        whole = lax.dynamic_update_slice_in_dim(whole, piece, place * rows, 0)
    return whole


def sum_over(value, axis):
    count = lax.axis_size(axis)
    half = value.shape[0] // 2
    steps = [1 << b for b in range(count.bit_length() - 1)]
    outs = []
    for part, order in ((value[:half], steps), (value[half:], steps[::-1])):
        for step in order:
            sent = lax.ppermute(part.astype(jnp.bfloat16), axis, [(i, i ^ step) for i in range(count)])
            part = part + sent.astype(jnp.float32)
        outs.append(part)
    return jnp.concatenate(outs, axis=0)


def entering(value, axis):
    count, mine = lax.axis_size(axis), lax.axis_index(axis)
    total = lax.ppermute(value, axis, [(i, i + 1) for i in range(count - 1)])
    reach = 1
    while reach < count - 1:
        total = total + lax.ppermute(total, axis, [(i, i + reach) for i in range(count - reach)])
        reach *= 2
    return total


def project(matrix, block):
    return jnp.dot(matrix, block, preferred_element_type=jnp.float32).astype(jnp.bfloat16)


def local(streams, w_query, w_key, w_value, gain):
    width = w_query.shape[1]
    heads = width // HEAD_DIM
    tokens = streams.shape[1]
    columns = jnp.swapaxes(streams, 1, 2)
    w_query, w_key, w_value = w_query.T, w_key.T, w_value.T
    gain_heads = gain.reshape(heads, HEAD_DIM, 1)
    prefix, results = None, []
    for stream in range(2):
        features = gather_blocks(columns[stream], "head")
        key = jnp.maximum(project(w_key, features), 0).reshape(heads, HEAD_DIM, tokens)
        value = project(w_value, features).reshape(heads, HEAD_DIM, tokens)
        query = jnp.maximum(project(w_query, features), 0).reshape(heads, HEAD_DIM, tokens)
        state = jnp.einsum("hat,hbt->hba", key, value, preferred_element_type=jnp.float32)
        state = sum_over(state.reshape(width, HEAD_DIM), "tok")
        if stream == 0:
            prefix = entering(state, "group")
        total = (prefix + state).reshape(heads, HEAD_DIM, HEAD_DIM).astype(jnp.bfloat16)
        reading = jnp.einsum("hba,hat->hbt", total, query, preferred_element_type=jnp.float32)
        scale = lax.rsqrt(jnp.mean(reading * reading, axis=1, keepdims=True) + 1e-06)
        normed = reading * scale * gain_heads
        results.append(normed.astype(jnp.bfloat16).reshape(width, tokens))
    return jnp.swapaxes(jnp.stack(results), 1, 2)


def solution(mesh):
    return jax.shard_map(
        local,
        mesh=mesh,
        in_specs=(
            P(None, ("group", "tok"), "head"),
            P(None, "head"),
            P(None, "head"),
            P(None, "head"),
            P("head"),
        ),
        out_specs=P(None, ("group", "tok"), "head"),
        check_vma=False,
    )
```

time: 170 us -> 123 us (0.72)
  waiting for transfers between devices: 129 us -> 44.9 us
  starting transfers between devices: 0.04 us -> 46.2 us
  between operations: 13.5 us -> 0.34 us
  other arithmetic: 2.42 us -> 10.4 us
  matrix products: 18.1 us -> 15.1 us
  blocking collectives: 2.42 us -> 0 us
  local copies, waits for them, and re-layouts: 3.64 us -> 5.54 us
    all_gather x1 -> x0, waiting for transfers between devices: 90.8 us -> none  [local(): pieces = lax.all_gather(streams, 'head', axis=2, tiled=True)]
    ppermute x0 -> x21, starting transfers between devices: none -> 46.2 us  [the longest x6 28.8 us: gather_blocks(): rising.append(lax.ppermute(rising[-1], axis, up))]
    ppermute x0 -> x21, waiting for transfers between devices: none -> 44.9 us  [the longest x6 37 us: gather_blocks(): falling.append(lax.ppermute(falling[-1], axis, down))]
    psum x1 -> x0, waiting for transfers between devices: 37.8 us -> none  [local(): clean_total, noisy_total = lax.psum((clean_part, noisy_part), 'tok')]
    dynamic_update_slice x0 -> x5, other arithmetic: none -> 8.77 us  [gather_blocks(): whole = lax.dynamic_update_slice_in_dim(whole, piece, place * rows, 0)]
    dot_general x5 -> x10, matrix products: 18.1 us -> 15.1 us  [the longest x6 13.9 us: project(): jnp.dot(matrix, block, preferred_element_type=jnp.float32)]
    all_gather x1 -> x0, blocking collectives: 2.42 us -> none  [entering(): pieces = lax.all_gather(value, axis)]
    slice x3 -> x2, local copies, waits for them, and re-layouts: 1.8 us -> 0.05 us  [sum_over(): value[:half]]
  transfers between devices with their start and end apart: 2 -> 21, of which waited for: 2 -> 10; matrix products, arithmetic and copies ran while one was open for 5% -> 12% of each run, Pallas kernels for 0% -> 0%
where the time goes in v1:
time: 123 us
  starting transfers between devices  46.2 us (38%)
  waiting for transfers between devices  44.9 us (37%)
  matrix products  15.1 us (12%)
  other arithmetic  10.4 us (8%)
  local copies, waits for them, and re-layouts  5.54 us (5%)
    ppermute x6, waiting for transfers between devices, gather_blocks(): falling.append(lax.ppermute(falling[-1], axis, down))  37 us
    ppermute x6, starting transfers between devices, gather_blocks(): rising.append(lax.ppermute(rising[-1], axis, up))  28.8 us
    dot_general x6, matrix products, project(): jnp.dot(matrix, block, preferred_element_type=jnp.float32)  13.9 us
    dynamic_update_slice x5, other arithmetic, gather_blocks(): whole = lax.dynamic_update_slice_in_dim(whole, piece, place * rows, 0)  8.77 us
    ppermute x8, starting transfers between devices, sum_over(): lax.ppermute(part.astype(jnp.bfloat16), axis, [(i, i ^ step) for i in ran...  8.36 us
    ppermute x6, starting transfers between devices, gather_blocks(): falling.append(lax.ppermute(falling[-1], axis, down))  7.71 us
    ppermute x6, waiting for transfers between devices, gather_blocks(): rising.append(lax.ppermute(rising[-1], axis, up))  4.59 us
    ppermute x8, waiting for transfers between devices, sum_over(): lax.ppermute(part.astype(jnp.bfloat16), axis, [(i, i ^ step) for i in ran...  3.35 us
  transfers between devices with their start and end apart: 21, of which 10 were waited for; matrix products, arithmetic and copies ran while one was open for 12% of the time, Pallas kernels for 0%

profile of v1, /device:TPU:0, one launch (start us, length us, event | category | flops | bytes accessed | tf_op | source)
XLA Modules:
  0.0 122.5 jit_solution(5801184379047833303)
XLA Ops:
  0.0 1.5 %slice_bitcast_fusion = (bf16[560,512]{1,0:T(8,128)(2,1)S(1)}, bf16[560,512]{1,0:T(8,128)(2,1)S(1)}) fusion(bf16[2,560,512]{2,1,0:T(8,128)(2,1)} %bitcast.55), kind=kLoop, calls=%fused_computation.15 | loop fusion | bytes 2293760 | tf_op jit(solution)/shard_map/squeeze | solution.py:63
  1.5 1.3 %collective-permute-start.1 = (bf16[560,512]{1,0:T(8,128)(2,1)S(1)}, bf16[560,512]{1,0:T(8,128)(2,1)S(1)}, u32[]{:S(2)}, u32[]{:S(2)}) collective-permute-start(bf16[560,512]{1,0:T(8,128)(2,1)S(1)} %get-tuple-element.6), channel_id=1, source_target_pairs={{1,0},{2,1},{3,2},{5,4},{6,5},{7,6},{9,8},{10,9},{11,10},{13,12},{... | collective-permute-start | bytes 1720328 | tf_op jit(solution)/shard_map/ppermute | solution.py:16
  2.8 1.3 %collective-permute-start.12 = (bf16[560,512]{1,0:T(8,128)(2,1)S(1)}, bf16[560,512]{1,0:T(8,128)(2,1)}, u32[]{:S(2)}, u32[]{:S(2)}) collective-permute-start(bf16[560,512]{1,0:T(8,128)(2,1)S(1)} %get-tuple-element.5), channel_id=1, source_target_pairs={{1,0},{2,1},{3,2},{5,4},{6,5},{7,6},{9,8},{10,9},{11,10},{13,12},{... | collective-permute-start | bytes 1720328 | tf_op jit(solution)/shard_map/ppermute | solution.py:16
  4.1 7.0 %collective-permute-start.11 = (bf16[560,512]{1,0:T(8,128)(2,1)S(1)}, bf16[560,512]{1,0:T(8,128)(2,1)}, u32[]{:S(2)}, u32[]{:S(2)}) collective-permute-start(bf16[560,512]{1,0:T(8,128)(2,1)S(1)} %get-tuple-element.5), channel_id=1, source_target_pairs={{0,1},{1,2},{2,3},{4,5},{5,6},{6,7},{8,9},{9,10},{10,11},{12,13},{... | collective-permute-start | bytes 1720328 | tf_op jit(solution)/shard_map/ppermute | solution.py:15
  11.1 3.9 %collective-permute-start = (bf16[560,512]{1,0:T(8,128)(2,1)S(1)}, bf16[560,512]{1,0:T(8,128)(2,1)}, u32[]{:S(2)}, u32[]{:S(2)}) collective-permute-start(bf16[560,512]{1,0:T(8,128)(2,1)S(1)} %get-tuple-element.6), channel_id=1, source_target_pairs={{0,1},{1,2},{2,3},{4,5},{5,6},{6,7},{8,9},{9,10},{10,11},{12,13},{... | collective-permute-start | bytes 1720328 | tf_op jit(solution)/shard_map/ppermute | solution.py:15
  15.0 5.2 %collective-permute-done.1 = bf16[560,512]{1,0:T(8,128)(2,1)S(1)} collective-permute-done((bf16[560,512]{1,0:T(8,128)(2,1)S(1)}, bf16[560,512]{1,0:T(8,128)(2,1)S(1)}, u32[]{:S(2)}, u32[]{:S(2)}) %collective-permute-start.1) | collective-permute-done | bytes 573472 | tf_op jit(solution)/shard_map/ppermute | solution.py:16
  21.5 11.1 %collective-permute-done.12 = bf16[560,512]{1,0:T(8,128)(2,1)} collective-permute-done((bf16[560,512]{1,0:T(8,128)(2,1)S(1)}, bf16[560,512]{1,0:T(8,128)(2,1)}, u32[]{:S(2)}, u32[]{:S(2)}) %collective-permute-start.12) | collective-permute-done | bytes 573472 | tf_op jit(solution)/shard_map/ppermute | solution.py:16
  32.6 1.3 %collective-permute-start.13 = (bf16[560,512]{1,0:T(8,128)(2,1)}, bf16[560,512]{1,0:T(8,128)(2,1)}, u32[]{:S(2)}, u32[]{:S(2)}) collective-permute-start(bf16[560,512]{1,0:T(8,128)(2,1)} %collective-permute-done.12), channel_id=1, source_target_pairs={{1,0},{2,1},{3,2},{5,4},{6,5},{7,6},{9,8},{10,9},{11,10},{13,12},{... | collective-permute-start | bytes 1720328 | tf_op jit(solution)/shard_map/ppermute | solution.py:16
  33.9 5.4 %collective-permute-start.15 = (bf16[560,512]{1,0:T(8,128)(2,1)}, bf16[560,512]{1,0:T(8,128)(2,1)}, u32[]{:S(2)}, u32[]{:S(2)}) collective-permute-start(bf16[560,512]{1,0:T(8,128)(2,1)} %collective-permute-done.11), channel_id=1, source_target_pairs={{0,1},{1,2},{2,3},{4,5},{5,6},{6,7},{8,9},{9,10},{10,11},{12,13},{... | collective-permute-start | bytes 1720328 | tf_op jit(solution)/shard_map/ppermute | solution.py:15
  39.3 3.9 %collective-permute-start.4 = (bf16[560,512]{1,0:T(8,128)(2,1)}, bf16[560,512]{1,0:T(8,128)(2,1)}, u32[]{:S(2)}, u32[]{:S(2)}) collective-permute-start(bf16[560,512]{1,0:T(8,128)(2,1)} %collective-permute-done), channel_id=1, source_target_pairs={{0,1},{1,2},{2,3},{4,5},{5,6},{6,7},{8,9},{9,10},{10,11},{12,13},{... | collective-permute-start | bytes 1720328 | tf_op jit(solution)/shard_map/ppermute | solution.py:15
  43.2 1.6 %collective-permute-done.2 = bf16[560,512]{1,0:T(8,128)(2,1)} collective-permute-done((bf16[560,512]{1,0:T(8,128)(2,1)S(1)}, bf16[560,512]{1,0:T(8,128)(2,1)}, u32[]{:S(2)}, u32[]{:S(2)}) %collective-permute-start.2) | collective-permute-done | bytes 573472 | tf_op jit(solution)/shard_map/ppermute | solution.py:16
  46.2 11.0 %collective-permute-done.13 = bf16[560,512]{1,0:T(8,128)(2,1)} collective-permute-done((bf16[560,512]{1,0:T(8,128)(2,1)}, bf16[560,512]{1,0:T(8,128)(2,1)}, u32[]{:S(2)}, u32[]{:S(2)}) %collective-permute-start.13) | collective-permute-done | bytes 573472 | tf_op jit(solution)/shard_map/ppermute | solution.py:16
  58.5 1.6 %broadcast.42.clone.1 = bf16[2240,512]{1,0:T(8,128)(2,1)} broadcast(bf16[]{:T(256)} %constant.29.clone.1), dimensions={} | broadcast | bytes 2293762 | tf_op jit(solution)/shard_map/broadcast.7
  62.3 4.6 %collective-permute-start.16 = (bf16[560,512]{1,0:T(8,128)(2,1)}, bf16[560,512]{1,0:T(8,128)(2,1)S(1)}, u32[]{:S(2)}, u32[]{:S(2)}) collective-permute-start(bf16[560,512]{1,0:T(8,128)(2,1)} %collective-permute-done.15), channel_id=1, source_target_pairs={{0,1},{1,2},{2,3},{4,5},{5,6},{6,7},{8,9},{9,10},{10,11},{12,13},{... | collective-permute-start | bytes 1720328 | tf_op jit(solution)/shard_map/ppermute | solution.py:15
  66.9 3.9 %collective-permute-start.5 = (bf16[560,512]{1,0:T(8,128)(2,1)}, bf16[560,512]{1,0:T(8,128)(2,1)S(1)}, u32[]{:S(2)}, u32[]{:S(2)}) collective-permute-start(bf16[560,512]{1,0:T(8,128)(2,1)} %collective-permute-done.4), channel_id=1, source_target_pairs={{0,1},{1,2},{2,3},{4,5},{5,6},{6,7},{8,9},{9,10},{10,11},{12,13},{... | collective-permute-start | bytes 1720328 | tf_op jit(solution)/shard_map/ppermute | solution.py:15
  70.9 2.0 %select_dynamic-update-slice_fusion.5 = bf16[2240,512]{1,0:T(8,128)(2,1)} fusion(bf16[2240,512]{1,0:T(8,128)(2,1)} %constant_dynamic-update-slice_fusion.1, s32[]{:T(128)S(6)} %select_n.51, bf16[560,512]{1,0:T(8,128)(2,1)} %collective-permute-done, bf16[560,512]{1,0:T(8,128)(2,1)} %collective-permute-done.3, pred[]{:T(512)S(6)} %ge.12), kind=kLoop, calls=%fused_computation.22 | loop fusion | flops 286720 | bytes 1720325 | tf_op jit(solution)/shard_map/dynamic_update_slice | solution.py:23
  72.9 8.0 %collective-permute-done.14 = bf16[560,512]{1,0:T(8,128)(2,1)} collective-permute-done((bf16[560,512]{1,0:T(8,128)(2,1)}, bf16[560,512]{1,0:T(8,128)(2,1)}, u32[]{:S(2)}, u32[]{:S(2)}) %collective-permute-start.14) | collective-permute-done | bytes 573472 | tf_op jit(solution)/shard_map/ppermute | solution.py:16
  82.1 2.0 %select_dynamic-update-slice_fusion.4 = bf16[2240,512]{1,0:T(8,128)(2,1)} fusion(bf16[2240,512]{1,0:T(8,128)(2,1)} %select_dynamic-update-slice_fusion.5, s32[]{:T(128)S(6)} %select_n.54, bf16[560,512]{1,0:T(8,128)(2,1)} %collective-permute-done.4, bf16[560,512]{1,0:T(8,128)(2,1)} %collective-permute-done.2, pred[]{:T(512)S(6)} %ge.13), kind=kLoop, calls=%fused_computation.21 | loop fusion | flops 286720 | bytes 1720325 | tf_op jit(solution)/shard_map/dynamic_update_slice | solution.py:23
  85.4 4.6 %collective-permute-done.5 = bf16[560,512]{1,0:T(8,128)(2,1)S(1)} collective-permute-done((bf16[560,512]{1,0:T(8,128)(2,1)}, bf16[560,512]{1,0:T(8,128)(2,1)S(1)}, u32[]{:S(2)}, u32[]{:S(2)}) %collective-permute-start.5) | collective-permute-done | bytes 573472 | tf_op jit(solution)/shard_map/ppermute | solution.py:15
  90.0 2.3 %select_dynamic-update-slice_fusion = (bf16[2240,512]{1,0:T(8,128)(2,1)S(1)}, bf16[2240,512]{1,0:T(8,128)(2,1)}) fusion(bf16[2240,512]{1,0:T(8,128)(2,1)S(1)} %select_dynamic-update-slice_fusion.1, s32[]{:T(128)S(6)} %select_n.57, bf16[560,512]{1,0:T(8,128)(2,1)S(1)} %collective-permute-done.16, bf16[560,512]{1,0:T(8,128)(2,1)} %collective-permute-done.12, ...), kind=kLoop, calls=%fused_computation.17 | loop fusion | flops 573440 | bytes 3440645 | tf_op jit(solution)/shard_map/dynamic_update_slice | solution.py:23
  92.3 1.5 %convolution_convert_fusion.2 = bf16[512,560]{0,1:T(8,128)(2,1)S(1)} fusion(bf16[2240,560]{0,1:T(8,128)(2,1)S(1)} %copy-done, bf16[2240,512]{1,0:T(8,128)(2,1)S(1)} %get-tuple-element.27), kind=kOutput, calls=%fused_computation.2 | convolution fusion | flops 1284792320 | bytes 5376000 | tf_op jit(solution)/shard_map/dot_general | solution.py:51
  94.0 1.5 %fusion.2 = bf16[512,560]{0,1:T(8,128)(2,1)S(1)} fusion(bf16[2240,560]{0,1:T(8,128)(2,1)S(1)} %copy-done.4, bf16[2240,512]{1,0:T(8,128)(2,1)S(1)} %get-tuple-element.27), kind=kOutput, calls=%fused_computation.8 | convolution fusion | flops 1285079040 | bytes 5376000 | tf_op jit(solution)/shard_map/dot_general | solution.py:51
  95.5 3.1 %convolution_convert_fusion.5 = bf16[512,560]{0,1:T(8,128)(2,1)S(1)} fusion(bf16[2240,560]{0,1:T(8,128)(2,1)S(1)} %copy-done, bf16[2240,512]{1,0:T(8,128)(2,1)} %get-tuple-element.28), kind=kOutput, calls=%fused_computation.5 | convolution fusion | flops 1284792320 | bytes 5376000 | tf_op jit(solution)/shard_map/dot_general | solution.py:51
  98.6 3.1 %fusion = bf16[512,560]{0,1:T(8,128)(2,1)S(1)} fusion(bf16[2240,560]{0,1:T(8,128)(2,1)S(1)} %copy-done.4, bf16[2240,512]{1,0:T(8,128)(2,1)} %get-tuple-element.28), kind=kOutput, calls=%fused_computation.6 | convolution fusion | flops 1285079040 | bytes 5376000 | tf_op jit(solution)/shard_map/dot_general | solution.py:51
  102.1 1.4 %collective-permute-start.17 = (bf16[280,112]{1,0:T(8,128)(2,1)S(1)}, bf16[280,112]{1,0:T(8,128)(2,1)S(1)}, u32[]{:S(2)}, u32[]{:S(2)}) collective-permute-start(bf16[280,112]{1,0:T(8,128)(2,1)S(1)} %get-tuple-element.13), channel_id=1, source_target_pairs={{0,4},{4,0},{8,12},{12,8},{1,5},{5,1},{9,13},{13,9},{2,6},{6,2},{1... | collective-permute-start | bytes 188168 | tf_op jit(solution)/shard_map/ppermute | solution.py:34
  103.5 1.5 %collective-permute-start.19 = (bf16[280,112]{1,0:T(8,128)(2,1)S(1)}, bf16[280,112]{1,0:T(8,128)(2,1)S(1)}, u32[]{:S(2)}, u32[]{:S(2)}) collective-permute-start(bf16[280,112]{1,0:T(8,128)(2,1)S(1)} %get-tuple-element.14), channel_id=1, source_target_pairs={{0,8},{4,12},{8,0},{12,4},{1,9},{5,13},{9,1},{13,5},{2,10},{6,14},... | collective-permute-start | bytes 188168 | tf_op jit(solution)/shard_map/ppermute | solution.py:34
  106.6 1.5 %fusion.3 = bf16[512,560]{0,1:T(8,128)(2,1)S(1)} fusion(bf16[2240,560]{0,1:T(8,128)(2,1)S(1)} %copy-done.5, bf16[2240,512]{1,0:T(8,128)(2,1)S(1)} %get-tuple-element.27), kind=kOutput, calls=%fused_computation.9 | convolution fusion | flops 1285079040 | bytes 5376000 | tf_op jit(solution)/shard_map/dot_general | solution.py:51
  108.1 2.0 %collective-permute-done.6 = bf16[280,112]{1,0:T(8,128)(2,1)S(1)} collective-permute-done((bf16[280,112]{1,0:T(8,128)(2,1)S(1)}, bf16[280,112]{1,0:T(8,128)(2,1)S(1)}, u32[]{:S(2)}, u32[]{:S(2)}) %collective-permute-start.6) | collective-permute-done | bytes 62752 | tf_op jit(solution)/shard_map/ppermute | solution.py:34
  111.4 1.5 %collective-permute-start.9 = (bf16[280,112]{1,0:T(8,128)(2,1)S(1)}, bf16[280,112]{1,0:T(8,128)(2,1)S(1)}, u32[]{:S(2)}, u32[]{:S(2)}) collective-permute-start(bf16[280,112]{1,0:T(8,128)(2,1)S(1)} %get-tuple-element.18), channel_id=1, source_target_pairs={{0,4},{4,0},{8,12},{12,8},{1,5},{5,1},{9,13},{13,9},{2,6},{6,2},{1... | collective-permute-start | bytes 188168 | tf_op jit(solution)/shard_map/ppermute | solution.py:34
  112.9 1.3 %collective-permute-start.18 = (bf16[280,112]{1,0:T(8,128)(2,1)S(1)}, bf16[280,112]{1,0:T(8,128)(2,1)S(1)}, u32[]{:S(2)}, u32[]{:S(2)}) collective-permute-start(bf16[280,112]{1,0:T(8,128)(2,1)S(1)} %get-tuple-element.11), channel_id=1, source_target_pairs={{0,8},{4,12},{8,0},{12,4},{1,9},{5,13},{9,1},{13,5},{2,10},{6,14},... | collective-permute-start | bytes 188168 | tf_op jit(solution)/shard_map/ppermute | solution.py:34
  115.8 1.3 %collective-permute-start.10 = (f32[560,112]{1,0:T(8,128)S(1)}, f32[560,112]{1,0:T(8,128)S(1)}, u32[]{:S(2)}, u32[]{:S(2)}) collective-permute-start(f32[560,112]{1,0:T(8,128)S(1)} %pad_maximum_fusion), channel_id=1, source_target_pairs={{0,16},{1,17},{2,18},{3,19},{4,20},{5,21},{6,22},{7,23},{8,24},{9,... | collective-permute-start | bytes 752648 | tf_op jit(solution)/shard_map/ppermute | solution.py:42
  117.2 3.1 %fusion.1 = bf16[512,560]{0,1:T(8,128)(2,1)S(1)} fusion(bf16[2240,560]{0,1:T(8,128)(2,1)S(1)} %copy-done.5, bf16[2240,512]{1,0:T(8,128)(2,1)} %get-tuple-element.28), kind=kOutput, calls=%fused_computation.7 | convolution fusion | flops 1285079040 | bytes 5376000 | tf_op jit(solution)/shard_map/dot_general | solution.py:51
  (55 shorter events, 15.6 us)
Async XLA Ops:
  0.0 92.3 %copy-start = (bf16[2240,560]{0,1:T(8,128)(2,1)S(1)}, bf16[2240,560]{0,1:T(8,128)(2,1)}, u32[]{:S(2)}) copy-start(bf16[2240,560]{0,1:T(8,128)(2,1)} %param.8) | copy-start | bytes 7526404
  1.5 59.4 %copy-start.3 = (f32[560]{0:T(1024)S(1)}, f32[560]{0:T(1024)}, u32[]{:S(2)}) copy-start(f32[560]{0:T(1024)} %param.9) | copy-start | bytes 6724
  1.5 18.7 %collective-permute-start.1 = (bf16[560,512]{1,0:T(8,128)(2,1)S(1)}, bf16[560,512]{1,0:T(8,128)(2,1)S(1)}, u32[]{:S(2)}, u32[]{:S(2)}) collective-permute-start(bf16[560,512]{1,0:T(8,128)(2,1)S(1)} %get-tuple-element.6), channel_id=1, source_target_pairs={{1,0},{2,1},{3,2},{5,4},{6,5},{7,6},{9,8},{10,9},{11,10},{13,12},{... | collective-permute-start | bytes 1720328 | tf_op jit(solution)/shard_map/ppermute | solution.py:16
  2.8 29.8 %collective-permute-start.12 = (bf16[560,512]{1,0:T(8,128)(2,1)S(1)}, bf16[560,512]{1,0:T(8,128)(2,1)}, u32[]{:S(2)}, u32[]{:S(2)}) collective-permute-start(bf16[560,512]{1,0:T(8,128)(2,1)S(1)} %get-tuple-element.5), channel_id=1, source_target_pairs={{1,0},{2,1},{3,2},{5,4},{6,5},{7,6},{9,8},{10,9},{11,10},{13,12},{... | collective-permute-start | bytes 1720328 | tf_op jit(solution)/shard_map/ppermute | solution.py:16
  4.1 29.8 %collective-permute-start.11 = (bf16[560,512]{1,0:T(8,128)(2,1)S(1)}, bf16[560,512]{1,0:T(8,128)(2,1)}, u32[]{:S(2)}, u32[]{:S(2)}) collective-permute-start(bf16[560,512]{1,0:T(8,128)(2,1)S(1)} %get-tuple-element.5), channel_id=1, source_target_pairs={{0,1},{1,2},{2,3},{4,5},{5,6},{6,7},{8,9},{9,10},{10,11},{12,13},{... | collective-permute-start | bytes 1720328 | tf_op jit(solution)/shard_map/ppermute | solution.py:15
  11.1 28.2 %collective-permute-start = (bf16[560,512]{1,0:T(8,128)(2,1)S(1)}, bf16[560,512]{1,0:T(8,128)(2,1)}, u32[]{:S(2)}, u32[]{:S(2)}) collective-permute-start(bf16[560,512]{1,0:T(8,128)(2,1)S(1)} %get-tuple-element.6), channel_id=1, source_target_pairs={{0,1},{1,2},{2,3},{4,5},{5,6},{6,7},{8,9},{9,10},{10,11},{12,13},{... | collective-permute-start | bytes 1720328 | tf_op jit(solution)/shard_map/ppermute | solution.py:15
  20.2 24.7 %collective-permute-start.2 = (bf16[560,512]{1,0:T(8,128)(2,1)S(1)}, bf16[560,512]{1,0:T(8,128)(2,1)}, u32[]{:S(2)}, u32[]{:S(2)}) collective-permute-start(bf16[560,512]{1,0:T(8,128)(2,1)S(1)} %collective-permute-done.1), channel_id=1, source_target_pairs={{1,0},{2,1},{3,2},{5,4},{6,5},{7,6},{9,8},{10,9},{11,10},{13,12},{... | collective-permute-start | bytes 1720328 | tf_op jit(solution)/shard_map/ppermute | solution.py:16
  32.6 24.6 %collective-permute-start.13 = (bf16[560,512]{1,0:T(8,128)(2,1)}, bf16[560,512]{1,0:T(8,128)(2,1)}, u32[]{:S(2)}, u32[]{:S(2)}) collective-permute-start(bf16[560,512]{1,0:T(8,128)(2,1)} %collective-permute-done.12), channel_id=1, source_target_pairs={{1,0},{2,1},{3,2},{5,4},{6,5},{7,6},{9,8},{10,9},{11,10},{13,12},{... | collective-permute-start | bytes 1720328 | tf_op jit(solution)/shard_map/ppermute | solution.py:16
  33.9 28.4 %collective-permute-start.15 = (bf16[560,512]{1,0:T(8,128)(2,1)}, bf16[560,512]{1,0:T(8,128)(2,1)}, u32[]{:S(2)}, u32[]{:S(2)}) collective-permute-start(bf16[560,512]{1,0:T(8,128)(2,1)} %collective-permute-done.11), channel_id=1, source_target_pairs={{0,1},{1,2},{2,3},{4,5},{5,6},{6,7},{8,9},{9,10},{10,11},{12,13},{... | collective-permute-start | bytes 1720328 | tf_op jit(solution)/shard_map/ppermute | solution.py:15
  39.3 27.6 %collective-permute-start.4 = (bf16[560,512]{1,0:T(8,128)(2,1)}, bf16[560,512]{1,0:T(8,128)(2,1)}, u32[]{:S(2)}, u32[]{:S(2)}) collective-permute-start(bf16[560,512]{1,0:T(8,128)(2,1)} %collective-permute-done), channel_id=1, source_target_pairs={{0,1},{1,2},{2,3},{4,5},{5,6},{6,7},{8,9},{9,10},{10,11},{12,13},{... | collective-permute-start | bytes 1720328 | tf_op jit(solution)/shard_map/ppermute | solution.py:15
  44.9 26.0 %collective-permute-start.3 = (bf16[560,512]{1,0:T(8,128)(2,1)}, bf16[560,512]{1,0:T(8,128)(2,1)}, u32[]{:S(2)}, u32[]{:S(2)}) collective-permute-start(bf16[560,512]{1,0:T(8,128)(2,1)} %collective-permute-done.2), channel_id=1, source_target_pairs={{1,0},{2,1},{3,2},{5,4},{6,5},{7,6},{9,8},{10,9},{11,10},{13,12},{... | collective-permute-start | bytes 1720328 | tf_op jit(solution)/shard_map/ppermute | solution.py:16
  46.2 13.8 %copy-start.1 = (bf16[2,512,560]{1,2,0:T(8,128)(2,1)S(1)}, bf16[2,512,560]{1,2,0:T(8,128)(2,1)}, u32[]{:S(2)}) copy-start(bf16[2,512,560]{1,2,0:T(8,128)(2,1)} %param.5) | copy-start | bytes 3440644
  57.2 23.7 %collective-permute-start.14 = (bf16[560,512]{1,0:T(8,128)(2,1)}, bf16[560,512]{1,0:T(8,128)(2,1)}, u32[]{:S(2)}, u32[]{:S(2)}) collective-permute-start(bf16[560,512]{1,0:T(8,128)(2,1)} %collective-permute-done.13), channel_id=1, source_target_pairs={{1,0},{2,1},{3,2},{5,4},{6,5},{7,6},{9,8},{10,9},{11,10},{13,12},{... | collective-permute-start | bytes 1720328 | tf_op jit(solution)/shard_map/ppermute | solution.py:16
  61.0 1.3 %copy-start.2 = (bf16[2,512,560]{1,2,0:T(8,128)(2,1)S(1)}, bf16[2,512,560]{1,2,0:T(8,128)(2,1)}, u32[]{:S(2)}) copy-start(bf16[2,512,560]{1,2,0:T(8,128)(2,1)} %param.5) | copy-start | bytes 3440644
  62.3 23.1 %collective-permute-start.16 = (bf16[560,512]{1,0:T(8,128)(2,1)}, bf16[560,512]{1,0:T(8,128)(2,1)S(1)}, u32[]{:S(2)}, u32[]{:S(2)}) collective-permute-start(bf16[560,512]{1,0:T(8,128)(2,1)} %collective-permute-done.15), channel_id=1, source_target_pairs={{0,1},{1,2},{2,3},{4,5},{5,6},{6,7},{8,9},{9,10},{10,11},{12,13},{... | collective-permute-start | bytes 1720328 | tf_op jit(solution)/shard_map/ppermute | solution.py:15
  66.9 23.1 %collective-permute-start.5 = (bf16[560,512]{1,0:T(8,128)(2,1)}, bf16[560,512]{1,0:T(8,128)(2,1)S(1)}, u32[]{:S(2)}, u32[]{:S(2)}) collective-permute-start(bf16[560,512]{1,0:T(8,128)(2,1)} %collective-permute-done.4), channel_id=1, source_target_pairs={{0,1},{1,2},{2,3},{4,5},{5,6},{6,7},{8,9},{9,10},{10,11},{12,13},{... | collective-permute-start | bytes 1720328 | tf_op jit(solution)/shard_map/ppermute | solution.py:15
  92.3 1.7 %copy-start.4 = (bf16[2240,560]{0,1:T(8,128)(2,1)S(1)}, bf16[2240,560]{0,1:T(8,128)(2,1)}, u32[]{:S(2)}) copy-start(bf16[2240,560]{0,1:T(8,128)(2,1)} %param.7) | copy-start | bytes 7526404
  101.8 4.9 %copy-start.5 = (bf16[2240,560]{0,1:T(8,128)(2,1)S(1)}, bf16[2240,560]{0,1:T(8,128)(2,1)}, u32[]{:S(2)}) copy-start(bf16[2240,560]{0,1:T(8,128)(2,1)} %param.6) | copy-start | bytes 7526404
  102.1 10.8 %collective-permute-start.17 = (bf16[280,112]{1,0:T(8,128)(2,1)S(1)}, bf16[280,112]{1,0:T(8,128)(2,1)S(1)}, u32[]{:S(2)}, u32[]{:S(2)}) collective-permute-start(bf16[280,112]{1,0:T(8,128)(2,1)S(1)} %get-tuple-element.13), channel_id=1, source_target_pairs={{0,4},{4,0},{8,12},{12,8},{1,5},{5,1},{9,13},{13,9},{2,6},{6,2},{1... | collective-permute-start | bytes 188168 | tf_op jit(solution)/shard_map/ppermute | solution.py:34
  103.5 9.4 %collective-permute-start.19 = (bf16[280,112]{1,0:T(8,128)(2,1)S(1)}, bf16[280,112]{1,0:T(8,128)(2,1)S(1)}, u32[]{:S(2)}, u32[]{:S(2)}) collective-permute-start(bf16[280,112]{1,0:T(8,128)(2,1)S(1)} %get-tuple-element.14), channel_id=1, source_target_pairs={{0,8},{4,12},{8,0},{12,4},{1,9},{5,13},{9,1},{13,5},{2,10},{6,14},... | collective-permute-start | bytes 188168 | tf_op jit(solution)/shard_map/ppermute | solution.py:34
  105.4 4.8 %collective-permute-start.6 = (bf16[280,112]{1,0:T(8,128)(2,1)S(1)}, bf16[280,112]{1,0:T(8,128)(2,1)S(1)}, u32[]{:S(2)}, u32[]{:S(2)}) collective-permute-start(bf16[280,112]{1,0:T(8,128)(2,1)S(1)} %get-tuple-element.19), channel_id=1, source_target_pairs={{0,4},{4,0},{8,12},{12,8},{1,5},{5,1},{9,13},{13,9},{2,6},{6,2},{1... | collective-permute-start | bytes 188168 | tf_op jit(solution)/shard_map/ppermute | solution.py:34
  106.0 4.7 %collective-permute-start.8 = (bf16[280,112]{1,0:T(8,128)(2,1)S(1)}, bf16[280,112]{1,0:T(8,128)(2,1)S(1)}, u32[]{:S(2)}, u32[]{:S(2)}) collective-permute-start(bf16[280,112]{1,0:T(8,128)(2,1)S(1)} %get-tuple-element.20), channel_id=1, source_target_pairs={{0,8},{4,12},{8,0},{12,4},{1,9},{5,13},{9,1},{13,5},{2,10},{6,14},... | collective-permute-start | bytes 188168 | tf_op jit(solution)/shard_map/ppermute | solution.py:34
  110.8 4.4 %collective-permute-start.7 = (bf16[280,112]{1,0:T(8,128)(2,1)S(1)}, bf16[280,112]{1,0:T(8,128)(2,1)S(1)}, u32[]{:S(2)}, u32[]{:S(2)}) collective-permute-start(bf16[280,112]{1,0:T(8,128)(2,1)S(1)} %get-tuple-element.17), channel_id=1, source_target_pairs={{0,8},{4,12},{8,0},{12,4},{1,9},{5,13},{9,1},{13,5},{2,10},{6,14},... | collective-permute-start | bytes 188168 | tf_op jit(solution)/shard_map/ppermute | solution.py:34
  111.4 4.3 %collective-permute-start.9 = (bf16[280,112]{1,0:T(8,128)(2,1)S(1)}, bf16[280,112]{1,0:T(8,128)(2,1)S(1)}, u32[]{:S(2)}, u32[]{:S(2)}) collective-permute-start(bf16[280,112]{1,0:T(8,128)(2,1)S(1)} %get-tuple-element.18), channel_id=1, source_target_pairs={{0,4},{4,0},{8,12},{12,8},{1,5},{5,1},{9,13},{13,9},{2,6},{6,2},{1... | collective-permute-start | bytes 188168 | tf_op jit(solution)/shard_map/ppermute | solution.py:34
  112.9 7.4 %collective-permute-start.18 = (bf16[280,112]{1,0:T(8,128)(2,1)S(1)}, bf16[280,112]{1,0:T(8,128)(2,1)S(1)}, u32[]{:S(2)}, u32[]{:S(2)}) collective-permute-start(bf16[280,112]{1,0:T(8,128)(2,1)S(1)} %get-tuple-element.11), channel_id=1, source_target_pairs={{0,8},{4,12},{8,0},{12,4},{1,9},{5,13},{9,1},{13,5},{2,10},{6,14},... | collective-permute-start | bytes 188168 | tf_op jit(solution)/shard_map/ppermute | solution.py:34
  114.3 6.0 %collective-permute-start.20 = (bf16[280,112]{1,0:T(8,128)(2,1)S(1)}, bf16[280,112]{1,0:T(8,128)(2,1)S(1)}, u32[]{:S(2)}, u32[]{:S(2)}) collective-permute-start(bf16[280,112]{1,0:T(8,128)(2,1)S(1)} %get-tuple-element.12), channel_id=1, source_target_pairs={{0,4},{4,0},{8,12},{12,8},{1,5},{5,1},{9,13},{13,9},{2,6},{6,2},{1... | collective-permute-start | bytes 188168 | tf_op jit(solution)/shard_map/ppermute | solution.py:34
  115.8 4.5 %collective-permute-start.10 = (f32[560,112]{1,0:T(8,128)S(1)}, f32[560,112]{1,0:T(8,128)S(1)}, u32[]{:S(2)}, u32[]{:S(2)}) collective-permute-start(f32[560,112]{1,0:T(8,128)S(1)} %pad_maximum_fusion), channel_id=1, source_target_pairs={{0,16},{1,17},{2,18},{3,19},{4,20},{5,21},{6,22},{7,23},{8,24},{9,... | collective-permute-start | bytes 752648 | tf_op jit(solution)/shard_map/ppermute | solution.py:42

commit v2 on v1

--- a/solution.py
+++ b/solution.py
@@ -6,21 +6,29 @@
 HEAD_DIM = 112
 
 
+def swap(value, axis, pairs):
+    ends = dict(pairs) | {j: i for i, j in pairs}
+    count = lax.axis_size(axis)
+    return lax.ppermute(value, axis, [(i, ends.get(i, i)) for i in range(count)])
+
+
 def gather_blocks(block, axis):
     count, mine = lax.axis_size(axis), lax.axis_index(axis)
-    up = [(i, i + 1) for i in range(count - 1)]
-    down = [(i + 1, i) for i in range(count - 1)]
-    rising, falling = [block], [block]
-    for _ in range(count - 1):
-        rising.append(lax.ppermute(rising[-1], axis, up))
-        falling.append(lax.ppermute(falling[-1], axis, down))
+    if count != 4:
+        return lax.all_gather(block, axis, axis=0, tiled=True)
+    partners, middle = [(0, 1), (2, 3)], [(1, 2)]
+    near = swap(block, axis, partners)
+    across = swap(block, axis, middle)
+    far = swap(near, axis, middle)
+    across_end = swap(across, axis, partners)
+    far_end = swap(far, axis, partners)
+    inner = (mine == 1) | (mine == 2)
+    second = jnp.where(inner, far, across_end)
+    third = jnp.where(inner, across, far_end)
     rows = block.shape[0]
     whole = jnp.zeros((rows * count,) + block.shape[1:], block.dtype)
-    whole = lax.dynamic_update_slice_in_dim(whole, block, mine * rows, 0)
-    for back in range(1, count):
-        piece = jnp.where(mine >= back, rising[back], falling[count - back])
-        place = lax.rem(mine - back + count, count)
-        whole = lax.dynamic_update_slice_in_dim(whole, piece, place * rows, 0)
+    for flip, piece in enumerate((block, near, second, third)):
+        whole = lax.dynamic_update_slice_in_dim(whole, piece, (mine ^ flip) * rows, 0)
     return whole
 
 

time: 123 us -> 121 us (0.984)
  waiting for transfers between devices: 44.9 us -> 29.8 us
  local copies, waits for them, and re-layouts: 5.54 us -> 11.3 us
  matrix products: 15.1 us -> 20.2 us
  starting transfers between devices: 46.2 us -> 51.3 us
  other arithmetic: 10.4 us -> 7.05 us
    ppermute x12 -> x10, waiting for transfers between devices: 41.5 us -> 28.1 us  [swap(): lax.ppermute(value, axis, [(i, ends.get(i, i)) for i in range(count)])]
    ppermute x12 -> x10, starting transfers between devices: 36.5 us -> 41.6 us  [swap(): lax.ppermute(value, axis, [(i, ends.get(i, i)) for i in range(count)])]
    dot_general x6, matrix products: 13.9 us -> 19 us  [project(): jnp.dot(matrix, block, preferred_element_type=jnp.float32)]
    dynamic_update_slice x2 -> x4, local copies, waits for them, and re-layouts: 0.89 us -> 5.55 us  [gather_blocks(): lax.dynamic_update_slice_in_dim(whole, piece, (mine ^ flip) * rows, 0)]
    dynamic_update_slice x5 -> x3, other arithmetic: 8.77 us -> 5.39 us  [gather_blocks(): lax.dynamic_update_slice_in_dim(whole, piece, (mine ^ flip) * rows, 0)]
    ppermute x8, waiting for transfers between devices: 3.35 us -> 1.71 us  [sum_over(): lax.ppermute(part.astype(jnp.bfloat16), axis, [(i, i ^ step) for i in ran...]
    another operation x2, local copies, waits for them, and re-layouts: 1.71 us -> 3.15 us
    unnamed x12 -> x10, local copies, waits for them, and re-layouts: 1.36 us -> 0.02 us
  transfers between devices with their start and end apart: 21 -> 19, of which waited for: 10 -> 8; matrix products, arithmetic and copies ran while one was open for 12% -> 16% of each run, Pallas kernels for 0% -> 0%
where the time goes in v2:
time: 121 us; the launch traced here: 120 us
  starting transfers between devices  51.3 us (42%)
  waiting for transfers between devices  29.8 us (25%)
  matrix products  20.2 us (17%)
  local copies, waits for them, and re-layouts  11.3 us (9%)
  other arithmetic  7.05 us (6%)
    ppermute x10, starting transfers between devices, swap(): lax.ppermute(value, axis, [(i, ends.get(i, i)) for i in range(count)])  41.6 us
    ppermute x10, waiting for transfers between devices, swap(): lax.ppermute(value, axis, [(i, ends.get(i, i)) for i in range(count)])  28.1 us
    dot_general x6, matrix products, project(): jnp.dot(matrix, block, preferred_element_type=jnp.float32)  19 us
    ppermute x8, starting transfers between devices, sum_over(): lax.ppermute(part.astype(jnp.bfloat16), axis, [(i, i ^ step) for i in ran...  8.36 us
    dynamic_update_slice x4, local copies, waits for them, and re-layouts, gather_blocks(): lax.dynamic_update_slice_in_dim(whole, piece, (mine ^ flip) * rows, 0)  5.55 us
    dynamic_update_slice x3, other arithmetic, gather_blocks(): lax.dynamic_update_slice_in_dim(whole, piece, (mine ^ flip) * rows, 0)  5.39 us
    another operation x2, local copies, waits for them, and re-layouts  3.15 us
    squeeze x1, local copies, waits for them, and re-layouts, local(): features = gather_blocks(columns[stream], 'head')  2.48 us
  transfers between devices with their start and end apart: 19, of which 8 were waited for; matrix products, arithmetic and copies ran while one was open for 16% of the time, Pallas kernels for 0%

profile of v2, /device:TPU:0, one launch (start us, length us, event | category | flops | bytes accessed | tf_op | source)
XLA Modules:
  0.0 119.9 jit_solution(14373362269698981103)
XLA Ops:
  0.0 2.5 %slice_bitcast_fusion = (bf16[560,512]{1,0:T(8,128)(2,1)}, bf16[560,512]{1,0:T(8,128)(2,1)}) fusion(bf16[2,560,512]{2,1,0:T(8,128)(2,1)} %bitcast.55), kind=kLoop, calls=%fused_computation.15 | loop fusion | bytes 2293760 | tf_op jit(solution)/shard_map/squeeze | solution.py:71
  2.5 3.0 %collective-permute-start = (bf16[560,512]{1,0:T(8,128)(2,1)}, bf16[560,512]{1,0:T(8,128)(2,1)}, u32[]{:S(2)}, u32[]{:S(2)}) collective-permute-start(bf16[560,512]{1,0:T(8,128)(2,1)} %get-tuple-element.6), channel_id=1, source_target_pairs={{0,1},{1,0},{2,3},{3,2},{4,5},{5,4},{6,7},{7,6},{8,9},{9,8},{10,11... | collective-permute-start | bytes 1720328 | tf_op jit(solution)/shard_map/ppermute | solution.py:12
  5.5 1.7 %collective-permute-start.2 = (bf16[560,512]{1,0:T(8,128)(2,1)}, bf16[560,512]{1,0:T(8,128)(2,1)S(1)}, u32[]{:S(2)}, u32[]{:S(2)}) collective-permute-start(bf16[560,512]{1,0:T(8,128)(2,1)} %get-tuple-element.6), channel_id=1, source_target_pairs={{0,0},{1,2},{2,1},{3,3},{4,4},{5,6},{6,5},{7,7},{8,8},{9,10},{10,9... | collective-permute-start | bytes 1720328 | tf_op jit(solution)/shard_map/ppermute | solution.py:12
  7.2 3.4 %collective-permute-start.10 = (bf16[560,512]{1,0:T(8,128)(2,1)}, bf16[560,512]{1,0:T(8,128)(2,1)}, u32[]{:S(2)}, u32[]{:S(2)}) collective-permute-start(bf16[560,512]{1,0:T(8,128)(2,1)} %get-tuple-element.5), channel_id=1, source_target_pairs={{0,1},{1,0},{2,3},{3,2},{4,5},{5,4},{6,7},{7,6},{8,9},{9,8},{10,11... | collective-permute-start | bytes 1720328 | tf_op jit(solution)/shard_map/ppermute | solution.py:12
  10.6 5.9 %collective-permute-start.12 = (bf16[560,512]{1,0:T(8,128)(2,1)}, bf16[560,512]{1,0:T(8,128)(2,1)}, u32[]{:S(2)}, u32[]{:S(2)}) collective-permute-start(bf16[560,512]{1,0:T(8,128)(2,1)} %get-tuple-element.5), channel_id=1, source_target_pairs={{0,0},{1,2},{2,1},{3,3},{4,4},{5,6},{6,5},{7,7},{8,8},{9,10},{10,9... | collective-permute-start | bytes 1720328 | tf_op jit(solution)/shard_map/ppermute | solution.py:12
  16.6 3.1 %collective-permute-done = bf16[560,512]{1,0:T(8,128)(2,1)} collective-permute-done((bf16[560,512]{1,0:T(8,128)(2,1)}, bf16[560,512]{1,0:T(8,128)(2,1)}, u32[]{:S(2)}, u32[]{:S(2)}) %collective-permute-start) | collective-permute-done | bytes 573472 | tf_op jit(solution)/shard_map/ppermute | solution.py:12
  19.6 5.9 %collective-permute-start.1 = (bf16[560,512]{1,0:T(8,128)(2,1)}, bf16[560,512]{1,0:T(8,128)(2,1)}, u32[]{:S(2)}, u32[]{:S(2)}) collective-permute-start(bf16[560,512]{1,0:T(8,128)(2,1)} %collective-permute-done), channel_id=1, source_target_pairs={{0,0},{1,2},{2,1},{3,3},{4,4},{5,6},{6,5},{7,7},{8,8},{9,10},{10,9... | collective-permute-start | bytes 1720328 | tf_op jit(solution)/shard_map/ppermute | solution.py:12
  25.5 6.4 %collective-permute-done.10 = bf16[560,512]{1,0:T(8,128)(2,1)} collective-permute-done((bf16[560,512]{1,0:T(8,128)(2,1)}, bf16[560,512]{1,0:T(8,128)(2,1)}, u32[]{:S(2)}, u32[]{:S(2)}) %collective-permute-start.10) | collective-permute-done | bytes 573472 | tf_op jit(solution)/shard_map/ppermute | solution.py:12
  31.9 5.9 %collective-permute-start.11 = (bf16[560,512]{1,0:T(8,128)(2,1)}, bf16[560,512]{1,0:T(8,128)(2,1)}, u32[]{:S(2)}, u32[]{:S(2)}) collective-permute-start(bf16[560,512]{1,0:T(8,128)(2,1)} %collective-permute-done.10), channel_id=1, source_target_pairs={{0,0},{1,2},{2,1},{3,3},{4,4},{5,6},{6,5},{7,7},{8,8},{9,10},{10,9... | collective-permute-start | bytes 1720328 | tf_op jit(solution)/shard_map/ppermute | solution.py:12
  37.8 1.6 %broadcast.39.clone.1 = bf16[2240,512]{1,0:T(8,128)(2,1)} broadcast(bf16[]{:T(256)} %constant.11.clone.1), dimensions={} | broadcast | bytes 2293762 | tf_op jit(solution)/shard_map/broadcast.7
  40.3 1.6 %broadcast.39.clone = bf16[2240,512]{1,0:T(8,128)(2,1)} broadcast(bf16[]{:T(256)} %constant.11.clone.1), dimensions={} | broadcast | bytes 2293762 | tf_op jit(solution)/shard_map/broadcast.7
  42.8 1.9 %constant_dynamic-update-slice_fusion.2 = bf16[2240,512]{1,0:T(8,128)(2,1)} fusion(bf16[2240,512]{1,0:T(8,128)(2,1)} %constant_dynamic-update-slice_fusion.3, bf16[560,512]{1,0:T(8,128)(2,1)} %collective-permute-done, s32[]{:T(128)S(6)} %select_n.37), kind=kLoop, calls=%fused_computation.45 | loop fusion | bytes 1146884 | tf_op jit(solution)/shard_map/dynamic_update_slice | solution.py:31
  44.7 15.7 %collective-permute-start.14 = (bf16[560,512]{1,0:T(8,128)(2,1)}, bf16[560,512]{1,0:T(8,128)(2,1)S(1)}, u32[]{:S(2)}, u32[]{:S(2)}) collective-permute-start(bf16[560,512]{1,0:T(8,128)(2,1)} %collective-permute-done.11), channel_id=1, source_target_pairs={{0,1},{1,0},{2,3},{3,2},{4,5},{5,4},{6,7},{7,6},{8,9},{9,8},{10,11... | collective-permute-start | bytes 1720328 | tf_op jit(solution)/shard_map/ppermute | solution.py:12
  60.5 1.9 %constant_dynamic-update-slice_fusion = bf16[2240,512]{1,0:T(8,128)(2,1)} fusion(bf16[2240,512]{1,0:T(8,128)(2,1)} %constant_dynamic-update-slice_fusion.1, bf16[560,512]{1,0:T(8,128)(2,1)} %collective-permute-done.10, s32[]{:T(128)S(6)} %select_n.37), kind=kLoop, calls=%fused_computation.43 | loop fusion | bytes 1146884 | tf_op jit(solution)/shard_map/dynamic_update_slice | solution.py:31
  62.4 2.0 %select_dynamic-update-slice_fusion.3 = bf16[2240,512]{1,0:T(8,128)(2,1)} fusion(bf16[2240,512]{1,0:T(8,128)(2,1)} %constant_dynamic-update-slice_fusion.2, s32[]{:T(128)S(6)} %select_n.40, bf16[560,512]{1,0:T(8,128)(2,1)} %collective-permute-done.1, bf16[560,512]{1,0:T(8,128)(2,1)} %collective-permute-done.3, pred[]{:T(512)S(6)} %or.4), kind=kLoop, calls=%fused_computation.20 | loop fusion | flops 286720 | bytes 1720325 | tf_op jit(solution)/shard_map/dynamic_update_slice | solution.py:31
  64.4 2.0 %select_dynamic-update-slice_fusion.1 = bf16[2240,512]{1,0:T(8,128)(2,1)} fusion(bf16[2240,512]{1,0:T(8,128)(2,1)} %constant_dynamic-update-slice_fusion, s32[]{:T(128)S(6)} %select_n.40, bf16[560,512]{1,0:T(8,128)(2,1)} %collective-permute-done.11, bf16[560,512]{1,0:T(8,128)(2,1)} %collective-permute-done.13, pred[]{:T(512)S(6)} %or.4), kind=kLoop, calls=%fused_computation.18 | loop fusion | flops 286720 | bytes 1720325 | tf_op jit(solution)/shard_map/dynamic_update_slice | solution.py:31
  66.4 8.1 %collective-permute-done.14 = bf16[560,512]{1,0:T(8,128)(2,1)S(1)} collective-permute-done((bf16[560,512]{1,0:T(8,128)(2,1)}, bf16[560,512]{1,0:T(8,128)(2,1)S(1)}, u32[]{:S(2)}, u32[]{:S(2)}) %collective-permute-start.14) | collective-permute-done | bytes 573472 | tf_op jit(solution)/shard_map/ppermute | solution.py:12
  74.5 10.5 %collective-permute-done.4 = bf16[560,512]{1,0:T(8,128)(2,1)S(1)} collective-permute-done((bf16[560,512]{1,0:T(8,128)(2,1)}, bf16[560,512]{1,0:T(8,128)(2,1)S(1)}, u32[]{:S(2)}, u32[]{:S(2)}) %collective-permute-start.4) | collective-permute-done | bytes 573472 | tf_op jit(solution)/shard_map/ppermute | solution.py:12
  85.0 1.3 %select_dynamic-update-slice_fusion = (bf16[2240,512]{1,0:T(8,128)(2,1)}, bf16[2240,512]{1,0:T(8,128)(2,1)}) fusion(bf16[2240,512]{1,0:T(8,128)(2,1)} %select_dynamic-update-slice_fusion.1, s32[]{:T(128)S(6)} %select_n.42, bf16[560,512]{1,0:T(8,128)(2,1)} %collective-permute-done.12, bf16[560,512]{1,0:T(8,128)(2,1)S(1)} %collective-permute-done.14, ...), kind=kLoop, calls=%fused_computation.17 | loop fusion | flops 573440 | bytes 3440645 | tf_op jit(solution)/shard_map/dynamic_update_slice | solution.py:31
  86.4 3.3 %convolution_convert_fusion.2 = bf16[512,560]{0,1:T(8,128)(2,1)S(1)} fusion(bf16[2240,560]{0,1:T(8,128)(2,1)S(1)} %copy-done, bf16[2240,512]{1,0:T(8,128)(2,1)} %get-tuple-element.27), kind=kOutput, calls=%fused_computation.2 | convolution fusion | flops 1284792320 | bytes 5376000 | tf_op jit(solution)/shard_map/dot_general | solution.py:59
  89.7 3.1 %fusion.2 = bf16[512,560]{0,1:T(8,128)(2,1)S(1)} fusion(bf16[2240,560]{0,1:T(8,128)(2,1)S(1)} %copy-done.3, bf16[2240,512]{1,0:T(8,128)(2,1)} %get-tuple-element.27), kind=kOutput, calls=%fused_computation.8 | convolution fusion | flops 1285079040 | bytes 5376000 | tf_op jit(solution)/shard_map/dot_general | solution.py:59
  92.8 3.1 %convolution_convert_fusion.5 = bf16[512,560]{0,1:T(8,128)(2,1)S(1)} fusion(bf16[2240,560]{0,1:T(8,128)(2,1)S(1)} %copy-done, bf16[2240,512]{1,0:T(8,128)(2,1)} %get-tuple-element.28), kind=kOutput, calls=%fused_computation.5 | convolution fusion | flops 1284792320 | bytes 5376000 | tf_op jit(solution)/shard_map/dot_general | solution.py:59
  96.0 3.1 %fusion = bf16[512,560]{0,1:T(8,128)(2,1)S(1)} fusion(bf16[2240,560]{0,1:T(8,128)(2,1)S(1)} %copy-done.3, bf16[2240,512]{1,0:T(8,128)(2,1)} %get-tuple-element.28), kind=kOutput, calls=%fused_computation.6 | convolution fusion | flops 1285079040 | bytes 5376000 | tf_op jit(solution)/shard_map/dot_general | solution.py:59
  99.5 1.6 %collective-permute-start.15 = (bf16[280,112]{1,0:T(8,128)(2,1)S(1)}, bf16[280,112]{1,0:T(8,128)(2,1)S(1)}, u32[]{:S(2)}, u32[]{:S(2)}) collective-permute-start(bf16[280,112]{1,0:T(8,128)(2,1)S(1)} %get-tuple-element.13), channel_id=1, source_target_pairs={{0,4},{4,0},{8,12},{12,8},{1,5},{5,1},{9,13},{13,9},{2,6},{6,2},{1... | collective-permute-start | bytes 188168 | tf_op jit(solution)/shard_map/ppermute | solution.py:42
  101.0 1.5 %collective-permute-start.17 = (bf16[280,112]{1,0:T(8,128)(2,1)S(1)}, bf16[280,112]{1,0:T(8,128)(2,1)S(1)}, u32[]{:S(2)}, u32[]{:S(2)}) collective-permute-start(bf16[280,112]{1,0:T(8,128)(2,1)S(1)} %get-tuple-element.14), channel_id=1, source_target_pairs={{0,8},{4,12},{8,0},{12,4},{1,9},{5,13},{9,1},{13,5},{2,10},{6,14},... | collective-permute-start | bytes 188168 | tf_op jit(solution)/shard_map/ppermute | solution.py:42
  104.0 3.1 %fusion.3 = bf16[512,560]{0,1:T(8,128)(2,1)S(1)} fusion(bf16[2240,560]{0,1:T(8,128)(2,1)S(1)} %copy-done.4, bf16[2240,512]{1,0:T(8,128)(2,1)} %get-tuple-element.27), kind=kOutput, calls=%fused_computation.9 | convolution fusion | flops 1285079040 | bytes 5376000 | tf_op jit(solution)/shard_map/dot_general | solution.py:59
  108.8 1.5 %collective-permute-start.8 = (bf16[280,112]{1,0:T(8,128)(2,1)S(1)}, bf16[280,112]{1,0:T(8,128)(2,1)S(1)}, u32[]{:S(2)}, u32[]{:S(2)}) collective-permute-start(bf16[280,112]{1,0:T(8,128)(2,1)S(1)} %get-tuple-element.18), channel_id=1, source_target_pairs={{0,4},{4,0},{8,12},{12,8},{1,5},{5,1},{9,13},{13,9},{2,6},{6,2},{1... | collective-permute-start | bytes 188168 | tf_op jit(solution)/shard_map/ppermute | solution.py:42
  110.3 1.2 %collective-permute-start.16 = (bf16[280,112]{1,0:T(8,128)(2,1)S(1)}, bf16[280,112]{1,0:T(8,128)(2,1)S(1)}, u32[]{:S(2)}, u32[]{:S(2)}) collective-permute-start(bf16[280,112]{1,0:T(8,128)(2,1)S(1)} %get-tuple-element.11), channel_id=1, source_target_pairs={{0,8},{4,12},{8,0},{12,4},{1,9},{5,13},{9,1},{13,5},{2,10},{6,14},... | collective-permute-start | bytes 188168 | tf_op jit(solution)/shard_map/ppermute | solution.py:42
  111.5 1.0 collective-permute-start.18
  113.2 1.3 %collective-permute-start.9 = (f32[560,112]{1,0:T(8,128)S(1)}, f32[560,112]{1,0:T(8,128)S(1)}, u32[]{:S(2)}, u32[]{:S(2)}) collective-permute-start(f32[560,112]{1,0:T(8,128)S(1)} %pad_maximum_fusion), channel_id=1, source_target_pairs={{0,16},{1,17},{2,18},{3,19},{4,20},{5,21},{6,22},{7,23},{8,24},{9,... | collective-permute-start | bytes 752648 | tf_op jit(solution)/shard_map/ppermute | solution.py:50
  114.5 3.1 %fusion.1 = bf16[512,560]{0,1:T(8,128)(2,1)S(1)} fusion(bf16[2240,560]{0,1:T(8,128)(2,1)S(1)} %copy-done.4, bf16[2240,512]{1,0:T(8,128)(2,1)} %get-tuple-element.28), kind=kOutput, calls=%fused_computation.7 | convolution fusion | flops 1285079040 | bytes 5376000 | tf_op jit(solution)/shard_map/dot_general | solution.py:59
  118.7 1.1 maximum_bitcast_fusion
  (49 shorter events, 7.0 us)
Async XLA Ops:
  0.0 86.4 %copy-start = (bf16[2240,560]{0,1:T(8,128)(2,1)S(1)}, bf16[2240,560]{0,1:T(8,128)(2,1)}, u32[]{:S(2)}) copy-start(bf16[2240,560]{0,1:T(8,128)(2,1)} %param.8) | copy-start | bytes 7526404
  2.5 17.1 %collective-permute-start = (bf16[560,512]{1,0:T(8,128)(2,1)}, bf16[560,512]{1,0:T(8,128)(2,1)}, u32[]{:S(2)}, u32[]{:S(2)}) collective-permute-start(bf16[560,512]{1,0:T(8,128)(2,1)} %get-tuple-element.6), channel_id=1, source_target_pairs={{0,1},{1,0},{2,3},{3,2},{4,5},{5,4},{6,7},{7,6},{8,9},{9,8},{10,11... | collective-permute-start | bytes 1720328 | tf_op jit(solution)/shard_map/ppermute | solution.py:12
  5.5 20.0 %collective-permute-start.2 = (bf16[560,512]{1,0:T(8,128)(2,1)}, bf16[560,512]{1,0:T(8,128)(2,1)S(1)}, u32[]{:S(2)}, u32[]{:S(2)}) collective-permute-start(bf16[560,512]{1,0:T(8,128)(2,1)} %get-tuple-element.6), channel_id=1, source_target_pairs={{0,0},{1,2},{2,1},{3,3},{4,4},{5,6},{6,5},{7,7},{8,8},{9,10},{10,9... | collective-permute-start | bytes 1720328 | tf_op jit(solution)/shard_map/ppermute | solution.py:12
  7.2 24.7 %collective-permute-start.10 = (bf16[560,512]{1,0:T(8,128)(2,1)}, bf16[560,512]{1,0:T(8,128)(2,1)}, u32[]{:S(2)}, u32[]{:S(2)}) collective-permute-start(bf16[560,512]{1,0:T(8,128)(2,1)} %get-tuple-element.5), channel_id=1, source_target_pairs={{0,1},{1,0},{2,3},{3,2},{4,5},{5,4},{6,7},{7,6},{8,9},{9,8},{10,11... | collective-permute-start | bytes 1720328 | tf_op jit(solution)/shard_map/ppermute | solution.py:12
  10.6 29.6 %collective-permute-start.12 = (bf16[560,512]{1,0:T(8,128)(2,1)}, bf16[560,512]{1,0:T(8,128)(2,1)}, u32[]{:S(2)}, u32[]{:S(2)}) collective-permute-start(bf16[560,512]{1,0:T(8,128)(2,1)} %get-tuple-element.5), channel_id=1, source_target_pairs={{0,0},{1,2},{2,1},{3,3},{4,4},{5,6},{6,5},{7,7},{8,8},{9,10},{10,9... | collective-permute-start | bytes 1720328 | tf_op jit(solution)/shard_map/ppermute | solution.py:12
  16.6 22.9 %copy-start.1 = (bf16[2,512,560]{1,2,0:T(8,128)(2,1)S(1)}, bf16[2,512,560]{1,2,0:T(8,128)(2,1)}, u32[]{:S(2)}) copy-start(bf16[2,512,560]{1,2,0:T(8,128)(2,1)} %param.5) | copy-start | bytes 3440644
  19.6 40.8 %collective-permute-start.1 = (bf16[560,512]{1,0:T(8,128)(2,1)}, bf16[560,512]{1,0:T(8,128)(2,1)}, u32[]{:S(2)}, u32[]{:S(2)}) collective-permute-start(bf16[560,512]{1,0:T(8,128)(2,1)} %collective-permute-done), channel_id=1, source_target_pairs={{0,0},{1,2},{2,1},{3,3},{4,4},{5,6},{6,5},{7,7},{8,8},{9,10},{10,9... | collective-permute-start | bytes 1720328 | tf_op jit(solution)/shard_map/ppermute | solution.py:12
  25.5 36.9 %collective-permute-start.3 = (bf16[560,512]{1,0:T(8,128)(2,1)S(1)}, bf16[560,512]{1,0:T(8,128)(2,1)}, u32[]{:S(2)}, u32[]{:S(2)}) collective-permute-start(bf16[560,512]{1,0:T(8,128)(2,1)S(1)} %collective-permute-done.2), channel_id=1, source_target_pairs={{0,1},{1,0},{2,3},{3,2},{4,5},{5,4},{6,7},{7,6},{8,9},{9,8},{10,11... | collective-permute-start | bytes 1720328 | tf_op jit(solution)/shard_map/ppermute | solution.py:12
  31.9 12.8 %collective-permute-start.11 = (bf16[560,512]{1,0:T(8,128)(2,1)}, bf16[560,512]{1,0:T(8,128)(2,1)}, u32[]{:S(2)}, u32[]{:S(2)}) collective-permute-start(bf16[560,512]{1,0:T(8,128)(2,1)} %collective-permute-done.10), channel_id=1, source_target_pairs={{0,0},{1,2},{2,1},{3,3},{4,4},{5,6},{6,5},{7,7},{8,8},{9,10},{10,9... | collective-permute-start | bytes 1720328 | tf_op jit(solution)/shard_map/ppermute | solution.py:12
  39.4 3.3 %copy-start.2 = (f32[560]{0:T(1024)S(1)}, f32[560]{0:T(1024)}, u32[]{:S(2)}) copy-start(f32[560]{0:T(1024)} %param.9) | copy-start | bytes 6724
  40.3 24.1 %collective-permute-start.13 = (bf16[560,512]{1,0:T(8,128)(2,1)}, bf16[560,512]{1,0:T(8,128)(2,1)}, u32[]{:S(2)}, u32[]{:S(2)}) collective-permute-start(bf16[560,512]{1,0:T(8,128)(2,1)} %collective-permute-done.12), channel_id=1, source_target_pairs={{0,1},{1,0},{2,3},{3,2},{4,5},{5,4},{6,7},{7,6},{8,9},{9,8},{10,11... | collective-permute-start | bytes 1720328 | tf_op jit(solution)/shard_map/ppermute | solution.py:12
  44.7 29.8 %collective-permute-start.14 = (bf16[560,512]{1,0:T(8,128)(2,1)}, bf16[560,512]{1,0:T(8,128)(2,1)S(1)}, u32[]{:S(2)}, u32[]{:S(2)}) collective-permute-start(bf16[560,512]{1,0:T(8,128)(2,1)} %collective-permute-done.11), channel_id=1, source_target_pairs={{0,1},{1,0},{2,3},{3,2},{4,5},{5,4},{6,7},{7,6},{8,9},{9,8},{10,11... | collective-permute-start | bytes 1720328 | tf_op jit(solution)/shard_map/ppermute | solution.py:12
  60.4 24.6 %collective-permute-start.4 = (bf16[560,512]{1,0:T(8,128)(2,1)}, bf16[560,512]{1,0:T(8,128)(2,1)S(1)}, u32[]{:S(2)}, u32[]{:S(2)}) collective-permute-start(bf16[560,512]{1,0:T(8,128)(2,1)} %collective-permute-done.1), channel_id=1, source_target_pairs={{0,1},{1,0},{2,3},{3,2},{4,5},{5,4},{6,7},{7,6},{8,9},{9,8},{10,11... | collective-permute-start | bytes 1720328 | tf_op jit(solution)/shard_map/ppermute | solution.py:12
  86.4 3.3 %copy-start.3 = (bf16[2240,560]{0,1:T(8,128)(2,1)S(1)}, bf16[2240,560]{0,1:T(8,128)(2,1)}, u32[]{:S(2)}) copy-start(bf16[2240,560]{0,1:T(8,128)(2,1)} %param.7) | copy-start | bytes 7526404
  99.1 4.9 %copy-start.4 = (bf16[2240,560]{0,1:T(8,128)(2,1)S(1)}, bf16[2240,560]{0,1:T(8,128)(2,1)}, u32[]{:S(2)}) copy-start(bf16[2240,560]{0,1:T(8,128)(2,1)} %param.6) | copy-start | bytes 7526404
  99.5 10.8 %collective-permute-start.15 = (bf16[280,112]{1,0:T(8,128)(2,1)S(1)}, bf16[280,112]{1,0:T(8,128)(2,1)S(1)}, u32[]{:S(2)}, u32[]{:S(2)}) collective-permute-start(bf16[280,112]{1,0:T(8,128)(2,1)S(1)} %get-tuple-element.13), channel_id=1, source_target_pairs={{0,4},{4,0},{8,12},{12,8},{1,5},{5,1},{9,13},{13,9},{2,6},{6,2},{1... | collective-permute-start | bytes 188168 | tf_op jit(solution)/shard_map/ppermute | solution.py:42
  101.0 9.3 %collective-permute-start.17 = (bf16[280,112]{1,0:T(8,128)(2,1)S(1)}, bf16[280,112]{1,0:T(8,128)(2,1)S(1)}, u32[]{:S(2)}, u32[]{:S(2)}) collective-permute-start(bf16[280,112]{1,0:T(8,128)(2,1)S(1)} %get-tuple-element.14), channel_id=1, source_target_pairs={{0,8},{4,12},{8,0},{12,4},{1,9},{5,13},{9,1},{13,5},{2,10},{6,14},... | collective-permute-start | bytes 188168 | tf_op jit(solution)/shard_map/ppermute | solution.py:42
  102.9 4.4 %collective-permute-start.5 = (bf16[280,112]{1,0:T(8,128)(2,1)S(1)}, bf16[280,112]{1,0:T(8,128)(2,1)S(1)}, u32[]{:S(2)}, u32[]{:S(2)}) collective-permute-start(bf16[280,112]{1,0:T(8,128)(2,1)S(1)} %get-tuple-element.19), channel_id=1, source_target_pairs={{0,4},{4,0},{8,12},{12,8},{1,5},{5,1},{9,13},{13,9},{2,6},{6,2},{1... | collective-permute-start | bytes 188168 | tf_op jit(solution)/shard_map/ppermute | solution.py:42
  103.5 4.8 %collective-permute-start.7 = (bf16[280,112]{1,0:T(8,128)(2,1)S(1)}, bf16[280,112]{1,0:T(8,128)(2,1)S(1)}, u32[]{:S(2)}, u32[]{:S(2)}) collective-permute-start(bf16[280,112]{1,0:T(8,128)(2,1)S(1)} %get-tuple-element.20), channel_id=1, source_target_pairs={{0,8},{4,12},{8,0},{12,4},{1,9},{5,13},{9,1},{13,5},{2,10},{6,14},... | collective-permute-start | bytes 188168 | tf_op jit(solution)/shard_map/ppermute | solution.py:42
  108.3 4.4 %collective-permute-start.6 = (bf16[280,112]{1,0:T(8,128)(2,1)S(1)}, bf16[280,112]{1,0:T(8,128)(2,1)S(1)}, u32[]{:S(2)}, u32[]{:S(2)}) collective-permute-start(bf16[280,112]{1,0:T(8,128)(2,1)S(1)} %get-tuple-element.17), channel_id=1, source_target_pairs={{0,8},{4,12},{8,0},{12,4},{1,9},{5,13},{9,1},{13,5},{2,10},{6,14},... | collective-permute-start | bytes 188168 | tf_op jit(solution)/shard_map/ppermute | solution.py:42
  108.8 4.3 %collective-permute-start.8 = (bf16[280,112]{1,0:T(8,128)(2,1)S(1)}, bf16[280,112]{1,0:T(8,128)(2,1)S(1)}, u32[]{:S(2)}, u32[]{:S(2)}) collective-permute-start(bf16[280,112]{1,0:T(8,128)(2,1)S(1)} %get-tuple-element.18), channel_id=1, source_target_pairs={{0,4},{4,0},{8,12},{12,8},{1,5},{5,1},{9,13},{13,9},{2,6},{6,2},{1... | collective-permute-start | bytes 188168 | tf_op jit(solution)/shard_map/ppermute | solution.py:42
  110.3 7.3 %collective-permute-start.16 = (bf16[280,112]{1,0:T(8,128)(2,1)S(1)}, bf16[280,112]{1,0:T(8,128)(2,1)S(1)}, u32[]{:S(2)}, u32[]{:S(2)}) collective-permute-start(bf16[280,112]{1,0:T(8,128)(2,1)S(1)} %get-tuple-element.11), channel_id=1, source_target_pairs={{0,8},{4,12},{8,0},{12,4},{1,9},{5,13},{9,1},{13,5},{2,10},{6,14},... | collective-permute-start | bytes 188168 | tf_op jit(solution)/shard_map/ppermute | solution.py:42
  111.5 6.1 %collective-permute-start.18 = (bf16[280,112]{1,0:T(8,128)(2,1)S(1)}, bf16[280,112]{1,0:T(8,128)(2,1)S(1)}, u32[]{:S(2)}, u32[]{:S(2)}) collective-permute-start(bf16[280,112]{1,0:T(8,128)(2,1)S(1)} %get-tuple-element.12), channel_id=1, source_target_pairs={{0,4},{4,0},{8,12},{12,8},{1,5},{5,1},{9,13},{13,9},{2,6},{6,2},{1... | collective-permute-start | bytes 188168 | tf_op jit(solution)/shard_map/ppermute | solution.py:42
  113.2 4.5 %collective-permute-start.9 = (f32[560,112]{1,0:T(8,128)S(1)}, f32[560,112]{1,0:T(8,128)S(1)}, u32[]{:S(2)}, u32[]{:S(2)}) collective-permute-start(f32[560,112]{1,0:T(8,128)S(1)} %pad_maximum_fusion), channel_id=1, source_target_pairs={{0,16},{1,17},{2,18},{3,19},{4,20},{5,21},{6,22},{7,23},{8,24},{9,... | collective-permute-start | bytes 752648 | tf_op jit(solution)/shard_map/ppermute | solution.py:50

commit v3 on v2

--- a/solution.py
+++ b/solution.py
@@ -6,22 +6,31 @@
 HEAD_DIM = 112
 
 
-def swap(value, axis, pairs):
-    ends = dict(pairs) | {j: i for i, j in pairs}
-    count = lax.axis_size(axis)
-    return lax.ppermute(value, axis, [(i, ends.get(i, i)) for i in range(count)])
+def partner_swap(value, axis):
+    return lax.ppermute(value, axis, [(i, i ^ 1) for i in range(lax.axis_size(axis))])
 
 
-def gather_blocks(block, axis):
+def middle_swap(value, axis, other):
+    wide, count = lax.axis_size(other), lax.axis_size(axis)
+    pairs = []
+    for j in range(wide):
+        for i in range(count):
+            if i in (1, 2):
+                pairs.append((j * count + i, j * count + 3 - i))
+            else:
+                pairs.append((j * count + i, (j ^ 1 if j ^ 1 < wide else j) * count + i))
+    return lax.ppermute(value, (other, axis), pairs)
+
+
+def gather_blocks(block, axis, other):
     count, mine = lax.axis_size(axis), lax.axis_index(axis)
     if count != 4:
         return lax.all_gather(block, axis, axis=0, tiled=True)
-    partners, middle = [(0, 1), (2, 3)], [(1, 2)]
-    near = swap(block, axis, partners)
-    across = swap(block, axis, middle)
-    far = swap(near, axis, middle)
-    across_end = swap(across, axis, partners)
-    far_end = swap(far, axis, partners)
+    near = partner_swap(block, axis)
+    across = middle_swap(block, axis, other)
+    far = middle_swap(near, axis, other)
+    across_end = partner_swap(across, axis)
+    far_end = partner_swap(far, axis)
     inner = (mine == 1) | (mine == 2)
     second = jnp.where(inner, far, across_end)
     third = jnp.where(inner, across, far_end)
@@ -68,7 +77,7 @@
     gain_heads = gain.reshape(heads, HEAD_DIM, 1)
     prefix, results = None, []
     for stream in range(2):
-        features = gather_blocks(columns[stream], "head")
+        features = gather_blocks(columns[stream], "head", "group")
         key = jnp.maximum(project(w_key, features), 0).reshape(heads, HEAD_DIM, tokens)
         value = project(w_value, features).reshape(heads, HEAD_DIM, tokens)
         query = jnp.maximum(project(w_query, features), 0).reshape(heads, HEAD_DIM, tokens)

time: 121 us -> 118 us (0.975)
  starting transfers between devices: 51.3 us -> 39.3 us
  waiting for transfers between devices: 29.8 us -> 39.9 us
    ppermute x10, starting transfers between devices: 41.6 us -> 29.6 us  [the longest x6 29.6 us: partner_swap(): lax.ppermute(value, axis, [(i, i ^ 1) for i in range(lax.axis_size(axis))])]
    ppermute x10, waiting for transfers between devices: 28.1 us -> 38.2 us  [the longest x6 38.2 us: partner_swap(): lax.ppermute(value, axis, [(i, i ^ 1) for i in range(lax.axis_size(axis))])]
  transfers between devices with their start and end apart: 19 -> 19, of which waited for: 8 -> 8; matrix products, arithmetic and copies ran while one was open for 16% -> 17% of each run, Pallas kernels for 0% -> 0%
where the time goes in v3:
time: 118 us
  waiting for transfers between devices  39.9 us (34%)
  starting transfers between devices  39.3 us (33%)
  matrix products  20.2 us (17%)
  local copies, waits for them, and re-layouts  11.3 us (10%)
  other arithmetic  7.05 us (6%)
    ppermute x6, waiting for transfers between devices, partner_swap(): lax.ppermute(value, axis, [(i, i ^ 1) for i in range(lax.axis_size(axis))])  38.2 us
    ppermute x6, starting transfers between devices, partner_swap(): lax.ppermute(value, axis, [(i, i ^ 1) for i in range(lax.axis_size(axis))])  29.6 us
    dot_general x6, matrix products, project(): jnp.dot(matrix, block, preferred_element_type=jnp.float32)  19 us
    ppermute x8, starting transfers between devices, sum_over(): lax.ppermute(part.astype(jnp.bfloat16), axis, [(i, i ^ step) for i in ran...  8.39 us
    dynamic_update_slice x4, local copies, waits for them, and re-layouts, gather_blocks(): lax.dynamic_update_slice_in_dim(whole, piece, (mine ^ flip) * rows, 0)  5.55 us
    dynamic_update_slice x3, other arithmetic, gather_blocks(): lax.dynamic_update_slice_in_dim(whole, piece, (mine ^ flip) * rows, 0)  5.39 us
    another operation x2, local copies, waits for them, and re-layouts  3.15 us
    squeeze x1, local copies, waits for them, and re-layouts, local(): features = gather_blocks(columns[stream], 'head', 'group')  2.48 us
  transfers between devices with their start and end apart: 19, of which 8 were waited for; matrix products, arithmetic and copies ran while one was open for 17% of the time, Pallas kernels for 0%

profile of v3, /device:TPU:0, one launch (start us, length us, event | category | flops | bytes accessed | tf_op | source)
XLA Modules:
  0.0 118.0 jit_solution(2155740641619856983)
XLA Ops:
  0.0 2.5 %slice_bitcast_fusion = (bf16[560,512]{1,0:T(8,128)(2,1)}, bf16[560,512]{1,0:T(8,128)(2,1)}) fusion(bf16[2,560,512]{2,1,0:T(8,128)(2,1)} %bitcast.55), kind=kLoop, calls=%fused_computation.15 | loop fusion | bytes 2293760 | tf_op jit(solution)/shard_map/squeeze | solution.py:80
  2.5 3.0 %collective-permute-start = (bf16[560,512]{1,0:T(8,128)(2,1)}, bf16[560,512]{1,0:T(8,128)(2,1)}, u32[]{:S(2)}, u32[]{:S(2)}) collective-permute-start(bf16[560,512]{1,0:T(8,128)(2,1)} %get-tuple-element.6), channel_id=1, source_target_pairs={{0,1},{1,0},{2,3},{3,2},{4,5},{5,4},{6,7},{7,6},{8,9},{9,8},{10,11... | collective-permute-start | bytes 1720328 | tf_op jit(solution)/shard_map/ppermute | solution.py:10
  5.5 3.1 %collective-permute-start.10 = (bf16[560,512]{1,0:T(8,128)(2,1)}, bf16[560,512]{1,0:T(8,128)(2,1)}, u32[]{:S(2)}, u32[]{:S(2)}) collective-permute-start(bf16[560,512]{1,0:T(8,128)(2,1)} %get-tuple-element.5), channel_id=1, source_target_pairs={{0,1},{1,0},{2,3},{3,2},{4,5},{5,4},{6,7},{7,6},{8,9},{9,8},{10,11... | collective-permute-start | bytes 1720328 | tf_op jit(solution)/shard_map/ppermute | solution.py:10
  8.7 11.0 %collective-permute-done = bf16[560,512]{1,0:T(8,128)(2,1)} collective-permute-done((bf16[560,512]{1,0:T(8,128)(2,1)}, bf16[560,512]{1,0:T(8,128)(2,1)}, u32[]{:S(2)}, u32[]{:S(2)}) %collective-permute-start) | collective-permute-done | bytes 573472 | tf_op jit(solution)/shard_map/ppermute | solution.py:10
  19.6 3.6 %collective-permute-start.3 = (bf16[560,512]{1,0:T(8,128)(2,1)S(1)}, bf16[560,512]{1,0:T(8,128)(2,1)}, u32[]{:S(2)}, u32[]{:S(2)}) collective-permute-start(bf16[560,512]{1,0:T(8,128)(2,1)S(1)} %collective-permute-done.2), channel_id=1, source_target_pairs={{0,1},{1,0},{2,3},{3,2},{4,5},{5,4},{6,7},{7,6},{8,9},{9,8},{10,11... | collective-permute-start | bytes 1720328 | tf_op jit(solution)/shard_map/ppermute | solution.py:10
  23.3 8.6 %collective-permute-done.10 = bf16[560,512]{1,0:T(8,128)(2,1)} collective-permute-done((bf16[560,512]{1,0:T(8,128)(2,1)}, bf16[560,512]{1,0:T(8,128)(2,1)}, u32[]{:S(2)}, u32[]{:S(2)}) %collective-permute-start.10) | collective-permute-done | bytes 573472 | tf_op jit(solution)/shard_map/ppermute | solution.py:10
  31.9 1.6 %broadcast.39.clone.1 = bf16[2240,512]{1,0:T(8,128)(2,1)} broadcast(bf16[]{:T(256)} %constant.11.clone.1), dimensions={} | broadcast | bytes 2293762 | tf_op jit(solution)/shard_map/broadcast.7
  34.4 3.6 %collective-permute-start.13 = (bf16[560,512]{1,0:T(8,128)(2,1)}, bf16[560,512]{1,0:T(8,128)(2,1)}, u32[]{:S(2)}, u32[]{:S(2)}) collective-permute-start(bf16[560,512]{1,0:T(8,128)(2,1)} %collective-permute-done.12), channel_id=1, source_target_pairs={{0,1},{1,0},{2,3},{3,2},{4,5},{5,4},{6,7},{7,6},{8,9},{9,8},{10,11... | collective-permute-start | bytes 1720328 | tf_op jit(solution)/shard_map/ppermute | solution.py:10
  38.0 1.6 %broadcast.39.clone = bf16[2240,512]{1,0:T(8,128)(2,1)} broadcast(bf16[]{:T(256)} %constant.11.clone.1), dimensions={} | broadcast | bytes 2293762 | tf_op jit(solution)/shard_map/broadcast.7
  39.6 0.9 constant_dynamic-update-slice_fusion.1
  40.5 1.9 %constant_dynamic-update-slice_fusion.2 = bf16[2240,512]{1,0:T(8,128)(2,1)} fusion(bf16[2240,512]{1,0:T(8,128)(2,1)} %constant_dynamic-update-slice_fusion.3, bf16[560,512]{1,0:T(8,128)(2,1)} %collective-permute-done, s32[]{:T(128)S(6)} %select_n.37), kind=kLoop, calls=%fused_computation.45 | loop fusion | bytes 1146884 | tf_op jit(solution)/shard_map/dynamic_update_slice | solution.py:40
  42.4 16.2 %collective-permute-start.14 = (bf16[560,512]{1,0:T(8,128)(2,1)}, bf16[560,512]{1,0:T(8,128)(2,1)S(1)}, u32[]{:S(2)}, u32[]{:S(2)}) collective-permute-start(bf16[560,512]{1,0:T(8,128)(2,1)} %collective-permute-done.11), channel_id=1, source_target_pairs={{0,1},{1,0},{2,3},{3,2},{4,5},{5,4},{6,7},{7,6},{8,9},{9,8},{10,11... | collective-permute-start | bytes 1720328 | tf_op jit(solution)/shard_map/ppermute | solution.py:10
  58.6 1.9 %constant_dynamic-update-slice_fusion = bf16[2240,512]{1,0:T(8,128)(2,1)} fusion(bf16[2240,512]{1,0:T(8,128)(2,1)} %constant_dynamic-update-slice_fusion.1, bf16[560,512]{1,0:T(8,128)(2,1)} %collective-permute-done.10, s32[]{:T(128)S(6)} %select_n.37), kind=kLoop, calls=%fused_computation.43 | loop fusion | bytes 1146884 | tf_op jit(solution)/shard_map/dynamic_update_slice | solution.py:40
  60.5 2.0 %select_dynamic-update-slice_fusion.3 = bf16[2240,512]{1,0:T(8,128)(2,1)} fusion(bf16[2240,512]{1,0:T(8,128)(2,1)} %constant_dynamic-update-slice_fusion.2, s32[]{:T(128)S(6)} %select_n.40, bf16[560,512]{1,0:T(8,128)(2,1)} %collective-permute-done.1, bf16[560,512]{1,0:T(8,128)(2,1)} %collective-permute-done.3, pred[]{:T(512)S(6)} %or.4), kind=kLoop, calls=%fused_computation.20 | loop fusion | flops 286720 | bytes 1720325 | tf_op jit(solution)/shard_map/dynamic_update_slice | solution.py:40
  62.6 2.0 %select_dynamic-update-slice_fusion.1 = bf16[2240,512]{1,0:T(8,128)(2,1)} fusion(bf16[2240,512]{1,0:T(8,128)(2,1)} %constant_dynamic-update-slice_fusion, s32[]{:T(128)S(6)} %select_n.40, bf16[560,512]{1,0:T(8,128)(2,1)} %collective-permute-done.11, bf16[560,512]{1,0:T(8,128)(2,1)} %collective-permute-done.13, pred[]{:T(512)S(6)} %or.4), kind=kLoop, calls=%fused_computation.18 | loop fusion | flops 286720 | bytes 1720325 | tf_op jit(solution)/shard_map/dynamic_update_slice | solution.py:40
  64.6 8.1 %collective-permute-done.14 = bf16[560,512]{1,0:T(8,128)(2,1)S(1)} collective-permute-done((bf16[560,512]{1,0:T(8,128)(2,1)}, bf16[560,512]{1,0:T(8,128)(2,1)S(1)}, u32[]{:S(2)}, u32[]{:S(2)}) %collective-permute-start.14) | collective-permute-done | bytes 573472 | tf_op jit(solution)/shard_map/ppermute | solution.py:10
  72.7 10.5 %collective-permute-done.4 = bf16[560,512]{1,0:T(8,128)(2,1)S(1)} collective-permute-done((bf16[560,512]{1,0:T(8,128)(2,1)}, bf16[560,512]{1,0:T(8,128)(2,1)S(1)}, u32[]{:S(2)}, u32[]{:S(2)}) %collective-permute-start.4) | collective-permute-done | bytes 573472 | tf_op jit(solution)/shard_map/ppermute | solution.py:10
  83.2 1.3 %select_dynamic-update-slice_fusion = (bf16[2240,512]{1,0:T(8,128)(2,1)}, bf16[2240,512]{1,0:T(8,128)(2,1)}) fusion(bf16[2240,512]{1,0:T(8,128)(2,1)} %select_dynamic-update-slice_fusion.1, s32[]{:T(128)S(6)} %select_n.42, bf16[560,512]{1,0:T(8,128)(2,1)} %collective-permute-done.12, bf16[560,512]{1,0:T(8,128)(2,1)S(1)} %collective-permute-done.14, ...), kind=kLoop, calls=%fused_computation.17 | loop fusion | flops 573440 | bytes 3440645 | tf_op jit(solution)/shard_map/dynamic_update_slice | solution.py:40
  84.5 3.3 %convolution_convert_fusion.2 = bf16[512,560]{0,1:T(8,128)(2,1)S(1)} fusion(bf16[2240,560]{0,1:T(8,128)(2,1)S(1)} %copy-done, bf16[2240,512]{1,0:T(8,128)(2,1)} %get-tuple-element.27), kind=kOutput, calls=%fused_computation.2 | convolution fusion | flops 1284792320 | bytes 5376000 | tf_op jit(solution)/shard_map/dot_general | solution.py:68
  87.8 3.1 %fusion.2 = bf16[512,560]{0,1:T(8,128)(2,1)S(1)} fusion(bf16[2240,560]{0,1:T(8,128)(2,1)S(1)} %copy-done.3, bf16[2240,512]{1,0:T(8,128)(2,1)} %get-tuple-element.27), kind=kOutput, calls=%fused_computation.8 | convolution fusion | flops 1285079040 | bytes 5376000 | tf_op jit(solution)/shard_map/dot_general | solution.py:68
  91.0 3.1 %convolution_convert_fusion.5 = bf16[512,560]{0,1:T(8,128)(2,1)S(1)} fusion(bf16[2240,560]{0,1:T(8,128)(2,1)S(1)} %copy-done, bf16[2240,512]{1,0:T(8,128)(2,1)} %get-tuple-element.28), kind=kOutput, calls=%fused_computation.5 | convolution fusion | flops 1284792320 | bytes 5376000 | tf_op jit(solution)/shard_map/dot_general | solution.py:68
  94.1 3.1 %fusion = bf16[512,560]{0,1:T(8,128)(2,1)S(1)} fusion(bf16[2240,560]{0,1:T(8,128)(2,1)S(1)} %copy-done.3, bf16[2240,512]{1,0:T(8,128)(2,1)} %get-tuple-element.28), kind=kOutput, calls=%fused_computation.6 | convolution fusion | flops 1285079040 | bytes 5376000 | tf_op jit(solution)/shard_map/dot_general | solution.py:68
  97.6 1.6 %collective-permute-start.15 = (bf16[280,112]{1,0:T(8,128)(2,1)S(1)}, bf16[280,112]{1,0:T(8,128)(2,1)S(1)}, u32[]{:S(2)}, u32[]{:S(2)}) collective-permute-start(bf16[280,112]{1,0:T(8,128)(2,1)S(1)} %get-tuple-element.13), channel_id=1, source_target_pairs={{0,4},{4,0},{8,12},{12,8},{1,5},{5,1},{9,13},{13,9},{2,6},{6,2},{1... | collective-permute-start | bytes 188168 | tf_op jit(solution)/shard_map/ppermute | solution.py:51
  99.2 1.5 %collective-permute-start.17 = (bf16[280,112]{1,0:T(8,128)(2,1)S(1)}, bf16[280,112]{1,0:T(8,128)(2,1)S(1)}, u32[]{:S(2)}, u32[]{:S(2)}) collective-permute-start(bf16[280,112]{1,0:T(8,128)(2,1)S(1)} %get-tuple-element.14), channel_id=1, source_target_pairs={{0,8},{4,12},{8,0},{12,4},{1,9},{5,13},{9,1},{13,5},{2,10},{6,14},... | collective-permute-start | bytes 188168 | tf_op jit(solution)/shard_map/ppermute | solution.py:51
  102.2 3.1 %fusion.3 = bf16[512,560]{0,1:T(8,128)(2,1)S(1)} fusion(bf16[2240,560]{0,1:T(8,128)(2,1)S(1)} %copy-done.4, bf16[2240,512]{1,0:T(8,128)(2,1)} %get-tuple-element.27), kind=kOutput, calls=%fused_computation.9 | convolution fusion | flops 1285079040 | bytes 5376000 | tf_op jit(solution)/shard_map/dot_general | solution.py:68
  105.4 1.0 collective-permute-done.7
  106.9 1.5 %collective-permute-start.8 = (bf16[280,112]{1,0:T(8,128)(2,1)S(1)}, bf16[280,112]{1,0:T(8,128)(2,1)S(1)}, u32[]{:S(2)}, u32[]{:S(2)}) collective-permute-start(bf16[280,112]{1,0:T(8,128)(2,1)S(1)} %get-tuple-element.18), channel_id=1, source_target_pairs={{0,4},{4,0},{8,12},{12,8},{1,5},{5,1},{9,13},{13,9},{2,6},{6,2},{1... | collective-permute-start | bytes 188168 | tf_op jit(solution)/shard_map/ppermute | solution.py:51
  108.5 1.2 %collective-permute-start.16 = (bf16[280,112]{1,0:T(8,128)(2,1)S(1)}, bf16[280,112]{1,0:T(8,128)(2,1)S(1)}, u32[]{:S(2)}, u32[]{:S(2)}) collective-permute-start(bf16[280,112]{1,0:T(8,128)(2,1)S(1)} %get-tuple-element.11), channel_id=1, source_target_pairs={{0,8},{4,12},{8,0},{12,4},{1,9},{5,13},{9,1},{13,5},{2,10},{6,14},... | collective-permute-start | bytes 188168 | tf_op jit(solution)/shard_map/ppermute | solution.py:51
  109.7 1.0 collective-permute-start.18
  111.3 1.3 %collective-permute-start.9 = (f32[560,112]{1,0:T(8,128)S(1)}, f32[560,112]{1,0:T(8,128)S(1)}, u32[]{:S(2)}, u32[]{:S(2)}) collective-permute-start(f32[560,112]{1,0:T(8,128)S(1)} %pad_maximum_fusion), channel_id=1, source_target_pairs={{0,16},{1,17},{2,18},{3,19},{4,20},{5,21},{6,22},{7,23},{8,24},{9,... | collective-permute-start | bytes 752648 | tf_op jit(solution)/shard_map/ppermute | solution.py:59
  112.7 3.1 %fusion.1 = bf16[512,560]{0,1:T(8,128)(2,1)S(1)} fusion(bf16[2240,560]{0,1:T(8,128)(2,1)S(1)} %copy-done.4, bf16[2240,512]{1,0:T(8,128)(2,1)} %get-tuple-element.28), kind=kOutput, calls=%fused_computation.7 | convolution fusion | flops 1285079040 | bytes 5376000 | tf_op jit(solution)/shard_map/dot_general | solution.py:68
  116.9 1.1 maximum_bitcast_fusion
  (49 shorter events, 5.1 us)
Async XLA Ops:
  0.0 84.5 %copy-start = (bf16[2240,560]{0,1:T(8,128)(2,1)S(1)}, bf16[2240,560]{0,1:T(8,128)(2,1)}, u32[]{:S(2)}) copy-start(bf16[2240,560]{0,1:T(8,128)(2,1)} %param.8) | copy-start | bytes 7526404
  2.5 17.1 %collective-permute-start = (bf16[560,512]{1,0:T(8,128)(2,1)}, bf16[560,512]{1,0:T(8,128)(2,1)}, u32[]{:S(2)}, u32[]{:S(2)}) collective-permute-start(bf16[560,512]{1,0:T(8,128)(2,1)} %get-tuple-element.6), channel_id=1, source_target_pairs={{0,1},{1,0},{2,3},{3,2},{4,5},{5,4},{6,7},{7,6},{8,9},{9,8},{10,11... | collective-permute-start | bytes 1720328 | tf_op jit(solution)/shard_map/ppermute | solution.py:10
  5.5 14.1 %collective-permute-start.2 = (bf16[560,512]{1,0:T(8,128)(2,1)}, bf16[560,512]{1,0:T(8,128)(2,1)S(1)}, u32[]{:S(2)}, u32[]{:S(2)}) collective-permute-start(bf16[560,512]{1,0:T(8,128)(2,1)} %get-tuple-element.6), channel_id=1, source_target_pairs={{0,16},{1,2},{2,1},{3,19},{16,0},{17,18},{18,17},{19,3},{4,20},{5,... | collective-permute-start | bytes 1720328 | tf_op jit(solution)/shard_map/ppermute | solution.py:22
  5.5 26.4 %collective-permute-start.10 = (bf16[560,512]{1,0:T(8,128)(2,1)}, bf16[560,512]{1,0:T(8,128)(2,1)}, u32[]{:S(2)}, u32[]{:S(2)}) collective-permute-start(bf16[560,512]{1,0:T(8,128)(2,1)} %get-tuple-element.5), channel_id=1, source_target_pairs={{0,1},{1,0},{2,3},{3,2},{4,5},{5,4},{6,7},{7,6},{8,9},{9,8},{10,11... | collective-permute-start | bytes 1720328 | tf_op jit(solution)/shard_map/ppermute | solution.py:10
  8.7 25.7 %collective-permute-start.12 = (bf16[560,512]{1,0:T(8,128)(2,1)}, bf16[560,512]{1,0:T(8,128)(2,1)}, u32[]{:S(2)}, u32[]{:S(2)}) collective-permute-start(bf16[560,512]{1,0:T(8,128)(2,1)} %get-tuple-element.5), channel_id=1, source_target_pairs={{0,16},{1,2},{2,1},{3,19},{16,0},{17,18},{18,17},{19,3},{4,20},{5,... | collective-permute-start | bytes 1720328 | tf_op jit(solution)/shard_map/ppermute | solution.py:22
  8.7 24.8 %copy-start.1 = (bf16[2,512,560]{1,2,0:T(8,128)(2,1)S(1)}, bf16[2,512,560]{1,2,0:T(8,128)(2,1)}, u32[]{:S(2)}) copy-start(bf16[2,512,560]{1,2,0:T(8,128)(2,1)} %param.5) | copy-start | bytes 3440644
  19.6 38.9 %collective-permute-start.1 = (bf16[560,512]{1,0:T(8,128)(2,1)}, bf16[560,512]{1,0:T(8,128)(2,1)}, u32[]{:S(2)}, u32[]{:S(2)}) collective-permute-start(bf16[560,512]{1,0:T(8,128)(2,1)} %collective-permute-done), channel_id=1, source_target_pairs={{0,16},{1,2},{2,1},{3,19},{16,0},{17,18},{18,17},{19,3},{4,20},{5,... | collective-permute-start | bytes 1720328 | tf_op jit(solution)/shard_map/ppermute | solution.py:22
  19.6 40.9 %collective-permute-start.3 = (bf16[560,512]{1,0:T(8,128)(2,1)S(1)}, bf16[560,512]{1,0:T(8,128)(2,1)}, u32[]{:S(2)}, u32[]{:S(2)}) collective-permute-start(bf16[560,512]{1,0:T(8,128)(2,1)S(1)} %collective-permute-done.2), channel_id=1, source_target_pairs={{0,1},{1,0},{2,3},{3,2},{4,5},{5,4},{6,7},{7,6},{8,9},{9,8},{10,11... | collective-permute-start | bytes 1720328 | tf_op jit(solution)/shard_map/ppermute | solution.py:10
  31.9 10.5 %collective-permute-start.11 = (bf16[560,512]{1,0:T(8,128)(2,1)}, bf16[560,512]{1,0:T(8,128)(2,1)}, u32[]{:S(2)}, u32[]{:S(2)}) collective-permute-start(bf16[560,512]{1,0:T(8,128)(2,1)} %collective-permute-done.10), channel_id=1, source_target_pairs={{0,16},{1,2},{2,1},{3,19},{16,0},{17,18},{18,17},{19,3},{4,20},{5,... | collective-permute-start | bytes 1720328 | tf_op jit(solution)/shard_map/ppermute | solution.py:22
  33.5 6.9 %copy-start.2 = (f32[560]{0:T(1024)S(1)}, f32[560]{0:T(1024)}, u32[]{:S(2)}) copy-start(f32[560]{0:T(1024)} %param.9) | copy-start | bytes 6724
  34.4 28.2 %collective-permute-start.13 = (bf16[560,512]{1,0:T(8,128)(2,1)}, bf16[560,512]{1,0:T(8,128)(2,1)}, u32[]{:S(2)}, u32[]{:S(2)}) collective-permute-start(bf16[560,512]{1,0:T(8,128)(2,1)} %collective-permute-done.12), channel_id=1, source_target_pairs={{0,1},{1,0},{2,3},{3,2},{4,5},{5,4},{6,7},{7,6},{8,9},{9,8},{10,11... | collective-permute-start | bytes 1720328 | tf_op jit(solution)/shard_map/ppermute | solution.py:10
  42.4 30.3 %collective-permute-start.14 = (bf16[560,512]{1,0:T(8,128)(2,1)}, bf16[560,512]{1,0:T(8,128)(2,1)S(1)}, u32[]{:S(2)}, u32[]{:S(2)}) collective-permute-start(bf16[560,512]{1,0:T(8,128)(2,1)} %collective-permute-done.11), channel_id=1, source_target_pairs={{0,1},{1,0},{2,3},{3,2},{4,5},{5,4},{6,7},{7,6},{8,9},{9,8},{10,11... | collective-permute-start | bytes 1720328 | tf_op jit(solution)/shard_map/ppermute | solution.py:10
  58.6 24.6 %collective-permute-start.4 = (bf16[560,512]{1,0:T(8,128)(2,1)}, bf16[560,512]{1,0:T(8,128)(2,1)S(1)}, u32[]{:S(2)}, u32[]{:S(2)}) collective-permute-start(bf16[560,512]{1,0:T(8,128)(2,1)} %collective-permute-done.1), channel_id=1, source_target_pairs={{0,1},{1,0},{2,3},{3,2},{4,5},{5,4},{6,7},{7,6},{8,9},{9,8},{10,11... | collective-permute-start | bytes 1720328 | tf_op jit(solution)/shard_map/ppermute | solution.py:10
  84.5 3.3 %copy-start.3 = (bf16[2240,560]{0,1:T(8,128)(2,1)S(1)}, bf16[2240,560]{0,1:T(8,128)(2,1)}, u32[]{:S(2)}) copy-start(bf16[2240,560]{0,1:T(8,128)(2,1)} %param.7) | copy-start | bytes 7526404
  97.3 4.9 %copy-start.4 = (bf16[2240,560]{0,1:T(8,128)(2,1)S(1)}, bf16[2240,560]{0,1:T(8,128)(2,1)}, u32[]{:S(2)}) copy-start(bf16[2240,560]{0,1:T(8,128)(2,1)} %param.6) | copy-start | bytes 7526404
  97.6 10.8 %collective-permute-start.15 = (bf16[280,112]{1,0:T(8,128)(2,1)S(1)}, bf16[280,112]{1,0:T(8,128)(2,1)S(1)}, u32[]{:S(2)}, u32[]{:S(2)}) collective-permute-start(bf16[280,112]{1,0:T(8,128)(2,1)S(1)} %get-tuple-element.13), channel_id=1, source_target_pairs={{0,4},{4,0},{8,12},{12,8},{1,5},{5,1},{9,13},{13,9},{2,6},{6,2},{1... | collective-permute-start | bytes 188168 | tf_op jit(solution)/shard_map/ppermute | solution.py:51
  99.2 9.3 %collective-permute-start.17 = (bf16[280,112]{1,0:T(8,128)(2,1)S(1)}, bf16[280,112]{1,0:T(8,128)(2,1)S(1)}, u32[]{:S(2)}, u32[]{:S(2)}) collective-permute-start(bf16[280,112]{1,0:T(8,128)(2,1)S(1)} %get-tuple-element.14), channel_id=1, source_target_pairs={{0,8},{4,12},{8,0},{12,4},{1,9},{5,13},{9,1},{13,5},{2,10},{6,14},... | collective-permute-start | bytes 188168 | tf_op jit(solution)/shard_map/ppermute | solution.py:51
  101.0 4.4 %collective-permute-start.5 = (bf16[280,112]{1,0:T(8,128)(2,1)S(1)}, bf16[280,112]{1,0:T(8,128)(2,1)S(1)}, u32[]{:S(2)}, u32[]{:S(2)}) collective-permute-start(bf16[280,112]{1,0:T(8,128)(2,1)S(1)} %get-tuple-element.19), channel_id=1, source_target_pairs={{0,4},{4,0},{8,12},{12,8},{1,5},{5,1},{9,13},{13,9},{2,6},{6,2},{1... | collective-permute-start | bytes 188168 | tf_op jit(solution)/shard_map/ppermute | solution.py:51
  101.6 4.8 %collective-permute-start.7 = (bf16[280,112]{1,0:T(8,128)(2,1)S(1)}, bf16[280,112]{1,0:T(8,128)(2,1)S(1)}, u32[]{:S(2)}, u32[]{:S(2)}) collective-permute-start(bf16[280,112]{1,0:T(8,128)(2,1)S(1)} %get-tuple-element.20), channel_id=1, source_target_pairs={{0,8},{4,12},{8,0},{12,4},{1,9},{5,13},{9,1},{13,5},{2,10},{6,14},... | collective-permute-start | bytes 188168 | tf_op jit(solution)/shard_map/ppermute | solution.py:51
  106.4 4.4 %collective-permute-start.6 = (bf16[280,112]{1,0:T(8,128)(2,1)S(1)}, bf16[280,112]{1,0:T(8,128)(2,1)S(1)}, u32[]{:S(2)}, u32[]{:S(2)}) collective-permute-start(bf16[280,112]{1,0:T(8,128)(2,1)S(1)} %get-tuple-element.17), channel_id=1, source_target_pairs={{0,8},{4,12},{8,0},{12,4},{1,9},{5,13},{9,1},{13,5},{2,10},{6,14},... | collective-permute-start | bytes 188168 | tf_op jit(solution)/shard_map/ppermute | solution.py:51
  106.9 4.3 %collective-permute-start.8 = (bf16[280,112]{1,0:T(8,128)(2,1)S(1)}, bf16[280,112]{1,0:T(8,128)(2,1)S(1)}, u32[]{:S(2)}, u32[]{:S(2)}) collective-permute-start(bf16[280,112]{1,0:T(8,128)(2,1)S(1)} %get-tuple-element.18), channel_id=1, source_target_pairs={{0,4},{4,0},{8,12},{12,8},{1,5},{5,1},{9,13},{13,9},{2,6},{6,2},{1... | collective-permute-start | bytes 188168 | tf_op jit(solution)/shard_map/ppermute | solution.py:51
  108.5 7.3 %collective-permute-start.16 = (bf16[280,112]{1,0:T(8,128)(2,1)S(1)}, bf16[280,112]{1,0:T(8,128)(2,1)S(1)}, u32[]{:S(2)}, u32[]{:S(2)}) collective-permute-start(bf16[280,112]{1,0:T(8,128)(2,1)S(1)} %get-tuple-element.11), channel_id=1, source_target_pairs={{0,8},{4,12},{8,0},{12,4},{1,9},{5,13},{9,1},{13,5},{2,10},{6,14},... | collective-permute-start | bytes 188168 | tf_op jit(solution)/shard_map/ppermute | solution.py:51
  109.7 6.1 %collective-permute-start.18 = (bf16[280,112]{1,0:T(8,128)(2,1)S(1)}, bf16[280,112]{1,0:T(8,128)(2,1)S(1)}, u32[]{:S(2)}, u32[]{:S(2)}) collective-permute-start(bf16[280,112]{1,0:T(8,128)(2,1)S(1)} %get-tuple-element.12), channel_id=1, source_target_pairs={{0,4},{4,0},{8,12},{12,8},{1,5},{5,1},{9,13},{13,9},{2,6},{6,2},{1... | collective-permute-start | bytes 188168 | tf_op jit(solution)/shard_map/ppermute | solution.py:51
  111.3 4.5 %collective-permute-start.9 = (f32[560,112]{1,0:T(8,128)S(1)}, f32[560,112]{1,0:T(8,128)S(1)}, u32[]{:S(2)}, u32[]{:S(2)}) collective-permute-start(f32[560,112]{1,0:T(8,128)S(1)} %pad_maximum_fusion), channel_id=1, source_target_pairs={{0,16},{1,17},{2,18},{3,19},{4,20},{5,21},{6,22},{7,23},{8,24},{9,... | collective-permute-start | bytes 752648 | tf_op jit(solution)/shard_map/ppermute | solution.py:59

commit v4 on v3

v4 whole, which is shorter than its diff:
```python
import functools

import jax
import jax.numpy as jnp
from jax import lax
from jax.experimental import pallas as pl
from jax.experimental.pallas import tpu as pltpu
from jax.sharding import PartitionSpec as P

HEAD_DIM = 112
LANES = 128
VMEM_LIMIT = 40 * 1024 * 1024
ANYWHERE = pl.BlockSpec(memory_space=pl.ANY)
IN_VMEM = pl.BlockSpec(memory_space=pltpu.VMEM)
IN_SMEM = pl.BlockSpec(memory_space=pltpu.SMEM)


def call(body, outs, out_specs, in_specs, scratch, flops, aliases=None):
    return pl.pallas_call(
        body,
        out_shape=outs,
        in_specs=in_specs,
        out_specs=out_specs,
        scratch_shapes=scratch,
        input_output_aliases=aliases or {},
        compiler_params=pltpu.CompilerParams(vmem_limit_bytes=VMEM_LIMIT),
        cost_estimate=pl.CostEstimate(flops=flops, bytes_accessed=8 << 20, transcendentals=0),
    )


def rounded_dot(matrix, block):
    return jnp.dot(matrix, block, preferred_element_type=jnp.float32)


def token_tiles(tokens):
    width = 256 if tokens % 256 == 0 else tokens
    return width, tokens // width


def add_state(sums, key, value):
    for start in range(0, key.shape[0], HEAD_DIM):
        rows = slice(start, start + HEAD_DIM)
        sums[rows, :] += lax.dot_general(
            value[rows], key[rows], (((1,), (1,)), ((), ())), preferred_element_type=jnp.float32
        )


def load_blocks(place, found, whole, sems):
    mine, inner = place[0], place[1]
    rows = found[0].shape[0]

    def at(flip):
        return whole.at[pl.ds(pl.multiple_of((mine ^ flip) * rows, 16), rows), :]

    for flip, source in enumerate(found):
        if isinstance(source, tuple):
            for want, ref in ((1, source[0]), (0, source[1])):

                @pl.when(inner == want)
                def _(ref=ref, flip=flip):
                    pltpu.make_async_copy(ref, at(flip), sems.at[flip]).start()
        else:
            pltpu.make_async_copy(source, at(flip), sems.at[flip]).start()
    for flip in range(len(found)):
        pltpu.make_async_copy(at(flip), at(flip), sems.at[flip]).wait()


def whole_kernel(place, b0, b1, b2i, b2o, b3i, b3o, wq, wk, wv, query, state, whole, sems):
    load_blocks(place, [b0, b1, (b2i, b2o), (b3i, b3o)], whole, sems)
    state[...] = jnp.zeros_like(state)
    width, tiles = token_tiles(whole.shape[1])

    @pl.loop(0, tiles)
    def _(tile):
        columns = pl.ds(pl.multiple_of(tile * width, width), width)
        block = whole[:, columns]
        key = jnp.maximum(rounded_dot(wk[...], block).astype(jnp.bfloat16), 0)
        value = rounded_dot(wv[...], block).astype(jnp.bfloat16)
        add_state(state, key, value)
        query[:, columns] = jnp.maximum(rounded_dot(wq[...], block).astype(jnp.bfloat16), 0)


def partial_kernel(place, b0, b1, b2i, b2o, wq, wk, wv, tie, sums, whole, sems):
    rows, tokens = b0.shape
    missing = pl.ds(pl.multiple_of((place[0] ^ 3) * rows, 16), rows)
    whole[missing, :] = jnp.zeros((rows, tokens), whole.dtype)
    load_blocks(place, [b0, b1, (b2i, b2o)], whole, sems)
    width, tiles = token_tiles(tokens)

    @pl.loop(0, tiles)
    def _(tile):
        columns = pl.ds(pl.multiple_of(tile * width, width), width)
        block = whole[:, columns]
        for k, matrix in enumerate((wk, wv, wq)):
            sums[k, :, columns] = rounded_dot(matrix[...], block)


def last_block(place, inner_ref, end_ref, last, sems, count, body):
    rows, tokens = inner_ref.shape
    span = last.shape[0]
    for owner in range(count):
        start = owner * rows
        low = start // LANES * LANES
        high = min(count * rows, -(-(start + rows) // LANES) * LANES)
        offset = start - low

        @pl.when((place[0] ^ 3) == owner)
        def _(low=low, high=high, offset=offset):
            target = last.at[pl.ds(offset, rows), :]

            @pl.when(place[1] == 1)
            def _():
                pltpu.make_async_copy(inner_ref, target, sems.at[0]).start()

            @pl.when(place[1] == 0)
            def _():
                pltpu.make_async_copy(end_ref, target, sems.at[0]).start()

            if offset:
                last[0:offset, :] = jnp.zeros((offset, tokens), last.dtype)
            if offset + rows < span:
                last[offset + rows : span, :] = jnp.zeros((span - offset - rows, tokens), last.dtype)
            pltpu.make_async_copy(target, target, sems.at[0]).wait()
            body(slice(low, high))


def state_kernel(count, place, inner_ref, end_ref, wk, wv, sums, state, last, sems):
    state[...] = jnp.zeros_like(state)
    width, tiles = token_tiles(inner_ref.shape[1])

    def body(span):
        depth = span.stop - span.start

        @pl.loop(0, tiles)
        def _(tile):
            columns = pl.ds(pl.multiple_of(tile * width, width), width)
            block = last[0:depth, columns]
            key = (sums[0, :, columns] + rounded_dot(wk[:, span], block)).astype(jnp.bfloat16)
            value = (sums[1, :, columns] + rounded_dot(wv[:, span], block)).astype(jnp.bfloat16)
            add_state(state, jnp.maximum(key, 0), value)

    last_block(place, inner_ref, end_ref, last, sems, count, body)


def query_kernel(count, place, inner_ref, end_ref, wq, sums, tie, query, last, sems):
    width, tiles = token_tiles(inner_ref.shape[1])

    def body(span):
        depth = span.stop - span.start

        @pl.loop(0, tiles)
        def _(tile):
            columns = pl.ds(pl.multiple_of(tile * width, width), width)
            block = last[0:depth, columns]
            row = (sums[2, :, columns] + rounded_dot(wq[:, span], block)).astype(jnp.bfloat16)
            query[:, columns] = jnp.maximum(row, 0)

    last_block(place, inner_ref, end_ref, last, sems, count, body)


def read_kernel(stream, prefix, state, query, gain, *rest):
    out, held, sem = rest[-3:]
    for start in range(0, query.shape[0], HEAD_DIM):
        rows = slice(start, start + HEAD_DIM)
        total = (prefix[rows, :] + state[rows, :]).astype(jnp.bfloat16)
        reading = rounded_dot(total, query[rows, :])
        scale = lax.rsqrt(jnp.mean(reading * reading, axis=0, keepdims=True) + 1e-06)
        held[rows, :] = (reading * scale * gain[rows, :]).astype(jnp.bfloat16)
    copy = pltpu.make_async_copy(held, out.at[stream], sem)
    copy.start()
    copy.wait()


def partner_swap(value, axis):
    return lax.ppermute(value, axis, [(i, i ^ 1) for i in range(lax.axis_size(axis))])


def middle_swap(value, axis, other):
    wide, count = lax.axis_size(other), lax.axis_size(axis)
    pairs = []
    for j in range(wide):
        for i in range(count):
            if i in (1, 2):
                pairs.append((j * count + i, j * count + 3 - i))
            else:
                pairs.append((j * count + i, (j ^ 1 if j ^ 1 < wide else j) * count + i))
    return lax.ppermute(value, (other, axis), pairs)


def sum_over(value, axis):
    count = lax.axis_size(axis)
    heads = value.shape[0] // HEAD_DIM
    half = (heads + 1) // 2 * HEAD_DIM
    steps = [1 << b for b in range(count.bit_length() - 1)]
    outs = []
    for part, order in ((value[:half], steps), (value[half:], steps[::-1])):
        for step in order:
            sent = lax.ppermute(part.astype(jnp.bfloat16), axis, [(i, i ^ step) for i in range(count)])
            part = part + sent.astype(jnp.float32)
        outs.append(part)
    return jnp.concatenate(outs, axis=0)


def entering(value, axis):
    count = lax.axis_size(axis)
    total = lax.ppermute(value, axis, [(i, i + 1) for i in range(count - 1)])
    reach = 1
    while reach < count - 1:
        total = total + lax.ppermute(total, axis, [(i, i + reach) for i in range(count - reach)])
        reach *= 2
    return total


def local(streams, w_query, w_key, w_value, gain):
    count, mine = lax.axis_size("head"), lax.axis_index("head")
    rows, tokens = streams.shape[2], streams.shape[1]
    width = w_query.shape[1]
    depth = rows * count
    columns = jnp.swapaxes(streams, 1, 2)
    matrices = (w_query.T, w_key.T, w_value.T)
    gain_column = gain.reshape(width, 1)
    inner = (mine == 1) | (mine == 2)
    place = jnp.stack([mine.astype(jnp.int32), inner.astype(jnp.int32)])

    own, near, across, far, across_end, far_end = [], [], [], [], [], []
    for stream in range(2):
        own.append(columns[stream])
        near.append(partner_swap(own[stream], "head"))
        across.append(middle_swap(own[stream], "head", "group"))
    for stream in range(2):
        far.append(middle_swap(near[stream], "head", "group"))
        across_end.append(partner_swap(across[stream], "head"))
    for stream in range(2):
        far_end.append(partner_swap(far[stream], "head"))

    whole = pltpu.VMEM((depth, tokens), jnp.bfloat16)
    sems = pltpu.SemaphoreType.DMA((4,))
    last = pltpu.VMEM((-(-(rows + LANES) // LANES) * LANES, tokens), jnp.bfloat16)
    query_type = jax.ShapeDtypeStruct((width, tokens), jnp.bfloat16)
    state_type = jax.ShapeDtypeStruct((width, HEAD_DIM), jnp.float32)
    out_type = jax.ShapeDtypeStruct((2, width, tokens), jnp.bfloat16)
    one = 2 * width * depth * tokens

    query0, state0 = call(
        whole_kernel, (query_type, state_type), (IN_VMEM, IN_VMEM),
        [IN_SMEM] + [ANYWHERE] * 6 + [IN_VMEM] * 3, [whole, sems], 3 * one,
    )(place, own[0], near[0], far[0], across_end[0], across[0], far_end[0], *matrices)
    state0 = sum_over(state0, "tok")
    prefix = entering(state0, "group")

    sums = call(
        partial_kernel, jax.ShapeDtypeStruct((3, width, tokens), jnp.float32), IN_VMEM,
        [IN_SMEM] + [ANYWHERE] * 4 + [IN_VMEM] * 3 + [ANYWHERE], [whole, sems], 3 * one,
    )(place, own[1], near[1], far[1], across_end[1], *matrices, query0)

    read_scratch = [pltpu.VMEM((width, tokens), jnp.bfloat16), pltpu.SemaphoreType.DMA(())]
    out = call(
        functools.partial(read_kernel, 0), out_type, ANYWHERE, [IN_VMEM] * 4, read_scratch, one // 20,
    )(prefix, state0, query0, gain_column)

    state1 = call(
        functools.partial(state_kernel, count), state_type, IN_VMEM,
        [IN_SMEM] + [ANYWHERE] * 2 + [IN_VMEM] * 3, [last, sems], one // 2,
    )(place, across[1], far_end[1], *matrices[1:], sums)
    query1 = call(
        functools.partial(query_kernel, count), query_type, IN_VMEM,
        [IN_SMEM] + [ANYWHERE] * 2 + [IN_VMEM] * 2 + [ANYWHERE], [last, sems], one // 4,
    )(place, across[1], far_end[1], matrices[0], sums, state1)
    state1 = sum_over(state1, "tok")
    out = call(
        functools.partial(read_kernel, 1), out_type, ANYWHERE, [IN_VMEM] * 4 + [ANYWHERE], read_scratch,
        one // 20, {4: 0},
    )(prefix, state1, query1, gain_column, out)
    return jnp.swapaxes(out, 1, 2)


def solution(mesh):
    return jax.shard_map(
        local,
        mesh=mesh,
        in_specs=(
            P(None, ("group", "tok"), "head"),
            P(None, "head"),
            P(None, "head"),
            P(None, "head"),
            P("head"),
        ),
        out_specs=P(None, ("group", "tok"), "head"),
        check_vma=False,
    )
```

time: 118 us -> 102 us (0.86)
  Pallas kernels: 0 us -> 22 us
  matrix products: 20.2 us -> 0 us
  waiting for transfers between devices: 39.9 us -> 27.6 us
  other arithmetic: 7.05 us -> 0.33 us
  starting transfers between devices: 39.3 us -> 41.4 us
    pallas_call x0 -> x6, Pallas kernels: none -> 22 us  [the longest x1 9.49 us: local(): call(whole_kernel, (query_type, state_type), (IN_VMEM, IN_VMEM), [IN_SMEM...]
    dot_general x10 -> x0, matrix products: 20.2 us -> none  [the longest x6 19 us: project(): jnp.dot(matrix, block, preferred_element_type=jnp.float32)]
    ppermute x6, waiting for transfers between devices: 38.2 us -> 24.2 us  [partner_swap(): lax.ppermute(value, axis, [(i, i ^ 1) for i in range(lax.axis_size(axis))])]
    unnamed x10 -> x20, local copies, waits for them, and re-layouts: 0.02 us -> 8.01 us
    dynamic_update_slice x4 -> x0, local copies, waits for them, and re-layouts: 5.55 us -> none  [gather_blocks(): lax.dynamic_update_slice_in_dim(whole, piece, (mine ^ flip) * rows, 0)]
    dynamic_update_slice x3 -> x0, other arithmetic: 5.39 us -> none  [gather_blocks(): lax.dynamic_update_slice_in_dim(whole, piece, (mine ^ flip) * rows, 0)]
    another operation x2 -> x0, local copies, waits for them, and re-layouts: 3.15 us -> none
  transfers between devices with their start and end apart: 19 -> 19, of which waited for: 8 -> 6; matrix products, arithmetic and copies ran while one was open for 17% -> 1% of each run, Pallas kernels for 0% -> 19%
where the time goes in v4:
time: 102 us
  starting transfers between devices  41.4 us (41%)
  waiting for transfers between devices  27.6 us (27%)
  Pallas kernels  22 us (22%)
  local copies, waits for them, and re-layouts  10.3 us (10%)
    ppermute x6, starting transfers between devices, partner_swap(): lax.ppermute(value, axis, [(i, i ^ 1) for i in range(lax.axis_size(axis))])  30.2 us
    ppermute x6, waiting for transfers between devices, partner_swap(): lax.ppermute(value, axis, [(i, i ^ 1) for i in range(lax.axis_size(axis))])  24.2 us
    pallas_call x1, Pallas kernels, local(): call(whole_kernel, (query_type, state_type), (IN_VMEM, IN_VMEM), [IN_SMEM...  9.49 us
    ppermute x8, starting transfers between devices, sum_over(): lax.ppermute(part.astype(jnp.bfloat16), axis, [(i, i ^ step) for i in ran...  9.31 us
    unnamed x20, local copies, waits for them, and re-layouts  8.01 us
    pallas_call x1, Pallas kernels, local(): call(partial_kernel, jax.ShapeDtypeStruct((3, width, tokens), jnp.float32...  6.29 us
    ppermute x8, waiting for transfers between devices, sum_over(): lax.ppermute(part.astype(jnp.bfloat16), axis, [(i, i ^ step) for i in ran...  2.33 us
    pallas_call x1, Pallas kernels, local(): call(functools.partial(state_kernel, count), state_type, IN_VMEM, [IN_SME...  2.25 us
  transfers between devices with their start and end apart: 19, of which 6 were waited for; matrix products, arithmetic and copies ran while one was open for 1% of the time, Pallas kernels for 19%

profile of v4, /device:TPU:0, one launch (start us, length us, event | category | flops | bytes accessed | tf_op | source)
XLA Modules:
  0.0 101.8 jit_solution(3646229558812669359)
XLA Ops:
  0.0 1.5 %slice_bitcast_fusion = (bf16[560,512]{1,0:T(8,128)(2,1)S(1)}, bf16[560,512]{1,0:T(8,128)(2,1)S(1)}) fusion(bf16[2,560,512]{2,1,0:T(8,128)(2,1)} %bitcast.20), kind=kLoop, calls=%fused_computation | loop fusion | bytes 2293760 | tf_op jit(solution)/shard_map/squeeze | solution.py:227
  1.5 3.1 %collective-permute-start = (bf16[560,512]{1,0:T(8,128)(2,1)S(1)}, bf16[560,512]{1,0:T(8,128)(2,1)S(1)}, u32[]{:S(2)}, u32[]{:S(2)}) collective-permute-start(bf16[560,512]{1,0:T(8,128)(2,1)S(1)} %get-tuple-element.10.b0), channel_id=1, source_target_pairs={{0,1},{1,0},{2,3},{3,2},{4,5},{5,4},{6,7},{7,6},{8,9},{9,8},{10,11... | collective-permute-start | bytes 1720328 | tf_op jit(solution)/shard_map/ppermute | solution.py:175
  4.6 0.8 copy-done.6
  5.4 12.9 %collective-permute-done.b1 = bf16[560,512]{1,0:T(8,128)(2,1)S(1)} collective-permute-done((bf16[560,512]{1,0:T(8,128)(2,1)S(1)}, bf16[560,512]{1,0:T(8,128)(2,1)S(1)}, u32[]{:S(2)}, u32[]{:S(2)}) %collective-permute-start) | collective-permute-done | bytes 573472 | tf_op jit(solution)/shard_map/ppermute | solution.py:175
  18.4 0.8 copy-done.8
  19.7 0.8 copy-done.4
  20.5 9.4 %collective-permute-done.11.b1 = bf16[560,512]{1,0:T(8,128)(2,1)} collective-permute-done((bf16[560,512]{1,0:T(8,128)(2,1)S(1)}, bf16[560,512]{1,0:T(8,128)(2,1)}, u32[]{:S(2)}, u32[]{:S(2)}) %collective-permute-start.11) | collective-permute-done | bytes 573472 | tf_op jit(solution)/shard_map/ppermute | solution.py:175
  29.9 3.3 %collective-permute-start.3 = (bf16[560,512]{1,0:T(8,128)(2,1)}, bf16[560,512]{1,0:T(8,128)(2,1)}, u32[]{:S(2)}, u32[]{:S(2)}) collective-permute-start(bf16[560,512]{1,0:T(8,128)(2,1)} %collective-permute-done.2.b3i), channel_id=1, source_target_pairs={{0,1},{1,0},{2,3},{3,2},{4,5},{5,4},{6,7},{7,6},{8,9},{9,8},{10,11... | collective-permute-start | bytes 1720328 | tf_op jit(solution)/shard_map/ppermute | solution.py:175
  33.2 3.2 %collective-permute-start.4 = (bf16[560,512]{1,0:T(8,128)(2,1)}, bf16[560,512]{1,0:T(8,128)(2,1)}, u32[]{:S(2)}, u32[]{:S(2)}) collective-permute-start(bf16[560,512]{1,0:T(8,128)(2,1)} %collective-permute-done.1.b2i), channel_id=1, source_target_pairs={{0,1},{1,0},{2,3},{3,2},{4,5},{5,4},{6,7},{7,6},{8,9},{9,8},{10,11... | collective-permute-start | bytes 1720328 | tf_op jit(solution)/shard_map/ppermute | solution.py:175
  36.4 12.2 %collective-permute-start.14 = (bf16[560,512]{1,0:T(8,128)(2,1)S(1)}, bf16[560,512]{1,0:T(8,128)(2,1)}, u32[]{:S(2)}, u32[]{:S(2)}) collective-permute-start(bf16[560,512]{1,0:T(8,128)(2,1)S(1)} %collective-permute-done.10.inner_ref), channel_id=1, source_target_pairs={{0,1},{1,0},{2,3},{3,2},{4,5},{5,4},{6,7},{7,6},{8,9},{9,8},{10,11... | collective-permute-start | bytes 1720328 | tf_op jit(solution)/shard_map/ppermute | solution.py:175
  48.6 0.8 reshape.5.gain
  49.5 8.4 %collective-permute-start.13 = (bf16[560,512]{1,0:T(8,128)(2,1)}, bf16[560,512]{1,0:T(8,128)(2,1)S(1)}, u32[]{:S(2)}, u32[]{:S(2)}) collective-permute-start(bf16[560,512]{1,0:T(8,128)(2,1)} %collective-permute-done.12.b2i), channel_id=1, source_target_pairs={{0,1},{1,0},{2,3},{3,2},{4,5},{5,4},{6,7},{7,6},{8,9},{9,8},{10,11... | collective-permute-start | bytes 1720328 | tf_op jit(solution)/shard_map/ppermute | solution.py:175
  57.9 1.8 %collective-permute-done.4.b3o = bf16[560,512]{1,0:T(8,128)(2,1)} collective-permute-done((bf16[560,512]{1,0:T(8,128)(2,1)}, bf16[560,512]{1,0:T(8,128)(2,1)}, u32[]{:S(2)}, u32[]{:S(2)}) %collective-permute-start.4) | collective-permute-done | bytes 573472 | tf_op jit(solution)/shard_map/ppermute | solution.py:175
  59.7 1.7 %copy-done.1 = bf16[2240,560]{0,1:T(8,128)(2,1)S(1)} copy-done((bf16[2240,560]{0,1:T(8,128)(2,1)S(1)}, bf16[2240,560]{0,1:T(8,128)(2,1)}, u32[]{:S(2)}) %copy-start.1) | copy-done | bytes 2508824
  61.5 1.7 %copy-done.3 = bf16[2240,560]{0,1:T(8,128)(2,1)S(1)} copy-done((bf16[2240,560]{0,1:T(8,128)(2,1)S(1)}, bf16[2240,560]{0,1:T(8,128)(2,1)}, u32[]{:S(2)}) %copy-start.3) | copy-done | bytes 2508824
  63.2 1.1 %copy-done.7 = bf16[560,512]{1,0:T(8,128)(2,1)S(1)} copy-done((bf16[560,512]{1,0:T(8,128)(2,1)S(1)}, bf16[560,512]{1,0:T(8,128)(2,1)}, u32[]{:S(2)}) %copy-start.7) | copy-done | bytes 573464
  64.3 1.1 %copy-done.9 = bf16[560,512]{1,0:T(8,128)(2,1)S(1)} copy-done((bf16[560,512]{1,0:T(8,128)(2,1)S(1)}, bf16[560,512]{1,0:T(8,128)(2,1)}, u32[]{:S(2)}) %copy-start.9) | copy-done | bytes 573464
  65.3 9.5 %shard_map.55 = (bf16[560,512]{1,0:T(8,128)(2,1)S(1)}, f32[560,112]{1,0:T(8,128)S(1)}) custom-call(s32[2]{0:T(128)S(1)} %pad_add_fusion.place, bf16[560,512]{1,0:T(8,128)(2,1)S(1)} %copy-done.7, bf16[560,512]{1,0:T(8,128)(2,1)S(1)} %copy-done.9, bf16[560,512]{1,0:T(8,128)(2,1)} %collective-permute-done.1.b2i, bf16[560,512]{1,0:T(8,128)(2,1)} %collective-permute-done.3.b2o, ...), custom_call_target="tpu_custom_call" | custom-call | flops 3853516800 | bytes 8388608 | tf_op jit(solution)/shard_map/pallas_call | solution.py:244
  74.8 1.6 %collective-permute-start.7 = (bf16[224,112]{1,0:T(8,128)(2,1)S(1)}, bf16[224,112]{1,0:T(8,128)(2,1)S(1)}, u32[]{:S(2)}, u32[]{:S(2)}) collective-permute-start(bf16[224,112]{1,0:T(8,128)(2,1)S(1)} %slice.57), channel_id=1, source_target_pairs={{0,8},{4,12},{8,0},{12,4},{1,9},{5,13},{9,1},{13,5},{2,10},{6,14},... | collective-permute-start | bytes 150536 | tf_op jit(solution)/shard_map/ppermute | solution.py:198
  76.4 6.3 %shard_map.56.sums = f32[3,560,512]{2,1,0:T(8,128)S(1)} custom-call(s32[2]{0:T(128)S(1)} %pad_add_fusion.place, bf16[560,512]{1,0:T(8,128)(2,1)S(1)} %copy-done.5, bf16[560,512]{1,0:T(8,128)(2,1)} %collective-permute-done.11.b1, bf16[560,512]{1,0:T(8,128)(2,1)} %collective-permute-done.12.b2i, bf16[560,512]{1,0:T(8,128)(2,1)} %collective-permute-done.14.b2o, ...), custom_call_target="tpu_custom_call" | custom-call | flops 3853516800 | bytes 8388608 | tf_op jit(solution)/shard_map/pallas_call | solution.py:251
  82.7 2.3 %shard_map.57.tie = f32[560,112]{1,0:T(8,128)S(1)} custom-call(s32[2]{0:T(128)S(1)} %pad_add_fusion.place, bf16[560,512]{1,0:T(8,128)(2,1)S(1)} %collective-permute-done.10.inner_ref, bf16[560,512]{1,0:T(8,128)(2,1)S(1)} %collective-permute-done.13.end_ref, bf16[560,2240]{1,0:T(8,128)(2,1)S(1)} %bitcast.13, bf16[560,2240]{1,0:T(8,128)(2,1)S(1)} %bitcast.16, ...), custom_call_target="tpu_custom_call" | custom-call | flops 642252800 | bytes 8388608 | tf_op jit(solution)/shard_map/pallas_call | solution.py:261
  85.1 1.6 %collective-permute-start.5 = (bf16[336,112]{1,0:T(8,128)(2,1)S(1)}, bf16[336,112]{1,0:T(8,128)(2,1)S(1)}, u32[]{:S(2)}, u32[]{:S(2)}) collective-permute-start(bf16[336,112]{1,0:T(8,128)(2,1)S(1)} %slice.55), channel_id=1, source_target_pairs={{0,4},{4,0},{8,12},{12,8},{1,5},{5,1},{9,13},{13,9},{2,6},{6,2},{1... | collective-permute-start | bytes 225800 | tf_op jit(solution)/shard_map/ppermute | solution.py:198
  86.6 1.3 %collective-permute-start.17 = (bf16[224,112]{1,0:T(8,128)(2,1)S(1)}, bf16[224,112]{1,0:T(8,128)(2,1)S(1)}, u32[]{:S(2)}, u32[]{:S(2)}) collective-permute-start(bf16[224,112]{1,0:T(8,128)(2,1)S(1)} %slice.56), channel_id=1, source_target_pairs={{0,8},{4,12},{8,0},{12,4},{1,9},{5,13},{9,1},{13,5},{2,10},{6,14},... | collective-permute-start | bytes 150536 | tf_op jit(solution)/shard_map/ppermute | solution.py:198
  88.5 1.5 %shard_map.58.query = bf16[560,512]{1,0:T(8,128)(2,1)S(1)} custom-call(s32[2]{0:T(128)S(1)} %pad_add_fusion.place, bf16[560,512]{1,0:T(8,128)(2,1)S(1)} %collective-permute-done.10.inner_ref, bf16[560,512]{1,0:T(8,128)(2,1)S(1)} %collective-permute-done.13.end_ref, bf16[560,2240]{1,0:T(8,128)(2,1)S(1)} %bitcast.19, f32[3,560,512]{2,1,0:T(8,128)S(1)} %shard_map.56.sums, ...), custom_call_target="tpu_custom_call" | custom-call | flops 321126400 | bytes 8388608 | tf_op jit(solution)/shard_map/pallas_call | solution.py:265
  90.1 1.6 %collective-permute-start.8 = (bf16[224,112]{1,0:T(8,128)(2,1)S(1)}, bf16[224,112]{1,0:T(8,128)(2,1)S(1)}, u32[]{:S(2)}, u32[]{:S(2)}) collective-permute-start(bf16[224,112]{1,0:T(8,128)(2,1)S(1)} %fusion.2), channel_id=1, source_target_pairs={{0,4},{4,0},{8,12},{12,8},{1,5},{5,1},{9,13},{13,9},{2,6},{6,2},{1... | collective-permute-start | bytes 150536 | tf_op jit(solution)/shard_map/ppermute | solution.py:198
  93.1 1.4 %collective-permute-start.16 = (bf16[336,112]{1,0:T(8,128)(2,1)S(1)}, bf16[336,112]{1,0:T(8,128)(2,1)S(1)}, u32[]{:S(2)}, u32[]{:S(2)}) collective-permute-start(bf16[336,112]{1,0:T(8,128)(2,1)S(1)} %fusion.1), channel_id=1, source_target_pairs={{0,8},{4,12},{8,0},{12,4},{1,9},{5,13},{9,1},{13,5},{2,10},{6,14},... | collective-permute-start | bytes 225800 | tf_op jit(solution)/shard_map/ppermute | solution.py:198
  94.5 1.4 %collective-permute-done.18 = bf16[224,112]{1,0:T(8,128)(2,1)S(1)} collective-permute-done((bf16[224,112]{1,0:T(8,128)(2,1)S(1)}, bf16[224,112]{1,0:T(8,128)(2,1)S(1)}, u32[]{:S(2)}, u32[]{:S(2)}) %collective-permute-start.18) | collective-permute-done | bytes 50208 | tf_op jit(solution)/shard_map/ppermute | solution.py:198
  95.9 0.9 collective-permute-done.6
  96.9 1.3 %collective-permute-start.9 = (f32[560,112]{1,0:T(8,128)S(1)}, f32[560,112]{1,0:T(8,128)S(1)}, u32[]{:S(2)}, u32[]{:S(2)}) collective-permute-start(f32[560,112]{1,0:T(8,128)S(1)} %pad_maximum_fusion.state), channel_id=1, source_target_pairs={{0,16},{1,17},{2,18},{3,19},{4,20},{5,21},{6,22},{7,23},{8,24},{9,... | collective-permute-start | bytes 752648 | tf_op jit(solution)/shard_map/ppermute | solution.py:206
  98.3 1.1 %collective-permute-done.9.prefix = f32[560,112]{1,0:T(8,128)S(1)} collective-permute-done((f32[560,112]{1,0:T(8,128)S(1)}, f32[560,112]{1,0:T(8,128)S(1)}, u32[]{:S(2)}, u32[]{:S(2)}) %collective-permute-start.9) | collective-permute-done | bytes 250912 | tf_op jit(solution)/shard_map/ppermute | solution.py:206
  99.4 1.2 %shard_map.59.rest_0_ = bf16[2,560,512]{2,1,0:T(8,128)(2,1)} custom-call(f32[560,112]{1,0:T(8,128)S(1)} %collective-permute-done.9.prefix, f32[560,112]{1,0:T(8,128)S(1)} %pad_maximum_fusion.state, bf16[560,512]{1,0:T(8,128)(2,1)S(1)} %get-tuple-element.8.tie.query, f32[560,1]{1,0:T(8,128)S(1)} %reshape.5.gain), custom_call_target="tpu_custom_call" | custom-call | flops 64225280 | bytes 8388608 | tf_op jit(solution)/shard_map/pallas_call | solution.py:257
  100.6 1.2 %shard_map.60 = bf16[2,560,512]{2,1,0:T(8,128)(2,1)} custom-call(f32[560,112]{1,0:T(8,128)S(1)} %collective-permute-done.9.prefix, f32[560,112]{1,0:T(8,128)S(1)} %pad_maximum_fusion.1.state, bf16[560,512]{1,0:T(8,128)(2,1)S(1)} %shard_map.58.query, f32[560,1]{1,0:T(8,128)S(1)} %reshape.5.gain, ...), custom_call_target="tpu_custom_call", output_to_operand_aliasing={{}: (4, {})} | custom-call | flops 64225280 | bytes 8388608 | tf_op jit(solution)/shard_map/pallas_call | solution.py:270
  (49 shorter events, 2.9 us)
Async XLA Ops:
  0.0 59.7 %copy-start = (bf16[2240,560]{0,1:T(8,128)(2,1)S(1)}, bf16[2240,560]{0,1:T(8,128)(2,1)}, u32[]{:S(2)}) copy-start(bf16[2240,560]{0,1:T(8,128)(2,1)} %param.7) | copy-start | bytes 7526404
  1.5 16.9 %collective-permute-start = (bf16[560,512]{1,0:T(8,128)(2,1)S(1)}, bf16[560,512]{1,0:T(8,128)(2,1)S(1)}, u32[]{:S(2)}, u32[]{:S(2)}) collective-permute-start(bf16[560,512]{1,0:T(8,128)(2,1)S(1)} %get-tuple-element.10.b0), channel_id=1, source_target_pairs={{0,1},{1,0},{2,3},{3,2},{4,5},{5,4},{6,7},{7,6},{8,9},{9,8},{10,11... | collective-permute-start | bytes 1720328 | tf_op jit(solution)/shard_map/ppermute | solution.py:175
  4.6 25.4 %collective-permute-start.11 = (bf16[560,512]{1,0:T(8,128)(2,1)S(1)}, bf16[560,512]{1,0:T(8,128)(2,1)}, u32[]{:S(2)}, u32[]{:S(2)}) collective-permute-start(bf16[560,512]{1,0:T(8,128)(2,1)S(1)} %get-tuple-element.9.b0), channel_id=1, source_target_pairs={{0,1},{1,0},{2,3},{3,2},{4,5},{5,4},{6,7},{7,6},{8,9},{9,8},{10,11... | collective-permute-start | bytes 1720328 | tf_op jit(solution)/shard_map/ppermute | solution.py:175
  4.6 25.3 %collective-permute-start.2 = (bf16[560,512]{1,0:T(8,128)(2,1)S(1)}, bf16[560,512]{1,0:T(8,128)(2,1)}, u32[]{:S(2)}, u32[]{:S(2)}) collective-permute-start(bf16[560,512]{1,0:T(8,128)(2,1)S(1)} %get-tuple-element.10.b0), channel_id=1, source_target_pairs={{0,16},{1,2},{2,1},{3,19},{16,0},{17,18},{18,17},{19,3},{4,20},{5,... | collective-permute-start | bytes 1720328 | tf_op jit(solution)/shard_map/ppermute | solution.py:187
  4.6 0.8 copy-start.6
  18.4 14.9 %collective-permute-start.1 = (bf16[560,512]{1,0:T(8,128)(2,1)S(1)}, bf16[560,512]{1,0:T(8,128)(2,1)}, u32[]{:S(2)}, u32[]{:S(2)}) collective-permute-start(bf16[560,512]{1,0:T(8,128)(2,1)S(1)} %collective-permute-done.b1), channel_id=1, source_target_pairs={{0,16},{1,2},{2,1},{3,19},{16,0},{17,18},{18,17},{19,3},{4,20},{5,... | collective-permute-start | bytes 1720328 | tf_op jit(solution)/shard_map/ppermute | solution.py:187
  18.4 0.8 copy-start.8
  19.2 17.3 %collective-permute-start.10 = (bf16[560,512]{1,0:T(8,128)(2,1)S(1)}, bf16[560,512]{1,0:T(8,128)(2,1)S(1)}, u32[]{:S(2)}, u32[]{:S(2)}) collective-permute-start(bf16[560,512]{1,0:T(8,128)(2,1)S(1)} %get-tuple-element.9.b0), channel_id=1, source_target_pairs={{0,16},{1,2},{2,1},{3,19},{16,0},{17,18},{18,17},{19,3},{4,20},{5,... | collective-permute-start | bytes 1720328 | tf_op jit(solution)/shard_map/ppermute | solution.py:187
  19.7 0.8 copy-start.4
  29.9 19.6 %collective-permute-start.12 = (bf16[560,512]{1,0:T(8,128)(2,1)}, bf16[560,512]{1,0:T(8,128)(2,1)}, u32[]{:S(2)}, u32[]{:S(2)}) collective-permute-start(bf16[560,512]{1,0:T(8,128)(2,1)} %collective-permute-done.11.b1), channel_id=1, source_target_pairs={{0,16},{1,2},{2,1},{3,19},{16,0},{17,18},{18,17},{19,3},{4,20},{5,... | collective-permute-start | bytes 1720328 | tf_op jit(solution)/shard_map/ppermute | solution.py:187
  29.9 28.0 %collective-permute-start.3 = (bf16[560,512]{1,0:T(8,128)(2,1)}, bf16[560,512]{1,0:T(8,128)(2,1)}, u32[]{:S(2)}, u32[]{:S(2)}) collective-permute-start(bf16[560,512]{1,0:T(8,128)(2,1)} %collective-permute-done.2.b3i), channel_id=1, source_target_pairs={{0,1},{1,0},{2,3},{3,2},{4,5},{5,4},{6,7},{7,6},{8,9},{9,8},{10,11... | collective-permute-start | bytes 1720328 | tf_op jit(solution)/shard_map/ppermute | solution.py:175
  33.2 26.5 %collective-permute-start.4 = (bf16[560,512]{1,0:T(8,128)(2,1)}, bf16[560,512]{1,0:T(8,128)(2,1)}, u32[]{:S(2)}, u32[]{:S(2)}) collective-permute-start(bf16[560,512]{1,0:T(8,128)(2,1)} %collective-permute-done.1.b2i), channel_id=1, source_target_pairs={{0,1},{1,0},{2,3},{3,2},{4,5},{5,4},{6,7},{7,6},{8,9},{9,8},{10,11... | collective-permute-start | bytes 1720328 | tf_op jit(solution)/shard_map/ppermute | solution.py:175
  36.4 40.0 %collective-permute-start.14 = (bf16[560,512]{1,0:T(8,128)(2,1)S(1)}, bf16[560,512]{1,0:T(8,128)(2,1)}, u32[]{:S(2)}, u32[]{:S(2)}) collective-permute-start(bf16[560,512]{1,0:T(8,128)(2,1)S(1)} %collective-permute-done.10.inner_ref), channel_id=1, source_target_pairs={{0,1},{1,0},{2,3},{3,2},{4,5},{5,4},{6,7},{7,6},{8,9},{9,8},{10,11... | collective-permute-start | bytes 1720328 | tf_op jit(solution)/shard_map/ppermute | solution.py:175
  49.5 33.2 %collective-permute-start.13 = (bf16[560,512]{1,0:T(8,128)(2,1)}, bf16[560,512]{1,0:T(8,128)(2,1)S(1)}, u32[]{:S(2)}, u32[]{:S(2)}) collective-permute-start(bf16[560,512]{1,0:T(8,128)(2,1)} %collective-permute-done.12.b2i), channel_id=1, source_target_pairs={{0,1},{1,0},{2,3},{3,2},{4,5},{5,4},{6,7},{7,6},{8,9},{9,8},{10,11... | collective-permute-start | bytes 1720328 | tf_op jit(solution)/shard_map/ppermute | solution.py:175
  59.7 1.7 %copy-start.1 = (bf16[2240,560]{0,1:T(8,128)(2,1)S(1)}, bf16[2240,560]{0,1:T(8,128)(2,1)}, u32[]{:S(2)}) copy-start(bf16[2240,560]{0,1:T(8,128)(2,1)} %param.8) | copy-start | bytes 7526404
  61.5 1.7 %copy-start.3 = (bf16[2240,560]{0,1:T(8,128)(2,1)S(1)}, bf16[2240,560]{0,1:T(8,128)(2,1)}, u32[]{:S(2)}) copy-start(bf16[2240,560]{0,1:T(8,128)(2,1)} %param.6) | copy-start | bytes 7526404
  63.2 1.1 %copy-start.7 = (bf16[560,512]{1,0:T(8,128)(2,1)S(1)}, bf16[560,512]{1,0:T(8,128)(2,1)}, u32[]{:S(2)}) copy-start(bf16[560,512]{1,0:T(8,128)(2,1)} %copy-done.6) | copy-start | bytes 1720324
  64.3 1.1 %copy-start.9 = (bf16[560,512]{1,0:T(8,128)(2,1)S(1)}, bf16[560,512]{1,0:T(8,128)(2,1)}, u32[]{:S(2)}) copy-start(bf16[560,512]{1,0:T(8,128)(2,1)} %copy-done.8) | copy-start | bytes 1720324
  65.3 11.1 %copy-start.2 = (bf16[2240,560]{0,1:T(8,128)(2,1)S(1)}, bf16[2240,560]{0,1:T(8,128)(2,1)}, u32[]{:S(2)}) copy-start(bf16[2240,560]{0,1:T(8,128)(2,1)} %param.8) | copy-start | bytes 7526404
  65.3 11.1 %copy-start.5 = (bf16[560,512]{1,0:T(8,128)(2,1)S(1)}, bf16[560,512]{1,0:T(8,128)(2,1)}, u32[]{:S(2)}) copy-start(bf16[560,512]{1,0:T(8,128)(2,1)} %copy-done.4) | copy-start | bytes 1720324
  74.8 15.2 %collective-permute-start.7 = (bf16[224,112]{1,0:T(8,128)(2,1)S(1)}, bf16[224,112]{1,0:T(8,128)(2,1)S(1)}, u32[]{:S(2)}, u32[]{:S(2)}) collective-permute-start(bf16[224,112]{1,0:T(8,128)(2,1)S(1)} %slice.57), channel_id=1, source_target_pairs={{0,8},{4,12},{8,0},{12,4},{1,9},{5,13},{9,1},{13,5},{2,10},{6,14},... | collective-permute-start | bytes 150536 | tf_op jit(solution)/shard_map/ppermute | solution.py:198
  85.1 7.2 %collective-permute-start.5 = (bf16[336,112]{1,0:T(8,128)(2,1)S(1)}, bf16[336,112]{1,0:T(8,128)(2,1)S(1)}, u32[]{:S(2)}, u32[]{:S(2)}) collective-permute-start(bf16[336,112]{1,0:T(8,128)(2,1)S(1)} %slice.55), channel_id=1, source_target_pairs={{0,4},{4,0},{8,12},{12,8},{1,5},{5,1},{9,13},{13,9},{2,6},{6,2},{1... | collective-permute-start | bytes 225800 | tf_op jit(solution)/shard_map/ppermute | solution.py:198
  86.6 5.0 %collective-permute-start.17 = (bf16[224,112]{1,0:T(8,128)(2,1)S(1)}, bf16[224,112]{1,0:T(8,128)(2,1)S(1)}, u32[]{:S(2)}, u32[]{:S(2)}) collective-permute-start(bf16[224,112]{1,0:T(8,128)(2,1)S(1)} %slice.56), channel_id=1, source_target_pairs={{0,8},{4,12},{8,0},{12,4},{1,9},{5,13},{9,1},{13,5},{2,10},{6,14},... | collective-permute-start | bytes 150536 | tf_op jit(solution)/shard_map/ppermute | solution.py:198
  88.0 5.1 %collective-permute-start.15 = (bf16[336,112]{1,0:T(8,128)(2,1)S(1)}, bf16[336,112]{1,0:T(8,128)(2,1)S(1)}, u32[]{:S(2)}, u32[]{:S(2)}) collective-permute-start(bf16[336,112]{1,0:T(8,128)(2,1)S(1)} %slice.54), channel_id=1, source_target_pairs={{0,4},{4,0},{8,12},{12,8},{1,5},{5,1},{9,13},{13,9},{2,6},{6,2},{1... | collective-permute-start | bytes 225800 | tf_op jit(solution)/shard_map/ppermute | solution.py:198
  90.1 4.4 %collective-permute-start.8 = (bf16[224,112]{1,0:T(8,128)(2,1)S(1)}, bf16[224,112]{1,0:T(8,128)(2,1)S(1)}, u32[]{:S(2)}, u32[]{:S(2)}) collective-permute-start(bf16[224,112]{1,0:T(8,128)(2,1)S(1)} %fusion.2), channel_id=1, source_target_pairs={{0,4},{4,0},{8,12},{12,8},{1,5},{5,1},{9,13},{13,9},{2,6},{6,2},{1... | collective-permute-start | bytes 150536 | tf_op jit(solution)/shard_map/ppermute | solution.py:198
  91.6 4.2 %collective-permute-start.18 = (bf16[224,112]{1,0:T(8,128)(2,1)S(1)}, bf16[224,112]{1,0:T(8,128)(2,1)S(1)}, u32[]{:S(2)}, u32[]{:S(2)}) collective-permute-start(bf16[224,112]{1,0:T(8,128)(2,1)S(1)} %fusion.3), channel_id=1, source_target_pairs={{0,4},{4,0},{8,12},{12,8},{1,5},{5,1},{9,13},{13,9},{2,6},{6,2},{1... | collective-permute-start | bytes 150536 | tf_op jit(solution)/shard_map/ppermute | solution.py:198
  92.3 4.6 %collective-permute-start.6 = (bf16[336,112]{1,0:T(8,128)(2,1)S(1)}, bf16[336,112]{1,0:T(8,128)(2,1)S(1)}, u32[]{:S(2)}, u32[]{:S(2)}) collective-permute-start(bf16[336,112]{1,0:T(8,128)(2,1)S(1)} %fusion), channel_id=1, source_target_pairs={{0,8},{4,12},{8,0},{12,4},{1,9},{5,13},{9,1},{13,5},{2,10},{6,14},... | collective-permute-start | bytes 225800 | tf_op jit(solution)/shard_map/ppermute | solution.py:198
  93.1 5.1 %collective-permute-start.16 = (bf16[336,112]{1,0:T(8,128)(2,1)S(1)}, bf16[336,112]{1,0:T(8,128)(2,1)S(1)}, u32[]{:S(2)}, u32[]{:S(2)}) collective-permute-start(bf16[336,112]{1,0:T(8,128)(2,1)S(1)} %fusion.1), channel_id=1, source_target_pairs={{0,8},{4,12},{8,0},{12,4},{1,9},{5,13},{9,1},{13,5},{2,10},{6,14},... | collective-permute-start | bytes 225800 | tf_op jit(solution)/shard_map/ppermute | solution.py:198
  96.9 2.5 %collective-permute-start.9 = (f32[560,112]{1,0:T(8,128)S(1)}, f32[560,112]{1,0:T(8,128)S(1)}, u32[]{:S(2)}, u32[]{:S(2)}) collective-permute-start(f32[560,112]{1,0:T(8,128)S(1)} %pad_maximum_fusion.state), channel_id=1, source_target_pairs={{0,16},{1,17},{2,18},{3,19},{4,20},{5,21},{6,22},{7,23},{8,24},{9,... | collective-permute-start | bytes 752648 | tf_op jit(solution)/shard_map/ppermute | solution.py:206

commit v5 on v4

--- a/solution.py
+++ b/solution.py
@@ -9,7 +9,7 @@
 
 HEAD_DIM = 112
 LANES = 128
-VMEM_LIMIT = 40 * 1024 * 1024
+VMEM_LIMIT = 20 * 1024 * 1024
 ANYWHERE = pl.BlockSpec(memory_space=pl.ANY)
 IN_VMEM = pl.BlockSpec(memory_space=pltpu.VMEM)
 IN_SMEM = pl.BlockSpec(memory_space=pltpu.SMEM)
@@ -24,7 +24,7 @@
         scratch_shapes=scratch,
         input_output_aliases=aliases or {},
         compiler_params=pltpu.CompilerParams(vmem_limit_bytes=VMEM_LIMIT),
-        cost_estimate=pl.CostEstimate(flops=flops, bytes_accessed=8 << 20, transcendentals=0),
+        cost_estimate=pl.CostEstimate(flops=flops // 64, bytes_accessed=1 << 10, transcendentals=0),
     )
 
 
@@ -65,22 +65,8 @@
         pltpu.make_async_copy(at(flip), at(flip), sems.at[flip]).wait()
 
 
-def whole_kernel(place, b0, b1, b2i, b2o, b3i, b3o, wq, wk, wv, query, state, whole, sems):
-    load_blocks(place, [b0, b1, (b2i, b2o), (b3i, b3o)], whole, sems)
-    state[...] = jnp.zeros_like(state)
-    width, tiles = token_tiles(whole.shape[1])
-
-    @pl.loop(0, tiles)
-    def _(tile):
-        columns = pl.ds(pl.multiple_of(tile * width, width), width)
-        block = whole[:, columns]
-        key = jnp.maximum(rounded_dot(wk[...], block).astype(jnp.bfloat16), 0)
-        value = rounded_dot(wv[...], block).astype(jnp.bfloat16)
-        add_state(state, key, value)
-        query[:, columns] = jnp.maximum(rounded_dot(wq[...], block).astype(jnp.bfloat16), 0)
-
-
-def partial_kernel(place, b0, b1, b2i, b2o, wq, wk, wv, tie, sums, whole, sems):
+def partial_kernel(place, b0, b1, b2i, b2o, wq, wk, wv, *rest):
+    sums, whole, sems = rest[-3:]
     rows, tokens = b0.shape
     missing = pl.ds(pl.multiple_of((place[0] ^ 3) * rows, 16), rows)
     whole[missing, :] = jnp.zeros((rows, tokens), whole.dtype)
@@ -124,7 +110,8 @@
             body(slice(low, high))
 
 
-def state_kernel(count, place, inner_ref, end_ref, wk, wv, sums, state, last, sems):
+def state_kernel(count, place, inner_ref, end_ref, wk, wv, sums, *rest):
+    state, last, sems = rest[-3:]
     state[...] = jnp.zeros_like(state)
     width, tiles = token_tiles(inner_ref.shape[1])
 
@@ -158,11 +145,11 @@
     last_block(place, inner_ref, end_ref, last, sems, count, body)
 
 
-def read_kernel(stream, prefix, state, query, gain, *rest):
+def read_kernel(stream, totals, query, gain, *rest):
     out, held, sem = rest[-3:]
     for start in range(0, query.shape[0], HEAD_DIM):
         rows = slice(start, start + HEAD_DIM)
-        total = (prefix[rows, :] + state[rows, :]).astype(jnp.bfloat16)
+        total = totals[rows, :].astype(jnp.bfloat16)
         reading = rounded_dot(total, query[rows, :])
         scale = lax.rsqrt(jnp.mean(reading * reading, axis=0, keepdims=True) + 1e-06)
         held[rows, :] = (reading * scale * gain[rows, :]).astype(jnp.bfloat16)
@@ -187,18 +174,13 @@
     return lax.ppermute(value, (other, axis), pairs)
 
 
-def sum_over(value, axis):
+def sum_over(value, axis, backwards):
     count = lax.axis_size(axis)
-    heads = value.shape[0] // HEAD_DIM
-    half = (heads + 1) // 2 * HEAD_DIM
     steps = [1 << b for b in range(count.bit_length() - 1)]
-    outs = []
-    for part, order in ((value[:half], steps), (value[half:], steps[::-1])):
-        for step in order:
-            sent = lax.ppermute(part.astype(jnp.bfloat16), axis, [(i, i ^ step) for i in range(count)])
-            part = part + sent.astype(jnp.float32)
-        outs.append(part)
-    return jnp.concatenate(outs, axis=0)
+    for step in steps[::-1] if backwards else steps:
+        sent = lax.ppermute(value.astype(jnp.bfloat16), axis, [(i, i ^ step) for i in range(count)])
+        value = value + sent.astype(jnp.float32)
+    return value
 
 
 def entering(value, axis):
@@ -241,36 +223,31 @@
     out_type = jax.ShapeDtypeStruct((2, width, tokens), jnp.bfloat16)
     one = 2 * width * depth * tokens
 
-    query0, state0 = call(
-        whole_kernel, (query_type, state_type), (IN_VMEM, IN_VMEM),
-        [IN_SMEM] + [ANYWHERE] * 6 + [IN_VMEM] * 3, [whole, sems], 3 * one,
-    )(place, own[0], near[0], far[0], across_end[0], across[0], far_end[0], *matrices)
-    state0 = sum_over(state0, "tok")
-    prefix = entering(state0, "group")
-
-    sums = call(
-        partial_kernel, jax.ShapeDtypeStruct((3, width, tokens), jnp.float32), IN_VMEM,
-        [IN_SMEM] + [ANYWHERE] * 4 + [IN_VMEM] * 3 + [ANYWHERE], [whole, sems], 3 * one,
-    )(place, own[1], near[1], far[1], across_end[1], *matrices, query0)
-
     read_scratch = [pltpu.VMEM((width, tokens), jnp.bfloat16), pltpu.SemaphoreType.DMA(())]
-    out = call(
-        functools.partial(read_kernel, 0), out_type, ANYWHERE, [IN_VMEM] * 4, read_scratch, one // 20,
-    )(prefix, state0, query0, gain_column)
-
-    state1 = call(
-        functools.partial(state_kernel, count), state_type, IN_VMEM,
-        [IN_SMEM] + [ANYWHERE] * 2 + [IN_VMEM] * 3, [last, sems], one // 2,
-    )(place, across[1], far_end[1], *matrices[1:], sums)
-    query1 = call(
-        functools.partial(query_kernel, count), query_type, IN_VMEM,
-        [IN_SMEM] + [ANYWHERE] * 2 + [IN_VMEM] * 2 + [ANYWHERE], [last, sems], one // 4,
-    )(place, across[1], far_end[1], matrices[0], sums, state1)
-    state1 = sum_over(state1, "tok")
-    out = call(
-        functools.partial(read_kernel, 1), out_type, ANYWHERE, [IN_VMEM] * 4 + [ANYWHERE], read_scratch,
-        one // 20, {4: 0},
-    )(prefix, state1, query1, gain_column, out)
+    prefix = query = out = None
+    for stream in range(2):
+        ties = (far[1], across[1]) if stream == 0 else ()
+        sums = call(
+            partial_kernel, jax.ShapeDtypeStruct((3, width, tokens), jnp.float32), IN_VMEM,
+            [IN_SMEM] + [ANYWHERE] * 4 + [IN_VMEM] * 3 + [ANYWHERE] * len(ties), [whole, sems], 3 * one,
+        )(place, own[stream], near[stream], far[stream], across_end[stream], *matrices, *ties)
+        ties = (across_end[1],) if stream == 0 else (prefix, query)
+        state = call(
+            functools.partial(state_kernel, count), state_type, IN_VMEM,
+            [IN_SMEM] + [ANYWHERE] * 2 + [IN_VMEM] * 3 + [ANYWHERE] * len(ties), [last, sems], one // 2,
+        )(place, across[stream], far_end[stream], *matrices[1:], sums, *ties)
+        query = call(
+            functools.partial(query_kernel, count), query_type, IN_VMEM,
+            [IN_SMEM] + [ANYWHERE] * 2 + [IN_VMEM] * 2 + [ANYWHERE], [last, sems], one // 4,
+        )(place, across[stream], far_end[stream], matrices[0], sums, state)
+        if stream == 0:
+            prefix = entering(state, "group")
+        total = sum_over(prefix + state, "tok", stream == 1)
+        kept = [] if out is None else [out]
+        out = call(
+            functools.partial(read_kernel, stream), out_type, ANYWHERE, [IN_VMEM] * 3 + [ANYWHERE] * len(kept),
+            read_scratch, one // 20, {3: 0} if kept else None,
+        )(total, query, gain_column, *kept)
     return jnp.swapaxes(out, 1, 2)
 
 

time: 102 us -> 100 us (0.980)
  starting transfers between devices: 41.4 us -> 37 us
  waiting for transfers between devices: 27.6 us -> 29.4 us
    pallas_call x3 -> x2, Pallas kernels: 11.9 us -> 2.45 us  [local(): call(functools.partial(read_kernel, stream), out_type, ANYWHERE, [IN_VMEM...]
    pallas_call x1 -> x2, Pallas kernels: 6.29 us -> 11.9 us  [local(): call(partial_kernel, jax.ShapeDtypeStruct((3, width, tokens), jnp.float32...]
    ppermute x8 -> x4, starting transfers between devices: 9.31 us -> 4.88 us  [sum_over(): lax.ppermute(value.astype(jnp.bfloat16), axis, [(i, i ^ step) for i in ra...]
    ppermute x8 -> x4, waiting for transfers between devices: 2.33 us -> 5.6 us  [sum_over(): lax.ppermute(value.astype(jnp.bfloat16), axis, [(i, i ^ step) for i in ra...]
    pallas_call x1 -> x2, Pallas kernels: 2.25 us -> 4.5 us  [local(): call(functools.partial(state_kernel, count), state_type, IN_VMEM, [IN_SME...]
    unnamed x20 -> x26, local copies, waits for them, and re-layouts: 8.01 us -> 9.78 us
    pallas_call x1 -> x2, Pallas kernels: 1.53 us -> 3.08 us  [local(): call(functools.partial(query_kernel, count), query_type, IN_VMEM, [IN_SME...]
    ppermute x1, waiting for transfers between devices: 1.08 us -> 0.01 us  [entering(): total = lax.ppermute(value, axis, [(i, i + 1) for i in range(count - 1)])]
  transfers between devices with their start and end apart: 19 -> 15, of which waited for: 6 -> 7; matrix products, arithmetic and copies ran while one was open for 1% -> 0% of each run, Pallas kernels for 19% -> 18%
where the time goes in v5:
time: 100 us
  starting transfers between devices  37 us (37%)
  waiting for transfers between devices  29.4 us (29%)
  Pallas kernels  21.9 us (22%)
  local copies, waits for them, and re-layouts  11.2 us (11%)
    ppermute x6, starting transfers between devices, partner_swap(): lax.ppermute(value, axis, [(i, i ^ 1) for i in range(lax.axis_size(axis))])  30.2 us
    ppermute x6, waiting for transfers between devices, partner_swap(): lax.ppermute(value, axis, [(i, i ^ 1) for i in range(lax.axis_size(axis))])  23.7 us
    pallas_call x2, Pallas kernels, local(): call(partial_kernel, jax.ShapeDtypeStruct((3, width, tokens), jnp.float32...  11.9 us
    unnamed x26, local copies, waits for them, and re-layouts  9.78 us
    ppermute x4, waiting for transfers between devices, sum_over(): lax.ppermute(value.astype(jnp.bfloat16), axis, [(i, i ^ step) for i in ra...  5.6 us
    ppermute x4, starting transfers between devices, sum_over(): lax.ppermute(value.astype(jnp.bfloat16), axis, [(i, i ^ step) for i in ra...  4.88 us
    pallas_call x2, Pallas kernels, local(): call(functools.partial(state_kernel, count), state_type, IN_VMEM, [IN_SME...  4.5 us
    pallas_call x2, Pallas kernels, local(): call(functools.partial(query_kernel, count), query_type, IN_VMEM, [IN_SME...  3.08 us
  transfers between devices with their start and end apart: 15, of which 7 were waited for; matrix products, arithmetic and copies ran while one was open for 0% of the time, Pallas kernels for 18%

profile of v5, /device:TPU:0, one launch (start us, length us, event | category | flops | bytes accessed | tf_op | source)
XLA Modules:
  0.0 100.0 jit_solution(937907578272731758)
XLA Ops:
  0.0 1.3 %slice_bitcast_fusion = (bf16[560,512]{1,0:T(8,128)(2,1)S(1)}, bf16[560,512]{1,0:T(8,128)(2,1)S(1)}) fusion(bf16[2,560,512]{2,1,0:T(8,128)(2,1)} %bitcast.23), kind=kLoop, calls=%fused_computation | loop fusion | bytes 2293760 | tf_op jit(solution)/shard_map/squeeze | solution.py:209
  1.3 3.1 %collective-permute-start.1 = (bf16[560,512]{1,0:T(8,128)(2,1)S(1)}, bf16[560,512]{1,0:T(8,128)(2,1)S(1)}, u32[]{:S(2)}, u32[]{:S(2)}) collective-permute-start(bf16[560,512]{1,0:T(8,128)(2,1)S(1)} %get-tuple-element.10.b0), channel_id=1, source_target_pairs={{0,1},{1,0},{2,3},{3,2},{4,5},{5,4},{6,7},{7,6},{8,9},{9,8},{10,11... | collective-permute-start | bytes 1720328 | tf_op jit(solution)/shard_map/ppermute | solution.py:162
  4.5 0.8 copy-done.6
  5.8 12.4 %collective-permute-done.1.b1 = bf16[560,512]{1,0:T(8,128)(2,1)S(1)} collective-permute-done((bf16[560,512]{1,0:T(8,128)(2,1)S(1)}, bf16[560,512]{1,0:T(8,128)(2,1)S(1)}, u32[]{:S(2)}, u32[]{:S(2)}) %collective-permute-start.1) | collective-permute-done | bytes 573472 | tf_op jit(solution)/shard_map/ppermute | solution.py:162
  18.2 0.8 copy-done.10
  19.0 10.6 %collective-permute-done.5.b1 = bf16[560,512]{1,0:T(8,128)(2,1)S(1)} collective-permute-done((bf16[560,512]{1,0:T(8,128)(2,1)S(1)}, bf16[560,512]{1,0:T(8,128)(2,1)S(1)}, u32[]{:S(2)}, u32[]{:S(2)}) %collective-permute-start.5) | collective-permute-done | bytes 573472 | tf_op jit(solution)/shard_map/ppermute | solution.py:162
  29.7 0.8 copy-done.8
  30.5 3.3 %collective-permute-start.4 = (bf16[560,512]{1,0:T(8,128)(2,1)S(1)}, bf16[560,512]{1,0:T(8,128)(2,1)}, u32[]{:S(2)}, u32[]{:S(2)}) collective-permute-start(bf16[560,512]{1,0:T(8,128)(2,1)S(1)} %collective-permute-done.inner_ref), channel_id=1, source_target_pairs={{0,1},{1,0},{2,3},{3,2},{4,5},{5,4},{6,7},{7,6},{8,9},{9,8},{10,11... | collective-permute-start | bytes 1720328 | tf_op jit(solution)/shard_map/ppermute | solution.py:162
  33.8 0.8 collective-permute-start.8
  34.6 12.4 %collective-permute-start.3 = (bf16[560,512]{1,0:T(8,128)(2,1)}, bf16[560,512]{1,0:T(8,128)(2,1)S(1)}, u32[]{:S(2)}, u32[]{:S(2)}) collective-permute-start(bf16[560,512]{1,0:T(8,128)(2,1)} %collective-permute-done.2.b2i), channel_id=1, source_target_pairs={{0,1},{1,0},{2,3},{3,2},{4,5},{5,4},{6,7},{7,6},{8,9},{9,8},{10,11... | collective-permute-start | bytes 1720328 | tf_op jit(solution)/shard_map/ppermute | solution.py:162
  47.0 10.5 %collective-permute-start.10 = (bf16[560,512]{1,0:T(8,128)(2,1)}, bf16[560,512]{1,0:T(8,128)(2,1)S(1)}, u32[]{:S(2)}, u32[]{:S(2)}) collective-permute-start(bf16[560,512]{1,0:T(8,128)(2,1)} %collective-permute-done.6.rest_0_.b2i), channel_id=1, source_target_pairs={{0,1},{1,0},{2,3},{3,2},{4,5},{5,4},{6,7},{7,6},{8,9},{9,8},{10,11... | collective-permute-start | bytes 1720328 | tf_op jit(solution)/shard_map/ppermute | solution.py:162
  57.6 1.7 %copy-done = bf16[2240,560]{0,1:T(8,128)(2,1)S(1)} copy-done((bf16[2240,560]{0,1:T(8,128)(2,1)S(1)}, bf16[2240,560]{0,1:T(8,128)(2,1)}, u32[]{:S(2)}) %copy-start) | copy-done | bytes 2508824
  59.4 1.7 %copy-done.2 = bf16[2240,560]{0,1:T(8,128)(2,1)S(1)} copy-done((bf16[2240,560]{0,1:T(8,128)(2,1)S(1)}, bf16[2240,560]{0,1:T(8,128)(2,1)}, u32[]{:S(2)}) %copy-start.2) | copy-done | bytes 2508824
  61.1 1.7 %copy-done.4 = bf16[2240,560]{0,1:T(8,128)(2,1)S(1)} copy-done((bf16[2240,560]{0,1:T(8,128)(2,1)S(1)}, bf16[2240,560]{0,1:T(8,128)(2,1)}, u32[]{:S(2)}) %copy-start.4) | copy-done | bytes 2508824
  62.8 1.1 %copy-done.7 = bf16[560,512]{1,0:T(8,128)(2,1)S(1)} copy-done((bf16[560,512]{1,0:T(8,128)(2,1)S(1)}, bf16[560,512]{1,0:T(8,128)(2,1)}, u32[]{:S(2)}) %copy-start.7) | copy-done | bytes 573464
  63.9 1.1 %copy-done.11 = bf16[560,512]{1,0:T(8,128)(2,1)S(1)} copy-done((bf16[560,512]{1,0:T(8,128)(2,1)S(1)}, bf16[560,512]{1,0:T(8,128)(2,1)}, u32[]{:S(2)}) %copy-start.11) | copy-done | bytes 573464
  64.9 6.6 %shard_map.55.sums = f32[3,560,512]{2,1,0:T(8,128)S(1)} custom-call(s32[2]{0:T(128)S(1)} %pad_add_fusion.place, bf16[560,512]{1,0:T(8,128)(2,1)S(1)} %copy-done.7, bf16[560,512]{1,0:T(8,128)(2,1)S(1)} %copy-done.11, bf16[560,512]{1,0:T(8,128)(2,1)} %collective-permute-done.2.b2i, bf16[560,512]{1,0:T(8,128)(2,1)} %collective-permute-done.4.b2o, ...), custom_call_target="tpu_custom_call" | custom-call | flops 60211200 | bytes 1024 | tf_op jit(solution)/shard_map/pallas_call | solution.py:230
  71.6 0.7 collective-permute-done.3.end_ref
  72.3 2.3 %shard_map.56.tie = f32[560,112]{1,0:T(8,128)S(1)} custom-call(s32[2]{0:T(128)S(1)} %pad_add_fusion.place, bf16[560,512]{1,0:T(8,128)(2,1)S(1)} %collective-permute-done.inner_ref, bf16[560,512]{1,0:T(8,128)(2,1)S(1)} %collective-permute-done.3.end_ref, bf16[560,2240]{1,0:T(8,128)(2,1)S(1)} %bitcast.12, bf16[560,2240]{1,0:T(8,128)(2,1)S(1)} %bitcast.16, ...), custom_call_target="tpu_custom_call" | custom-call | flops 10035200 | bytes 1024 | tf_op jit(solution)/shard_map/pallas_call | solution.py:235
  74.6 1.4 %collective-permute-start.9 = (f32[560,112]{1,0:T(8,128)S(1)}, f32[560,112]{1,0:T(8,128)S(1)}, u32[]{:S(2)}, u32[]{:S(2)}) collective-permute-start(f32[560,112]{1,0:T(8,128)S(1)} %shard_map.56.tie), channel_id=1, source_target_pairs={{0,16},{1,17},{2,18},{3,19},{4,20},{5,21},{6,22},{7,23},{8,24},{9,... | collective-permute-start | bytes 752648 | tf_op jit(solution)/shard_map/ppermute | solution.py:188
  76.0 5.3 %shard_map.57.sums = f32[3,560,512]{2,1,0:T(8,128)S(1)} custom-call(s32[2]{0:T(128)S(1)} %pad_add_fusion.place, bf16[560,512]{1,0:T(8,128)(2,1)S(1)} %get-tuple-element.9.b0, bf16[560,512]{1,0:T(8,128)(2,1)S(1)} %copy-done.9, bf16[560,512]{1,0:T(8,128)(2,1)} %collective-permute-done.6.rest_0_.b2i, bf16[560,512]{1,0:T(8,128)(2,1)S(1)} %collective-permute-done.8.rest_0_.b2o, ...), custom_call_target="tpu_custom_call" | custom-call | flops 60211200 | bytes 1024 | tf_op jit(solution)/shard_map/pallas_call | solution.py:230
  81.3 1.5 %shard_map.58.rest_1_.query = bf16[560,512]{1,0:T(8,128)(2,1)S(1)} custom-call(s32[2]{0:T(128)S(1)} %pad_add_fusion.place, bf16[560,512]{1,0:T(8,128)(2,1)S(1)} %collective-permute-done.inner_ref, bf16[560,512]{1,0:T(8,128)(2,1)S(1)} %collective-permute-done.3.end_ref, bf16[560,2240]{1,0:T(8,128)(2,1)S(1)} %bitcast.21, f32[3,560,512]{2,1,0:T(8,128)S(1)} %shard_map.55.sums, ...), custom_call_target="tpu_custom_call" | custom-call | flops 5017600 | bytes 1024 | tf_op jit(solution)/shard_map/pallas_call | solution.py:239
  82.9 2.3 %shard_map.59.tie = f32[560,112]{1,0:T(8,128)S(1)} custom-call(s32[2]{0:T(128)S(1)} %pad_add_fusion.place, bf16[560,512]{1,0:T(8,128)(2,1)S(1)} %collective-permute-done.7.rest_1_.inner_ref, bf16[560,512]{1,0:T(8,128)(2,1)S(1)} %collective-permute-done.10.end_ref, bf16[560,2240]{1,0:T(8,128)(2,1)S(1)} %bitcast.14, bf16[560,2240]{1,0:T(8,128)(2,1)S(1)} %bitcast.18, ...), custom_call_target="tpu_custom_call" | custom-call | flops 10035200 | bytes 1024 | tf_op jit(solution)/shard_map/pallas_call | solution.py:235
  85.2 1.6 %collective-permute-start.13 = (bf16[560,112]{1,0:T(8,128)(2,1)S(1)}, bf16[560,112]{1,0:T(8,128)(2,1)S(1)}, u32[]{:S(2)}, u32[]{:S(2)}) collective-permute-start(bf16[560,112]{1,0:T(8,128)(2,1)S(1)} %get-tuple-element.5), channel_id=1, source_target_pairs={{0,4},{4,0},{8,12},{12,8},{1,5},{5,1},{9,13},{13,9},{2,6},{6,2},{1... | collective-permute-start | bytes 376328 | tf_op jit(solution)/shard_map/ppermute | solution.py:181
  87.0 1.6 %collective-permute-start.11 = (bf16[560,112]{1,0:T(8,128)(2,1)S(1)}, bf16[560,112]{1,0:T(8,128)(2,1)S(1)}, u32[]{:S(2)}, u32[]{:S(2)}) collective-permute-start(bf16[560,112]{1,0:T(8,128)(2,1)S(1)} %get-tuple-element.11), channel_id=1, source_target_pairs={{0,8},{4,12},{8,0},{12,4},{1,9},{5,13},{9,1},{13,5},{2,10},{6,14},... | collective-permute-start | bytes 376328 | tf_op jit(solution)/shard_map/ppermute | solution.py:181
  88.5 1.5 %shard_map.60.query = bf16[560,512]{1,0:T(8,128)(2,1)S(1)} custom-call(s32[2]{0:T(128)S(1)} %pad_add_fusion.place, bf16[560,512]{1,0:T(8,128)(2,1)S(1)} %collective-permute-done.7.rest_1_.inner_ref, bf16[560,512]{1,0:T(8,128)(2,1)S(1)} %collective-permute-done.10.end_ref, bf16[560,2240]{1,0:T(8,128)(2,1)S(1)} %bitcast.22, ...), custom_call_target="tpu_custom_call" | custom-call | flops 5017600 | bytes 1024 | tf_op jit(solution)/shard_map/pallas_call | solution.py:239
  90.4 1.6 %collective-permute-start.14 = (bf16[560,112]{1,0:T(8,128)(2,1)S(1)}, bf16[560,112]{1,0:T(8,128)(2,1)S(1)}, u32[]{:S(2)}, u32[]{:S(2)}) collective-permute-start(bf16[560,112]{1,0:T(8,128)(2,1)S(1)} %fusion.1), channel_id=1, source_target_pairs={{0,8},{4,12},{8,0},{12,4},{1,9},{5,13},{9,1},{13,5},{2,10},{6,14},... | collective-permute-start | bytes 376328 | tf_op jit(solution)/shard_map/ppermute | solution.py:181
  92.0 1.5 %collective-permute-done.11 = bf16[560,112]{1,0:T(8,128)(2,1)S(1)} collective-permute-done((bf16[560,112]{1,0:T(8,128)(2,1)S(1)}, bf16[560,112]{1,0:T(8,128)(2,1)S(1)}, u32[]{:S(2)}, u32[]{:S(2)}) %collective-permute-start.11) | collective-permute-done | bytes 125472 | tf_op jit(solution)/shard_map/ppermute | solution.py:181
  93.7 1.9 %collective-permute-done.14 = bf16[560,112]{1,0:T(8,128)(2,1)S(1)} collective-permute-done((bf16[560,112]{1,0:T(8,128)(2,1)S(1)}, bf16[560,112]{1,0:T(8,128)(2,1)S(1)}, u32[]{:S(2)}, u32[]{:S(2)}) %collective-permute-start.14) | collective-permute-done | bytes 125472 | tf_op jit(solution)/shard_map/ppermute | solution.py:181
  95.6 1.2 %shard_map.61.rest_0_ = bf16[2,560,512]{2,1,0:T(8,128)(2,1)} custom-call(f32[560,112]{1,0:T(8,128)S(1)} %convert_add_fusion.totals, bf16[560,512]{1,0:T(8,128)(2,1)S(1)} %shard_map.58.rest_1_.query, f32[560,1]{1,0:T(8,128)S(1)} %reshape.5.gain), custom_call_target="tpu_custom_call" | custom-call | flops 1003520 | bytes 1024 | tf_op jit(solution)/shard_map/pallas_call | solution.py:247
  96.9 1.9 %collective-permute-done.12 = bf16[560,112]{1,0:T(8,128)(2,1)S(1)} collective-permute-done((bf16[560,112]{1,0:T(8,128)(2,1)S(1)}, bf16[560,112]{1,0:T(8,128)(2,1)S(1)}, u32[]{:S(2)}, u32[]{:S(2)}) %collective-permute-start.12) | collective-permute-done | bytes 125472 | tf_op jit(solution)/shard_map/ppermute | solution.py:181
  98.8 1.2 %shard_map.62 = bf16[2,560,512]{2,1,0:T(8,128)(2,1)} custom-call(f32[560,112]{1,0:T(8,128)S(1)} %convert_add_fusion.2.totals, bf16[560,512]{1,0:T(8,128)(2,1)S(1)} %shard_map.60.query, f32[560,1]{1,0:T(8,128)S(1)} %reshape.5.gain, bf16[2,560,512]{2,1,0:T(8,128)(2,1)} %shard_map.61.rest_0_), custom_call_target="tpu_custom_call", output_to_operand_aliasing={{}: (3, {})} | custom-call | flops 1003520 | bytes 1024 | tf_op jit(solution)/shard_map/pallas_call | solution.py:247
  (40 shorter events, 1.5 us)
Async XLA Ops:
  1.3 16.9 %collective-permute-start.1 = (bf16[560,512]{1,0:T(8,128)(2,1)S(1)}, bf16[560,512]{1,0:T(8,128)(2,1)S(1)}, u32[]{:S(2)}, u32[]{:S(2)}) collective-permute-start(bf16[560,512]{1,0:T(8,128)(2,1)S(1)} %get-tuple-element.10.b0), channel_id=1, source_target_pairs={{0,1},{1,0},{2,3},{3,2},{4,5},{5,4},{6,7},{7,6},{8,9},{9,8},{10,11... | collective-permute-start | bytes 1720328 | tf_op jit(solution)/shard_map/ppermute | solution.py:162
  4.4 25.3 %collective-permute-start.5 = (bf16[560,512]{1,0:T(8,128)(2,1)S(1)}, bf16[560,512]{1,0:T(8,128)(2,1)S(1)}, u32[]{:S(2)}, u32[]{:S(2)}) collective-permute-start(bf16[560,512]{1,0:T(8,128)(2,1)S(1)} %get-tuple-element.9.b0), channel_id=1, source_target_pairs={{0,1},{1,0},{2,3},{3,2},{4,5},{5,4},{6,7},{7,6},{8,9},{9,8},{10,11... | collective-permute-start | bytes 1720328 | tf_op jit(solution)/shard_map/ppermute | solution.py:162
  4.5 26.0 %collective-permute-start = (bf16[560,512]{1,0:T(8,128)(2,1)S(1)}, bf16[560,512]{1,0:T(8,128)(2,1)S(1)}, u32[]{:S(2)}, u32[]{:S(2)}) collective-permute-start(bf16[560,512]{1,0:T(8,128)(2,1)S(1)} %get-tuple-element.10.b0), channel_id=1, source_target_pairs={{0,16},{1,2},{2,1},{3,19},{16,0},{17,18},{18,17},{19,3},{4,20},{5,... | collective-permute-start | bytes 1720328 | tf_op jit(solution)/shard_map/ppermute | solution.py:174
  4.5 0.8 copy-start.6
  5.3 28.5 %collective-permute-start.7 = (bf16[560,512]{1,0:T(8,128)(2,1)S(1)}, bf16[560,512]{1,0:T(8,128)(2,1)S(1)}, u32[]{:S(2)}, u32[]{:S(2)}) collective-permute-start(bf16[560,512]{1,0:T(8,128)(2,1)S(1)} %get-tuple-element.9.b0), channel_id=1, source_target_pairs={{0,16},{1,2},{2,1},{3,19},{16,0},{17,18},{18,17},{19,3},{4,20},{5,... | collective-permute-start | bytes 1720328 | tf_op jit(solution)/shard_map/ppermute | solution.py:174
  18.2 16.4 %collective-permute-start.2 = (bf16[560,512]{1,0:T(8,128)(2,1)S(1)}, bf16[560,512]{1,0:T(8,128)(2,1)}, u32[]{:S(2)}, u32[]{:S(2)}) collective-permute-start(bf16[560,512]{1,0:T(8,128)(2,1)S(1)} %collective-permute-done.1.b1), channel_id=1, source_target_pairs={{0,16},{1,2},{2,1},{3,19},{16,0},{17,18},{18,17},{19,3},{4,20},{5,... | collective-permute-start | bytes 1720328 | tf_op jit(solution)/shard_map/ppermute | solution.py:174
  18.2 0.8 copy-start.10
  29.7 17.4 %collective-permute-start.6 = (bf16[560,512]{1,0:T(8,128)(2,1)S(1)}, bf16[560,512]{1,0:T(8,128)(2,1)}, u32[]{:S(2)}, u32[]{:S(2)}) collective-permute-start(bf16[560,512]{1,0:T(8,128)(2,1)S(1)} %collective-permute-done.5.b1), channel_id=1, source_target_pairs={{0,16},{1,2},{2,1},{3,19},{16,0},{17,18},{18,17},{19,3},{4,20},{5,... | collective-permute-start | bytes 1720328 | tf_op jit(solution)/shard_map/ppermute | solution.py:174
  29.7 0.8 copy-start.8
  30.5 27.1 %collective-permute-start.4 = (bf16[560,512]{1,0:T(8,128)(2,1)S(1)}, bf16[560,512]{1,0:T(8,128)(2,1)}, u32[]{:S(2)}, u32[]{:S(2)}) collective-permute-start(bf16[560,512]{1,0:T(8,128)(2,1)S(1)} %collective-permute-done.inner_ref), channel_id=1, source_target_pairs={{0,1},{1,0},{2,3},{3,2},{4,5},{5,4},{6,7},{7,6},{8,9},{9,8},{10,11... | collective-permute-start | bytes 1720328 | tf_op jit(solution)/shard_map/ppermute | solution.py:162
  33.8 37.8 %collective-permute-start.8 = (bf16[560,512]{1,0:T(8,128)(2,1)S(1)}, bf16[560,512]{1,0:T(8,128)(2,1)S(1)}, u32[]{:S(2)}, u32[]{:S(2)}) collective-permute-start(bf16[560,512]{1,0:T(8,128)(2,1)S(1)} %collective-permute-done.7.rest_1_.inner_ref), channel_id=1, source_target_pairs={{0,1},{1,0},{2,3},{3,2},{4,5},{5,4},{6,7},{7,6},{8,9},{9,8},{10,11... | collective-permute-start | bytes 1720328 | tf_op jit(solution)/shard_map/ppermute | solution.py:162
  34.6 37.6 %collective-permute-start.3 = (bf16[560,512]{1,0:T(8,128)(2,1)}, bf16[560,512]{1,0:T(8,128)(2,1)S(1)}, u32[]{:S(2)}, u32[]{:S(2)}) collective-permute-start(bf16[560,512]{1,0:T(8,128)(2,1)} %collective-permute-done.2.b2i), channel_id=1, source_target_pairs={{0,1},{1,0},{2,3},{3,2},{4,5},{5,4},{6,7},{7,6},{8,9},{9,8},{10,11... | collective-permute-start | bytes 1720328 | tf_op jit(solution)/shard_map/ppermute | solution.py:162
  47.0 35.8 %collective-permute-start.10 = (bf16[560,512]{1,0:T(8,128)(2,1)}, bf16[560,512]{1,0:T(8,128)(2,1)S(1)}, u32[]{:S(2)}, u32[]{:S(2)}) collective-permute-start(bf16[560,512]{1,0:T(8,128)(2,1)} %collective-permute-done.6.rest_0_.b2i), channel_id=1, source_target_pairs={{0,1},{1,0},{2,3},{3,2},{4,5},{5,4},{6,7},{7,6},{8,9},{9,8},{10,11... | collective-permute-start | bytes 1720328 | tf_op jit(solution)/shard_map/ppermute | solution.py:162
  57.6 1.7 %copy-start = (bf16[2240,560]{0,1:T(8,128)(2,1)S(1)}, bf16[2240,560]{0,1:T(8,128)(2,1)}, u32[]{:S(2)}) copy-start(bf16[2240,560]{0,1:T(8,128)(2,1)} %param.7) | copy-start | bytes 7526404
  59.4 1.7 %copy-start.2 = (bf16[2240,560]{0,1:T(8,128)(2,1)S(1)}, bf16[2240,560]{0,1:T(8,128)(2,1)}, u32[]{:S(2)}) copy-start(bf16[2240,560]{0,1:T(8,128)(2,1)} %param.8) | copy-start | bytes 7526404
  61.1 1.7 %copy-start.4 = (bf16[2240,560]{0,1:T(8,128)(2,1)S(1)}, bf16[2240,560]{0,1:T(8,128)(2,1)}, u32[]{:S(2)}) copy-start(bf16[2240,560]{0,1:T(8,128)(2,1)} %param.6) | copy-start | bytes 7526404
  62.8 1.1 %copy-start.7 = (bf16[560,512]{1,0:T(8,128)(2,1)S(1)}, bf16[560,512]{1,0:T(8,128)(2,1)}, u32[]{:S(2)}) copy-start(bf16[560,512]{1,0:T(8,128)(2,1)} %copy-done.6) | copy-start | bytes 1720324
  63.9 1.1 %copy-start.11 = (bf16[560,512]{1,0:T(8,128)(2,1)S(1)}, bf16[560,512]{1,0:T(8,128)(2,1)}, u32[]{:S(2)}) copy-start(bf16[560,512]{1,0:T(8,128)(2,1)} %copy-done.10) | copy-start | bytes 1720324
  64.9 7.3 %copy-start.1 = (bf16[2240,560]{0,1:T(8,128)(2,1)S(1)}, bf16[2240,560]{0,1:T(8,128)(2,1)}, u32[]{:S(2)}) copy-start(bf16[2240,560]{0,1:T(8,128)(2,1)} %param.7) | copy-start | bytes 7526404
  64.9 7.3 %copy-start.3 = (bf16[2240,560]{0,1:T(8,128)(2,1)S(1)}, bf16[2240,560]{0,1:T(8,128)(2,1)}, u32[]{:S(2)}) copy-start(bf16[2240,560]{0,1:T(8,128)(2,1)} %param.8) | copy-start | bytes 7526404
  71.6 4.4 %copy-start.9 = (bf16[560,512]{1,0:T(8,128)(2,1)S(1)}, bf16[560,512]{1,0:T(8,128)(2,1)}, u32[]{:S(2)}) copy-start(bf16[560,512]{1,0:T(8,128)(2,1)} %copy-done.8) | copy-start | bytes 1720324
  74.5 6.7 %copy-start.5 = (bf16[2240,560]{0,1:T(8,128)(2,1)S(1)}, bf16[2240,560]{0,1:T(8,128)(2,1)}, u32[]{:S(2)}) copy-start(bf16[2240,560]{0,1:T(8,128)(2,1)} %param.6) | copy-start | bytes 7526404
  74.6 8.3 %collective-permute-start.9 = (f32[560,112]{1,0:T(8,128)S(1)}, f32[560,112]{1,0:T(8,128)S(1)}, u32[]{:S(2)}, u32[]{:S(2)}) collective-permute-start(f32[560,112]{1,0:T(8,128)S(1)} %shard_map.56.tie), channel_id=1, source_target_pairs={{0,16},{1,17},{2,18},{3,19},{4,20},{5,21},{6,22},{7,23},{8,24},{9,... | collective-permute-start | bytes 752648 | tf_op jit(solution)/shard_map/ppermute | solution.py:188
  82.8 4.0 %copy-start.12 = (f32[560]{0:T(1024)S(1)}, f32[560]{0:T(1024)}, u32[]{:S(2)}) copy-start(f32[560]{0:T(1024)} %param.9) | copy-start | bytes 6724
  85.2 5.2 %collective-permute-start.13 = (bf16[560,112]{1,0:T(8,128)(2,1)S(1)}, bf16[560,112]{1,0:T(8,128)(2,1)S(1)}, u32[]{:S(2)}, u32[]{:S(2)}) collective-permute-start(bf16[560,112]{1,0:T(8,128)(2,1)S(1)} %get-tuple-element.5), channel_id=1, source_target_pairs={{0,4},{4,0},{8,12},{12,8},{1,5},{5,1},{9,13},{13,9},{2,6},{6,2},{1... | collective-permute-start | bytes 376328 | tf_op jit(solution)/shard_map/ppermute | solution.py:181
  87.0 6.6 %collective-permute-start.11 = (bf16[560,112]{1,0:T(8,128)(2,1)S(1)}, bf16[560,112]{1,0:T(8,128)(2,1)S(1)}, u32[]{:S(2)}, u32[]{:S(2)}) collective-permute-start(bf16[560,112]{1,0:T(8,128)(2,1)S(1)} %get-tuple-element.11), channel_id=1, source_target_pairs={{0,8},{4,12},{8,0},{12,4},{1,9},{5,13},{9,1},{13,5},{2,10},{6,14},... | collective-permute-start | bytes 376328 | tf_op jit(solution)/shard_map/ppermute | solution.py:181
  90.4 5.2 %collective-permute-start.14 = (bf16[560,112]{1,0:T(8,128)(2,1)S(1)}, bf16[560,112]{1,0:T(8,128)(2,1)S(1)}, u32[]{:S(2)}, u32[]{:S(2)}) collective-permute-start(bf16[560,112]{1,0:T(8,128)(2,1)S(1)} %fusion.1), channel_id=1, source_target_pairs={{0,8},{4,12},{8,0},{12,4},{1,9},{5,13},{9,1},{13,5},{2,10},{6,14},... | collective-permute-start | bytes 376328 | tf_op jit(solution)/shard_map/ppermute | solution.py:181
  93.6 5.2 %collective-permute-start.12 = (bf16[560,112]{1,0:T(8,128)(2,1)S(1)}, bf16[560,112]{1,0:T(8,128)(2,1)S(1)}, u32[]{:S(2)}, u32[]{:S(2)}) collective-permute-start(bf16[560,112]{1,0:T(8,128)(2,1)S(1)} %fusion), channel_id=1, source_target_pairs={{0,4},{4,0},{8,12},{12,8},{1,5},{5,1},{9,13},{13,9},{2,6},{6,2},{1... | collective-permute-start | bytes 376328 | tf_op jit(solution)/shard_map/ppermute | solution.py:181

commit v6 on v5

--- a/solution.py
+++ b/solution.py
@@ -65,8 +65,7 @@
         pltpu.make_async_copy(at(flip), at(flip), sems.at[flip]).wait()
 
 
-def partial_kernel(place, b0, b1, b2i, b2o, wq, wk, wv, *rest):
-    sums, whole, sems = rest[-3:]
+def partial_kernel(place, b0, b1, b2i, b2o, wq, wk, wv, sums, whole, sems):
     rows, tokens = b0.shape
     missing = pl.ds(pl.multiple_of((place[0] ^ 3) * rows, 16), rows)
     whole[missing, :] = jnp.zeros((rows, tokens), whole.dtype)
@@ -211,10 +210,8 @@
         across.append(middle_swap(own[stream], "head", "group"))
     for stream in range(2):
         far.append(middle_swap(near[stream], "head", "group"))
-        across_end.append(partner_swap(across[stream], "head"))
-    for stream in range(2):
-        far_end.append(partner_swap(far[stream], "head"))
-
+        ready, _ = lax.optimization_barrier((across[stream], near[stream]))
+        across_end.append(partner_swap(ready, "head"))
     whole = pltpu.VMEM((depth, tokens), jnp.bfloat16)
     sems = pltpu.SemaphoreType.DMA((4,))
     last = pltpu.VMEM((-(-(rows + LANES) // LANES) * LANES, tokens), jnp.bfloat16)
@@ -224,22 +221,25 @@
     one = 2 * width * depth * tokens
 
     read_scratch = [pltpu.VMEM((width, tokens), jnp.bfloat16), pltpu.SemaphoreType.DMA(())]
+    sums = []
+    for stream in range(2):
+        ready, *_ = lax.optimization_barrier((far[stream], across_end[stream], *sums))
+        far_end.append(partner_swap(ready, "head"))
+        sums.append(call(
+            partial_kernel, jax.ShapeDtypeStruct((3, width, tokens), jnp.float32), IN_VMEM,
+            [IN_SMEM] + [ANYWHERE] * 4 + [IN_VMEM] * 3, [whole, sems], 3 * one,
+        )(place, own[stream], near[stream], far[stream], across_end[stream], *matrices))
     prefix = query = out = None
     for stream in range(2):
-        ties = (far[1], across[1]) if stream == 0 else ()
-        sums = call(
-            partial_kernel, jax.ShapeDtypeStruct((3, width, tokens), jnp.float32), IN_VMEM,
-            [IN_SMEM] + [ANYWHERE] * 4 + [IN_VMEM] * 3 + [ANYWHERE] * len(ties), [whole, sems], 3 * one,
-        )(place, own[stream], near[stream], far[stream], across_end[stream], *matrices, *ties)
-        ties = (across_end[1],) if stream == 0 else (prefix, query)
+        ties = (sums[1],) if stream == 0 else (prefix, query)
         state = call(
             functools.partial(state_kernel, count), state_type, IN_VMEM,
             [IN_SMEM] + [ANYWHERE] * 2 + [IN_VMEM] * 3 + [ANYWHERE] * len(ties), [last, sems], one // 2,
-        )(place, across[stream], far_end[stream], *matrices[1:], sums, *ties)
+        )(place, across[stream], far_end[stream], *matrices[1:], sums[stream], *ties)
         query = call(
             functools.partial(query_kernel, count), query_type, IN_VMEM,
             [IN_SMEM] + [ANYWHERE] * 2 + [IN_VMEM] * 2 + [ANYWHERE], [last, sems], one // 4,
-        )(place, across[stream], far_end[stream], matrices[0], sums, state)
+        )(place, across[stream], far_end[stream], matrices[0], sums[stream], state)
         if stream == 0:
             prefix = entering(state, "group")
         total = sum_over(prefix + state, "tok", stream == 1)

time: 100 us -> 97.2 us (0.972)
  starting transfers between devices: 37 us -> 19.7 us
  waiting for transfers between devices: 29.4 us -> 44.7 us
    ppermute x6, starting transfers between devices: 30.2 us -> 12.6 us  [partner_swap(): lax.ppermute(value, axis, [(i, i ^ 1) for i in range(lax.axis_size(axis))])]
    ppermute x6, waiting for transfers between devices: 23.7 us -> 40 us  [partner_swap(): lax.ppermute(value, axis, [(i, i ^ 1) for i in range(lax.axis_size(axis))])]
    unnamed x26 -> x22, local copies, waits for them, and re-layouts: 9.78 us -> 8.94 us
  transfers between devices with their start and end apart: 15 -> 15, of which waited for: 7 -> 9; matrix products, arithmetic and copies ran while one was open for 0% -> 0% of each run, Pallas kernels for 18% -> 19%
where the time goes in v6:
time: 97.2 us; the launch traced here: 96.8 us
  waiting for transfers between devices  44.7 us (46%)
  Pallas kernels  21.5 us (22%)
  starting transfers between devices  19.7 us (20%)
  local copies, waits for them, and re-layouts  10.4 us (11%)
    ppermute x6, waiting for transfers between devices, partner_swap(): lax.ppermute(value, axis, [(i, i ^ 1) for i in range(lax.axis_size(axis))])  40 us
    ppermute x6, starting transfers between devices, partner_swap(): lax.ppermute(value, axis, [(i, i ^ 1) for i in range(lax.axis_size(axis))])  12.6 us
    pallas_call x2, Pallas kernels, local(): call(partial_kernel, jax.ShapeDtypeStruct((3, width, tokens), jnp.float32...  11.5 us
    unnamed x22, local copies, waits for them, and re-layouts  8.94 us
    ppermute x4, starting transfers between devices, sum_over(): lax.ppermute(value.astype(jnp.bfloat16), axis, [(i, i ^ step) for i in ra...  5.24 us
    ppermute x4, waiting for transfers between devices, sum_over(): lax.ppermute(value.astype(jnp.bfloat16), axis, [(i, i ^ step) for i in ra...  4.74 us
    pallas_call x2, Pallas kernels, local(): call(functools.partial(state_kernel, count), state_type, IN_VMEM, [IN_SME...  4.5 us
    pallas_call x2, Pallas kernels, local(): call(functools.partial(query_kernel, count), query_type, IN_VMEM, [IN_SME...  3.08 us
  transfers between devices with their start and end apart: 15, of which 9 were waited for; matrix products, arithmetic and copies ran while one was open for 0% of the time, Pallas kernels for 19%

profile of v6, /device:TPU:0, one launch (start us, length us, event | category | flops | bytes accessed | tf_op | source)
XLA Modules:
  0.0 96.8 jit_solution(14254980795408743559)
XLA Ops:
  0.0 1.3 %slice_bitcast_fusion = (bf16[560,512]{1,0:T(8,128)(2,1)S(1)}, bf16[560,512]{1,0:T(8,128)(2,1)S(1)}) fusion(bf16[2,560,512]{2,1,0:T(8,128)(2,1)} %bitcast.23), kind=kLoop, calls=%fused_computation | loop fusion | bytes 2293760 | tf_op jit(solution)/shard_map/squeeze | solution.py:208
  1.8 4.1 %collective-permute-start.1 = (bf16[560,512]{1,0:T(8,128)(2,1)S(1)}, bf16[560,512]{1,0:T(8,128)(2,1)S(1)}, u32[]{:S(2)}, u32[]{:S(2)}) collective-permute-start(bf16[560,512]{1,0:T(8,128)(2,1)S(1)} %get-tuple-element.18.b0), channel_id=1, source_target_pairs={{0,1},{1,0},{2,3},{3,2},{4,5},{5,4},{6,7},{7,6},{8,9},{9,8},{10,11... | collective-permute-start | bytes 1720328 | tf_op jit(solution)/shard_map/ppermute | solution.py:161
  6.0 13.8 %collective-permute-done.1.b1 = bf16[560,512]{1,0:T(8,128)(2,1)S(1)} collective-permute-done((bf16[560,512]{1,0:T(8,128)(2,1)S(1)}, bf16[560,512]{1,0:T(8,128)(2,1)S(1)}, u32[]{:S(2)}, u32[]{:S(2)}) %collective-permute-start.1) | collective-permute-done | bytes 573472 | tf_op jit(solution)/shard_map/ppermute | solution.py:161
  20.6 2.5 %collective-permute-start.3 = (bf16[560,512]{1,0:T(8,128)(2,1)S(1)}, bf16[560,512]{1,0:T(8,128)(2,1)S(1)}, u32[]{:S(2)}, u32[]{:S(2)}) collective-permute-start(bf16[560,512]{1,0:T(8,128)(2,1)S(1)} %collective-permute-done.inner_ref), channel_id=1, source_target_pairs={{0,1},{1,0},{2,3},{3,2},{4,5},{5,4},{6,7},{7,6},{8,9},{9,8},{10,11... | collective-permute-start | bytes 1720328 | tf_op jit(solution)/shard_map/ppermute | solution.py:161
  23.1 9.0 %collective-permute-done.5.b1 = bf16[560,512]{1,0:T(8,128)(2,1)S(1)} collective-permute-done((bf16[560,512]{1,0:T(8,128)(2,1)S(1)}, bf16[560,512]{1,0:T(8,128)(2,1)S(1)}, u32[]{:S(2)}, u32[]{:S(2)}) %collective-permute-start.5) | collective-permute-done | bytes 573472 | tf_op jit(solution)/shard_map/ppermute | solution.py:161
  32.1 2.5 %collective-permute-start.8 = (bf16[560,512]{1,0:T(8,128)(2,1)S(1)}, bf16[560,512]{1,0:T(8,128)(2,1)}, u32[]{:S(2)}, u32[]{:S(2)}) collective-permute-start(bf16[560,512]{1,0:T(8,128)(2,1)S(1)} %collective-permute-done.7.inner_ref), channel_id=1, source_target_pairs={{0,1},{1,0},{2,3},{3,2},{4,5},{5,4},{6,7},{7,6},{8,9},{9,8},{10,11... | collective-permute-start | bytes 1720328 | tf_op jit(solution)/shard_map/ppermute | solution.py:161
  34.6 9.8 %collective-permute-done.3.b2o = bf16[560,512]{1,0:T(8,128)(2,1)S(1)} collective-permute-done((bf16[560,512]{1,0:T(8,128)(2,1)S(1)}, bf16[560,512]{1,0:T(8,128)(2,1)S(1)}, u32[]{:S(2)}, u32[]{:S(2)}) %collective-permute-start.3) | collective-permute-done | bytes 573472 | tf_op jit(solution)/shard_map/ppermute | solution.py:161
  44.4 0.8 copy-done.8
  45.2 2.1 %collective-permute-start.4 = (bf16[560,512]{1,0:T(8,128)(2,1)}, bf16[560,512]{1,0:T(8,128)(2,1)S(1)}, u32[]{:S(2)}, u32[]{:S(2)}) collective-permute-start(bf16[560,512]{1,0:T(8,128)(2,1)} %collective-permute-done.2.b2i), channel_id=1, source_target_pairs={{0,1},{1,0},{2,3},{3,2},{4,5},{5,4},{6,7},{7,6},{8,9},{9,8},{10,11... | collective-permute-start | bytes 1720328 | tf_op jit(solution)/shard_map/ppermute | solution.py:161
  47.3 1.7 %copy-done = bf16[2240,560]{0,1:T(8,128)(2,1)S(1)} copy-done((bf16[2240,560]{0,1:T(8,128)(2,1)S(1)}, bf16[2240,560]{0,1:T(8,128)(2,1)}, u32[]{:S(2)}) %copy-start) | copy-done | bytes 2508824
  49.1 1.7 %copy-done.2 = bf16[2240,560]{0,1:T(8,128)(2,1)S(1)} copy-done((bf16[2240,560]{0,1:T(8,128)(2,1)S(1)}, bf16[2240,560]{0,1:T(8,128)(2,1)}, u32[]{:S(2)}) %copy-start.2) | copy-done | bytes 2508824
  50.8 1.7 %copy-done.4 = bf16[2240,560]{0,1:T(8,128)(2,1)S(1)} copy-done((bf16[2240,560]{0,1:T(8,128)(2,1)S(1)}, bf16[2240,560]{0,1:T(8,128)(2,1)}, u32[]{:S(2)}) %copy-start.4) | copy-done | bytes 2508824
  52.5 1.1 %copy-done.7 = bf16[560,512]{1,0:T(8,128)(2,1)S(1)} copy-done((bf16[560,512]{1,0:T(8,128)(2,1)S(1)}, bf16[560,512]{1,0:T(8,128)(2,1)}, u32[]{:S(2)}) %copy-start.7) | copy-done | bytes 573464
  53.6 1.1 %copy-done.9 = bf16[560,512]{1,0:T(8,128)(2,1)S(1)} copy-done((bf16[560,512]{1,0:T(8,128)(2,1)S(1)}, bf16[560,512]{1,0:T(8,128)(2,1)}, u32[]{:S(2)}) %copy-start.9) | copy-done | bytes 573464
  54.7 5.3 %shard_map.55.sums = f32[3,560,512]{2,1,0:T(8,128)S(1)} custom-call(s32[2]{0:T(128)S(1)} %pad_add_fusion.place, bf16[560,512]{1,0:T(8,128)(2,1)S(1)} %get-tuple-element.18.b0, bf16[560,512]{1,0:T(8,128)(2,1)S(1)} %copy-done.7, bf16[560,512]{1,0:T(8,128)(2,1)} %collective-permute-done.2.b2i, bf16[560,512]{1,0:T(8,128)(2,1)S(1)} %copy-done.9, ...), custom_call_target="tpu_custom_call" | custom-call | flops 60211200 | bytes 1024 | tf_op jit(solution)/shard_map/pallas_call | solution.py:228
  59.9 1.4 %collective-permute-start.10 = (bf16[560,512]{1,0:T(8,128)(2,1)}, bf16[560,512]{1,0:T(8,128)(2,1)S(1)}, u32[]{:S(2)}, u32[]{:S(2)}) collective-permute-start(bf16[560,512]{1,0:T(8,128)(2,1)} %collective-permute-done.6.b2i), channel_id=1, source_target_pairs={{0,1},{1,0},{2,3},{3,2},{4,5},{5,4},{6,7},{7,6},{8,9},{9,8},{10,11... | collective-permute-start | bytes 1720328 | tf_op jit(solution)/shard_map/ppermute | solution.py:161
  61.4 6.2 %shard_map.56.rest_0_.sums = f32[3,560,512]{2,1,0:T(8,128)S(1)} custom-call(s32[2]{0:T(128)S(1)} %pad_add_fusion.place, bf16[560,512]{1,0:T(8,128)(2,1)S(1)} %get-tuple-element.17.b0, bf16[560,512]{1,0:T(8,128)(2,1)S(1)} %collective-permute-done.5.b1, bf16[560,512]{1,0:T(8,128)(2,1)} %collective-permute-done.6.b2i, ...), custom_call_target="tpu_custom_call" | custom-call | flops 60211200 | bytes 1024 | tf_op jit(solution)/shard_map/pallas_call | solution.py:228
  67.6 1.4 %collective-permute-done.4.end_ref = bf16[560,512]{1,0:T(8,128)(2,1)S(1)} collective-permute-done((bf16[560,512]{1,0:T(8,128)(2,1)}, bf16[560,512]{1,0:T(8,128)(2,1)S(1)}, u32[]{:S(2)}, u32[]{:S(2)}) %collective-permute-start.4) | collective-permute-done | bytes 573472 | tf_op jit(solution)/shard_map/ppermute | solution.py:161
  69.0 2.2 %shard_map.57.tie = f32[560,112]{1,0:T(8,128)S(1)} custom-call(s32[2]{0:T(128)S(1)} %pad_add_fusion.place, bf16[560,512]{1,0:T(8,128)(2,1)S(1)} %collective-permute-done.inner_ref, bf16[560,512]{1,0:T(8,128)(2,1)S(1)} %collective-permute-done.4.end_ref, bf16[560,2240]{1,0:T(8,128)(2,1)S(1)} %bitcast.13, bf16[560,2240]{1,0:T(8,128)(2,1)S(1)} %bitcast.17, ...), custom_call_target="tpu_custom_call" | custom-call | flops 10035200 | bytes 1024 | tf_op jit(solution)/shard_map/pallas_call | solution.py:235
  71.2 1.3 %collective-permute-start.9 = (f32[560,112]{1,0:T(8,128)S(1)}, f32[560,112]{1,0:T(8,128)S(1)}, u32[]{:S(2)}, u32[]{:S(2)}) collective-permute-start(f32[560,112]{1,0:T(8,128)S(1)} %shard_map.57.tie), channel_id=1, source_target_pairs={{0,16},{1,17},{2,18},{3,19},{4,20},{5,21},{6,22},{7,23},{8,24},{9,... | collective-permute-start | bytes 752648 | tf_op jit(solution)/shard_map/ppermute | solution.py:187
  72.6 1.5 %shard_map.58.rest_1_.query = bf16[560,512]{1,0:T(8,128)(2,1)S(1)} custom-call(s32[2]{0:T(128)S(1)} %pad_add_fusion.place, bf16[560,512]{1,0:T(8,128)(2,1)S(1)} %collective-permute-done.inner_ref, bf16[560,512]{1,0:T(8,128)(2,1)S(1)} %collective-permute-done.4.end_ref, bf16[560,2240]{1,0:T(8,128)(2,1)S(1)} %bitcast.21, f32[3,560,512]{2,1,0:T(8,128)S(1)} %shard_map.55.sums, ...), custom_call_target="tpu_custom_call" | custom-call | flops 5017600 | bytes 1024 | tf_op jit(solution)/shard_map/pallas_call | solution.py:239
  74.1 6.0 %collective-permute-done.10.end_ref = bf16[560,512]{1,0:T(8,128)(2,1)S(1)} collective-permute-done((bf16[560,512]{1,0:T(8,128)(2,1)}, bf16[560,512]{1,0:T(8,128)(2,1)S(1)}, u32[]{:S(2)}, u32[]{:S(2)}) %collective-permute-start.10) | collective-permute-done | bytes 573472 | tf_op jit(solution)/shard_map/ppermute | solution.py:161
  80.1 2.3 %shard_map.59.tie = f32[560,112]{1,0:T(8,128)S(1)} custom-call(s32[2]{0:T(128)S(1)} %pad_add_fusion.place, bf16[560,512]{1,0:T(8,128)(2,1)S(1)} %collective-permute-done.7.inner_ref, bf16[560,512]{1,0:T(8,128)(2,1)S(1)} %collective-permute-done.10.end_ref, bf16[560,2240]{1,0:T(8,128)(2,1)S(1)} %bitcast.14, bf16[560,2240]{1,0:T(8,128)(2,1)S(1)} %bitcast.18, ...), custom_call_target="tpu_custom_call" | custom-call | flops 10035200 | bytes 1024 | tf_op jit(solution)/shard_map/pallas_call | solution.py:235
  82.5 1.6 %collective-permute-start.13 = (bf16[560,112]{1,0:T(8,128)(2,1)S(1)}, bf16[560,112]{1,0:T(8,128)(2,1)S(1)}, u32[]{:S(2)}, u32[]{:S(2)}) collective-permute-start(bf16[560,112]{1,0:T(8,128)(2,1)S(1)} %get-tuple-element.13), channel_id=1, source_target_pairs={{0,4},{4,0},{8,12},{12,8},{1,5},{5,1},{9,13},{13,9},{2,6},{6,2},{1... | collective-permute-start | bytes 376328 | tf_op jit(solution)/shard_map/ppermute | solution.py:180
  84.2 1.6 %collective-permute-start.11 = (bf16[560,112]{1,0:T(8,128)(2,1)S(1)}, bf16[560,112]{1,0:T(8,128)(2,1)S(1)}, u32[]{:S(2)}, u32[]{:S(2)}) collective-permute-start(bf16[560,112]{1,0:T(8,128)(2,1)S(1)} %get-tuple-element.19), channel_id=1, source_target_pairs={{0,8},{4,12},{8,0},{12,4},{1,9},{5,13},{9,1},{13,5},{2,10},{6,14},... | collective-permute-start | bytes 376328 | tf_op jit(solution)/shard_map/ppermute | solution.py:180
  85.7 1.5 %shard_map.60.query = bf16[560,512]{1,0:T(8,128)(2,1)S(1)} custom-call(s32[2]{0:T(128)S(1)} %pad_add_fusion.place, bf16[560,512]{1,0:T(8,128)(2,1)S(1)} %collective-permute-done.7.inner_ref, bf16[560,512]{1,0:T(8,128)(2,1)S(1)} %collective-permute-done.10.end_ref, bf16[560,2240]{1,0:T(8,128)(2,1)S(1)} %bitcast.22, ...), custom_call_target="tpu_custom_call" | custom-call | flops 5017600 | bytes 1024 | tf_op jit(solution)/shard_map/pallas_call | solution.py:239
  87.7 1.6 %collective-permute-start.14 = (bf16[560,112]{1,0:T(8,128)(2,1)S(1)}, bf16[560,112]{1,0:T(8,128)(2,1)S(1)}, u32[]{:S(2)}, u32[]{:S(2)}) collective-permute-start(bf16[560,112]{1,0:T(8,128)(2,1)S(1)} %fusion.1), channel_id=1, source_target_pairs={{0,8},{4,12},{8,0},{12,4},{1,9},{5,13},{9,1},{13,5},{2,10},{6,14},... | collective-permute-start | bytes 376328 | tf_op jit(solution)/shard_map/ppermute | solution.py:180
  89.3 1.0 %collective-permute-done.11 = bf16[560,112]{1,0:T(8,128)(2,1)S(1)} collective-permute-done((bf16[560,112]{1,0:T(8,128)(2,1)S(1)}, bf16[560,112]{1,0:T(8,128)(2,1)S(1)}, u32[]{:S(2)}, u32[]{:S(2)}) %collective-permute-start.11) | collective-permute-done | bytes 125472 | tf_op jit(solution)/shard_map/ppermute | solution.py:180
  90.8 2.0 %collective-permute-done.14 = bf16[560,112]{1,0:T(8,128)(2,1)S(1)} collective-permute-done((bf16[560,112]{1,0:T(8,128)(2,1)S(1)}, bf16[560,112]{1,0:T(8,128)(2,1)S(1)}, u32[]{:S(2)}, u32[]{:S(2)}) %collective-permute-start.14) | collective-permute-done | bytes 125472 | tf_op jit(solution)/shard_map/ppermute | solution.py:180
  92.9 1.2 %shard_map.61.rest_0_ = bf16[2,560,512]{2,1,0:T(8,128)(2,1)} custom-call(f32[560,112]{1,0:T(8,128)S(1)} %convert_add_fusion.totals, bf16[560,512]{1,0:T(8,128)(2,1)S(1)} %shard_map.58.rest_1_.query, f32[560,1]{1,0:T(8,128)S(1)} %reshape.5.gain), custom_call_target="tpu_custom_call" | custom-call | flops 1003520 | bytes 1024 | tf_op jit(solution)/shard_map/pallas_call | solution.py:247
  94.1 1.4 %collective-permute-done.12 = bf16[560,112]{1,0:T(8,128)(2,1)S(1)} collective-permute-done((bf16[560,112]{1,0:T(8,128)(2,1)S(1)}, bf16[560,112]{1,0:T(8,128)(2,1)S(1)}, u32[]{:S(2)}, u32[]{:S(2)}) %collective-permute-start.12) | collective-permute-done | bytes 125472 | tf_op jit(solution)/shard_map/ppermute | solution.py:180
  95.5 1.2 %shard_map.62 = bf16[2,560,512]{2,1,0:T(8,128)(2,1)} custom-call(f32[560,112]{1,0:T(8,128)S(1)} %convert_add_fusion.2.totals, bf16[560,512]{1,0:T(8,128)(2,1)S(1)} %shard_map.60.query, f32[560,1]{1,0:T(8,128)S(1)} %reshape.5.gain, bf16[2,560,512]{2,1,0:T(8,128)(2,1)} %shard_map.61.rest_0_), custom_call_target="tpu_custom_call", output_to_operand_aliasing={{}: (3, {})} | custom-call | flops 1003520 | bytes 1024 | tf_op jit(solution)/shard_map/pallas_call | solution.py:247
  (36 shorter events, 2.7 us)
Async XLA Ops:
  1.3 4.7 %collective-permute-start = (bf16[560,512]{1,0:T(8,128)(2,1)S(1)}, bf16[560,512]{1,0:T(8,128)(2,1)S(1)}, u32[]{:S(2)}, u32[]{:S(2)}) collective-permute-start(bf16[560,512]{1,0:T(8,128)(2,1)S(1)} %get-tuple-element.18.b0), channel_id=1, source_target_pairs={{0,16},{1,2},{2,1},{3,19},{16,0},{17,18},{18,17},{19,3},{4,20},{5,... | collective-permute-start | bytes 1720328 | tf_op jit(solution)/shard_map/ppermute | solution.py:173
  1.8 18.0 %collective-permute-start.1 = (bf16[560,512]{1,0:T(8,128)(2,1)S(1)}, bf16[560,512]{1,0:T(8,128)(2,1)S(1)}, u32[]{:S(2)}, u32[]{:S(2)}) collective-permute-start(bf16[560,512]{1,0:T(8,128)(2,1)S(1)} %get-tuple-element.18.b0), channel_id=1, source_target_pairs={{0,1},{1,0},{2,3},{3,2},{4,5},{5,4},{6,7},{7,6},{8,9},{9,8},{10,11... | collective-permute-start | bytes 1720328 | tf_op jit(solution)/shard_map/ppermute | solution.py:161
  6.0 26.1 %collective-permute-start.5 = (bf16[560,512]{1,0:T(8,128)(2,1)S(1)}, bf16[560,512]{1,0:T(8,128)(2,1)S(1)}, u32[]{:S(2)}, u32[]{:S(2)}) collective-permute-start(bf16[560,512]{1,0:T(8,128)(2,1)S(1)} %get-tuple-element.17.b0), channel_id=1, source_target_pairs={{0,1},{1,0},{2,3},{3,2},{4,5},{5,4},{6,7},{7,6},{8,9},{9,8},{10,11... | collective-permute-start | bytes 1720328 | tf_op jit(solution)/shard_map/ppermute | solution.py:161
  6.0 26.1 %collective-permute-start.7 = (bf16[560,512]{1,0:T(8,128)(2,1)S(1)}, bf16[560,512]{1,0:T(8,128)(2,1)S(1)}, u32[]{:S(2)}, u32[]{:S(2)}) collective-permute-start(bf16[560,512]{1,0:T(8,128)(2,1)S(1)} %get-tuple-element.17.b0), channel_id=1, source_target_pairs={{0,16},{1,2},{2,1},{3,19},{16,0},{17,18},{18,17},{19,3},{4,20},{5,... | collective-permute-start | bytes 1720328 | tf_op jit(solution)/shard_map/ppermute | solution.py:173
  19.8 14.8 %collective-permute-start.2 = (bf16[560,512]{1,0:T(8,128)(2,1)S(1)}, bf16[560,512]{1,0:T(8,128)(2,1)}, u32[]{:S(2)}, u32[]{:S(2)}) collective-permute-start(bf16[560,512]{1,0:T(8,128)(2,1)S(1)} %collective-permute-done.1.b1), channel_id=1, source_target_pairs={{0,16},{1,2},{2,1},{3,19},{16,0},{17,18},{18,17},{19,3},{4,20},{5,... | collective-permute-start | bytes 1720328 | tf_op jit(solution)/shard_map/ppermute | solution.py:173
  19.8 0.8 copy-start.6
  20.6 23.8 %collective-permute-start.3 = (bf16[560,512]{1,0:T(8,128)(2,1)S(1)}, bf16[560,512]{1,0:T(8,128)(2,1)S(1)}, u32[]{:S(2)}, u32[]{:S(2)}) collective-permute-start(bf16[560,512]{1,0:T(8,128)(2,1)S(1)} %collective-permute-done.inner_ref), channel_id=1, source_target_pairs={{0,1},{1,0},{2,3},{3,2},{4,5},{5,4},{6,7},{7,6},{8,9},{9,8},{10,11... | collective-permute-start | bytes 1720328 | tf_op jit(solution)/shard_map/ppermute | solution.py:161
  32.1 27.8 %collective-permute-start.6 = (bf16[560,512]{1,0:T(8,128)(2,1)S(1)}, bf16[560,512]{1,0:T(8,128)(2,1)}, u32[]{:S(2)}, u32[]{:S(2)}) collective-permute-start(bf16[560,512]{1,0:T(8,128)(2,1)S(1)} %collective-permute-done.5.b1), channel_id=1, source_target_pairs={{0,16},{1,2},{2,1},{3,19},{16,0},{17,18},{18,17},{19,3},{4,20},{5,... | collective-permute-start | bytes 1720328 | tf_op jit(solution)/shard_map/ppermute | solution.py:173
  32.1 27.8 %collective-permute-start.8 = (bf16[560,512]{1,0:T(8,128)(2,1)S(1)}, bf16[560,512]{1,0:T(8,128)(2,1)}, u32[]{:S(2)}, u32[]{:S(2)}) collective-permute-start(bf16[560,512]{1,0:T(8,128)(2,1)S(1)} %collective-permute-done.7.inner_ref), channel_id=1, source_target_pairs={{0,1},{1,0},{2,3},{3,2},{4,5},{5,4},{6,7},{7,6},{8,9},{9,8},{10,11... | collective-permute-start | bytes 1720328 | tf_op jit(solution)/shard_map/ppermute | solution.py:161
  44.4 0.8 copy-start.8
  45.2 23.8 %collective-permute-start.4 = (bf16[560,512]{1,0:T(8,128)(2,1)}, bf16[560,512]{1,0:T(8,128)(2,1)S(1)}, u32[]{:S(2)}, u32[]{:S(2)}) collective-permute-start(bf16[560,512]{1,0:T(8,128)(2,1)} %collective-permute-done.2.b2i), channel_id=1, source_target_pairs={{0,1},{1,0},{2,3},{3,2},{4,5},{5,4},{6,7},{7,6},{8,9},{9,8},{10,11... | collective-permute-start | bytes 1720328 | tf_op jit(solution)/shard_map/ppermute | solution.py:161
  47.3 1.7 %copy-start = (bf16[2240,560]{0,1:T(8,128)(2,1)S(1)}, bf16[2240,560]{0,1:T(8,128)(2,1)}, u32[]{:S(2)}) copy-start(bf16[2240,560]{0,1:T(8,128)(2,1)} %param.7) | copy-start | bytes 7526404
  49.1 1.7 %copy-start.2 = (bf16[2240,560]{0,1:T(8,128)(2,1)S(1)}, bf16[2240,560]{0,1:T(8,128)(2,1)}, u32[]{:S(2)}) copy-start(bf16[2240,560]{0,1:T(8,128)(2,1)} %param.8) | copy-start | bytes 7526404
  50.8 1.7 %copy-start.4 = (bf16[2240,560]{0,1:T(8,128)(2,1)S(1)}, bf16[2240,560]{0,1:T(8,128)(2,1)}, u32[]{:S(2)}) copy-start(bf16[2240,560]{0,1:T(8,128)(2,1)} %param.6) | copy-start | bytes 7526404
  52.5 1.1 %copy-start.7 = (bf16[560,512]{1,0:T(8,128)(2,1)S(1)}, bf16[560,512]{1,0:T(8,128)(2,1)}, u32[]{:S(2)}) copy-start(bf16[560,512]{1,0:T(8,128)(2,1)} %copy-done.6) | copy-start | bytes 1720324
  53.6 1.1 %copy-start.9 = (bf16[560,512]{1,0:T(8,128)(2,1)S(1)}, bf16[560,512]{1,0:T(8,128)(2,1)}, u32[]{:S(2)}) copy-start(bf16[560,512]{1,0:T(8,128)(2,1)} %copy-done.8) | copy-start | bytes 1720324
  54.7 6.7 %copy-start.1 = (bf16[2240,560]{0,1:T(8,128)(2,1)S(1)}, bf16[2240,560]{0,1:T(8,128)(2,1)}, u32[]{:S(2)}) copy-start(bf16[2240,560]{0,1:T(8,128)(2,1)} %param.7) | copy-start | bytes 7526404
  54.7 6.7 %copy-start.3 = (bf16[2240,560]{0,1:T(8,128)(2,1)S(1)}, bf16[2240,560]{0,1:T(8,128)(2,1)}, u32[]{:S(2)}) copy-start(bf16[2240,560]{0,1:T(8,128)(2,1)} %param.8) | copy-start | bytes 7526404
  59.9 20.2 %collective-permute-start.10 = (bf16[560,512]{1,0:T(8,128)(2,1)}, bf16[560,512]{1,0:T(8,128)(2,1)S(1)}, u32[]{:S(2)}, u32[]{:S(2)}) collective-permute-start(bf16[560,512]{1,0:T(8,128)(2,1)} %collective-permute-done.6.b2i), channel_id=1, source_target_pairs={{0,1},{1,0},{2,3},{3,2},{4,5},{5,4},{6,7},{7,6},{8,9},{9,8},{10,11... | collective-permute-start | bytes 1720328 | tf_op jit(solution)/shard_map/ppermute | solution.py:161
  67.6 5.0 %copy-start.5 = (bf16[2240,560]{0,1:T(8,128)(2,1)S(1)}, bf16[2240,560]{0,1:T(8,128)(2,1)}, u32[]{:S(2)}) copy-start(bf16[2240,560]{0,1:T(8,128)(2,1)} %param.6) | copy-start | bytes 7526404
  71.2 8.9 %collective-permute-start.9 = (f32[560,112]{1,0:T(8,128)S(1)}, f32[560,112]{1,0:T(8,128)S(1)}, u32[]{:S(2)}, u32[]{:S(2)}) collective-permute-start(f32[560,112]{1,0:T(8,128)S(1)} %shard_map.57.tie), channel_id=1, source_target_pairs={{0,16},{1,17},{2,18},{3,19},{4,20},{5,21},{6,22},{7,23},{8,24},{9,... | collective-permute-start | bytes 752648 | tf_op jit(solution)/shard_map/ppermute | solution.py:187
  74.1 9.9 %copy-start.10 = (f32[560]{0:T(1024)S(1)}, f32[560]{0:T(1024)}, u32[]{:S(2)}) copy-start(f32[560]{0:T(1024)} %param.9) | copy-start | bytes 6724
  82.5 5.2 %collective-permute-start.13 = (bf16[560,112]{1,0:T(8,128)(2,1)S(1)}, bf16[560,112]{1,0:T(8,128)(2,1)S(1)}, u32[]{:S(2)}, u32[]{:S(2)}) collective-permute-start(bf16[560,112]{1,0:T(8,128)(2,1)S(1)} %get-tuple-element.13), channel_id=1, source_target_pairs={{0,4},{4,0},{8,12},{12,8},{1,5},{5,1},{9,13},{13,9},{2,6},{6,2},{1... | collective-permute-start | bytes 376328 | tf_op jit(solution)/shard_map/ppermute | solution.py:180
  84.2 6.1 %collective-permute-start.11 = (bf16[560,112]{1,0:T(8,128)(2,1)S(1)}, bf16[560,112]{1,0:T(8,128)(2,1)S(1)}, u32[]{:S(2)}, u32[]{:S(2)}) collective-permute-start(bf16[560,112]{1,0:T(8,128)(2,1)S(1)} %get-tuple-element.19), channel_id=1, source_target_pairs={{0,8},{4,12},{8,0},{12,4},{1,9},{5,13},{9,1},{13,5},{2,10},{6,14},... | collective-permute-start | bytes 376328 | tf_op jit(solution)/shard_map/ppermute | solution.py:180
  87.7 5.2 %collective-permute-start.14 = (bf16[560,112]{1,0:T(8,128)(2,1)S(1)}, bf16[560,112]{1,0:T(8,128)(2,1)S(1)}, u32[]{:S(2)}, u32[]{:S(2)}) collective-permute-start(bf16[560,112]{1,0:T(8,128)(2,1)S(1)} %fusion.1), channel_id=1, source_target_pairs={{0,8},{4,12},{8,0},{12,4},{1,9},{5,13},{9,1},{13,5},{2,10},{6,14},... | collective-permute-start | bytes 376328 | tf_op jit(solution)/shard_map/ppermute | solution.py:180
  90.3 5.2 %collective-permute-start.12 = (bf16[560,112]{1,0:T(8,128)(2,1)S(1)}, bf16[560,112]{1,0:T(8,128)(2,1)S(1)}, u32[]{:S(2)}, u32[]{:S(2)}) collective-permute-start(bf16[560,112]{1,0:T(8,128)(2,1)S(1)} %fusion), channel_id=1, source_target_pairs={{0,4},{4,0},{8,12},{12,8},{1,5},{5,1},{9,13},{13,9},{2,6},{6,2},{1... | collective-permute-start | bytes 376328 | tf_op jit(solution)/shard_map/ppermute | solution.py:180

commit v7 on v6

--- a/solution.py
+++ b/solution.py
@@ -144,11 +144,11 @@
     last_block(place, inner_ref, end_ref, last, sems, count, body)
 
 
-def read_kernel(stream, totals, query, gain, *rest):
+def read_kernel(stream, prefix, states, query, gain, *rest):
     out, held, sem = rest[-3:]
     for start in range(0, query.shape[0], HEAD_DIM):
         rows = slice(start, start + HEAD_DIM)
-        total = totals[rows, :].astype(jnp.bfloat16)
+        total = (prefix[rows, :] + states[rows, :]).astype(jnp.bfloat16)
         reading = rounded_dot(total, query[rows, :])
         scale = lax.rsqrt(jnp.mean(reading * reading, axis=0, keepdims=True) + 1e-06)
         held[rows, :] = (reading * scale * gain[rows, :]).astype(jnp.bfloat16)
@@ -173,12 +173,14 @@
     return lax.ppermute(value, (other, axis), pairs)
 
 
-def sum_over(value, axis, backwards):
+def sum_over(value, axis):
     count = lax.axis_size(axis)
-    steps = [1 << b for b in range(count.bit_length() - 1)]
-    for step in steps[::-1] if backwards else steps:
-        sent = lax.ppermute(value.astype(jnp.bfloat16), axis, [(i, i ^ step) for i in range(count)])
-        value = value + sent.astype(jnp.float32)
+    sent = value.astype(jnp.bfloat16)
+    for step in range(count - 1, 0, -1):
+        pairs = [(i, (i + step) % count) for i in range(count)]
+        if count & (count - 1) == 0:
+            pairs = [(i, i ^ step) for i in range(count)]
+        value = value + lax.ppermute(sent, axis, pairs).astype(jnp.float32)
     return value
 
 
@@ -231,7 +233,7 @@
         )(place, own[stream], near[stream], far[stream], across_end[stream], *matrices))
     prefix = query = out = None
     for stream in range(2):
-        ties = (sums[1],) if stream == 0 else (prefix, query)
+        ties = (sums[1],) if stream == 0 else (total, query)
         state = call(
             functools.partial(state_kernel, count), state_type, IN_VMEM,
             [IN_SMEM] + [ANYWHERE] * 2 + [IN_VMEM] * 3 + [ANYWHERE] * len(ties), [last, sems], one // 2,
@@ -240,14 +242,14 @@
             functools.partial(query_kernel, count), query_type, IN_VMEM,
             [IN_SMEM] + [ANYWHERE] * 2 + [IN_VMEM] * 2 + [ANYWHERE], [last, sems], one // 4,
         )(place, across[stream], far_end[stream], matrices[0], sums[stream], state)
+        total = sum_over(state, "tok")
         if stream == 0:
-            prefix = entering(state, "group")
-        total = sum_over(prefix + state, "tok", stream == 1)
+            prefix = entering(total, "group")
         kept = [] if out is None else [out]
         out = call(
-            functools.partial(read_kernel, stream), out_type, ANYWHERE, [IN_VMEM] * 3 + [ANYWHERE] * len(kept),
-            read_scratch, one // 20, {3: 0} if kept else None,
-        )(total, query, gain_column, *kept)
+            functools.partial(read_kernel, stream), out_type, ANYWHERE, [IN_VMEM] * 4 + [ANYWHERE] * len(kept),
+            read_scratch, one // 20, {4: 0} if kept else None,
+        )(prefix, total, query, gain_column, *kept)
     return jnp.swapaxes(out, 1, 2)
 
 

time: 97.2 us -> 94.9 us (0.976)
  waiting for transfers between devices: 44.7 us -> 40.6 us
  starting transfers between devices: 19.7 us -> 21.5 us
    ppermute x6, waiting for transfers between devices: 40 us -> 33.9 us  [partner_swap(): lax.ppermute(value, axis, [(i, i ^ 1) for i in range(lax.axis_size(axis))])]
    ppermute x4 -> x6, waiting for transfers between devices: 4.74 us -> 6.7 us  [sum_over(): value = value + lax.ppermute(sent, axis, pairs).astype(jnp.float32)]
    ppermute x4 -> x6, starting transfers between devices: 5.24 us -> 7.11 us  [sum_over(): value = value + lax.ppermute(sent, axis, pairs).astype(jnp.float32)]
  transfers between devices with their start and end apart: 15 -> 17, of which waited for: 9 -> 9; matrix products, arithmetic and copies ran while one was open for 0% -> 0% of each run, Pallas kernels for 19% -> 18%
where the time goes in v7:
time: 94.9 us; the launch traced here: 94.6 us
  waiting for transfers between devices  40.6 us (43%)
  Pallas kernels  21.6 us (23%)
  starting transfers between devices  21.5 us (23%)
  local copies, waits for them, and re-layouts  10.4 us (11%)
    ppermute x6, waiting for transfers between devices, partner_swap(): lax.ppermute(value, axis, [(i, i ^ 1) for i in range(lax.axis_size(axis))])  33.9 us
    ppermute x6, starting transfers between devices, partner_swap(): lax.ppermute(value, axis, [(i, i ^ 1) for i in range(lax.axis_size(axis))])  12.6 us
    pallas_call x2, Pallas kernels, local(): call(partial_kernel, jax.ShapeDtypeStruct((3, width, tokens), jnp.float32...  11.6 us
    unnamed x22, local copies, waits for them, and re-layouts  8.96 us
    ppermute x6, starting transfers between devices, sum_over(): value = value + lax.ppermute(sent, axis, pairs).astype(jnp.float32)  7.11 us
    ppermute x6, waiting for transfers between devices, sum_over(): value = value + lax.ppermute(sent, axis, pairs).astype(jnp.float32)  6.7 us
    pallas_call x2, Pallas kernels, local(): call(functools.partial(state_kernel, count), state_type, IN_VMEM, [IN_SME...  4.5 us
    pallas_call x2, Pallas kernels, local(): call(functools.partial(query_kernel, count), query_type, IN_VMEM, [IN_SME...  3.08 us
  transfers between devices with their start and end apart: 17, of which 9 were waited for; matrix products, arithmetic and copies ran while one was open for 0% of the time, Pallas kernels for 18%

profile of v7, /device:TPU:0, one launch (start us, length us, event | category | flops | bytes accessed | tf_op | source)
XLA Modules:
  0.0 94.6 jit_solution(556893671578042703)
XLA Ops:
  0.0 1.3 %slice_bitcast_fusion = (bf16[560,512]{1,0:T(8,128)(2,1)S(1)}, bf16[560,512]{1,0:T(8,128)(2,1)S(1)}) fusion(bf16[2,560,512]{2,1,0:T(8,128)(2,1)} %bitcast.23), kind=kLoop, calls=%fused_computation | loop fusion | bytes 2293760 | tf_op jit(solution)/shard_map/squeeze | solution.py:210
  1.8 4.1 %collective-permute-start.1 = (bf16[560,512]{1,0:T(8,128)(2,1)S(1)}, bf16[560,512]{1,0:T(8,128)(2,1)S(1)}, u32[]{:S(2)}, u32[]{:S(2)}) collective-permute-start(bf16[560,512]{1,0:T(8,128)(2,1)S(1)} %get-tuple-element.14.b0), channel_id=1, source_target_pairs={{0,1},{1,0},{2,3},{3,2},{4,5},{5,4},{6,7},{7,6},{8,9},{9,8},{10,11... | collective-permute-start | bytes 1720328 | tf_op jit(solution)/shard_map/ppermute | solution.py:161
  6.0 13.8 %collective-permute-done.1.b1 = bf16[560,512]{1,0:T(8,128)(2,1)S(1)} collective-permute-done((bf16[560,512]{1,0:T(8,128)(2,1)S(1)}, bf16[560,512]{1,0:T(8,128)(2,1)S(1)}, u32[]{:S(2)}, u32[]{:S(2)}) %collective-permute-start.1) | collective-permute-done | bytes 573472 | tf_op jit(solution)/shard_map/ppermute | solution.py:161
  20.6 2.5 %collective-permute-start.3 = (bf16[560,512]{1,0:T(8,128)(2,1)S(1)}, bf16[560,512]{1,0:T(8,128)(2,1)S(1)}, u32[]{:S(2)}, u32[]{:S(2)}) collective-permute-start(bf16[560,512]{1,0:T(8,128)(2,1)S(1)} %collective-permute-done.inner_ref), channel_id=1, source_target_pairs={{0,1},{1,0},{2,3},{3,2},{4,5},{5,4},{6,7},{7,6},{8,9},{9,8},{10,11... | collective-permute-start | bytes 1720328 | tf_op jit(solution)/shard_map/ppermute | solution.py:161
  23.1 9.1 %collective-permute-done.5.b1 = bf16[560,512]{1,0:T(8,128)(2,1)} collective-permute-done((bf16[560,512]{1,0:T(8,128)(2,1)S(1)}, bf16[560,512]{1,0:T(8,128)(2,1)}, u32[]{:S(2)}, u32[]{:S(2)}) %collective-permute-start.5) | collective-permute-done | bytes 573472 | tf_op jit(solution)/shard_map/ppermute | solution.py:161
  32.2 2.5 %collective-permute-start.8 = (bf16[560,512]{1,0:T(8,128)(2,1)S(1)}, bf16[560,512]{1,0:T(8,128)(2,1)}, u32[]{:S(2)}, u32[]{:S(2)}) collective-permute-start(bf16[560,512]{1,0:T(8,128)(2,1)S(1)} %collective-permute-done.7.inner_ref), channel_id=1, source_target_pairs={{0,1},{1,0},{2,3},{3,2},{4,5},{5,4},{6,7},{7,6},{8,9},{9,8},{10,11... | collective-permute-start | bytes 1720328 | tf_op jit(solution)/shard_map/ppermute | solution.py:161
  34.7 9.7 %collective-permute-done.3.b2o = bf16[560,512]{1,0:T(8,128)(2,1)S(1)} collective-permute-done((bf16[560,512]{1,0:T(8,128)(2,1)S(1)}, bf16[560,512]{1,0:T(8,128)(2,1)S(1)}, u32[]{:S(2)}, u32[]{:S(2)}) %collective-permute-start.3) | collective-permute-done | bytes 573472 | tf_op jit(solution)/shard_map/ppermute | solution.py:161
  45.2 2.1 %collective-permute-start.4 = (bf16[560,512]{1,0:T(8,128)(2,1)}, bf16[560,512]{1,0:T(8,128)(2,1)S(1)}, u32[]{:S(2)}, u32[]{:S(2)}) collective-permute-start(bf16[560,512]{1,0:T(8,128)(2,1)} %collective-permute-done.2.b2i), channel_id=1, source_target_pairs={{0,1},{1,0},{2,3},{3,2},{4,5},{5,4},{6,7},{7,6},{8,9},{9,8},{10,11... | collective-permute-start | bytes 1720328 | tf_op jit(solution)/shard_map/ppermute | solution.py:161
  47.4 1.7 %copy-done = bf16[2240,560]{0,1:T(8,128)(2,1)S(1)} copy-done((bf16[2240,560]{0,1:T(8,128)(2,1)S(1)}, bf16[2240,560]{0,1:T(8,128)(2,1)}, u32[]{:S(2)}) %copy-start) | copy-done | bytes 2508824
  49.1 1.7 %copy-done.2 = bf16[2240,560]{0,1:T(8,128)(2,1)S(1)} copy-done((bf16[2240,560]{0,1:T(8,128)(2,1)S(1)}, bf16[2240,560]{0,1:T(8,128)(2,1)}, u32[]{:S(2)}) %copy-start.2) | copy-done | bytes 2508824
  50.8 1.7 %copy-done.4 = bf16[2240,560]{0,1:T(8,128)(2,1)S(1)} copy-done((bf16[2240,560]{0,1:T(8,128)(2,1)S(1)}, bf16[2240,560]{0,1:T(8,128)(2,1)}, u32[]{:S(2)}) %copy-start.4) | copy-done | bytes 2508824
  52.5 1.1 %copy-done.7 = bf16[560,512]{1,0:T(8,128)(2,1)S(1)} copy-done((bf16[560,512]{1,0:T(8,128)(2,1)S(1)}, bf16[560,512]{1,0:T(8,128)(2,1)}, u32[]{:S(2)}) %copy-start.7) | copy-done | bytes 573464
  53.6 1.1 %copy-done.9 = bf16[560,512]{1,0:T(8,128)(2,1)S(1)} copy-done((bf16[560,512]{1,0:T(8,128)(2,1)S(1)}, bf16[560,512]{1,0:T(8,128)(2,1)}, u32[]{:S(2)}) %copy-start.9) | copy-done | bytes 573464
  54.7 5.3 %shard_map.55.sums = f32[3,560,512]{2,1,0:T(8,128)S(1)} custom-call(s32[2]{0:T(128)S(1)} %pad_add_fusion.place, bf16[560,512]{1,0:T(8,128)(2,1)S(1)} %get-tuple-element.14.b0, bf16[560,512]{1,0:T(8,128)(2,1)S(1)} %copy-done.7, bf16[560,512]{1,0:T(8,128)(2,1)} %collective-permute-done.2.b2i, bf16[560,512]{1,0:T(8,128)(2,1)S(1)} %copy-done.9, ...), custom_call_target="tpu_custom_call" | custom-call | flops 60211200 | bytes 1024 | tf_op jit(solution)/shard_map/pallas_call | solution.py:230
  60.0 1.4 %collective-permute-start.13 = (bf16[560,512]{1,0:T(8,128)(2,1)S(1)}, bf16[560,512]{1,0:T(8,128)(2,1)S(1)}, u32[]{:S(2)}, u32[]{:S(2)}) collective-permute-start(bf16[560,512]{1,0:T(8,128)(2,1)S(1)} %collective-permute-done.6.b2i), channel_id=1, source_target_pairs={{0,1},{1,0},{2,3},{3,2},{4,5},{5,4},{6,7},{7,6},{8,9},{9,8},{10,11... | collective-permute-start | bytes 1720328 | tf_op jit(solution)/shard_map/ppermute | solution.py:161
  61.4 6.3 %shard_map.56.rest_0_.sums = f32[3,560,512]{2,1,0:T(8,128)S(1)} custom-call(s32[2]{0:T(128)S(1)} %pad_add_fusion.place, bf16[560,512]{1,0:T(8,128)(2,1)S(1)} %get-tuple-element.13.b0, bf16[560,512]{1,0:T(8,128)(2,1)} %collective-permute-done.5.b1, bf16[560,512]{1,0:T(8,128)(2,1)S(1)} %collective-permute-done.6.b2i, ...), custom_call_target="tpu_custom_call" | custom-call | flops 60211200 | bytes 1024 | tf_op jit(solution)/shard_map/pallas_call | solution.py:230
  67.7 1.3 %collective-permute-done.4.end_ref = bf16[560,512]{1,0:T(8,128)(2,1)S(1)} collective-permute-done((bf16[560,512]{1,0:T(8,128)(2,1)}, bf16[560,512]{1,0:T(8,128)(2,1)S(1)}, u32[]{:S(2)}, u32[]{:S(2)}) %collective-permute-start.4) | collective-permute-done | bytes 573472 | tf_op jit(solution)/shard_map/ppermute | solution.py:161
  69.0 2.2 %shard_map.57.tie = f32[560,112]{1,0:T(8,128)S(1)} custom-call(s32[2]{0:T(128)S(1)} %pad_add_fusion.place, bf16[560,512]{1,0:T(8,128)(2,1)S(1)} %collective-permute-done.inner_ref, bf16[560,512]{1,0:T(8,128)(2,1)S(1)} %collective-permute-done.4.end_ref, bf16[560,2240]{1,0:T(8,128)(2,1)S(1)} %bitcast.13, bf16[560,2240]{1,0:T(8,128)(2,1)S(1)} %bitcast.17, ...), custom_call_target="tpu_custom_call" | custom-call | flops 10035200 | bytes 1024 | tf_op jit(solution)/shard_map/pallas_call | solution.py:237
  71.3 1.6 %collective-permute-start.11 = (bf16[560,112]{1,0:T(8,128)(2,1)S(1)}, bf16[560,112]{1,0:T(8,128)(2,1)S(1)}, u32[]{:S(2)}, u32[]{:S(2)}) collective-permute-start(bf16[560,112]{1,0:T(8,128)(2,1)S(1)} %convert_element_type.25), channel_id=1, source_target_pairs={{0,4},{4,0},{8,12},{12,8},{1,5},{5,1},{9,13},{13,9},{2,6},{6,2},{1... | collective-permute-start | bytes 376328 | tf_op jit(solution)/shard_map/ppermute | solution.py:183
  72.8 1.5 %collective-permute-start.10 = (bf16[560,112]{1,0:T(8,128)(2,1)S(1)}, bf16[560,112]{1,0:T(8,128)(2,1)S(1)}, u32[]{:S(2)}, u32[]{:S(2)}) collective-permute-start(bf16[560,112]{1,0:T(8,128)(2,1)S(1)} %convert_element_type.25), channel_id=1, source_target_pairs={{0,8},{4,12},{8,0},{12,4},{1,9},{5,13},{9,1},{13,5},{2,10},{6,14},... | collective-permute-start | bytes 376328 | tf_op jit(solution)/shard_map/ppermute | solution.py:183
  74.8 1.5 %shard_map.58.rest_1_.query = bf16[560,512]{1,0:T(8,128)(2,1)S(1)} custom-call(s32[2]{0:T(128)S(1)} %pad_add_fusion.place, bf16[560,512]{1,0:T(8,128)(2,1)S(1)} %collective-permute-done.inner_ref, bf16[560,512]{1,0:T(8,128)(2,1)S(1)} %collective-permute-done.4.end_ref, bf16[560,2240]{1,0:T(8,128)(2,1)S(1)} %bitcast.21, f32[3,560,512]{2,1,0:T(8,128)S(1)} %shard_map.55.sums, ...), custom_call_target="tpu_custom_call" | custom-call | flops 5017600 | bytes 1024 | tf_op jit(solution)/shard_map/pallas_call | solution.py:241
  76.4 0.8 collective-permute-done.11
  77.2 1.2 %collective-permute-done.10 = bf16[560,112]{1,0:T(8,128)(2,1)S(1)} collective-permute-done((bf16[560,112]{1,0:T(8,128)(2,1)S(1)}, bf16[560,112]{1,0:T(8,128)(2,1)S(1)}, u32[]{:S(2)}, u32[]{:S(2)}) %collective-permute-start.10) | collective-permute-done | bytes 125472 | tf_op jit(solution)/shard_map/ppermute | solution.py:183
  78.4 1.9 %collective-permute-done.9 = bf16[560,112]{1,0:T(8,128)(2,1)S(1)} collective-permute-done((bf16[560,112]{1,0:T(8,128)(2,1)S(1)}, bf16[560,112]{1,0:T(8,128)(2,1)S(1)}, u32[]{:S(2)}, u32[]{:S(2)}) %collective-permute-start.9) | collective-permute-done | bytes 125472 | tf_op jit(solution)/shard_map/ppermute | solution.py:183
  80.4 2.3 %shard_map.59.tie = f32[560,112]{1,0:T(8,128)S(1)} custom-call(s32[2]{0:T(128)S(1)} %pad_add_fusion.place, bf16[560,512]{1,0:T(8,128)(2,1)S(1)} %collective-permute-done.7.inner_ref, bf16[560,512]{1,0:T(8,128)(2,1)S(1)} %collective-permute-done.13.end_ref, bf16[560,2240]{1,0:T(8,128)(2,1)S(1)} %bitcast.14, bf16[560,2240]{1,0:T(8,128)(2,1)S(1)} %bitcast.18, ...), custom_call_target="tpu_custom_call" | custom-call | flops 10035200 | bytes 1024 | tf_op jit(solution)/shard_map/pallas_call | solution.py:237
  82.7 1.2 %collective-permute-start.16 = (bf16[560,112]{1,0:T(8,128)(2,1)S(1)}, bf16[560,112]{1,0:T(8,128)(2,1)S(1)}, u32[]{:S(2)}, u32[]{:S(2)}) collective-permute-start(bf16[560,112]{1,0:T(8,128)(2,1)S(1)} %convert_element_type.29), channel_id=1, source_target_pairs={{0,4},{4,0},{8,12},{12,8},{1,5},{5,1},{9,13},{13,9},{2,6},{6,2},{1... | collective-permute-start | bytes 376328 | tf_op jit(solution)/shard_map/ppermute | solution.py:183
  84.0 1.5 %collective-permute-start.15 = (bf16[560,112]{1,0:T(8,128)(2,1)S(1)}, bf16[560,112]{1,0:T(8,128)(2,1)S(1)}, u32[]{:S(2)}, u32[]{:S(2)}) collective-permute-start(bf16[560,112]{1,0:T(8,128)(2,1)S(1)} %convert_element_type.29), channel_id=1, source_target_pairs={{0,8},{4,12},{8,0},{12,4},{1,9},{5,13},{9,1},{13,5},{2,10},{6,14},... | collective-permute-start | bytes 376328 | tf_op jit(solution)/shard_map/ppermute | solution.py:183
  86.3 1.3 %collective-permute-start.12 = (f32[560,112]{1,0:T(8,128)S(1)}, f32[560,112]{1,0:T(8,128)S(1)}, u32[]{:S(2)}, u32[]{:S(2)}) collective-permute-start(f32[560,112]{1,0:T(8,128)S(1)} %convert_add_fusion.1.rest_0_.states), channel_id=1, source_target_pairs={{0,16},{1,17},{2,18},{3,19},{4,20},{5,21},{6,22},{7,23},{8,24},{9,... | collective-permute-start | bytes 752648 | tf_op jit(solution)/shard_map/ppermute | solution.py:189
  87.7 1.5 %shard_map.60.query = bf16[560,512]{1,0:T(8,128)(2,1)S(1)} custom-call(s32[2]{0:T(128)S(1)} %pad_add_fusion.place, bf16[560,512]{1,0:T(8,128)(2,1)S(1)} %collective-permute-done.7.inner_ref, bf16[560,512]{1,0:T(8,128)(2,1)S(1)} %collective-permute-done.13.end_ref, bf16[560,2240]{1,0:T(8,128)(2,1)S(1)} %bitcast.22, ...), custom_call_target="tpu_custom_call" | custom-call | flops 5017600 | bytes 1024 | tf_op jit(solution)/shard_map/pallas_call | solution.py:241
  89.4 2.6 %collective-permute-done.15 = bf16[560,112]{1,0:T(8,128)(2,1)S(1)} collective-permute-done((bf16[560,112]{1,0:T(8,128)(2,1)S(1)}, bf16[560,112]{1,0:T(8,128)(2,1)S(1)}, u32[]{:S(2)}, u32[]{:S(2)}) %collective-permute-start.15) | collective-permute-done | bytes 125472 | tf_op jit(solution)/shard_map/ppermute | solution.py:183
  92.1 1.2 %shard_map.61.rest_0_ = bf16[2,560,512]{2,1,0:T(8,128)(2,1)} custom-call(f32[560,112]{1,0:T(8,128)S(1)} %collective-permute-done.12.prefix, f32[560,112]{1,0:T(8,128)S(1)} %convert_add_fusion.1.rest_0_.states, bf16[560,512]{1,0:T(8,128)(2,1)S(1)} %shard_map.58.rest_1_.query, f32[560,1]{1,0:T(8,128)S(1)} %reshape.5.gain), custom_call_target="tpu_custom_call" | custom-call | flops 1003520 | bytes 1024 | tf_op jit(solution)/shard_map/pallas_call | solution.py:249
  93.3 1.2 %shard_map.62 = bf16[2,560,512]{2,1,0:T(8,128)(2,1)} custom-call(f32[560,112]{1,0:T(8,128)S(1)} %collective-permute-done.12.prefix, f32[560,112]{1,0:T(8,128)S(1)} %convert_add_fusion.states, bf16[560,512]{1,0:T(8,128)(2,1)S(1)} %shard_map.60.query, f32[560,1]{1,0:T(8,128)S(1)} %reshape.5.gain, ...), custom_call_target="tpu_custom_call", output_to_operand_aliasing={{}: (4, {})} | custom-call | flops 1003520 | bytes 1024 | tf_op jit(solution)/shard_map/pallas_call | solution.py:249
  (39 shorter events, 4.0 us)
Async XLA Ops:
  1.3 4.7 %collective-permute-start = (bf16[560,512]{1,0:T(8,128)(2,1)S(1)}, bf16[560,512]{1,0:T(8,128)(2,1)S(1)}, u32[]{:S(2)}, u32[]{:S(2)}) collective-permute-start(bf16[560,512]{1,0:T(8,128)(2,1)S(1)} %get-tuple-element.14.b0), channel_id=1, source_target_pairs={{0,16},{1,2},{2,1},{3,19},{16,0},{17,18},{18,17},{19,3},{4,20},{5,... | collective-permute-start | bytes 1720328 | tf_op jit(solution)/shard_map/ppermute | solution.py:173
  1.8 18.0 %collective-permute-start.1 = (bf16[560,512]{1,0:T(8,128)(2,1)S(1)}, bf16[560,512]{1,0:T(8,128)(2,1)S(1)}, u32[]{:S(2)}, u32[]{:S(2)}) collective-permute-start(bf16[560,512]{1,0:T(8,128)(2,1)S(1)} %get-tuple-element.14.b0), channel_id=1, source_target_pairs={{0,1},{1,0},{2,3},{3,2},{4,5},{5,4},{6,7},{7,6},{8,9},{9,8},{10,11... | collective-permute-start | bytes 1720328 | tf_op jit(solution)/shard_map/ppermute | solution.py:161
  6.0 26.2 %collective-permute-start.5 = (bf16[560,512]{1,0:T(8,128)(2,1)S(1)}, bf16[560,512]{1,0:T(8,128)(2,1)}, u32[]{:S(2)}, u32[]{:S(2)}) collective-permute-start(bf16[560,512]{1,0:T(8,128)(2,1)S(1)} %get-tuple-element.13.b0), channel_id=1, source_target_pairs={{0,1},{1,0},{2,3},{3,2},{4,5},{5,4},{6,7},{7,6},{8,9},{9,8},{10,11... | collective-permute-start | bytes 1720328 | tf_op jit(solution)/shard_map/ppermute | solution.py:161
  6.0 26.2 %collective-permute-start.7 = (bf16[560,512]{1,0:T(8,128)(2,1)S(1)}, bf16[560,512]{1,0:T(8,128)(2,1)S(1)}, u32[]{:S(2)}, u32[]{:S(2)}) collective-permute-start(bf16[560,512]{1,0:T(8,128)(2,1)S(1)} %get-tuple-element.13.b0), channel_id=1, source_target_pairs={{0,16},{1,2},{2,1},{3,19},{16,0},{17,18},{18,17},{19,3},{4,20},{5,... | collective-permute-start | bytes 1720328 | tf_op jit(solution)/shard_map/ppermute | solution.py:173
  19.8 14.9 %collective-permute-start.2 = (bf16[560,512]{1,0:T(8,128)(2,1)S(1)}, bf16[560,512]{1,0:T(8,128)(2,1)}, u32[]{:S(2)}, u32[]{:S(2)}) collective-permute-start(bf16[560,512]{1,0:T(8,128)(2,1)S(1)} %collective-permute-done.1.b1), channel_id=1, source_target_pairs={{0,16},{1,2},{2,1},{3,19},{16,0},{17,18},{18,17},{19,3},{4,20},{5,... | collective-permute-start | bytes 1720328 | tf_op jit(solution)/shard_map/ppermute | solution.py:173
  19.8 0.8 copy-start.6
  20.6 23.8 %collective-permute-start.3 = (bf16[560,512]{1,0:T(8,128)(2,1)S(1)}, bf16[560,512]{1,0:T(8,128)(2,1)S(1)}, u32[]{:S(2)}, u32[]{:S(2)}) collective-permute-start(bf16[560,512]{1,0:T(8,128)(2,1)S(1)} %collective-permute-done.inner_ref), channel_id=1, source_target_pairs={{0,1},{1,0},{2,3},{3,2},{4,5},{5,4},{6,7},{7,6},{8,9},{9,8},{10,11... | collective-permute-start | bytes 1720328 | tf_op jit(solution)/shard_map/ppermute | solution.py:161
  32.2 27.7 %collective-permute-start.6 = (bf16[560,512]{1,0:T(8,128)(2,1)}, bf16[560,512]{1,0:T(8,128)(2,1)S(1)}, u32[]{:S(2)}, u32[]{:S(2)}) collective-permute-start(bf16[560,512]{1,0:T(8,128)(2,1)} %collective-permute-done.5.b1), channel_id=1, source_target_pairs={{0,16},{1,2},{2,1},{3,19},{16,0},{17,18},{18,17},{19,3},{4,20},{5,... | collective-permute-start | bytes 1720328 | tf_op jit(solution)/shard_map/ppermute | solution.py:173
  32.2 27.7 %collective-permute-start.8 = (bf16[560,512]{1,0:T(8,128)(2,1)S(1)}, bf16[560,512]{1,0:T(8,128)(2,1)}, u32[]{:S(2)}, u32[]{:S(2)}) collective-permute-start(bf16[560,512]{1,0:T(8,128)(2,1)S(1)} %collective-permute-done.7.inner_ref), channel_id=1, source_target_pairs={{0,1},{1,0},{2,3},{3,2},{4,5},{5,4},{6,7},{7,6},{8,9},{9,8},{10,11... | collective-permute-start | bytes 1720328 | tf_op jit(solution)/shard_map/ppermute | solution.py:161
  44.4 0.8 copy-start.8
  45.2 23.7 %collective-permute-start.4 = (bf16[560,512]{1,0:T(8,128)(2,1)}, bf16[560,512]{1,0:T(8,128)(2,1)S(1)}, u32[]{:S(2)}, u32[]{:S(2)}) collective-permute-start(bf16[560,512]{1,0:T(8,128)(2,1)} %collective-permute-done.2.b2i), channel_id=1, source_target_pairs={{0,1},{1,0},{2,3},{3,2},{4,5},{5,4},{6,7},{7,6},{8,9},{9,8},{10,11... | collective-permute-start | bytes 1720328 | tf_op jit(solution)/shard_map/ppermute | solution.py:161
  47.4 1.7 %copy-start = (bf16[2240,560]{0,1:T(8,128)(2,1)S(1)}, bf16[2240,560]{0,1:T(8,128)(2,1)}, u32[]{:S(2)}) copy-start(bf16[2240,560]{0,1:T(8,128)(2,1)} %param.7) | copy-start | bytes 7526404
  49.1 1.7 %copy-start.2 = (bf16[2240,560]{0,1:T(8,128)(2,1)S(1)}, bf16[2240,560]{0,1:T(8,128)(2,1)}, u32[]{:S(2)}) copy-start(bf16[2240,560]{0,1:T(8,128)(2,1)} %param.8) | copy-start | bytes 7526404
  50.8 1.7 %copy-start.4 = (bf16[2240,560]{0,1:T(8,128)(2,1)S(1)}, bf16[2240,560]{0,1:T(8,128)(2,1)}, u32[]{:S(2)}) copy-start(bf16[2240,560]{0,1:T(8,128)(2,1)} %param.6) | copy-start | bytes 7526404
  52.5 1.1 %copy-start.7 = (bf16[560,512]{1,0:T(8,128)(2,1)S(1)}, bf16[560,512]{1,0:T(8,128)(2,1)}, u32[]{:S(2)}) copy-start(bf16[560,512]{1,0:T(8,128)(2,1)} %copy-done.6) | copy-start | bytes 1720324
  53.6 1.1 %copy-start.9 = (bf16[560,512]{1,0:T(8,128)(2,1)S(1)}, bf16[560,512]{1,0:T(8,128)(2,1)}, u32[]{:S(2)}) copy-start(bf16[560,512]{1,0:T(8,128)(2,1)} %copy-done.8) | copy-start | bytes 1720324
  54.7 6.7 %copy-start.1 = (bf16[2240,560]{0,1:T(8,128)(2,1)S(1)}, bf16[2240,560]{0,1:T(8,128)(2,1)}, u32[]{:S(2)}) copy-start(bf16[2240,560]{0,1:T(8,128)(2,1)} %param.7) | copy-start | bytes 7526404
  54.7 6.7 %copy-start.3 = (bf16[2240,560]{0,1:T(8,128)(2,1)S(1)}, bf16[2240,560]{0,1:T(8,128)(2,1)}, u32[]{:S(2)}) copy-start(bf16[2240,560]{0,1:T(8,128)(2,1)} %param.8) | copy-start | bytes 7526404
  60.0 20.5 %collective-permute-start.13 = (bf16[560,512]{1,0:T(8,128)(2,1)S(1)}, bf16[560,512]{1,0:T(8,128)(2,1)S(1)}, u32[]{:S(2)}, u32[]{:S(2)}) collective-permute-start(bf16[560,512]{1,0:T(8,128)(2,1)S(1)} %collective-permute-done.6.b2i), channel_id=1, source_target_pairs={{0,1},{1,0},{2,3},{3,2},{4,5},{5,4},{6,7},{7,6},{8,9},{9,8},{10,11... | collective-permute-start | bytes 1720328 | tf_op jit(solution)/shard_map/ppermute | solution.py:161
  67.7 7.1 %copy-start.5 = (bf16[2240,560]{0,1:T(8,128)(2,1)S(1)}, bf16[2240,560]{0,1:T(8,128)(2,1)}, u32[]{:S(2)}) copy-start(bf16[2240,560]{0,1:T(8,128)(2,1)} %param.6) | copy-start | bytes 7526404
  71.3 5.9 %collective-permute-start.11 = (bf16[560,112]{1,0:T(8,128)(2,1)S(1)}, bf16[560,112]{1,0:T(8,128)(2,1)S(1)}, u32[]{:S(2)}, u32[]{:S(2)}) collective-permute-start(bf16[560,112]{1,0:T(8,128)(2,1)S(1)} %convert_element_type.25), channel_id=1, source_target_pairs={{0,4},{4,0},{8,12},{12,8},{1,5},{5,1},{9,13},{13,9},{2,6},{6,2},{1... | collective-permute-start | bytes 376328 | tf_op jit(solution)/shard_map/ppermute | solution.py:183
  72.8 5.6 %collective-permute-start.10 = (bf16[560,112]{1,0:T(8,128)(2,1)S(1)}, bf16[560,112]{1,0:T(8,128)(2,1)S(1)}, u32[]{:S(2)}, u32[]{:S(2)}) collective-permute-start(bf16[560,112]{1,0:T(8,128)(2,1)S(1)} %convert_element_type.25), channel_id=1, source_target_pairs={{0,8},{4,12},{8,0},{12,4},{1,9},{5,13},{9,1},{13,5},{2,10},{6,14},... | collective-permute-start | bytes 376328 | tf_op jit(solution)/shard_map/ppermute | solution.py:183
  74.3 6.0 %collective-permute-start.9 = (bf16[560,112]{1,0:T(8,128)(2,1)S(1)}, bf16[560,112]{1,0:T(8,128)(2,1)S(1)}, u32[]{:S(2)}, u32[]{:S(2)}) collective-permute-start(bf16[560,112]{1,0:T(8,128)(2,1)S(1)} %convert_element_type.25), channel_id=1, source_target_pairs={{0,12},{4,8},{8,4},{12,0},{1,13},{5,9},{9,5},{13,1},{2,14},{6,10},... | collective-permute-start | bytes 376328 | tf_op jit(solution)/shard_map/ppermute | solution.py:183
  80.4 7.2 %copy-start.10 = (f32[560]{0:T(1024)S(1)}, f32[560]{0:T(1024)}, u32[]{:S(2)}) copy-start(f32[560]{0:T(1024)} %param.9) | copy-start | bytes 6724
  82.7 6.6 %collective-permute-start.16 = (bf16[560,112]{1,0:T(8,128)(2,1)S(1)}, bf16[560,112]{1,0:T(8,128)(2,1)S(1)}, u32[]{:S(2)}, u32[]{:S(2)}) collective-permute-start(bf16[560,112]{1,0:T(8,128)(2,1)S(1)} %convert_element_type.29), channel_id=1, source_target_pairs={{0,4},{4,0},{8,12},{12,8},{1,5},{5,1},{9,13},{13,9},{2,6},{6,2},{1... | collective-permute-start | bytes 376328 | tf_op jit(solution)/shard_map/ppermute | solution.py:183
  84.0 8.1 %collective-permute-start.15 = (bf16[560,112]{1,0:T(8,128)(2,1)S(1)}, bf16[560,112]{1,0:T(8,128)(2,1)S(1)}, u32[]{:S(2)}, u32[]{:S(2)}) collective-permute-start(bf16[560,112]{1,0:T(8,128)(2,1)S(1)} %convert_element_type.29), channel_id=1, source_target_pairs={{0,8},{4,12},{8,0},{12,4},{1,9},{5,13},{9,1},{13,5},{2,10},{6,14},... | collective-permute-start | bytes 376328 | tf_op jit(solution)/shard_map/ppermute | solution.py:183
  85.5 6.5 %collective-permute-start.14 = (bf16[560,112]{1,0:T(8,128)(2,1)S(1)}, bf16[560,112]{1,0:T(8,128)(2,1)S(1)}, u32[]{:S(2)}, u32[]{:S(2)}) collective-permute-start(bf16[560,112]{1,0:T(8,128)(2,1)S(1)} %convert_element_type.29), channel_id=1, source_target_pairs={{0,12},{4,8},{8,4},{12,0},{1,13},{5,9},{9,5},{13,1},{2,14},{6,10},... | collective-permute-start | bytes 376328 | tf_op jit(solution)/shard_map/ppermute | solution.py:183
  86.3 5.8 %collective-permute-start.12 = (f32[560,112]{1,0:T(8,128)S(1)}, f32[560,112]{1,0:T(8,128)S(1)}, u32[]{:S(2)}, u32[]{:S(2)}) collective-permute-start(f32[560,112]{1,0:T(8,128)S(1)} %convert_add_fusion.1.rest_0_.states), channel_id=1, source_target_pairs={{0,16},{1,17},{2,18},{3,19},{4,20},{5,21},{6,22},{7,23},{8,24},{9,... | collective-permute-start | bytes 752648 | tf_op jit(solution)/shard_map/ppermute | solution.py:189

commit v8 on v7

v8 whole, which is shorter than its diff:
```python
import functools

import jax
import jax.numpy as jnp
from jax import lax
from jax.experimental import pallas as pl
from jax.experimental.pallas import tpu as pltpu
from jax.sharding import PartitionSpec as P

HEAD_DIM = 112
VMEM_LIMIT = 20 * 1024 * 1024
ANYWHERE = pl.BlockSpec(memory_space=pl.ANY)
IN_VMEM = pl.BlockSpec(memory_space=pltpu.VMEM)
IN_SMEM = pl.BlockSpec(memory_space=pltpu.SMEM)


def call(body, outs, out_specs, in_specs, scratch, flops, aliases=None):
    return pl.pallas_call(
        body,
        out_shape=outs,
        in_specs=in_specs,
        out_specs=out_specs,
        scratch_shapes=scratch,
        input_output_aliases=aliases or {},
        compiler_params=pltpu.CompilerParams(vmem_limit_bytes=VMEM_LIMIT),
        cost_estimate=pl.CostEstimate(flops=flops // 64, bytes_accessed=1 << 10, transcendentals=0),
    )


def rounded_dot(matrix, block):
    return jnp.dot(matrix, block, preferred_element_type=jnp.float32)


def token_tiles(tokens):
    width = 256 if tokens % 256 == 0 else tokens
    return width, tokens // width


def load_blocks(place, found, whole, sems):
    mine, inner = place[0], place[1]
    rows = found[0].shape[0]

    def at(flip):
        return whole.at[pl.ds(pl.multiple_of((mine ^ flip) * rows, 16), rows), :]

    for flip, source in enumerate(found):
        if isinstance(source, tuple):
            for want, ref in ((1, source[0]), (0, source[1])):

                @pl.when(inner == want)
                def _(ref=ref, flip=flip):
                    pltpu.make_async_copy(ref, at(flip), sems.at[flip]).start()
        else:
            pltpu.make_async_copy(source, at(flip), sems.at[flip]).start()
    for flip in range(len(found)):
        pltpu.make_async_copy(at(flip), at(flip), sems.at[flip]).wait()


def partial_kernel(place, b0, b1, b2i, b2o, wq, wk, wv, tie, sums, whole, sems):
    rows, tokens = b0.shape
    missing = pl.ds(pl.multiple_of((place[0] ^ 3) * rows, 16), rows)
    whole[missing, :] = jnp.zeros((rows, tokens), whole.dtype)
    load_blocks(place, [b0, b1, (b2i, b2o)], whole, sems)
    width, tiles = token_tiles(tokens)

    @pl.loop(0, tiles)
    def _(tile):
        columns = pl.ds(pl.multiple_of(tile * width, width), width)
        block = whole[:, columns]
        for k, matrix in enumerate((wk, wv, wq)):
            sums[k, :, columns] = rounded_dot(matrix[...], block)


def cut_kernel(count, place, *rest):
    matrices, (cut,) = rest[:-1], rest[-1:]
    rows = cut.shape[2]
    for owner in range(count):

        @pl.when((place[0] ^ 3) == owner)
        def _(owner=owner):
            for k, matrix in enumerate(matrices):
                cut[k] = matrix[:, owner * rows : (owner + 1) * rows]


def on_last(place, inner_ref, end_ref, body):
    for want, ref in ((1, inner_ref), (0, end_ref)):

        @pl.when(place[1] == want)
        def _(ref=ref):
            body(ref)


def state_kernel(place, inner_ref, end_ref, cut, sums, *rest):
    state = rest[-1]

    def body(block):
        key = (sums[0] + rounded_dot(cut[0], block[...])).astype(jnp.bfloat16)
        value = (sums[1] + rounded_dot(cut[1], block[...])).astype(jnp.bfloat16)
        key = jnp.maximum(key, 0)
        for start in range(0, key.shape[0], HEAD_DIM):
            rows = slice(start, start + HEAD_DIM)
            state[rows, :] = lax.dot_general(
                value[rows], key[rows], (((1,), (1,)), ((), ())), preferred_element_type=jnp.float32
            )

    on_last(place, inner_ref, end_ref, body)


def query_kernel(place, inner_ref, end_ref, cut, sums, tie, query):
    def body(block):
        row = (sums[2] + rounded_dot(cut[2], block[...])).astype(jnp.bfloat16)
        query[...] = jnp.maximum(row, 0)

    on_last(place, inner_ref, end_ref, body)


def read_kernel(stream, parts, query, gain, *rest):
    out, held, sem = rest[-3:]
    for start in range(0, query.shape[0], HEAD_DIM):
        rows = slice(start, start + HEAD_DIM)
        total = sum(part[rows, :].astype(jnp.float32) for part in rest[:parts])
        reading = rounded_dot(total.astype(jnp.bfloat16), query[rows, :])
        scale = lax.rsqrt(jnp.mean(reading * reading, axis=0, keepdims=True) + 1e-06)
        held[rows, :] = (reading * scale * gain[rows, :]).astype(jnp.bfloat16)
    copy = pltpu.make_async_copy(held, out.at[stream], sem)
    copy.start()
    copy.wait()


def partner_swap(value, axis):
    return lax.ppermute(value, axis, [(i, i ^ 1) for i in range(lax.axis_size(axis))])


def middle_swap(value, axis, other):
    wide, count = lax.axis_size(other), lax.axis_size(axis)
    pairs = []
    for j in range(wide):
        for i in range(count):
            if i in (1, 2):
                pairs.append((j * count + i, j * count + 3 - i))
            else:
                pairs.append((j * count + i, (j ^ 1 if j ^ 1 < wide else j) * count + i))
    return lax.ppermute(value, (other, axis), pairs)


def from_others(value, axis):
    count = lax.axis_size(axis)
    sent = value.astype(jnp.bfloat16)
    got = []
    for step in range(count - 1, 0, -1):
        pairs = [(i, (i + step) % count) for i in range(count)]
        if count & (count - 1) == 0:
            pairs = [(i, i ^ step) for i in range(count)]
        got.append(lax.ppermute(sent, axis, pairs))
    return got


def entering(value, axis):
    count = lax.axis_size(axis)
    total = lax.ppermute(value, axis, [(i, i + 1) for i in range(count - 1)])
    reach = 1
    while reach < count - 1:
        total = total + lax.ppermute(total, axis, [(i, i + reach) for i in range(count - reach)])
        reach *= 2
    return total


def local(streams, w_query, w_key, w_value, gain):
    count, mine = lax.axis_size("head"), lax.axis_index("head")
    rows, tokens = streams.shape[2], streams.shape[1]
    width = w_query.shape[1]
    depth = rows * count
    columns = jnp.swapaxes(streams, 1, 2)
    matrices = (w_query.T, w_key.T, w_value.T)
    gain_column = gain.reshape(width, 1)
    inner = (mine == 1) | (mine == 2)
    place = jnp.stack([mine.astype(jnp.int32), inner.astype(jnp.int32)])

    one = 2 * width * depth * tokens
    cut = call(
        functools.partial(cut_kernel, count), jax.ShapeDtypeStruct((3, width, rows), jnp.bfloat16), IN_VMEM,
        [IN_SMEM] + [IN_VMEM] * 3, [], one // 4,
    )(place, matrices[1], matrices[2], matrices[0])
    own, near, across, far, across_end, far_end = [], [], [], [], [], []
    for stream in range(2):
        if own:
            columns, own[0] = lax.optimization_barrier((columns, own[0]))
        own.append(columns[stream])
        near.append(partner_swap(own[stream], "head"))
        across.append(middle_swap(own[stream], "head", "group"))
    for stream in range(2):
        far.append(middle_swap(near[stream], "head", "group"))
        ready, *_ = lax.optimization_barrier((across[stream], near[stream], *([cut] if stream else [])))
        across_end.append(partner_swap(ready, "head"))
    whole = pltpu.VMEM((depth, tokens), jnp.bfloat16)
    sems = pltpu.SemaphoreType.DMA((4,))
    query_type = jax.ShapeDtypeStruct((width, tokens), jnp.bfloat16)
    state_type = jax.ShapeDtypeStruct((width, HEAD_DIM), jnp.float32)
    out_type = jax.ShapeDtypeStruct((2, width, tokens), jnp.bfloat16)

    read_scratch = [pltpu.VMEM((width, tokens), jnp.bfloat16), pltpu.SemaphoreType.DMA(())]
    sums = []
    for stream in range(2):
        ready, *_ = lax.optimization_barrier((far[stream], across_end[stream], *sums))
        far_end.append(partner_swap(ready, "head"))
        sums.append(call(
            partial_kernel, jax.ShapeDtypeStruct((3, width, tokens), jnp.float32), IN_VMEM,
            [IN_SMEM] + [ANYWHERE] * 4 + [IN_VMEM] * 3 + [ANYWHERE], [whole, sems], 3 * one,
        )(place, own[stream], near[stream], far[stream], across_end[stream], *matrices, cut))
    prefix = parts = query = out = None
    for stream in range(2):
        ties = (sums[1],) if stream == 0 else (parts[0], query)
        state = call(
            state_kernel, state_type, IN_VMEM,
            [IN_SMEM] + [IN_VMEM] * 4 + [ANYWHERE] * len(ties), [], one // 2,
        )(place, across[stream], far_end[stream], cut, sums[stream], *ties)
        query = call(
            query_kernel, query_type, IN_VMEM, [IN_SMEM] + [IN_VMEM] * 4 + [ANYWHERE], [], one // 4,
        )(place, across[stream], far_end[stream], cut, sums[stream], state)
        parts = [state, *from_others(state, "tok")]
        if stream == 0:
            parts = [sum(part.astype(jnp.float32) for part in parts)]
            prefix = entering(parts[0], "group")
        kept = [] if out is None else [out]
        out = call(
            functools.partial(read_kernel, stream, len(parts) + 1), out_type, ANYWHERE,
            [IN_VMEM] * (3 + len(parts)) + [ANYWHERE] * len(kept),
            read_scratch, one // 20, {3 + len(parts): 0} if kept else None,
        )(query, gain_column, prefix, *parts, *kept)
    return jnp.swapaxes(out, 1, 2)


def solution(mesh):
    return jax.shard_map(
        local,
        mesh=mesh,
        in_specs=(
            P(None, ("group", "tok"), "head"),
            P(None, "head"),
            P(None, "head"),
            P(None, "head"),
            P("head"),
        ),
        out_specs=P(None, ("group", "tok"), "head"),
        check_vma=False,
    )
```

time: 94.9 us -> 91.5 us (0.964)
  starting transfers between devices: 21.5 us -> 26.5 us
  waiting for transfers between devices: 40.6 us -> 35.6 us
  local copies, waits for them, and re-layouts: 10.4 us -> 7.51 us
    ppermute x6, waiting for transfers between devices: 33.9 us -> 28.8 us  [partner_swap(): lax.ppermute(value, axis, [(i, i ^ 1) for i in range(lax.axis_size(axis))])]
    ppermute x6, starting transfers between devices: 12.6 us -> 17.4 us  [partner_swap(): lax.ppermute(value, axis, [(i, i ^ 1) for i in range(lax.axis_size(axis))])]
    unnamed x22 -> x8, local copies, waits for them, and re-layouts: 8.96 us -> 5.19 us
    squeeze x1 -> x2, local copies, waits for them, and re-layouts: 1.31 us -> 2.19 us  [local(): own.append(columns[stream])]
    pallas_call x6 -> x7, Pallas kernels: 10 us -> 9.65 us  [the longest x2 3.53 us: local(): call(state_kernel, state_type, IN_VMEM, [IN_SMEM] + [IN_VMEM] * 4 + [ANYW...]
  transfers between devices with their start and end apart: 17 -> 17, of which waited for: 9 -> 9; matrix products, arithmetic and copies ran while one was open for 0% -> 2% of each run, Pallas kernels for 18% -> 22%
where the time goes in v8:
time: 91.5 us; the launch traced here: 91.1 us
  waiting for transfers between devices  35.6 us (39%)
  starting transfers between devices  26.5 us (29%)
  Pallas kernels  21.2 us (23%)
  local copies, waits for them, and re-layouts  7.51 us (8%)
    ppermute x6, waiting for transfers between devices, partner_swap(): lax.ppermute(value, axis, [(i, i ^ 1) for i in range(lax.axis_size(axis))])  28.8 us
    ppermute x6, starting transfers between devices, partner_swap(): lax.ppermute(value, axis, [(i, i ^ 1) for i in range(lax.axis_size(axis))])  17.4 us
    pallas_call x2, Pallas kernels, local(): call(partial_kernel, jax.ShapeDtypeStruct((3, width, tokens), jnp.float32...  11.5 us
    ppermute x6, starting transfers between devices, from_others(): got.append(lax.ppermute(sent, axis, pairs))  7.19 us
    ppermute x6, waiting for transfers between devices, from_others(): got.append(lax.ppermute(sent, axis, pairs))  6.75 us
    unnamed x8, local copies, waits for them, and re-layouts  5.19 us
    pallas_call x2, Pallas kernels, local(): call(state_kernel, state_type, IN_VMEM, [IN_SMEM] + [IN_VMEM] * 4 + [ANYW...  3.53 us
    pallas_call x2, Pallas kernels, local(): call(functools.partial(read_kernel, stream, len(parts) + 1), out_type, AN...  2.48 us
  transfers between devices with their start and end apart: 17, of which 9 were waited for; matrix products, arithmetic and copies ran while one was open for 2% of the time, Pallas kernels for 22%

profile of v8, /device:TPU:0, one launch (start us, length us, event | category | flops | bytes accessed | tf_op | source)
XLA Modules:
  0.0 91.1 jit_solution(3346948202960654956)
XLA Ops:
  0.0 1.1 %slice_bitcast_fusion.b0 = bf16[560,512]{1,0:T(8,128)(2,1)S(1)} fusion(bf16[2,560,512]{2,1,0:T(8,128)(2,1)} %bitcast.20), kind=kLoop, calls=%fused_computation | loop fusion | bytes 1146880 | tf_op jit(solution)/shard_map/squeeze | solution.py:188
  1.1 3.1 %collective-permute-start.4 = (bf16[560,512]{1,0:T(8,128)(2,1)S(1)}, bf16[560,512]{1,0:T(8,128)(2,1)S(1)}, u32[]{:S(2)}, u32[]{:S(2)}) collective-permute-start(bf16[560,512]{1,0:T(8,128)(2,1)S(1)} %slice_bitcast_fusion.b0), channel_id=1, source_target_pairs={{0,1},{1,0},{2,3},{3,2},{4,5},{5,4},{6,7},{7,6},{8,9},{9,8},{10,11... | collective-permute-start | bytes 1720328 | tf_op jit(solution)/shard_map/ppermute | solution.py:131
  4.2 1.1 %slice_bitcast_fusion.1.b0 = bf16[560,512]{1,0:T(8,128)(2,1)S(1)} fusion(bf16[2,560,512]{2,1,0:T(8,128)(2,1)} %bitcast.21), kind=kLoop, calls=%fused_computation.1 | loop fusion | bytes 1146880 | tf_op jit(solution)/shard_map/squeeze | solution.py:188
  5.9 2.7 %collective-permute-start.1 = (bf16[560,512]{1,0:T(8,128)(2,1)S(1)}, bf16[560,512]{1,0:T(8,128)(2,1)S(1)}, u32[]{:S(2)}, u32[]{:S(2)}) collective-permute-start(bf16[560,512]{1,0:T(8,128)(2,1)S(1)} %slice_bitcast_fusion.1.b0), channel_id=1, source_target_pairs={{0,1},{1,0},{2,3},{3,2},{4,5},{5,4},{6,7},{7,6},{8,9},{9,8},{10,11... | collective-permute-start | bytes 1720328 | tf_op jit(solution)/shard_map/ppermute | solution.py:131
  8.6 9.4 %collective-permute-done.4.b1 = bf16[560,512]{1,0:T(8,128)(2,1)S(1)} collective-permute-done((bf16[560,512]{1,0:T(8,128)(2,1)S(1)}, bf16[560,512]{1,0:T(8,128)(2,1)S(1)}, u32[]{:S(2)}, u32[]{:S(2)}) %collective-permute-start.4) | collective-permute-done | bytes 573472 | tf_op jit(solution)/shard_map/ppermute | solution.py:131
  18.0 3.2 %collective-permute-start.7 = (bf16[560,512]{1,0:T(8,128)(2,1)S(1)}, bf16[560,512]{1,0:T(8,128)(2,1)}, u32[]{:S(2)}, u32[]{:S(2)}) collective-permute-start(bf16[560,512]{1,0:T(8,128)(2,1)S(1)} %collective-permute-done.6.inner_ref), channel_id=1, source_target_pairs={{0,1},{1,0},{2,3},{3,2},{4,5},{5,4},{6,7},{7,6},{8,9},{9,8},{10,11... | collective-permute-start | bytes 1720328 | tf_op jit(solution)/shard_map/ppermute | solution.py:131
  21.3 1.7 %copy-done = bf16[2240,560]{0,1:T(8,128)(2,1)S(1)} copy-done((bf16[2240,560]{0,1:T(8,128)(2,1)S(1)}, bf16[2240,560]{0,1:T(8,128)(2,1)}, u32[]{:S(2)}) %copy-start) | copy-done | bytes 2508824
  23.0 1.7 %copy-done.1 = bf16[2240,560]{0,1:T(8,128)(2,1)S(1)} copy-done((bf16[2240,560]{0,1:T(8,128)(2,1)S(1)}, bf16[2240,560]{0,1:T(8,128)(2,1)}, u32[]{:S(2)}) %copy-start.1) | copy-done | bytes 2508824
  24.7 1.7 %copy-done.2 = bf16[2240,560]{0,1:T(8,128)(2,1)S(1)} copy-done((bf16[2240,560]{0,1:T(8,128)(2,1)S(1)}, bf16[2240,560]{0,1:T(8,128)(2,1)}, u32[]{:S(2)}) %copy-start.2) | copy-done | bytes 2508824
  26.4 1.3 %shard_map.55.tie.cut = bf16[3,560,560]{2,1,0:T(8,128)(2,1)S(1)} custom-call(s32[2]{0:T(128)S(1)} %pad_add_fusion.place, bf16[560,2240]{1,0:T(8,128)(2,1)S(1)} %bitcast.11, bf16[560,2240]{1,0:T(8,128)(2,1)S(1)} %bitcast.14, bf16[560,2240]{1,0:T(8,128)(2,1)S(1)} %bitcast.17), custom_call_target="tpu_custom_call" | custom-call | flops 5017600 | bytes 1024 | tf_op jit(solution)/shard_map/pallas_call | solution.py:180
  27.8 2.5 %collective-permute-done.1.b1 = bf16[560,512]{1,0:T(8,128)(2,1)S(1)} collective-permute-done((bf16[560,512]{1,0:T(8,128)(2,1)S(1)}, bf16[560,512]{1,0:T(8,128)(2,1)S(1)}, u32[]{:S(2)}, u32[]{:S(2)}) %collective-permute-start.1) | collective-permute-done | bytes 573472 | tf_op jit(solution)/shard_map/ppermute | solution.py:131
  30.3 3.2 %collective-permute-start.3 = (bf16[560,512]{1,0:T(8,128)(2,1)S(1)}, bf16[560,512]{1,0:T(8,128)(2,1)S(1)}, u32[]{:S(2)}, u32[]{:S(2)}) collective-permute-start(bf16[560,512]{1,0:T(8,128)(2,1)S(1)} %collective-permute-done.inner_ref), channel_id=1, source_target_pairs={{0,1},{1,0},{2,3},{3,2},{4,5},{5,4},{6,7},{7,6},{8,9},{9,8},{10,11... | collective-permute-start | bytes 1720328 | tf_op jit(solution)/shard_map/ppermute | solution.py:131
  33.5 9.2 %collective-permute-done.7.b2o = bf16[560,512]{1,0:T(8,128)(2,1)} collective-permute-done((bf16[560,512]{1,0:T(8,128)(2,1)S(1)}, bf16[560,512]{1,0:T(8,128)(2,1)}, u32[]{:S(2)}, u32[]{:S(2)}) %collective-permute-start.7) | collective-permute-done | bytes 573472 | tf_op jit(solution)/shard_map/ppermute | solution.py:131
  42.7 3.2 %collective-permute-start.9 = (bf16[560,512]{1,0:T(8,128)(2,1)}, bf16[560,512]{1,0:T(8,128)(2,1)S(1)}, u32[]{:S(2)}, u32[]{:S(2)}) collective-permute-start(bf16[560,512]{1,0:T(8,128)(2,1)} %collective-permute-done.5.b2i), channel_id=1, source_target_pairs={{0,1},{1,0},{2,3},{3,2},{4,5},{5,4},{6,7},{7,6},{8,9},{9,8},{10,11... | collective-permute-start | bytes 1720328 | tf_op jit(solution)/shard_map/ppermute | solution.py:131
  45.9 6.2 %shard_map.56.sums = f32[3,560,512]{2,1,0:T(8,128)S(1)} custom-call(s32[2]{0:T(128)S(1)} %pad_add_fusion.place, bf16[560,512]{1,0:T(8,128)(2,1)S(1)} %slice_bitcast_fusion.b0, bf16[560,512]{1,0:T(8,128)(2,1)S(1)} %collective-permute-done.4.b1, bf16[560,512]{1,0:T(8,128)(2,1)} %collective-permute-done.5.b2i, bf16[560,512]{1,0:T(8,128)(2,1)} %collective-permute-done.7.b2o, ...), custom_call_target="tpu_custom_call" | custom-call | flops 60211200 | bytes 1024 | tf_op jit(solution)/shard_map/pallas_call | solution.py:206
  52.1 2.8 %collective-permute-done.3.b2o = bf16[560,512]{1,0:T(8,128)(2,1)S(1)} collective-permute-done((bf16[560,512]{1,0:T(8,128)(2,1)S(1)}, bf16[560,512]{1,0:T(8,128)(2,1)S(1)}, u32[]{:S(2)}, u32[]{:S(2)}) %collective-permute-start.3) | collective-permute-done | bytes 573472 | tf_op jit(solution)/shard_map/ppermute | solution.py:131
  54.9 2.1 %collective-permute-start.8 = (bf16[560,512]{1,0:T(8,128)(2,1)S(1)}, bf16[560,512]{1,0:T(8,128)(2,1)S(1)}, u32[]{:S(2)}, u32[]{:S(2)}) collective-permute-start(bf16[560,512]{1,0:T(8,128)(2,1)S(1)} %collective-permute-done.2.b2i), channel_id=1, source_target_pairs={{0,1},{1,0},{2,3},{3,2},{4,5},{5,4},{6,7},{7,6},{8,9},{9,8},{10,11... | collective-permute-start | bytes 1720328 | tf_op jit(solution)/shard_map/ppermute | solution.py:131
  56.9 5.3 %shard_map.57.rest_0_.sums = f32[3,560,512]{2,1,0:T(8,128)S(1)} custom-call(s32[2]{0:T(128)S(1)} %pad_add_fusion.place, bf16[560,512]{1,0:T(8,128)(2,1)S(1)} %slice_bitcast_fusion.1.b0, bf16[560,512]{1,0:T(8,128)(2,1)S(1)} %collective-permute-done.1.b1, bf16[560,512]{1,0:T(8,128)(2,1)S(1)} %collective-permute-done.2.b2i, ...), custom_call_target="tpu_custom_call" | custom-call | flops 60211200 | bytes 1024 | tf_op jit(solution)/shard_map/pallas_call | solution.py:206
  62.2 4.9 %collective-permute-done.9.end_ref = bf16[560,512]{1,0:T(8,128)(2,1)S(1)} collective-permute-done((bf16[560,512]{1,0:T(8,128)(2,1)}, bf16[560,512]{1,0:T(8,128)(2,1)S(1)}, u32[]{:S(2)}, u32[]{:S(2)}) %collective-permute-start.9) | collective-permute-done | bytes 573472 | tf_op jit(solution)/shard_map/ppermute | solution.py:131
  67.1 1.8 %shard_map.58.tie = f32[560,112]{1,0:T(8,128)S(1)} custom-call(s32[2]{0:T(128)S(1)} %pad_add_fusion.place, bf16[560,512]{1,0:T(8,128)(2,1)S(1)} %collective-permute-done.6.inner_ref, bf16[560,512]{1,0:T(8,128)(2,1)S(1)} %collective-permute-done.9.end_ref, bf16[3,560,560]{2,1,0:T(8,128)(2,1)S(1)} %shard_map.55.tie.cut, f32[3,560,512]{2,1,0:T(8,128)S(1)} %shard_map.56.sums, ...), custom_call_target="tpu_custom_call" | custom-call | flops 10035200 | bytes 1024 | tf_op jit(solution)/shard_map/pallas_call | solution.py:213
  69.0 3.0 %collective-permute-start.10 = (bf16[560,112]{1,0:T(8,128)(2,1)S(1)}, bf16[560,112]{1,0:T(8,128)(2,1)S(1)}, u32[]{:S(2)}, u32[]{:S(2)}) collective-permute-start(bf16[560,112]{1,0:T(8,128)(2,1)S(1)} %convert_element_type.16), channel_id=1, source_target_pairs={{0,12},{4,8},{8,4},{12,0},{1,13},{5,9},{9,5},{13,1},{2,14},{6,10},... | collective-permute-start | bytes 376328 | tf_op jit(solution)/shard_map/ppermute | solution.py:154
  72.6 3.8 %collective-permute-done.10 = bf16[560,112]{1,0:T(8,128)(2,1)S(1)} collective-permute-done((bf16[560,112]{1,0:T(8,128)(2,1)S(1)}, bf16[560,112]{1,0:T(8,128)(2,1)S(1)}, u32[]{:S(2)}, u32[]{:S(2)}) %collective-permute-start.10) | collective-permute-done | bytes 125472 | tf_op jit(solution)/shard_map/ppermute | solution.py:154
  76.4 1.1 %collective-permute-done.11 = bf16[560,112]{1,0:T(8,128)(2,1)S(1)} collective-permute-done((bf16[560,112]{1,0:T(8,128)(2,1)S(1)}, bf16[560,112]{1,0:T(8,128)(2,1)S(1)}, u32[]{:S(2)}, u32[]{:S(2)}) %collective-permute-start.11) | collective-permute-done | bytes 125472 | tf_op jit(solution)/shard_map/ppermute | solution.py:154
  77.6 1.3 %collective-permute-start.13 = (f32[560,112]{1,0:T(8,128)S(1)}, f32[560,112]{1,0:T(8,128)S(1)}, u32[]{:S(2)}, u32[]{:S(2)}) collective-permute-start(f32[560,112]{1,0:T(8,128)S(1)} %convert_add_fusion.rest_0_.rest_1_), channel_id=1, source_target_pairs={{0,16},{1,17},{2,18},{3,19},{4,20},{5,21},{6,22},{7,23},{8,24},{9,... | collective-permute-start | bytes 752648 | tf_op jit(solution)/shard_map/ppermute | solution.py:160
  79.0 1.2 %shard_map.59.rest_1_.query = bf16[560,512]{1,0:T(8,128)(2,1)S(1)} custom-call(s32[2]{0:T(128)S(1)} %pad_add_fusion.place, bf16[560,512]{1,0:T(8,128)(2,1)S(1)} %collective-permute-done.6.inner_ref, bf16[560,512]{1,0:T(8,128)(2,1)S(1)} %collective-permute-done.9.end_ref, bf16[3,560,560]{2,1,0:T(8,128)(2,1)S(1)} %shard_map.55.tie.cut, ...), custom_call_target="tpu_custom_call" | custom-call | flops 5017600 | bytes 1024 | tf_op jit(solution)/shard_map/pallas_call | solution.py:217
  80.2 1.8 %shard_map.60.tie.rest_1_ = f32[560,112]{1,0:T(8,128)S(1)} custom-call(s32[2]{0:T(128)S(1)} %pad_add_fusion.place, bf16[560,512]{1,0:T(8,128)(2,1)S(1)} %collective-permute-done.inner_ref, bf16[560,512]{1,0:T(8,128)(2,1)S(1)} %collective-permute-done.8.end_ref, bf16[3,560,560]{2,1,0:T(8,128)(2,1)S(1)} %shard_map.55.tie.cut, ...), custom_call_target="tpu_custom_call" | custom-call | flops 10035200 | bytes 1024 | tf_op jit(solution)/shard_map/pallas_call | solution.py:213
  82.0 1.5 %collective-permute-start.14 = (bf16[560,112]{1,0:T(8,128)(2,1)S(1)}, bf16[560,112]{1,0:T(8,128)(2,1)S(1)}, u32[]{:S(2)}, u32[]{:S(2)}) collective-permute-start(bf16[560,112]{1,0:T(8,128)(2,1)S(1)} %convert_element_type.20), channel_id=1, source_target_pairs={{0,12},{4,8},{8,4},{12,0},{1,13},{5,9},{9,5},{13,1},{2,14},{6,10},... | collective-permute-start | bytes 376328 | tf_op jit(solution)/shard_map/ppermute | solution.py:154
  83.5 1.0 %collective-permute-start.15 = (bf16[560,112]{1,0:T(8,128)(2,1)S(1)}, bf16[560,112]{1,0:T(8,128)(2,1)S(1)}, u32[]{:S(2)}, u32[]{:S(2)}) collective-permute-start(bf16[560,112]{1,0:T(8,128)(2,1)S(1)} %convert_element_type.20), channel_id=1, source_target_pairs={{0,8},{4,12},{8,0},{12,4},{1,9},{5,13},{9,1},{13,5},{2,10},{6,14},... | collective-permute-start | bytes 376328 | tf_op jit(solution)/shard_map/ppermute | solution.py:154
  85.6 1.2 %shard_map.61.query = bf16[560,512]{1,0:T(8,128)(2,1)S(1)} custom-call(s32[2]{0:T(128)S(1)} %pad_add_fusion.place, bf16[560,512]{1,0:T(8,128)(2,1)S(1)} %collective-permute-done.inner_ref, bf16[560,512]{1,0:T(8,128)(2,1)S(1)} %collective-permute-done.8.end_ref, bf16[3,560,560]{2,1,0:T(8,128)(2,1)S(1)} %shard_map.55.tie.cut, ...), custom_call_target="tpu_custom_call" | custom-call | flops 5017600 | bytes 1024 | tf_op jit(solution)/shard_map/pallas_call | solution.py:217
  86.8 1.2 %shard_map.62.rest_5_ = bf16[2,560,512]{2,1,0:T(8,128)(2,1)} custom-call(bf16[560,512]{1,0:T(8,128)(2,1)S(1)} %shard_map.59.rest_1_.query, f32[560,1]{1,0:T(8,128)S(1)} %reshape.5.gain, f32[560,112]{1,0:T(8,128)S(1)} %collective-permute-done.13.rest_0_, f32[560,112]{1,0:T(8,128)S(1)} %convert_add_fusion.rest_0_.rest_1_), custom_call_target="tpu_custom_call" | custom-call | flops 1003520 | bytes 1024 | tf_op jit(solution)/shard_map/pallas_call | solution.py:225
  88.7 1.1 %collective-permute-done.15.rest_3_ = bf16[560,112]{1,0:T(8,128)(2,1)S(1)} collective-permute-done((bf16[560,112]{1,0:T(8,128)(2,1)S(1)}, bf16[560,112]{1,0:T(8,128)(2,1)S(1)}, u32[]{:S(2)}, u32[]{:S(2)}) %collective-permute-start.15) | collective-permute-done | bytes 125472 | tf_op jit(solution)/shard_map/ppermute | solution.py:154
  89.8 1.3 %shard_map.63 = bf16[2,560,512]{2,1,0:T(8,128)(2,1)} custom-call(bf16[560,512]{1,0:T(8,128)(2,1)S(1)} %shard_map.61.query, f32[560,1]{1,0:T(8,128)S(1)} %reshape.5.gain, f32[560,112]{1,0:T(8,128)S(1)} %collective-permute-done.13.rest_0_, f32[560,112]{1,0:T(8,128)S(1)} %shard_map.60.tie.rest_1_, ...), custom_call_target="tpu_custom_call", output_to_operand_aliasing={{}: (7, {})} | custom-call | flops 1003520 | bytes 1024 | tf_op jit(solution)/shard_map/pallas_call | solution.py:225
  (26 shorter events, 3.2 us)
Async XLA Ops:
  1.1 16.9 %collective-permute-start.4 = (bf16[560,512]{1,0:T(8,128)(2,1)S(1)}, bf16[560,512]{1,0:T(8,128)(2,1)S(1)}, u32[]{:S(2)}, u32[]{:S(2)}) collective-permute-start(bf16[560,512]{1,0:T(8,128)(2,1)S(1)} %slice_bitcast_fusion.b0), channel_id=1, source_target_pairs={{0,1},{1,0},{2,3},{3,2},{4,5},{5,4},{6,7},{7,6},{8,9},{9,8},{10,11... | collective-permute-start | bytes 1720328 | tf_op jit(solution)/shard_map/ppermute | solution.py:131
  4.2 13.8 %collective-permute-start.6 = (bf16[560,512]{1,0:T(8,128)(2,1)S(1)}, bf16[560,512]{1,0:T(8,128)(2,1)S(1)}, u32[]{:S(2)}, u32[]{:S(2)}) collective-permute-start(bf16[560,512]{1,0:T(8,128)(2,1)S(1)} %slice_bitcast_fusion.b0), channel_id=1, source_target_pairs={{0,16},{1,2},{2,1},{3,19},{16,0},{17,18},{18,17},{19,3},{4,20},{5,... | collective-permute-start | bytes 1720328 | tf_op jit(solution)/shard_map/ppermute | solution.py:143
  5.3 22.5 %collective-permute-start = (bf16[560,512]{1,0:T(8,128)(2,1)S(1)}, bf16[560,512]{1,0:T(8,128)(2,1)S(1)}, u32[]{:S(2)}, u32[]{:S(2)}) collective-permute-start(bf16[560,512]{1,0:T(8,128)(2,1)S(1)} %slice_bitcast_fusion.1.b0), channel_id=1, source_target_pairs={{0,16},{1,2},{2,1},{3,19},{16,0},{17,18},{18,17},{19,3},{4,20},{5,... | collective-permute-start | bytes 1720328 | tf_op jit(solution)/shard_map/ppermute | solution.py:143
  5.9 24.4 %collective-permute-start.1 = (bf16[560,512]{1,0:T(8,128)(2,1)S(1)}, bf16[560,512]{1,0:T(8,128)(2,1)S(1)}, u32[]{:S(2)}, u32[]{:S(2)}) collective-permute-start(bf16[560,512]{1,0:T(8,128)(2,1)S(1)} %slice_bitcast_fusion.1.b0), channel_id=1, source_target_pairs={{0,1},{1,0},{2,3},{3,2},{4,5},{5,4},{6,7},{7,6},{8,9},{9,8},{10,11... | collective-permute-start | bytes 1720328 | tf_op jit(solution)/shard_map/ppermute | solution.py:131
  18.0 24.7 %collective-permute-start.7 = (bf16[560,512]{1,0:T(8,128)(2,1)S(1)}, bf16[560,512]{1,0:T(8,128)(2,1)}, u32[]{:S(2)}, u32[]{:S(2)}) collective-permute-start(bf16[560,512]{1,0:T(8,128)(2,1)S(1)} %collective-permute-done.6.inner_ref), channel_id=1, source_target_pairs={{0,1},{1,0},{2,3},{3,2},{4,5},{5,4},{6,7},{7,6},{8,9},{9,8},{10,11... | collective-permute-start | bytes 1720328 | tf_op jit(solution)/shard_map/ppermute | solution.py:131
  21.2 21.5 %collective-permute-start.5 = (bf16[560,512]{1,0:T(8,128)(2,1)S(1)}, bf16[560,512]{1,0:T(8,128)(2,1)}, u32[]{:S(2)}, u32[]{:S(2)}) collective-permute-start(bf16[560,512]{1,0:T(8,128)(2,1)S(1)} %collective-permute-done.4.b1), channel_id=1, source_target_pairs={{0,16},{1,2},{2,1},{3,19},{16,0},{17,18},{18,17},{19,3},{4,20},{5,... | collective-permute-start | bytes 1720328 | tf_op jit(solution)/shard_map/ppermute | solution.py:143
  21.3 1.7 %copy-start = (bf16[2240,560]{0,1:T(8,128)(2,1)S(1)}, bf16[2240,560]{0,1:T(8,128)(2,1)}, u32[]{:S(2)}) copy-start(bf16[2240,560]{0,1:T(8,128)(2,1)} %param.7) | copy-start | bytes 7526404
  23.0 1.7 %copy-start.1 = (bf16[2240,560]{0,1:T(8,128)(2,1)S(1)}, bf16[2240,560]{0,1:T(8,128)(2,1)}, u32[]{:S(2)}) copy-start(bf16[2240,560]{0,1:T(8,128)(2,1)} %param.8) | copy-start | bytes 7526404
  24.7 1.7 %copy-start.2 = (bf16[2240,560]{0,1:T(8,128)(2,1)S(1)}, bf16[2240,560]{0,1:T(8,128)(2,1)}, u32[]{:S(2)}) copy-start(bf16[2240,560]{0,1:T(8,128)(2,1)} %param.6) | copy-start | bytes 7526404
  30.3 24.6 %collective-permute-start.3 = (bf16[560,512]{1,0:T(8,128)(2,1)S(1)}, bf16[560,512]{1,0:T(8,128)(2,1)S(1)}, u32[]{:S(2)}, u32[]{:S(2)}) collective-permute-start(bf16[560,512]{1,0:T(8,128)(2,1)S(1)} %collective-permute-done.inner_ref), channel_id=1, source_target_pairs={{0,1},{1,0},{2,3},{3,2},{4,5},{5,4},{6,7},{7,6},{8,9},{9,8},{10,11... | collective-permute-start | bytes 1720328 | tf_op jit(solution)/shard_map/ppermute | solution.py:131
  33.5 21.4 %collective-permute-start.2 = (bf16[560,512]{1,0:T(8,128)(2,1)S(1)}, bf16[560,512]{1,0:T(8,128)(2,1)S(1)}, u32[]{:S(2)}, u32[]{:S(2)}) collective-permute-start(bf16[560,512]{1,0:T(8,128)(2,1)S(1)} %collective-permute-done.1.b1), channel_id=1, source_target_pairs={{0,16},{1,2},{2,1},{3,19},{16,0},{17,18},{18,17},{19,3},{4,20},{5,... | collective-permute-start | bytes 1720328 | tf_op jit(solution)/shard_map/ppermute | solution.py:143
  42.7 24.5 %collective-permute-start.9 = (bf16[560,512]{1,0:T(8,128)(2,1)}, bf16[560,512]{1,0:T(8,128)(2,1)S(1)}, u32[]{:S(2)}, u32[]{:S(2)}) collective-permute-start(bf16[560,512]{1,0:T(8,128)(2,1)} %collective-permute-done.5.b2i), channel_id=1, source_target_pairs={{0,1},{1,0},{2,3},{3,2},{4,5},{5,4},{6,7},{7,6},{8,9},{9,8},{10,11... | collective-permute-start | bytes 1720328 | tf_op jit(solution)/shard_map/ppermute | solution.py:131
  54.9 25.3 %collective-permute-start.8 = (bf16[560,512]{1,0:T(8,128)(2,1)S(1)}, bf16[560,512]{1,0:T(8,128)(2,1)S(1)}, u32[]{:S(2)}, u32[]{:S(2)}) collective-permute-start(bf16[560,512]{1,0:T(8,128)(2,1)S(1)} %collective-permute-done.2.b2i), channel_id=1, source_target_pairs={{0,1},{1,0},{2,3},{3,2},{4,5},{5,4},{6,7},{7,6},{8,9},{9,8},{10,11... | collective-permute-start | bytes 1720328 | tf_op jit(solution)/shard_map/ppermute | solution.py:131
  69.0 7.5 %collective-permute-start.10 = (bf16[560,112]{1,0:T(8,128)(2,1)S(1)}, bf16[560,112]{1,0:T(8,128)(2,1)S(1)}, u32[]{:S(2)}, u32[]{:S(2)}) collective-permute-start(bf16[560,112]{1,0:T(8,128)(2,1)S(1)} %convert_element_type.16), channel_id=1, source_target_pairs={{0,12},{4,8},{8,4},{12,0},{1,13},{5,9},{9,5},{13,1},{2,14},{6,10},... | collective-permute-start | bytes 376328 | tf_op jit(solution)/shard_map/ppermute | solution.py:154
  71.9 5.6 %collective-permute-start.11 = (bf16[560,112]{1,0:T(8,128)(2,1)S(1)}, bf16[560,112]{1,0:T(8,128)(2,1)S(1)}, u32[]{:S(2)}, u32[]{:S(2)}) collective-permute-start(bf16[560,112]{1,0:T(8,128)(2,1)S(1)} %convert_element_type.16), channel_id=1, source_target_pairs={{0,8},{4,12},{8,0},{12,4},{1,9},{5,13},{9,1},{13,5},{2,10},{6,14},... | collective-permute-start | bytes 376328 | tf_op jit(solution)/shard_map/ppermute | solution.py:154
  72.5 5.1 %collective-permute-start.12 = (bf16[560,112]{1,0:T(8,128)(2,1)S(1)}, bf16[560,112]{1,0:T(8,128)(2,1)S(1)}, u32[]{:S(2)}, u32[]{:S(2)}) collective-permute-start(bf16[560,112]{1,0:T(8,128)(2,1)S(1)} %convert_element_type.16), channel_id=1, source_target_pairs={{0,4},{4,0},{8,12},{12,8},{1,5},{5,1},{9,13},{13,9},{2,6},{6,2},{1... | collective-permute-start | bytes 376328 | tf_op jit(solution)/shard_map/ppermute | solution.py:154
  77.6 9.2 %collective-permute-start.13 = (f32[560,112]{1,0:T(8,128)S(1)}, f32[560,112]{1,0:T(8,128)S(1)}, u32[]{:S(2)}, u32[]{:S(2)}) collective-permute-start(f32[560,112]{1,0:T(8,128)S(1)} %convert_add_fusion.rest_0_.rest_1_), channel_id=1, source_target_pairs={{0,16},{1,17},{2,18},{3,19},{4,20},{5,21},{6,22},{7,23},{8,24},{9,... | collective-permute-start | bytes 752648 | tf_op jit(solution)/shard_map/ppermute | solution.py:160
  80.1 5.4 %copy-start.3 = (f32[560]{0:T(1024)S(1)}, f32[560]{0:T(1024)}, u32[]{:S(2)}) copy-start(f32[560]{0:T(1024)} %param.9) | copy-start | bytes 6724
  82.0 6.8 %collective-permute-start.14 = (bf16[560,112]{1,0:T(8,128)(2,1)S(1)}, bf16[560,112]{1,0:T(8,128)(2,1)S(1)}, u32[]{:S(2)}, u32[]{:S(2)}) collective-permute-start(bf16[560,112]{1,0:T(8,128)(2,1)S(1)} %convert_element_type.20), channel_id=1, source_target_pairs={{0,12},{4,8},{8,4},{12,0},{1,13},{5,9},{9,5},{13,1},{2,14},{6,10},... | collective-permute-start | bytes 376328 | tf_op jit(solution)/shard_map/ppermute | solution.py:154
  83.5 6.3 %collective-permute-start.15 = (bf16[560,112]{1,0:T(8,128)(2,1)S(1)}, bf16[560,112]{1,0:T(8,128)(2,1)S(1)}, u32[]{:S(2)}, u32[]{:S(2)}) collective-permute-start(bf16[560,112]{1,0:T(8,128)(2,1)S(1)} %convert_element_type.20), channel_id=1, source_target_pairs={{0,8},{4,12},{8,0},{12,4},{1,9},{5,13},{9,1},{13,5},{2,10},{6,14},... | collective-permute-start | bytes 376328 | tf_op jit(solution)/shard_map/ppermute | solution.py:154
  84.5 5.3 %collective-permute-start.16 = (bf16[560,112]{1,0:T(8,128)(2,1)S(1)}, bf16[560,112]{1,0:T(8,128)(2,1)S(1)}, u32[]{:S(2)}, u32[]{:S(2)}) collective-permute-start(bf16[560,112]{1,0:T(8,128)(2,1)S(1)} %convert_element_type.20), channel_id=1, source_target_pairs={{0,4},{4,0},{8,12},{12,8},{1,5},{5,1},{9,13},{13,9},{2,6},{6,2},{1... | collective-permute-start | bytes 376328 | tf_op jit(solution)/shard_map/ppermute | solution.py:154

commit v9 on v8

--- a/solution.py
+++ b/solution.py
@@ -56,11 +56,11 @@
         pltpu.make_async_copy(at(flip), at(flip), sems.at[flip]).wait()
 
 
-def partial_kernel(place, b0, b1, b2i, b2o, wq, wk, wv, tie, sums, whole, sems):
-    rows, tokens = b0.shape
+def partial_kernel(stream, place, own, near, b2i, b2o, wq, wk, wv, tie, sums, whole, sems):
+    rows, tokens = b2i.shape
     missing = pl.ds(pl.multiple_of((place[0] ^ 3) * rows, 16), rows)
     whole[missing, :] = jnp.zeros((rows, tokens), whole.dtype)
-    load_blocks(place, [b0, b1, (b2i, b2o)], whole, sems)
+    load_blocks(place, [own.at[stream], near.at[stream], (b2i, b2o)], whole, sems)
     width, tiles = token_tiles(tokens)
 
     @pl.loop(0, tiles)
@@ -181,16 +181,13 @@
         functools.partial(cut_kernel, count), jax.ShapeDtypeStruct((3, width, rows), jnp.bfloat16), IN_VMEM,
         [IN_SMEM] + [IN_VMEM] * 3, [], one // 4,
     )(place, matrices[1], matrices[2], matrices[0])
-    own, near, across, far, across_end, far_end = [], [], [], [], [], []
-    for stream in range(2):
-        if own:
-            columns, own[0] = lax.optimization_barrier((columns, own[0]))
-        own.append(columns[stream])
-        near.append(partner_swap(own[stream], "head"))
-        across.append(middle_swap(own[stream], "head", "group"))
+    across, far, across_end, far_end = [], [], [], []
+    near = partner_swap(columns, "head")
+    for stream in range(2):
+        across.append(middle_swap(columns[stream], "head", "group"))
     for stream in range(2):
         far.append(middle_swap(near[stream], "head", "group"))
-        ready, *_ = lax.optimization_barrier((across[stream], near[stream], *([cut] if stream else [])))
+        ready, *_ = lax.optimization_barrier((across[stream], *([cut] if stream else [])))
         across_end.append(partner_swap(ready, "head"))
     whole = pltpu.VMEM((depth, tokens), jnp.bfloat16)
     sems = pltpu.SemaphoreType.DMA((4,))
@@ -204,9 +201,9 @@
         ready, *_ = lax.optimization_barrier((far[stream], across_end[stream], *sums))
         far_end.append(partner_swap(ready, "head"))
         sums.append(call(
-            partial_kernel, jax.ShapeDtypeStruct((3, width, tokens), jnp.float32), IN_VMEM,
+            functools.partial(partial_kernel, stream), jax.ShapeDtypeStruct((3, width, tokens), jnp.float32), IN_VMEM,
             [IN_SMEM] + [ANYWHERE] * 4 + [IN_VMEM] * 3 + [ANYWHERE], [whole, sems], 3 * one,
-        )(place, own[stream], near[stream], far[stream], across_end[stream], *matrices, cut))
+        )(place, columns, near, far[stream], across_end[stream], *matrices, cut))
     prefix = parts = query = out = None
     for stream in range(2):
         ties = (sums[1],) if stream == 0 else (parts[0], query)
@@ -219,6 +216,7 @@
         )(place, across[stream], far_end[stream], cut, sums[stream], state)
         parts = [state, *from_others(state, "tok")]
         if stream == 0:
+            query, *parts = lax.optimization_barrier((query, *parts))
             parts = [sum(part.astype(jnp.float32) for part in parts)]
             prefix = entering(parts[0], "group")
         kept = [] if out is None else [out]

time: 91.5 us -> 90.7 us (level)
  waiting for transfers between devices: 35.6 us -> 19.3 us
  starting transfers between devices: 26.5 us -> 40.6 us
  Pallas kernels: 21.2 us -> 22.2 us
    ppermute x6 -> x5, waiting for transfers between devices: 28.8 us -> 11 us  [partner_swap(): lax.ppermute(value, axis, [(i, i ^ 1) for i in range(lax.axis_size(axis))])]
    ppermute x6 -> x5, starting transfers between devices: 17.4 us -> 31.6 us  [partner_swap(): lax.ppermute(value, axis, [(i, i ^ 1) for i in range(lax.axis_size(axis))])]
    ppermute x4, waiting for transfers between devices: 0.01 us -> 2.4 us  [middle_swap(): return lax.ppermute(value, (other, axis), pairs)]
    squeeze x2, local copies, waits for them, and re-layouts: 2.19 us -> 3.22 us  [the longest x1 2.12 us: local(): across.append(middle_swap(columns[stream], 'head', 'group'))]
    unnamed x8 -> x16, local copies, waits for them, and re-layouts: 5.19 us -> 4.48 us
  transfers between devices with their start and end apart: 17 -> 16, of which waited for: 9 -> 9; matrix products, arithmetic and copies ran while one was open for 2% -> 4% of each run, Pallas kernels for 22% -> 23%
where the time goes in v9:
time: 90.7 us; the launch traced here: 90.3 us
  starting transfers between devices  40.6 us (45%)
  Pallas kernels  22.2 us (24%)
  waiting for transfers between devices  19.3 us (21%)
  local copies, waits for them, and re-layouts  7.83 us (9%)
    ppermute x5, starting transfers between devices, partner_swap(): lax.ppermute(value, axis, [(i, i ^ 1) for i in range(lax.axis_size(axis))])  31.6 us
    pallas_call x2, Pallas kernels, local(): call(functools.partial(partial_kernel, stream), jax.ShapeDtypeStruct((3,...  11.5 us
    ppermute x5, waiting for transfers between devices, partner_swap(): lax.ppermute(value, axis, [(i, i ^ 1) for i in range(lax.axis_size(axis))])  11 us
    ppermute x6, starting transfers between devices, from_others(): got.append(lax.ppermute(sent, axis, pairs))  7.11 us
    ppermute x6, waiting for transfers between devices, from_others(): got.append(lax.ppermute(sent, axis, pairs))  5.93 us
    unnamed x16, local copies, waits for them, and re-layouts  4.48 us
    pallas_call x2, Pallas kernels, local(): call(state_kernel, state_type, IN_VMEM, [IN_SMEM] + [IN_VMEM] * 4 + [ANYW...  4.05 us
    pallas_call x2, Pallas kernels, local(): call(query_kernel, query_type, IN_VMEM, [IN_SMEM] + [IN_VMEM] * 4 + [ANYW...  2.86 us
  transfers between devices with their start and end apart: 16, of which 9 were waited for; matrix products, arithmetic and copies ran while one was open for 4% of the time, Pallas kernels for 23%

profile of v9, /device:TPU:0, one launch (start us, length us, event | category | flops | bytes accessed | tf_op | source)
XLA Modules:
  0.0 90.3 jit_solution(16570157418112362207)
XLA Ops:
  0.0 3.0 %collective-permute-start.1 = (bf16[2,560,512]{2,1,0:T(8,128)(2,1)}, bf16[2,560,512]{2,1,0:T(8,128)(2,1)S(1)}, u32[]{:S(2)}, u32[]{:S(2)}) collective-permute-start(bf16[2,560,512]{2,1,0:T(8,128)(2,1)} %bitcast.24), channel_id=1, source_target_pairs={{0,1},{1,0},{2,3},{3,2},{4,5},{5,4},{6,7},{7,6},{8,9},{9,8},{10,11... | collective-permute-start | bytes 3440648 | tf_op jit(solution)/shard_map/ppermute | solution.py:131
  3.0 2.1 %slice_bitcast_fusion = (bf16[560,512]{1,0:T(8,128)(2,1)S(1)}, bf16[560,512]{1,0:T(8,128)(2,1)}) fusion(bf16[2,560,512]{2,1,0:T(8,128)(2,1)} %bitcast.25), kind=kLoop, calls=%fused_computation | loop fusion | bytes 2293760 | tf_op jit(solution)/shard_map/squeeze | solution.py:187
  5.7 2.4 %collective-permute-done.5.inner_ref = bf16[560,512]{1,0:T(8,128)(2,1)} collective-permute-done((bf16[560,512]{1,0:T(8,128)(2,1)S(1)}, bf16[560,512]{1,0:T(8,128)(2,1)}, u32[]{:S(2)}, u32[]{:S(2)}) %collective-permute-start.5) | collective-permute-done | bytes 573472 | tf_op jit(solution)/shard_map/ppermute | solution.py:143
  8.0 14.2 %collective-permute-start.6 = (bf16[560,512]{1,0:T(8,128)(2,1)}, bf16[560,512]{1,0:T(8,128)(2,1)}, u32[]{:S(2)}, u32[]{:S(2)}) collective-permute-start(bf16[560,512]{1,0:T(8,128)(2,1)} %collective-permute-done.5.inner_ref), channel_id=1, source_target_pairs={{0,1},{1,0},{2,3},{3,2},{4,5},{5,4},{6,7},{7,6},{8,9},{9,8},{10,11... | collective-permute-start | bytes 1720328 | tf_op jit(solution)/shard_map/ppermute | solution.py:131
  22.2 7.1 %collective-permute-done.1.near = bf16[2,560,512]{2,1,0:T(8,128)(2,1)S(1)} collective-permute-done((bf16[2,560,512]{2,1,0:T(8,128)(2,1)}, bf16[2,560,512]{2,1,0:T(8,128)(2,1)S(1)}, u32[]{:S(2)}, u32[]{:S(2)}) %collective-permute-start.1) | collective-permute-done | bytes 1146912 | tf_op jit(solution)/shard_map/ppermute | solution.py:131
  29.3 1.1 %slice_bitcast_fusion.1 = (bf16[560,512]{1,0:T(8,128)(2,1)}, bf16[560,512]{1,0:T(8,128)(2,1)}) fusion(bf16[2,560,512]{2,1,0:T(8,128)(2,1)S(1)} %collective-permute-done.1.near), kind=kLoop, calls=%fused_computation.1 | loop fusion | bytes 2293760 | tf_op jit(solution)/shard_map/squeeze | solution.py:189
  30.4 1.0 %copy-done.4 = bf16[2,560,512]{2,1,0:T(8,128)(2,1)} copy-done((bf16[2,560,512]{2,1,0:T(8,128)(2,1)}, bf16[2,560,512]{2,1,0:T(8,128)(2,1)S(1)}, u32[]{:S(2)}) %copy-start.4) | copy-done | bytes 1146904
  31.5 1.7 %copy-done.1 = bf16[2240,560]{0,1:T(8,128)(2,1)S(1)} copy-done((bf16[2240,560]{0,1:T(8,128)(2,1)S(1)}, bf16[2240,560]{0,1:T(8,128)(2,1)}, u32[]{:S(2)}) %copy-start.1) | copy-done | bytes 2508824
  33.2 1.7 %copy-done.2 = bf16[2240,560]{0,1:T(8,128)(2,1)S(1)} copy-done((bf16[2240,560]{0,1:T(8,128)(2,1)S(1)}, bf16[2240,560]{0,1:T(8,128)(2,1)}, u32[]{:S(2)}) %copy-start.2) | copy-done | bytes 2508824
  35.0 1.3 %shard_map.55.tie.cut = bf16[3,560,560]{2,1,0:T(8,128)(2,1)S(1)} custom-call(s32[2]{0:T(128)S(1)} %pad_add_fusion.place, bf16[560,2240]{1,0:T(8,128)(2,1)S(1)} %bitcast.15, bf16[560,2240]{1,0:T(8,128)(2,1)S(1)} %bitcast.18, bf16[560,2240]{1,0:T(8,128)(2,1)S(1)} %bitcast.21), custom_call_target="tpu_custom_call" | custom-call | flops 5017600 | bytes 1024 | tf_op jit(solution)/shard_map/pallas_call | solution.py:180
  36.3 3.7 %collective-permute-start.3 = (bf16[560,512]{1,0:T(8,128)(2,1)S(1)}, bf16[560,512]{1,0:T(8,128)(2,1)S(1)}, u32[]{:S(2)}, u32[]{:S(2)}) collective-permute-start(bf16[560,512]{1,0:T(8,128)(2,1)S(1)} %collective-permute-done.inner_ref), channel_id=1, source_target_pairs={{0,1},{1,0},{2,3},{3,2},{4,5},{5,4},{6,7},{7,6},{8,9},{9,8},{10,11... | collective-permute-start | bytes 1720328 | tf_op jit(solution)/shard_map/ppermute | solution.py:131
  40.0 1.7 %collective-permute-done.6.b2o = bf16[560,512]{1,0:T(8,128)(2,1)} collective-permute-done((bf16[560,512]{1,0:T(8,128)(2,1)}, bf16[560,512]{1,0:T(8,128)(2,1)}, u32[]{:S(2)}, u32[]{:S(2)}) %collective-permute-start.6) | collective-permute-done | bytes 573472 | tf_op jit(solution)/shard_map/ppermute | solution.py:131
  41.7 8.0 %collective-permute-start.8 = (bf16[560,512]{1,0:T(8,128)(2,1)}, bf16[560,512]{1,0:T(8,128)(2,1)S(1)}, u32[]{:S(2)}, u32[]{:S(2)}) collective-permute-start(bf16[560,512]{1,0:T(8,128)(2,1)} %collective-permute-done.4.b2i), channel_id=1, source_target_pairs={{0,1},{1,0},{2,3},{3,2},{4,5},{5,4},{6,7},{7,6},{8,9},{9,8},{10,11... | collective-permute-start | bytes 1720328 | tf_op jit(solution)/shard_map/ppermute | solution.py:131
  49.7 6.2 %shard_map.56.sums = f32[3,560,512]{2,1,0:T(8,128)S(1)} custom-call(s32[2]{0:T(128)S(1)} %pad_add_fusion.place, bf16[2,560,512]{2,1,0:T(8,128)(2,1)S(1)} %bitcast.26, bf16[2,560,512]{2,1,0:T(8,128)(2,1)S(1)} %copy-done.5, bf16[560,512]{1,0:T(8,128)(2,1)} %collective-permute-done.4.b2i, bf16[560,512]{1,0:T(8,128)(2,1)} %collective-permute-done.6.b2o, ...), custom_call_target="tpu_custom_call" | custom-call | flops 60211200 | bytes 1024 | tf_op jit(solution)/shard_map/pallas_call | solution.py:203
  56.0 2.7 %collective-permute-start.7 = (bf16[560,512]{1,0:T(8,128)(2,1)S(1)}, bf16[560,512]{1,0:T(8,128)(2,1)S(1)}, u32[]{:S(2)}, u32[]{:S(2)}) collective-permute-start(bf16[560,512]{1,0:T(8,128)(2,1)S(1)} %collective-permute-done.2.b2i), channel_id=1, source_target_pairs={{0,1},{1,0},{2,3},{3,2},{4,5},{5,4},{6,7},{7,6},{8,9},{9,8},{10,11... | collective-permute-start | bytes 1720328 | tf_op jit(solution)/shard_map/ppermute | solution.py:131
  58.7 5.3 %shard_map.57.rest_0_.sums = f32[3,560,512]{2,1,0:T(8,128)S(1)} custom-call(s32[2]{0:T(128)S(1)} %pad_add_fusion.place, bf16[2,560,512]{2,1,0:T(8,128)(2,1)S(1)} %bitcast.27, bf16[2,560,512]{2,1,0:T(8,128)(2,1)S(1)} %copy-done.5, bf16[560,512]{1,0:T(8,128)(2,1)S(1)} %collective-permute-done.2.b2i, bf16[560,512]{1,0:T(8,128)(2,1)S(1)} %collective-permute-done.3.b2o, ...), custom_call_target="tpu_custom_call" | custom-call | flops 60211200 | bytes 1024 | tf_op jit(solution)/shard_map/pallas_call | solution.py:203
  64.0 2.2 %collective-permute-done.8.end_ref = bf16[560,512]{1,0:T(8,128)(2,1)S(1)} collective-permute-done((bf16[560,512]{1,0:T(8,128)(2,1)}, bf16[560,512]{1,0:T(8,128)(2,1)S(1)}, u32[]{:S(2)}, u32[]{:S(2)}) %collective-permute-start.8) | collective-permute-done | bytes 573472 | tf_op jit(solution)/shard_map/ppermute | solution.py:131
  66.2 2.3 %shard_map.58.tie = f32[560,112]{1,0:T(8,128)S(1)} custom-call(s32[2]{0:T(128)S(1)} %pad_add_fusion.place, bf16[560,512]{1,0:T(8,128)(2,1)} %collective-permute-done.5.inner_ref, bf16[560,512]{1,0:T(8,128)(2,1)S(1)} %collective-permute-done.8.end_ref, bf16[3,560,560]{2,1,0:T(8,128)(2,1)S(1)} %shard_map.55.tie.cut, f32[3,560,512]{2,1,0:T(8,128)S(1)} %shard_map.56.sums, ...), custom_call_target="tpu_custom_call" | custom-call | flops 10035200 | bytes 1024 | tf_op jit(solution)/shard_map/pallas_call | solution.py:210
  68.5 1.9 %collective-permute-start.10 = (bf16[560,112]{1,0:T(8,128)(2,1)S(1)}, bf16[560,112]{1,0:T(8,128)(2,1)S(1)}, u32[]{:S(2)}, u32[]{:S(2)}) collective-permute-start(bf16[560,112]{1,0:T(8,128)(2,1)S(1)} %convert_element_type.16), channel_id=1, source_target_pairs={{0,8},{4,12},{8,0},{12,4},{1,9},{5,13},{9,1},{13,5},{2,10},{6,14},... | collective-permute-start | bytes 376328 | tf_op jit(solution)/shard_map/ppermute | solution.py:154
  70.4 1.5 %collective-permute-start.11 = (bf16[560,112]{1,0:T(8,128)(2,1)S(1)}, bf16[560,112]{1,0:T(8,128)(2,1)S(1)}, u32[]{:S(2)}, u32[]{:S(2)}) collective-permute-start(bf16[560,112]{1,0:T(8,128)(2,1)S(1)} %convert_element_type.16), channel_id=1, source_target_pairs={{0,4},{4,0},{8,12},{12,8},{1,5},{5,1},{9,13},{13,9},{2,6},{6,2},{1... | collective-permute-start | bytes 376328 | tf_op jit(solution)/shard_map/ppermute | solution.py:154
  72.1 1.7 %shard_map.59.rest_1_.query = bf16[560,512]{1,0:T(8,128)(2,1)S(1)} custom-call(s32[2]{0:T(128)S(1)} %pad_add_fusion.place, bf16[560,512]{1,0:T(8,128)(2,1)} %collective-permute-done.5.inner_ref, bf16[560,512]{1,0:T(8,128)(2,1)S(1)} %collective-permute-done.8.end_ref, bf16[3,560,560]{2,1,0:T(8,128)(2,1)S(1)} %shard_map.55.tie.cut, ...), custom_call_target="tpu_custom_call" | custom-call | flops 5017600 | bytes 1024 | tf_op jit(solution)/shard_map/pallas_call | solution.py:214
  73.8 1.1 %collective-permute-done.10 = bf16[560,112]{1,0:T(8,128)(2,1)S(1)} collective-permute-done((bf16[560,112]{1,0:T(8,128)(2,1)S(1)}, bf16[560,112]{1,0:T(8,128)(2,1)S(1)}, u32[]{:S(2)}, u32[]{:S(2)}) %collective-permute-start.10) | collective-permute-done | bytes 125472 | tf_op jit(solution)/shard_map/ppermute | solution.py:154
  75.6 2.3 %collective-permute-done.9 = bf16[560,112]{1,0:T(8,128)(2,1)S(1)} collective-permute-done((bf16[560,112]{1,0:T(8,128)(2,1)S(1)}, bf16[560,112]{1,0:T(8,128)(2,1)S(1)}, u32[]{:S(2)}, u32[]{:S(2)}) %collective-permute-start.9) | collective-permute-done | bytes 125472 | tf_op jit(solution)/shard_map/ppermute | solution.py:154
  78.0 1.3 %collective-permute-start.12 = (f32[560,112]{1,0:T(8,128)S(1)}, f32[560,112]{1,0:T(8,128)S(1)}, u32[]{:S(2)}, u32[]{:S(2)}) collective-permute-start(f32[560,112]{1,0:T(8,128)S(1)} %convert_add_fusion.rest_0_.rest_1_), channel_id=1, source_target_pairs={{0,16},{1,17},{2,18},{3,19},{4,20},{5,21},{6,22},{7,23},{8,24},{9,... | collective-permute-start | bytes 752648 | tf_op jit(solution)/shard_map/ppermute | solution.py:160
  79.3 1.7 %shard_map.60.tie.rest_1_ = f32[560,112]{1,0:T(8,128)S(1)} custom-call(s32[2]{0:T(128)S(1)} %pad_add_fusion.place, bf16[560,512]{1,0:T(8,128)(2,1)S(1)} %collective-permute-done.inner_ref, bf16[560,512]{1,0:T(8,128)(2,1)S(1)} %collective-permute-done.7.end_ref, bf16[3,560,560]{2,1,0:T(8,128)(2,1)S(1)} %shard_map.55.tie.cut, ...), custom_call_target="tpu_custom_call" | custom-call | flops 10035200 | bytes 1024 | tf_op jit(solution)/shard_map/pallas_call | solution.py:210
  81.1 1.7 %collective-permute-start.13 = (bf16[560,112]{1,0:T(8,128)(2,1)S(1)}, bf16[560,112]{1,0:T(8,128)(2,1)S(1)}, u32[]{:S(2)}, u32[]{:S(2)}) collective-permute-start(bf16[560,112]{1,0:T(8,128)(2,1)S(1)} %convert_element_type.20), channel_id=1, source_target_pairs={{0,12},{4,8},{8,4},{12,0},{1,13},{5,9},{9,5},{13,1},{2,14},{6,10},... | collective-permute-start | bytes 376328 | tf_op jit(solution)/shard_map/ppermute | solution.py:154
  83.3 1.4 %collective-permute-start.15 = (bf16[560,112]{1,0:T(8,128)(2,1)S(1)}, bf16[560,112]{1,0:T(8,128)(2,1)S(1)}, u32[]{:S(2)}, u32[]{:S(2)}) collective-permute-start(bf16[560,112]{1,0:T(8,128)(2,1)S(1)} %convert_element_type.20), channel_id=1, source_target_pairs={{0,4},{4,0},{8,12},{12,8},{1,5},{5,1},{9,13},{13,9},{2,6},{6,2},{1... | collective-permute-start | bytes 376328 | tf_op jit(solution)/shard_map/ppermute | solution.py:154
  84.8 1.2 %shard_map.61.query = bf16[560,512]{1,0:T(8,128)(2,1)S(1)} custom-call(s32[2]{0:T(128)S(1)} %pad_add_fusion.place, bf16[560,512]{1,0:T(8,128)(2,1)S(1)} %collective-permute-done.inner_ref, bf16[560,512]{1,0:T(8,128)(2,1)S(1)} %collective-permute-done.7.end_ref, bf16[3,560,560]{2,1,0:T(8,128)(2,1)S(1)} %shard_map.55.tie.cut, ...), custom_call_target="tpu_custom_call" | custom-call | flops 5017600 | bytes 1024 | tf_op jit(solution)/shard_map/pallas_call | solution.py:214
  86.0 1.2 %shard_map.62.rest_5_ = bf16[2,560,512]{2,1,0:T(8,128)(2,1)} custom-call(bf16[560,512]{1,0:T(8,128)(2,1)S(1)} %shard_map.59.rest_1_.query, f32[560,1]{1,0:T(8,128)S(1)} %reshape.5.gain, f32[560,112]{1,0:T(8,128)S(1)} %collective-permute-done.12.rest_0_, f32[560,112]{1,0:T(8,128)S(1)} %convert_add_fusion.rest_0_.rest_1_), custom_call_target="tpu_custom_call" | custom-call | flops 1003520 | bytes 1024 | tf_op jit(solution)/shard_map/pallas_call | solution.py:223
  87.2 0.8 collective-permute-done.13.rest_2_
  88.0 1.1 %collective-permute-done.14.rest_3_ = bf16[560,112]{1,0:T(8,128)(2,1)S(1)} collective-permute-done((bf16[560,112]{1,0:T(8,128)(2,1)S(1)}, bf16[560,112]{1,0:T(8,128)(2,1)S(1)}, u32[]{:S(2)}, u32[]{:S(2)}) %collective-permute-start.14) | collective-permute-done | bytes 125472 | tf_op jit(solution)/shard_map/ppermute | solution.py:154
  89.0 1.3 %shard_map.63 = bf16[2,560,512]{2,1,0:T(8,128)(2,1)} custom-call(bf16[560,512]{1,0:T(8,128)(2,1)S(1)} %shard_map.61.query, f32[560,1]{1,0:T(8,128)S(1)} %reshape.5.gain, f32[560,112]{1,0:T(8,128)S(1)} %collective-permute-done.12.rest_0_, f32[560,112]{1,0:T(8,128)S(1)} %shard_map.60.tie.rest_1_, ...), custom_call_target="tpu_custom_call", output_to_operand_aliasing={{}: (7, {})} | custom-call | flops 1003520 | bytes 1024 | tf_op jit(solution)/shard_map/pallas_call | solution.py:223
  (32 shorter events, 2.3 us)
Async XLA Ops:
  0.0 31.5 %copy-start = (bf16[2240,560]{0,1:T(8,128)(2,1)S(1)}, bf16[2240,560]{0,1:T(8,128)(2,1)}, u32[]{:S(2)}) copy-start(bf16[2240,560]{0,1:T(8,128)(2,1)} %param.7) | copy-start | bytes 7526404
  0.0 29.3 %collective-permute-start.1 = (bf16[2,560,512]{2,1,0:T(8,128)(2,1)}, bf16[2,560,512]{2,1,0:T(8,128)(2,1)S(1)}, u32[]{:S(2)}, u32[]{:S(2)}) collective-permute-start(bf16[2,560,512]{2,1,0:T(8,128)(2,1)} %bitcast.24), channel_id=1, source_target_pairs={{0,1},{1,0},{2,3},{3,2},{4,5},{5,4},{6,7},{7,6},{8,9},{9,8},{10,11... | collective-permute-start | bytes 3440648 | tf_op jit(solution)/shard_map/ppermute | solution.py:131
  5.1 2.9 %collective-permute-start.5 = (bf16[560,512]{1,0:T(8,128)(2,1)S(1)}, bf16[560,512]{1,0:T(8,128)(2,1)}, u32[]{:S(2)}, u32[]{:S(2)}) collective-permute-start(bf16[560,512]{1,0:T(8,128)(2,1)S(1)} %get-tuple-element.21), channel_id=1, source_target_pairs={{0,16},{1,2},{2,1},{3,19},{16,0},{17,18},{18,17},{19,3},{4,20},{5,... | collective-permute-start | bytes 1720328 | tf_op jit(solution)/shard_map/ppermute | solution.py:143
  5.1 31.1 %collective-permute-start = (bf16[560,512]{1,0:T(8,128)(2,1)}, bf16[560,512]{1,0:T(8,128)(2,1)S(1)}, u32[]{:S(2)}, u32[]{:S(2)}) collective-permute-start(bf16[560,512]{1,0:T(8,128)(2,1)} %get-tuple-element.22), channel_id=1, source_target_pairs={{0,16},{1,2},{2,1},{3,19},{16,0},{17,18},{18,17},{19,3},{4,20},{5,... | collective-permute-start | bytes 1720328 | tf_op jit(solution)/shard_map/ppermute | solution.py:143
  8.0 33.7 %collective-permute-start.6 = (bf16[560,512]{1,0:T(8,128)(2,1)}, bf16[560,512]{1,0:T(8,128)(2,1)}, u32[]{:S(2)}, u32[]{:S(2)}) collective-permute-start(bf16[560,512]{1,0:T(8,128)(2,1)} %collective-permute-done.5.inner_ref), channel_id=1, source_target_pairs={{0,1},{1,0},{2,3},{3,2},{4,5},{5,4},{6,7},{7,6},{8,9},{9,8},{10,11... | collective-permute-start | bytes 1720328 | tf_op jit(solution)/shard_map/ppermute | solution.py:131
  30.4 1.0 %copy-start.4 = (bf16[2,560,512]{2,1,0:T(8,128)(2,1)}, bf16[2,560,512]{2,1,0:T(8,128)(2,1)S(1)}, u32[]{:S(2)}) copy-start(bf16[2,560,512]{2,1,0:T(8,128)(2,1)S(1)} %collective-permute-done.1.near) | copy-start | bytes 3440644
  31.4 10.3 %collective-permute-start.4 = (bf16[560,512]{1,0:T(8,128)(2,1)}, bf16[560,512]{1,0:T(8,128)(2,1)}, u32[]{:S(2)}, u32[]{:S(2)}) collective-permute-start(bf16[560,512]{1,0:T(8,128)(2,1)} %get-tuple-element.23), channel_id=1, source_target_pairs={{0,16},{1,2},{2,1},{3,19},{16,0},{17,18},{18,17},{19,3},{4,20},{5,... | collective-permute-start | bytes 1720328 | tf_op jit(solution)/shard_map/ppermute | solution.py:143
  31.5 1.7 %copy-start.1 = (bf16[2240,560]{0,1:T(8,128)(2,1)S(1)}, bf16[2240,560]{0,1:T(8,128)(2,1)}, u32[]{:S(2)}) copy-start(bf16[2240,560]{0,1:T(8,128)(2,1)} %param.8) | copy-start | bytes 7526404
  33.2 1.7 %copy-start.2 = (bf16[2240,560]{0,1:T(8,128)(2,1)S(1)}, bf16[2240,560]{0,1:T(8,128)(2,1)}, u32[]{:S(2)}) copy-start(bf16[2240,560]{0,1:T(8,128)(2,1)} %param.6) | copy-start | bytes 7526404
  35.0 5.0 %copy-start.6 = (bf16[560,512]{1,0:T(8,128)(2,1)S(1)}, bf16[560,512]{1,0:T(8,128)(2,1)}, u32[]{:S(2)}) copy-start(bf16[560,512]{1,0:T(8,128)(2,1)} %get-tuple-element.24) | copy-start | bytes 1720324
  35.0 14.8 %copy-start.3 = (bf16[2,512,560]{1,2,0:T(8,128)(2,1)S(1)}, bf16[2,512,560]{1,2,0:T(8,128)(2,1)}, u32[]{:S(2)}) copy-start(bf16[2,512,560]{1,2,0:T(8,128)(2,1)} %param.5) | copy-start | bytes 3440644
  35.0 14.8 %copy-start.5 = (bf16[2,560,512]{2,1,0:T(8,128)(2,1)S(1)}, bf16[2,560,512]{2,1,0:T(8,128)(2,1)}, u32[]{:S(2)}) copy-start(bf16[2,560,512]{2,1,0:T(8,128)(2,1)} %copy-done.4) | copy-start | bytes 3440644
  36.3 19.7 %collective-permute-start.3 = (bf16[560,512]{1,0:T(8,128)(2,1)S(1)}, bf16[560,512]{1,0:T(8,128)(2,1)S(1)}, u32[]{:S(2)}, u32[]{:S(2)}) collective-permute-start(bf16[560,512]{1,0:T(8,128)(2,1)S(1)} %collective-permute-done.inner_ref), channel_id=1, source_target_pairs={{0,1},{1,0},{2,3},{3,2},{4,5},{5,4},{6,7},{7,6},{8,9},{9,8},{10,11... | collective-permute-start | bytes 1720328 | tf_op jit(solution)/shard_map/ppermute | solution.py:131
  40.0 16.0 %collective-permute-start.2 = (bf16[560,512]{1,0:T(8,128)(2,1)S(1)}, bf16[560,512]{1,0:T(8,128)(2,1)S(1)}, u32[]{:S(2)}, u32[]{:S(2)}) collective-permute-start(bf16[560,512]{1,0:T(8,128)(2,1)S(1)} %copy-done.6), channel_id=1, source_target_pairs={{0,16},{1,2},{2,1},{3,19},{16,0},{17,18},{18,17},{19,3},{4,20},{5,... | collective-permute-start | bytes 1720328 | tf_op jit(solution)/shard_map/ppermute | solution.py:143
  41.7 24.5 %collective-permute-start.8 = (bf16[560,512]{1,0:T(8,128)(2,1)}, bf16[560,512]{1,0:T(8,128)(2,1)S(1)}, u32[]{:S(2)}, u32[]{:S(2)}) collective-permute-start(bf16[560,512]{1,0:T(8,128)(2,1)} %collective-permute-done.4.b2i), channel_id=1, source_target_pairs={{0,1},{1,0},{2,3},{3,2},{4,5},{5,4},{6,7},{7,6},{8,9},{9,8},{10,11... | collective-permute-start | bytes 1720328 | tf_op jit(solution)/shard_map/ppermute | solution.py:131
  56.0 23.3 %collective-permute-start.7 = (bf16[560,512]{1,0:T(8,128)(2,1)S(1)}, bf16[560,512]{1,0:T(8,128)(2,1)S(1)}, u32[]{:S(2)}, u32[]{:S(2)}) collective-permute-start(bf16[560,512]{1,0:T(8,128)(2,1)S(1)} %collective-permute-done.2.b2i), channel_id=1, source_target_pairs={{0,1},{1,0},{2,3},{3,2},{4,5},{5,4},{6,7},{7,6},{8,9},{9,8},{10,11... | collective-permute-start | bytes 1720328 | tf_op jit(solution)/shard_map/ppermute | solution.py:131
  68.5 6.3 %collective-permute-start.10 = (bf16[560,112]{1,0:T(8,128)(2,1)S(1)}, bf16[560,112]{1,0:T(8,128)(2,1)S(1)}, u32[]{:S(2)}, u32[]{:S(2)}) collective-permute-start(bf16[560,112]{1,0:T(8,128)(2,1)S(1)} %convert_element_type.16), channel_id=1, source_target_pairs={{0,8},{4,12},{8,0},{12,4},{1,9},{5,13},{9,1},{13,5},{2,10},{6,14},... | collective-permute-start | bytes 376328 | tf_op jit(solution)/shard_map/ppermute | solution.py:154
  70.4 5.2 %collective-permute-start.11 = (bf16[560,112]{1,0:T(8,128)(2,1)S(1)}, bf16[560,112]{1,0:T(8,128)(2,1)S(1)}, u32[]{:S(2)}, u32[]{:S(2)}) collective-permute-start(bf16[560,112]{1,0:T(8,128)(2,1)S(1)} %convert_element_type.16), channel_id=1, source_target_pairs={{0,4},{4,0},{8,12},{12,8},{1,5},{5,1},{9,13},{13,9},{2,6},{6,2},{1... | collective-permute-start | bytes 376328 | tf_op jit(solution)/shard_map/ppermute | solution.py:154
  71.9 6.0 %collective-permute-start.9 = (bf16[560,112]{1,0:T(8,128)(2,1)S(1)}, bf16[560,112]{1,0:T(8,128)(2,1)S(1)}, u32[]{:S(2)}, u32[]{:S(2)}) collective-permute-start(bf16[560,112]{1,0:T(8,128)(2,1)S(1)} %convert_element_type.16), channel_id=1, source_target_pairs={{0,12},{4,8},{8,4},{12,0},{1,13},{5,9},{9,5},{13,1},{2,14},{6,10},... | collective-permute-start | bytes 376328 | tf_op jit(solution)/shard_map/ppermute | solution.py:154
  78.0 6.7 %copy-start.7 = (f32[560]{0:T(1024)S(1)}, f32[560]{0:T(1024)}, u32[]{:S(2)}) copy-start(f32[560]{0:T(1024)} %param.9) | copy-start | bytes 6724
  78.0 8.0 %collective-permute-start.12 = (f32[560,112]{1,0:T(8,128)S(1)}, f32[560,112]{1,0:T(8,128)S(1)}, u32[]{:S(2)}, u32[]{:S(2)}) collective-permute-start(f32[560,112]{1,0:T(8,128)S(1)} %convert_add_fusion.rest_0_.rest_1_), channel_id=1, source_target_pairs={{0,16},{1,17},{2,18},{3,19},{4,20},{5,21},{6,22},{7,23},{8,24},{9,... | collective-permute-start | bytes 752648 | tf_op jit(solution)/shard_map/ppermute | solution.py:160
  81.1 6.9 %collective-permute-start.13 = (bf16[560,112]{1,0:T(8,128)(2,1)S(1)}, bf16[560,112]{1,0:T(8,128)(2,1)S(1)}, u32[]{:S(2)}, u32[]{:S(2)}) collective-permute-start(bf16[560,112]{1,0:T(8,128)(2,1)S(1)} %convert_element_type.20), channel_id=1, source_target_pairs={{0,12},{4,8},{8,4},{12,0},{1,13},{5,9},{9,5},{13,1},{2,14},{6,10},... | collective-permute-start | bytes 376328 | tf_op jit(solution)/shard_map/ppermute | solution.py:154
  82.8 6.3 %collective-permute-start.14 = (bf16[560,112]{1,0:T(8,128)(2,1)S(1)}, bf16[560,112]{1,0:T(8,128)(2,1)S(1)}, u32[]{:S(2)}, u32[]{:S(2)}) collective-permute-start(bf16[560,112]{1,0:T(8,128)(2,1)S(1)} %convert_element_type.20), channel_id=1, source_target_pairs={{0,8},{4,12},{8,0},{12,4},{1,9},{5,13},{9,1},{13,5},{2,10},{6,14},... | collective-permute-start | bytes 376328 | tf_op jit(solution)/shard_map/ppermute | solution.py:154
  83.3 5.8 %collective-permute-start.15 = (bf16[560,112]{1,0:T(8,128)(2,1)S(1)}, bf16[560,112]{1,0:T(8,128)(2,1)S(1)}, u32[]{:S(2)}, u32[]{:S(2)}) collective-permute-start(bf16[560,112]{1,0:T(8,128)(2,1)S(1)} %convert_element_type.20), channel_id=1, source_target_pairs={{0,4},{4,0},{8,12},{12,8},{1,5},{5,1},{9,13},{13,9},{2,6},{6,2},{1... | collective-permute-start | bytes 376328 | tf_op jit(solution)/shard_map/ppermute | solution.py:154

commit v10 on v9

--- a/solution.py
+++ b/solution.py
@@ -115,16 +115,18 @@
 
 
 def read_kernel(stream, parts, query, gain, *rest):
-    out, held, sem = rest[-3:]
+    out, held, sems = rest[-3:]
+    copies = []
     for start in range(0, query.shape[0], HEAD_DIM):
         rows = slice(start, start + HEAD_DIM)
         total = sum(part[rows, :].astype(jnp.float32) for part in rest[:parts])
         reading = rounded_dot(total.astype(jnp.bfloat16), query[rows, :])
         scale = lax.rsqrt(jnp.mean(reading * reading, axis=0, keepdims=True) + 1e-06)
         held[rows, :] = (reading * scale * gain[rows, :]).astype(jnp.bfloat16)
-    copy = pltpu.make_async_copy(held, out.at[stream], sem)
-    copy.start()
-    copy.wait()
+        copies.append(pltpu.make_async_copy(held.at[rows, :], out.at[stream, rows, :], sems.at[len(copies)]))
+        copies[-1].start()
+    for copy in copies:
+        copy.wait()
 
 
 def partner_swap(value, axis):
@@ -155,6 +157,22 @@
     return got
 
 
+def pairwise_sum(value, axis, other):
+    count, wide = lax.axis_size(axis), lax.axis_size(other)
+    if count & (count - 1):
+        return [value, *from_others(value, axis)]
+    steps = [1 << b for b in range(count.bit_length() - 1)]
+    terms = [value]
+    for k in range(len(steps)):
+        value = sum(term.astype(jnp.float32) for term in terms)
+        pairs = []
+        for j in range(wide):
+            step = steps[-1 - k] if j % 2 else steps[k]
+            pairs += [(j * count + i, j * count + (i ^ step)) for i in range(count)]
+        terms = [value, lax.ppermute(value.astype(jnp.bfloat16), (other, axis), pairs)]
+    return terms
+
+
 def entering(value, axis):
     count = lax.axis_size(axis)
     total = lax.ppermute(value, axis, [(i, i + 1) for i in range(count - 1)])
@@ -195,7 +213,7 @@
     state_type = jax.ShapeDtypeStruct((width, HEAD_DIM), jnp.float32)
     out_type = jax.ShapeDtypeStruct((2, width, tokens), jnp.bfloat16)
 
-    read_scratch = [pltpu.VMEM((width, tokens), jnp.bfloat16), pltpu.SemaphoreType.DMA(())]
+    read_scratch = [pltpu.VMEM((width, tokens), jnp.bfloat16), pltpu.SemaphoreType.DMA((width // HEAD_DIM,))]
     sums = []
     for stream in range(2):
         ready, *_ = lax.optimization_barrier((far[stream], across_end[stream], *sums))
@@ -204,9 +222,9 @@
             functools.partial(partial_kernel, stream), jax.ShapeDtypeStruct((3, width, tokens), jnp.float32), IN_VMEM,
             [IN_SMEM] + [ANYWHERE] * 4 + [IN_VMEM] * 3 + [ANYWHERE], [whole, sems], 3 * one,
         )(place, columns, near, far[stream], across_end[stream], *matrices, cut))
-    prefix = parts = query = out = None
-    for stream in range(2):
-        ties = (sums[1],) if stream == 0 else (parts[0], query)
+    queries, query, clean = [], None, None
+    for stream in range(2):
+        ties = (sums[1],) if stream == 0 else (clean, query)
         state = call(
             state_kernel, state_type, IN_VMEM,
             [IN_SMEM] + [IN_VMEM] * 4 + [ANYWHERE] * len(ties), [], one // 2,
@@ -214,17 +232,20 @@
         query = call(
             query_kernel, query_type, IN_VMEM, [IN_SMEM] + [IN_VMEM] * 4 + [ANYWHERE], [], one // 4,
         )(place, across[stream], far_end[stream], cut, sums[stream], state)
-        parts = [state, *from_others(state, "tok")]
+        queries.append(query)
         if stream == 0:
-            query, *parts = lax.optimization_barrier((query, *parts))
-            parts = [sum(part.astype(jnp.float32) for part in parts)]
-            prefix = entering(parts[0], "group")
+            query, *got = lax.optimization_barrier((query, *from_others(state, "tok")))
+            clean = state + sum(part.astype(jnp.float32) for part in got)
+    clean, state = lax.optimization_barrier((clean, state))
+    prefix = entering(clean, "group")
+    out = None
+    for stream, parts in enumerate(([clean], pairwise_sum(state, "tok", "group"))):
         kept = [] if out is None else [out]
         out = call(
             functools.partial(read_kernel, stream, len(parts) + 1), out_type, ANYWHERE,
             [IN_VMEM] * (3 + len(parts)) + [ANYWHERE] * len(kept),
             read_scratch, one // 20, {3 + len(parts): 0} if kept else None,
-        )(query, gain_column, prefix, *parts, *kept)
+        )(queries[stream], gain_column, prefix, *parts, *kept)
     return jnp.swapaxes(out, 1, 2)
 
 

time: 90.7 us -> 91.6 us (level)
  waiting for transfers between devices: 19.3 us -> 21.3 us
    ppermute x0 -> x2, waiting for transfers between devices: none -> 3.75 us  [pairwise_sum(): lax.ppermute(value.astype(jnp.bfloat16), (other, axis), pairs)]
    ppermute x6 -> x3, starting transfers between devices: 7.11 us -> 3.55 us  [from_others(): got.append(lax.ppermute(sent, axis, pairs))]
    ppermute x0 -> x2, starting transfers between devices: none -> 2.82 us  [pairwise_sum(): lax.ppermute(value.astype(jnp.bfloat16), (other, axis), pairs)]
    ppermute x6 -> x3, waiting for transfers between devices: 5.93 us -> 4.1 us  [from_others(): got.append(lax.ppermute(sent, axis, pairs))]
  transfers between devices with their start and end apart: 16 -> 15, of which waited for: 9 -> 9; matrix products, arithmetic and copies ran while one was open for 4% -> 4% of each run, Pallas kernels for 23% -> 21%
where the time goes in v10:
time: 91.6 us; the launch traced here: 91.3 us
  starting transfers between devices  39.8 us (43%)
  Pallas kernels  22 us (24%)
  waiting for transfers between devices  21.3 us (23%)
  local copies, waits for them, and re-layouts  7.83 us (9%)
    ppermute x5, starting transfers between devices, partner_swap(): lax.ppermute(value, axis, [(i, i ^ 1) for i in range(lax.axis_size(axis))])  31.6 us
    pallas_call x2, Pallas kernels, local(): call(functools.partial(partial_kernel, stream), jax.ShapeDtypeStruct((3,...  11.5 us
    ppermute x5, waiting for transfers between devices, partner_swap(): lax.ppermute(value, axis, [(i, i ^ 1) for i in range(lax.axis_size(axis))])  11 us
    unnamed x16, local copies, waits for them, and re-layouts  4.48 us
    ppermute x3, waiting for transfers between devices, from_others(): got.append(lax.ppermute(sent, axis, pairs))  4.1 us
    pallas_call x2, Pallas kernels, local(): call(state_kernel, state_type, IN_VMEM, [IN_SMEM] + [IN_VMEM] * 4 + [ANYW...  4.05 us
    ppermute x2, waiting for transfers between devices, pairwise_sum(): lax.ppermute(value.astype(jnp.bfloat16), (other, axis), pairs)  3.75 us
    ppermute x3, starting transfers between devices, from_others(): got.append(lax.ppermute(sent, axis, pairs))  3.55 us
  transfers between devices with their start and end apart: 15, of which 9 were waited for; matrix products, arithmetic and copies ran while one was open for 4% of the time, Pallas kernels for 21%

profile of v10, /device:TPU:0, one launch (start us, length us, event | category | flops | bytes accessed | tf_op | source)
XLA Modules:
  0.0 91.3 jit_solution(8206478222938414351)
XLA Ops:
  0.0 3.0 %collective-permute-start.1 = (bf16[2,560,512]{2,1,0:T(8,128)(2,1)}, bf16[2,560,512]{2,1,0:T(8,128)(2,1)S(1)}, u32[]{:S(2)}, u32[]{:S(2)}) collective-permute-start(bf16[2,560,512]{2,1,0:T(8,128)(2,1)} %bitcast.24), channel_id=1, source_target_pairs={{0,1},{1,0},{2,3},{3,2},{4,5},{5,4},{6,7},{7,6},{8,9},{9,8},{10,11... | collective-permute-start | bytes 3440648 | tf_op jit(solution)/shard_map/ppermute | solution.py:133
  3.0 2.1 %slice_bitcast_fusion = (bf16[560,512]{1,0:T(8,128)(2,1)S(1)}, bf16[560,512]{1,0:T(8,128)(2,1)}) fusion(bf16[2,560,512]{2,1,0:T(8,128)(2,1)} %bitcast.25), kind=kLoop, calls=%fused_computation | loop fusion | bytes 2293760 | tf_op jit(solution)/shard_map/squeeze | solution.py:205
  5.7 2.4 %collective-permute-done.5.inner_ref = bf16[560,512]{1,0:T(8,128)(2,1)} collective-permute-done((bf16[560,512]{1,0:T(8,128)(2,1)S(1)}, bf16[560,512]{1,0:T(8,128)(2,1)}, u32[]{:S(2)}, u32[]{:S(2)}) %collective-permute-start.5) | collective-permute-done | bytes 573472 | tf_op jit(solution)/shard_map/ppermute | solution.py:145
  8.0 14.2 %collective-permute-start.6 = (bf16[560,512]{1,0:T(8,128)(2,1)}, bf16[560,512]{1,0:T(8,128)(2,1)}, u32[]{:S(2)}, u32[]{:S(2)}) collective-permute-start(bf16[560,512]{1,0:T(8,128)(2,1)} %collective-permute-done.5.inner_ref), channel_id=1, source_target_pairs={{0,1},{1,0},{2,3},{3,2},{4,5},{5,4},{6,7},{7,6},{8,9},{9,8},{10,11... | collective-permute-start | bytes 1720328 | tf_op jit(solution)/shard_map/ppermute | solution.py:133
  22.2 7.1 %collective-permute-done.1.near = bf16[2,560,512]{2,1,0:T(8,128)(2,1)S(1)} collective-permute-done((bf16[2,560,512]{2,1,0:T(8,128)(2,1)}, bf16[2,560,512]{2,1,0:T(8,128)(2,1)S(1)}, u32[]{:S(2)}, u32[]{:S(2)}) %collective-permute-start.1) | collective-permute-done | bytes 1146912 | tf_op jit(solution)/shard_map/ppermute | solution.py:133
  29.3 1.1 %slice_bitcast_fusion.1 = (bf16[560,512]{1,0:T(8,128)(2,1)}, bf16[560,512]{1,0:T(8,128)(2,1)}) fusion(bf16[2,560,512]{2,1,0:T(8,128)(2,1)S(1)} %collective-permute-done.1.near), kind=kLoop, calls=%fused_computation.1 | loop fusion | bytes 2293760 | tf_op jit(solution)/shard_map/squeeze | solution.py:207
  30.4 1.0 %copy-done.4 = bf16[2,560,512]{2,1,0:T(8,128)(2,1)} copy-done((bf16[2,560,512]{2,1,0:T(8,128)(2,1)}, bf16[2,560,512]{2,1,0:T(8,128)(2,1)S(1)}, u32[]{:S(2)}) %copy-start.4) | copy-done | bytes 1146904
  31.5 1.7 %copy-done.1 = bf16[2240,560]{0,1:T(8,128)(2,1)S(1)} copy-done((bf16[2240,560]{0,1:T(8,128)(2,1)S(1)}, bf16[2240,560]{0,1:T(8,128)(2,1)}, u32[]{:S(2)}) %copy-start.1) | copy-done | bytes 2508824
  33.2 1.7 %copy-done.2 = bf16[2240,560]{0,1:T(8,128)(2,1)S(1)} copy-done((bf16[2240,560]{0,1:T(8,128)(2,1)S(1)}, bf16[2240,560]{0,1:T(8,128)(2,1)}, u32[]{:S(2)}) %copy-start.2) | copy-done | bytes 2508824
  35.0 1.3 %shard_map.55.tie.cut = bf16[3,560,560]{2,1,0:T(8,128)(2,1)S(1)} custom-call(s32[2]{0:T(128)S(1)} %pad_add_fusion.place, bf16[560,2240]{1,0:T(8,128)(2,1)S(1)} %bitcast.15, bf16[560,2240]{1,0:T(8,128)(2,1)S(1)} %bitcast.18, bf16[560,2240]{1,0:T(8,128)(2,1)S(1)} %bitcast.21), custom_call_target="tpu_custom_call" | custom-call | flops 5017600 | bytes 1024 | tf_op jit(solution)/shard_map/pallas_call | solution.py:198
  36.3 3.7 %collective-permute-start.3 = (bf16[560,512]{1,0:T(8,128)(2,1)S(1)}, bf16[560,512]{1,0:T(8,128)(2,1)S(1)}, u32[]{:S(2)}, u32[]{:S(2)}) collective-permute-start(bf16[560,512]{1,0:T(8,128)(2,1)S(1)} %collective-permute-done.inner_ref), channel_id=1, source_target_pairs={{0,1},{1,0},{2,3},{3,2},{4,5},{5,4},{6,7},{7,6},{8,9},{9,8},{10,11... | collective-permute-start | bytes 1720328 | tf_op jit(solution)/shard_map/ppermute | solution.py:133
  40.0 1.7 %collective-permute-done.6.b2o = bf16[560,512]{1,0:T(8,128)(2,1)} collective-permute-done((bf16[560,512]{1,0:T(8,128)(2,1)}, bf16[560,512]{1,0:T(8,128)(2,1)}, u32[]{:S(2)}, u32[]{:S(2)}) %collective-permute-start.6) | collective-permute-done | bytes 573472 | tf_op jit(solution)/shard_map/ppermute | solution.py:133
  41.7 8.0 %collective-permute-start.8 = (bf16[560,512]{1,0:T(8,128)(2,1)}, bf16[560,512]{1,0:T(8,128)(2,1)S(1)}, u32[]{:S(2)}, u32[]{:S(2)}) collective-permute-start(bf16[560,512]{1,0:T(8,128)(2,1)} %collective-permute-done.4.b2i), channel_id=1, source_target_pairs={{0,1},{1,0},{2,3},{3,2},{4,5},{5,4},{6,7},{7,6},{8,9},{9,8},{10,11... | collective-permute-start | bytes 1720328 | tf_op jit(solution)/shard_map/ppermute | solution.py:133
  49.7 6.2 %shard_map.56.sums = f32[3,560,512]{2,1,0:T(8,128)S(1)} custom-call(s32[2]{0:T(128)S(1)} %pad_add_fusion.place, bf16[2,560,512]{2,1,0:T(8,128)(2,1)S(1)} %bitcast.26, bf16[2,560,512]{2,1,0:T(8,128)(2,1)S(1)} %copy-done.5, bf16[560,512]{1,0:T(8,128)(2,1)} %collective-permute-done.4.b2i, bf16[560,512]{1,0:T(8,128)(2,1)} %collective-permute-done.6.b2o, ...), custom_call_target="tpu_custom_call" | custom-call | flops 60211200 | bytes 1024 | tf_op jit(solution)/shard_map/pallas_call | solution.py:221
  56.0 2.7 %collective-permute-start.7 = (bf16[560,512]{1,0:T(8,128)(2,1)S(1)}, bf16[560,512]{1,0:T(8,128)(2,1)S(1)}, u32[]{:S(2)}, u32[]{:S(2)}) collective-permute-start(bf16[560,512]{1,0:T(8,128)(2,1)S(1)} %collective-permute-done.2.b2i), channel_id=1, source_target_pairs={{0,1},{1,0},{2,3},{3,2},{4,5},{5,4},{6,7},{7,6},{8,9},{9,8},{10,11... | collective-permute-start | bytes 1720328 | tf_op jit(solution)/shard_map/ppermute | solution.py:133
  58.7 5.3 %shard_map.57.rest_0_.sums = f32[3,560,512]{2,1,0:T(8,128)S(1)} custom-call(s32[2]{0:T(128)S(1)} %pad_add_fusion.place, bf16[2,560,512]{2,1,0:T(8,128)(2,1)S(1)} %bitcast.27, bf16[2,560,512]{2,1,0:T(8,128)(2,1)S(1)} %copy-done.5, bf16[560,512]{1,0:T(8,128)(2,1)S(1)} %collective-permute-done.2.b2i, bf16[560,512]{1,0:T(8,128)(2,1)S(1)} %collective-permute-done.3.b2o, ...), custom_call_target="tpu_custom_call" | custom-call | flops 60211200 | bytes 1024 | tf_op jit(solution)/shard_map/pallas_call | solution.py:221
  64.0 2.2 %collective-permute-done.8.end_ref = bf16[560,512]{1,0:T(8,128)(2,1)S(1)} collective-permute-done((bf16[560,512]{1,0:T(8,128)(2,1)}, bf16[560,512]{1,0:T(8,128)(2,1)S(1)}, u32[]{:S(2)}, u32[]{:S(2)}) %collective-permute-start.8) | collective-permute-done | bytes 573472 | tf_op jit(solution)/shard_map/ppermute | solution.py:133
  66.2 2.3 %shard_map.58.tie = f32[560,112]{1,0:T(8,128)S(1)} custom-call(s32[2]{0:T(128)S(1)} %pad_add_fusion.place, bf16[560,512]{1,0:T(8,128)(2,1)} %collective-permute-done.5.inner_ref, bf16[560,512]{1,0:T(8,128)(2,1)S(1)} %collective-permute-done.8.end_ref, bf16[3,560,560]{2,1,0:T(8,128)(2,1)S(1)} %shard_map.55.tie.cut, f32[3,560,512]{2,1,0:T(8,128)S(1)} %shard_map.56.sums, ...), custom_call_target="tpu_custom_call" | custom-call | flops 10035200 | bytes 1024 | tf_op jit(solution)/shard_map/pallas_call | solution.py:228
  68.5 1.9 %collective-permute-start.10 = (bf16[560,112]{1,0:T(8,128)(2,1)S(1)}, bf16[560,112]{1,0:T(8,128)(2,1)S(1)}, u32[]{:S(2)}, u32[]{:S(2)}) collective-permute-start(bf16[560,112]{1,0:T(8,128)(2,1)S(1)} %convert_element_type.22), channel_id=1, source_target_pairs={{0,8},{4,12},{8,0},{12,4},{1,9},{5,13},{9,1},{13,5},{2,10},{6,14},... | collective-permute-start | bytes 376328 | tf_op jit(solution)/shard_map/ppermute | solution.py:156
  70.4 1.5 %collective-permute-start.11 = (bf16[560,112]{1,0:T(8,128)(2,1)S(1)}, bf16[560,112]{1,0:T(8,128)(2,1)S(1)}, u32[]{:S(2)}, u32[]{:S(2)}) collective-permute-start(bf16[560,112]{1,0:T(8,128)(2,1)S(1)} %convert_element_type.22), channel_id=1, source_target_pairs={{0,4},{4,0},{8,12},{12,8},{1,5},{5,1},{9,13},{13,9},{2,6},{6,2},{1... | collective-permute-start | bytes 376328 | tf_op jit(solution)/shard_map/ppermute | solution.py:156
  72.1 1.7 %shard_map.59.rest_1_.query = bf16[560,512]{1,0:T(8,128)(2,1)S(1)} custom-call(s32[2]{0:T(128)S(1)} %pad_add_fusion.place, bf16[560,512]{1,0:T(8,128)(2,1)} %collective-permute-done.5.inner_ref, bf16[560,512]{1,0:T(8,128)(2,1)S(1)} %collective-permute-done.8.end_ref, bf16[3,560,560]{2,1,0:T(8,128)(2,1)S(1)} %shard_map.55.tie.cut, ...), custom_call_target="tpu_custom_call" | custom-call | flops 5017600 | bytes 1024 | tf_op jit(solution)/shard_map/pallas_call | solution.py:232
  73.8 1.1 %collective-permute-done.10 = bf16[560,112]{1,0:T(8,128)(2,1)S(1)} collective-permute-done((bf16[560,112]{1,0:T(8,128)(2,1)S(1)}, bf16[560,112]{1,0:T(8,128)(2,1)S(1)}, u32[]{:S(2)}, u32[]{:S(2)}) %collective-permute-start.10) | collective-permute-done | bytes 125472 | tf_op jit(solution)/shard_map/ppermute | solution.py:156
  75.6 2.3 %collective-permute-done.9 = bf16[560,112]{1,0:T(8,128)(2,1)S(1)} collective-permute-done((bf16[560,112]{1,0:T(8,128)(2,1)S(1)}, bf16[560,112]{1,0:T(8,128)(2,1)S(1)}, u32[]{:S(2)}, u32[]{:S(2)}) %collective-permute-start.9) | collective-permute-done | bytes 125472 | tf_op jit(solution)/shard_map/ppermute | solution.py:156
  78.0 1.7 %shard_map.60.tie = f32[560,112]{1,0:T(8,128)S(1)} custom-call(s32[2]{0:T(128)S(1)} %pad_add_fusion.place, bf16[560,512]{1,0:T(8,128)(2,1)S(1)} %collective-permute-done.inner_ref, bf16[560,512]{1,0:T(8,128)(2,1)S(1)} %collective-permute-done.7.end_ref, bf16[3,560,560]{2,1,0:T(8,128)(2,1)S(1)} %shard_map.55.tie.cut, ...), custom_call_target="tpu_custom_call" | custom-call | flops 10035200 | bytes 1024 | tf_op jit(solution)/shard_map/pallas_call | solution.py:228
  79.8 1.4 %collective-permute-start.13 = (bf16[560,112]{1,0:T(8,128)(2,1)S(1)}, bf16[560,112]{1,0:T(8,128)(2,1)S(1)}, u32[]{:S(2)}, u32[]{:S(2)}) collective-permute-start(bf16[560,112]{1,0:T(8,128)(2,1)S(1)} %convert_element_type.26), channel_id=1, source_target_pairs={{0,4},{4,0},{8,12},{12,8},{16,24},{20,28},{24,16},{28,20},{1,5},{5... | collective-permute-start | bytes 376328 | tf_op jit(solution)/shard_map/ppermute | solution.py:172
  81.2 1.3 %collective-permute-start.12 = (f32[560,112]{1,0:T(8,128)S(1)}, f32[560,112]{1,0:T(8,128)S(1)}, u32[]{:S(2)}, u32[]{:S(2)}) collective-permute-start(f32[560,112]{1,0:T(8,128)S(1)} %add_add_fusion.rest_0_.rest_1_), channel_id=1, source_target_pairs={{0,16},{1,17},{2,18},{3,19},{4,20},{5,21},{6,22},{7,23},{8,24},{9,... | collective-permute-start | bytes 752648 | tf_op jit(solution)/shard_map/ppermute | solution.py:178
  82.5 2.5 %collective-permute-done.13 = bf16[560,112]{1,0:T(8,128)(2,1)S(1)} collective-permute-done((bf16[560,112]{1,0:T(8,128)(2,1)S(1)}, bf16[560,112]{1,0:T(8,128)(2,1)S(1)}, u32[]{:S(2)}, u32[]{:S(2)}) %collective-permute-start.13) | collective-permute-done | bytes 125472 | tf_op jit(solution)/shard_map/ppermute | solution.py:172
  85.0 1.4 %collective-permute-start.14 = (bf16[560,112]{1,0:T(8,128)(2,1)S(1)}, bf16[560,112]{1,0:T(8,128)(2,1)S(1)}, u32[]{:S(2)}, u32[]{:S(2)}) collective-permute-start(bf16[560,112]{1,0:T(8,128)(2,1)S(1)} %get-tuple-element.23), channel_id=1, source_target_pairs={{0,8},{4,12},{8,0},{12,4},{16,20},{20,16},{24,28},{28,24},{1,9},{5... | collective-permute-start | bytes 376328 | tf_op jit(solution)/shard_map/ppermute | solution.py:172
  86.5 1.2 %shard_map.61.query = bf16[560,512]{1,0:T(8,128)(2,1)S(1)} custom-call(s32[2]{0:T(128)S(1)} %pad_add_fusion.place, bf16[560,512]{1,0:T(8,128)(2,1)S(1)} %collective-permute-done.inner_ref, bf16[560,512]{1,0:T(8,128)(2,1)S(1)} %collective-permute-done.7.end_ref, bf16[3,560,560]{2,1,0:T(8,128)(2,1)S(1)} %shard_map.55.tie.cut, ...), custom_call_target="tpu_custom_call" | custom-call | flops 5017600 | bytes 1024 | tf_op jit(solution)/shard_map/pallas_call | solution.py:232
  87.7 1.1 %shard_map.62.rest_3_ = bf16[2,560,512]{2,1,0:T(8,128)(2,1)} custom-call(bf16[560,512]{1,0:T(8,128)(2,1)S(1)} %shard_map.59.rest_1_.query, f32[560,1]{1,0:T(8,128)S(1)} %reshape.5.gain, f32[560,112]{1,0:T(8,128)S(1)} %collective-permute-done.12.rest_0_, f32[560,112]{1,0:T(8,128)S(1)} %add_add_fusion.rest_0_.rest_1_), custom_call_target="tpu_custom_call" | custom-call | flops 1003520 | bytes 1024 | tf_op jit(solution)/shard_map/pallas_call | solution.py:244
  88.8 1.3 %collective-permute-done.14.rest_2_ = bf16[560,112]{1,0:T(8,128)(2,1)S(1)} collective-permute-done((bf16[560,112]{1,0:T(8,128)(2,1)S(1)}, bf16[560,112]{1,0:T(8,128)(2,1)S(1)}, u32[]{:S(2)}, u32[]{:S(2)}) %collective-permute-start.14) | collective-permute-done | bytes 125472 | tf_op jit(solution)/shard_map/ppermute | solution.py:172
  90.1 1.1 %shard_map.63 = bf16[2,560,512]{2,1,0:T(8,128)(2,1)} custom-call(bf16[560,512]{1,0:T(8,128)(2,1)S(1)} %shard_map.61.query, f32[560,1]{1,0:T(8,128)S(1)} %reshape.5.gain, f32[560,112]{1,0:T(8,128)S(1)} %collective-permute-done.12.rest_0_, f32[560,112]{1,0:T(8,128)S(1)} %get-tuple-element.24.rest_1_, ...), custom_call_target="tpu_custom_call", output_to_operand_aliasing={{}: (5, {})} | custom-call | flops 1003520 | bytes 1024 | tf_op jit(solution)/shard_map/pallas_call | solution.py:244
  (31 shorter events, 1.8 us)
Async XLA Ops:
  0.0 31.5 %copy-start = (bf16[2240,560]{0,1:T(8,128)(2,1)S(1)}, bf16[2240,560]{0,1:T(8,128)(2,1)}, u32[]{:S(2)}) copy-start(bf16[2240,560]{0,1:T(8,128)(2,1)} %param.7) | copy-start | bytes 7526404
  0.0 29.3 %collective-permute-start.1 = (bf16[2,560,512]{2,1,0:T(8,128)(2,1)}, bf16[2,560,512]{2,1,0:T(8,128)(2,1)S(1)}, u32[]{:S(2)}, u32[]{:S(2)}) collective-permute-start(bf16[2,560,512]{2,1,0:T(8,128)(2,1)} %bitcast.24), channel_id=1, source_target_pairs={{0,1},{1,0},{2,3},{3,2},{4,5},{5,4},{6,7},{7,6},{8,9},{9,8},{10,11... | collective-permute-start | bytes 3440648 | tf_op jit(solution)/shard_map/ppermute | solution.py:133
  5.1 2.9 %collective-permute-start.5 = (bf16[560,512]{1,0:T(8,128)(2,1)S(1)}, bf16[560,512]{1,0:T(8,128)(2,1)}, u32[]{:S(2)}, u32[]{:S(2)}) collective-permute-start(bf16[560,512]{1,0:T(8,128)(2,1)S(1)} %get-tuple-element.25), channel_id=1, source_target_pairs={{0,16},{1,2},{2,1},{3,19},{16,0},{17,18},{18,17},{19,3},{4,20},{5,... | collective-permute-start | bytes 1720328 | tf_op jit(solution)/shard_map/ppermute | solution.py:145
  5.1 31.1 %collective-permute-start = (bf16[560,512]{1,0:T(8,128)(2,1)}, bf16[560,512]{1,0:T(8,128)(2,1)S(1)}, u32[]{:S(2)}, u32[]{:S(2)}) collective-permute-start(bf16[560,512]{1,0:T(8,128)(2,1)} %get-tuple-element.26), channel_id=1, source_target_pairs={{0,16},{1,2},{2,1},{3,19},{16,0},{17,18},{18,17},{19,3},{4,20},{5,... | collective-permute-start | bytes 1720328 | tf_op jit(solution)/shard_map/ppermute | solution.py:145
  8.0 33.7 %collective-permute-start.6 = (bf16[560,512]{1,0:T(8,128)(2,1)}, bf16[560,512]{1,0:T(8,128)(2,1)}, u32[]{:S(2)}, u32[]{:S(2)}) collective-permute-start(bf16[560,512]{1,0:T(8,128)(2,1)} %collective-permute-done.5.inner_ref), channel_id=1, source_target_pairs={{0,1},{1,0},{2,3},{3,2},{4,5},{5,4},{6,7},{7,6},{8,9},{9,8},{10,11... | collective-permute-start | bytes 1720328 | tf_op jit(solution)/shard_map/ppermute | solution.py:133
  30.4 1.0 %copy-start.4 = (bf16[2,560,512]{2,1,0:T(8,128)(2,1)}, bf16[2,560,512]{2,1,0:T(8,128)(2,1)S(1)}, u32[]{:S(2)}) copy-start(bf16[2,560,512]{2,1,0:T(8,128)(2,1)S(1)} %collective-permute-done.1.near) | copy-start | bytes 3440644
  31.4 10.3 %collective-permute-start.4 = (bf16[560,512]{1,0:T(8,128)(2,1)}, bf16[560,512]{1,0:T(8,128)(2,1)}, u32[]{:S(2)}, u32[]{:S(2)}) collective-permute-start(bf16[560,512]{1,0:T(8,128)(2,1)} %get-tuple-element.27), channel_id=1, source_target_pairs={{0,16},{1,2},{2,1},{3,19},{16,0},{17,18},{18,17},{19,3},{4,20},{5,... | collective-permute-start | bytes 1720328 | tf_op jit(solution)/shard_map/ppermute | solution.py:145
  31.5 1.7 %copy-start.1 = (bf16[2240,560]{0,1:T(8,128)(2,1)S(1)}, bf16[2240,560]{0,1:T(8,128)(2,1)}, u32[]{:S(2)}) copy-start(bf16[2240,560]{0,1:T(8,128)(2,1)} %param.8) | copy-start | bytes 7526404
  33.2 1.7 %copy-start.2 = (bf16[2240,560]{0,1:T(8,128)(2,1)S(1)}, bf16[2240,560]{0,1:T(8,128)(2,1)}, u32[]{:S(2)}) copy-start(bf16[2240,560]{0,1:T(8,128)(2,1)} %param.6) | copy-start | bytes 7526404
  35.0 5.0 %copy-start.6 = (bf16[560,512]{1,0:T(8,128)(2,1)S(1)}, bf16[560,512]{1,0:T(8,128)(2,1)}, u32[]{:S(2)}) copy-start(bf16[560,512]{1,0:T(8,128)(2,1)} %get-tuple-element.28) | copy-start | bytes 1720324
  35.0 14.8 %copy-start.3 = (bf16[2,512,560]{1,2,0:T(8,128)(2,1)S(1)}, bf16[2,512,560]{1,2,0:T(8,128)(2,1)}, u32[]{:S(2)}) copy-start(bf16[2,512,560]{1,2,0:T(8,128)(2,1)} %param.5) | copy-start | bytes 3440644
  35.0 14.8 %copy-start.5 = (bf16[2,560,512]{2,1,0:T(8,128)(2,1)S(1)}, bf16[2,560,512]{2,1,0:T(8,128)(2,1)}, u32[]{:S(2)}) copy-start(bf16[2,560,512]{2,1,0:T(8,128)(2,1)} %copy-done.4) | copy-start | bytes 3440644
  36.3 19.7 %collective-permute-start.3 = (bf16[560,512]{1,0:T(8,128)(2,1)S(1)}, bf16[560,512]{1,0:T(8,128)(2,1)S(1)}, u32[]{:S(2)}, u32[]{:S(2)}) collective-permute-start(bf16[560,512]{1,0:T(8,128)(2,1)S(1)} %collective-permute-done.inner_ref), channel_id=1, source_target_pairs={{0,1},{1,0},{2,3},{3,2},{4,5},{5,4},{6,7},{7,6},{8,9},{9,8},{10,11... | collective-permute-start | bytes 1720328 | tf_op jit(solution)/shard_map/ppermute | solution.py:133
  40.0 16.0 %collective-permute-start.2 = (bf16[560,512]{1,0:T(8,128)(2,1)S(1)}, bf16[560,512]{1,0:T(8,128)(2,1)S(1)}, u32[]{:S(2)}, u32[]{:S(2)}) collective-permute-start(bf16[560,512]{1,0:T(8,128)(2,1)S(1)} %copy-done.6), channel_id=1, source_target_pairs={{0,16},{1,2},{2,1},{3,19},{16,0},{17,18},{18,17},{19,3},{4,20},{5,... | collective-permute-start | bytes 1720328 | tf_op jit(solution)/shard_map/ppermute | solution.py:145
  41.7 24.5 %collective-permute-start.8 = (bf16[560,512]{1,0:T(8,128)(2,1)}, bf16[560,512]{1,0:T(8,128)(2,1)S(1)}, u32[]{:S(2)}, u32[]{:S(2)}) collective-permute-start(bf16[560,512]{1,0:T(8,128)(2,1)} %collective-permute-done.4.b2i), channel_id=1, source_target_pairs={{0,1},{1,0},{2,3},{3,2},{4,5},{5,4},{6,7},{7,6},{8,9},{9,8},{10,11... | collective-permute-start | bytes 1720328 | tf_op jit(solution)/shard_map/ppermute | solution.py:133
  56.0 22.0 %collective-permute-start.7 = (bf16[560,512]{1,0:T(8,128)(2,1)S(1)}, bf16[560,512]{1,0:T(8,128)(2,1)S(1)}, u32[]{:S(2)}, u32[]{:S(2)}) collective-permute-start(bf16[560,512]{1,0:T(8,128)(2,1)S(1)} %collective-permute-done.2.b2i), channel_id=1, source_target_pairs={{0,1},{1,0},{2,3},{3,2},{4,5},{5,4},{6,7},{7,6},{8,9},{9,8},{10,11... | collective-permute-start | bytes 1720328 | tf_op jit(solution)/shard_map/ppermute | solution.py:133
  68.5 6.3 %collective-permute-start.10 = (bf16[560,112]{1,0:T(8,128)(2,1)S(1)}, bf16[560,112]{1,0:T(8,128)(2,1)S(1)}, u32[]{:S(2)}, u32[]{:S(2)}) collective-permute-start(bf16[560,112]{1,0:T(8,128)(2,1)S(1)} %convert_element_type.22), channel_id=1, source_target_pairs={{0,8},{4,12},{8,0},{12,4},{1,9},{5,13},{9,1},{13,5},{2,10},{6,14},... | collective-permute-start | bytes 376328 | tf_op jit(solution)/shard_map/ppermute | solution.py:156
  70.4 5.2 %collective-permute-start.11 = (bf16[560,112]{1,0:T(8,128)(2,1)S(1)}, bf16[560,112]{1,0:T(8,128)(2,1)S(1)}, u32[]{:S(2)}, u32[]{:S(2)}) collective-permute-start(bf16[560,112]{1,0:T(8,128)(2,1)S(1)} %convert_element_type.22), channel_id=1, source_target_pairs={{0,4},{4,0},{8,12},{12,8},{1,5},{5,1},{9,13},{13,9},{2,6},{6,2},{1... | collective-permute-start | bytes 376328 | tf_op jit(solution)/shard_map/ppermute | solution.py:156
  71.9 6.0 %collective-permute-start.9 = (bf16[560,112]{1,0:T(8,128)(2,1)S(1)}, bf16[560,112]{1,0:T(8,128)(2,1)S(1)}, u32[]{:S(2)}, u32[]{:S(2)}) collective-permute-start(bf16[560,112]{1,0:T(8,128)(2,1)S(1)} %convert_element_type.22), channel_id=1, source_target_pairs={{0,12},{4,8},{8,4},{12,0},{1,13},{5,9},{9,5},{13,1},{2,14},{6,10},... | collective-permute-start | bytes 376328 | tf_op jit(solution)/shard_map/ppermute | solution.py:156
  78.0 8.4 %copy-start.7 = (f32[560]{0:T(1024)S(1)}, f32[560]{0:T(1024)}, u32[]{:S(2)}) copy-start(f32[560]{0:T(1024)} %param.9) | copy-start | bytes 6724
  79.8 5.2 %collective-permute-start.13 = (bf16[560,112]{1,0:T(8,128)(2,1)S(1)}, bf16[560,112]{1,0:T(8,128)(2,1)S(1)}, u32[]{:S(2)}, u32[]{:S(2)}) collective-permute-start(bf16[560,112]{1,0:T(8,128)(2,1)S(1)} %convert_element_type.26), channel_id=1, source_target_pairs={{0,4},{4,0},{8,12},{12,8},{16,24},{20,28},{24,16},{28,20},{1,5},{5... | collective-permute-start | bytes 376328 | tf_op jit(solution)/shard_map/ppermute | solution.py:172
  81.2 6.5 %collective-permute-start.12 = (f32[560,112]{1,0:T(8,128)S(1)}, f32[560,112]{1,0:T(8,128)S(1)}, u32[]{:S(2)}, u32[]{:S(2)}) collective-permute-start(f32[560,112]{1,0:T(8,128)S(1)} %add_add_fusion.rest_0_.rest_1_), channel_id=1, source_target_pairs={{0,16},{1,17},{2,18},{3,19},{4,20},{5,21},{6,22},{7,23},{8,24},{9,... | collective-permute-start | bytes 752648 | tf_op jit(solution)/shard_map/ppermute | solution.py:178
  85.0 5.2 %collective-permute-start.14 = (bf16[560,112]{1,0:T(8,128)(2,1)S(1)}, bf16[560,112]{1,0:T(8,128)(2,1)S(1)}, u32[]{:S(2)}, u32[]{:S(2)}) collective-permute-start(bf16[560,112]{1,0:T(8,128)(2,1)S(1)} %get-tuple-element.23), channel_id=1, source_target_pairs={{0,8},{4,12},{8,0},{12,4},{16,20},{20,16},{24,28},{28,24},{1,9},{5... | collective-permute-start | bytes 376328 | tf_op jit(solution)/shard_map/ppermute | solution.py:172

commit v11 on v10

--- a/solution.py
+++ b/solution.py
@@ -157,29 +157,16 @@
     return got
 
 
-def pairwise_sum(value, axis, other):
-    count, wide = lax.axis_size(axis), lax.axis_size(other)
-    if count & (count - 1):
-        return [value, *from_others(value, axis)]
-    steps = [1 << b for b in range(count.bit_length() - 1)]
-    terms = [value]
-    for k in range(len(steps)):
-        value = sum(term.astype(jnp.float32) for term in terms)
-        pairs = []
-        for j in range(wide):
-            step = steps[-1 - k] if j % 2 else steps[k]
-            pairs += [(j * count + i, j * count + (i ^ step)) for i in range(count)]
-        terms = [value, lax.ppermute(value.astype(jnp.bfloat16), (other, axis), pairs)]
-    return terms
-
-
 def entering(value, axis):
-    count = lax.axis_size(axis)
-    total = lax.ppermute(value, axis, [(i, i + 1) for i in range(count - 1)])
-    reach = 1
+    count, mine = lax.axis_size(axis), lax.axis_index(axis)
+
+    def earlier(value, reach):
+        sent = lax.ppermute(value.astype(jnp.bfloat16), axis, [(i, (i + reach) % count) for i in range(count)])
+        return jnp.where(mine >= reach, sent.astype(jnp.float32), 0.0)
+
+    total, reach = earlier(value, 1), 1
     while reach < count - 1:
-        total = total + lax.ppermute(total, axis, [(i, i + reach) for i in range(count - reach)])
-        reach *= 2
+        total, reach = total + earlier(total, reach), 2 * reach
     return total
 
 
@@ -236,10 +223,9 @@
         if stream == 0:
             query, *got = lax.optimization_barrier((query, *from_others(state, "tok")))
             clean = state + sum(part.astype(jnp.float32) for part in got)
-    clean, state = lax.optimization_barrier((clean, state))
-    prefix = entering(clean, "group")
+            prefix = entering(clean, "group")
     out = None
-    for stream, parts in enumerate(([clean], pairwise_sum(state, "tok", "group"))):
+    for stream, parts in enumerate(([clean], [state, *from_others(state, "tok")])):
         kept = [] if out is None else [out]
         out = call(
             functools.partial(read_kernel, stream, len(parts) + 1), out_type, ANYWHERE,

time: 91.6 us -> 95.1 us (1.038)
  local copies, waits for them, and re-layouts: 7.83 us -> 10.5 us
  Pallas kernels: 22 us -> 23.4 us
  starting transfers between devices: 39.8 us -> 38.8 us
    ppermute x3 -> x1, starting transfers between devices: 4.12 us -> 0.07 us  [earlier(): lax.ppermute(value.astype(jnp.bfloat16), axis, [(i, (i + reach) % count)...]
    ppermute x3 -> x1, waiting for transfers between devices: 3.76 us -> 0.01 us  [earlier(): lax.ppermute(value.astype(jnp.bfloat16), axis, [(i, (i + reach) % count)...]
    ppermute x3 -> x6, starting transfers between devices: 3.55 us -> 7.11 us  [from_others(): got.append(lax.ppermute(sent, axis, pairs))]
    ppermute x3 -> x6, waiting for transfers between devices: 4.1 us -> 7.41 us  [from_others(): got.append(lax.ppermute(sent, axis, pairs))]
    unnamed x16, local copies, waits for them, and re-layouts: 4.48 us -> 7.17 us
  transfers between devices with their start and end apart: 15 -> 16, of which waited for: 9 -> 10; matrix products, arithmetic and copies ran while one was open for 4% -> 4% of each run, Pallas kernels for 21% -> 24%
where the time goes in v11:
time: 95.1 us; the launch traced here: 94.6 us
  starting transfers between devices  38.8 us (41%)
  Pallas kernels  23.4 us (25%)
  waiting for transfers between devices  21.6 us (23%)
  local copies, waits for them, and re-layouts  10.5 us (11%)
    ppermute x5, starting transfers between devices, partner_swap(): lax.ppermute(value, axis, [(i, i ^ 1) for i in range(lax.axis_size(axis))])  31.1 us
    ppermute x5, waiting for transfers between devices, partner_swap(): lax.ppermute(value, axis, [(i, i ^ 1) for i in range(lax.axis_size(axis))])  11.8 us
    pallas_call x2, Pallas kernels, local(): call(functools.partial(partial_kernel, stream), jax.ShapeDtypeStruct((3,...  11.5 us
    ppermute x6, waiting for transfers between devices, from_others(): got.append(lax.ppermute(sent, axis, pairs))  7.41 us
    unnamed x16, local copies, waits for them, and re-layouts  7.17 us
    ppermute x6, starting transfers between devices, from_others(): got.append(lax.ppermute(sent, axis, pairs))  7.11 us
    pallas_call x2, Pallas kernels, local(): call(state_kernel, state_type, IN_VMEM, [IN_SMEM] + [IN_VMEM] * 4 + [ANYW...  4.75 us
    pallas_call x2, Pallas kernels, local(): call(query_kernel, query_type, IN_VMEM, [IN_SMEM] + [IN_VMEM] * 4 + [ANYW...  3.55 us
  transfers between devices with their start and end apart: 16, of which 10 were waited for; matrix products, arithmetic and copies ran while one was open for 4% of the time, Pallas kernels for 24%

profile of v11, /device:TPU:0, one launch (start us, length us, event | category | flops | bytes accessed | tf_op | source)
XLA Modules:
  0.0 94.6 jit_solution(16414025969012456133)
XLA Ops:
  0.0 3.0 %collective-permute-start.1 = (bf16[2,560,512]{2,1,0:T(8,128)(2,1)}, bf16[2,560,512]{2,1,0:T(8,128)(2,1)S(1)}, u32[]{:S(2)}, u32[]{:S(2)}) collective-permute-start(bf16[2,560,512]{2,1,0:T(8,128)(2,1)} %bitcast.24), channel_id=1, source_target_pairs={{0,1},{1,0},{2,3},{3,2},{4,5},{5,4},{6,7},{7,6},{8,9},{9,8},{10,11... | collective-permute-start | bytes 3440648 | tf_op jit(solution)/shard_map/ppermute | solution.py:133
  3.0 2.1 %slice_bitcast_fusion = (bf16[560,512]{1,0:T(8,128)(2,1)S(1)}, bf16[560,512]{1,0:T(8,128)(2,1)}) fusion(bf16[2,560,512]{2,1,0:T(8,128)(2,1)} %bitcast.25), kind=kLoop, calls=%fused_computation | loop fusion | bytes 2293760 | tf_op jit(solution)/shard_map/squeeze | solution.py:192
  5.7 2.4 %collective-permute-done.5.inner_ref = bf16[560,512]{1,0:T(8,128)(2,1)} collective-permute-done((bf16[560,512]{1,0:T(8,128)(2,1)S(1)}, bf16[560,512]{1,0:T(8,128)(2,1)}, u32[]{:S(2)}, u32[]{:S(2)}) %collective-permute-start.5) | collective-permute-done | bytes 573472 | tf_op jit(solution)/shard_map/ppermute | solution.py:145
  8.0 14.2 %collective-permute-start.6 = (bf16[560,512]{1,0:T(8,128)(2,1)}, bf16[560,512]{1,0:T(8,128)(2,1)}, u32[]{:S(2)}, u32[]{:S(2)}) collective-permute-start(bf16[560,512]{1,0:T(8,128)(2,1)} %collective-permute-done.5.inner_ref), channel_id=1, source_target_pairs={{0,1},{1,0},{2,3},{3,2},{4,5},{5,4},{6,7},{7,6},{8,9},{9,8},{10,11... | collective-permute-start | bytes 1720328 | tf_op jit(solution)/shard_map/ppermute | solution.py:133
  22.2 7.1 %collective-permute-done.1.near = bf16[2,560,512]{2,1,0:T(8,128)(2,1)S(1)} collective-permute-done((bf16[2,560,512]{2,1,0:T(8,128)(2,1)}, bf16[2,560,512]{2,1,0:T(8,128)(2,1)S(1)}, u32[]{:S(2)}, u32[]{:S(2)}) %collective-permute-start.1) | collective-permute-done | bytes 1146912 | tf_op jit(solution)/shard_map/ppermute | solution.py:133
  29.3 1.1 %slice_bitcast_fusion.1 = (bf16[560,512]{1,0:T(8,128)(2,1)}, bf16[560,512]{1,0:T(8,128)(2,1)}) fusion(bf16[2,560,512]{2,1,0:T(8,128)(2,1)S(1)} %collective-permute-done.1.near), kind=kLoop, calls=%fused_computation.1 | loop fusion | bytes 2293760 | tf_op jit(solution)/shard_map/squeeze | solution.py:194
  30.5 1.7 %copy-done.2 = bf16[2240,560]{0,1:T(8,128)(2,1)S(1)} copy-done((bf16[2240,560]{0,1:T(8,128)(2,1)S(1)}, bf16[2240,560]{0,1:T(8,128)(2,1)}, u32[]{:S(2)}) %copy-start.2) | copy-done | bytes 2508824
  32.3 1.7 %copy-done.3 = bf16[2240,560]{0,1:T(8,128)(2,1)S(1)} copy-done((bf16[2240,560]{0,1:T(8,128)(2,1)S(1)}, bf16[2240,560]{0,1:T(8,128)(2,1)}, u32[]{:S(2)}) %copy-start.3) | copy-done | bytes 2508824
  34.0 1.7 %copy-done.4 = bf16[2240,560]{0,1:T(8,128)(2,1)S(1)} copy-done((bf16[2240,560]{0,1:T(8,128)(2,1)S(1)}, bf16[2240,560]{0,1:T(8,128)(2,1)}, u32[]{:S(2)}) %copy-start.4) | copy-done | bytes 2508824
  35.7 1.3 %shard_map.55.tie.cut = bf16[3,560,560]{2,1,0:T(8,128)(2,1)S(1)} custom-call(s32[2]{0:T(128)S(1)} %pad_add_fusion.place, bf16[560,2240]{1,0:T(8,128)(2,1)S(1)} %bitcast.15, bf16[560,2240]{1,0:T(8,128)(2,1)S(1)} %bitcast.18, bf16[560,2240]{1,0:T(8,128)(2,1)S(1)} %bitcast.21), custom_call_target="tpu_custom_call" | custom-call | flops 5017600 | bytes 1024 | tf_op jit(solution)/shard_map/pallas_call | solution.py:185
  37.0 3.7 %collective-permute-start.3 = (bf16[560,512]{1,0:T(8,128)(2,1)}, bf16[560,512]{1,0:T(8,128)(2,1)S(1)}, u32[]{:S(2)}, u32[]{:S(2)}) collective-permute-start(bf16[560,512]{1,0:T(8,128)(2,1)} %collective-permute-done.inner_ref), channel_id=1, source_target_pairs={{0,1},{1,0},{2,3},{3,2},{4,5},{5,4},{6,7},{7,6},{8,9},{9,8},{10,11... | collective-permute-start | bytes 1720328 | tf_op jit(solution)/shard_map/ppermute | solution.py:133
  41.3 7.0 %collective-permute-start.8 = (bf16[560,512]{1,0:T(8,128)(2,1)}, bf16[560,512]{1,0:T(8,128)(2,1)S(1)}, u32[]{:S(2)}, u32[]{:S(2)}) collective-permute-start(bf16[560,512]{1,0:T(8,128)(2,1)} %collective-permute-done.4.b2i), channel_id=1, source_target_pairs={{0,1},{1,0},{2,3},{3,2},{4,5},{5,4},{6,7},{7,6},{8,9},{9,8},{10,11... | collective-permute-start | bytes 1720328 | tf_op jit(solution)/shard_map/ppermute | solution.py:133
  48.3 6.2 %shard_map.56.sums = f32[3,560,512]{2,1,0:T(8,128)S(1)} custom-call(s32[2]{0:T(128)S(1)} %pad_add_fusion.place, bf16[2,560,512]{2,1,0:T(8,128)(2,1)S(1)} %bitcast.26, bf16[2,560,512]{2,1,0:T(8,128)(2,1)S(1)} %collective-permute-done.1.near, bf16[560,512]{1,0:T(8,128)(2,1)} %collective-permute-done.4.b2i, bf16[560,512]{1,0:T(8,128)(2,1)} %collective-permute-done.6.b2o, ...), custom_call_target="tpu_custom_call" | custom-call | flops 60211200 | bytes 1024 | tf_op jit(solution)/shard_map/pallas_call | solution.py:208
  54.8 3.1 %collective-permute-start.7 = (bf16[560,512]{1,0:T(8,128)(2,1)}, bf16[560,512]{1,0:T(8,128)(2,1)}, u32[]{:S(2)}, u32[]{:S(2)}) collective-permute-start(bf16[560,512]{1,0:T(8,128)(2,1)} %collective-permute-done.2.b2i), channel_id=1, source_target_pairs={{0,1},{1,0},{2,3},{3,2},{4,5},{5,4},{6,7},{7,6},{8,9},{9,8},{10,11... | collective-permute-start | bytes 1720328 | tf_op jit(solution)/shard_map/ppermute | solution.py:133
  58.0 5.3 %shard_map.57.rest_0_.sums = f32[3,560,512]{2,1,0:T(8,128)S(1)} custom-call(s32[2]{0:T(128)S(1)} %pad_add_fusion.place, bf16[2,560,512]{2,1,0:T(8,128)(2,1)S(1)} %bitcast.27, bf16[2,560,512]{2,1,0:T(8,128)(2,1)S(1)} %collective-permute-done.1.near, bf16[560,512]{1,0:T(8,128)(2,1)} %collective-permute-done.2.b2i, ...), custom_call_target="tpu_custom_call" | custom-call | flops 60211200 | bytes 1024 | tf_op jit(solution)/shard_map/pallas_call | solution.py:208
  63.3 3.9 %collective-permute-done.8.end_ref = bf16[560,512]{1,0:T(8,128)(2,1)S(1)} collective-permute-done((bf16[560,512]{1,0:T(8,128)(2,1)}, bf16[560,512]{1,0:T(8,128)(2,1)S(1)}, u32[]{:S(2)}, u32[]{:S(2)}) %collective-permute-start.8) | collective-permute-done | bytes 573472 | tf_op jit(solution)/shard_map/ppermute | solution.py:133
  67.1 2.3 %shard_map.58.tie = f32[560,112]{1,0:T(8,128)S(1)} custom-call(s32[2]{0:T(128)S(1)} %pad_add_fusion.place, bf16[560,512]{1,0:T(8,128)(2,1)} %collective-permute-done.5.inner_ref, bf16[560,512]{1,0:T(8,128)(2,1)S(1)} %collective-permute-done.8.end_ref, bf16[3,560,560]{2,1,0:T(8,128)(2,1)S(1)} %shard_map.55.tie.cut, f32[3,560,512]{2,1,0:T(8,128)S(1)} %shard_map.56.sums, ...), custom_call_target="tpu_custom_call" | custom-call | flops 10035200 | bytes 1024 | tf_op jit(solution)/shard_map/pallas_call | solution.py:215
  69.5 1.6 %collective-permute-start.10 = (bf16[560,112]{1,0:T(8,128)(2,1)S(1)}, bf16[560,112]{1,0:T(8,128)(2,1)S(1)}, u32[]{:S(2)}, u32[]{:S(2)}) collective-permute-start(bf16[560,112]{1,0:T(8,128)(2,1)S(1)} %convert_element_type.22), channel_id=1, source_target_pairs={{0,8},{4,12},{8,0},{12,4},{1,9},{5,13},{9,1},{13,5},{2,10},{6,14},... | collective-permute-start | bytes 376328 | tf_op jit(solution)/shard_map/ppermute | solution.py:156
  71.0 1.5 %collective-permute-start.11 = (bf16[560,112]{1,0:T(8,128)(2,1)S(1)}, bf16[560,112]{1,0:T(8,128)(2,1)S(1)}, u32[]{:S(2)}, u32[]{:S(2)}) collective-permute-start(bf16[560,112]{1,0:T(8,128)(2,1)S(1)} %convert_element_type.22), channel_id=1, source_target_pairs={{0,4},{4,0},{8,12},{12,8},{1,5},{5,1},{9,13},{13,9},{2,6},{6,2},{1... | collective-permute-start | bytes 376328 | tf_op jit(solution)/shard_map/ppermute | solution.py:156
  73.0 1.7 %shard_map.59.rest_1_.query = bf16[560,512]{1,0:T(8,128)(2,1)S(1)} custom-call(s32[2]{0:T(128)S(1)} %pad_add_fusion.place, bf16[560,512]{1,0:T(8,128)(2,1)} %collective-permute-done.5.inner_ref, bf16[560,512]{1,0:T(8,128)(2,1)S(1)} %collective-permute-done.8.end_ref, bf16[3,560,560]{2,1,0:T(8,128)(2,1)S(1)} %shard_map.55.tie.cut, ...), custom_call_target="tpu_custom_call" | custom-call | flops 5017600 | bytes 1024 | tf_op jit(solution)/shard_map/pallas_call | solution.py:219
  74.7 0.8 collective-permute-done.10
  75.5 0.7 collective-permute-done.11
  76.1 2.4 %collective-permute-done.9 = bf16[560,112]{1,0:T(8,128)(2,1)S(1)} collective-permute-done((bf16[560,112]{1,0:T(8,128)(2,1)S(1)}, bf16[560,112]{1,0:T(8,128)(2,1)S(1)}, u32[]{:S(2)}, u32[]{:S(2)}) %collective-permute-start.9) | collective-permute-done | bytes 125472 | tf_op jit(solution)/shard_map/ppermute | solution.py:156
  78.9 2.0 %copy-done.1 = f32[3,560,512]{2,1,0:T(8,128)S(1)} copy-done((f32[3,560,512]{2,1,0:T(8,128)S(1)}, f32[3,560,512]{2,1,0:T(8,128)}, u32[]{:S(2)}) %copy-start.1) | copy-done | bytes 3440664
  80.8 2.5 %shard_map.60.tie.rest_1_ = f32[560,112]{1,0:T(8,128)S(1)} custom-call(s32[2]{0:T(128)S(1)} %pad_add_fusion.place, bf16[560,512]{1,0:T(8,128)(2,1)} %collective-permute-done.inner_ref, bf16[560,512]{1,0:T(8,128)(2,1)} %collective-permute-done.7.end_ref, bf16[3,560,560]{2,1,0:T(8,128)(2,1)S(1)} %shard_map.55.tie.cut, f32[3,560,512]{2,1,0:T(8,128)S(1)} %copy-done.1, ...), custom_call_target="tpu_custom_call" | custom-call | flops 10035200 | bytes 1024 | tf_op jit(solution)/shard_map/pallas_call | solution.py:215
  83.3 1.6 %collective-permute-start.13 = (bf16[560,112]{1,0:T(8,128)(2,1)S(1)}, bf16[560,112]{1,0:T(8,128)(2,1)S(1)}, u32[]{:S(2)}, u32[]{:S(2)}) collective-permute-start(bf16[560,112]{1,0:T(8,128)(2,1)S(1)} %convert_element_type.28), channel_id=1, source_target_pairs={{0,12},{4,8},{8,4},{12,0},{1,13},{5,9},{9,5},{13,1},{2,14},{6,10},... | collective-permute-start | bytes 376328 | tf_op jit(solution)/shard_map/ppermute | solution.py:156
  85.4 1.4 %collective-permute-start.15 = (bf16[560,112]{1,0:T(8,128)(2,1)S(1)}, bf16[560,112]{1,0:T(8,128)(2,1)S(1)}, u32[]{:S(2)}, u32[]{:S(2)}) collective-permute-start(bf16[560,112]{1,0:T(8,128)(2,1)S(1)} %convert_element_type.28), channel_id=1, source_target_pairs={{0,4},{4,0},{8,12},{12,8},{1,5},{5,1},{9,13},{13,9},{2,6},{6,2},{1... | collective-permute-start | bytes 376328 | tf_op jit(solution)/shard_map/ppermute | solution.py:156
  86.9 1.9 %shard_map.61.query = bf16[560,512]{1,0:T(8,128)(2,1)S(1)} custom-call(s32[2]{0:T(128)S(1)} %pad_add_fusion.place, bf16[560,512]{1,0:T(8,128)(2,1)} %collective-permute-done.inner_ref, bf16[560,512]{1,0:T(8,128)(2,1)} %collective-permute-done.7.end_ref, bf16[3,560,560]{2,1,0:T(8,128)(2,1)S(1)} %shard_map.55.tie.cut, f32[3,560,512]{2,1,0:T(8,128)S(1)} %copy-done.1, ...), custom_call_target="tpu_custom_call" | custom-call | flops 5017600 | bytes 1024 | tf_op jit(solution)/shard_map/pallas_call | solution.py:219
  88.8 1.1 %shard_map.62.rest_5_ = bf16[2,560,512]{2,1,0:T(8,128)(2,1)} custom-call(bf16[560,512]{1,0:T(8,128)(2,1)S(1)} %shard_map.59.rest_1_.query, f32[560,1]{1,0:T(8,128)S(1)} %reshape.5.gain, f32[560,112]{1,0:T(8,128)S(1)} %convert_select_fusion.rest_0_, f32[560,112]{1,0:T(8,128)S(1)} %get-tuple-element.20.rest_0_.rest_1_), custom_call_target="tpu_custom_call" | custom-call | flops 1003520 | bytes 1024 | tf_op jit(solution)/shard_map/pallas_call | solution.py:230
  89.9 1.0 %collective-permute-done.13.rest_2_ = bf16[560,112]{1,0:T(8,128)(2,1)S(1)} collective-permute-done((bf16[560,112]{1,0:T(8,128)(2,1)S(1)}, bf16[560,112]{1,0:T(8,128)(2,1)S(1)}, u32[]{:S(2)}, u32[]{:S(2)}) %collective-permute-start.13) | collective-permute-done | bytes 125472 | tf_op jit(solution)/shard_map/ppermute | solution.py:156
  90.9 2.6 %collective-permute-done.14.rest_3_ = bf16[560,112]{1,0:T(8,128)(2,1)S(1)} collective-permute-done((bf16[560,112]{1,0:T(8,128)(2,1)S(1)}, bf16[560,112]{1,0:T(8,128)(2,1)S(1)}, u32[]{:S(2)}, u32[]{:S(2)}) %collective-permute-start.14) | collective-permute-done | bytes 125472 | tf_op jit(solution)/shard_map/ppermute | solution.py:156
  93.5 1.1 %shard_map.63 = bf16[2,560,512]{2,1,0:T(8,128)(2,1)} custom-call(bf16[560,512]{1,0:T(8,128)(2,1)S(1)} %shard_map.61.query, f32[560,1]{1,0:T(8,128)S(1)} %reshape.5.gain, f32[560,112]{1,0:T(8,128)S(1)} %convert_select_fusion.rest_0_, f32[560,112]{1,0:T(8,128)S(1)} %shard_map.60.tie.rest_1_, ...), custom_call_target="tpu_custom_call", output_to_operand_aliasing={{}: (7, {})} | custom-call | flops 1003520 | bytes 1024 | tf_op jit(solution)/shard_map/pallas_call | solution.py:230
  (33 shorter events, 2.8 us)
Async XLA Ops:
  0.0 29.3 %collective-permute-start.1 = (bf16[2,560,512]{2,1,0:T(8,128)(2,1)}, bf16[2,560,512]{2,1,0:T(8,128)(2,1)S(1)}, u32[]{:S(2)}, u32[]{:S(2)}) collective-permute-start(bf16[2,560,512]{2,1,0:T(8,128)(2,1)} %bitcast.24), channel_id=1, source_target_pairs={{0,1},{1,0},{2,3},{3,2},{4,5},{5,4},{6,7},{7,6},{8,9},{9,8},{10,11... | collective-permute-start | bytes 3440648 | tf_op jit(solution)/shard_map/ppermute | solution.py:133
  5.1 2.9 %collective-permute-start.5 = (bf16[560,512]{1,0:T(8,128)(2,1)S(1)}, bf16[560,512]{1,0:T(8,128)(2,1)}, u32[]{:S(2)}, u32[]{:S(2)}) collective-permute-start(bf16[560,512]{1,0:T(8,128)(2,1)S(1)} %get-tuple-element.21), channel_id=1, source_target_pairs={{0,16},{1,2},{2,1},{3,19},{16,0},{17,18},{18,17},{19,3},{4,20},{5,... | collective-permute-start | bytes 1720328 | tf_op jit(solution)/shard_map/ppermute | solution.py:145
  5.1 31.9 %collective-permute-start = (bf16[560,512]{1,0:T(8,128)(2,1)}, bf16[560,512]{1,0:T(8,128)(2,1)}, u32[]{:S(2)}, u32[]{:S(2)}) collective-permute-start(bf16[560,512]{1,0:T(8,128)(2,1)} %get-tuple-element.22), channel_id=1, source_target_pairs={{0,16},{1,2},{2,1},{3,19},{16,0},{17,18},{18,17},{19,3},{4,20},{5,... | collective-permute-start | bytes 1720328 | tf_op jit(solution)/shard_map/ppermute | solution.py:145
  8.0 33.3 %collective-permute-start.6 = (bf16[560,512]{1,0:T(8,128)(2,1)}, bf16[560,512]{1,0:T(8,128)(2,1)}, u32[]{:S(2)}, u32[]{:S(2)}) collective-permute-start(bf16[560,512]{1,0:T(8,128)(2,1)} %collective-permute-done.5.inner_ref), channel_id=1, source_target_pairs={{0,1},{1,0},{2,3},{3,2},{4,5},{5,4},{6,7},{7,6},{8,9},{9,8},{10,11... | collective-permute-start | bytes 1720328 | tf_op jit(solution)/shard_map/ppermute | solution.py:133
  30.4 10.9 %collective-permute-start.4 = (bf16[560,512]{1,0:T(8,128)(2,1)}, bf16[560,512]{1,0:T(8,128)(2,1)}, u32[]{:S(2)}, u32[]{:S(2)}) collective-permute-start(bf16[560,512]{1,0:T(8,128)(2,1)} %get-tuple-element.23), channel_id=1, source_target_pairs={{0,16},{1,2},{2,1},{3,19},{16,0},{17,18},{18,17},{19,3},{4,20},{5,... | collective-permute-start | bytes 1720328 | tf_op jit(solution)/shard_map/ppermute | solution.py:145
  30.5 1.7 %copy-start.2 = (bf16[2240,560]{0,1:T(8,128)(2,1)S(1)}, bf16[2240,560]{0,1:T(8,128)(2,1)}, u32[]{:S(2)}) copy-start(bf16[2240,560]{0,1:T(8,128)(2,1)} %param.7) | copy-start | bytes 7526404
  32.3 1.7 %copy-start.3 = (bf16[2240,560]{0,1:T(8,128)(2,1)S(1)}, bf16[2240,560]{0,1:T(8,128)(2,1)}, u32[]{:S(2)}) copy-start(bf16[2240,560]{0,1:T(8,128)(2,1)} %param.8) | copy-start | bytes 7526404
  34.0 1.7 %copy-start.4 = (bf16[2240,560]{0,1:T(8,128)(2,1)S(1)}, bf16[2240,560]{0,1:T(8,128)(2,1)}, u32[]{:S(2)}) copy-start(bf16[2240,560]{0,1:T(8,128)(2,1)} %param.6) | copy-start | bytes 7526404
  35.7 5.0 %copy-start.6 = (bf16[560,512]{1,0:T(8,128)(2,1)S(1)}, bf16[560,512]{1,0:T(8,128)(2,1)}, u32[]{:S(2)}) copy-start(bf16[560,512]{1,0:T(8,128)(2,1)} %get-tuple-element.24) | copy-start | bytes 1720324
  35.7 12.6 %copy-start.5 = (bf16[2,512,560]{1,2,0:T(8,128)(2,1)S(1)}, bf16[2,512,560]{1,2,0:T(8,128)(2,1)}, u32[]{:S(2)}) copy-start(bf16[2,512,560]{1,2,0:T(8,128)(2,1)} %param.5) | copy-start | bytes 3440644
  37.0 17.8 %collective-permute-start.3 = (bf16[560,512]{1,0:T(8,128)(2,1)}, bf16[560,512]{1,0:T(8,128)(2,1)S(1)}, u32[]{:S(2)}, u32[]{:S(2)}) collective-permute-start(bf16[560,512]{1,0:T(8,128)(2,1)} %collective-permute-done.inner_ref), channel_id=1, source_target_pairs={{0,1},{1,0},{2,3},{3,2},{4,5},{5,4},{6,7},{7,6},{8,9},{9,8},{10,11... | collective-permute-start | bytes 1720328 | tf_op jit(solution)/shard_map/ppermute | solution.py:133
  40.7 14.1 %collective-permute-start.2 = (bf16[560,512]{1,0:T(8,128)(2,1)S(1)}, bf16[560,512]{1,0:T(8,128)(2,1)}, u32[]{:S(2)}, u32[]{:S(2)}) collective-permute-start(bf16[560,512]{1,0:T(8,128)(2,1)S(1)} %copy-done.6), channel_id=1, source_target_pairs={{0,16},{1,2},{2,1},{3,19},{16,0},{17,18},{18,17},{19,3},{4,20},{5,... | collective-permute-start | bytes 1720328 | tf_op jit(solution)/shard_map/ppermute | solution.py:145
  41.3 25.8 %collective-permute-start.8 = (bf16[560,512]{1,0:T(8,128)(2,1)}, bf16[560,512]{1,0:T(8,128)(2,1)S(1)}, u32[]{:S(2)}, u32[]{:S(2)}) collective-permute-start(bf16[560,512]{1,0:T(8,128)(2,1)} %collective-permute-done.4.b2i), channel_id=1, source_target_pairs={{0,1},{1,0},{2,3},{3,2},{4,5},{5,4},{6,7},{7,6},{8,9},{9,8},{10,11... | collective-permute-start | bytes 1720328 | tf_op jit(solution)/shard_map/ppermute | solution.py:133
  54.8 24.0 %collective-permute-start.7 = (bf16[560,512]{1,0:T(8,128)(2,1)}, bf16[560,512]{1,0:T(8,128)(2,1)}, u32[]{:S(2)}, u32[]{:S(2)}) collective-permute-start(bf16[560,512]{1,0:T(8,128)(2,1)} %collective-permute-done.2.b2i), channel_id=1, source_target_pairs={{0,1},{1,0},{2,3},{3,2},{4,5},{5,4},{6,7},{7,6},{8,9},{9,8},{10,11... | collective-permute-start | bytes 1720328 | tf_op jit(solution)/shard_map/ppermute | solution.py:133
  63.2 6.2 %copy-start = (f32[3,560,512]{2,1,0:T(8,128)}, f32[3,560,512]{2,1,0:T(8,128)S(1)}, u32[]{:S(2)}) copy-start(f32[3,560,512]{2,1,0:T(8,128)S(1)} %shard_map.57.rest_0_.sums) | copy-start | bytes 10321924
  69.4 9.3 %copy-start.7 = (f32[560]{0:T(1024)S(1)}, f32[560]{0:T(1024)}, u32[]{:S(2)}) copy-start(f32[560]{0:T(1024)} %param.9) | copy-start | bytes 6724
  69.5 6.0 %collective-permute-start.10 = (bf16[560,112]{1,0:T(8,128)(2,1)S(1)}, bf16[560,112]{1,0:T(8,128)(2,1)S(1)}, u32[]{:S(2)}, u32[]{:S(2)}) collective-permute-start(bf16[560,112]{1,0:T(8,128)(2,1)S(1)} %convert_element_type.22), channel_id=1, source_target_pairs={{0,8},{4,12},{8,0},{12,4},{1,9},{5,13},{9,1},{13,5},{2,10},{6,14},... | collective-permute-start | bytes 376328 | tf_op jit(solution)/shard_map/ppermute | solution.py:156
  71.0 5.1 %collective-permute-start.11 = (bf16[560,112]{1,0:T(8,128)(2,1)S(1)}, bf16[560,112]{1,0:T(8,128)(2,1)S(1)}, u32[]{:S(2)}, u32[]{:S(2)}) collective-permute-start(bf16[560,112]{1,0:T(8,128)(2,1)S(1)} %convert_element_type.22), channel_id=1, source_target_pairs={{0,4},{4,0},{8,12},{12,8},{1,5},{5,1},{9,13},{13,9},{2,6},{6,2},{1... | collective-permute-start | bytes 376328 | tf_op jit(solution)/shard_map/ppermute | solution.py:156
  72.5 6.0 %collective-permute-start.9 = (bf16[560,112]{1,0:T(8,128)(2,1)S(1)}, bf16[560,112]{1,0:T(8,128)(2,1)S(1)}, u32[]{:S(2)}, u32[]{:S(2)}) collective-permute-start(bf16[560,112]{1,0:T(8,128)(2,1)S(1)} %convert_element_type.22), channel_id=1, source_target_pairs={{0,12},{4,8},{8,4},{12,0},{1,13},{5,9},{9,5},{13,1},{2,14},{6,10},... | collective-permute-start | bytes 376328 | tf_op jit(solution)/shard_map/ppermute | solution.py:156
  78.6 10.2 %collective-permute-start.12 = (bf16[560,112]{1,0:T(8,128)(2,1)S(1)}, bf16[560,112]{1,0:T(8,128)(2,1)S(1)}, u32[]{:S(2)}, u32[]{:S(2)}) collective-permute-start(bf16[560,112]{1,0:T(8,128)(2,1)S(1)} %get-tuple-element.19), channel_id=1, source_target_pairs={{0,16},{16,0},{1,17},{17,1},{2,18},{18,2},{3,19},{19,3},{4,20},{20... | collective-permute-start | bytes 376328 | tf_op jit(solution)/shard_map/ppermute | solution.py:164
  78.8 2.0 %copy-start.1 = (f32[3,560,512]{2,1,0:T(8,128)S(1)}, f32[3,560,512]{2,1,0:T(8,128)}, u32[]{:S(2)}) copy-start(f32[3,560,512]{2,1,0:T(8,128)} %copy-done) | copy-start | bytes 10321924
  83.3 7.6 %collective-permute-start.13 = (bf16[560,112]{1,0:T(8,128)(2,1)S(1)}, bf16[560,112]{1,0:T(8,128)(2,1)S(1)}, u32[]{:S(2)}, u32[]{:S(2)}) collective-permute-start(bf16[560,112]{1,0:T(8,128)(2,1)S(1)} %convert_element_type.28), channel_id=1, source_target_pairs={{0,12},{4,8},{8,4},{12,0},{1,13},{5,9},{9,5},{13,1},{2,14},{6,10},... | collective-permute-start | bytes 376328 | tf_op jit(solution)/shard_map/ppermute | solution.py:156
  84.9 8.6 %collective-permute-start.14 = (bf16[560,112]{1,0:T(8,128)(2,1)S(1)}, bf16[560,112]{1,0:T(8,128)(2,1)S(1)}, u32[]{:S(2)}, u32[]{:S(2)}) collective-permute-start(bf16[560,112]{1,0:T(8,128)(2,1)S(1)} %convert_element_type.28), channel_id=1, source_target_pairs={{0,8},{4,12},{8,0},{12,4},{1,9},{5,13},{9,1},{13,5},{2,10},{6,14},... | collective-permute-start | bytes 376328 | tf_op jit(solution)/shard_map/ppermute | solution.py:156
  85.4 8.1 %collective-permute-start.15 = (bf16[560,112]{1,0:T(8,128)(2,1)S(1)}, bf16[560,112]{1,0:T(8,128)(2,1)S(1)}, u32[]{:S(2)}, u32[]{:S(2)}) collective-permute-start(bf16[560,112]{1,0:T(8,128)(2,1)S(1)} %convert_element_type.28), channel_id=1, source_target_pairs={{0,4},{4,0},{8,12},{12,8},{1,5},{5,1},{9,13},{13,9},{2,6},{6,2},{1... | collective-permute-start | bytes 376328 | tf_op jit(solution)/shard_map/ppermute | solution.py:156

commit v12 on v11

--- a/solution.py
+++ b/solution.py
@@ -8,7 +8,7 @@
 from jax.sharding import PartitionSpec as P
 
 HEAD_DIM = 112
-VMEM_LIMIT = 20 * 1024 * 1024
+VMEM_LIMIT = 8 * 1024 * 1024
 ANYWHERE = pl.BlockSpec(memory_space=pl.ANY)
 IN_VMEM = pl.BlockSpec(memory_space=pltpu.VMEM)
 IN_SMEM = pl.BlockSpec(memory_space=pltpu.SMEM)

time: 95.1 us -> 95.2 us (level)
    unnamed x16 -> x18, local copies, waits for them, and re-layouts: 7.17 us -> 7.17 us
where the time goes in v12:
time: 95.2 us; the launch traced here: 94.8 us
  starting transfers between devices  38.8 us (41%)
  Pallas kernels  23.5 us (25%)
  waiting for transfers between devices  21.6 us (23%)
  local copies, waits for them, and re-layouts  10.5 us (11%)
    ppermute x5, starting transfers between devices, partner_swap(): lax.ppermute(value, axis, [(i, i ^ 1) for i in range(lax.axis_size(axis))])  31.1 us
    ppermute x5, waiting for transfers between devices, partner_swap(): lax.ppermute(value, axis, [(i, i ^ 1) for i in range(lax.axis_size(axis))])  11.8 us
    pallas_call x2, Pallas kernels, local(): call(functools.partial(partial_kernel, stream), jax.ShapeDtypeStruct((3,...  11.5 us
    ppermute x6, waiting for transfers between devices, from_others(): got.append(lax.ppermute(sent, axis, pairs))  7.42 us
    unnamed x18, local copies, waits for them, and re-layouts  7.17 us
    ppermute x6, starting transfers between devices, from_others(): got.append(lax.ppermute(sent, axis, pairs))  7.11 us
    pallas_call x2, Pallas kernels, local(): call(state_kernel, state_type, IN_VMEM, [IN_SMEM] + [IN_VMEM] * 4 + [ANYW...  4.9 us
    pallas_call x2, Pallas kernels, local(): call(query_kernel, query_type, IN_VMEM, [IN_SMEM] + [IN_VMEM] * 4 + [ANYW...  3.55 us
  transfers between devices with their start and end apart: 16, of which 10 were waited for; matrix products, arithmetic and copies ran while one was open for 4% of the time, Pallas kernels for 24%

profile of v12, /device:TPU:0, one launch (start us, length us, event | category | flops | bytes accessed | tf_op | source)
XLA Modules:
  0.0 94.8 jit_solution(7612189309017842262)
XLA Ops:
  0.0 3.0 %collective-permute-start.1 = (bf16[2,560,512]{2,1,0:T(8,128)(2,1)}, bf16[2,560,512]{2,1,0:T(8,128)(2,1)S(1)}, u32[]{:S(2)}, u32[]{:S(2)}) collective-permute-start(bf16[2,560,512]{2,1,0:T(8,128)(2,1)} %bitcast.24), channel_id=1, source_target_pairs={{0,1},{1,0},{2,3},{3,2},{4,5},{5,4},{6,7},{7,6},{8,9},{9,8},{10,11... | collective-permute-start | bytes 3440648 | tf_op jit(solution)/shard_map/ppermute | solution.py:133
  3.0 2.1 %slice_bitcast_fusion = (bf16[560,512]{1,0:T(8,128)(2,1)S(1)}, bf16[560,512]{1,0:T(8,128)(2,1)}) fusion(bf16[2,560,512]{2,1,0:T(8,128)(2,1)} %bitcast.25), kind=kLoop, calls=%fused_computation | loop fusion | bytes 2293760 | tf_op jit(solution)/shard_map/squeeze | solution.py:192
  5.7 2.4 %collective-permute-done.5.inner_ref = bf16[560,512]{1,0:T(8,128)(2,1)} collective-permute-done((bf16[560,512]{1,0:T(8,128)(2,1)S(1)}, bf16[560,512]{1,0:T(8,128)(2,1)}, u32[]{:S(2)}, u32[]{:S(2)}) %collective-permute-start.5) | collective-permute-done | bytes 573472 | tf_op jit(solution)/shard_map/ppermute | solution.py:145
  8.0 14.2 %collective-permute-start.6 = (bf16[560,512]{1,0:T(8,128)(2,1)}, bf16[560,512]{1,0:T(8,128)(2,1)}, u32[]{:S(2)}, u32[]{:S(2)}) collective-permute-start(bf16[560,512]{1,0:T(8,128)(2,1)} %collective-permute-done.5.inner_ref), channel_id=1, source_target_pairs={{0,1},{1,0},{2,3},{3,2},{4,5},{5,4},{6,7},{7,6},{8,9},{9,8},{10,11... | collective-permute-start | bytes 1720328 | tf_op jit(solution)/shard_map/ppermute | solution.py:133
  22.2 7.1 %collective-permute-done.1.near = bf16[2,560,512]{2,1,0:T(8,128)(2,1)S(1)} collective-permute-done((bf16[2,560,512]{2,1,0:T(8,128)(2,1)}, bf16[2,560,512]{2,1,0:T(8,128)(2,1)S(1)}, u32[]{:S(2)}, u32[]{:S(2)}) %collective-permute-start.1) | collective-permute-done | bytes 1146912 | tf_op jit(solution)/shard_map/ppermute | solution.py:133
  29.3 1.1 %slice_bitcast_fusion.1 = (bf16[560,512]{1,0:T(8,128)(2,1)}, bf16[560,512]{1,0:T(8,128)(2,1)}) fusion(bf16[2,560,512]{2,1,0:T(8,128)(2,1)S(1)} %collective-permute-done.1.near), kind=kLoop, calls=%fused_computation.1 | loop fusion | bytes 2293760 | tf_op jit(solution)/shard_map/squeeze | solution.py:194
  30.5 1.7 %copy-done.3 = bf16[2240,560]{0,1:T(8,128)(2,1)S(1)} copy-done((bf16[2240,560]{0,1:T(8,128)(2,1)S(1)}, bf16[2240,560]{0,1:T(8,128)(2,1)}, u32[]{:S(2)}) %copy-start.3) | copy-done | bytes 2508824
  32.3 1.7 %copy-done.4 = bf16[2240,560]{0,1:T(8,128)(2,1)S(1)} copy-done((bf16[2240,560]{0,1:T(8,128)(2,1)S(1)}, bf16[2240,560]{0,1:T(8,128)(2,1)}, u32[]{:S(2)}) %copy-start.4) | copy-done | bytes 2508824
  34.0 1.7 %copy-done.5 = bf16[2240,560]{0,1:T(8,128)(2,1)S(1)} copy-done((bf16[2240,560]{0,1:T(8,128)(2,1)S(1)}, bf16[2240,560]{0,1:T(8,128)(2,1)}, u32[]{:S(2)}) %copy-start.5) | copy-done | bytes 2508824
  35.7 1.3 %shard_map.55.tie.cut = bf16[3,560,560]{2,1,0:T(8,128)(2,1)S(1)} custom-call(s32[2]{0:T(128)S(1)} %pad_add_fusion.place, bf16[560,2240]{1,0:T(8,128)(2,1)S(1)} %bitcast.15, bf16[560,2240]{1,0:T(8,128)(2,1)S(1)} %bitcast.18, bf16[560,2240]{1,0:T(8,128)(2,1)S(1)} %bitcast.21), custom_call_target="tpu_custom_call" | custom-call | flops 5017600 | bytes 1024 | tf_op jit(solution)/shard_map/pallas_call | solution.py:185
  37.0 3.7 %collective-permute-start.3 = (bf16[560,512]{1,0:T(8,128)(2,1)}, bf16[560,512]{1,0:T(8,128)(2,1)S(1)}, u32[]{:S(2)}, u32[]{:S(2)}) collective-permute-start(bf16[560,512]{1,0:T(8,128)(2,1)} %collective-permute-done.inner_ref), channel_id=1, source_target_pairs={{0,1},{1,0},{2,3},{3,2},{4,5},{5,4},{6,7},{7,6},{8,9},{9,8},{10,11... | collective-permute-start | bytes 1720328 | tf_op jit(solution)/shard_map/ppermute | solution.py:133
  41.3 7.0 %collective-permute-start.8 = (bf16[560,512]{1,0:T(8,128)(2,1)}, bf16[560,512]{1,0:T(8,128)(2,1)S(1)}, u32[]{:S(2)}, u32[]{:S(2)}) collective-permute-start(bf16[560,512]{1,0:T(8,128)(2,1)} %collective-permute-done.4.b2i), channel_id=1, source_target_pairs={{0,1},{1,0},{2,3},{3,2},{4,5},{5,4},{6,7},{7,6},{8,9},{9,8},{10,11... | collective-permute-start | bytes 1720328 | tf_op jit(solution)/shard_map/ppermute | solution.py:133
  48.3 6.2 %shard_map.56.sums = f32[3,560,512]{2,1,0:T(8,128)S(1)} custom-call(s32[2]{0:T(128)S(1)} %pad_add_fusion.place, bf16[2,560,512]{2,1,0:T(8,128)(2,1)S(1)} %bitcast.26, bf16[2,560,512]{2,1,0:T(8,128)(2,1)S(1)} %collective-permute-done.1.near, bf16[560,512]{1,0:T(8,128)(2,1)} %collective-permute-done.4.b2i, bf16[560,512]{1,0:T(8,128)(2,1)} %collective-permute-done.6.b2o, ...), custom_call_target="tpu_custom_call" | custom-call | flops 60211200 | bytes 1024 | tf_op jit(solution)/shard_map/pallas_call | solution.py:208
  54.8 3.1 %collective-permute-start.7 = (bf16[560,512]{1,0:T(8,128)(2,1)}, bf16[560,512]{1,0:T(8,128)(2,1)}, u32[]{:S(2)}, u32[]{:S(2)}) collective-permute-start(bf16[560,512]{1,0:T(8,128)(2,1)} %collective-permute-done.2.b2i), channel_id=1, source_target_pairs={{0,1},{1,0},{2,3},{3,2},{4,5},{5,4},{6,7},{7,6},{8,9},{9,8},{10,11... | collective-permute-start | bytes 1720328 | tf_op jit(solution)/shard_map/ppermute | solution.py:133
  58.0 5.3 %shard_map.57.rest_0_.sums = f32[3,560,512]{2,1,0:T(8,128)S(1)} custom-call(s32[2]{0:T(128)S(1)} %pad_add_fusion.place, bf16[2,560,512]{2,1,0:T(8,128)(2,1)S(1)} %bitcast.27, bf16[2,560,512]{2,1,0:T(8,128)(2,1)S(1)} %collective-permute-done.1.near, bf16[560,512]{1,0:T(8,128)(2,1)} %collective-permute-done.2.b2i, ...), custom_call_target="tpu_custom_call" | custom-call | flops 60211200 | bytes 1024 | tf_op jit(solution)/shard_map/pallas_call | solution.py:208
  63.3 3.9 %collective-permute-done.8.end_ref = bf16[560,512]{1,0:T(8,128)(2,1)S(1)} collective-permute-done((bf16[560,512]{1,0:T(8,128)(2,1)}, bf16[560,512]{1,0:T(8,128)(2,1)S(1)}, u32[]{:S(2)}, u32[]{:S(2)}) %collective-permute-start.8) | collective-permute-done | bytes 573472 | tf_op jit(solution)/shard_map/ppermute | solution.py:133
  67.1 2.3 %shard_map.58.tie = f32[560,112]{1,0:T(8,128)S(1)} custom-call(s32[2]{0:T(128)S(1)} %pad_add_fusion.place, bf16[560,512]{1,0:T(8,128)(2,1)} %collective-permute-done.5.inner_ref, bf16[560,512]{1,0:T(8,128)(2,1)S(1)} %collective-permute-done.8.end_ref, bf16[3,560,560]{2,1,0:T(8,128)(2,1)S(1)} %shard_map.55.tie.cut, f32[3,560,512]{2,1,0:T(8,128)S(1)} %shard_map.56.sums, ...), custom_call_target="tpu_custom_call" | custom-call | flops 10035200 | bytes 1024 | tf_op jit(solution)/shard_map/pallas_call | solution.py:215
  69.4 1.6 %collective-permute-start.10 = (bf16[560,112]{1,0:T(8,128)(2,1)S(1)}, bf16[560,112]{1,0:T(8,128)(2,1)S(1)}, u32[]{:S(2)}, u32[]{:S(2)}) collective-permute-start(bf16[560,112]{1,0:T(8,128)(2,1)S(1)} %convert_element_type.22), channel_id=1, source_target_pairs={{0,8},{4,12},{8,0},{12,4},{1,9},{5,13},{9,1},{13,5},{2,10},{6,14},... | collective-permute-start | bytes 376328 | tf_op jit(solution)/shard_map/ppermute | solution.py:156
  71.0 1.5 %collective-permute-start.11 = (bf16[560,112]{1,0:T(8,128)(2,1)S(1)}, bf16[560,112]{1,0:T(8,128)(2,1)S(1)}, u32[]{:S(2)}, u32[]{:S(2)}) collective-permute-start(bf16[560,112]{1,0:T(8,128)(2,1)S(1)} %convert_element_type.22), channel_id=1, source_target_pairs={{0,4},{4,0},{8,12},{12,8},{1,5},{5,1},{9,13},{13,9},{2,6},{6,2},{1... | collective-permute-start | bytes 376328 | tf_op jit(solution)/shard_map/ppermute | solution.py:156
  73.0 1.7 %shard_map.59.rest_1_.query = bf16[560,512]{1,0:T(8,128)(2,1)S(1)} custom-call(s32[2]{0:T(128)S(1)} %pad_add_fusion.place, bf16[560,512]{1,0:T(8,128)(2,1)} %collective-permute-done.5.inner_ref, bf16[560,512]{1,0:T(8,128)(2,1)S(1)} %collective-permute-done.8.end_ref, bf16[3,560,560]{2,1,0:T(8,128)(2,1)S(1)} %shard_map.55.tie.cut, ...), custom_call_target="tpu_custom_call" | custom-call | flops 5017600 | bytes 1024 | tf_op jit(solution)/shard_map/pallas_call | solution.py:219
  74.7 0.8 collective-permute-done.10
  75.5 0.7 collective-permute-done.11
  76.1 2.4 %collective-permute-done.9 = bf16[560,112]{1,0:T(8,128)(2,1)S(1)} collective-permute-done((bf16[560,112]{1,0:T(8,128)(2,1)S(1)}, bf16[560,112]{1,0:T(8,128)(2,1)S(1)}, u32[]{:S(2)}, u32[]{:S(2)}) %collective-permute-start.9) | collective-permute-done | bytes 125472 | tf_op jit(solution)/shard_map/ppermute | solution.py:156
  78.8 2.0 %copy-done.1 = f32[3,560,512]{2,1,0:T(8,128)S(1)} copy-done((f32[3,560,512]{2,1,0:T(8,128)S(1)}, f32[3,560,512]{2,1,0:T(8,128)}, u32[]{:S(2)}) %copy-start.1) | copy-done | bytes 3440664
  80.8 2.6 %shard_map.60.tie.rest_1_ = f32[560,112]{1,0:T(8,128)S(1)} custom-call(s32[2]{0:T(128)S(1)} %pad_add_fusion.place, bf16[560,512]{1,0:T(8,128)(2,1)} %collective-permute-done.inner_ref, bf16[560,512]{1,0:T(8,128)(2,1)} %collective-permute-done.7.end_ref, bf16[3,560,560]{2,1,0:T(8,128)(2,1)S(1)} %shard_map.55.tie.cut, f32[3,560,512]{2,1,0:T(8,128)S(1)} %copy-done.1, ...), custom_call_target="tpu_custom_call" | custom-call | flops 10035200 | bytes 1024 | tf_op jit(solution)/shard_map/pallas_call | solution.py:215
  83.5 1.6 %collective-permute-start.13 = (bf16[560,112]{1,0:T(8,128)(2,1)S(1)}, bf16[560,112]{1,0:T(8,128)(2,1)S(1)}, u32[]{:S(2)}, u32[]{:S(2)}) collective-permute-start(bf16[560,112]{1,0:T(8,128)(2,1)S(1)} %convert_element_type.28), channel_id=1, source_target_pairs={{0,12},{4,8},{8,4},{12,0},{1,13},{5,9},{9,5},{13,1},{2,14},{6,10},... | collective-permute-start | bytes 376328 | tf_op jit(solution)/shard_map/ppermute | solution.py:156
  85.6 1.4 %collective-permute-start.15 = (bf16[560,112]{1,0:T(8,128)(2,1)S(1)}, bf16[560,112]{1,0:T(8,128)(2,1)S(1)}, u32[]{:S(2)}, u32[]{:S(2)}) collective-permute-start(bf16[560,112]{1,0:T(8,128)(2,1)S(1)} %convert_element_type.28), channel_id=1, source_target_pairs={{0,4},{4,0},{8,12},{12,8},{1,5},{5,1},{9,13},{13,9},{2,6},{6,2},{1... | collective-permute-start | bytes 376328 | tf_op jit(solution)/shard_map/ppermute | solution.py:156
  87.0 1.9 %shard_map.61.query = bf16[560,512]{1,0:T(8,128)(2,1)S(1)} custom-call(s32[2]{0:T(128)S(1)} %pad_add_fusion.place, bf16[560,512]{1,0:T(8,128)(2,1)} %collective-permute-done.inner_ref, bf16[560,512]{1,0:T(8,128)(2,1)} %collective-permute-done.7.end_ref, bf16[3,560,560]{2,1,0:T(8,128)(2,1)S(1)} %shard_map.55.tie.cut, f32[3,560,512]{2,1,0:T(8,128)S(1)} %copy-done.2, ...), custom_call_target="tpu_custom_call" | custom-call | flops 5017600 | bytes 1024 | tf_op jit(solution)/shard_map/pallas_call | solution.py:219
  88.9 1.1 %shard_map.62.rest_5_ = bf16[2,560,512]{2,1,0:T(8,128)(2,1)} custom-call(bf16[560,512]{1,0:T(8,128)(2,1)S(1)} %shard_map.59.rest_1_.query, f32[560,1]{1,0:T(8,128)S(1)} %reshape.5.gain, f32[560,112]{1,0:T(8,128)S(1)} %convert_select_fusion.rest_0_, f32[560,112]{1,0:T(8,128)S(1)} %get-tuple-element.20.rest_0_.rest_1_), custom_call_target="tpu_custom_call" | custom-call | flops 1003520 | bytes 1024 | tf_op jit(solution)/shard_map/pallas_call | solution.py:230
  90.1 1.0 %collective-permute-done.13.rest_2_ = bf16[560,112]{1,0:T(8,128)(2,1)S(1)} collective-permute-done((bf16[560,112]{1,0:T(8,128)(2,1)S(1)}, bf16[560,112]{1,0:T(8,128)(2,1)S(1)}, u32[]{:S(2)}, u32[]{:S(2)}) %collective-permute-start.13) | collective-permute-done | bytes 125472 | tf_op jit(solution)/shard_map/ppermute | solution.py:156
  91.0 2.6 %collective-permute-done.14.rest_3_ = bf16[560,112]{1,0:T(8,128)(2,1)S(1)} collective-permute-done((bf16[560,112]{1,0:T(8,128)(2,1)S(1)}, bf16[560,112]{1,0:T(8,128)(2,1)S(1)}, u32[]{:S(2)}, u32[]{:S(2)}) %collective-permute-start.14) | collective-permute-done | bytes 125472 | tf_op jit(solution)/shard_map/ppermute | solution.py:156
  93.7 1.1 %shard_map.63 = bf16[2,560,512]{2,1,0:T(8,128)(2,1)} custom-call(bf16[560,512]{1,0:T(8,128)(2,1)S(1)} %shard_map.61.query, f32[560,1]{1,0:T(8,128)S(1)} %reshape.5.gain, f32[560,112]{1,0:T(8,128)S(1)} %convert_select_fusion.rest_0_, f32[560,112]{1,0:T(8,128)S(1)} %shard_map.60.tie.rest_1_, ...), custom_call_target="tpu_custom_call", output_to_operand_aliasing={{}: (7, {})} | custom-call | flops 1003520 | bytes 1024 | tf_op jit(solution)/shard_map/pallas_call | solution.py:230
  (35 shorter events, 2.8 us)
Async XLA Ops:
  0.0 29.3 %collective-permute-start.1 = (bf16[2,560,512]{2,1,0:T(8,128)(2,1)}, bf16[2,560,512]{2,1,0:T(8,128)(2,1)S(1)}, u32[]{:S(2)}, u32[]{:S(2)}) collective-permute-start(bf16[2,560,512]{2,1,0:T(8,128)(2,1)} %bitcast.24), channel_id=1, source_target_pairs={{0,1},{1,0},{2,3},{3,2},{4,5},{5,4},{6,7},{7,6},{8,9},{9,8},{10,11... | collective-permute-start | bytes 3440648 | tf_op jit(solution)/shard_map/ppermute | solution.py:133
  5.1 2.9 %collective-permute-start.5 = (bf16[560,512]{1,0:T(8,128)(2,1)S(1)}, bf16[560,512]{1,0:T(8,128)(2,1)}, u32[]{:S(2)}, u32[]{:S(2)}) collective-permute-start(bf16[560,512]{1,0:T(8,128)(2,1)S(1)} %get-tuple-element.21), channel_id=1, source_target_pairs={{0,16},{1,2},{2,1},{3,19},{16,0},{17,18},{18,17},{19,3},{4,20},{5,... | collective-permute-start | bytes 1720328 | tf_op jit(solution)/shard_map/ppermute | solution.py:145
  5.1 31.9 %collective-permute-start = (bf16[560,512]{1,0:T(8,128)(2,1)}, bf16[560,512]{1,0:T(8,128)(2,1)}, u32[]{:S(2)}, u32[]{:S(2)}) collective-permute-start(bf16[560,512]{1,0:T(8,128)(2,1)} %get-tuple-element.22), channel_id=1, source_target_pairs={{0,16},{1,2},{2,1},{3,19},{16,0},{17,18},{18,17},{19,3},{4,20},{5,... | collective-permute-start | bytes 1720328 | tf_op jit(solution)/shard_map/ppermute | solution.py:145
  8.0 33.3 %collective-permute-start.6 = (bf16[560,512]{1,0:T(8,128)(2,1)}, bf16[560,512]{1,0:T(8,128)(2,1)}, u32[]{:S(2)}, u32[]{:S(2)}) collective-permute-start(bf16[560,512]{1,0:T(8,128)(2,1)} %collective-permute-done.5.inner_ref), channel_id=1, source_target_pairs={{0,1},{1,0},{2,3},{3,2},{4,5},{5,4},{6,7},{7,6},{8,9},{9,8},{10,11... | collective-permute-start | bytes 1720328 | tf_op jit(solution)/shard_map/ppermute | solution.py:133
  30.4 10.9 %collective-permute-start.4 = (bf16[560,512]{1,0:T(8,128)(2,1)}, bf16[560,512]{1,0:T(8,128)(2,1)}, u32[]{:S(2)}, u32[]{:S(2)}) collective-permute-start(bf16[560,512]{1,0:T(8,128)(2,1)} %get-tuple-element.23), channel_id=1, source_target_pairs={{0,16},{1,2},{2,1},{3,19},{16,0},{17,18},{18,17},{19,3},{4,20},{5,... | collective-permute-start | bytes 1720328 | tf_op jit(solution)/shard_map/ppermute | solution.py:145
  30.5 1.7 %copy-start.3 = (bf16[2240,560]{0,1:T(8,128)(2,1)S(1)}, bf16[2240,560]{0,1:T(8,128)(2,1)}, u32[]{:S(2)}) copy-start(bf16[2240,560]{0,1:T(8,128)(2,1)} %param.7) | copy-start | bytes 7526404
  32.2 1.7 %copy-start.4 = (bf16[2240,560]{0,1:T(8,128)(2,1)S(1)}, bf16[2240,560]{0,1:T(8,128)(2,1)}, u32[]{:S(2)}) copy-start(bf16[2240,560]{0,1:T(8,128)(2,1)} %param.8) | copy-start | bytes 7526404
  34.0 1.7 %copy-start.5 = (bf16[2240,560]{0,1:T(8,128)(2,1)S(1)}, bf16[2240,560]{0,1:T(8,128)(2,1)}, u32[]{:S(2)}) copy-start(bf16[2240,560]{0,1:T(8,128)(2,1)} %param.6) | copy-start | bytes 7526404
  35.7 5.0 %copy-start.7 = (bf16[560,512]{1,0:T(8,128)(2,1)S(1)}, bf16[560,512]{1,0:T(8,128)(2,1)}, u32[]{:S(2)}) copy-start(bf16[560,512]{1,0:T(8,128)(2,1)} %get-tuple-element.24) | copy-start | bytes 1720324
  35.7 12.6 %copy-start.6 = (bf16[2,512,560]{1,2,0:T(8,128)(2,1)S(1)}, bf16[2,512,560]{1,2,0:T(8,128)(2,1)}, u32[]{:S(2)}) copy-start(bf16[2,512,560]{1,2,0:T(8,128)(2,1)} %param.5) | copy-start | bytes 3440644
  37.0 17.8 %collective-permute-start.3 = (bf16[560,512]{1,0:T(8,128)(2,1)}, bf16[560,512]{1,0:T(8,128)(2,1)S(1)}, u32[]{:S(2)}, u32[]{:S(2)}) collective-permute-start(bf16[560,512]{1,0:T(8,128)(2,1)} %collective-permute-done.inner_ref), channel_id=1, source_target_pairs={{0,1},{1,0},{2,3},{3,2},{4,5},{5,4},{6,7},{7,6},{8,9},{9,8},{10,11... | collective-permute-start | bytes 1720328 | tf_op jit(solution)/shard_map/ppermute | solution.py:133
  40.7 14.1 %collective-permute-start.2 = (bf16[560,512]{1,0:T(8,128)(2,1)S(1)}, bf16[560,512]{1,0:T(8,128)(2,1)}, u32[]{:S(2)}, u32[]{:S(2)}) collective-permute-start(bf16[560,512]{1,0:T(8,128)(2,1)S(1)} %copy-done.7), channel_id=1, source_target_pairs={{0,16},{1,2},{2,1},{3,19},{16,0},{17,18},{18,17},{19,3},{4,20},{5,... | collective-permute-start | bytes 1720328 | tf_op jit(solution)/shard_map/ppermute | solution.py:145
  41.3 25.8 %collective-permute-start.8 = (bf16[560,512]{1,0:T(8,128)(2,1)}, bf16[560,512]{1,0:T(8,128)(2,1)S(1)}, u32[]{:S(2)}, u32[]{:S(2)}) collective-permute-start(bf16[560,512]{1,0:T(8,128)(2,1)} %collective-permute-done.4.b2i), channel_id=1, source_target_pairs={{0,1},{1,0},{2,3},{3,2},{4,5},{5,4},{6,7},{7,6},{8,9},{9,8},{10,11... | collective-permute-start | bytes 1720328 | tf_op jit(solution)/shard_map/ppermute | solution.py:133
  54.8 24.0 %collective-permute-start.7 = (bf16[560,512]{1,0:T(8,128)(2,1)}, bf16[560,512]{1,0:T(8,128)(2,1)}, u32[]{:S(2)}, u32[]{:S(2)}) collective-permute-start(bf16[560,512]{1,0:T(8,128)(2,1)} %collective-permute-done.2.b2i), channel_id=1, source_target_pairs={{0,1},{1,0},{2,3},{3,2},{4,5},{5,4},{6,7},{7,6},{8,9},{9,8},{10,11... | collective-permute-start | bytes 1720328 | tf_op jit(solution)/shard_map/ppermute | solution.py:133
  63.2 6.1 %copy-start = (f32[3,560,512]{2,1,0:T(8,128)}, f32[3,560,512]{2,1,0:T(8,128)S(1)}, u32[]{:S(2)}) copy-start(f32[3,560,512]{2,1,0:T(8,128)S(1)} %shard_map.57.rest_0_.sums) | copy-start | bytes 10321924
  69.4 9.3 %copy-start.8 = (f32[560]{0:T(1024)S(1)}, f32[560]{0:T(1024)}, u32[]{:S(2)}) copy-start(f32[560]{0:T(1024)} %param.9) | copy-start | bytes 6724
  69.4 6.0 %collective-permute-start.10 = (bf16[560,112]{1,0:T(8,128)(2,1)S(1)}, bf16[560,112]{1,0:T(8,128)(2,1)S(1)}, u32[]{:S(2)}, u32[]{:S(2)}) collective-permute-start(bf16[560,112]{1,0:T(8,128)(2,1)S(1)} %convert_element_type.22), channel_id=1, source_target_pairs={{0,8},{4,12},{8,0},{12,4},{1,9},{5,13},{9,1},{13,5},{2,10},{6,14},... | collective-permute-start | bytes 376328 | tf_op jit(solution)/shard_map/ppermute | solution.py:156
  71.0 5.1 %collective-permute-start.11 = (bf16[560,112]{1,0:T(8,128)(2,1)S(1)}, bf16[560,112]{1,0:T(8,128)(2,1)S(1)}, u32[]{:S(2)}, u32[]{:S(2)}) collective-permute-start(bf16[560,112]{1,0:T(8,128)(2,1)S(1)} %convert_element_type.22), channel_id=1, source_target_pairs={{0,4},{4,0},{8,12},{12,8},{1,5},{5,1},{9,13},{13,9},{2,6},{6,2},{1... | collective-permute-start | bytes 376328 | tf_op jit(solution)/shard_map/ppermute | solution.py:156
  72.5 6.0 %collective-permute-start.9 = (bf16[560,112]{1,0:T(8,128)(2,1)S(1)}, bf16[560,112]{1,0:T(8,128)(2,1)S(1)}, u32[]{:S(2)}, u32[]{:S(2)}) collective-permute-start(bf16[560,112]{1,0:T(8,128)(2,1)S(1)} %convert_element_type.22), channel_id=1, source_target_pairs={{0,12},{4,8},{8,4},{12,0},{1,13},{5,9},{9,5},{13,1},{2,14},{6,10},... | collective-permute-start | bytes 376328 | tf_op jit(solution)/shard_map/ppermute | solution.py:156
  78.6 10.3 %collective-permute-start.12 = (bf16[560,112]{1,0:T(8,128)(2,1)S(1)}, bf16[560,112]{1,0:T(8,128)(2,1)S(1)}, u32[]{:S(2)}, u32[]{:S(2)}) collective-permute-start(bf16[560,112]{1,0:T(8,128)(2,1)S(1)} %get-tuple-element.19), channel_id=1, source_target_pairs={{0,16},{16,0},{1,17},{17,1},{2,18},{18,2},{3,19},{19,3},{4,20},{20... | collective-permute-start | bytes 376328 | tf_op jit(solution)/shard_map/ppermute | solution.py:164
  78.8 2.0 %copy-start.1 = (f32[3,560,512]{2,1,0:T(8,128)S(1)}, f32[3,560,512]{2,1,0:T(8,128)}, u32[]{:S(2)}) copy-start(f32[3,560,512]{2,1,0:T(8,128)} %copy-done) | copy-start | bytes 10321924
  80.8 6.2 %copy-start.2 = (f32[3,560,512]{2,1,0:T(8,128)S(1)}, f32[3,560,512]{2,1,0:T(8,128)}, u32[]{:S(2)}) copy-start(f32[3,560,512]{2,1,0:T(8,128)} %copy-done) | copy-start | bytes 10321924
  83.5 7.6 %collective-permute-start.13 = (bf16[560,112]{1,0:T(8,128)(2,1)S(1)}, bf16[560,112]{1,0:T(8,128)(2,1)S(1)}, u32[]{:S(2)}, u32[]{:S(2)}) collective-permute-start(bf16[560,112]{1,0:T(8,128)(2,1)S(1)} %convert_element_type.28), channel_id=1, source_target_pairs={{0,12},{4,8},{8,4},{12,0},{1,13},{5,9},{9,5},{13,1},{2,14},{6,10},... | collective-permute-start | bytes 376328 | tf_op jit(solution)/shard_map/ppermute | solution.py:156
  85.1 8.6 %collective-permute-start.14 = (bf16[560,112]{1,0:T(8,128)(2,1)S(1)}, bf16[560,112]{1,0:T(8,128)(2,1)S(1)}, u32[]{:S(2)}, u32[]{:S(2)}) collective-permute-start(bf16[560,112]{1,0:T(8,128)(2,1)S(1)} %convert_element_type.28), channel_id=1, source_target_pairs={{0,8},{4,12},{8,0},{12,4},{1,9},{5,13},{9,1},{13,5},{2,10},{6,14},... | collective-permute-start | bytes 376328 | tf_op jit(solution)/shard_map/ppermute | solution.py:156
  85.6 8.1 %collective-permute-start.15 = (bf16[560,112]{1,0:T(8,128)(2,1)S(1)}, bf16[560,112]{1,0:T(8,128)(2,1)S(1)}, u32[]{:S(2)}, u32[]{:S(2)}) collective-permute-start(bf16[560,112]{1,0:T(8,128)(2,1)S(1)} %convert_element_type.28), channel_id=1, source_target_pairs={{0,4},{4,0},{8,12},{12,8},{1,5},{5,1},{9,13},{13,9},{2,6},{6,2},{1... | collective-permute-start | bytes 376328 | tf_op jit(solution)/shard_map/ppermute | solution.py:156

commit v13 on v11

--- a/solution.py
+++ b/solution.py
@@ -56,7 +56,8 @@
         pltpu.make_async_copy(at(flip), at(flip), sems.at[flip]).wait()
 
 
-def partial_kernel(stream, place, own, near, b2i, b2o, wq, wk, wv, tie, sums, whole, sems):
+def partial_kernel(stream, place, own, near, b2i, b2o, wq, wk, wv, sums, query_sums, token, whole, sems):
+    token[...] = jnp.zeros_like(token)
     rows, tokens = b2i.shape
     missing = pl.ds(pl.multiple_of((place[0] ^ 3) * rows, 16), rows)
     whole[missing, :] = jnp.zeros((rows, tokens), whole.dtype)
@@ -67,8 +68,9 @@
     def _(tile):
         columns = pl.ds(pl.multiple_of(tile * width, width), width)
         block = whole[:, columns]
-        for k, matrix in enumerate((wk, wv, wq)):
+        for k, matrix in enumerate((wk, wv)):
             sums[k, :, columns] = rounded_dot(matrix[...], block)
+        query_sums[:, columns] = rounded_dot(wq[...], block)
 
 
 def cut_kernel(count, place, *rest):
@@ -108,7 +110,7 @@
 
 def query_kernel(place, inner_ref, end_ref, cut, sums, tie, query):
     def body(block):
-        row = (sums[2] + rounded_dot(cut[2], block[...])).astype(jnp.bfloat16)
+        row = (sums[...] + rounded_dot(cut[2], block[...])).astype(jnp.bfloat16)
         query[...] = jnp.maximum(row, 0)
 
     on_last(place, inner_ref, end_ref, body)
@@ -201,24 +203,32 @@
     out_type = jax.ShapeDtypeStruct((2, width, tokens), jnp.bfloat16)
 
     read_scratch = [pltpu.VMEM((width, tokens), jnp.bfloat16), pltpu.SemaphoreType.DMA((width // HEAD_DIM,))]
-    sums = []
-    for stream in range(2):
-        ready, *_ = lax.optimization_barrier((far[stream], across_end[stream], *sums))
+    partial_types = (
+        jax.ShapeDtypeStruct((2, width, tokens), jnp.float32),
+        jax.ShapeDtypeStruct((width, tokens), jnp.float32),
+        jax.ShapeDtypeStruct((8, 128), jnp.float32),
+    )
+    sums, query_sums, done = [], [], []
+    for stream in range(2):
+        ready, *_ = lax.optimization_barrier((far[stream], across_end[stream], *done))
         far_end.append(partner_swap(ready, "head"))
-        sums.append(call(
-            functools.partial(partial_kernel, stream), jax.ShapeDtypeStruct((3, width, tokens), jnp.float32), IN_VMEM,
-            [IN_SMEM] + [ANYWHERE] * 4 + [IN_VMEM] * 3 + [ANYWHERE], [whole, sems], 3 * one,
-        )(place, columns, near, far[stream], across_end[stream], *matrices, cut))
+        key_value, query, token = call(
+            functools.partial(partial_kernel, stream), partial_types, (IN_VMEM,) * 3,
+            [IN_SMEM] + [ANYWHERE] * 4 + [IN_VMEM] * 3, [whole, sems], 3 * one,
+        )(place, columns, near, far[stream], across_end[stream], *matrices)
+        sums.append(key_value)
+        query_sums.append(query)
+        done.append(token)
     queries, query, clean = [], None, None
     for stream in range(2):
-        ties = (sums[1],) if stream == 0 else (clean, query)
+        ties = (done[1],) if stream == 0 else (clean, query)
         state = call(
             state_kernel, state_type, IN_VMEM,
             [IN_SMEM] + [IN_VMEM] * 4 + [ANYWHERE] * len(ties), [], one // 2,
         )(place, across[stream], far_end[stream], cut, sums[stream], *ties)
         query = call(
             query_kernel, query_type, IN_VMEM, [IN_SMEM] + [IN_VMEM] * 4 + [ANYWHERE], [], one // 4,
-        )(place, across[stream], far_end[stream], cut, sums[stream], state)
+        )(place, across[stream], far_end[stream], cut, query_sums[stream], state)
         queries.append(query)
         if stream == 0:
             query, *got = lax.optimization_barrier((query, *from_others(state, "tok")))

time: 95.1 us -> 99.7 us (1.048)
  waiting for transfers between devices: 21.6 us -> 23.9 us
  local copies, waits for them, and re-layouts: 10.5 us -> 12.6 us
    ppermute x5, waiting for transfers between devices: 11.8 us -> 14.1 us  [partner_swap(): lax.ppermute(value, axis, [(i, i ^ 1) for i in range(lax.axis_size(axis))])]
    unnamed x16 -> x20, local copies, waits for them, and re-layouts: 7.17 us -> 9.26 us
  transfers between devices with their start and end apart: 16 -> 16, of which waited for: 10 -> 9; matrix products, arithmetic and copies ran while one was open for 4% -> 4% of each run, Pallas kernels for 24% -> 23%
where the time goes in v13:
time: 99.7 us; the launch traced here: 99.2 us
  starting transfers between devices  38.8 us (39%)
  waiting for transfers between devices  23.9 us (24%)
  Pallas kernels  23.5 us (24%)
  local copies, waits for them, and re-layouts  12.6 us (13%)
    ppermute x5, starting transfers between devices, partner_swap(): lax.ppermute(value, axis, [(i, i ^ 1) for i in range(lax.axis_size(axis))])  31.1 us
    ppermute x5, waiting for transfers between devices, partner_swap(): lax.ppermute(value, axis, [(i, i ^ 1) for i in range(lax.axis_size(axis))])  14.1 us
    pallas_call x2, Pallas kernels, local(): call(functools.partial(partial_kernel, stream), partial_types, (IN_VMEM,)...  11.5 us
    unnamed x20, local copies, waits for them, and re-layouts  9.26 us
    ppermute x6, waiting for transfers between devices, from_others(): got.append(lax.ppermute(sent, axis, pairs))  7.39 us
    ppermute x6, starting transfers between devices, from_others(): got.append(lax.ppermute(sent, axis, pairs))  7.11 us
    pallas_call x2, Pallas kernels, local(): call(state_kernel, state_type, IN_VMEM, [IN_SMEM] + [IN_VMEM] * 4 + [ANYW...  4.89 us
    pallas_call x2, Pallas kernels, local(): call(query_kernel, query_type, IN_VMEM, [IN_SMEM] + [IN_VMEM] * 4 + [ANYW...  3.56 us
  transfers between devices with their start and end apart: 16, of which 9 were waited for; matrix products, arithmetic and copies ran while one was open for 4% of the time, Pallas kernels for 23%

profile of v13, /device:TPU:0, one launch (start us, length us, event | category | flops | bytes accessed | tf_op | source)
XLA Modules:
  0.0 99.2 jit_solution(9073236995186086229)
XLA Ops:
  0.0 3.0 %collective-permute-start.1 = (bf16[2,560,512]{2,1,0:T(8,128)(2,1)}, bf16[2,560,512]{2,1,0:T(8,128)(2,1)S(1)}, u32[]{:S(2)}, u32[]{:S(2)}) collective-permute-start(bf16[2,560,512]{2,1,0:T(8,128)(2,1)} %bitcast.24), channel_id=1, source_target_pairs={{0,1},{1,0},{2,3},{3,2},{4,5},{5,4},{6,7},{7,6},{8,9},{9,8},{10,11... | collective-permute-start | bytes 3440648 | tf_op jit(solution)/shard_map/ppermute | solution.py:135
  3.0 2.1 %slice_bitcast_fusion.1 = (bf16[560,512]{1,0:T(8,128)(2,1)S(1)}, bf16[560,512]{1,0:T(8,128)(2,1)}) fusion(bf16[2,560,512]{2,1,0:T(8,128)(2,1)} %bitcast.25), kind=kLoop, calls=%fused_computation.1 | loop fusion | bytes 2293760 | tf_op jit(solution)/shard_map/squeeze | solution.py:194
  5.7 2.4 %collective-permute-done.5.inner_ref = bf16[560,512]{1,0:T(8,128)(2,1)} collective-permute-done((bf16[560,512]{1,0:T(8,128)(2,1)S(1)}, bf16[560,512]{1,0:T(8,128)(2,1)}, u32[]{:S(2)}, u32[]{:S(2)}) %collective-permute-start.5) | collective-permute-done | bytes 573472 | tf_op jit(solution)/shard_map/ppermute | solution.py:147
  8.0 14.2 %collective-permute-start.7 = (bf16[560,512]{1,0:T(8,128)(2,1)}, bf16[560,512]{1,0:T(8,128)(2,1)}, u32[]{:S(2)}, u32[]{:S(2)}) collective-permute-start(bf16[560,512]{1,0:T(8,128)(2,1)} %collective-permute-done.5.inner_ref), channel_id=1, source_target_pairs={{0,1},{1,0},{2,3},{3,2},{4,5},{5,4},{6,7},{7,6},{8,9},{9,8},{10,11... | collective-permute-start | bytes 1720328 | tf_op jit(solution)/shard_map/ppermute | solution.py:135
  22.2 7.1 %collective-permute-done.1.near = bf16[2,560,512]{2,1,0:T(8,128)(2,1)S(1)} collective-permute-done((bf16[2,560,512]{2,1,0:T(8,128)(2,1)}, bf16[2,560,512]{2,1,0:T(8,128)(2,1)S(1)}, u32[]{:S(2)}, u32[]{:S(2)}) %collective-permute-start.1) | collective-permute-done | bytes 1146912 | tf_op jit(solution)/shard_map/ppermute | solution.py:135
  29.3 1.1 %slice_bitcast_fusion = (bf16[560,512]{1,0:T(8,128)(2,1)}, bf16[560,512]{1,0:T(8,128)(2,1)}) fusion(bf16[2,560,512]{2,1,0:T(8,128)(2,1)S(1)} %collective-permute-done.1.near), kind=kLoop, calls=%fused_computation | loop fusion | bytes 2293760 | tf_op jit(solution)/shard_map/squeeze | solution.py:196
  30.5 1.7 %copy-done = bf16[2240,560]{0,1:T(8,128)(2,1)S(1)} copy-done((bf16[2240,560]{0,1:T(8,128)(2,1)S(1)}, bf16[2240,560]{0,1:T(8,128)(2,1)}, u32[]{:S(2)}) %copy-start) | copy-done | bytes 2508824
  32.2 1.7 %copy-done.1 = bf16[2240,560]{0,1:T(8,128)(2,1)S(1)} copy-done((bf16[2240,560]{0,1:T(8,128)(2,1)S(1)}, bf16[2240,560]{0,1:T(8,128)(2,1)}, u32[]{:S(2)}) %copy-start.1) | copy-done | bytes 2508824
  34.0 1.7 %copy-done.2 = bf16[2240,560]{0,1:T(8,128)(2,1)S(1)} copy-done((bf16[2240,560]{0,1:T(8,128)(2,1)S(1)}, bf16[2240,560]{0,1:T(8,128)(2,1)}, u32[]{:S(2)}) %copy-start.2) | copy-done | bytes 2508824
  35.7 1.3 %shard_map.55.cut = bf16[3,560,560]{2,1,0:T(8,128)(2,1)S(1)} custom-call(s32[2]{0:T(128)S(1)} %pad_add_fusion.place, bf16[560,2240]{1,0:T(8,128)(2,1)S(1)} %bitcast.15, bf16[560,2240]{1,0:T(8,128)(2,1)S(1)} %bitcast.18, bf16[560,2240]{1,0:T(8,128)(2,1)S(1)} %bitcast.21), custom_call_target="tpu_custom_call" | custom-call | flops 5017600 | bytes 1024 | tf_op jit(solution)/shard_map/pallas_call | solution.py:187
  37.0 3.7 %collective-permute-start.3 = (bf16[560,512]{1,0:T(8,128)(2,1)}, bf16[560,512]{1,0:T(8,128)(2,1)S(1)}, u32[]{:S(2)}, u32[]{:S(2)}) collective-permute-start(bf16[560,512]{1,0:T(8,128)(2,1)} %collective-permute-done.inner_ref), channel_id=1, source_target_pairs={{0,1},{1,0},{2,3},{3,2},{4,5},{5,4},{6,7},{7,6},{8,9},{9,8},{10,11... | collective-permute-start | bytes 1720328 | tf_op jit(solution)/shard_map/ppermute | solution.py:135
  41.3 7.0 %collective-permute-start.8 = (bf16[560,512]{1,0:T(8,128)(2,1)}, bf16[560,512]{1,0:T(8,128)(2,1)S(1)}, u32[]{:S(2)}, u32[]{:S(2)}) collective-permute-start(bf16[560,512]{1,0:T(8,128)(2,1)} %collective-permute-done.6.b2i), channel_id=1, source_target_pairs={{0,1},{1,0},{2,3},{3,2},{4,5},{5,4},{6,7},{7,6},{8,9},{9,8},{10,11... | collective-permute-start | bytes 1720328 | tf_op jit(solution)/shard_map/ppermute | solution.py:135
  48.4 6.5 %collective-permute-done.3.b2o = bf16[560,512]{1,0:T(8,128)(2,1)S(1)} collective-permute-done((bf16[560,512]{1,0:T(8,128)(2,1)}, bf16[560,512]{1,0:T(8,128)(2,1)S(1)}, u32[]{:S(2)}, u32[]{:S(2)}) %collective-permute-start.3) | collective-permute-done | bytes 573472 | tf_op jit(solution)/shard_map/ppermute | solution.py:135
  54.8 3.1 %collective-permute-start.4 = (bf16[560,512]{1,0:T(8,128)(2,1)}, bf16[560,512]{1,0:T(8,128)(2,1)}, u32[]{:S(2)}, u32[]{:S(2)}) collective-permute-start(bf16[560,512]{1,0:T(8,128)(2,1)} %collective-permute-done.2.b2i), channel_id=1, source_target_pairs={{0,1},{1,0},{2,3},{3,2},{4,5},{5,4},{6,7},{7,6},{8,9},{9,8},{10,11... | collective-permute-start | bytes 1720328 | tf_op jit(solution)/shard_map/ppermute | solution.py:135
  58.0 5.3 %shard_map.56 = (f32[2,560,512]{2,1,0:T(8,128)S(1)}, f32[560,512]{1,0:T(8,128)S(1)}, f32[8,128]{1,0:T(8,128)S(1)}) custom-call(s32[2]{0:T(128)S(1)} %pad_add_fusion.place, bf16[2,560,512]{2,1,0:T(8,128)(2,1)S(1)} %bitcast.26, bf16[2,560,512]{2,1,0:T(8,128)(2,1)S(1)} %collective-permute-done.1.near, bf16[560,512]{1,0:T(8,128)(2,1)} %collective-permute-done.2.b2i, ...), custom_call_target="tpu_custom_call" | custom-call | flops 60211200 | bytes 1024 | tf_op jit(solution)/shard_map/pallas_call | solution.py:215
  63.3 1.4 %copy-done.4 = f32[2,560,512]{2,1,0:T(8,128)} copy-done((f32[2,560,512]{2,1,0:T(8,128)}, f32[2,560,512]{2,1,0:T(8,128)S(1)}, u32[]{:S(2)}) %copy-start.4) | copy-done | bytes 2293784
  64.7 1.0 %copy-done.6 = f32[560,512]{1,0:T(8,128)} copy-done((f32[560,512]{1,0:T(8,128)}, f32[560,512]{1,0:T(8,128)S(1)}, u32[]{:S(2)}) %copy-start.6) | copy-done | bytes 1146904
  65.7 6.2 %shard_map.57 = (f32[2,560,512]{2,1,0:T(8,128)S(1)}, f32[560,512]{1,0:T(8,128)S(1)}, f32[8,128]{1,0:T(8,128)}) custom-call(s32[2]{0:T(128)S(1)} %pad_add_fusion.place, bf16[2,560,512]{2,1,0:T(8,128)(2,1)S(1)} %bitcast.27, bf16[2,560,512]{2,1,0:T(8,128)(2,1)S(1)} %collective-permute-done.1.near, bf16[560,512]{1,0:T(8,128)(2,1)} %collective-permute-done.6.b2i, ...), custom_call_target="tpu_custom_call" | custom-call | flops 60211200 | bytes 1024 | tf_op jit(solution)/shard_map/pallas_call | solution.py:215
  71.9 2.3 %shard_map.58.tie = f32[560,112]{1,0:T(8,128)S(1)} custom-call(s32[2]{0:T(128)S(1)} %pad_add_fusion.place, bf16[560,512]{1,0:T(8,128)(2,1)} %collective-permute-done.5.inner_ref, bf16[560,512]{1,0:T(8,128)(2,1)S(1)} %collective-permute-done.8.end_ref, bf16[3,560,560]{2,1,0:T(8,128)(2,1)S(1)} %shard_map.55.cut, f32[2,560,512]{2,1,0:T(8,128)S(1)} %get-tuple-element.22.sums, ...), custom_call_target="tpu_custom_call" | custom-call | flops 10035200 | bytes 1024 | tf_op jit(solution)/shard_map/pallas_call | solution.py:225
  74.3 1.6 %collective-permute-start.10 = (bf16[560,112]{1,0:T(8,128)(2,1)S(1)}, bf16[560,112]{1,0:T(8,128)(2,1)S(1)}, u32[]{:S(2)}, u32[]{:S(2)}) collective-permute-start(bf16[560,112]{1,0:T(8,128)(2,1)S(1)} %convert_element_type.22), channel_id=1, source_target_pairs={{0,8},{4,12},{8,0},{12,4},{1,9},{5,13},{9,1},{13,5},{2,10},{6,14},... | collective-permute-start | bytes 376328 | tf_op jit(solution)/shard_map/ppermute | solution.py:158
  75.9 1.5 %collective-permute-start.11 = (bf16[560,112]{1,0:T(8,128)(2,1)S(1)}, bf16[560,112]{1,0:T(8,128)(2,1)S(1)}, u32[]{:S(2)}, u32[]{:S(2)}) collective-permute-start(bf16[560,112]{1,0:T(8,128)(2,1)S(1)} %convert_element_type.22), channel_id=1, source_target_pairs={{0,4},{4,0},{8,12},{12,8},{1,5},{5,1},{9,13},{13,9},{2,6},{6,2},{1... | collective-permute-start | bytes 376328 | tf_op jit(solution)/shard_map/ppermute | solution.py:158
  77.8 1.7 %shard_map.59.rest_1_.query = bf16[560,512]{1,0:T(8,128)(2,1)S(1)} custom-call(s32[2]{0:T(128)S(1)} %pad_add_fusion.place, bf16[560,512]{1,0:T(8,128)(2,1)} %collective-permute-done.5.inner_ref, bf16[560,512]{1,0:T(8,128)(2,1)S(1)} %collective-permute-done.8.end_ref, bf16[3,560,560]{2,1,0:T(8,128)(2,1)S(1)} %shard_map.55.cut, ...), custom_call_target="tpu_custom_call" | custom-call | flops 5017600 | bytes 1024 | tf_op jit(solution)/shard_map/pallas_call | solution.py:229
  81.0 2.4 %collective-permute-done.9 = bf16[560,112]{1,0:T(8,128)(2,1)S(1)} collective-permute-done((bf16[560,112]{1,0:T(8,128)(2,1)S(1)}, bf16[560,112]{1,0:T(8,128)(2,1)S(1)}, u32[]{:S(2)}, u32[]{:S(2)}) %collective-permute-start.9) | collective-permute-done | bytes 125472 | tf_op jit(solution)/shard_map/ppermute | solution.py:158
  83.7 1.6 %copy-done.5 = f32[2,560,512]{2,1,0:T(8,128)S(1)} copy-done((f32[2,560,512]{2,1,0:T(8,128)S(1)}, f32[2,560,512]{2,1,0:T(8,128)}, u32[]{:S(2)}) %copy-start.5) | copy-done | bytes 2293784
  85.3 2.6 %shard_map.60.tie.rest_1_ = f32[560,112]{1,0:T(8,128)S(1)} custom-call(s32[2]{0:T(128)S(1)} %pad_add_fusion.place, bf16[560,512]{1,0:T(8,128)(2,1)} %collective-permute-done.inner_ref, bf16[560,512]{1,0:T(8,128)(2,1)} %collective-permute-done.4.end_ref, bf16[3,560,560]{2,1,0:T(8,128)(2,1)S(1)} %shard_map.55.cut, f32[2,560,512]{2,1,0:T(8,128)S(1)} %copy-done.5, ...), custom_call_target="tpu_custom_call" | custom-call | flops 10035200 | bytes 1024 | tf_op jit(solution)/shard_map/pallas_call | solution.py:225
  87.9 1.6 %collective-permute-start.13 = (bf16[560,112]{1,0:T(8,128)(2,1)S(1)}, bf16[560,112]{1,0:T(8,128)(2,1)S(1)}, u32[]{:S(2)}, u32[]{:S(2)}) collective-permute-start(bf16[560,112]{1,0:T(8,128)(2,1)S(1)} %convert_element_type.28), channel_id=1, source_target_pairs={{0,12},{4,8},{8,4},{12,0},{1,13},{5,9},{9,5},{13,1},{2,14},{6,10},... | collective-permute-start | bytes 376328 | tf_op jit(solution)/shard_map/ppermute | solution.py:158
  90.0 1.4 %collective-permute-start.15 = (bf16[560,112]{1,0:T(8,128)(2,1)S(1)}, bf16[560,112]{1,0:T(8,128)(2,1)S(1)}, u32[]{:S(2)}, u32[]{:S(2)}) collective-permute-start(bf16[560,112]{1,0:T(8,128)(2,1)S(1)} %convert_element_type.28), channel_id=1, source_target_pairs={{0,4},{4,0},{8,12},{12,8},{1,5},{5,1},{9,13},{13,9},{2,6},{6,2},{1... | collective-permute-start | bytes 376328 | tf_op jit(solution)/shard_map/ppermute | solution.py:158
  91.5 1.9 %shard_map.61.query = bf16[560,512]{1,0:T(8,128)(2,1)S(1)} custom-call(s32[2]{0:T(128)S(1)} %pad_add_fusion.place, bf16[560,512]{1,0:T(8,128)(2,1)} %collective-permute-done.inner_ref, bf16[560,512]{1,0:T(8,128)(2,1)} %collective-permute-done.4.end_ref, bf16[3,560,560]{2,1,0:T(8,128)(2,1)S(1)} %shard_map.55.cut, f32[560,512]{1,0:T(8,128)S(1)} %copy-done.7, ...), custom_call_target="tpu_custom_call" | custom-call | flops 5017600 | bytes 1024 | tf_op jit(solution)/shard_map/pallas_call | solution.py:229
  93.4 1.1 %shard_map.62.rest_5_ = bf16[2,560,512]{2,1,0:T(8,128)(2,1)} custom-call(bf16[560,512]{1,0:T(8,128)(2,1)S(1)} %shard_map.59.rest_1_.query, f32[560,1]{1,0:T(8,128)S(1)} %reshape.5.gain, f32[560,112]{1,0:T(8,128)S(1)} %convert_select_fusion.rest_0_, f32[560,112]{1,0:T(8,128)S(1)} %get-tuple-element.30.rest_0_.rest_1_), custom_call_target="tpu_custom_call" | custom-call | flops 1003520 | bytes 1024 | tf_op jit(solution)/shard_map/pallas_call | solution.py:240
  94.5 1.0 collective-permute-done.13.rest_2_
  95.5 2.6 %collective-permute-done.14.rest_3_ = bf16[560,112]{1,0:T(8,128)(2,1)S(1)} collective-permute-done((bf16[560,112]{1,0:T(8,128)(2,1)S(1)}, bf16[560,112]{1,0:T(8,128)(2,1)S(1)}, u32[]{:S(2)}, u32[]{:S(2)}) %collective-permute-start.14) | collective-permute-done | bytes 125472 | tf_op jit(solution)/shard_map/ppermute | solution.py:158
  98.1 1.1 %shard_map.63 = bf16[2,560,512]{2,1,0:T(8,128)(2,1)} custom-call(bf16[560,512]{1,0:T(8,128)(2,1)S(1)} %shard_map.61.query, f32[560,1]{1,0:T(8,128)S(1)} %reshape.5.gain, f32[560,112]{1,0:T(8,128)S(1)} %convert_select_fusion.rest_0_, f32[560,112]{1,0:T(8,128)S(1)} %shard_map.60.tie.rest_1_, ...), custom_call_target="tpu_custom_call", output_to_operand_aliasing={{}: (7, {})} | custom-call | flops 1003520 | bytes 1024 | tf_op jit(solution)/shard_map/pallas_call | solution.py:240
  (37 shorter events, 4.0 us)
Async XLA Ops:
  0.0 29.3 %collective-permute-start.1 = (bf16[2,560,512]{2,1,0:T(8,128)(2,1)}, bf16[2,560,512]{2,1,0:T(8,128)(2,1)S(1)}, u32[]{:S(2)}, u32[]{:S(2)}) collective-permute-start(bf16[2,560,512]{2,1,0:T(8,128)(2,1)} %bitcast.24), channel_id=1, source_target_pairs={{0,1},{1,0},{2,3},{3,2},{4,5},{5,4},{6,7},{7,6},{8,9},{9,8},{10,11... | collective-permute-start | bytes 3440648 | tf_op jit(solution)/shard_map/ppermute | solution.py:135
  5.1 2.9 %collective-permute-start.5 = (bf16[560,512]{1,0:T(8,128)(2,1)S(1)}, bf16[560,512]{1,0:T(8,128)(2,1)}, u32[]{:S(2)}, u32[]{:S(2)}) collective-permute-start(bf16[560,512]{1,0:T(8,128)(2,1)S(1)} %get-tuple-element.33), channel_id=1, source_target_pairs={{0,16},{1,2},{2,1},{3,19},{16,0},{17,18},{18,17},{19,3},{4,20},{5,... | collective-permute-start | bytes 1720328 | tf_op jit(solution)/shard_map/ppermute | solution.py:147
  5.1 31.9 %collective-permute-start = (bf16[560,512]{1,0:T(8,128)(2,1)}, bf16[560,512]{1,0:T(8,128)(2,1)}, u32[]{:S(2)}, u32[]{:S(2)}) collective-permute-start(bf16[560,512]{1,0:T(8,128)(2,1)} %get-tuple-element.34), channel_id=1, source_target_pairs={{0,16},{1,2},{2,1},{3,19},{16,0},{17,18},{18,17},{19,3},{4,20},{5,... | collective-permute-start | bytes 1720328 | tf_op jit(solution)/shard_map/ppermute | solution.py:147
  8.0 33.3 %collective-permute-start.7 = (bf16[560,512]{1,0:T(8,128)(2,1)}, bf16[560,512]{1,0:T(8,128)(2,1)}, u32[]{:S(2)}, u32[]{:S(2)}) collective-permute-start(bf16[560,512]{1,0:T(8,128)(2,1)} %collective-permute-done.5.inner_ref), channel_id=1, source_target_pairs={{0,1},{1,0},{2,3},{3,2},{4,5},{5,4},{6,7},{7,6},{8,9},{9,8},{10,11... | collective-permute-start | bytes 1720328 | tf_op jit(solution)/shard_map/ppermute | solution.py:135
  30.4 10.9 %collective-permute-start.6 = (bf16[560,512]{1,0:T(8,128)(2,1)}, bf16[560,512]{1,0:T(8,128)(2,1)}, u32[]{:S(2)}, u32[]{:S(2)}) collective-permute-start(bf16[560,512]{1,0:T(8,128)(2,1)} %get-tuple-element.31), channel_id=1, source_target_pairs={{0,16},{1,2},{2,1},{3,19},{16,0},{17,18},{18,17},{19,3},{4,20},{5,... | collective-permute-start | bytes 1720328 | tf_op jit(solution)/shard_map/ppermute | solution.py:147
  30.5 1.7 %copy-start = (bf16[2240,560]{0,1:T(8,128)(2,1)S(1)}, bf16[2240,560]{0,1:T(8,128)(2,1)}, u32[]{:S(2)}) copy-start(bf16[2240,560]{0,1:T(8,128)(2,1)} %param.7) | copy-start | bytes 7526404
  32.2 1.7 %copy-start.1 = (bf16[2240,560]{0,1:T(8,128)(2,1)S(1)}, bf16[2240,560]{0,1:T(8,128)(2,1)}, u32[]{:S(2)}) copy-start(bf16[2240,560]{0,1:T(8,128)(2,1)} %param.8) | copy-start | bytes 7526404
  34.0 1.7 %copy-start.2 = (bf16[2240,560]{0,1:T(8,128)(2,1)S(1)}, bf16[2240,560]{0,1:T(8,128)(2,1)}, u32[]{:S(2)}) copy-start(bf16[2240,560]{0,1:T(8,128)(2,1)} %param.6) | copy-start | bytes 7526404
  35.7 5.0 %copy-start.8 = (bf16[560,512]{1,0:T(8,128)(2,1)S(1)}, bf16[560,512]{1,0:T(8,128)(2,1)}, u32[]{:S(2)}) copy-start(bf16[560,512]{1,0:T(8,128)(2,1)} %get-tuple-element.32) | copy-start | bytes 1720324
  35.7 22.3 %copy-start.3 = (bf16[2,512,560]{1,2,0:T(8,128)(2,1)S(1)}, bf16[2,512,560]{1,2,0:T(8,128)(2,1)}, u32[]{:S(2)}) copy-start(bf16[2,512,560]{1,2,0:T(8,128)(2,1)} %param.5) | copy-start | bytes 3440644
  37.0 17.8 %collective-permute-start.3 = (bf16[560,512]{1,0:T(8,128)(2,1)}, bf16[560,512]{1,0:T(8,128)(2,1)S(1)}, u32[]{:S(2)}, u32[]{:S(2)}) collective-permute-start(bf16[560,512]{1,0:T(8,128)(2,1)} %collective-permute-done.inner_ref), channel_id=1, source_target_pairs={{0,1},{1,0},{2,3},{3,2},{4,5},{5,4},{6,7},{7,6},{8,9},{9,8},{10,11... | collective-permute-start | bytes 1720328 | tf_op jit(solution)/shard_map/ppermute | solution.py:135
  40.7 14.1 %collective-permute-start.2 = (bf16[560,512]{1,0:T(8,128)(2,1)S(1)}, bf16[560,512]{1,0:T(8,128)(2,1)}, u32[]{:S(2)}, u32[]{:S(2)}) collective-permute-start(bf16[560,512]{1,0:T(8,128)(2,1)S(1)} %copy-done.8), channel_id=1, source_target_pairs={{0,16},{1,2},{2,1},{3,19},{16,0},{17,18},{18,17},{19,3},{4,20},{5,... | collective-permute-start | bytes 1720328 | tf_op jit(solution)/shard_map/ppermute | solution.py:147
  41.3 30.6 %collective-permute-start.8 = (bf16[560,512]{1,0:T(8,128)(2,1)}, bf16[560,512]{1,0:T(8,128)(2,1)S(1)}, u32[]{:S(2)}, u32[]{:S(2)}) collective-permute-start(bf16[560,512]{1,0:T(8,128)(2,1)} %collective-permute-done.6.b2i), channel_id=1, source_target_pairs={{0,1},{1,0},{2,3},{3,2},{4,5},{5,4},{6,7},{7,6},{8,9},{9,8},{10,11... | collective-permute-start | bytes 1720328 | tf_op jit(solution)/shard_map/ppermute | solution.py:135
  54.8 28.8 %collective-permute-start.4 = (bf16[560,512]{1,0:T(8,128)(2,1)}, bf16[560,512]{1,0:T(8,128)(2,1)}, u32[]{:S(2)}, u32[]{:S(2)}) collective-permute-start(bf16[560,512]{1,0:T(8,128)(2,1)} %collective-permute-done.2.b2i), channel_id=1, source_target_pairs={{0,1},{1,0},{2,3},{3,2},{4,5},{5,4},{6,7},{7,6},{8,9},{9,8},{10,11... | collective-permute-start | bytes 1720328 | tf_op jit(solution)/shard_map/ppermute | solution.py:135
  63.2 1.4 %copy-start.4 = (f32[2,560,512]{2,1,0:T(8,128)}, f32[2,560,512]{2,1,0:T(8,128)S(1)}, u32[]{:S(2)}) copy-start(f32[2,560,512]{2,1,0:T(8,128)S(1)} %get-tuple-element.20.sums) | copy-start | bytes 6881284
  64.7 1.0 %copy-start.6 = (f32[560,512]{1,0:T(8,128)}, f32[560,512]{1,0:T(8,128)S(1)}, u32[]{:S(2)}) copy-start(f32[560,512]{1,0:T(8,128)S(1)} %get-tuple-element.19.sums) | copy-start | bytes 3440644
  74.3 6.2 %collective-permute-start.10 = (bf16[560,112]{1,0:T(8,128)(2,1)S(1)}, bf16[560,112]{1,0:T(8,128)(2,1)S(1)}, u32[]{:S(2)}, u32[]{:S(2)}) collective-permute-start(bf16[560,112]{1,0:T(8,128)(2,1)S(1)} %convert_element_type.22), channel_id=1, source_target_pairs={{0,8},{4,12},{8,0},{12,4},{1,9},{5,13},{9,1},{13,5},{2,10},{6,14},... | collective-permute-start | bytes 376328 | tf_op jit(solution)/shard_map/ppermute | solution.py:158
  75.9 5.1 %collective-permute-start.11 = (bf16[560,112]{1,0:T(8,128)(2,1)S(1)}, bf16[560,112]{1,0:T(8,128)(2,1)S(1)}, u32[]{:S(2)}, u32[]{:S(2)}) collective-permute-start(bf16[560,112]{1,0:T(8,128)(2,1)S(1)} %convert_element_type.22), channel_id=1, source_target_pairs={{0,4},{4,0},{8,12},{12,8},{1,5},{5,1},{9,13},{13,9},{2,6},{6,2},{1... | collective-permute-start | bytes 376328 | tf_op jit(solution)/shard_map/ppermute | solution.py:158
  77.4 6.0 %collective-permute-start.9 = (bf16[560,112]{1,0:T(8,128)(2,1)S(1)}, bf16[560,112]{1,0:T(8,128)(2,1)S(1)}, u32[]{:S(2)}, u32[]{:S(2)}) collective-permute-start(bf16[560,112]{1,0:T(8,128)(2,1)S(1)} %convert_element_type.22), channel_id=1, source_target_pairs={{0,12},{4,8},{8,4},{12,0},{1,13},{5,9},{9,5},{13,1},{2,14},{6,10},... | collective-permute-start | bytes 376328 | tf_op jit(solution)/shard_map/ppermute | solution.py:158
  79.5 4.0 %copy-start.9 = (f32[560]{0:T(1024)S(1)}, f32[560]{0:T(1024)}, u32[]{:S(2)}) copy-start(f32[560]{0:T(1024)} %param.9) | copy-start | bytes 6724
  83.4 9.9 %collective-permute-start.12 = (bf16[560,112]{1,0:T(8,128)(2,1)S(1)}, bf16[560,112]{1,0:T(8,128)(2,1)S(1)}, u32[]{:S(2)}, u32[]{:S(2)}) collective-permute-start(bf16[560,112]{1,0:T(8,128)(2,1)S(1)} %get-tuple-element.29), channel_id=1, source_target_pairs={{0,16},{16,0},{1,17},{17,1},{2,18},{18,2},{3,19},{19,3},{4,20},{20... | collective-permute-start | bytes 376328 | tf_op jit(solution)/shard_map/ppermute | solution.py:166
  83.7 1.6 %copy-start.5 = (f32[2,560,512]{2,1,0:T(8,128)S(1)}, f32[2,560,512]{2,1,0:T(8,128)}, u32[]{:S(2)}) copy-start(f32[2,560,512]{2,1,0:T(8,128)} %copy-done.4) | copy-start | bytes 6881284
  85.3 6.2 %copy-start.7 = (f32[560,512]{1,0:T(8,128)S(1)}, f32[560,512]{1,0:T(8,128)}, u32[]{:S(2)}) copy-start(f32[560,512]{1,0:T(8,128)} %copy-done.6) | copy-start | bytes 3440644
  87.9 7.6 %collective-permute-start.13 = (bf16[560,112]{1,0:T(8,128)(2,1)S(1)}, bf16[560,112]{1,0:T(8,128)(2,1)S(1)}, u32[]{:S(2)}, u32[]{:S(2)}) collective-permute-start(bf16[560,112]{1,0:T(8,128)(2,1)S(1)} %convert_element_type.28), channel_id=1, source_target_pairs={{0,12},{4,8},{8,4},{12,0},{1,13},{5,9},{9,5},{13,1},{2,14},{6,10},... | collective-permute-start | bytes 376328 | tf_op jit(solution)/shard_map/ppermute | solution.py:158
  89.5 8.6 %collective-permute-start.14 = (bf16[560,112]{1,0:T(8,128)(2,1)S(1)}, bf16[560,112]{1,0:T(8,128)(2,1)S(1)}, u32[]{:S(2)}, u32[]{:S(2)}) collective-permute-start(bf16[560,112]{1,0:T(8,128)(2,1)S(1)} %convert_element_type.28), channel_id=1, source_target_pairs={{0,8},{4,12},{8,0},{12,4},{1,9},{5,13},{9,1},{13,5},{2,10},{6,14},... | collective-permute-start | bytes 376328 | tf_op jit(solution)/shard_map/ppermute | solution.py:158
  90.0 8.1 %collective-permute-start.15 = (bf16[560,112]{1,0:T(8,128)(2,1)S(1)}, bf16[560,112]{1,0:T(8,128)(2,1)S(1)}, u32[]{:S(2)}, u32[]{:S(2)}) collective-permute-start(bf16[560,112]{1,0:T(8,128)(2,1)S(1)} %convert_element_type.28), channel_id=1, source_target_pairs={{0,4},{4,0},{8,12},{12,8},{1,5},{5,1},{9,13},{13,9},{2,6},{6,2},{1... | collective-permute-start | bytes 376328 | tf_op jit(solution)/shard_map/ppermute | solution.py:158

commit v14 on v11

--- a/solution.py
+++ b/solution.py
@@ -161,8 +161,8 @@
     count, mine = lax.axis_size(axis), lax.axis_index(axis)
 
     def earlier(value, reach):
-        sent = lax.ppermute(value.astype(jnp.bfloat16), axis, [(i, (i + reach) % count) for i in range(count)])
-        return jnp.where(mine >= reach, sent.astype(jnp.float32), 0.0)
+        sent = jnp.where(mine + reach < count, value, 0.0)
+        return lax.ppermute(sent, axis, [(i, (i + reach) % count) for i in range(count)])
 
     total, reach = earlier(value, 1), 1
     while reach < count - 1:
@@ -209,9 +209,9 @@
             functools.partial(partial_kernel, stream), jax.ShapeDtypeStruct((3, width, tokens), jnp.float32), IN_VMEM,
             [IN_SMEM] + [ANYWHERE] * 4 + [IN_VMEM] * 3 + [ANYWHERE], [whole, sems], 3 * one,
         )(place, columns, near, far[stream], across_end[stream], *matrices, cut))
-    queries, query, clean = [], None, None
-    for stream in range(2):
-        ties = (sums[1],) if stream == 0 else (clean, query)
+    prefix = parts = query = out = None
+    for stream in range(2):
+        ties = (sums[1],) if stream == 0 else (parts[0], query)
         state = call(
             state_kernel, state_type, IN_VMEM,
             [IN_SMEM] + [IN_VMEM] * 4 + [ANYWHERE] * len(ties), [], one // 2,
@@ -219,19 +219,17 @@
         query = call(
             query_kernel, query_type, IN_VMEM, [IN_SMEM] + [IN_VMEM] * 4 + [ANYWHERE], [], one // 4,
         )(place, across[stream], far_end[stream], cut, sums[stream], state)
-        queries.append(query)
+        parts = [state, *from_others(state, "tok")]
         if stream == 0:
-            query, *got = lax.optimization_barrier((query, *from_others(state, "tok")))
-            clean = state + sum(part.astype(jnp.float32) for part in got)
-            prefix = entering(clean, "group")
-    out = None
-    for stream, parts in enumerate(([clean], [state, *from_others(state, "tok")])):
+            query, *parts = lax.optimization_barrier((query, *parts))
+            parts = [sum(part.astype(jnp.float32) for part in parts)]
+            prefix = entering(parts[0], "group")
         kept = [] if out is None else [out]
         out = call(
             functools.partial(read_kernel, stream, len(parts) + 1), out_type, ANYWHERE,
             [IN_VMEM] * (3 + len(parts)) + [ANYWHERE] * len(kept),
             read_scratch, one // 20, {3 + len(parts): 0} if kept else None,
-        )(queries[stream], gain_column, prefix, *parts, *kept)
+        )(query, gain_column, prefix, *parts, *kept)
     return jnp.swapaxes(out, 1, 2)
 
 

time: 95.1 us -> 93.2 us (0.980)
  waiting for transfers between devices: 21.6 us -> 18.3 us
  local copies, waits for them, and re-layouts: 10.5 us -> 11.6 us
    ppermute x6, waiting for transfers between devices: 7.41 us -> 4.08 us  [from_others(): got.append(lax.ppermute(sent, axis, pairs))]
    unnamed x16 -> x24, local copies, waits for them, and re-layouts: 7.17 us -> 8.24 us
  transfers between devices with their start and end apart: 16 -> 16, of which waited for: 10 -> 8; matrix products, arithmetic and copies ran while one was open for 4% -> 4% of each run, Pallas kernels for 24% -> 24%
where the time goes in v14:
time: 93.2 us; the launch traced here: 92.8 us
  starting transfers between devices  38.7 us (42%)
  Pallas kernels  23.7 us (25%)
  waiting for transfers between devices  18.3 us (20%)
  local copies, waits for them, and re-layouts  11.6 us (12%)
    ppermute x5, starting transfers between devices, partner_swap(): lax.ppermute(value, axis, [(i, i ^ 1) for i in range(lax.axis_size(axis))])  31 us
    ppermute x5, waiting for transfers between devices, partner_swap(): lax.ppermute(value, axis, [(i, i ^ 1) for i in range(lax.axis_size(axis))])  11.8 us
    pallas_call x2, Pallas kernels, local(): call(functools.partial(partial_kernel, stream), jax.ShapeDtypeStruct((3,...  11.5 us
    unnamed x24, local copies, waits for them, and re-layouts  8.24 us
    ppermute x6, starting transfers between devices, from_others(): got.append(lax.ppermute(sent, axis, pairs))  7.11 us
    pallas_call x2, Pallas kernels, local(): call(state_kernel, state_type, IN_VMEM, [IN_SMEM] + [IN_VMEM] * 4 + [ANYW...  4.95 us
    ppermute x6, waiting for transfers between devices, from_others(): got.append(lax.ppermute(sent, axis, pairs))  4.08 us
    pallas_call x2, Pallas kernels, local(): call(query_kernel, query_type, IN_VMEM, [IN_SMEM] + [IN_VMEM] * 4 + [ANYW...  3.71 us
  transfers between devices with their start and end apart: 16, of which 8 were waited for; matrix products, arithmetic and copies ran while one was open for 4% of the time, Pallas kernels for 24%

profile of v14, /device:TPU:0, one launch (start us, length us, event | category | flops | bytes accessed | tf_op | source)
XLA Modules:
  0.0 92.8 jit_solution(13321354990953995572)
XLA Ops:
  0.0 3.0 %collective-permute-start.1 = (bf16[2,560,512]{2,1,0:T(8,128)(2,1)}, bf16[2,560,512]{2,1,0:T(8,128)(2,1)S(1)}, u32[]{:S(2)}, u32[]{:S(2)}) collective-permute-start(bf16[2,560,512]{2,1,0:T(8,128)(2,1)} %bitcast.24), channel_id=1, source_target_pairs={{0,1},{1,0},{2,3},{3,2},{4,5},{5,4},{6,7},{7,6},{8,9},{9,8},{10,11... | collective-permute-start | bytes 3440648 | tf_op jit(solution)/shard_map/ppermute | solution.py:133
  3.0 2.1 %slice_bitcast_fusion = (bf16[560,512]{1,0:T(8,128)(2,1)S(1)}, bf16[560,512]{1,0:T(8,128)(2,1)}) fusion(bf16[2,560,512]{2,1,0:T(8,128)(2,1)} %bitcast.25), kind=kLoop, calls=%fused_computation | loop fusion | bytes 2293760 | tf_op jit(solution)/shard_map/squeeze | solution.py:192
  5.7 2.4 %collective-permute-done.5.inner_ref = bf16[560,512]{1,0:T(8,128)(2,1)} collective-permute-done((bf16[560,512]{1,0:T(8,128)(2,1)S(1)}, bf16[560,512]{1,0:T(8,128)(2,1)}, u32[]{:S(2)}, u32[]{:S(2)}) %collective-permute-start.5) | collective-permute-done | bytes 573472 | tf_op jit(solution)/shard_map/ppermute | solution.py:145
  8.0 14.2 %collective-permute-start.6 = (bf16[560,512]{1,0:T(8,128)(2,1)}, bf16[560,512]{1,0:T(8,128)(2,1)}, u32[]{:S(2)}, u32[]{:S(2)}) collective-permute-start(bf16[560,512]{1,0:T(8,128)(2,1)} %collective-permute-done.5.inner_ref), channel_id=1, source_target_pairs={{0,1},{1,0},{2,3},{3,2},{4,5},{5,4},{6,7},{7,6},{8,9},{9,8},{10,11... | collective-permute-start | bytes 1720328 | tf_op jit(solution)/shard_map/ppermute | solution.py:133
  22.2 7.1 %collective-permute-done.1.near = bf16[2,560,512]{2,1,0:T(8,128)(2,1)S(1)} collective-permute-done((bf16[2,560,512]{2,1,0:T(8,128)(2,1)}, bf16[2,560,512]{2,1,0:T(8,128)(2,1)S(1)}, u32[]{:S(2)}, u32[]{:S(2)}) %collective-permute-start.1) | collective-permute-done | bytes 1146912 | tf_op jit(solution)/shard_map/ppermute | solution.py:133
  29.3 1.1 %slice_bitcast_fusion.1 = (bf16[560,512]{1,0:T(8,128)(2,1)}, bf16[560,512]{1,0:T(8,128)(2,1)}) fusion(bf16[2,560,512]{2,1,0:T(8,128)(2,1)S(1)} %collective-permute-done.1.near), kind=kLoop, calls=%fused_computation.1 | loop fusion | bytes 2293760 | tf_op jit(solution)/shard_map/squeeze | solution.py:194
  30.5 1.7 %copy-done.4 = bf16[2240,560]{0,1:T(8,128)(2,1)S(1)} copy-done((bf16[2240,560]{0,1:T(8,128)(2,1)S(1)}, bf16[2240,560]{0,1:T(8,128)(2,1)}, u32[]{:S(2)}) %copy-start.4) | copy-done | bytes 2508824
  32.3 1.7 %copy-done.5 = bf16[2240,560]{0,1:T(8,128)(2,1)S(1)} copy-done((bf16[2240,560]{0,1:T(8,128)(2,1)S(1)}, bf16[2240,560]{0,1:T(8,128)(2,1)}, u32[]{:S(2)}) %copy-start.5) | copy-done | bytes 2508824
  34.0 1.7 %copy-done.6 = bf16[2240,560]{0,1:T(8,128)(2,1)S(1)} copy-done((bf16[2240,560]{0,1:T(8,128)(2,1)S(1)}, bf16[2240,560]{0,1:T(8,128)(2,1)}, u32[]{:S(2)}) %copy-start.6) | copy-done | bytes 2508824
  35.7 1.3 %shard_map.55.tie.cut = bf16[3,560,560]{2,1,0:T(8,128)(2,1)S(1)} custom-call(s32[2]{0:T(128)S(1)} %pad_add_fusion.place, bf16[560,2240]{1,0:T(8,128)(2,1)S(1)} %bitcast.15, bf16[560,2240]{1,0:T(8,128)(2,1)S(1)} %bitcast.18, bf16[560,2240]{1,0:T(8,128)(2,1)S(1)} %bitcast.21), custom_call_target="tpu_custom_call" | custom-call | flops 5017600 | bytes 1024 | tf_op jit(solution)/shard_map/pallas_call | solution.py:185
  37.0 3.7 %collective-permute-start.3 = (bf16[560,512]{1,0:T(8,128)(2,1)}, bf16[560,512]{1,0:T(8,128)(2,1)S(1)}, u32[]{:S(2)}, u32[]{:S(2)}) collective-permute-start(bf16[560,512]{1,0:T(8,128)(2,1)} %collective-permute-done.inner_ref), channel_id=1, source_target_pairs={{0,1},{1,0},{2,3},{3,2},{4,5},{5,4},{6,7},{7,6},{8,9},{9,8},{10,11... | collective-permute-start | bytes 1720328 | tf_op jit(solution)/shard_map/ppermute | solution.py:133
  40.8 0.5 collective-permute-done.6.b2o
  41.3 7.0 %collective-permute-start.8 = (bf16[560,512]{1,0:T(8,128)(2,1)}, bf16[560,512]{1,0:T(8,128)(2,1)S(1)}, u32[]{:S(2)}, u32[]{:S(2)}) collective-permute-start(bf16[560,512]{1,0:T(8,128)(2,1)} %collective-permute-done.4.b2i), channel_id=1, source_target_pairs={{0,1},{1,0},{2,3},{3,2},{4,5},{5,4},{6,7},{7,6},{8,9},{9,8},{10,11... | collective-permute-start | bytes 1720328 | tf_op jit(solution)/shard_map/ppermute | solution.py:133
  48.3 6.2 %shard_map.56.sums = f32[3,560,512]{2,1,0:T(8,128)S(1)} custom-call(s32[2]{0:T(128)S(1)} %pad_add_fusion.place, bf16[2,560,512]{2,1,0:T(8,128)(2,1)S(1)} %bitcast.26, bf16[2,560,512]{2,1,0:T(8,128)(2,1)S(1)} %collective-permute-done.1.near, bf16[560,512]{1,0:T(8,128)(2,1)} %collective-permute-done.4.b2i, bf16[560,512]{1,0:T(8,128)(2,1)} %collective-permute-done.6.b2o, ...), custom_call_target="tpu_custom_call" | custom-call | flops 60211200 | bytes 1024 | tf_op jit(solution)/shard_map/pallas_call | solution.py:208
  54.9 3.1 %collective-permute-start.7 = (bf16[560,512]{1,0:T(8,128)(2,1)}, bf16[560,512]{1,0:T(8,128)(2,1)}, u32[]{:S(2)}, u32[]{:S(2)}) collective-permute-start(bf16[560,512]{1,0:T(8,128)(2,1)} %collective-permute-done.2.b2i), channel_id=1, source_target_pairs={{0,1},{1,0},{2,3},{3,2},{4,5},{5,4},{6,7},{7,6},{8,9},{9,8},{10,11... | collective-permute-start | bytes 1720328 | tf_op jit(solution)/shard_map/ppermute | solution.py:133
  58.0 5.3 %shard_map.57.rest_0_.sums = f32[3,560,512]{2,1,0:T(8,128)S(1)} custom-call(s32[2]{0:T(128)S(1)} %pad_add_fusion.place, bf16[2,560,512]{2,1,0:T(8,128)(2,1)S(1)} %bitcast.27, bf16[2,560,512]{2,1,0:T(8,128)(2,1)S(1)} %collective-permute-done.1.near, bf16[560,512]{1,0:T(8,128)(2,1)} %collective-permute-done.2.b2i, ...), custom_call_target="tpu_custom_call" | custom-call | flops 60211200 | bytes 1024 | tf_op jit(solution)/shard_map/pallas_call | solution.py:208
  63.3 3.9 %collective-permute-done.8.end_ref = bf16[560,512]{1,0:T(8,128)(2,1)S(1)} collective-permute-done((bf16[560,512]{1,0:T(8,128)(2,1)}, bf16[560,512]{1,0:T(8,128)(2,1)S(1)}, u32[]{:S(2)}, u32[]{:S(2)}) %collective-permute-start.8) | collective-permute-done | bytes 573472 | tf_op jit(solution)/shard_map/ppermute | solution.py:133
  67.1 2.5 %shard_map.58.tie = f32[560,112]{1,0:T(8,128)S(1)} custom-call(s32[2]{0:T(128)S(1)} %pad_add_fusion.place, bf16[560,512]{1,0:T(8,128)(2,1)} %collective-permute-done.5.inner_ref, bf16[560,512]{1,0:T(8,128)(2,1)S(1)} %collective-permute-done.8.end_ref, bf16[3,560,560]{2,1,0:T(8,128)(2,1)S(1)} %shard_map.55.tie.cut, f32[3,560,512]{2,1,0:T(8,128)S(1)} %shard_map.56.sums, ...), custom_call_target="tpu_custom_call" | custom-call | flops 10035200 | bytes 1024 | tf_op jit(solution)/shard_map/pallas_call | solution.py:215
  69.7 1.6 %collective-permute-start.10 = (bf16[560,112]{1,0:T(8,128)(2,1)S(1)}, bf16[560,112]{1,0:T(8,128)(2,1)S(1)}, u32[]{:S(2)}, u32[]{:S(2)}) collective-permute-start(bf16[560,112]{1,0:T(8,128)(2,1)S(1)} %convert_element_type.16), channel_id=1, source_target_pairs={{0,8},{4,12},{8,0},{12,4},{1,9},{5,13},{9,1},{13,5},{2,10},{6,14},... | collective-permute-start | bytes 376328 | tf_op jit(solution)/shard_map/ppermute | solution.py:156
  71.3 1.5 %collective-permute-start.11 = (bf16[560,112]{1,0:T(8,128)(2,1)S(1)}, bf16[560,112]{1,0:T(8,128)(2,1)S(1)}, u32[]{:S(2)}, u32[]{:S(2)}) collective-permute-start(bf16[560,112]{1,0:T(8,128)(2,1)S(1)} %convert_element_type.16), channel_id=1, source_target_pairs={{0,4},{4,0},{8,12},{12,8},{1,5},{5,1},{9,13},{13,9},{2,6},{6,2},{1... | collective-permute-start | bytes 376328 | tf_op jit(solution)/shard_map/ppermute | solution.py:156
  73.2 2.0 %copy-done.3 = f32[3,560,512]{2,1,0:T(8,128)S(1)} copy-done((f32[3,560,512]{2,1,0:T(8,128)S(1)}, f32[3,560,512]{2,1,0:T(8,128)}, u32[]{:S(2)}) %copy-start.3) | copy-done | bytes 3440664
  75.2 1.1 %copy-done.9 = bf16[560,512]{1,0:T(8,128)(2,1)S(1)} copy-done((bf16[560,512]{1,0:T(8,128)(2,1)S(1)}, bf16[560,512]{1,0:T(8,128)(2,1)}, u32[]{:S(2)}) %copy-start.9) | copy-done | bytes 573464
  76.3 1.8 %shard_map.59.rest_1_.query = bf16[560,512]{1,0:T(8,128)(2,1)S(1)} custom-call(s32[2]{0:T(128)S(1)} %pad_add_fusion.place, bf16[560,512]{1,0:T(8,128)(2,1)} %collective-permute-done.5.inner_ref, bf16[560,512]{1,0:T(8,128)(2,1)S(1)} %copy-done.9, bf16[3,560,560]{2,1,0:T(8,128)(2,1)S(1)} %shard_map.55.tie.cut, f32[3,560,512]{2,1,0:T(8,128)S(1)} %copy-done.3, ...), custom_call_target="tpu_custom_call" | custom-call | flops 5017600 | bytes 1024 | tf_op jit(solution)/shard_map/pallas_call | solution.py:219
  78.1 0.6 collective-permute-done.9
  78.9 2.5 %shard_map.60.tie.rest_1_ = f32[560,112]{1,0:T(8,128)S(1)} custom-call(s32[2]{0:T(128)S(1)} %pad_add_fusion.place, bf16[560,512]{1,0:T(8,128)(2,1)} %collective-permute-done.inner_ref, bf16[560,512]{1,0:T(8,128)(2,1)} %collective-permute-done.7.end_ref, bf16[3,560,560]{2,1,0:T(8,128)(2,1)S(1)} %shard_map.55.tie.cut, f32[3,560,512]{2,1,0:T(8,128)S(1)} %copy-done.1, ...), custom_call_target="tpu_custom_call" | custom-call | flops 10035200 | bytes 1024 | tf_op jit(solution)/shard_map/pallas_call | solution.py:215
  81.4 2.0 %collective-permute-start.13 = (bf16[560,112]{1,0:T(8,128)(2,1)S(1)}, bf16[560,112]{1,0:T(8,128)(2,1)S(1)}, u32[]{:S(2)}, u32[]{:S(2)}) collective-permute-start(bf16[560,112]{1,0:T(8,128)(2,1)S(1)} %convert_element_type.20), channel_id=1, source_target_pairs={{0,12},{4,8},{8,4},{12,0},{1,13},{5,9},{9,5},{13,1},{2,14},{6,10},... | collective-permute-start | bytes 376328 | tf_op jit(solution)/shard_map/ppermute | solution.py:156
  83.9 1.1 %collective-permute-start.15 = (bf16[560,112]{1,0:T(8,128)(2,1)S(1)}, bf16[560,112]{1,0:T(8,128)(2,1)S(1)}, u32[]{:S(2)}, u32[]{:S(2)}) collective-permute-start(bf16[560,112]{1,0:T(8,128)(2,1)S(1)} %convert_element_type.20), channel_id=1, source_target_pairs={{0,4},{4,0},{8,12},{12,8},{1,5},{5,1},{9,13},{13,9},{2,6},{6,2},{1... | collective-permute-start | bytes 376328 | tf_op jit(solution)/shard_map/ppermute | solution.py:156
  85.1 1.9 %shard_map.61.query = bf16[560,512]{1,0:T(8,128)(2,1)S(1)} custom-call(s32[2]{0:T(128)S(1)} %pad_add_fusion.place, bf16[560,512]{1,0:T(8,128)(2,1)} %collective-permute-done.inner_ref, bf16[560,512]{1,0:T(8,128)(2,1)} %collective-permute-done.7.end_ref, bf16[3,560,560]{2,1,0:T(8,128)(2,1)S(1)} %shard_map.55.tie.cut, f32[3,560,512]{2,1,0:T(8,128)S(1)} %copy-done.1, ...), custom_call_target="tpu_custom_call" | custom-call | flops 5017600 | bytes 1024 | tf_op jit(solution)/shard_map/pallas_call | solution.py:219
  87.0 1.1 %shard_map.62.rest_5_ = bf16[2,560,512]{2,1,0:T(8,128)(2,1)} custom-call(bf16[560,512]{1,0:T(8,128)(2,1)S(1)} %shard_map.59.rest_1_.query, f32[560,1]{1,0:T(8,128)S(1)} %reshape.5.gain, f32[560,112]{1,0:T(8,128)S(1)} %collective-permute-done.12.rest_0_, f32[560,112]{1,0:T(8,128)S(1)} %get-tuple-element.22.rest_0_.rest_1_), custom_call_target="tpu_custom_call" | custom-call | flops 1003520 | bytes 1024 | tf_op jit(solution)/shard_map/pallas_call | solution.py:228
  88.2 0.9 collective-permute-done.13.rest_2_
  89.0 2.6 %collective-permute-done.14.rest_3_ = bf16[560,112]{1,0:T(8,128)(2,1)S(1)} collective-permute-done((bf16[560,112]{1,0:T(8,128)(2,1)S(1)}, bf16[560,112]{1,0:T(8,128)(2,1)S(1)}, u32[]{:S(2)}, u32[]{:S(2)}) %collective-permute-start.14) | collective-permute-done | bytes 125472 | tf_op jit(solution)/shard_map/ppermute | solution.py:156
  91.6 1.1 %shard_map.63 = bf16[2,560,512]{2,1,0:T(8,128)(2,1)} custom-call(bf16[560,512]{1,0:T(8,128)(2,1)S(1)} %shard_map.61.query, f32[560,1]{1,0:T(8,128)S(1)} %reshape.5.gain, f32[560,112]{1,0:T(8,128)S(1)} %collective-permute-done.12.rest_0_, f32[560,112]{1,0:T(8,128)S(1)} %shard_map.60.tie.rest_1_, ...), custom_call_target="tpu_custom_call", output_to_operand_aliasing={{}: (7, {})} | custom-call | flops 1003520 | bytes 1024 | tf_op jit(solution)/shard_map/pallas_call | solution.py:228
  (40 shorter events, 2.2 us)
Async XLA Ops:
  0.0 29.3 %collective-permute-start.1 = (bf16[2,560,512]{2,1,0:T(8,128)(2,1)}, bf16[2,560,512]{2,1,0:T(8,128)(2,1)S(1)}, u32[]{:S(2)}, u32[]{:S(2)}) collective-permute-start(bf16[2,560,512]{2,1,0:T(8,128)(2,1)} %bitcast.24), channel_id=1, source_target_pairs={{0,1},{1,0},{2,3},{3,2},{4,5},{5,4},{6,7},{7,6},{8,9},{9,8},{10,11... | collective-permute-start | bytes 3440648 | tf_op jit(solution)/shard_map/ppermute | solution.py:133
  5.1 2.9 %collective-permute-start.5 = (bf16[560,512]{1,0:T(8,128)(2,1)S(1)}, bf16[560,512]{1,0:T(8,128)(2,1)}, u32[]{:S(2)}, u32[]{:S(2)}) collective-permute-start(bf16[560,512]{1,0:T(8,128)(2,1)S(1)} %get-tuple-element.23), channel_id=1, source_target_pairs={{0,16},{1,2},{2,1},{3,19},{16,0},{17,18},{18,17},{19,3},{4,20},{5,... | collective-permute-start | bytes 1720328 | tf_op jit(solution)/shard_map/ppermute | solution.py:145
  5.1 31.9 %collective-permute-start = (bf16[560,512]{1,0:T(8,128)(2,1)}, bf16[560,512]{1,0:T(8,128)(2,1)}, u32[]{:S(2)}, u32[]{:S(2)}) collective-permute-start(bf16[560,512]{1,0:T(8,128)(2,1)} %get-tuple-element.24), channel_id=1, source_target_pairs={{0,16},{1,2},{2,1},{3,19},{16,0},{17,18},{18,17},{19,3},{4,20},{5,... | collective-permute-start | bytes 1720328 | tf_op jit(solution)/shard_map/ppermute | solution.py:145
  8.0 33.3 %collective-permute-start.6 = (bf16[560,512]{1,0:T(8,128)(2,1)}, bf16[560,512]{1,0:T(8,128)(2,1)}, u32[]{:S(2)}, u32[]{:S(2)}) collective-permute-start(bf16[560,512]{1,0:T(8,128)(2,1)} %collective-permute-done.5.inner_ref), channel_id=1, source_target_pairs={{0,1},{1,0},{2,3},{3,2},{4,5},{5,4},{6,7},{7,6},{8,9},{9,8},{10,11... | collective-permute-start | bytes 1720328 | tf_op jit(solution)/shard_map/ppermute | solution.py:133
  30.5 10.8 %collective-permute-start.4 = (bf16[560,512]{1,0:T(8,128)(2,1)}, bf16[560,512]{1,0:T(8,128)(2,1)}, u32[]{:S(2)}, u32[]{:S(2)}) collective-permute-start(bf16[560,512]{1,0:T(8,128)(2,1)} %get-tuple-element.25), channel_id=1, source_target_pairs={{0,16},{1,2},{2,1},{3,19},{16,0},{17,18},{18,17},{19,3},{4,20},{5,... | collective-permute-start | bytes 1720328 | tf_op jit(solution)/shard_map/ppermute | solution.py:145
  30.5 1.7 %copy-start.4 = (bf16[2240,560]{0,1:T(8,128)(2,1)S(1)}, bf16[2240,560]{0,1:T(8,128)(2,1)}, u32[]{:S(2)}) copy-start(bf16[2240,560]{0,1:T(8,128)(2,1)} %param.7) | copy-start | bytes 7526404
  32.3 1.7 %copy-start.5 = (bf16[2240,560]{0,1:T(8,128)(2,1)S(1)}, bf16[2240,560]{0,1:T(8,128)(2,1)}, u32[]{:S(2)}) copy-start(bf16[2240,560]{0,1:T(8,128)(2,1)} %param.8) | copy-start | bytes 7526404
  34.0 1.7 %copy-start.6 = (bf16[2240,560]{0,1:T(8,128)(2,1)S(1)}, bf16[2240,560]{0,1:T(8,128)(2,1)}, u32[]{:S(2)}) copy-start(bf16[2240,560]{0,1:T(8,128)(2,1)} %param.6) | copy-start | bytes 7526404
  35.7 5.0 %copy-start.10 = (bf16[560,512]{1,0:T(8,128)(2,1)S(1)}, bf16[560,512]{1,0:T(8,128)(2,1)}, u32[]{:S(2)}) copy-start(bf16[560,512]{1,0:T(8,128)(2,1)} %get-tuple-element.26) | copy-start | bytes 1720324
  35.7 12.6 %copy-start.7 = (bf16[2,512,560]{1,2,0:T(8,128)(2,1)S(1)}, bf16[2,512,560]{1,2,0:T(8,128)(2,1)}, u32[]{:S(2)}) copy-start(bf16[2,512,560]{1,2,0:T(8,128)(2,1)} %param.5) | copy-start | bytes 3440644
  37.0 17.8 %collective-permute-start.3 = (bf16[560,512]{1,0:T(8,128)(2,1)}, bf16[560,512]{1,0:T(8,128)(2,1)S(1)}, u32[]{:S(2)}, u32[]{:S(2)}) collective-permute-start(bf16[560,512]{1,0:T(8,128)(2,1)} %collective-permute-done.inner_ref), channel_id=1, source_target_pairs={{0,1},{1,0},{2,3},{3,2},{4,5},{5,4},{6,7},{7,6},{8,9},{9,8},{10,11... | collective-permute-start | bytes 1720328 | tf_op jit(solution)/shard_map/ppermute | solution.py:133
  40.7 14.1 %collective-permute-start.2 = (bf16[560,512]{1,0:T(8,128)(2,1)S(1)}, bf16[560,512]{1,0:T(8,128)(2,1)}, u32[]{:S(2)}, u32[]{:S(2)}) collective-permute-start(bf16[560,512]{1,0:T(8,128)(2,1)S(1)} %copy-done.10), channel_id=1, source_target_pairs={{0,16},{1,2},{2,1},{3,19},{16,0},{17,18},{18,17},{19,3},{4,20},{5,... | collective-permute-start | bytes 1720328 | tf_op jit(solution)/shard_map/ppermute | solution.py:145
  41.3 25.8 %collective-permute-start.8 = (bf16[560,512]{1,0:T(8,128)(2,1)}, bf16[560,512]{1,0:T(8,128)(2,1)S(1)}, u32[]{:S(2)}, u32[]{:S(2)}) collective-permute-start(bf16[560,512]{1,0:T(8,128)(2,1)} %collective-permute-done.4.b2i), channel_id=1, source_target_pairs={{0,1},{1,0},{2,3},{3,2},{4,5},{5,4},{6,7},{7,6},{8,9},{9,8},{10,11... | collective-permute-start | bytes 1720328 | tf_op jit(solution)/shard_map/ppermute | solution.py:133
  54.6 12.6 %copy-start.2 = (f32[3,560,512]{2,1,0:T(8,128)}, f32[3,560,512]{2,1,0:T(8,128)S(1)}, u32[]{:S(2)}) copy-start(f32[3,560,512]{2,1,0:T(8,128)S(1)} %shard_map.56.sums) | copy-start | bytes 10321924
  54.9 24.1 %collective-permute-start.7 = (bf16[560,512]{1,0:T(8,128)(2,1)}, bf16[560,512]{1,0:T(8,128)(2,1)}, u32[]{:S(2)}, u32[]{:S(2)}) collective-permute-start(bf16[560,512]{1,0:T(8,128)(2,1)} %collective-permute-done.2.b2i), channel_id=1, source_target_pairs={{0,1},{1,0},{2,3},{3,2},{4,5},{5,4},{6,7},{7,6},{8,9},{9,8},{10,11... | collective-permute-start | bytes 1720328 | tf_op jit(solution)/shard_map/ppermute | solution.py:133
  63.2 6.4 %copy-start = (f32[3,560,512]{2,1,0:T(8,128)}, f32[3,560,512]{2,1,0:T(8,128)S(1)}, u32[]{:S(2)}) copy-start(f32[3,560,512]{2,1,0:T(8,128)S(1)} %shard_map.57.rest_0_.sums) | copy-start | bytes 10321924
  67.1 2.5 %copy-start.8 = (bf16[560,512]{1,0:T(8,128)(2,1)}, bf16[560,512]{1,0:T(8,128)(2,1)S(1)}, u32[]{:S(2)}) copy-start(bf16[560,512]{1,0:T(8,128)(2,1)S(1)} %collective-permute-done.8.end_ref) | copy-start | bytes 1720324
  69.7 8.4 %collective-permute-start.10 = (bf16[560,112]{1,0:T(8,128)(2,1)S(1)}, bf16[560,112]{1,0:T(8,128)(2,1)S(1)}, u32[]{:S(2)}, u32[]{:S(2)}) collective-permute-start(bf16[560,112]{1,0:T(8,128)(2,1)S(1)} %convert_element_type.16), channel_id=1, source_target_pairs={{0,8},{4,12},{8,0},{12,4},{1,9},{5,13},{9,1},{13,5},{2,10},{6,14},... | collective-permute-start | bytes 376328 | tf_op jit(solution)/shard_map/ppermute | solution.py:156
  71.3 6.9 %collective-permute-start.11 = (bf16[560,112]{1,0:T(8,128)(2,1)S(1)}, bf16[560,112]{1,0:T(8,128)(2,1)S(1)}, u32[]{:S(2)}, u32[]{:S(2)}) collective-permute-start(bf16[560,112]{1,0:T(8,128)(2,1)S(1)} %convert_element_type.16), channel_id=1, source_target_pairs={{0,4},{4,0},{8,12},{12,8},{1,5},{5,1},{9,13},{13,9},{2,6},{6,2},{1... | collective-permute-start | bytes 376328 | tf_op jit(solution)/shard_map/ppermute | solution.py:156
  72.8 6.0 %collective-permute-start.9 = (bf16[560,112]{1,0:T(8,128)(2,1)S(1)}, bf16[560,112]{1,0:T(8,128)(2,1)S(1)}, u32[]{:S(2)}, u32[]{:S(2)}) collective-permute-start(bf16[560,112]{1,0:T(8,128)(2,1)S(1)} %convert_element_type.16), channel_id=1, source_target_pairs={{0,12},{4,8},{8,4},{12,0},{1,13},{5,9},{9,5},{13,1},{2,14},{6,10},... | collective-permute-start | bytes 376328 | tf_op jit(solution)/shard_map/ppermute | solution.py:156
  73.2 2.0 %copy-start.3 = (f32[3,560,512]{2,1,0:T(8,128)S(1)}, f32[3,560,512]{2,1,0:T(8,128)}, u32[]{:S(2)}) copy-start(f32[3,560,512]{2,1,0:T(8,128)} %copy-done.2) | copy-start | bytes 10321924
  75.2 1.1 %copy-start.9 = (bf16[560,512]{1,0:T(8,128)(2,1)S(1)}, bf16[560,512]{1,0:T(8,128)(2,1)}, u32[]{:S(2)}) copy-start(bf16[560,512]{1,0:T(8,128)(2,1)} %copy-done.8) | copy-start | bytes 1720324
  76.3 2.7 %copy-start.1 = (f32[3,560,512]{2,1,0:T(8,128)S(1)}, f32[3,560,512]{2,1,0:T(8,128)}, u32[]{:S(2)}) copy-start(f32[3,560,512]{2,1,0:T(8,128)} %copy-done) | copy-start | bytes 10321924
  78.8 8.2 %collective-permute-start.12 = (f32[560,112]{1,0:T(8,128)S(1)}, f32[560,112]{1,0:T(8,128)S(1)}, u32[]{:S(2)}, u32[]{:S(2)}) collective-permute-start(f32[560,112]{1,0:T(8,128)S(1)} %get-tuple-element.21), channel_id=1, source_target_pairs={{0,16},{16,0},{1,17},{17,1},{2,18},{18,2},{3,19},{19,3},{4,20},{20... | collective-permute-start | bytes 752648 | tf_op jit(solution)/shard_map/ppermute | solution.py:165
  78.9 6.1 %copy-start.11 = (f32[560]{0:T(1024)S(1)}, f32[560]{0:T(1024)}, u32[]{:S(2)}) copy-start(f32[560]{0:T(1024)} %param.9) | copy-start | bytes 6724
  81.4 7.6 %collective-permute-start.13 = (bf16[560,112]{1,0:T(8,128)(2,1)S(1)}, bf16[560,112]{1,0:T(8,128)(2,1)S(1)}, u32[]{:S(2)}, u32[]{:S(2)}) collective-permute-start(bf16[560,112]{1,0:T(8,128)(2,1)S(1)} %convert_element_type.20), channel_id=1, source_target_pairs={{0,12},{4,8},{8,4},{12,0},{1,13},{5,9},{9,5},{13,1},{2,14},{6,10},... | collective-permute-start | bytes 376328 | tf_op jit(solution)/shard_map/ppermute | solution.py:156
  83.4 8.2 %collective-permute-start.14 = (bf16[560,112]{1,0:T(8,128)(2,1)S(1)}, bf16[560,112]{1,0:T(8,128)(2,1)S(1)}, u32[]{:S(2)}, u32[]{:S(2)}) collective-permute-start(bf16[560,112]{1,0:T(8,128)(2,1)S(1)} %convert_element_type.20), channel_id=1, source_target_pairs={{0,8},{4,12},{8,0},{12,4},{1,9},{5,13},{9,1},{13,5},{2,10},{6,14},... | collective-permute-start | bytes 376328 | tf_op jit(solution)/shard_map/ppermute | solution.py:156
  83.9 7.7 %collective-permute-start.15 = (bf16[560,112]{1,0:T(8,128)(2,1)S(1)}, bf16[560,112]{1,0:T(8,128)(2,1)S(1)}, u32[]{:S(2)}, u32[]{:S(2)}) collective-permute-start(bf16[560,112]{1,0:T(8,128)(2,1)S(1)} %convert_element_type.20), channel_id=1, source_target_pairs={{0,4},{4,0},{8,12},{12,8},{1,5},{5,1},{9,13},{13,9},{2,6},{6,2},{1... | collective-permute-start | bytes 376328 | tf_op jit(solution)/shard_map/ppermute | solution.py:156

commit v15 on v14

--- a/solution.py
+++ b/solution.py
@@ -114,12 +114,13 @@
     on_last(place, inner_ref, end_ref, body)
 
 
-def read_kernel(stream, parts, query, gain, *rest):
+def read_kernel(stream, parts, place, query, gain, prefix, *rest):
     out, held, sems = rest[-3:]
     copies = []
     for start in range(0, query.shape[0], HEAD_DIM):
         rows = slice(start, start + HEAD_DIM)
         total = sum(part[rows, :].astype(jnp.float32) for part in rest[:parts])
+        total += jnp.where(place[2] == 1, prefix[rows, :], 0.0)
         reading = rounded_dot(total.astype(jnp.bfloat16), query[rows, :])
         scale = lax.rsqrt(jnp.mean(reading * reading, axis=0, keepdims=True) + 1e-06)
         held[rows, :] = (reading * scale * gain[rows, :]).astype(jnp.bfloat16)
@@ -161,12 +162,12 @@
     count, mine = lax.axis_size(axis), lax.axis_index(axis)
 
     def earlier(value, reach):
-        sent = jnp.where(mine + reach < count, value, 0.0)
-        return lax.ppermute(sent, axis, [(i, (i + reach) % count) for i in range(count)])
+        return lax.ppermute(value, axis, [(i, (i + reach) % count) for i in range(count)])
 
     total, reach = earlier(value, 1), 1
     while reach < count - 1:
-        total, reach = total + earlier(total, reach), 2 * reach
+        total = jnp.where(mine >= 1, total, 0.0)
+        total, reach = total + jnp.where(mine >= reach, earlier(total, reach), 0.0), 2 * reach
     return total
 
 
@@ -179,7 +180,8 @@
     matrices = (w_query.T, w_key.T, w_value.T)
     gain_column = gain.reshape(width, 1)
     inner = (mine == 1) | (mine == 2)
-    place = jnp.stack([mine.astype(jnp.int32), inner.astype(jnp.int32)])
+    later = lax.axis_index("group") > 0
+    place = jnp.stack([value.astype(jnp.int32) for value in (mine, inner, later)])
 
     one = 2 * width * depth * tokens
     cut = call(
@@ -226,10 +228,10 @@
             prefix = entering(parts[0], "group")
         kept = [] if out is None else [out]
         out = call(
-            functools.partial(read_kernel, stream, len(parts) + 1), out_type, ANYWHERE,
-            [IN_VMEM] * (3 + len(parts)) + [ANYWHERE] * len(kept),
-            read_scratch, one // 20, {3 + len(parts): 0} if kept else None,
-        )(query, gain_column, prefix, *parts, *kept)
+            functools.partial(read_kernel, stream, len(parts)), out_type, ANYWHERE,
+            [IN_SMEM] + [IN_VMEM] * (3 + len(parts)) + [ANYWHERE] * len(kept),
+            read_scratch, one // 20, {4 + len(parts): 0} if kept else None,
+        )(place, query, gain_column, prefix, *parts, *kept)
     return jnp.swapaxes(out, 1, 2)
 
 

time: 93.2 us -> 92 us (0.987)
  local copies, waits for them, and re-layouts: 11.6 us -> 7.83 us
  waiting for transfers between devices: 18.3 us -> 21.2 us
    unnamed x24 -> x16, local copies, waits for them, and re-layouts: 8.24 us -> 4.48 us
    ppermute x6, waiting for transfers between devices: 4.08 us -> 7.76 us  [from_others(): got.append(lax.ppermute(sent, axis, pairs))]
    pallas_call x2, Pallas kernels: 2.25 us -> 3.32 us  [local(): call(functools.partial(read_kernel, stream, len(parts)), out_type, ANYWHE...]
  transfers between devices with their start and end apart: 16 -> 16, of which waited for: 8 -> 9; matrix products, arithmetic and copies ran while one was open for 4% -> 4% of each run, Pallas kernels for 24% -> 23%
where the time goes in v15:
time: 92 us; the launch traced here: 91.7 us
  starting transfers between devices  39.3 us (43%)
  Pallas kernels  23 us (25%)
  waiting for transfers between devices  21.2 us (23%)
  local copies, waits for them, and re-layouts  7.83 us (9%)
    ppermute x5, starting transfers between devices, partner_swap(): lax.ppermute(value, axis, [(i, i ^ 1) for i in range(lax.axis_size(axis))])  31.6 us
    pallas_call x2, Pallas kernels, local(): call(functools.partial(partial_kernel, stream), jax.ShapeDtypeStruct((3,...  11.5 us
    ppermute x5, waiting for transfers between devices, partner_swap(): lax.ppermute(value, axis, [(i, i ^ 1) for i in range(lax.axis_size(axis))])  11 us
    ppermute x6, waiting for transfers between devices, from_others(): got.append(lax.ppermute(sent, axis, pairs))  7.76 us
    ppermute x6, starting transfers between devices, from_others(): got.append(lax.ppermute(sent, axis, pairs))  7.11 us
    unnamed x16, local copies, waits for them, and re-layouts  4.48 us
    pallas_call x2, Pallas kernels, local(): call(state_kernel, state_type, IN_VMEM, [IN_SMEM] + [IN_VMEM] * 4 + [ANYW...  4.05 us
    pallas_call x2, Pallas kernels, local(): call(functools.partial(read_kernel, stream, len(parts)), out_type, ANYWHE...  3.32 us
  transfers between devices with their start and end apart: 16, of which 9 were waited for; matrix products, arithmetic and copies ran while one was open for 4% of the time, Pallas kernels for 23%

profile of v15, /device:TPU:0, one launch (start us, length us, event | category | flops | bytes accessed | tf_op | source)
XLA Modules:
  0.0 91.7 jit_solution(15464137793243373317)
XLA Ops:
  0.0 3.0 %collective-permute-start.1 = (bf16[2,560,512]{2,1,0:T(8,128)(2,1)}, bf16[2,560,512]{2,1,0:T(8,128)(2,1)S(1)}, u32[]{:S(2)}, u32[]{:S(2)}) collective-permute-start(bf16[2,560,512]{2,1,0:T(8,128)(2,1)} %bitcast.25), channel_id=1, source_target_pairs={{0,1},{1,0},{2,3},{3,2},{4,5},{5,4},{6,7},{7,6},{8,9},{9,8},{10,11... | collective-permute-start | bytes 3440648 | tf_op jit(solution)/shard_map/ppermute | solution.py:134
  3.0 2.1 %slice_bitcast_fusion = (bf16[560,512]{1,0:T(8,128)(2,1)S(1)}, bf16[560,512]{1,0:T(8,128)(2,1)}) fusion(bf16[2,560,512]{2,1,0:T(8,128)(2,1)} %bitcast.26), kind=kLoop, calls=%fused_computation | loop fusion | bytes 2293760 | tf_op jit(solution)/shard_map/squeeze | solution.py:194
  5.7 2.4 %collective-permute-done.5.inner_ref = bf16[560,512]{1,0:T(8,128)(2,1)} collective-permute-done((bf16[560,512]{1,0:T(8,128)(2,1)S(1)}, bf16[560,512]{1,0:T(8,128)(2,1)}, u32[]{:S(2)}, u32[]{:S(2)}) %collective-permute-start.5) | collective-permute-done | bytes 573472 | tf_op jit(solution)/shard_map/ppermute | solution.py:146
  8.0 14.2 %collective-permute-start.6 = (bf16[560,512]{1,0:T(8,128)(2,1)}, bf16[560,512]{1,0:T(8,128)(2,1)}, u32[]{:S(2)}, u32[]{:S(2)}) collective-permute-start(bf16[560,512]{1,0:T(8,128)(2,1)} %collective-permute-done.5.inner_ref), channel_id=1, source_target_pairs={{0,1},{1,0},{2,3},{3,2},{4,5},{5,4},{6,7},{7,6},{8,9},{9,8},{10,11... | collective-permute-start | bytes 1720328 | tf_op jit(solution)/shard_map/ppermute | solution.py:134
  22.2 7.1 %collective-permute-done.1.near = bf16[2,560,512]{2,1,0:T(8,128)(2,1)S(1)} collective-permute-done((bf16[2,560,512]{2,1,0:T(8,128)(2,1)}, bf16[2,560,512]{2,1,0:T(8,128)(2,1)S(1)}, u32[]{:S(2)}, u32[]{:S(2)}) %collective-permute-start.1) | collective-permute-done | bytes 1146912 | tf_op jit(solution)/shard_map/ppermute | solution.py:134
  29.3 1.1 %slice_bitcast_fusion.1 = (bf16[560,512]{1,0:T(8,128)(2,1)}, bf16[560,512]{1,0:T(8,128)(2,1)}) fusion(bf16[2,560,512]{2,1,0:T(8,128)(2,1)S(1)} %collective-permute-done.1.near), kind=kLoop, calls=%fused_computation.1 | loop fusion | bytes 2293760 | tf_op jit(solution)/shard_map/squeeze | solution.py:196
  30.4 1.0 %copy-done.4 = bf16[2,560,512]{2,1,0:T(8,128)(2,1)} copy-done((bf16[2,560,512]{2,1,0:T(8,128)(2,1)}, bf16[2,560,512]{2,1,0:T(8,128)(2,1)S(1)}, u32[]{:S(2)}) %copy-start.4) | copy-done | bytes 1146904
  31.5 1.7 %copy-done.1 = bf16[2240,560]{0,1:T(8,128)(2,1)S(1)} copy-done((bf16[2240,560]{0,1:T(8,128)(2,1)S(1)}, bf16[2240,560]{0,1:T(8,128)(2,1)}, u32[]{:S(2)}) %copy-start.1) | copy-done | bytes 2508824
  33.3 1.7 %copy-done.2 = bf16[2240,560]{0,1:T(8,128)(2,1)S(1)} copy-done((bf16[2240,560]{0,1:T(8,128)(2,1)S(1)}, bf16[2240,560]{0,1:T(8,128)(2,1)}, u32[]{:S(2)}) %copy-start.2) | copy-done | bytes 2508824
  35.0 1.3 %shard_map.55.tie.cut = bf16[3,560,560]{2,1,0:T(8,128)(2,1)S(1)} custom-call(s32[3]{0:T(128)S(1)} %pad_add_fusion.place, bf16[560,2240]{1,0:T(8,128)(2,1)S(1)} %bitcast.16, bf16[560,2240]{1,0:T(8,128)(2,1)S(1)} %bitcast.19, bf16[560,2240]{1,0:T(8,128)(2,1)S(1)} %bitcast.22), custom_call_target="tpu_custom_call" | custom-call | flops 5017600 | bytes 1024 | tf_op jit(solution)/shard_map/pallas_call | solution.py:187
  36.3 3.7 %collective-permute-start.3 = (bf16[560,512]{1,0:T(8,128)(2,1)S(1)}, bf16[560,512]{1,0:T(8,128)(2,1)S(1)}, u32[]{:S(2)}, u32[]{:S(2)}) collective-permute-start(bf16[560,512]{1,0:T(8,128)(2,1)S(1)} %collective-permute-done.inner_ref), channel_id=1, source_target_pairs={{0,1},{1,0},{2,3},{3,2},{4,5},{5,4},{6,7},{7,6},{8,9},{9,8},{10,11... | collective-permute-start | bytes 1720328 | tf_op jit(solution)/shard_map/ppermute | solution.py:134
  40.0 1.7 %collective-permute-done.6.b2o = bf16[560,512]{1,0:T(8,128)(2,1)} collective-permute-done((bf16[560,512]{1,0:T(8,128)(2,1)}, bf16[560,512]{1,0:T(8,128)(2,1)}, u32[]{:S(2)}, u32[]{:S(2)}) %collective-permute-start.6) | collective-permute-done | bytes 573472 | tf_op jit(solution)/shard_map/ppermute | solution.py:134
  41.7 8.0 %collective-permute-start.8 = (bf16[560,512]{1,0:T(8,128)(2,1)}, bf16[560,512]{1,0:T(8,128)(2,1)S(1)}, u32[]{:S(2)}, u32[]{:S(2)}) collective-permute-start(bf16[560,512]{1,0:T(8,128)(2,1)} %collective-permute-done.4.b2i), channel_id=1, source_target_pairs={{0,1},{1,0},{2,3},{3,2},{4,5},{5,4},{6,7},{7,6},{8,9},{9,8},{10,11... | collective-permute-start | bytes 1720328 | tf_op jit(solution)/shard_map/ppermute | solution.py:134
  49.7 6.2 %shard_map.56.sums = f32[3,560,512]{2,1,0:T(8,128)S(1)} custom-call(s32[3]{0:T(128)S(1)} %pad_add_fusion.place, bf16[2,560,512]{2,1,0:T(8,128)(2,1)S(1)} %bitcast.27, bf16[2,560,512]{2,1,0:T(8,128)(2,1)S(1)} %copy-done.5, bf16[560,512]{1,0:T(8,128)(2,1)} %collective-permute-done.4.b2i, bf16[560,512]{1,0:T(8,128)(2,1)} %collective-permute-done.6.b2o, ...), custom_call_target="tpu_custom_call" | custom-call | flops 60211200 | bytes 1024 | tf_op jit(solution)/shard_map/pallas_call | solution.py:210
  56.0 2.7 %collective-permute-start.7 = (bf16[560,512]{1,0:T(8,128)(2,1)S(1)}, bf16[560,512]{1,0:T(8,128)(2,1)S(1)}, u32[]{:S(2)}, u32[]{:S(2)}) collective-permute-start(bf16[560,512]{1,0:T(8,128)(2,1)S(1)} %collective-permute-done.2.b2i), channel_id=1, source_target_pairs={{0,1},{1,0},{2,3},{3,2},{4,5},{5,4},{6,7},{7,6},{8,9},{9,8},{10,11... | collective-permute-start | bytes 1720328 | tf_op jit(solution)/shard_map/ppermute | solution.py:134
  58.7 5.3 %shard_map.57.rest_0_.sums = f32[3,560,512]{2,1,0:T(8,128)S(1)} custom-call(s32[3]{0:T(128)S(1)} %pad_add_fusion.place, bf16[2,560,512]{2,1,0:T(8,128)(2,1)S(1)} %bitcast.28, bf16[2,560,512]{2,1,0:T(8,128)(2,1)S(1)} %copy-done.5, bf16[560,512]{1,0:T(8,128)(2,1)S(1)} %collective-permute-done.2.b2i, bf16[560,512]{1,0:T(8,128)(2,1)S(1)} %collective-permute-done.3.b2o, ...), custom_call_target="tpu_custom_call" | custom-call | flops 60211200 | bytes 1024 | tf_op jit(solution)/shard_map/pallas_call | solution.py:210
  64.0 2.2 %collective-permute-done.8.end_ref = bf16[560,512]{1,0:T(8,128)(2,1)S(1)} collective-permute-done((bf16[560,512]{1,0:T(8,128)(2,1)}, bf16[560,512]{1,0:T(8,128)(2,1)S(1)}, u32[]{:S(2)}, u32[]{:S(2)}) %collective-permute-start.8) | collective-permute-done | bytes 573472 | tf_op jit(solution)/shard_map/ppermute | solution.py:134
  66.2 2.3 %shard_map.58.tie = f32[560,112]{1,0:T(8,128)S(1)} custom-call(s32[3]{0:T(128)S(1)} %pad_add_fusion.place, bf16[560,512]{1,0:T(8,128)(2,1)} %collective-permute-done.5.inner_ref, bf16[560,512]{1,0:T(8,128)(2,1)S(1)} %collective-permute-done.8.end_ref, bf16[3,560,560]{2,1,0:T(8,128)(2,1)S(1)} %shard_map.55.tie.cut, f32[3,560,512]{2,1,0:T(8,128)S(1)} %shard_map.56.sums, ...), custom_call_target="tpu_custom_call" | custom-call | flops 10035200 | bytes 1024 | tf_op jit(solution)/shard_map/pallas_call | solution.py:217
  68.5 1.9 %collective-permute-start.10 = (bf16[560,112]{1,0:T(8,128)(2,1)S(1)}, bf16[560,112]{1,0:T(8,128)(2,1)S(1)}, u32[]{:S(2)}, u32[]{:S(2)}) collective-permute-start(bf16[560,112]{1,0:T(8,128)(2,1)S(1)} %convert_element_type.17), channel_id=1, source_target_pairs={{0,8},{4,12},{8,0},{12,4},{1,9},{5,13},{9,1},{13,5},{2,10},{6,14},... | collective-permute-start | bytes 376328 | tf_op jit(solution)/shard_map/ppermute | solution.py:157
  70.4 1.5 %collective-permute-start.11 = (bf16[560,112]{1,0:T(8,128)(2,1)S(1)}, bf16[560,112]{1,0:T(8,128)(2,1)S(1)}, u32[]{:S(2)}, u32[]{:S(2)}) collective-permute-start(bf16[560,112]{1,0:T(8,128)(2,1)S(1)} %convert_element_type.17), channel_id=1, source_target_pairs={{0,4},{4,0},{8,12},{12,8},{1,5},{5,1},{9,13},{13,9},{2,6},{6,2},{1... | collective-permute-start | bytes 376328 | tf_op jit(solution)/shard_map/ppermute | solution.py:157
  72.1 1.7 %shard_map.59.rest_1_.query = bf16[560,512]{1,0:T(8,128)(2,1)S(1)} custom-call(s32[3]{0:T(128)S(1)} %pad_add_fusion.place, bf16[560,512]{1,0:T(8,128)(2,1)} %collective-permute-done.5.inner_ref, bf16[560,512]{1,0:T(8,128)(2,1)S(1)} %collective-permute-done.8.end_ref, bf16[3,560,560]{2,1,0:T(8,128)(2,1)S(1)} %shard_map.55.tie.cut, ...), custom_call_target="tpu_custom_call" | custom-call | flops 5017600 | bytes 1024 | tf_op jit(solution)/shard_map/pallas_call | solution.py:221
  73.8 1.1 %collective-permute-done.10 = bf16[560,112]{1,0:T(8,128)(2,1)S(1)} collective-permute-done((bf16[560,112]{1,0:T(8,128)(2,1)S(1)}, bf16[560,112]{1,0:T(8,128)(2,1)S(1)}, u32[]{:S(2)}, u32[]{:S(2)}) %collective-permute-start.10) | collective-permute-done | bytes 125472 | tf_op jit(solution)/shard_map/ppermute | solution.py:157
  74.8 0.7 collective-permute-done.11
  75.6 2.3 %collective-permute-done.9 = bf16[560,112]{1,0:T(8,128)(2,1)S(1)} collective-permute-done((bf16[560,112]{1,0:T(8,128)(2,1)S(1)}, bf16[560,112]{1,0:T(8,128)(2,1)S(1)}, u32[]{:S(2)}, u32[]{:S(2)}) %collective-permute-start.9) | collective-permute-done | bytes 125472 | tf_op jit(solution)/shard_map/ppermute | solution.py:157
  78.1 1.7 %shard_map.60.tie.rest_0_ = f32[560,112]{1,0:T(8,128)S(1)} custom-call(s32[3]{0:T(128)S(1)} %pad_add_fusion.place, bf16[560,512]{1,0:T(8,128)(2,1)S(1)} %collective-permute-done.inner_ref, bf16[560,512]{1,0:T(8,128)(2,1)S(1)} %collective-permute-done.7.end_ref, bf16[3,560,560]{2,1,0:T(8,128)(2,1)S(1)} %shard_map.55.tie.cut, ...), custom_call_target="tpu_custom_call" | custom-call | flops 10035200 | bytes 1024 | tf_op jit(solution)/shard_map/pallas_call | solution.py:217
  79.8 2.3 %collective-permute-start.13 = (bf16[560,112]{1,0:T(8,128)(2,1)S(1)}, bf16[560,112]{1,0:T(8,128)(2,1)S(1)}, u32[]{:S(2)}, u32[]{:S(2)}) collective-permute-start(bf16[560,112]{1,0:T(8,128)(2,1)S(1)} %convert_element_type.21), channel_id=1, source_target_pairs={{0,12},{4,8},{8,4},{12,0},{1,13},{5,9},{9,5},{13,1},{2,14},{6,10},... | collective-permute-start | bytes 376328 | tf_op jit(solution)/shard_map/ppermute | solution.py:157
  82.6 0.8 collective-permute-start.15
  83.5 1.2 %shard_map.61.query = bf16[560,512]{1,0:T(8,128)(2,1)S(1)} custom-call(s32[3]{0:T(128)S(1)} %pad_add_fusion.place, bf16[560,512]{1,0:T(8,128)(2,1)S(1)} %collective-permute-done.inner_ref, bf16[560,512]{1,0:T(8,128)(2,1)S(1)} %collective-permute-done.7.end_ref, bf16[3,560,560]{2,1,0:T(8,128)(2,1)S(1)} %shard_map.55.tie.cut, ...), custom_call_target="tpu_custom_call" | custom-call | flops 5017600 | bytes 1024 | tf_op jit(solution)/shard_map/pallas_call | solution.py:221
  84.7 1.6 %shard_map.62.rest_4_ = bf16[2,560,512]{2,1,0:T(8,128)(2,1)} custom-call(s32[3]{0:T(128)S(1)} %pad_add_fusion.place, bf16[560,512]{1,0:T(8,128)(2,1)S(1)} %shard_map.59.rest_1_.query, f32[560,1]{1,0:T(8,128)S(1)} %reshape.6.gain, f32[560,112]{1,0:T(8,128)S(1)} %collective-permute-done.12.prefix, f32[560,112]{1,0:T(8,128)S(1)} %convert_add_fusion.rest_0_), custom_call_target="tpu_custom_call" | custom-call | flops 1003520 | bytes 1024 | tf_op jit(solution)/shard_map/pallas_call | solution.py:230
  86.4 1.0 %collective-permute-done.13.rest_1_ = bf16[560,112]{1,0:T(8,128)(2,1)S(1)} collective-permute-done((bf16[560,112]{1,0:T(8,128)(2,1)S(1)}, bf16[560,112]{1,0:T(8,128)(2,1)S(1)}, u32[]{:S(2)}, u32[]{:S(2)}) %collective-permute-start.13) | collective-permute-done | bytes 125472 | tf_op jit(solution)/shard_map/ppermute | solution.py:157
  87.4 2.6 %collective-permute-done.14.rest_2_ = bf16[560,112]{1,0:T(8,128)(2,1)S(1)} collective-permute-done((bf16[560,112]{1,0:T(8,128)(2,1)S(1)}, bf16[560,112]{1,0:T(8,128)(2,1)S(1)}, u32[]{:S(2)}, u32[]{:S(2)}) %collective-permute-start.14) | collective-permute-done | bytes 125472 | tf_op jit(solution)/shard_map/ppermute | solution.py:157
  90.0 1.7 %shard_map.63 = bf16[2,560,512]{2,1,0:T(8,128)(2,1)} custom-call(s32[3]{0:T(128)S(1)} %pad_add_fusion.place, bf16[560,512]{1,0:T(8,128)(2,1)S(1)} %shard_map.61.query, f32[560,1]{1,0:T(8,128)S(1)} %reshape.6.gain, f32[560,112]{1,0:T(8,128)S(1)} %collective-permute-done.12.prefix, ...), custom_call_target="tpu_custom_call", output_to_operand_aliasing={{}: (8, {})} | custom-call | flops 1003520 | bytes 1024 | tf_op jit(solution)/shard_map/pallas_call | solution.py:230
  (32 shorter events, 1.6 us)
Async XLA Ops:
  0.0 31.5 %copy-start = (bf16[2240,560]{0,1:T(8,128)(2,1)S(1)}, bf16[2240,560]{0,1:T(8,128)(2,1)}, u32[]{:S(2)}) copy-start(bf16[2240,560]{0,1:T(8,128)(2,1)} %param.7) | copy-start | bytes 7526404
  0.0 29.3 %collective-permute-start.1 = (bf16[2,560,512]{2,1,0:T(8,128)(2,1)}, bf16[2,560,512]{2,1,0:T(8,128)(2,1)S(1)}, u32[]{:S(2)}, u32[]{:S(2)}) collective-permute-start(bf16[2,560,512]{2,1,0:T(8,128)(2,1)} %bitcast.25), channel_id=1, source_target_pairs={{0,1},{1,0},{2,3},{3,2},{4,5},{5,4},{6,7},{7,6},{8,9},{9,8},{10,11... | collective-permute-start | bytes 3440648 | tf_op jit(solution)/shard_map/ppermute | solution.py:134
  5.1 2.9 %collective-permute-start.5 = (bf16[560,512]{1,0:T(8,128)(2,1)S(1)}, bf16[560,512]{1,0:T(8,128)(2,1)}, u32[]{:S(2)}, u32[]{:S(2)}) collective-permute-start(bf16[560,512]{1,0:T(8,128)(2,1)S(1)} %get-tuple-element.21), channel_id=1, source_target_pairs={{0,16},{1,2},{2,1},{3,19},{16,0},{17,18},{18,17},{19,3},{4,20},{5,... | collective-permute-start | bytes 1720328 | tf_op jit(solution)/shard_map/ppermute | solution.py:146
  5.1 31.1 %collective-permute-start = (bf16[560,512]{1,0:T(8,128)(2,1)}, bf16[560,512]{1,0:T(8,128)(2,1)S(1)}, u32[]{:S(2)}, u32[]{:S(2)}) collective-permute-start(bf16[560,512]{1,0:T(8,128)(2,1)} %get-tuple-element.22), channel_id=1, source_target_pairs={{0,16},{1,2},{2,1},{3,19},{16,0},{17,18},{18,17},{19,3},{4,20},{5,... | collective-permute-start | bytes 1720328 | tf_op jit(solution)/shard_map/ppermute | solution.py:146
  8.0 33.7 %collective-permute-start.6 = (bf16[560,512]{1,0:T(8,128)(2,1)}, bf16[560,512]{1,0:T(8,128)(2,1)}, u32[]{:S(2)}, u32[]{:S(2)}) collective-permute-start(bf16[560,512]{1,0:T(8,128)(2,1)} %collective-permute-done.5.inner_ref), channel_id=1, source_target_pairs={{0,1},{1,0},{2,3},{3,2},{4,5},{5,4},{6,7},{7,6},{8,9},{9,8},{10,11... | collective-permute-start | bytes 1720328 | tf_op jit(solution)/shard_map/ppermute | solution.py:134
  30.4 1.0 %copy-start.4 = (bf16[2,560,512]{2,1,0:T(8,128)(2,1)}, bf16[2,560,512]{2,1,0:T(8,128)(2,1)S(1)}, u32[]{:S(2)}) copy-start(bf16[2,560,512]{2,1,0:T(8,128)(2,1)S(1)} %collective-permute-done.1.near) | copy-start | bytes 3440644
  31.4 10.3 %collective-permute-start.4 = (bf16[560,512]{1,0:T(8,128)(2,1)}, bf16[560,512]{1,0:T(8,128)(2,1)}, u32[]{:S(2)}, u32[]{:S(2)}) collective-permute-start(bf16[560,512]{1,0:T(8,128)(2,1)} %get-tuple-element.23), channel_id=1, source_target_pairs={{0,16},{1,2},{2,1},{3,19},{16,0},{17,18},{18,17},{19,3},{4,20},{5,... | collective-permute-start | bytes 1720328 | tf_op jit(solution)/shard_map/ppermute | solution.py:146
  31.5 1.7 %copy-start.1 = (bf16[2240,560]{0,1:T(8,128)(2,1)S(1)}, bf16[2240,560]{0,1:T(8,128)(2,1)}, u32[]{:S(2)}) copy-start(bf16[2240,560]{0,1:T(8,128)(2,1)} %param.8) | copy-start | bytes 7526404
  33.2 1.7 %copy-start.2 = (bf16[2240,560]{0,1:T(8,128)(2,1)S(1)}, bf16[2240,560]{0,1:T(8,128)(2,1)}, u32[]{:S(2)}) copy-start(bf16[2240,560]{0,1:T(8,128)(2,1)} %param.6) | copy-start | bytes 7526404
  35.0 5.0 %copy-start.6 = (bf16[560,512]{1,0:T(8,128)(2,1)S(1)}, bf16[560,512]{1,0:T(8,128)(2,1)}, u32[]{:S(2)}) copy-start(bf16[560,512]{1,0:T(8,128)(2,1)} %get-tuple-element.24) | copy-start | bytes 1720324
  35.0 14.7 %copy-start.3 = (bf16[2,512,560]{1,2,0:T(8,128)(2,1)S(1)}, bf16[2,512,560]{1,2,0:T(8,128)(2,1)}, u32[]{:S(2)}) copy-start(bf16[2,512,560]{1,2,0:T(8,128)(2,1)} %param.5) | copy-start | bytes 3440644
  35.0 14.8 %copy-start.5 = (bf16[2,560,512]{2,1,0:T(8,128)(2,1)S(1)}, bf16[2,560,512]{2,1,0:T(8,128)(2,1)}, u32[]{:S(2)}) copy-start(bf16[2,560,512]{2,1,0:T(8,128)(2,1)} %copy-done.4) | copy-start | bytes 3440644
  36.3 19.7 %collective-permute-start.3 = (bf16[560,512]{1,0:T(8,128)(2,1)S(1)}, bf16[560,512]{1,0:T(8,128)(2,1)S(1)}, u32[]{:S(2)}, u32[]{:S(2)}) collective-permute-start(bf16[560,512]{1,0:T(8,128)(2,1)S(1)} %collective-permute-done.inner_ref), channel_id=1, source_target_pairs={{0,1},{1,0},{2,3},{3,2},{4,5},{5,4},{6,7},{7,6},{8,9},{9,8},{10,11... | collective-permute-start | bytes 1720328 | tf_op jit(solution)/shard_map/ppermute | solution.py:134
  40.0 16.0 %collective-permute-start.2 = (bf16[560,512]{1,0:T(8,128)(2,1)S(1)}, bf16[560,512]{1,0:T(8,128)(2,1)S(1)}, u32[]{:S(2)}, u32[]{:S(2)}) collective-permute-start(bf16[560,512]{1,0:T(8,128)(2,1)S(1)} %copy-done.6), channel_id=1, source_target_pairs={{0,16},{1,2},{2,1},{3,19},{16,0},{17,18},{18,17},{19,3},{4,20},{5,... | collective-permute-start | bytes 1720328 | tf_op jit(solution)/shard_map/ppermute | solution.py:146
  41.7 24.5 %collective-permute-start.8 = (bf16[560,512]{1,0:T(8,128)(2,1)}, bf16[560,512]{1,0:T(8,128)(2,1)S(1)}, u32[]{:S(2)}, u32[]{:S(2)}) collective-permute-start(bf16[560,512]{1,0:T(8,128)(2,1)} %collective-permute-done.4.b2i), channel_id=1, source_target_pairs={{0,1},{1,0},{2,3},{3,2},{4,5},{5,4},{6,7},{7,6},{8,9},{9,8},{10,11... | collective-permute-start | bytes 1720328 | tf_op jit(solution)/shard_map/ppermute | solution.py:134
  56.0 22.0 %collective-permute-start.7 = (bf16[560,512]{1,0:T(8,128)(2,1)S(1)}, bf16[560,512]{1,0:T(8,128)(2,1)S(1)}, u32[]{:S(2)}, u32[]{:S(2)}) collective-permute-start(bf16[560,512]{1,0:T(8,128)(2,1)S(1)} %collective-permute-done.2.b2i), channel_id=1, source_target_pairs={{0,1},{1,0},{2,3},{3,2},{4,5},{5,4},{6,7},{7,6},{8,9},{9,8},{10,11... | collective-permute-start | bytes 1720328 | tf_op jit(solution)/shard_map/ppermute | solution.py:134
  68.5 6.3 %collective-permute-start.10 = (bf16[560,112]{1,0:T(8,128)(2,1)S(1)}, bf16[560,112]{1,0:T(8,128)(2,1)S(1)}, u32[]{:S(2)}, u32[]{:S(2)}) collective-permute-start(bf16[560,112]{1,0:T(8,128)(2,1)S(1)} %convert_element_type.17), channel_id=1, source_target_pairs={{0,8},{4,12},{8,0},{12,4},{1,9},{5,13},{9,1},{13,5},{2,10},{6,14},... | collective-permute-start | bytes 376328 | tf_op jit(solution)/shard_map/ppermute | solution.py:157
  70.4 5.2 %collective-permute-start.11 = (bf16[560,112]{1,0:T(8,128)(2,1)S(1)}, bf16[560,112]{1,0:T(8,128)(2,1)S(1)}, u32[]{:S(2)}, u32[]{:S(2)}) collective-permute-start(bf16[560,112]{1,0:T(8,128)(2,1)S(1)} %convert_element_type.17), channel_id=1, source_target_pairs={{0,4},{4,0},{8,12},{12,8},{1,5},{5,1},{9,13},{13,9},{2,6},{6,2},{1... | collective-permute-start | bytes 376328 | tf_op jit(solution)/shard_map/ppermute | solution.py:157
  71.9 6.0 %collective-permute-start.9 = (bf16[560,112]{1,0:T(8,128)(2,1)S(1)}, bf16[560,112]{1,0:T(8,128)(2,1)S(1)}, u32[]{:S(2)}, u32[]{:S(2)}) collective-permute-start(bf16[560,112]{1,0:T(8,128)(2,1)S(1)} %convert_element_type.17), channel_id=1, source_target_pairs={{0,12},{4,8},{8,4},{12,0},{1,13},{5,9},{9,5},{13,1},{2,14},{6,10},... | collective-permute-start | bytes 376328 | tf_op jit(solution)/shard_map/ppermute | solution.py:157
  78.0 5.4 %copy-start.7 = (f32[560]{0:T(1024)S(1)}, f32[560]{0:T(1024)}, u32[]{:S(2)}) copy-start(f32[560]{0:T(1024)} %param.9) | copy-start | bytes 6724
  78.0 6.7 %collective-permute-start.12 = (f32[560,112]{1,0:T(8,128)S(1)}, f32[560,112]{1,0:T(8,128)S(1)}, u32[]{:S(2)}, u32[]{:S(2)}) collective-permute-start(f32[560,112]{1,0:T(8,128)S(1)} %convert_add_fusion.rest_0_), channel_id=1, source_target_pairs={{0,16},{16,0},{1,17},{17,1},{2,18},{18,2},{3,19},{19,3},{4,20},{20... | collective-permute-start | bytes 752648 | tf_op jit(solution)/shard_map/ppermute | solution.py:165
  79.8 7.6 %collective-permute-start.13 = (bf16[560,112]{1,0:T(8,128)(2,1)S(1)}, bf16[560,112]{1,0:T(8,128)(2,1)S(1)}, u32[]{:S(2)}, u32[]{:S(2)}) collective-permute-start(bf16[560,112]{1,0:T(8,128)(2,1)S(1)} %convert_element_type.21), channel_id=1, source_target_pairs={{0,12},{4,8},{8,4},{12,0},{1,13},{5,9},{9,5},{13,1},{2,14},{6,10},... | collective-permute-start | bytes 376328 | tf_op jit(solution)/shard_map/ppermute | solution.py:157
  82.1 7.9 %collective-permute-start.14 = (bf16[560,112]{1,0:T(8,128)(2,1)S(1)}, bf16[560,112]{1,0:T(8,128)(2,1)S(1)}, u32[]{:S(2)}, u32[]{:S(2)}) collective-permute-start(bf16[560,112]{1,0:T(8,128)(2,1)S(1)} %convert_element_type.21), channel_id=1, source_target_pairs={{0,8},{4,12},{8,0},{12,4},{1,9},{5,13},{9,1},{13,5},{2,10},{6,14},... | collective-permute-start | bytes 376328 | tf_op jit(solution)/shard_map/ppermute | solution.py:157
  82.6 7.4 %collective-permute-start.15 = (bf16[560,112]{1,0:T(8,128)(2,1)S(1)}, bf16[560,112]{1,0:T(8,128)(2,1)S(1)}, u32[]{:S(2)}, u32[]{:S(2)}) collective-permute-start(bf16[560,112]{1,0:T(8,128)(2,1)S(1)} %convert_element_type.21), channel_id=1, source_target_pairs={{0,4},{4,0},{8,12},{12,8},{1,5},{5,1},{9,13},{13,9},{2,6},{6,2},{1... | collective-permute-start | bytes 376328 | tf_op jit(solution)/shard_map/ppermute | solution.py:157

commit v16 on v14

--- a/solution.py
+++ b/solution.py
@@ -11,7 +11,6 @@
 VMEM_LIMIT = 20 * 1024 * 1024
 ANYWHERE = pl.BlockSpec(memory_space=pl.ANY)
 IN_VMEM = pl.BlockSpec(memory_space=pltpu.VMEM)
-IN_SMEM = pl.BlockSpec(memory_space=pltpu.SMEM)
 
 
 def call(body, outs, out_specs, in_specs, scratch, flops, aliases=None):
@@ -36,8 +35,12 @@
     return width, tokens // width
 
 
-def load_blocks(place, found, whole, sems):
-    mine, inner = place[0], place[1]
+def is_inner(position):
+    return (position == 1) | (position == 2)
+
+
+def load_blocks(found, whole, sems):
+    mine = lax.axis_index("head")
     rows = found[0].shape[0]
 
     def at(flip):
@@ -45,9 +48,9 @@
 
     for flip, source in enumerate(found):
         if isinstance(source, tuple):
-            for want, ref in ((1, source[0]), (0, source[1])):
-
-                @pl.when(inner == want)
+            for want, ref in ((True, source[0]), (False, source[1])):
+
+                @pl.when(is_inner(mine) == want)
                 def _(ref=ref, flip=flip):
                     pltpu.make_async_copy(ref, at(flip), sems.at[flip]).start()
         else:
@@ -56,11 +59,11 @@
         pltpu.make_async_copy(at(flip), at(flip), sems.at[flip]).wait()
 
 
-def partial_kernel(stream, place, own, near, b2i, b2o, wq, wk, wv, tie, sums, whole, sems):
+def partial_kernel(stream, own, near, b2i, b2o, wq, wk, wv, tie, sums, whole, sems):
     rows, tokens = b2i.shape
-    missing = pl.ds(pl.multiple_of((place[0] ^ 3) * rows, 16), rows)
+    missing = pl.ds(pl.multiple_of((lax.axis_index("head") ^ 3) * rows, 16), rows)
     whole[missing, :] = jnp.zeros((rows, tokens), whole.dtype)
-    load_blocks(place, [own.at[stream], near.at[stream], (b2i, b2o)], whole, sems)
+    load_blocks([own.at[stream], near.at[stream], (b2i, b2o)], whole, sems)
     width, tiles = token_tiles(tokens)
 
     @pl.loop(0, tiles)
@@ -71,26 +74,26 @@
             sums[k, :, columns] = rounded_dot(matrix[...], block)
 
 
-def cut_kernel(count, place, *rest):
+def cut_kernel(count, *rest):
     matrices, (cut,) = rest[:-1], rest[-1:]
     rows = cut.shape[2]
     for owner in range(count):
 
-        @pl.when((place[0] ^ 3) == owner)
+        @pl.when((lax.axis_index("head") ^ 3) == owner)
         def _(owner=owner):
             for k, matrix in enumerate(matrices):
                 cut[k] = matrix[:, owner * rows : (owner + 1) * rows]
 
 
-def on_last(place, inner_ref, end_ref, body):
-    for want, ref in ((1, inner_ref), (0, end_ref)):
-
-        @pl.when(place[1] == want)
+def on_last(inner_ref, end_ref, body):
+    for want, ref in ((True, inner_ref), (False, end_ref)):
+
+        @pl.when(is_inner(lax.axis_index("head")) == want)
         def _(ref=ref):
             body(ref)
 
 
-def state_kernel(place, inner_ref, end_ref, cut, sums, *rest):
+def state_kernel(inner_ref, end_ref, cut, sums, *rest):
     state = rest[-1]
 
     def body(block):
@@ -103,15 +106,15 @@
                 value[rows], key[rows], (((1,), (1,)), ((), ())), preferred_element_type=jnp.float32
             )
 
-    on_last(place, inner_ref, end_ref, body)
-
-
-def query_kernel(place, inner_ref, end_ref, cut, sums, tie, query):
+    on_last(inner_ref, end_ref, body)
+
+
+def query_kernel(inner_ref, end_ref, cut, sums, tie, query):
     def body(block):
         row = (sums[2] + rounded_dot(cut[2], block[...])).astype(jnp.bfloat16)
         query[...] = jnp.maximum(row, 0)
 
-    on_last(place, inner_ref, end_ref, body)
+    on_last(inner_ref, end_ref, body)
 
 
 def read_kernel(stream, parts, query, gain, *rest):
@@ -158,34 +161,29 @@
 
 
 def entering(value, axis):
-    count, mine = lax.axis_size(axis), lax.axis_index(axis)
-
-    def earlier(value, reach):
-        sent = jnp.where(mine + reach < count, value, 0.0)
-        return lax.ppermute(sent, axis, [(i, (i + reach) % count) for i in range(count)])
-
-    total, reach = earlier(value, 1), 1
+    count = lax.axis_size(axis)
+    total = lax.ppermute(value, axis, [(i, i + 1) for i in range(count - 1)])
+    reach = 1
     while reach < count - 1:
-        total, reach = total + earlier(total, reach), 2 * reach
+        total = total + lax.ppermute(total, axis, [(i, i + reach) for i in range(count - reach)])
+        reach *= 2
     return total
 
 
 def local(streams, w_query, w_key, w_value, gain):
-    count, mine = lax.axis_size("head"), lax.axis_index("head")
+    count = lax.axis_size("head")
     rows, tokens = streams.shape[2], streams.shape[1]
     width = w_query.shape[1]
     depth = rows * count
     columns = jnp.swapaxes(streams, 1, 2)
     matrices = (w_query.T, w_key.T, w_value.T)
     gain_column = gain.reshape(width, 1)
-    inner = (mine == 1) | (mine == 2)
-    place = jnp.stack([mine.astype(jnp.int32), inner.astype(jnp.int32)])
 
     one = 2 * width * depth * tokens
     cut = call(
         functools.partial(cut_kernel, count), jax.ShapeDtypeStruct((3, width, rows), jnp.bfloat16), IN_VMEM,
-        [IN_SMEM] + [IN_VMEM] * 3, [], one // 4,
-    )(place, matrices[1], matrices[2], matrices[0])
+        [IN_VMEM] * 3, [], one // 4,
+    )(matrices[1], matrices[2], matrices[0])
     across, far, across_end, far_end = [], [], [], []
     near = partner_swap(columns, "head")
     for stream in range(2):
@@ -207,18 +205,18 @@
         far_end.append(partner_swap(ready, "head"))
         sums.append(call(
             functools.partial(partial_kernel, stream), jax.ShapeDtypeStruct((3, width, tokens), jnp.float32), IN_VMEM,
-            [IN_SMEM] + [ANYWHERE] * 4 + [IN_VMEM] * 3 + [ANYWHERE], [whole, sems], 3 * one,
-        )(place, columns, near, far[stream], across_end[stream], *matrices, cut))
+            [ANYWHERE] * 4 + [IN_VMEM] * 3 + [ANYWHERE], [whole, sems], 3 * one,
+        )(columns, near, far[stream], across_end[stream], *matrices, cut))
     prefix = parts = query = out = None
     for stream in range(2):
         ties = (sums[1],) if stream == 0 else (parts[0], query)
         state = call(
             state_kernel, state_type, IN_VMEM,
-            [IN_SMEM] + [IN_VMEM] * 4 + [ANYWHERE] * len(ties), [], one // 2,
-        )(place, across[stream], far_end[stream], cut, sums[stream], *ties)
+            [IN_VMEM] * 4 + [ANYWHERE] * len(ties), [], one // 2,
+        )(across[stream], far_end[stream], cut, sums[stream], *ties)
         query = call(
-            query_kernel, query_type, IN_VMEM, [IN_SMEM] + [IN_VMEM] * 4 + [ANYWHERE], [], one // 4,
-        )(place, across[stream], far_end[stream], cut, sums[stream], state)
+            query_kernel, query_type, IN_VMEM, [IN_VMEM] * 4 + [ANYWHERE], [], one // 4,
+        )(across[stream], far_end[stream], cut, sums[stream], state)
         parts = [state, *from_others(state, "tok")]
         if stream == 0:
             query, *parts = lax.optimization_barrier((query, *parts))

time: 93.2 us -> 89.3 us (0.958)
  waiting for transfers between devices: 18.3 us -> 27.8 us
  Pallas kernels: 23.7 us -> 16.1 us
  local copies, waits for them, and re-layouts: 11.6 us -> 4.98 us
  starting transfers between devices: 38.7 us -> 39.9 us
    ppermute x5, waiting for transfers between devices: 11.8 us -> 18.2 us  [partner_swap(): lax.ppermute(value, axis, [(i, i ^ 1) for i in range(lax.axis_size(axis))])]
    pallas_call x4, Pallas kernels: 8.67 us -> 3.67 us  [the longest x2 2.44 us: local(): call(state_kernel, state_type, IN_VMEM, [IN_VMEM] * 4 + [ANYWHERE] * len(...]
    unnamed x24 -> x12, local copies, waits for them, and re-layouts: 8.24 us -> 3.47 us
    ppermute x6, waiting for transfers between devices: 4.08 us -> 8.08 us  [from_others(): got.append(lax.ppermute(sent, axis, pairs))]
    pallas_call x2, Pallas kernels: 11.5 us -> 9.47 us  [local(): call(functools.partial(partial_kernel, stream), jax.ShapeDtypeStruct((3,...]
    ppermute x1, starting transfers between devices: 0.07 us -> 1.31 us  [entering(): total = lax.ppermute(value, axis, [(i, i + 1) for i in range(count - 1)])]
    squeeze x1, local copies, waits for them, and re-layouts: 1.14 us -> 0.07 us  [local(): far.append(middle_swap(near[stream], 'head', 'group'))]
  transfers between devices with their start and end apart: 16 -> 16, of which waited for: 8 -> 10; matrix products, arithmetic and copies ran while one was open for 4% -> 2% of each run, Pallas kernels for 24% -> 17%
where the time goes in v16:
time: 89.3 us; the launch traced here: 89 us
  starting transfers between devices  39.9 us (45%)
  waiting for transfers between devices  27.8 us (31%)
  Pallas kernels  16.1 us (18%)
  local copies, waits for them, and re-layouts  4.98 us (6%)
    ppermute x5, starting transfers between devices, partner_swap(): lax.ppermute(value, axis, [(i, i ^ 1) for i in range(lax.axis_size(axis))])  30.8 us
    ppermute x5, waiting for transfers between devices, partner_swap(): lax.ppermute(value, axis, [(i, i ^ 1) for i in range(lax.axis_size(axis))])  18.2 us
    pallas_call x2, Pallas kernels, local(): call(functools.partial(partial_kernel, stream), jax.ShapeDtypeStruct((3,...  9.47 us
    ppermute x6, waiting for transfers between devices, from_others(): got.append(lax.ppermute(sent, axis, pairs))  8.08 us
    ppermute x6, starting transfers between devices, from_others(): got.append(lax.ppermute(sent, axis, pairs))  7.17 us
    unnamed x12, local copies, waits for them, and re-layouts  3.47 us
    pallas_call x2, Pallas kernels, local(): call(state_kernel, state_type, IN_VMEM, [IN_VMEM] * 4 + [ANYWHERE] * len(...  2.44 us
    pallas_call x2, Pallas kernels, local(): call(functools.partial(read_kernel, stream, len(parts) + 1), out_type, AN...  2.27 us
  transfers between devices with their start and end apart: 16, of which 10 were waited for; matrix products, arithmetic and copies ran while one was open for 2% of the time, Pallas kernels for 17%

profile of v16, /device:TPU:0, one launch (start us, length us, event | category | flops | bytes accessed | tf_op | source)
XLA Modules:
  0.0 89.0 jit_solution(240265407482971718)
XLA Ops:
  0.0 3.0 %collective-permute-start.1 = (bf16[2,560,512]{2,1,0:T(8,128)(2,1)}, bf16[2,560,512]{2,1,0:T(8,128)(2,1)S(1)}, u32[]{:S(2)}, u32[]{:S(2)}) collective-permute-start(bf16[2,560,512]{2,1,0:T(8,128)(2,1)} %bitcast.22), channel_id=1, source_target_pairs={{0,1},{1,0},{2,3},{3,2},{4,5},{5,4},{6,7},{7,6},{8,9},{9,8},{10,11... | collective-permute-start | bytes 3440648 | tf_op jit(solution)/shard_map/ppermute | solution.py:136
  3.0 1.3 %slice_bitcast_fusion = (bf16[560,512]{1,0:T(8,128)(2,1)S(1)}, bf16[560,512]{1,0:T(8,128)(2,1)S(1)}) fusion(bf16[2,560,512]{2,1,0:T(8,128)(2,1)} %bitcast.23), kind=kLoop, calls=%fused_computation | loop fusion | bytes 2293760 | tf_op jit(solution)/shard_map/squeeze | solution.py:190
  4.9 1.5 %collective-permute-done.5.inner_ref = bf16[560,512]{1,0:T(8,128)(2,1)S(1)} collective-permute-done((bf16[560,512]{1,0:T(8,128)(2,1)S(1)}, bf16[560,512]{1,0:T(8,128)(2,1)S(1)}, u32[]{:S(2)}, u32[]{:S(2)}) %collective-permute-start.5) | collective-permute-done | bytes 573472 | tf_op jit(solution)/shard_map/ppermute | solution.py:148
  6.4 15.0 %collective-permute-start.6 = (bf16[560,512]{1,0:T(8,128)(2,1)S(1)}, bf16[560,512]{1,0:T(8,128)(2,1)S(1)}, u32[]{:S(2)}, u32[]{:S(2)}) collective-permute-start(bf16[560,512]{1,0:T(8,128)(2,1)S(1)} %collective-permute-done.5.inner_ref), channel_id=1, source_target_pairs={{0,1},{1,0},{2,3},{3,2},{4,5},{5,4},{6,7},{7,6},{8,9},{9,8},{10,11... | collective-permute-start | bytes 1720328 | tf_op jit(solution)/shard_map/ppermute | solution.py:136
  21.4 7.9 %collective-permute-done.1.near = bf16[2,560,512]{2,1,0:T(8,128)(2,1)S(1)} collective-permute-done((bf16[2,560,512]{2,1,0:T(8,128)(2,1)}, bf16[2,560,512]{2,1,0:T(8,128)(2,1)S(1)}, u32[]{:S(2)}, u32[]{:S(2)}) %collective-permute-start.1) | collective-permute-done | bytes 1146912 | tf_op jit(solution)/shard_map/ppermute | solution.py:136
  29.5 1.7 %copy-done.1 = bf16[2240,560]{0,1:T(8,128)(2,1)S(1)} copy-done((bf16[2240,560]{0,1:T(8,128)(2,1)S(1)}, bf16[2240,560]{0,1:T(8,128)(2,1)}, u32[]{:S(2)}) %copy-start.1) | copy-done | bytes 2508824
  31.2 1.7 %copy-done.3 = bf16[2240,560]{0,1:T(8,128)(2,1)S(1)} copy-done((bf16[2240,560]{0,1:T(8,128)(2,1)S(1)}, bf16[2240,560]{0,1:T(8,128)(2,1)}, u32[]{:S(2)}) %copy-start.3) | copy-done | bytes 2508824
  33.0 0.7 shard_map.55.tie.cut
  33.7 3.7 %collective-permute-start.3 = (bf16[560,512]{1,0:T(8,128)(2,1)S(1)}, bf16[560,512]{1,0:T(8,128)(2,1)S(1)}, u32[]{:S(2)}, u32[]{:S(2)}) collective-permute-start(bf16[560,512]{1,0:T(8,128)(2,1)S(1)} %collective-permute-done.inner_ref), channel_id=1, source_target_pairs={{0,1},{1,0},{2,3},{3,2},{4,5},{5,4},{6,7},{7,6},{8,9},{9,8},{10,11... | collective-permute-start | bytes 1720328 | tf_op jit(solution)/shard_map/ppermute | solution.py:136
  37.4 4.2 %collective-permute-done.6.b2o = bf16[560,512]{1,0:T(8,128)(2,1)S(1)} collective-permute-done((bf16[560,512]{1,0:T(8,128)(2,1)S(1)}, bf16[560,512]{1,0:T(8,128)(2,1)S(1)}, u32[]{:S(2)}, u32[]{:S(2)}) %collective-permute-start.6) | collective-permute-done | bytes 573472 | tf_op jit(solution)/shard_map/ppermute | solution.py:136
  41.6 5.8 %collective-permute-start.8 = (bf16[560,512]{1,0:T(8,128)(2,1)S(1)}, bf16[560,512]{1,0:T(8,128)(2,1)S(1)}, u32[]{:S(2)}, u32[]{:S(2)}) collective-permute-start(bf16[560,512]{1,0:T(8,128)(2,1)S(1)} %collective-permute-done.4.b2i), channel_id=1, source_target_pairs={{0,1},{1,0},{2,3},{3,2},{4,5},{5,4},{6,7},{7,6},{8,9},{9,8},{10,11... | collective-permute-start | bytes 1720328 | tf_op jit(solution)/shard_map/ppermute | solution.py:136
  47.5 4.7 %shard_map.56.sums = f32[3,560,512]{2,1,0:T(8,128)S(1)} custom-call(bf16[2,560,512]{2,1,0:T(8,128)(2,1)S(1)} %bitcast.24, bf16[2,560,512]{2,1,0:T(8,128)(2,1)S(1)} %collective-permute-done.1.near, bf16[560,512]{1,0:T(8,128)(2,1)S(1)} %collective-permute-done.4.b2i, bf16[560,512]{1,0:T(8,128)(2,1)S(1)} %collective-permute-done.6.b2o, ...), custom_call_target="tpu_custom_call" | custom-call | flops 60211200 | bytes 1024 | tf_op jit(solution)/shard_map/pallas_call | solution.py:206
  52.2 1.7 %collective-permute-done.3.b2o = bf16[560,512]{1,0:T(8,128)(2,1)S(1)} collective-permute-done((bf16[560,512]{1,0:T(8,128)(2,1)S(1)}, bf16[560,512]{1,0:T(8,128)(2,1)S(1)}, u32[]{:S(2)}, u32[]{:S(2)}) %collective-permute-start.3) | collective-permute-done | bytes 573472 | tf_op jit(solution)/shard_map/ppermute | solution.py:136
  53.9 3.2 %collective-permute-start.7 = (bf16[560,512]{1,0:T(8,128)(2,1)S(1)}, bf16[560,512]{1,0:T(8,128)(2,1)S(1)}, u32[]{:S(2)}, u32[]{:S(2)}) collective-permute-start(bf16[560,512]{1,0:T(8,128)(2,1)S(1)} %collective-permute-done.2.b2i), channel_id=1, source_target_pairs={{0,1},{1,0},{2,3},{3,2},{4,5},{5,4},{6,7},{7,6},{8,9},{9,8},{10,11... | collective-permute-start | bytes 1720328 | tf_op jit(solution)/shard_map/ppermute | solution.py:136
  57.1 4.7 %shard_map.57.rest_0_.sums = f32[3,560,512]{2,1,0:T(8,128)S(1)} custom-call(bf16[2,560,512]{2,1,0:T(8,128)(2,1)S(1)} %bitcast.25, bf16[2,560,512]{2,1,0:T(8,128)(2,1)S(1)} %collective-permute-done.1.near, bf16[560,512]{1,0:T(8,128)(2,1)S(1)} %collective-permute-done.2.b2i, bf16[560,512]{1,0:T(8,128)(2,1)S(1)} %collective-permute-done.3.b2o, ...), custom_call_target="tpu_custom_call" | custom-call | flops 60211200 | bytes 1024 | tf_op jit(solution)/shard_map/pallas_call | solution.py:206
  61.9 4.3 %collective-permute-done.8.end_ref = bf16[560,512]{1,0:T(8,128)(2,1)S(1)} collective-permute-done((bf16[560,512]{1,0:T(8,128)(2,1)S(1)}, bf16[560,512]{1,0:T(8,128)(2,1)S(1)}, u32[]{:S(2)}, u32[]{:S(2)}) %collective-permute-start.8) | collective-permute-done | bytes 573472 | tf_op jit(solution)/shard_map/ppermute | solution.py:136
  66.2 1.2 %shard_map.58.tie = f32[560,112]{1,0:T(8,128)S(1)} custom-call(bf16[560,512]{1,0:T(8,128)(2,1)S(1)} %collective-permute-done.5.inner_ref, bf16[560,512]{1,0:T(8,128)(2,1)S(1)} %collective-permute-done.8.end_ref, bf16[3,560,560]{2,1,0:T(8,128)(2,1)S(1)} %shard_map.55.tie.cut, f32[3,560,512]{2,1,0:T(8,128)S(1)} %shard_map.56.sums, ...), custom_call_target="tpu_custom_call" | custom-call | flops 10035200 | bytes 1024 | tf_op jit(solution)/shard_map/pallas_call | solution.py:213
  67.4 2.1 %collective-permute-start.10 = (bf16[560,112]{1,0:T(8,128)(2,1)S(1)}, bf16[560,112]{1,0:T(8,128)(2,1)S(1)}, u32[]{:S(2)}, u32[]{:S(2)}) collective-permute-start(bf16[560,112]{1,0:T(8,128)(2,1)S(1)} %convert_element_type.15), channel_id=1, source_target_pairs={{0,8},{4,12},{8,0},{12,4},{1,9},{5,13},{9,1},{13,5},{2,10},{6,14},... | collective-permute-start | bytes 376328 | tf_op jit(solution)/shard_map/ppermute | solution.py:159
  69.5 1.5 %collective-permute-start.11 = (bf16[560,112]{1,0:T(8,128)(2,1)S(1)}, bf16[560,112]{1,0:T(8,128)(2,1)S(1)}, u32[]{:S(2)}, u32[]{:S(2)}) collective-permute-start(bf16[560,112]{1,0:T(8,128)(2,1)S(1)} %convert_element_type.15), channel_id=1, source_target_pairs={{0,4},{4,0},{8,12},{12,8},{1,5},{5,1},{9,13},{13,9},{2,6},{6,2},{1... | collective-permute-start | bytes 376328 | tf_op jit(solution)/shard_map/ppermute | solution.py:159
  71.1 0.6 shard_map.59.rest_1_.query
  71.7 2.5 %collective-permute-done.10 = bf16[560,112]{1,0:T(8,128)(2,1)S(1)} collective-permute-done((bf16[560,112]{1,0:T(8,128)(2,1)S(1)}, bf16[560,112]{1,0:T(8,128)(2,1)S(1)}, u32[]{:S(2)}, u32[]{:S(2)}) %collective-permute-start.10) | collective-permute-done | bytes 125472 | tf_op jit(solution)/shard_map/ppermute | solution.py:159
  74.6 2.4 %collective-permute-done.9 = bf16[560,112]{1,0:T(8,128)(2,1)S(1)} collective-permute-done((bf16[560,112]{1,0:T(8,128)(2,1)S(1)}, bf16[560,112]{1,0:T(8,128)(2,1)S(1)}, u32[]{:S(2)}, u32[]{:S(2)}) %collective-permute-start.9) | collective-permute-done | bytes 125472 | tf_op jit(solution)/shard_map/ppermute | solution.py:159
  77.1 1.3 %collective-permute-start.12 = (f32[560,112]{1,0:T(8,128)S(1)}, f32[560,112]{1,0:T(8,128)S(1)}, u32[]{:S(2)}, u32[]{:S(2)}) collective-permute-start(f32[560,112]{1,0:T(8,128)S(1)} %convert_add_fusion.rest_0_.rest_1_), channel_id=1, source_target_pairs={{0,16},{1,17},{2,18},{3,19},{4,20},{5,21},{6,22},{7,23},{8,24},{9,... | collective-permute-start | bytes 752648 | tf_op jit(solution)/shard_map/ppermute | solution.py:165
  78.4 1.2 %shard_map.60.tie.rest_1_ = f32[560,112]{1,0:T(8,128)S(1)} custom-call(bf16[560,512]{1,0:T(8,128)(2,1)S(1)} %collective-permute-done.inner_ref, bf16[560,512]{1,0:T(8,128)(2,1)S(1)} %collective-permute-done.7.end_ref, bf16[3,560,560]{2,1,0:T(8,128)(2,1)S(1)} %shard_map.55.tie.cut, f32[3,560,512]{2,1,0:T(8,128)S(1)} %shard_map.57.rest_0_.sums, ...), custom_call_target="tpu_custom_call" | custom-call | flops 10035200 | bytes 1024 | tf_op jit(solution)/shard_map/pallas_call | solution.py:213
  79.7 1.9 %collective-permute-start.13 = (bf16[560,112]{1,0:T(8,128)(2,1)S(1)}, bf16[560,112]{1,0:T(8,128)(2,1)S(1)}, u32[]{:S(2)}, u32[]{:S(2)}) collective-permute-start(bf16[560,112]{1,0:T(8,128)(2,1)S(1)} %convert_element_type.19), channel_id=1, source_target_pairs={{0,12},{4,8},{8,4},{12,0},{1,13},{5,9},{9,5},{13,1},{2,14},{6,10},... | collective-permute-start | bytes 376328 | tf_op jit(solution)/shard_map/ppermute | solution.py:159
  81.6 0.5 collective-permute-start.14
  82.1 1.1 %collective-permute-start.15 = (bf16[560,112]{1,0:T(8,128)(2,1)S(1)}, bf16[560,112]{1,0:T(8,128)(2,1)S(1)}, u32[]{:S(2)}, u32[]{:S(2)}) collective-permute-start(bf16[560,112]{1,0:T(8,128)(2,1)S(1)} %convert_element_type.19), channel_id=1, source_target_pairs={{0,4},{4,0},{8,12},{12,8},{1,5},{5,1},{9,13},{13,9},{2,6},{6,2},{1... | collective-permute-start | bytes 376328 | tf_op jit(solution)/shard_map/ppermute | solution.py:159
  83.4 0.6 shard_map.61.query
  84.0 1.1 %shard_map.62.rest_5_ = bf16[2,560,512]{2,1,0:T(8,128)(2,1)} custom-call(bf16[560,512]{1,0:T(8,128)(2,1)S(1)} %shard_map.59.rest_1_.query, f32[560,1]{1,0:T(8,128)S(1)} %reshape.4.gain, f32[560,112]{1,0:T(8,128)S(1)} %collective-permute-done.12.rest_0_, f32[560,112]{1,0:T(8,128)S(1)} %convert_add_fusion.rest_0_.rest_1_), custom_call_target="tpu_custom_call" | custom-call | flops 1003520 | bytes 1024 | tf_op jit(solution)/shard_map/pallas_call | solution.py:226
  85.1 2.1 %collective-permute-done.13.rest_2_ = bf16[560,112]{1,0:T(8,128)(2,1)S(1)} collective-permute-done((bf16[560,112]{1,0:T(8,128)(2,1)S(1)}, bf16[560,112]{1,0:T(8,128)(2,1)S(1)}, u32[]{:S(2)}, u32[]{:S(2)}) %collective-permute-start.13) | collective-permute-done | bytes 125472 | tf_op jit(solution)/shard_map/ppermute | solution.py:159
  87.2 0.7 collective-permute-done.14.rest_3_
  87.9 1.2 %shard_map.63 = bf16[2,560,512]{2,1,0:T(8,128)(2,1)} custom-call(bf16[560,512]{1,0:T(8,128)(2,1)S(1)} %shard_map.61.query, f32[560,1]{1,0:T(8,128)S(1)} %reshape.4.gain, f32[560,112]{1,0:T(8,128)S(1)} %collective-permute-done.12.rest_0_, f32[560,112]{1,0:T(8,128)S(1)} %shard_map.60.tie.rest_1_, ...), custom_call_target="tpu_custom_call", output_to_operand_aliasing={{}: (7, {})} | custom-call | flops 1003520 | bytes 1024 | tf_op jit(solution)/shard_map/pallas_call | solution.py:226
  (27 shorter events, 1.5 us)
Async XLA Ops:
  0.0 29.5 %copy-start = (bf16[2240,560]{0,1:T(8,128)(2,1)S(1)}, bf16[2240,560]{0,1:T(8,128)(2,1)}, u32[]{:S(2)}) copy-start(bf16[2240,560]{0,1:T(8,128)(2,1)} %param.7) | copy-start | bytes 7526404
  0.0 29.3 %collective-permute-start.1 = (bf16[2,560,512]{2,1,0:T(8,128)(2,1)}, bf16[2,560,512]{2,1,0:T(8,128)(2,1)S(1)}, u32[]{:S(2)}, u32[]{:S(2)}) collective-permute-start(bf16[2,560,512]{2,1,0:T(8,128)(2,1)} %bitcast.22), channel_id=1, source_target_pairs={{0,1},{1,0},{2,3},{3,2},{4,5},{5,4},{6,7},{7,6},{8,9},{9,8},{10,11... | collective-permute-start | bytes 3440648 | tf_op jit(solution)/shard_map/ppermute | solution.py:136
  4.3 2.0 %collective-permute-start.5 = (bf16[560,512]{1,0:T(8,128)(2,1)S(1)}, bf16[560,512]{1,0:T(8,128)(2,1)S(1)}, u32[]{:S(2)}, u32[]{:S(2)}) collective-permute-start(bf16[560,512]{1,0:T(8,128)(2,1)S(1)} %get-tuple-element.21), channel_id=1, source_target_pairs={{0,16},{1,2},{2,1},{3,19},{16,0},{17,18},{18,17},{19,3},{4,20},{5,... | collective-permute-start | bytes 1720328 | tf_op jit(solution)/shard_map/ppermute | solution.py:148
  4.4 29.3 %collective-permute-start = (bf16[560,512]{1,0:T(8,128)(2,1)S(1)}, bf16[560,512]{1,0:T(8,128)(2,1)S(1)}, u32[]{:S(2)}, u32[]{:S(2)}) collective-permute-start(bf16[560,512]{1,0:T(8,128)(2,1)S(1)} %get-tuple-element.22), channel_id=1, source_target_pairs={{0,16},{1,2},{2,1},{3,19},{16,0},{17,18},{18,17},{19,3},{4,20},{5,... | collective-permute-start | bytes 1720328 | tf_op jit(solution)/shard_map/ppermute | solution.py:148
  6.4 35.2 %collective-permute-start.6 = (bf16[560,512]{1,0:T(8,128)(2,1)S(1)}, bf16[560,512]{1,0:T(8,128)(2,1)S(1)}, u32[]{:S(2)}, u32[]{:S(2)}) collective-permute-start(bf16[560,512]{1,0:T(8,128)(2,1)S(1)} %collective-permute-done.5.inner_ref), channel_id=1, source_target_pairs={{0,1},{1,0},{2,3},{3,2},{4,5},{5,4},{6,7},{7,6},{8,9},{9,8},{10,11... | collective-permute-start | bytes 1720328 | tf_op jit(solution)/shard_map/ppermute | solution.py:136
  29.4 12.2 %collective-permute-start.4 = (bf16[560,512]{1,0:T(8,128)(2,1)S(1)}, bf16[560,512]{1,0:T(8,128)(2,1)S(1)}, u32[]{:S(2)}, u32[]{:S(2)}) collective-permute-start(bf16[560,512]{1,0:T(8,128)(2,1)S(1)} %get-tuple-element.23), channel_id=1, source_target_pairs={{0,16},{1,2},{2,1},{3,19},{16,0},{17,18},{18,17},{19,3},{4,20},{5,... | collective-permute-start | bytes 1720328 | tf_op jit(solution)/shard_map/ppermute | solution.py:148
  29.5 1.7 %copy-start.1 = (bf16[2240,560]{0,1:T(8,128)(2,1)S(1)}, bf16[2240,560]{0,1:T(8,128)(2,1)}, u32[]{:S(2)}) copy-start(bf16[2240,560]{0,1:T(8,128)(2,1)} %param.8) | copy-start | bytes 7526404
  31.2 1.7 %copy-start.3 = (bf16[2240,560]{0,1:T(8,128)(2,1)S(1)}, bf16[2240,560]{0,1:T(8,128)(2,1)}, u32[]{:S(2)}) copy-start(bf16[2240,560]{0,1:T(8,128)(2,1)} %param.6) | copy-start | bytes 7526404
  33.0 14.5 %copy-start.2 = (bf16[2240,560]{0,1:T(8,128)(2,1)S(1)}, bf16[2240,560]{0,1:T(8,128)(2,1)}, u32[]{:S(2)}) copy-start(bf16[2240,560]{0,1:T(8,128)(2,1)} %param.8) | copy-start | bytes 7526404
  33.0 14.5 %copy-start.4 = (bf16[2,512,560]{1,2,0:T(8,128)(2,1)S(1)}, bf16[2,512,560]{1,2,0:T(8,128)(2,1)}, u32[]{:S(2)}) copy-start(bf16[2,512,560]{1,2,0:T(8,128)(2,1)} %param.5) | copy-start | bytes 3440644
  33.7 20.2 %collective-permute-start.3 = (bf16[560,512]{1,0:T(8,128)(2,1)S(1)}, bf16[560,512]{1,0:T(8,128)(2,1)S(1)}, u32[]{:S(2)}, u32[]{:S(2)}) collective-permute-start(bf16[560,512]{1,0:T(8,128)(2,1)S(1)} %collective-permute-done.inner_ref), channel_id=1, source_target_pairs={{0,1},{1,0},{2,3},{3,2},{4,5},{5,4},{6,7},{7,6},{8,9},{9,8},{10,11... | collective-permute-start | bytes 1720328 | tf_op jit(solution)/shard_map/ppermute | solution.py:136
  37.4 16.5 %collective-permute-start.2 = (bf16[560,512]{1,0:T(8,128)(2,1)S(1)}, bf16[560,512]{1,0:T(8,128)(2,1)S(1)}, u32[]{:S(2)}, u32[]{:S(2)}) collective-permute-start(bf16[560,512]{1,0:T(8,128)(2,1)S(1)} %get-tuple-element.24), channel_id=1, source_target_pairs={{0,16},{1,2},{2,1},{3,19},{16,0},{17,18},{18,17},{19,3},{4,20},{5,... | collective-permute-start | bytes 1720328 | tf_op jit(solution)/shard_map/ppermute | solution.py:148
  41.6 24.6 %collective-permute-start.8 = (bf16[560,512]{1,0:T(8,128)(2,1)S(1)}, bf16[560,512]{1,0:T(8,128)(2,1)S(1)}, u32[]{:S(2)}, u32[]{:S(2)}) collective-permute-start(bf16[560,512]{1,0:T(8,128)(2,1)S(1)} %collective-permute-done.4.b2i), channel_id=1, source_target_pairs={{0,1},{1,0},{2,3},{3,2},{4,5},{5,4},{6,7},{7,6},{8,9},{9,8},{10,11... | collective-permute-start | bytes 1720328 | tf_op jit(solution)/shard_map/ppermute | solution.py:136
  53.9 24.5 %collective-permute-start.7 = (bf16[560,512]{1,0:T(8,128)(2,1)S(1)}, bf16[560,512]{1,0:T(8,128)(2,1)S(1)}, u32[]{:S(2)}, u32[]{:S(2)}) collective-permute-start(bf16[560,512]{1,0:T(8,128)(2,1)S(1)} %collective-permute-done.2.b2i), channel_id=1, source_target_pairs={{0,1},{1,0},{2,3},{3,2},{4,5},{5,4},{6,7},{7,6},{8,9},{9,8},{10,11... | collective-permute-start | bytes 1720328 | tf_op jit(solution)/shard_map/ppermute | solution.py:136
  67.4 6.7 %collective-permute-start.10 = (bf16[560,112]{1,0:T(8,128)(2,1)S(1)}, bf16[560,112]{1,0:T(8,128)(2,1)S(1)}, u32[]{:S(2)}, u32[]{:S(2)}) collective-permute-start(bf16[560,112]{1,0:T(8,128)(2,1)S(1)} %convert_element_type.15), channel_id=1, source_target_pairs={{0,8},{4,12},{8,0},{12,4},{1,9},{5,13},{9,1},{13,5},{2,10},{6,14},... | collective-permute-start | bytes 376328 | tf_op jit(solution)/shard_map/ppermute | solution.py:159
  69.5 5.1 %collective-permute-start.11 = (bf16[560,112]{1,0:T(8,128)(2,1)S(1)}, bf16[560,112]{1,0:T(8,128)(2,1)S(1)}, u32[]{:S(2)}, u32[]{:S(2)}) collective-permute-start(bf16[560,112]{1,0:T(8,128)(2,1)S(1)} %convert_element_type.15), channel_id=1, source_target_pairs={{0,4},{4,0},{8,12},{12,8},{1,5},{5,1},{9,13},{13,9},{2,6},{6,2},{1... | collective-permute-start | bytes 376328 | tf_op jit(solution)/shard_map/ppermute | solution.py:159
  71.0 6.0 %collective-permute-start.9 = (bf16[560,112]{1,0:T(8,128)(2,1)S(1)}, bf16[560,112]{1,0:T(8,128)(2,1)S(1)}, u32[]{:S(2)}, u32[]{:S(2)}) collective-permute-start(bf16[560,112]{1,0:T(8,128)(2,1)S(1)} %convert_element_type.15), channel_id=1, source_target_pairs={{0,12},{4,8},{8,4},{12,0},{1,13},{5,9},{9,5},{13,1},{2,14},{6,10},... | collective-permute-start | bytes 376328 | tf_op jit(solution)/shard_map/ppermute | solution.py:159
  77.1 6.2 %copy-start.5 = (f32[560]{0:T(1024)S(1)}, f32[560]{0:T(1024)}, u32[]{:S(2)}) copy-start(f32[560]{0:T(1024)} %param.9) | copy-start | bytes 6724
  77.1 6.9 %collective-permute-start.12 = (f32[560,112]{1,0:T(8,128)S(1)}, f32[560,112]{1,0:T(8,128)S(1)}, u32[]{:S(2)}, u32[]{:S(2)}) collective-permute-start(f32[560,112]{1,0:T(8,128)S(1)} %convert_add_fusion.rest_0_.rest_1_), channel_id=1, source_target_pairs={{0,16},{1,17},{2,18},{3,19},{4,20},{5,21},{6,22},{7,23},{8,24},{9,... | collective-permute-start | bytes 752648 | tf_op jit(solution)/shard_map/ppermute | solution.py:165
  79.7 7.6 %collective-permute-start.13 = (bf16[560,112]{1,0:T(8,128)(2,1)S(1)}, bf16[560,112]{1,0:T(8,128)(2,1)S(1)}, u32[]{:S(2)}, u32[]{:S(2)}) collective-permute-start(bf16[560,112]{1,0:T(8,128)(2,1)S(1)} %convert_element_type.19), channel_id=1, source_target_pairs={{0,12},{4,8},{8,4},{12,0},{1,13},{5,9},{9,5},{13,1},{2,14},{6,10},... | collective-permute-start | bytes 376328 | tf_op jit(solution)/shard_map/ppermute | solution.py:159
  81.6 6.3 %collective-permute-start.14 = (bf16[560,112]{1,0:T(8,128)(2,1)S(1)}, bf16[560,112]{1,0:T(8,128)(2,1)S(1)}, u32[]{:S(2)}, u32[]{:S(2)}) collective-permute-start(bf16[560,112]{1,0:T(8,128)(2,1)S(1)} %convert_element_type.19), channel_id=1, source_target_pairs={{0,8},{4,12},{8,0},{12,4},{1,9},{5,13},{9,1},{13,5},{2,10},{6,14},... | collective-permute-start | bytes 376328 | tf_op jit(solution)/shard_map/ppermute | solution.py:159
  82.1 5.8 %collective-permute-start.15 = (bf16[560,112]{1,0:T(8,128)(2,1)S(1)}, bf16[560,112]{1,0:T(8,128)(2,1)S(1)}, u32[]{:S(2)}, u32[]{:S(2)}) collective-permute-start(bf16[560,112]{1,0:T(8,128)(2,1)S(1)} %convert_element_type.19), channel_id=1, source_target_pairs={{0,4},{4,0},{8,12},{12,8},{1,5},{5,1},{9,13},{13,9},{2,6},{6,2},{1... | collective-permute-start | bytes 376328 | tf_op jit(solution)/shard_map/ppermute | solution.py:159

commit v17 on v16

--- a/solution.py
+++ b/solution.py
@@ -94,7 +94,7 @@
 
 
 def state_kernel(inner_ref, end_ref, cut, sums, *rest):
-    state = rest[-1]
+    state, rounded = rest[-2:]
 
     def body(block):
         key = (sums[0] + rounded_dot(cut[0], block[...])).astype(jnp.bfloat16)
@@ -102,9 +102,11 @@
         key = jnp.maximum(key, 0)
         for start in range(0, key.shape[0], HEAD_DIM):
             rows = slice(start, start + HEAD_DIM)
-            state[rows, :] = lax.dot_general(
+            total = lax.dot_general(
                 value[rows], key[rows], (((1,), (1,)), ((), ())), preferred_element_type=jnp.float32
             )
+            state[rows, :] = total
+            rounded[rows, :] = total.astype(jnp.bfloat16)
 
     on_last(inner_ref, end_ref, body)
 
@@ -148,9 +150,8 @@
     return lax.ppermute(value, (other, axis), pairs)
 
 
-def from_others(value, axis):
+def from_others(sent, axis):
     count = lax.axis_size(axis)
-    sent = value.astype(jnp.bfloat16)
     got = []
     for step in range(count - 1, 0, -1):
         pairs = [(i, (i + step) % count) for i in range(count)]
@@ -162,11 +163,14 @@
 
 def entering(value, axis):
     count = lax.axis_size(axis)
-    total = lax.ppermute(value, axis, [(i, i + 1) for i in range(count - 1)])
-    reach = 1
+
+    def earlier(value, reach):
+        return lax.ppermute(value.astype(jnp.bfloat16), axis, [(i, i + reach) for i in range(count - reach)])
+
+    total, reach = earlier(value, 1), 1
     while reach < count - 1:
-        total = total + lax.ppermute(total, axis, [(i, i + reach) for i in range(count - reach)])
-        reach *= 2
+        total = total.astype(jnp.float32)
+        total, reach = total + earlier(total, reach).astype(jnp.float32), 2 * reach
     return total
 
 
@@ -195,7 +199,7 @@
     whole = pltpu.VMEM((depth, tokens), jnp.bfloat16)
     sems = pltpu.SemaphoreType.DMA((4,))
     query_type = jax.ShapeDtypeStruct((width, tokens), jnp.bfloat16)
-    state_type = jax.ShapeDtypeStruct((width, HEAD_DIM), jnp.float32)
+    state_types = [jax.ShapeDtypeStruct((width, HEAD_DIM), kind) for kind in (jnp.float32, jnp.bfloat16)]
     out_type = jax.ShapeDtypeStruct((2, width, tokens), jnp.bfloat16)
 
     read_scratch = [pltpu.VMEM((width, tokens), jnp.bfloat16), pltpu.SemaphoreType.DMA((width // HEAD_DIM,))]
@@ -210,14 +214,14 @@
     prefix = parts = query = out = None
     for stream in range(2):
         ties = (sums[1],) if stream == 0 else (parts[0], query)
-        state = call(
-            state_kernel, state_type, IN_VMEM,
+        state, rounded = call(
+            state_kernel, state_types, (IN_VMEM,) * 2,
             [IN_VMEM] * 4 + [ANYWHERE] * len(ties), [], one // 2,
         )(across[stream], far_end[stream], cut, sums[stream], *ties)
         query = call(
             query_kernel, query_type, IN_VMEM, [IN_VMEM] * 4 + [ANYWHERE], [], one // 4,
         )(across[stream], far_end[stream], cut, sums[stream], state)
-        parts = [state, *from_others(state, "tok")]
+        parts = [state, *from_others(rounded, "tok")]
         if stream == 0:
             query, *parts = lax.optimization_barrier((query, *parts))
             parts = [sum(part.astype(jnp.float32) for part in parts)]

time: 89.3 us -> 89.2 us (level)
  no operation moved by 1% of the time
where the time goes in v17:
time: 89.2 us; the launch traced here: 89 us
  starting transfers between devices  39.9 us (45%)
  waiting for transfers between devices  27.8 us (31%)
  Pallas kernels  16.2 us (18%)
  local copies, waits for them, and re-layouts  4.98 us (6%)
    ppermute x5, starting transfers between devices, partner_swap(): lax.ppermute(value, axis, [(i, i ^ 1) for i in range(lax.axis_size(axis))])  30.8 us
    ppermute x5, waiting for transfers between devices, partner_swap(): lax.ppermute(value, axis, [(i, i ^ 1) for i in range(lax.axis_size(axis))])  18.2 us
    pallas_call x2, Pallas kernels, local(): call(functools.partial(partial_kernel, stream), jax.ShapeDtypeStruct((3,...  9.47 us
    ppermute x6, waiting for transfers between devices, from_others(): got.append(lax.ppermute(sent, axis, pairs))  8.1 us
    ppermute x6, starting transfers between devices, from_others(): got.append(lax.ppermute(sent, axis, pairs))  7.16 us
    unnamed x12, local copies, waits for them, and re-layouts  3.47 us
    pallas_call x2, Pallas kernels, local(): call(state_kernel, state_types, (IN_VMEM,) * 2, [IN_VMEM] * 4 + [ANYWHERE...  2.45 us
    pallas_call x2, Pallas kernels, local(): call(functools.partial(read_kernel, stream, len(parts) + 1), out_type, AN...  2.27 us
  transfers between devices with their start and end apart: 16, of which 10 were waited for; matrix products, arithmetic and copies ran while one was open for 2% of the time, Pallas kernels for 17%

profile of v17, /device:TPU:0, one launch (start us, length us, event | category | flops | bytes accessed | tf_op | source)
XLA Modules:
  0.0 89.0 jit_solution(9086635812792720230)
XLA Ops:
  0.0 3.0 %collective-permute-start.1 = (bf16[2,560,512]{2,1,0:T(8,128)(2,1)}, bf16[2,560,512]{2,1,0:T(8,128)(2,1)S(1)}, u32[]{:S(2)}, u32[]{:S(2)}) collective-permute-start(bf16[2,560,512]{2,1,0:T(8,128)(2,1)} %bitcast.22), channel_id=1, source_target_pairs={{0,1},{1,0},{2,3},{3,2},{4,5},{5,4},{6,7},{7,6},{8,9},{9,8},{10,11... | collective-permute-start | bytes 3440648 | tf_op jit(solution)/shard_map/ppermute | solution.py:138
  3.0 1.3 %slice_bitcast_fusion = (bf16[560,512]{1,0:T(8,128)(2,1)S(1)}, bf16[560,512]{1,0:T(8,128)(2,1)S(1)}) fusion(bf16[2,560,512]{2,1,0:T(8,128)(2,1)} %bitcast.23), kind=kLoop, calls=%fused_computation | loop fusion | bytes 2293760 | tf_op jit(solution)/shard_map/squeeze | solution.py:194
  4.9 1.5 %collective-permute-done.5.inner_ref = bf16[560,512]{1,0:T(8,128)(2,1)S(1)} collective-permute-done((bf16[560,512]{1,0:T(8,128)(2,1)S(1)}, bf16[560,512]{1,0:T(8,128)(2,1)S(1)}, u32[]{:S(2)}, u32[]{:S(2)}) %collective-permute-start.5) | collective-permute-done | bytes 573472 | tf_op jit(solution)/shard_map/ppermute | solution.py:150
  6.4 15.0 %collective-permute-start.6 = (bf16[560,512]{1,0:T(8,128)(2,1)S(1)}, bf16[560,512]{1,0:T(8,128)(2,1)S(1)}, u32[]{:S(2)}, u32[]{:S(2)}) collective-permute-start(bf16[560,512]{1,0:T(8,128)(2,1)S(1)} %collective-permute-done.5.inner_ref), channel_id=1, source_target_pairs={{0,1},{1,0},{2,3},{3,2},{4,5},{5,4},{6,7},{7,6},{8,9},{9,8},{10,11... | collective-permute-start | bytes 1720328 | tf_op jit(solution)/shard_map/ppermute | solution.py:138
  21.4 7.9 %collective-permute-done.1.near = bf16[2,560,512]{2,1,0:T(8,128)(2,1)S(1)} collective-permute-done((bf16[2,560,512]{2,1,0:T(8,128)(2,1)}, bf16[2,560,512]{2,1,0:T(8,128)(2,1)S(1)}, u32[]{:S(2)}, u32[]{:S(2)}) %collective-permute-start.1) | collective-permute-done | bytes 1146912 | tf_op jit(solution)/shard_map/ppermute | solution.py:138
  29.5 1.7 %copy-done.1 = bf16[2240,560]{0,1:T(8,128)(2,1)S(1)} copy-done((bf16[2240,560]{0,1:T(8,128)(2,1)S(1)}, bf16[2240,560]{0,1:T(8,128)(2,1)}, u32[]{:S(2)}) %copy-start.1) | copy-done | bytes 2508824
  31.2 1.7 %copy-done.3 = bf16[2240,560]{0,1:T(8,128)(2,1)S(1)} copy-done((bf16[2240,560]{0,1:T(8,128)(2,1)S(1)}, bf16[2240,560]{0,1:T(8,128)(2,1)}, u32[]{:S(2)}) %copy-start.3) | copy-done | bytes 2508824
  33.0 0.7 shard_map.55.tie.cut
  33.7 3.7 %collective-permute-start.3 = (bf16[560,512]{1,0:T(8,128)(2,1)S(1)}, bf16[560,512]{1,0:T(8,128)(2,1)S(1)}, u32[]{:S(2)}, u32[]{:S(2)}) collective-permute-start(bf16[560,512]{1,0:T(8,128)(2,1)S(1)} %collective-permute-done.inner_ref), channel_id=1, source_target_pairs={{0,1},{1,0},{2,3},{3,2},{4,5},{5,4},{6,7},{7,6},{8,9},{9,8},{10,11... | collective-permute-start | bytes 1720328 | tf_op jit(solution)/shard_map/ppermute | solution.py:138
  37.4 4.2 %collective-permute-done.6.b2o = bf16[560,512]{1,0:T(8,128)(2,1)S(1)} collective-permute-done((bf16[560,512]{1,0:T(8,128)(2,1)S(1)}, bf16[560,512]{1,0:T(8,128)(2,1)S(1)}, u32[]{:S(2)}, u32[]{:S(2)}) %collective-permute-start.6) | collective-permute-done | bytes 573472 | tf_op jit(solution)/shard_map/ppermute | solution.py:138
  41.6 5.8 %collective-permute-start.8 = (bf16[560,512]{1,0:T(8,128)(2,1)S(1)}, bf16[560,512]{1,0:T(8,128)(2,1)S(1)}, u32[]{:S(2)}, u32[]{:S(2)}) collective-permute-start(bf16[560,512]{1,0:T(8,128)(2,1)S(1)} %collective-permute-done.4.b2i), channel_id=1, source_target_pairs={{0,1},{1,0},{2,3},{3,2},{4,5},{5,4},{6,7},{7,6},{8,9},{9,8},{10,11... | collective-permute-start | bytes 1720328 | tf_op jit(solution)/shard_map/ppermute | solution.py:138
  47.5 4.7 %shard_map.56.sums = f32[3,560,512]{2,1,0:T(8,128)S(1)} custom-call(bf16[2,560,512]{2,1,0:T(8,128)(2,1)S(1)} %bitcast.24, bf16[2,560,512]{2,1,0:T(8,128)(2,1)S(1)} %collective-permute-done.1.near, bf16[560,512]{1,0:T(8,128)(2,1)S(1)} %collective-permute-done.4.b2i, bf16[560,512]{1,0:T(8,128)(2,1)S(1)} %collective-permute-done.6.b2o, ...), custom_call_target="tpu_custom_call" | custom-call | flops 60211200 | bytes 1024 | tf_op jit(solution)/shard_map/pallas_call | solution.py:210
  52.2 1.7 %collective-permute-done.3.b2o = bf16[560,512]{1,0:T(8,128)(2,1)S(1)} collective-permute-done((bf16[560,512]{1,0:T(8,128)(2,1)S(1)}, bf16[560,512]{1,0:T(8,128)(2,1)S(1)}, u32[]{:S(2)}, u32[]{:S(2)}) %collective-permute-start.3) | collective-permute-done | bytes 573472 | tf_op jit(solution)/shard_map/ppermute | solution.py:138
  53.9 3.2 %collective-permute-start.7 = (bf16[560,512]{1,0:T(8,128)(2,1)S(1)}, bf16[560,512]{1,0:T(8,128)(2,1)S(1)}, u32[]{:S(2)}, u32[]{:S(2)}) collective-permute-start(bf16[560,512]{1,0:T(8,128)(2,1)S(1)} %collective-permute-done.2.b2i), channel_id=1, source_target_pairs={{0,1},{1,0},{2,3},{3,2},{4,5},{5,4},{6,7},{7,6},{8,9},{9,8},{10,11... | collective-permute-start | bytes 1720328 | tf_op jit(solution)/shard_map/ppermute | solution.py:138
  57.1 4.7 %shard_map.57.rest_0_.sums = f32[3,560,512]{2,1,0:T(8,128)S(1)} custom-call(bf16[2,560,512]{2,1,0:T(8,128)(2,1)S(1)} %bitcast.25, bf16[2,560,512]{2,1,0:T(8,128)(2,1)S(1)} %collective-permute-done.1.near, bf16[560,512]{1,0:T(8,128)(2,1)S(1)} %collective-permute-done.2.b2i, bf16[560,512]{1,0:T(8,128)(2,1)S(1)} %collective-permute-done.3.b2o, ...), custom_call_target="tpu_custom_call" | custom-call | flops 60211200 | bytes 1024 | tf_op jit(solution)/shard_map/pallas_call | solution.py:210
  61.9 4.3 %collective-permute-done.8.end_ref = bf16[560,512]{1,0:T(8,128)(2,1)S(1)} collective-permute-done((bf16[560,512]{1,0:T(8,128)(2,1)S(1)}, bf16[560,512]{1,0:T(8,128)(2,1)S(1)}, u32[]{:S(2)}, u32[]{:S(2)}) %collective-permute-start.8) | collective-permute-done | bytes 573472 | tf_op jit(solution)/shard_map/ppermute | solution.py:138
  66.2 1.2 %shard_map.58 = (f32[560,112]{1,0:T(8,128)S(1)}, bf16[560,112]{1,0:T(8,128)(2,1)S(1)}) custom-call(bf16[560,512]{1,0:T(8,128)(2,1)S(1)} %collective-permute-done.5.inner_ref, bf16[560,512]{1,0:T(8,128)(2,1)S(1)} %collective-permute-done.8.end_ref, bf16[3,560,560]{2,1,0:T(8,128)(2,1)S(1)} %shard_map.55.tie.cut, f32[3,560,512]{2,1,0:T(8,128)S(1)} %shard_map.56.sums, ...), custom_call_target="tpu_custom_call" | custom-call | flops 10035200 | bytes 1024 | tf_op jit(solution)/shard_map/pallas_call | solution.py:217
  67.4 2.1 %collective-permute-start.10 = (bf16[560,112]{1,0:T(8,128)(2,1)S(1)}, bf16[560,112]{1,0:T(8,128)(2,1)S(1)}, u32[]{:S(2)}, u32[]{:S(2)}) collective-permute-start(bf16[560,112]{1,0:T(8,128)(2,1)S(1)} %get-tuple-element.21), channel_id=1, source_target_pairs={{0,8},{4,12},{8,0},{12,4},{1,9},{5,13},{9,1},{13,5},{2,10},{6,14},... | collective-permute-start | bytes 376328 | tf_op jit(solution)/shard_map/ppermute | solution.py:160
  69.5 1.5 %collective-permute-start.11 = (bf16[560,112]{1,0:T(8,128)(2,1)S(1)}, bf16[560,112]{1,0:T(8,128)(2,1)S(1)}, u32[]{:S(2)}, u32[]{:S(2)}) collective-permute-start(bf16[560,112]{1,0:T(8,128)(2,1)S(1)} %get-tuple-element.21), channel_id=1, source_target_pairs={{0,4},{4,0},{8,12},{12,8},{1,5},{5,1},{9,13},{13,9},{2,6},{6,2},{1... | collective-permute-start | bytes 376328 | tf_op jit(solution)/shard_map/ppermute | solution.py:160
  71.0 0.6 shard_map.59.rest_1_.query
  71.6 2.5 %collective-permute-done.10 = bf16[560,112]{1,0:T(8,128)(2,1)S(1)} collective-permute-done((bf16[560,112]{1,0:T(8,128)(2,1)S(1)}, bf16[560,112]{1,0:T(8,128)(2,1)S(1)}, u32[]{:S(2)}, u32[]{:S(2)}) %collective-permute-start.10) | collective-permute-done | bytes 125472 | tf_op jit(solution)/shard_map/ppermute | solution.py:160
  74.6 2.4 %collective-permute-done.9 = bf16[560,112]{1,0:T(8,128)(2,1)S(1)} collective-permute-done((bf16[560,112]{1,0:T(8,128)(2,1)S(1)}, bf16[560,112]{1,0:T(8,128)(2,1)S(1)}, u32[]{:S(2)}, u32[]{:S(2)}) %collective-permute-start.9) | collective-permute-done | bytes 125472 | tf_op jit(solution)/shard_map/ppermute | solution.py:160
  77.0 1.3 %collective-permute-start.12 = (bf16[560,112]{1,0:T(8,128)(2,1)S(1)}, bf16[560,112]{1,0:T(8,128)(2,1)S(1)}, u32[]{:S(2)}, u32[]{:S(2)}) collective-permute-start(bf16[560,112]{1,0:T(8,128)(2,1)S(1)} %get-tuple-element.29), channel_id=1, source_target_pairs={{0,16},{1,17},{2,18},{3,19},{4,20},{5,21},{6,22},{7,23},{8,24},{9,... | collective-permute-start | bytes 376328 | tf_op jit(solution)/shard_map/ppermute | solution.py:168
  78.4 1.2 %shard_map.60 = (f32[560,112]{1,0:T(8,128)S(1)}, bf16[560,112]{1,0:T(8,128)(2,1)S(1)}) custom-call(bf16[560,512]{1,0:T(8,128)(2,1)S(1)} %collective-permute-done.inner_ref, bf16[560,512]{1,0:T(8,128)(2,1)S(1)} %collective-permute-done.7.end_ref, bf16[3,560,560]{2,1,0:T(8,128)(2,1)S(1)} %shard_map.55.tie.cut, f32[3,560,512]{2,1,0:T(8,128)S(1)} %shard_map.57.rest_0_.sums, ...), custom_call_target="tpu_custom_call" | custom-call | flops 10035200 | bytes 1024 | tf_op jit(solution)/shard_map/pallas_call | solution.py:217
  79.6 1.9 %collective-permute-start.13 = (bf16[560,112]{1,0:T(8,128)(2,1)S(1)}, bf16[560,112]{1,0:T(8,128)(2,1)S(1)}, u32[]{:S(2)}, u32[]{:S(2)}) collective-permute-start(bf16[560,112]{1,0:T(8,128)(2,1)S(1)} %get-tuple-element.28), channel_id=1, source_target_pairs={{0,12},{4,8},{8,4},{12,0},{1,13},{5,9},{9,5},{13,1},{2,14},{6,10},... | collective-permute-start | bytes 376328 | tf_op jit(solution)/shard_map/ppermute | solution.py:160
  81.6 0.5 collective-permute-start.14
  82.1 1.1 %collective-permute-start.15 = (bf16[560,112]{1,0:T(8,128)(2,1)S(1)}, bf16[560,112]{1,0:T(8,128)(2,1)S(1)}, u32[]{:S(2)}, u32[]{:S(2)}) collective-permute-start(bf16[560,112]{1,0:T(8,128)(2,1)S(1)} %get-tuple-element.28), channel_id=1, source_target_pairs={{0,4},{4,0},{8,12},{12,8},{1,5},{5,1},{9,13},{13,9},{2,6},{6,2},{1... | collective-permute-start | bytes 376328 | tf_op jit(solution)/shard_map/ppermute | solution.py:160
  83.3 0.6 shard_map.61.query
  84.0 1.1 %shard_map.62.rest_5_ = bf16[2,560,512]{2,1,0:T(8,128)(2,1)} custom-call(bf16[560,512]{1,0:T(8,128)(2,1)S(1)} %shard_map.59.rest_1_.query, f32[560,1]{1,0:T(8,128)S(1)} %reshape.4.gain, bf16[560,112]{1,0:T(8,128)(2,1)S(1)} %collective-permute-done.12.rest_0_, f32[560,112]{1,0:T(8,128)S(1)} %get-tuple-element.30.rest_0_.rest_1_), custom_call_target="tpu_custom_call" | custom-call | flops 1003520 | bytes 1024 | tf_op jit(solution)/shard_map/pallas_call | solution.py:230
  85.1 2.1 %collective-permute-done.13.rest_2_ = bf16[560,112]{1,0:T(8,128)(2,1)S(1)} collective-permute-done((bf16[560,112]{1,0:T(8,128)(2,1)S(1)}, bf16[560,112]{1,0:T(8,128)(2,1)S(1)}, u32[]{:S(2)}, u32[]{:S(2)}) %collective-permute-start.13) | collective-permute-done | bytes 125472 | tf_op jit(solution)/shard_map/ppermute | solution.py:160
  87.2 0.7 collective-permute-done.14.rest_3_
  87.9 1.1 %shard_map.63 = bf16[2,560,512]{2,1,0:T(8,128)(2,1)} custom-call(bf16[560,512]{1,0:T(8,128)(2,1)S(1)} %shard_map.61.query, f32[560,1]{1,0:T(8,128)S(1)} %reshape.4.gain, bf16[560,112]{1,0:T(8,128)(2,1)S(1)} %collective-permute-done.12.rest_0_, f32[560,112]{1,0:T(8,128)S(1)} %get-tuple-element.27.tie.rest_1_, ...), custom_call_target="tpu_custom_call", output_to_operand_aliasing={{}: (7, {})} | custom-call | flops 1003520 | bytes 1024 | tf_op jit(solution)/shard_map/pallas_call | solution.py:230
  (25 shorter events, 1.5 us)
Async XLA Ops:
  0.0 29.5 %copy-start = (bf16[2240,560]{0,1:T(8,128)(2,1)S(1)}, bf16[2240,560]{0,1:T(8,128)(2,1)}, u32[]{:S(2)}) copy-start(bf16[2240,560]{0,1:T(8,128)(2,1)} %param.7) | copy-start | bytes 7526404
  0.0 29.3 %collective-permute-start.1 = (bf16[2,560,512]{2,1,0:T(8,128)(2,1)}, bf16[2,560,512]{2,1,0:T(8,128)(2,1)S(1)}, u32[]{:S(2)}, u32[]{:S(2)}) collective-permute-start(bf16[2,560,512]{2,1,0:T(8,128)(2,1)} %bitcast.22), channel_id=1, source_target_pairs={{0,1},{1,0},{2,3},{3,2},{4,5},{5,4},{6,7},{7,6},{8,9},{9,8},{10,11... | collective-permute-start | bytes 3440648 | tf_op jit(solution)/shard_map/ppermute | solution.py:138
  4.3 2.0 %collective-permute-start.5 = (bf16[560,512]{1,0:T(8,128)(2,1)S(1)}, bf16[560,512]{1,0:T(8,128)(2,1)S(1)}, u32[]{:S(2)}, u32[]{:S(2)}) collective-permute-start(bf16[560,512]{1,0:T(8,128)(2,1)S(1)} %get-tuple-element.31), channel_id=1, source_target_pairs={{0,16},{1,2},{2,1},{3,19},{16,0},{17,18},{18,17},{19,3},{4,20},{5,... | collective-permute-start | bytes 1720328 | tf_op jit(solution)/shard_map/ppermute | solution.py:150
  4.4 29.3 %collective-permute-start = (bf16[560,512]{1,0:T(8,128)(2,1)S(1)}, bf16[560,512]{1,0:T(8,128)(2,1)S(1)}, u32[]{:S(2)}, u32[]{:S(2)}) collective-permute-start(bf16[560,512]{1,0:T(8,128)(2,1)S(1)} %get-tuple-element.32), channel_id=1, source_target_pairs={{0,16},{1,2},{2,1},{3,19},{16,0},{17,18},{18,17},{19,3},{4,20},{5,... | collective-permute-start | bytes 1720328 | tf_op jit(solution)/shard_map/ppermute | solution.py:150
  6.4 35.2 %collective-permute-start.6 = (bf16[560,512]{1,0:T(8,128)(2,1)S(1)}, bf16[560,512]{1,0:T(8,128)(2,1)S(1)}, u32[]{:S(2)}, u32[]{:S(2)}) collective-permute-start(bf16[560,512]{1,0:T(8,128)(2,1)S(1)} %collective-permute-done.5.inner_ref), channel_id=1, source_target_pairs={{0,1},{1,0},{2,3},{3,2},{4,5},{5,4},{6,7},{7,6},{8,9},{9,8},{10,11... | collective-permute-start | bytes 1720328 | tf_op jit(solution)/shard_map/ppermute | solution.py:138
  29.4 12.2 %collective-permute-start.4 = (bf16[560,512]{1,0:T(8,128)(2,1)S(1)}, bf16[560,512]{1,0:T(8,128)(2,1)S(1)}, u32[]{:S(2)}, u32[]{:S(2)}) collective-permute-start(bf16[560,512]{1,0:T(8,128)(2,1)S(1)} %get-tuple-element.33), channel_id=1, source_target_pairs={{0,16},{1,2},{2,1},{3,19},{16,0},{17,18},{18,17},{19,3},{4,20},{5,... | collective-permute-start | bytes 1720328 | tf_op jit(solution)/shard_map/ppermute | solution.py:150
  29.5 1.7 %copy-start.1 = (bf16[2240,560]{0,1:T(8,128)(2,1)S(1)}, bf16[2240,560]{0,1:T(8,128)(2,1)}, u32[]{:S(2)}) copy-start(bf16[2240,560]{0,1:T(8,128)(2,1)} %param.8) | copy-start | bytes 7526404
  31.2 1.7 %copy-start.3 = (bf16[2240,560]{0,1:T(8,128)(2,1)S(1)}, bf16[2240,560]{0,1:T(8,128)(2,1)}, u32[]{:S(2)}) copy-start(bf16[2240,560]{0,1:T(8,128)(2,1)} %param.6) | copy-start | bytes 7526404
  33.0 14.5 %copy-start.2 = (bf16[2240,560]{0,1:T(8,128)(2,1)S(1)}, bf16[2240,560]{0,1:T(8,128)(2,1)}, u32[]{:S(2)}) copy-start(bf16[2240,560]{0,1:T(8,128)(2,1)} %param.8) | copy-start | bytes 7526404
  33.0 14.5 %copy-start.4 = (bf16[2,512,560]{1,2,0:T(8,128)(2,1)S(1)}, bf16[2,512,560]{1,2,0:T(8,128)(2,1)}, u32[]{:S(2)}) copy-start(bf16[2,512,560]{1,2,0:T(8,128)(2,1)} %param.5) | copy-start | bytes 3440644
  33.7 20.2 %collective-permute-start.3 = (bf16[560,512]{1,0:T(8,128)(2,1)S(1)}, bf16[560,512]{1,0:T(8,128)(2,1)S(1)}, u32[]{:S(2)}, u32[]{:S(2)}) collective-permute-start(bf16[560,512]{1,0:T(8,128)(2,1)S(1)} %collective-permute-done.inner_ref), channel_id=1, source_target_pairs={{0,1},{1,0},{2,3},{3,2},{4,5},{5,4},{6,7},{7,6},{8,9},{9,8},{10,11... | collective-permute-start | bytes 1720328 | tf_op jit(solution)/shard_map/ppermute | solution.py:138
  37.4 16.5 %collective-permute-start.2 = (bf16[560,512]{1,0:T(8,128)(2,1)S(1)}, bf16[560,512]{1,0:T(8,128)(2,1)S(1)}, u32[]{:S(2)}, u32[]{:S(2)}) collective-permute-start(bf16[560,512]{1,0:T(8,128)(2,1)S(1)} %get-tuple-element.34), channel_id=1, source_target_pairs={{0,16},{1,2},{2,1},{3,19},{16,0},{17,18},{18,17},{19,3},{4,20},{5,... | collective-permute-start | bytes 1720328 | tf_op jit(solution)/shard_map/ppermute | solution.py:150
  41.6 24.6 %collective-permute-start.8 = (bf16[560,512]{1,0:T(8,128)(2,1)S(1)}, bf16[560,512]{1,0:T(8,128)(2,1)S(1)}, u32[]{:S(2)}, u32[]{:S(2)}) collective-permute-start(bf16[560,512]{1,0:T(8,128)(2,1)S(1)} %collective-permute-done.4.b2i), channel_id=1, source_target_pairs={{0,1},{1,0},{2,3},{3,2},{4,5},{5,4},{6,7},{7,6},{8,9},{9,8},{10,11... | collective-permute-start | bytes 1720328 | tf_op jit(solution)/shard_map/ppermute | solution.py:138
  53.9 24.4 %collective-permute-start.7 = (bf16[560,512]{1,0:T(8,128)(2,1)S(1)}, bf16[560,512]{1,0:T(8,128)(2,1)S(1)}, u32[]{:S(2)}, u32[]{:S(2)}) collective-permute-start(bf16[560,512]{1,0:T(8,128)(2,1)S(1)} %collective-permute-done.2.b2i), channel_id=1, source_target_pairs={{0,1},{1,0},{2,3},{3,2},{4,5},{5,4},{6,7},{7,6},{8,9},{9,8},{10,11... | collective-permute-start | bytes 1720328 | tf_op jit(solution)/shard_map/ppermute | solution.py:138
  67.4 6.7 %collective-permute-start.10 = (bf16[560,112]{1,0:T(8,128)(2,1)S(1)}, bf16[560,112]{1,0:T(8,128)(2,1)S(1)}, u32[]{:S(2)}, u32[]{:S(2)}) collective-permute-start(bf16[560,112]{1,0:T(8,128)(2,1)S(1)} %get-tuple-element.21), channel_id=1, source_target_pairs={{0,8},{4,12},{8,0},{12,4},{1,9},{5,13},{9,1},{13,5},{2,10},{6,14},... | collective-permute-start | bytes 376328 | tf_op jit(solution)/shard_map/ppermute | solution.py:160
  69.5 5.1 %collective-permute-start.11 = (bf16[560,112]{1,0:T(8,128)(2,1)S(1)}, bf16[560,112]{1,0:T(8,128)(2,1)S(1)}, u32[]{:S(2)}, u32[]{:S(2)}) collective-permute-start(bf16[560,112]{1,0:T(8,128)(2,1)S(1)} %get-tuple-element.21), channel_id=1, source_target_pairs={{0,4},{4,0},{8,12},{12,8},{1,5},{5,1},{9,13},{13,9},{2,6},{6,2},{1... | collective-permute-start | bytes 376328 | tf_op jit(solution)/shard_map/ppermute | solution.py:160
  71.0 6.0 %collective-permute-start.9 = (bf16[560,112]{1,0:T(8,128)(2,1)S(1)}, bf16[560,112]{1,0:T(8,128)(2,1)S(1)}, u32[]{:S(2)}, u32[]{:S(2)}) collective-permute-start(bf16[560,112]{1,0:T(8,128)(2,1)S(1)} %get-tuple-element.21), channel_id=1, source_target_pairs={{0,12},{4,8},{8,4},{12,0},{1,13},{5,9},{9,5},{13,1},{2,14},{6,10},... | collective-permute-start | bytes 376328 | tf_op jit(solution)/shard_map/ppermute | solution.py:160
  77.0 6.9 %collective-permute-start.12 = (bf16[560,112]{1,0:T(8,128)(2,1)S(1)}, bf16[560,112]{1,0:T(8,128)(2,1)S(1)}, u32[]{:S(2)}, u32[]{:S(2)}) collective-permute-start(bf16[560,112]{1,0:T(8,128)(2,1)S(1)} %get-tuple-element.29), channel_id=1, source_target_pairs={{0,16},{1,17},{2,18},{3,19},{4,20},{5,21},{6,22},{7,23},{8,24},{9,... | collective-permute-start | bytes 376328 | tf_op jit(solution)/shard_map/ppermute | solution.py:168
  78.4 4.8 %copy-start.5 = (f32[560]{0:T(1024)S(1)}, f32[560]{0:T(1024)}, u32[]{:S(2)}) copy-start(f32[560]{0:T(1024)} %param.9) | copy-start | bytes 6724
  79.6 7.6 %collective-permute-start.13 = (bf16[560,112]{1,0:T(8,128)(2,1)S(1)}, bf16[560,112]{1,0:T(8,128)(2,1)S(1)}, u32[]{:S(2)}, u32[]{:S(2)}) collective-permute-start(bf16[560,112]{1,0:T(8,128)(2,1)S(1)} %get-tuple-element.28), channel_id=1, source_target_pairs={{0,12},{4,8},{8,4},{12,0},{1,13},{5,9},{9,5},{13,1},{2,14},{6,10},... | collective-permute-start | bytes 376328 | tf_op jit(solution)/shard_map/ppermute | solution.py:160
  81.6 6.3 %collective-permute-start.14 = (bf16[560,112]{1,0:T(8,128)(2,1)S(1)}, bf16[560,112]{1,0:T(8,128)(2,1)S(1)}, u32[]{:S(2)}, u32[]{:S(2)}) collective-permute-start(bf16[560,112]{1,0:T(8,128)(2,1)S(1)} %get-tuple-element.28), channel_id=1, source_target_pairs={{0,8},{4,12},{8,0},{12,4},{1,9},{5,13},{9,1},{13,5},{2,10},{6,14},... | collective-permute-start | bytes 376328 | tf_op jit(solution)/shard_map/ppermute | solution.py:160
  82.1 5.8 %collective-permute-start.15 = (bf16[560,112]{1,0:T(8,128)(2,1)S(1)}, bf16[560,112]{1,0:T(8,128)(2,1)S(1)}, u32[]{:S(2)}, u32[]{:S(2)}) collective-permute-start(bf16[560,112]{1,0:T(8,128)(2,1)S(1)} %get-tuple-element.28), channel_id=1, source_target_pairs={{0,4},{4,0},{8,12},{12,8},{1,5},{5,1},{9,13},{13,9},{2,6},{6,2},{1... | collective-permute-start | bytes 376328 | tf_op jit(solution)/shard_map/ppermute | solution.py:160

commit v18 on v16

--- a/solution.py
+++ b/solution.py
@@ -93,12 +93,12 @@
             body(ref)
 
 
-def state_kernel(inner_ref, end_ref, cut, sums, *rest):
+def state_kernel(span, inner_ref, end_ref, cut, sums, *rest):
     state = rest[-1]
 
     def body(block):
-        key = (sums[0] + rounded_dot(cut[0], block[...])).astype(jnp.bfloat16)
-        value = (sums[1] + rounded_dot(cut[1], block[...])).astype(jnp.bfloat16)
+        key = (sums[0, span] + rounded_dot(cut[0, span], block[...])).astype(jnp.bfloat16)
+        value = (sums[1, span] + rounded_dot(cut[1, span], block[...])).astype(jnp.bfloat16)
         key = jnp.maximum(key, 0)
         for start in range(0, key.shape[0], HEAD_DIM):
             rows = slice(start, start + HEAD_DIM)
@@ -117,12 +117,12 @@
     on_last(inner_ref, end_ref, body)
 
 
-def read_kernel(stream, parts, query, gain, *rest):
+def read_kernel(stream, span, parts, query, gain, prefix, *rest):
     out, held, sems = rest[-3:]
     copies = []
-    for start in range(0, query.shape[0], HEAD_DIM):
-        rows = slice(start, start + HEAD_DIM)
-        total = sum(part[rows, :].astype(jnp.float32) for part in rest[:parts])
+    for start in range(span.start, span.stop, HEAD_DIM):
+        rows, within = slice(start, start + HEAD_DIM), slice(start - span.start, start - span.start + HEAD_DIM)
+        total = prefix[rows, :] + sum(part[within, :].astype(jnp.float32) for part in rest[:parts])
         reading = rounded_dot(total.astype(jnp.bfloat16), query[rows, :])
         scale = lax.rsqrt(jnp.mean(reading * reading, axis=0, keepdims=True) + 1e-06)
         held[rows, :] = (reading * scale * gain[rows, :]).astype(jnp.bfloat16)
@@ -195,7 +195,6 @@
     whole = pltpu.VMEM((depth, tokens), jnp.bfloat16)
     sems = pltpu.SemaphoreType.DMA((4,))
     query_type = jax.ShapeDtypeStruct((width, tokens), jnp.bfloat16)
-    state_type = jax.ShapeDtypeStruct((width, HEAD_DIM), jnp.float32)
     out_type = jax.ShapeDtypeStruct((2, width, tokens), jnp.bfloat16)
 
     read_scratch = [pltpu.VMEM((width, tokens), jnp.bfloat16), pltpu.SemaphoreType.DMA((width // HEAD_DIM,))]
@@ -207,27 +206,36 @@
             functools.partial(partial_kernel, stream), jax.ShapeDtypeStruct((3, width, tokens), jnp.float32), IN_VMEM,
             [ANYWHERE] * 4 + [IN_VMEM] * 3 + [ANYWHERE], [whole, sems], 3 * one,
         )(columns, near, far[stream], across_end[stream], *matrices, cut))
-    prefix = parts = query = out = None
-    for stream in range(2):
-        ties = (sums[1],) if stream == 0 else (parts[0], query)
-        state = call(
-            state_kernel, state_type, IN_VMEM,
-            [IN_VMEM] * 4 + [ANYWHERE] * len(ties), [], one // 2,
-        )(across[stream], far_end[stream], cut, sums[stream], *ties)
+    everything = slice(0, width)
+    middle = (width // HEAD_DIM + 1) // 2 * HEAD_DIM
+    spans = ([everything], [span for span in (slice(0, middle), slice(middle, width)) if span.stop > span.start])
+    prefix = clean = query = out = None
+    for stream in range(2):
+        ties = (sums[1],) if stream == 0 else (clean, query)
+        parts = []
+        for span in spans[stream]:
+            state = call(
+                functools.partial(state_kernel, span),
+                jax.ShapeDtypeStruct((span.stop - span.start, HEAD_DIM), jnp.float32), IN_VMEM,
+                [IN_VMEM] * 4 + [ANYWHERE] * len(ties), [], one // 2,
+            )(across[stream], far_end[stream], cut, sums[stream], *ties)
+            ties = (state,)
+            parts.append([state, *from_others(state, "tok")])
         query = call(
             query_kernel, query_type, IN_VMEM, [IN_VMEM] * 4 + [ANYWHERE], [], one // 4,
         )(across[stream], far_end[stream], cut, sums[stream], state)
-        parts = [state, *from_others(state, "tok")]
         if stream == 0:
-            query, *parts = lax.optimization_barrier((query, *parts))
-            parts = [sum(part.astype(jnp.float32) for part in parts)]
-            prefix = entering(parts[0], "group")
-        kept = [] if out is None else [out]
-        out = call(
-            functools.partial(read_kernel, stream, len(parts) + 1), out_type, ANYWHERE,
-            [IN_VMEM] * (3 + len(parts)) + [ANYWHERE] * len(kept),
-            read_scratch, one // 20, {3 + len(parts): 0} if kept else None,
-        )(query, gain_column, prefix, *parts, *kept)
+            query, *terms = lax.optimization_barrier((query, *parts[0]))
+            clean = sum(term.astype(jnp.float32) for term in terms)
+            parts = [[clean]]
+            prefix = entering(clean, "group")
+        for span, terms in zip(spans[stream], parts):
+            kept = [] if out is None else [out]
+            out = call(
+                functools.partial(read_kernel, stream, span, len(terms)), out_type, ANYWHERE,
+                [IN_VMEM] * (3 + len(terms)) + [ANYWHERE] * len(kept),
+                read_scratch, one // 20, {3 + len(terms): 0} if kept else None,
+            )(query, gain_column, prefix, *terms, *kept)
     return jnp.swapaxes(out, 1, 2)
 
 

time: 89.3 us -> 91.5 us (1.025)
  starting transfers between devices: 39.9 us -> 43.4 us
  waiting for transfers between devices: 27.8 us -> 25.1 us
  Pallas kernels: 16.1 us -> 17.3 us
    ppermute x6 -> x9, starting transfers between devices: 7.17 us -> 10.6 us  [from_others(): got.append(lax.ppermute(sent, axis, pairs))]
    ppermute x6 -> x9, waiting for transfers between devices: 8.08 us -> 5.7 us  [from_others(): got.append(lax.ppermute(sent, axis, pairs))]
    pallas_call x4 -> x6, Pallas kernels: 4.71 us -> 5.88 us  [the longest x3 3.14 us: local(): call(functools.partial(read_kernel, stream, span, len(terms)), out_type,...]
  transfers between devices with their start and end apart: 16 -> 19, of which waited for: 10 -> 10; matrix products, arithmetic and copies ran while one was open for 2% -> 2% of each run, Pallas kernels for 17% -> 18%
where the time goes in v18:
time: 91.5 us; the launch traced here: 91.3 us
  starting transfers between devices  43.4 us (47%)
  waiting for transfers between devices  25.1 us (27%)
  Pallas kernels  17.3 us (19%)
  local copies, waits for them, and re-layouts  5.13 us (6%)
    ppermute x5, starting transfers between devices, partner_swap(): lax.ppermute(value, axis, [(i, i ^ 1) for i in range(lax.axis_size(axis))])  30.9 us
    ppermute x5, waiting for transfers between devices, partner_swap(): lax.ppermute(value, axis, [(i, i ^ 1) for i in range(lax.axis_size(axis))])  17.9 us
    ppermute x9, starting transfers between devices, from_others(): got.append(lax.ppermute(sent, axis, pairs))  10.6 us
    pallas_call x2, Pallas kernels, local(): call(functools.partial(partial_kernel, stream), jax.ShapeDtypeStruct((3,...  9.47 us
    ppermute x9, waiting for transfers between devices, from_others(): got.append(lax.ppermute(sent, axis, pairs))  5.7 us
    unnamed x12, local copies, waits for them, and re-layouts  3.47 us
    pallas_call x3, Pallas kernels, local(): call(functools.partial(read_kernel, stream, span, len(terms)), out_type,...  3.14 us
    pallas_call x3, Pallas kernels, local(): call(functools.partial(state_kernel, span), jax.ShapeDtypeStruct((span.st...  2.74 us
  transfers between devices with their start and end apart: 19, of which 10 were waited for; matrix products, arithmetic and copies ran while one was open for 2% of the time, Pallas kernels for 18%

profile of v18, /device:TPU:0, one launch (start us, length us, event | category | flops | bytes accessed | tf_op | source)
XLA Modules:
  0.0 91.3 jit_solution(13686048704547003484)
XLA Ops:
  0.0 3.0 %collective-permute-start.1 = (bf16[2,560,512]{2,1,0:T(8,128)(2,1)}, bf16[2,560,512]{2,1,0:T(8,128)(2,1)S(1)}, u32[]{:S(2)}, u32[]{:S(2)}) collective-permute-start(bf16[2,560,512]{2,1,0:T(8,128)(2,1)} %bitcast.22), channel_id=1, source_target_pairs={{0,1},{1,0},{2,3},{3,2},{4,5},{5,4},{6,7},{7,6},{8,9},{9,8},{10,11... | collective-permute-start | bytes 3440648 | tf_op jit(solution)/shard_map/ppermute | solution.py:136
  3.0 1.5 %slice_bitcast_fusion = (bf16[560,512]{1,0:T(8,128)(2,1)S(1)}, bf16[560,512]{1,0:T(8,128)(2,1)S(1)}) fusion(bf16[2,560,512]{2,1,0:T(8,128)(2,1)} %bitcast.23), kind=kLoop, calls=%fused_computation | loop fusion | bytes 2293760 | tf_op jit(solution)/shard_map/squeeze | solution.py:190
  5.1 1.5 %collective-permute-done.5.inner_ref = bf16[560,512]{1,0:T(8,128)(2,1)S(1)} collective-permute-done((bf16[560,512]{1,0:T(8,128)(2,1)S(1)}, bf16[560,512]{1,0:T(8,128)(2,1)S(1)}, u32[]{:S(2)}, u32[]{:S(2)}) %collective-permute-start.5) | collective-permute-done | bytes 573472 | tf_op jit(solution)/shard_map/ppermute | solution.py:148
  6.5 15.0 %collective-permute-start.6 = (bf16[560,512]{1,0:T(8,128)(2,1)S(1)}, bf16[560,512]{1,0:T(8,128)(2,1)S(1)}, u32[]{:S(2)}, u32[]{:S(2)}) collective-permute-start(bf16[560,512]{1,0:T(8,128)(2,1)S(1)} %collective-permute-done.5.inner_ref), channel_id=1, source_target_pairs={{0,1},{1,0},{2,3},{3,2},{4,5},{5,4},{6,7},{7,6},{8,9},{9,8},{10,11... | collective-permute-start | bytes 1720328 | tf_op jit(solution)/shard_map/ppermute | solution.py:136
  21.6 7.8 %collective-permute-done.1.near = bf16[2,560,512]{2,1,0:T(8,128)(2,1)S(1)} collective-permute-done((bf16[2,560,512]{2,1,0:T(8,128)(2,1)}, bf16[2,560,512]{2,1,0:T(8,128)(2,1)S(1)}, u32[]{:S(2)}, u32[]{:S(2)}) %collective-permute-start.1) | collective-permute-done | bytes 1146912 | tf_op jit(solution)/shard_map/ppermute | solution.py:136
  29.5 1.7 %copy-done.1 = bf16[2240,560]{0,1:T(8,128)(2,1)S(1)} copy-done((bf16[2240,560]{0,1:T(8,128)(2,1)S(1)}, bf16[2240,560]{0,1:T(8,128)(2,1)}, u32[]{:S(2)}) %copy-start.1) | copy-done | bytes 2508824
  31.2 1.7 %copy-done.3 = bf16[2240,560]{0,1:T(8,128)(2,1)S(1)} copy-done((bf16[2240,560]{0,1:T(8,128)(2,1)S(1)}, bf16[2240,560]{0,1:T(8,128)(2,1)}, u32[]{:S(2)}) %copy-start.3) | copy-done | bytes 2508824
  33.0 0.7 shard_map.55.tie.cut
  33.7 3.7 %collective-permute-start.3 = (bf16[560,512]{1,0:T(8,128)(2,1)S(1)}, bf16[560,512]{1,0:T(8,128)(2,1)S(1)}, u32[]{:S(2)}, u32[]{:S(2)}) collective-permute-start(bf16[560,512]{1,0:T(8,128)(2,1)S(1)} %collective-permute-done.inner_ref), channel_id=1, source_target_pairs={{0,1},{1,0},{2,3},{3,2},{4,5},{5,4},{6,7},{7,6},{8,9},{9,8},{10,11... | collective-permute-start | bytes 1720328 | tf_op jit(solution)/shard_map/ppermute | solution.py:136
  37.4 4.2 %collective-permute-done.6.b2o = bf16[560,512]{1,0:T(8,128)(2,1)S(1)} collective-permute-done((bf16[560,512]{1,0:T(8,128)(2,1)S(1)}, bf16[560,512]{1,0:T(8,128)(2,1)S(1)}, u32[]{:S(2)}, u32[]{:S(2)}) %collective-permute-start.6) | collective-permute-done | bytes 573472 | tf_op jit(solution)/shard_map/ppermute | solution.py:136
  41.6 5.8 %collective-permute-start.8 = (bf16[560,512]{1,0:T(8,128)(2,1)S(1)}, bf16[560,512]{1,0:T(8,128)(2,1)S(1)}, u32[]{:S(2)}, u32[]{:S(2)}) collective-permute-start(bf16[560,512]{1,0:T(8,128)(2,1)S(1)} %collective-permute-done.4.b2i), channel_id=1, source_target_pairs={{0,1},{1,0},{2,3},{3,2},{4,5},{5,4},{6,7},{7,6},{8,9},{9,8},{10,11... | collective-permute-start | bytes 1720328 | tf_op jit(solution)/shard_map/ppermute | solution.py:136
  47.5 4.7 %shard_map.56.sums = f32[3,560,512]{2,1,0:T(8,128)S(1)} custom-call(bf16[2,560,512]{2,1,0:T(8,128)(2,1)S(1)} %bitcast.24, bf16[2,560,512]{2,1,0:T(8,128)(2,1)S(1)} %collective-permute-done.1.near, bf16[560,512]{1,0:T(8,128)(2,1)S(1)} %collective-permute-done.4.b2i, bf16[560,512]{1,0:T(8,128)(2,1)S(1)} %collective-permute-done.6.b2o, ...), custom_call_target="tpu_custom_call" | custom-call | flops 60211200 | bytes 1024 | tf_op jit(solution)/shard_map/pallas_call | solution.py:205
  52.2 1.7 %collective-permute-done.3.b2o = bf16[560,512]{1,0:T(8,128)(2,1)S(1)} collective-permute-done((bf16[560,512]{1,0:T(8,128)(2,1)S(1)}, bf16[560,512]{1,0:T(8,128)(2,1)S(1)}, u32[]{:S(2)}, u32[]{:S(2)}) %collective-permute-start.3) | collective-permute-done | bytes 573472 | tf_op jit(solution)/shard_map/ppermute | solution.py:136
  53.9 3.4 %collective-permute-start.7 = (bf16[560,512]{1,0:T(8,128)(2,1)S(1)}, bf16[560,512]{1,0:T(8,128)(2,1)S(1)}, u32[]{:S(2)}, u32[]{:S(2)}) collective-permute-start(bf16[560,512]{1,0:T(8,128)(2,1)S(1)} %collective-permute-done.2.b2i), channel_id=1, source_target_pairs={{0,1},{1,0},{2,3},{3,2},{4,5},{5,4},{6,7},{7,6},{8,9},{9,8},{10,11... | collective-permute-start | bytes 1720328 | tf_op jit(solution)/shard_map/ppermute | solution.py:136
  57.3 4.7 %shard_map.57.rest_0_.sums = f32[3,560,512]{2,1,0:T(8,128)S(1)} custom-call(bf16[2,560,512]{2,1,0:T(8,128)(2,1)S(1)} %bitcast.25, bf16[2,560,512]{2,1,0:T(8,128)(2,1)S(1)} %collective-permute-done.1.near, bf16[560,512]{1,0:T(8,128)(2,1)S(1)} %collective-permute-done.2.b2i, bf16[560,512]{1,0:T(8,128)(2,1)S(1)} %collective-permute-done.3.b2o, ...), custom_call_target="tpu_custom_call" | custom-call | flops 60211200 | bytes 1024 | tf_op jit(solution)/shard_map/pallas_call | solution.py:205
  62.0 4.2 %collective-permute-done.8.end_ref = bf16[560,512]{1,0:T(8,128)(2,1)S(1)} collective-permute-done((bf16[560,512]{1,0:T(8,128)(2,1)S(1)}, bf16[560,512]{1,0:T(8,128)(2,1)S(1)}, u32[]{:S(2)}, u32[]{:S(2)}) %collective-permute-start.8) | collective-permute-done | bytes 573472 | tf_op jit(solution)/shard_map/ppermute | solution.py:136
  66.2 1.2 %shard_map.58.tie = f32[560,112]{1,0:T(8,128)S(1)} custom-call(bf16[560,512]{1,0:T(8,128)(2,1)S(1)} %collective-permute-done.5.inner_ref, bf16[560,512]{1,0:T(8,128)(2,1)S(1)} %collective-permute-done.8.end_ref, bf16[3,560,560]{2,1,0:T(8,128)(2,1)S(1)} %shard_map.55.tie.cut, f32[3,560,512]{2,1,0:T(8,128)S(1)} %shard_map.56.sums, ...), custom_call_target="tpu_custom_call" | custom-call | flops 10035200 | bytes 1024 | tf_op jit(solution)/shard_map/pallas_call | solution.py:217
  67.4 2.1 %collective-permute-start.10 = (bf16[560,112]{1,0:T(8,128)(2,1)S(1)}, bf16[560,112]{1,0:T(8,128)(2,1)S(1)}, u32[]{:S(2)}, u32[]{:S(2)}) collective-permute-start(bf16[560,112]{1,0:T(8,128)(2,1)S(1)} %convert_element_type.18), channel_id=1, source_target_pairs={{0,8},{4,12},{8,0},{12,4},{1,9},{5,13},{9,1},{13,5},{2,10},{6,14},... | collective-permute-start | bytes 376328 | tf_op jit(solution)/shard_map/ppermute | solution.py:159
  69.5 1.5 %collective-permute-start.11 = (bf16[560,112]{1,0:T(8,128)(2,1)S(1)}, bf16[560,112]{1,0:T(8,128)(2,1)S(1)}, u32[]{:S(2)}, u32[]{:S(2)}) collective-permute-start(bf16[560,112]{1,0:T(8,128)(2,1)S(1)} %convert_element_type.18), channel_id=1, source_target_pairs={{0,4},{4,0},{8,12},{12,8},{1,5},{5,1},{9,13},{13,9},{2,6},{6,2},{1... | collective-permute-start | bytes 376328 | tf_op jit(solution)/shard_map/ppermute | solution.py:159
  71.7 2.5 %collective-permute-done.10 = bf16[560,112]{1,0:T(8,128)(2,1)S(1)} collective-permute-done((bf16[560,112]{1,0:T(8,128)(2,1)S(1)}, bf16[560,112]{1,0:T(8,128)(2,1)S(1)}, u32[]{:S(2)}, u32[]{:S(2)}) %collective-permute-start.10) | collective-permute-done | bytes 125472 | tf_op jit(solution)/shard_map/ppermute | solution.py:159
  74.6 2.4 %collective-permute-done.9 = bf16[560,112]{1,0:T(8,128)(2,1)S(1)} collective-permute-done((bf16[560,112]{1,0:T(8,128)(2,1)S(1)}, bf16[560,112]{1,0:T(8,128)(2,1)S(1)}, u32[]{:S(2)}, u32[]{:S(2)}) %collective-permute-start.9) | collective-permute-done | bytes 125472 | tf_op jit(solution)/shard_map/ppermute | solution.py:159
  77.1 1.3 %collective-permute-start.12 = (f32[560,112]{1,0:T(8,128)S(1)}, f32[560,112]{1,0:T(8,128)S(1)}, u32[]{:S(2)}, u32[]{:S(2)}) collective-permute-start(f32[560,112]{1,0:T(8,128)S(1)} %convert_add_fusion.rest_0_), channel_id=1, source_target_pairs={{0,16},{1,17},{2,18},{3,19},{4,20},{5,21},{6,22},{7,23},{8,24},{9,... | collective-permute-start | bytes 752648 | tf_op jit(solution)/shard_map/ppermute | solution.py:165
  78.4 0.8 shard_map.60.rest_0_
  79.3 1.9 %collective-permute-start.16 = (bf16[336,112]{1,0:T(8,128)(2,1)S(1)}, bf16[336,112]{1,0:T(8,128)(2,1)S(1)}, u32[]{:S(2)}, u32[]{:S(2)}) collective-permute-start(bf16[336,112]{1,0:T(8,128)(2,1)S(1)} %convert_element_type.23), channel_id=1, source_target_pairs={{0,12},{4,8},{8,4},{12,0},{1,13},{5,9},{9,5},{13,1},{2,14},{6,10},... | collective-permute-start | bytes 225800 | tf_op jit(solution)/shard_map/ppermute | solution.py:159
  81.7 1.1 %collective-permute-start.18 = (bf16[336,112]{1,0:T(8,128)(2,1)S(1)}, bf16[336,112]{1,0:T(8,128)(2,1)S(1)}, u32[]{:S(2)}, u32[]{:S(2)}) collective-permute-start(bf16[336,112]{1,0:T(8,128)(2,1)S(1)} %convert_element_type.23), channel_id=1, source_target_pairs={{0,4},{4,0},{8,12},{12,8},{1,5},{5,1},{9,13},{13,9},{2,6},{6,2},{1... | collective-permute-start | bytes 225800 | tf_op jit(solution)/shard_map/ppermute | solution.py:159
  82.8 0.7 shard_map.61.tie.rest_0_
  83.5 1.9 %collective-permute-start.13 = (bf16[224,112]{1,0:T(8,128)(2,1)S(1)}, bf16[224,112]{1,0:T(8,128)(2,1)S(1)}, u32[]{:S(2)}, u32[]{:S(2)}) collective-permute-start(bf16[224,112]{1,0:T(8,128)(2,1)S(1)} %convert_element_type.22), channel_id=1, source_target_pairs={{0,12},{4,8},{8,4},{12,0},{1,13},{5,9},{9,5},{13,1},{2,14},{6,10},... | collective-permute-start | bytes 150536 | tf_op jit(solution)/shard_map/ppermute | solution.py:159
  86.1 1.1 %collective-permute-start.15 = (bf16[224,112]{1,0:T(8,128)(2,1)S(1)}, bf16[224,112]{1,0:T(8,128)(2,1)S(1)}, u32[]{:S(2)}, u32[]{:S(2)}) collective-permute-start(bf16[224,112]{1,0:T(8,128)(2,1)S(1)} %convert_element_type.22), channel_id=1, source_target_pairs={{0,4},{4,0},{8,12},{12,8},{1,5},{5,1},{9,13},{13,9},{2,6},{6,2},{1... | collective-permute-start | bytes 150536 | tf_op jit(solution)/shard_map/ppermute | solution.py:159
  87.4 0.6 shard_map.62.query
  88.0 1.1 %shard_map.63.rest_4_ = bf16[2,560,512]{2,1,0:T(8,128)(2,1)} custom-call(bf16[560,512]{1,0:T(8,128)(2,1)S(1)} %shard_map.59.rest_1_.query, f32[560,1]{1,0:T(8,128)S(1)} %reshape.4.gain, f32[560,112]{1,0:T(8,128)S(1)} %collective-permute-done.12.prefix, f32[560,112]{1,0:T(8,128)S(1)} %convert_add_fusion.rest_0_), custom_call_target="tpu_custom_call" | custom-call | flops 1003520 | bytes 1024 | tf_op jit(solution)/shard_map/pallas_call | solution.py:234
  89.2 1.0 %shard_map.64.rest_4_ = bf16[2,560,512]{2,1,0:T(8,128)(2,1)} custom-call(bf16[560,512]{1,0:T(8,128)(2,1)S(1)} %shard_map.62.query, f32[560,1]{1,0:T(8,128)S(1)} %reshape.4.gain, f32[560,112]{1,0:T(8,128)S(1)} %collective-permute-done.12.prefix, f32[336,112]{1,0:T(8,128)S(1)} %shard_map.60.rest_0_, ...), custom_call_target="tpu_custom_call", output_to_operand_aliasing={{}: (7, {})} | custom-call | flops 1003520 | bytes 1024 | tf_op jit(solution)/shard_map/pallas_call | solution.py:234
  90.3 1.0 %shard_map.65 = bf16[2,560,512]{2,1,0:T(8,128)(2,1)} custom-call(bf16[560,512]{1,0:T(8,128)(2,1)S(1)} %shard_map.62.query, f32[560,1]{1,0:T(8,128)S(1)} %reshape.4.gain, f32[560,112]{1,0:T(8,128)S(1)} %collective-permute-done.12.prefix, f32[224,112]{1,0:T(8,128)S(1)} %shard_map.61.tie.rest_0_, ...), custom_call_target="tpu_custom_call", output_to_operand_aliasing={{}: (7, {})} | custom-call | flops 1003520 | bytes 1024 | tf_op jit(solution)/shard_map/pallas_call | solution.py:234
  (36 shorter events, 3.3 us)
Async XLA Ops:
  0.0 29.3 %collective-permute-start.1 = (bf16[2,560,512]{2,1,0:T(8,128)(2,1)}, bf16[2,560,512]{2,1,0:T(8,128)(2,1)S(1)}, u32[]{:S(2)}, u32[]{:S(2)}) collective-permute-start(bf16[2,560,512]{2,1,0:T(8,128)(2,1)} %bitcast.22), channel_id=1, source_target_pairs={{0,1},{1,0},{2,3},{3,2},{4,5},{5,4},{6,7},{7,6},{8,9},{9,8},{10,11... | collective-permute-start | bytes 3440648 | tf_op jit(solution)/shard_map/ppermute | solution.py:136
  3.0 26.5 %copy-start = (bf16[2240,560]{0,1:T(8,128)(2,1)S(1)}, bf16[2240,560]{0,1:T(8,128)(2,1)}, u32[]{:S(2)}) copy-start(bf16[2240,560]{0,1:T(8,128)(2,1)} %param.7) | copy-start | bytes 7526404
  4.5 2.0 %collective-permute-start.5 = (bf16[560,512]{1,0:T(8,128)(2,1)S(1)}, bf16[560,512]{1,0:T(8,128)(2,1)S(1)}, u32[]{:S(2)}, u32[]{:S(2)}) collective-permute-start(bf16[560,512]{1,0:T(8,128)(2,1)S(1)} %get-tuple-element.21), channel_id=1, source_target_pairs={{0,16},{1,2},{2,1},{3,19},{16,0},{17,18},{18,17},{19,3},{4,20},{5,... | collective-permute-start | bytes 1720328 | tf_op jit(solution)/shard_map/ppermute | solution.py:148
  4.6 29.1 %collective-permute-start = (bf16[560,512]{1,0:T(8,128)(2,1)S(1)}, bf16[560,512]{1,0:T(8,128)(2,1)S(1)}, u32[]{:S(2)}, u32[]{:S(2)}) collective-permute-start(bf16[560,512]{1,0:T(8,128)(2,1)S(1)} %get-tuple-element.22), channel_id=1, source_target_pairs={{0,16},{1,2},{2,1},{3,19},{16,0},{17,18},{18,17},{19,3},{4,20},{5,... | collective-permute-start | bytes 1720328 | tf_op jit(solution)/shard_map/ppermute | solution.py:148
  6.5 35.1 %collective-permute-start.6 = (bf16[560,512]{1,0:T(8,128)(2,1)S(1)}, bf16[560,512]{1,0:T(8,128)(2,1)S(1)}, u32[]{:S(2)}, u32[]{:S(2)}) collective-permute-start(bf16[560,512]{1,0:T(8,128)(2,1)S(1)} %collective-permute-done.5.inner_ref), channel_id=1, source_target_pairs={{0,1},{1,0},{2,3},{3,2},{4,5},{5,4},{6,7},{7,6},{8,9},{9,8},{10,11... | collective-permute-start | bytes 1720328 | tf_op jit(solution)/shard_map/ppermute | solution.py:136
  29.4 12.2 %collective-permute-start.4 = (bf16[560,512]{1,0:T(8,128)(2,1)S(1)}, bf16[560,512]{1,0:T(8,128)(2,1)S(1)}, u32[]{:S(2)}, u32[]{:S(2)}) collective-permute-start(bf16[560,512]{1,0:T(8,128)(2,1)S(1)} %get-tuple-element.23), channel_id=1, source_target_pairs={{0,16},{1,2},{2,1},{3,19},{16,0},{17,18},{18,17},{19,3},{4,20},{5,... | collective-permute-start | bytes 1720328 | tf_op jit(solution)/shard_map/ppermute | solution.py:148
  29.5 1.7 %copy-start.1 = (bf16[2240,560]{0,1:T(8,128)(2,1)S(1)}, bf16[2240,560]{0,1:T(8,128)(2,1)}, u32[]{:S(2)}) copy-start(bf16[2240,560]{0,1:T(8,128)(2,1)} %param.8) | copy-start | bytes 7526404
  31.2 1.7 %copy-start.3 = (bf16[2240,560]{0,1:T(8,128)(2,1)S(1)}, bf16[2240,560]{0,1:T(8,128)(2,1)}, u32[]{:S(2)}) copy-start(bf16[2240,560]{0,1:T(8,128)(2,1)} %param.6) | copy-start | bytes 7526404
  33.0 14.5 %copy-start.2 = (bf16[2240,560]{0,1:T(8,128)(2,1)S(1)}, bf16[2240,560]{0,1:T(8,128)(2,1)}, u32[]{:S(2)}) copy-start(bf16[2240,560]{0,1:T(8,128)(2,1)} %param.8) | copy-start | bytes 7526404
  33.0 14.5 %copy-start.4 = (bf16[2,512,560]{1,2,0:T(8,128)(2,1)S(1)}, bf16[2,512,560]{1,2,0:T(8,128)(2,1)}, u32[]{:S(2)}) copy-start(bf16[2,512,560]{1,2,0:T(8,128)(2,1)} %param.5) | copy-start | bytes 3440644
  33.7 20.2 %collective-permute-start.3 = (bf16[560,512]{1,0:T(8,128)(2,1)S(1)}, bf16[560,512]{1,0:T(8,128)(2,1)S(1)}, u32[]{:S(2)}, u32[]{:S(2)}) collective-permute-start(bf16[560,512]{1,0:T(8,128)(2,1)S(1)} %collective-permute-done.inner_ref), channel_id=1, source_target_pairs={{0,1},{1,0},{2,3},{3,2},{4,5},{5,4},{6,7},{7,6},{8,9},{9,8},{10,11... | collective-permute-start | bytes 1720328 | tf_op jit(solution)/shard_map/ppermute | solution.py:136
  37.4 16.5 %collective-permute-start.2 = (bf16[560,512]{1,0:T(8,128)(2,1)S(1)}, bf16[560,512]{1,0:T(8,128)(2,1)S(1)}, u32[]{:S(2)}, u32[]{:S(2)}) collective-permute-start(bf16[560,512]{1,0:T(8,128)(2,1)S(1)} %get-tuple-element.24), channel_id=1, source_target_pairs={{0,16},{1,2},{2,1},{3,19},{16,0},{17,18},{18,17},{19,3},{4,20},{5,... | collective-permute-start | bytes 1720328 | tf_op jit(solution)/shard_map/ppermute | solution.py:148
  41.6 24.6 %collective-permute-start.8 = (bf16[560,512]{1,0:T(8,128)(2,1)S(1)}, bf16[560,512]{1,0:T(8,128)(2,1)S(1)}, u32[]{:S(2)}, u32[]{:S(2)}) collective-permute-start(bf16[560,512]{1,0:T(8,128)(2,1)S(1)} %collective-permute-done.4.b2i), channel_id=1, source_target_pairs={{0,1},{1,0},{2,3},{3,2},{4,5},{5,4},{6,7},{7,6},{8,9},{9,8},{10,11... | collective-permute-start | bytes 1720328 | tf_op jit(solution)/shard_map/ppermute | solution.py:136
  53.9 24.5 %collective-permute-start.7 = (bf16[560,512]{1,0:T(8,128)(2,1)S(1)}, bf16[560,512]{1,0:T(8,128)(2,1)S(1)}, u32[]{:S(2)}, u32[]{:S(2)}) collective-permute-start(bf16[560,512]{1,0:T(8,128)(2,1)S(1)} %collective-permute-done.2.b2i), channel_id=1, source_target_pairs={{0,1},{1,0},{2,3},{3,2},{4,5},{5,4},{6,7},{7,6},{8,9},{9,8},{10,11... | collective-permute-start | bytes 1720328 | tf_op jit(solution)/shard_map/ppermute | solution.py:136
  67.4 6.7 %collective-permute-start.10 = (bf16[560,112]{1,0:T(8,128)(2,1)S(1)}, bf16[560,112]{1,0:T(8,128)(2,1)S(1)}, u32[]{:S(2)}, u32[]{:S(2)}) collective-permute-start(bf16[560,112]{1,0:T(8,128)(2,1)S(1)} %convert_element_type.18), channel_id=1, source_target_pairs={{0,8},{4,12},{8,0},{12,4},{1,9},{5,13},{9,1},{13,5},{2,10},{6,14},... | collective-permute-start | bytes 376328 | tf_op jit(solution)/shard_map/ppermute | solution.py:159
  69.5 5.1 %collective-permute-start.11 = (bf16[560,112]{1,0:T(8,128)(2,1)S(1)}, bf16[560,112]{1,0:T(8,128)(2,1)S(1)}, u32[]{:S(2)}, u32[]{:S(2)}) collective-permute-start(bf16[560,112]{1,0:T(8,128)(2,1)S(1)} %convert_element_type.18), channel_id=1, source_target_pairs={{0,4},{4,0},{8,12},{12,8},{1,5},{5,1},{9,13},{13,9},{2,6},{6,2},{1... | collective-permute-start | bytes 376328 | tf_op jit(solution)/shard_map/ppermute | solution.py:159
  71.0 6.0 %collective-permute-start.9 = (bf16[560,112]{1,0:T(8,128)(2,1)S(1)}, bf16[560,112]{1,0:T(8,128)(2,1)S(1)}, u32[]{:S(2)}, u32[]{:S(2)}) collective-permute-start(bf16[560,112]{1,0:T(8,128)(2,1)S(1)} %convert_element_type.18), channel_id=1, source_target_pairs={{0,12},{4,8},{8,4},{12,0},{1,13},{5,9},{9,5},{13,1},{2,14},{6,10},... | collective-permute-start | bytes 376328 | tf_op jit(solution)/shard_map/ppermute | solution.py:159
  77.1 9.0 %collective-permute-start.12 = (f32[560,112]{1,0:T(8,128)S(1)}, f32[560,112]{1,0:T(8,128)S(1)}, u32[]{:S(2)}, u32[]{:S(2)}) collective-permute-start(f32[560,112]{1,0:T(8,128)S(1)} %convert_add_fusion.rest_0_), channel_id=1, source_target_pairs={{0,16},{1,17},{2,18},{3,19},{4,20},{5,21},{6,22},{7,23},{8,24},{9,... | collective-permute-start | bytes 752648 | tf_op jit(solution)/shard_map/ppermute | solution.py:165
  79.3 8.0 %copy-start.5 = (f32[560]{0:T(1024)S(1)}, f32[560]{0:T(1024)}, u32[]{:S(2)}) copy-start(f32[560]{0:T(1024)} %param.9) | copy-start | bytes 6724
  79.3 6.5 %collective-permute-start.16 = (bf16[336,112]{1,0:T(8,128)(2,1)S(1)}, bf16[336,112]{1,0:T(8,128)(2,1)S(1)}, u32[]{:S(2)}, u32[]{:S(2)}) collective-permute-start(bf16[336,112]{1,0:T(8,128)(2,1)S(1)} %convert_element_type.23), channel_id=1, source_target_pairs={{0,12},{4,8},{8,4},{12,0},{1,13},{5,9},{9,5},{13,1},{2,14},{6,10},... | collective-permute-start | bytes 225800 | tf_op jit(solution)/shard_map/ppermute | solution.py:159
  81.2 7.9 %collective-permute-start.17 = (bf16[336,112]{1,0:T(8,128)(2,1)S(1)}, bf16[336,112]{1,0:T(8,128)(2,1)S(1)}, u32[]{:S(2)}, u32[]{:S(2)}) collective-permute-start(bf16[336,112]{1,0:T(8,128)(2,1)S(1)} %convert_element_type.23), channel_id=1, source_target_pairs={{0,8},{4,12},{8,0},{12,4},{1,9},{5,13},{9,1},{13,5},{2,10},{6,14},... | collective-permute-start | bytes 225800 | tf_op jit(solution)/shard_map/ppermute | solution.py:159
  81.7 7.4 %collective-permute-start.18 = (bf16[336,112]{1,0:T(8,128)(2,1)S(1)}, bf16[336,112]{1,0:T(8,128)(2,1)S(1)}, u32[]{:S(2)}, u32[]{:S(2)}) collective-permute-start(bf16[336,112]{1,0:T(8,128)(2,1)S(1)} %convert_element_type.23), channel_id=1, source_target_pairs={{0,4},{4,0},{8,12},{12,8},{1,5},{5,1},{9,13},{13,9},{2,6},{6,2},{1... | collective-permute-start | bytes 225800 | tf_op jit(solution)/shard_map/ppermute | solution.py:159
  83.5 6.7 %collective-permute-start.13 = (bf16[224,112]{1,0:T(8,128)(2,1)S(1)}, bf16[224,112]{1,0:T(8,128)(2,1)S(1)}, u32[]{:S(2)}, u32[]{:S(2)}) collective-permute-start(bf16[224,112]{1,0:T(8,128)(2,1)S(1)} %convert_element_type.22), channel_id=1, source_target_pairs={{0,12},{4,8},{8,4},{12,0},{1,13},{5,9},{9,5},{13,1},{2,14},{6,10},... | collective-permute-start | bytes 150536 | tf_op jit(solution)/shard_map/ppermute | solution.py:159
  85.8 4.5 %collective-permute-start.14 = (bf16[224,112]{1,0:T(8,128)(2,1)S(1)}, bf16[224,112]{1,0:T(8,128)(2,1)S(1)}, u32[]{:S(2)}, u32[]{:S(2)}) collective-permute-start(bf16[224,112]{1,0:T(8,128)(2,1)S(1)} %convert_element_type.22), channel_id=1, source_target_pairs={{0,8},{4,12},{8,0},{12,4},{1,9},{5,13},{9,1},{13,5},{2,10},{6,14},... | collective-permute-start | bytes 150536 | tf_op jit(solution)/shard_map/ppermute | solution.py:159
  86.1 4.2 %collective-permute-start.15 = (bf16[224,112]{1,0:T(8,128)(2,1)S(1)}, bf16[224,112]{1,0:T(8,128)(2,1)S(1)}, u32[]{:S(2)}, u32[]{:S(2)}) collective-permute-start(bf16[224,112]{1,0:T(8,128)(2,1)S(1)} %convert_element_type.22), channel_id=1, source_target_pairs={{0,4},{4,0},{8,12},{12,8},{1,5},{5,1},{9,13},{13,9},{2,6},{6,2},{1... | collective-permute-start | bytes 150536 | tf_op jit(solution)/shard_map/ppermute | solution.py:159

commit v19 on v16

--- a/solution.py
+++ b/solution.py
@@ -152,7 +152,7 @@
     count = lax.axis_size(axis)
     sent = value.astype(jnp.bfloat16)
     got = []
-    for step in range(count - 1, 0, -1):
+    for step in sorted(range(1, count), key=lambda step: (step != count // 2, -step)):
         pairs = [(i, (i + step) % count) for i in range(count)]
         if count & (count - 1) == 0:
             pairs = [(i, i ^ step) for i in range(count)]

time: 89.3 us -> 89.6 us (level)
  transfers between devices with their start and end apart: 16 -> 16, of which waited for: 10 -> 12; matrix products, arithmetic and copies ran while one was open for 2% -> 2% of each run, Pallas kernels for 17% -> 17%
where the time goes in v19:
time: 89.6 us; the launch traced here: 89.4 us
  starting transfers between devices  39.9 us (45%)
  waiting for transfers between devices  28.1 us (31%)
  Pallas kernels  16.1 us (18%)
  local copies, waits for them, and re-layouts  4.98 us (6%)
    ppermute x5, starting transfers between devices, partner_swap(): lax.ppermute(value, axis, [(i, i ^ 1) for i in range(lax.axis_size(axis))])  30.8 us
    ppermute x5, waiting for transfers between devices, partner_swap(): lax.ppermute(value, axis, [(i, i ^ 1) for i in range(lax.axis_size(axis))])  18.4 us
    pallas_call x2, Pallas kernels, local(): call(functools.partial(partial_kernel, stream), jax.ShapeDtypeStruct((3,...  9.47 us
    ppermute x6, waiting for transfers between devices, from_others(): got.append(lax.ppermute(sent, axis, pairs))  8.21 us
    ppermute x6, starting transfers between devices, from_others(): got.append(lax.ppermute(sent, axis, pairs))  7.19 us
    unnamed x12, local copies, waits for them, and re-layouts  3.47 us
    pallas_call x2, Pallas kernels, local(): call(state_kernel, state_type, IN_VMEM, [IN_VMEM] * 4 + [ANYWHERE] * len(...  2.43 us
    pallas_call x2, Pallas kernels, local(): call(functools.partial(read_kernel, stream, len(parts) + 1), out_type, AN...  2.28 us
  transfers between devices with their start and end apart: 16, of which 12 were waited for; matrix products, arithmetic and copies ran while one was open for 2% of the time, Pallas kernels for 17%

profile of v19, /device:TPU:0, one launch (start us, length us, event | category | flops | bytes accessed | tf_op | source)
XLA Modules:
  0.0 89.4 jit_solution(9181450886111263286)
XLA Ops:
  0.0 3.0 %collective-permute-start.1 = (bf16[2,560,512]{2,1,0:T(8,128)(2,1)}, bf16[2,560,512]{2,1,0:T(8,128)(2,1)S(1)}, u32[]{:S(2)}, u32[]{:S(2)}) collective-permute-start(bf16[2,560,512]{2,1,0:T(8,128)(2,1)} %bitcast.22), channel_id=1, source_target_pairs={{0,1},{1,0},{2,3},{3,2},{4,5},{5,4},{6,7},{7,6},{8,9},{9,8},{10,11... | collective-permute-start | bytes 3440648 | tf_op jit(solution)/shard_map/ppermute | solution.py:136
  3.0 1.3 %slice_bitcast_fusion = (bf16[560,512]{1,0:T(8,128)(2,1)S(1)}, bf16[560,512]{1,0:T(8,128)(2,1)S(1)}) fusion(bf16[2,560,512]{2,1,0:T(8,128)(2,1)} %bitcast.23), kind=kLoop, calls=%fused_computation | loop fusion | bytes 2293760 | tf_op jit(solution)/shard_map/squeeze | solution.py:190
  4.9 1.5 %collective-permute-done.5.inner_ref = bf16[560,512]{1,0:T(8,128)(2,1)S(1)} collective-permute-done((bf16[560,512]{1,0:T(8,128)(2,1)S(1)}, bf16[560,512]{1,0:T(8,128)(2,1)S(1)}, u32[]{:S(2)}, u32[]{:S(2)}) %collective-permute-start.5) | collective-permute-done | bytes 573472 | tf_op jit(solution)/shard_map/ppermute | solution.py:148
  6.4 15.0 %collective-permute-start.6 = (bf16[560,512]{1,0:T(8,128)(2,1)S(1)}, bf16[560,512]{1,0:T(8,128)(2,1)S(1)}, u32[]{:S(2)}, u32[]{:S(2)}) collective-permute-start(bf16[560,512]{1,0:T(8,128)(2,1)S(1)} %collective-permute-done.5.inner_ref), channel_id=1, source_target_pairs={{0,1},{1,0},{2,3},{3,2},{4,5},{5,4},{6,7},{7,6},{8,9},{9,8},{10,11... | collective-permute-start | bytes 1720328 | tf_op jit(solution)/shard_map/ppermute | solution.py:136
  21.4 7.9 %collective-permute-done.1.near = bf16[2,560,512]{2,1,0:T(8,128)(2,1)S(1)} collective-permute-done((bf16[2,560,512]{2,1,0:T(8,128)(2,1)}, bf16[2,560,512]{2,1,0:T(8,128)(2,1)S(1)}, u32[]{:S(2)}, u32[]{:S(2)}) %collective-permute-start.1) | collective-permute-done | bytes 1146912 | tf_op jit(solution)/shard_map/ppermute | solution.py:136
  29.5 1.7 %copy-done.1 = bf16[2240,560]{0,1:T(8,128)(2,1)S(1)} copy-done((bf16[2240,560]{0,1:T(8,128)(2,1)S(1)}, bf16[2240,560]{0,1:T(8,128)(2,1)}, u32[]{:S(2)}) %copy-start.1) | copy-done | bytes 2508824
  31.2 1.7 %copy-done.3 = bf16[2240,560]{0,1:T(8,128)(2,1)S(1)} copy-done((bf16[2240,560]{0,1:T(8,128)(2,1)S(1)}, bf16[2240,560]{0,1:T(8,128)(2,1)}, u32[]{:S(2)}) %copy-start.3) | copy-done | bytes 2508824
  33.0 0.7 shard_map.55.tie.cut
  33.7 3.7 %collective-permute-start.3 = (bf16[560,512]{1,0:T(8,128)(2,1)S(1)}, bf16[560,512]{1,0:T(8,128)(2,1)S(1)}, u32[]{:S(2)}, u32[]{:S(2)}) collective-permute-start(bf16[560,512]{1,0:T(8,128)(2,1)S(1)} %collective-permute-done.inner_ref), channel_id=1, source_target_pairs={{0,1},{1,0},{2,3},{3,2},{4,5},{5,4},{6,7},{7,6},{8,9},{9,8},{10,11... | collective-permute-start | bytes 1720328 | tf_op jit(solution)/shard_map/ppermute | solution.py:136
  37.4 4.2 %collective-permute-done.6.b2o = bf16[560,512]{1,0:T(8,128)(2,1)S(1)} collective-permute-done((bf16[560,512]{1,0:T(8,128)(2,1)S(1)}, bf16[560,512]{1,0:T(8,128)(2,1)S(1)}, u32[]{:S(2)}, u32[]{:S(2)}) %collective-permute-start.6) | collective-permute-done | bytes 573472 | tf_op jit(solution)/shard_map/ppermute | solution.py:136
  41.6 5.8 %collective-permute-start.8 = (bf16[560,512]{1,0:T(8,128)(2,1)S(1)}, bf16[560,512]{1,0:T(8,128)(2,1)S(1)}, u32[]{:S(2)}, u32[]{:S(2)}) collective-permute-start(bf16[560,512]{1,0:T(8,128)(2,1)S(1)} %collective-permute-done.4.b2i), channel_id=1, source_target_pairs={{0,1},{1,0},{2,3},{3,2},{4,5},{5,4},{6,7},{7,6},{8,9},{9,8},{10,11... | collective-permute-start | bytes 1720328 | tf_op jit(solution)/shard_map/ppermute | solution.py:136
  47.5 4.7 %shard_map.56.sums = f32[3,560,512]{2,1,0:T(8,128)S(1)} custom-call(bf16[2,560,512]{2,1,0:T(8,128)(2,1)S(1)} %bitcast.24, bf16[2,560,512]{2,1,0:T(8,128)(2,1)S(1)} %collective-permute-done.1.near, bf16[560,512]{1,0:T(8,128)(2,1)S(1)} %collective-permute-done.4.b2i, bf16[560,512]{1,0:T(8,128)(2,1)S(1)} %collective-permute-done.6.b2o, ...), custom_call_target="tpu_custom_call" | custom-call | flops 60211200 | bytes 1024 | tf_op jit(solution)/shard_map/pallas_call | solution.py:206
  52.2 1.7 %collective-permute-done.3.b2o = bf16[560,512]{1,0:T(8,128)(2,1)S(1)} collective-permute-done((bf16[560,512]{1,0:T(8,128)(2,1)S(1)}, bf16[560,512]{1,0:T(8,128)(2,1)S(1)}, u32[]{:S(2)}, u32[]{:S(2)}) %collective-permute-start.3) | collective-permute-done | bytes 573472 | tf_op jit(solution)/shard_map/ppermute | solution.py:136
  53.9 3.2 %collective-permute-start.7 = (bf16[560,512]{1,0:T(8,128)(2,1)S(1)}, bf16[560,512]{1,0:T(8,128)(2,1)S(1)}, u32[]{:S(2)}, u32[]{:S(2)}) collective-permute-start(bf16[560,512]{1,0:T(8,128)(2,1)S(1)} %collective-permute-done.2.b2i), channel_id=1, source_target_pairs={{0,1},{1,0},{2,3},{3,2},{4,5},{5,4},{6,7},{7,6},{8,9},{9,8},{10,11... | collective-permute-start | bytes 1720328 | tf_op jit(solution)/shard_map/ppermute | solution.py:136
  57.1 4.7 %shard_map.57.rest_0_.sums = f32[3,560,512]{2,1,0:T(8,128)S(1)} custom-call(bf16[2,560,512]{2,1,0:T(8,128)(2,1)S(1)} %bitcast.25, bf16[2,560,512]{2,1,0:T(8,128)(2,1)S(1)} %collective-permute-done.1.near, bf16[560,512]{1,0:T(8,128)(2,1)S(1)} %collective-permute-done.2.b2i, bf16[560,512]{1,0:T(8,128)(2,1)S(1)} %collective-permute-done.3.b2o, ...), custom_call_target="tpu_custom_call" | custom-call | flops 60211200 | bytes 1024 | tf_op jit(solution)/shard_map/pallas_call | solution.py:206
  61.9 4.3 %collective-permute-done.8.end_ref = bf16[560,512]{1,0:T(8,128)(2,1)S(1)} collective-permute-done((bf16[560,512]{1,0:T(8,128)(2,1)S(1)}, bf16[560,512]{1,0:T(8,128)(2,1)S(1)}, u32[]{:S(2)}, u32[]{:S(2)}) %collective-permute-start.8) | collective-permute-done | bytes 573472 | tf_op jit(solution)/shard_map/ppermute | solution.py:136
  66.2 1.2 %shard_map.58.tie = f32[560,112]{1,0:T(8,128)S(1)} custom-call(bf16[560,512]{1,0:T(8,128)(2,1)S(1)} %collective-permute-done.5.inner_ref, bf16[560,512]{1,0:T(8,128)(2,1)S(1)} %collective-permute-done.8.end_ref, bf16[3,560,560]{2,1,0:T(8,128)(2,1)S(1)} %shard_map.55.tie.cut, f32[3,560,512]{2,1,0:T(8,128)S(1)} %shard_map.56.sums, ...), custom_call_target="tpu_custom_call" | custom-call | flops 10035200 | bytes 1024 | tf_op jit(solution)/shard_map/pallas_call | solution.py:213
  67.4 3.0 %collective-permute-start.10 = (bf16[560,112]{1,0:T(8,128)(2,1)S(1)}, bf16[560,112]{1,0:T(8,128)(2,1)S(1)}, u32[]{:S(2)}, u32[]{:S(2)}) collective-permute-start(bf16[560,112]{1,0:T(8,128)(2,1)S(1)} %convert_element_type.15), channel_id=1, source_target_pairs={{0,12},{4,8},{8,4},{12,0},{1,13},{5,9},{9,5},{13,1},{2,14},{6,10},... | collective-permute-start | bytes 376328 | tf_op jit(solution)/shard_map/ppermute | solution.py:159
  70.4 0.5 collective-permute-start.11
  71.1 0.6 shard_map.59.rest_1_.query
  71.7 2.4 %collective-permute-done.10 = bf16[560,112]{1,0:T(8,128)(2,1)S(1)} collective-permute-done((bf16[560,112]{1,0:T(8,128)(2,1)S(1)}, bf16[560,112]{1,0:T(8,128)(2,1)S(1)}, u32[]{:S(2)}, u32[]{:S(2)}) %collective-permute-start.10) | collective-permute-done | bytes 125472 | tf_op jit(solution)/shard_map/ppermute | solution.py:159
  74.1 1.5 %collective-permute-done.11 = bf16[560,112]{1,0:T(8,128)(2,1)S(1)} collective-permute-done((bf16[560,112]{1,0:T(8,128)(2,1)S(1)}, bf16[560,112]{1,0:T(8,128)(2,1)S(1)}, u32[]{:S(2)}, u32[]{:S(2)}) %collective-permute-start.11) | collective-permute-done | bytes 125472 | tf_op jit(solution)/shard_map/ppermute | solution.py:159
  76.2 1.3 %collective-permute-start.12 = (f32[560,112]{1,0:T(8,128)S(1)}, f32[560,112]{1,0:T(8,128)S(1)}, u32[]{:S(2)}, u32[]{:S(2)}) collective-permute-start(f32[560,112]{1,0:T(8,128)S(1)} %convert_add_fusion.rest_0_.rest_1_), channel_id=1, source_target_pairs={{0,16},{1,17},{2,18},{3,19},{4,20},{5,21},{6,22},{7,23},{8,24},{9,... | collective-permute-start | bytes 752648 | tf_op jit(solution)/shard_map/ppermute | solution.py:165
  77.7 1.2 %shard_map.60.tie.rest_1_ = f32[560,112]{1,0:T(8,128)S(1)} custom-call(bf16[560,512]{1,0:T(8,128)(2,1)S(1)} %collective-permute-done.inner_ref, bf16[560,512]{1,0:T(8,128)(2,1)S(1)} %collective-permute-done.7.end_ref, bf16[3,560,560]{2,1,0:T(8,128)(2,1)S(1)} %shard_map.55.tie.cut, f32[3,560,512]{2,1,0:T(8,128)S(1)} %shard_map.57.rest_0_.sums, ...), custom_call_target="tpu_custom_call" | custom-call | flops 10035200 | bytes 1024 | tf_op jit(solution)/shard_map/pallas_call | solution.py:213
  78.9 1.8 %collective-permute-start.13 = (bf16[560,112]{1,0:T(8,128)(2,1)S(1)}, bf16[560,112]{1,0:T(8,128)(2,1)S(1)}, u32[]{:S(2)}, u32[]{:S(2)}) collective-permute-start(bf16[560,112]{1,0:T(8,128)(2,1)S(1)} %convert_element_type.19), channel_id=1, source_target_pairs={{0,8},{4,12},{8,0},{12,4},{1,9},{5,13},{9,1},{13,5},{2,10},{6,14},... | collective-permute-start | bytes 376328 | tf_op jit(solution)/shard_map/ppermute | solution.py:159
  80.7 1.4 %collective-permute-start.14 = (bf16[560,112]{1,0:T(8,128)(2,1)S(1)}, bf16[560,112]{1,0:T(8,128)(2,1)S(1)}, u32[]{:S(2)}, u32[]{:S(2)}) collective-permute-start(bf16[560,112]{1,0:T(8,128)(2,1)S(1)} %convert_element_type.19), channel_id=1, source_target_pairs={{0,12},{4,8},{8,4},{12,0},{1,13},{5,9},{9,5},{13,1},{2,14},{6,10},... | collective-permute-start | bytes 376328 | tf_op jit(solution)/shard_map/ppermute | solution.py:159
  82.6 0.6 shard_map.61.query
  83.2 1.1 %shard_map.62.rest_5_ = bf16[2,560,512]{2,1,0:T(8,128)(2,1)} custom-call(bf16[560,512]{1,0:T(8,128)(2,1)S(1)} %shard_map.59.rest_1_.query, f32[560,1]{1,0:T(8,128)S(1)} %reshape.4.gain, f32[560,112]{1,0:T(8,128)S(1)} %collective-permute-done.12.rest_0_, f32[560,112]{1,0:T(8,128)S(1)} %convert_add_fusion.rest_0_.rest_1_), custom_call_target="tpu_custom_call" | custom-call | flops 1003520 | bytes 1024 | tf_op jit(solution)/shard_map/pallas_call | solution.py:226
  84.4 1.6 %collective-permute-done.13.rest_2_ = bf16[560,112]{1,0:T(8,128)(2,1)S(1)} collective-permute-done((bf16[560,112]{1,0:T(8,128)(2,1)S(1)}, bf16[560,112]{1,0:T(8,128)(2,1)S(1)}, u32[]{:S(2)}, u32[]{:S(2)}) %collective-permute-start.13) | collective-permute-done | bytes 125472 | tf_op jit(solution)/shard_map/ppermute | solution.py:159
  86.0 1.5 %collective-permute-done.14.rest_3_ = bf16[560,112]{1,0:T(8,128)(2,1)S(1)} collective-permute-done((bf16[560,112]{1,0:T(8,128)(2,1)S(1)}, bf16[560,112]{1,0:T(8,128)(2,1)S(1)}, u32[]{:S(2)}, u32[]{:S(2)}) %collective-permute-start.14) | collective-permute-done | bytes 125472 | tf_op jit(solution)/shard_map/ppermute | solution.py:159
  87.5 0.7 collective-permute-done.15.rest_4_
  88.2 1.2 %shard_map.63 = bf16[2,560,512]{2,1,0:T(8,128)(2,1)} custom-call(bf16[560,512]{1,0:T(8,128)(2,1)S(1)} %shard_map.61.query, f32[560,1]{1,0:T(8,128)S(1)} %reshape.4.gain, f32[560,112]{1,0:T(8,128)S(1)} %collective-permute-done.12.rest_0_, f32[560,112]{1,0:T(8,128)S(1)} %shard_map.60.tie.rest_1_, ...), custom_call_target="tpu_custom_call", output_to_operand_aliasing={{}: (7, {})} | custom-call | flops 1003520 | bytes 1024 | tf_op jit(solution)/shard_map/pallas_call | solution.py:226
  (27 shorter events, 2.1 us)
Async XLA Ops:
  0.0 29.5 %copy-start = (bf16[2240,560]{0,1:T(8,128)(2,1)S(1)}, bf16[2240,560]{0,1:T(8,128)(2,1)}, u32[]{:S(2)}) copy-start(bf16[2240,560]{0,1:T(8,128)(2,1)} %param.7) | copy-start | bytes 7526404
  0.0 29.3 %collective-permute-start.1 = (bf16[2,560,512]{2,1,0:T(8,128)(2,1)}, bf16[2,560,512]{2,1,0:T(8,128)(2,1)S(1)}, u32[]{:S(2)}, u32[]{:S(2)}) collective-permute-start(bf16[2,560,512]{2,1,0:T(8,128)(2,1)} %bitcast.22), channel_id=1, source_target_pairs={{0,1},{1,0},{2,3},{3,2},{4,5},{5,4},{6,7},{7,6},{8,9},{9,8},{10,11... | collective-permute-start | bytes 3440648 | tf_op jit(solution)/shard_map/ppermute | solution.py:136
  4.3 2.0 %collective-permute-start.5 = (bf16[560,512]{1,0:T(8,128)(2,1)S(1)}, bf16[560,512]{1,0:T(8,128)(2,1)S(1)}, u32[]{:S(2)}, u32[]{:S(2)}) collective-permute-start(bf16[560,512]{1,0:T(8,128)(2,1)S(1)} %get-tuple-element.21), channel_id=1, source_target_pairs={{0,16},{1,2},{2,1},{3,19},{16,0},{17,18},{18,17},{19,3},{4,20},{5,... | collective-permute-start | bytes 1720328 | tf_op jit(solution)/shard_map/ppermute | solution.py:148
  4.4 29.3 %collective-permute-start = (bf16[560,512]{1,0:T(8,128)(2,1)S(1)}, bf16[560,512]{1,0:T(8,128)(2,1)S(1)}, u32[]{:S(2)}, u32[]{:S(2)}) collective-permute-start(bf16[560,512]{1,0:T(8,128)(2,1)S(1)} %get-tuple-element.22), channel_id=1, source_target_pairs={{0,16},{1,2},{2,1},{3,19},{16,0},{17,18},{18,17},{19,3},{4,20},{5,... | collective-permute-start | bytes 1720328 | tf_op jit(solution)/shard_map/ppermute | solution.py:148
  6.4 35.2 %collective-permute-start.6 = (bf16[560,512]{1,0:T(8,128)(2,1)S(1)}, bf16[560,512]{1,0:T(8,128)(2,1)S(1)}, u32[]{:S(2)}, u32[]{:S(2)}) collective-permute-start(bf16[560,512]{1,0:T(8,128)(2,1)S(1)} %collective-permute-done.5.inner_ref), channel_id=1, source_target_pairs={{0,1},{1,0},{2,3},{3,2},{4,5},{5,4},{6,7},{7,6},{8,9},{9,8},{10,11... | collective-permute-start | bytes 1720328 | tf_op jit(solution)/shard_map/ppermute | solution.py:136
  29.4 12.2 %collective-permute-start.4 = (bf16[560,512]{1,0:T(8,128)(2,1)S(1)}, bf16[560,512]{1,0:T(8,128)(2,1)S(1)}, u32[]{:S(2)}, u32[]{:S(2)}) collective-permute-start(bf16[560,512]{1,0:T(8,128)(2,1)S(1)} %get-tuple-element.23), channel_id=1, source_target_pairs={{0,16},{1,2},{2,1},{3,19},{16,0},{17,18},{18,17},{19,3},{4,20},{5,... | collective-permute-start | bytes 1720328 | tf_op jit(solution)/shard_map/ppermute | solution.py:148
  29.5 1.7 %copy-start.1 = (bf16[2240,560]{0,1:T(8,128)(2,1)S(1)}, bf16[2240,560]{0,1:T(8,128)(2,1)}, u32[]{:S(2)}) copy-start(bf16[2240,560]{0,1:T(8,128)(2,1)} %param.8) | copy-start | bytes 7526404
  31.2 1.7 %copy-start.3 = (bf16[2240,560]{0,1:T(8,128)(2,1)S(1)}, bf16[2240,560]{0,1:T(8,128)(2,1)}, u32[]{:S(2)}) copy-start(bf16[2240,560]{0,1:T(8,128)(2,1)} %param.6) | copy-start | bytes 7526404
  33.0 14.5 %copy-start.2 = (bf16[2240,560]{0,1:T(8,128)(2,1)S(1)}, bf16[2240,560]{0,1:T(8,128)(2,1)}, u32[]{:S(2)}) copy-start(bf16[2240,560]{0,1:T(8,128)(2,1)} %param.8) | copy-start | bytes 7526404
  33.0 14.5 %copy-start.4 = (bf16[2,512,560]{1,2,0:T(8,128)(2,1)S(1)}, bf16[2,512,560]{1,2,0:T(8,128)(2,1)}, u32[]{:S(2)}) copy-start(bf16[2,512,560]{1,2,0:T(8,128)(2,1)} %param.5) | copy-start | bytes 3440644
  33.7 20.2 %collective-permute-start.3 = (bf16[560,512]{1,0:T(8,128)(2,1)S(1)}, bf16[560,512]{1,0:T(8,128)(2,1)S(1)}, u32[]{:S(2)}, u32[]{:S(2)}) collective-permute-start(bf16[560,512]{1,0:T(8,128)(2,1)S(1)} %collective-permute-done.inner_ref), channel_id=1, source_target_pairs={{0,1},{1,0},{2,3},{3,2},{4,5},{5,4},{6,7},{7,6},{8,9},{9,8},{10,11... | collective-permute-start | bytes 1720328 | tf_op jit(solution)/shard_map/ppermute | solution.py:136
  37.4 16.5 %collective-permute-start.2 = (bf16[560,512]{1,0:T(8,128)(2,1)S(1)}, bf16[560,512]{1,0:T(8,128)(2,1)S(1)}, u32[]{:S(2)}, u32[]{:S(2)}) collective-permute-start(bf16[560,512]{1,0:T(8,128)(2,1)S(1)} %get-tuple-element.24), channel_id=1, source_target_pairs={{0,16},{1,2},{2,1},{3,19},{16,0},{17,18},{18,17},{19,3},{4,20},{5,... | collective-permute-start | bytes 1720328 | tf_op jit(solution)/shard_map/ppermute | solution.py:148
  41.6 24.6 %collective-permute-start.8 = (bf16[560,512]{1,0:T(8,128)(2,1)S(1)}, bf16[560,512]{1,0:T(8,128)(2,1)S(1)}, u32[]{:S(2)}, u32[]{:S(2)}) collective-permute-start(bf16[560,512]{1,0:T(8,128)(2,1)S(1)} %collective-permute-done.4.b2i), channel_id=1, source_target_pairs={{0,1},{1,0},{2,3},{3,2},{4,5},{5,4},{6,7},{7,6},{8,9},{9,8},{10,11... | collective-permute-start | bytes 1720328 | tf_op jit(solution)/shard_map/ppermute | solution.py:136
  53.9 23.7 %collective-permute-start.7 = (bf16[560,512]{1,0:T(8,128)(2,1)S(1)}, bf16[560,512]{1,0:T(8,128)(2,1)S(1)}, u32[]{:S(2)}, u32[]{:S(2)}) collective-permute-start(bf16[560,512]{1,0:T(8,128)(2,1)S(1)} %collective-permute-done.2.b2i), channel_id=1, source_target_pairs={{0,1},{1,0},{2,3},{3,2},{4,5},{5,4},{6,7},{7,6},{8,9},{9,8},{10,11... | collective-permute-start | bytes 1720328 | tf_op jit(solution)/shard_map/ppermute | solution.py:136
  67.4 6.6 %collective-permute-start.10 = (bf16[560,112]{1,0:T(8,128)(2,1)S(1)}, bf16[560,112]{1,0:T(8,128)(2,1)S(1)}, u32[]{:S(2)}, u32[]{:S(2)}) collective-permute-start(bf16[560,112]{1,0:T(8,128)(2,1)S(1)} %convert_element_type.15), channel_id=1, source_target_pairs={{0,12},{4,8},{8,4},{12,0},{1,13},{5,9},{9,5},{13,1},{2,14},{6,10},... | collective-permute-start | bytes 376328 | tf_op jit(solution)/shard_map/ppermute | solution.py:159
  70.4 5.1 %collective-permute-start.11 = (bf16[560,112]{1,0:T(8,128)(2,1)S(1)}, bf16[560,112]{1,0:T(8,128)(2,1)S(1)}, u32[]{:S(2)}, u32[]{:S(2)}) collective-permute-start(bf16[560,112]{1,0:T(8,128)(2,1)S(1)} %convert_element_type.15), channel_id=1, source_target_pairs={{0,4},{4,0},{8,12},{12,8},{1,5},{5,1},{9,13},{13,9},{2,6},{6,2},{1... | collective-permute-start | bytes 376328 | tf_op jit(solution)/shard_map/ppermute | solution.py:159
  71.0 5.1 %collective-permute-start.9 = (bf16[560,112]{1,0:T(8,128)(2,1)S(1)}, bf16[560,112]{1,0:T(8,128)(2,1)S(1)}, u32[]{:S(2)}, u32[]{:S(2)}) collective-permute-start(bf16[560,112]{1,0:T(8,128)(2,1)S(1)} %convert_element_type.15), channel_id=1, source_target_pairs={{0,8},{4,12},{8,0},{12,4},{1,9},{5,13},{9,1},{13,5},{2,10},{6,14},... | collective-permute-start | bytes 376328 | tf_op jit(solution)/shard_map/ppermute | solution.py:159
  76.1 6.3 %copy-start.5 = (f32[560]{0:T(1024)S(1)}, f32[560]{0:T(1024)}, u32[]{:S(2)}) copy-start(f32[560]{0:T(1024)} %param.9) | copy-start | bytes 6724
  76.2 7.1 %collective-permute-start.12 = (f32[560,112]{1,0:T(8,128)S(1)}, f32[560,112]{1,0:T(8,128)S(1)}, u32[]{:S(2)}, u32[]{:S(2)}) collective-permute-start(f32[560,112]{1,0:T(8,128)S(1)} %convert_add_fusion.rest_0_.rest_1_), channel_id=1, source_target_pairs={{0,16},{1,17},{2,18},{3,19},{4,20},{5,21},{6,22},{7,23},{8,24},{9,... | collective-permute-start | bytes 752648 | tf_op jit(solution)/shard_map/ppermute | solution.py:165
  78.9 7.1 %collective-permute-start.13 = (bf16[560,112]{1,0:T(8,128)(2,1)S(1)}, bf16[560,112]{1,0:T(8,128)(2,1)S(1)}, u32[]{:S(2)}, u32[]{:S(2)}) collective-permute-start(bf16[560,112]{1,0:T(8,128)(2,1)S(1)} %convert_element_type.19), channel_id=1, source_target_pairs={{0,8},{4,12},{8,0},{12,4},{1,9},{5,13},{9,1},{13,5},{2,10},{6,14},... | collective-permute-start | bytes 376328 | tf_op jit(solution)/shard_map/ppermute | solution.py:159
  80.7 6.8 %collective-permute-start.14 = (bf16[560,112]{1,0:T(8,128)(2,1)S(1)}, bf16[560,112]{1,0:T(8,128)(2,1)S(1)}, u32[]{:S(2)}, u32[]{:S(2)}) collective-permute-start(bf16[560,112]{1,0:T(8,128)(2,1)S(1)} %convert_element_type.19), channel_id=1, source_target_pairs={{0,12},{4,8},{8,4},{12,0},{1,13},{5,9},{9,5},{13,1},{2,14},{6,10},... | collective-permute-start | bytes 376328 | tf_op jit(solution)/shard_map/ppermute | solution.py:159
  82.1 6.1 %collective-permute-start.15 = (bf16[560,112]{1,0:T(8,128)(2,1)S(1)}, bf16[560,112]{1,0:T(8,128)(2,1)S(1)}, u32[]{:S(2)}, u32[]{:S(2)}) collective-permute-start(bf16[560,112]{1,0:T(8,128)(2,1)S(1)} %convert_element_type.19), channel_id=1, source_target_pairs={{0,4},{4,0},{8,12},{12,8},{1,5},{5,1},{9,13},{13,9},{2,6},{6,2},{1... | collective-permute-start | bytes 376328 | tf_op jit(solution)/shard_map/ppermute | solution.py:159

commit v20 on v16

--- a/solution.py
+++ b/solution.py
@@ -85,36 +85,42 @@
                 cut[k] = matrix[:, owner * rows : (owner + 1) * rows]
 
 
-def on_last(inner_ref, end_ref, body):
-    for want, ref in ((True, inner_ref), (False, end_ref)):
-
-        @pl.when(is_inner(lax.axis_index("head")) == want)
-        def _(ref=ref):
-            body(ref)
-
-
-def state_kernel(inner_ref, end_ref, cut, sums, *rest):
+def on_last(columns, inner_ref, end_ref, body):
+    @pl.when(is_inner(lax.axis_index("head")))
+    def _():
+        body(inner_ref[:, columns])
+
+    @pl.when(jnp.logical_not(is_inner(lax.axis_index("head"))))
+    def _():
+        body(end_ref[...])
+
+
+def state_kernel(columns, before, inner_ref, end_ref, cut, sums, *rest):
     state = rest[-1]
 
     def body(block):
-        key = (sums[0] + rounded_dot(cut[0], block[...])).astype(jnp.bfloat16)
-        value = (sums[1] + rounded_dot(cut[1], block[...])).astype(jnp.bfloat16)
+        key = (sums[0, :, columns] + rounded_dot(cut[0], block)).astype(jnp.bfloat16)
+        value = (sums[1, :, columns] + rounded_dot(cut[1], block)).astype(jnp.bfloat16)
         key = jnp.maximum(key, 0)
         for start in range(0, key.shape[0], HEAD_DIM):
             rows = slice(start, start + HEAD_DIM)
-            state[rows, :] = lax.dot_general(
+            total = lax.dot_general(
                 value[rows], key[rows], (((1,), (1,)), ((), ())), preferred_element_type=jnp.float32
             )
-
-    on_last(inner_ref, end_ref, body)
-
-
-def query_kernel(inner_ref, end_ref, cut, sums, tie, query):
-    def body(block):
-        row = (sums[2] + rounded_dot(cut[2], block[...])).astype(jnp.bfloat16)
-        query[...] = jnp.maximum(row, 0)
-
-    on_last(inner_ref, end_ref, body)
+            state[rows, :] = total + rest[0][rows, :] if before else total
+
+    on_last(columns, inner_ref, end_ref, body)
+
+
+def query_kernel(pieces, inner_ref, *rest):
+    cut, sums, _, query = rest[-4:]
+    for columns, end_ref in zip(pieces, rest):
+
+        def body(block, columns=columns):
+            row = (sums[2, :, columns] + rounded_dot(cut[2], block)).astype(jnp.bfloat16)
+            query[:, columns] = jnp.maximum(row, 0)
+
+        on_last(columns, inner_ref, end_ref, body)
 
 
 def read_kernel(stream, parts, query, gain, *rest):
@@ -199,27 +205,34 @@
     out_type = jax.ShapeDtypeStruct((2, width, tokens), jnp.bfloat16)
 
     read_scratch = [pltpu.VMEM((width, tokens), jnp.bfloat16), pltpu.SemaphoreType.DMA((width // HEAD_DIM,))]
+    most = tokens - 128 if tokens % 128 == 0 and tokens > 128 else 0
+    pieces = ([slice(0, tokens)], [slice(a, b) for a, b in ((0, most), (most, tokens)) if b > a])
     sums = []
     for stream in range(2):
         ready, *_ = lax.optimization_barrier((far[stream], across_end[stream], *sums))
-        far_end.append(partner_swap(ready, "head"))
+        far_end.append([partner_swap(ready[:, columns], "head") for columns in pieces[stream]])
         sums.append(call(
             functools.partial(partial_kernel, stream), jax.ShapeDtypeStruct((3, width, tokens), jnp.float32), IN_VMEM,
             [ANYWHERE] * 4 + [IN_VMEM] * 3 + [ANYWHERE], [whole, sems], 3 * one,
         )(columns, near, far[stream], across_end[stream], *matrices, cut))
+    state_of = lambda stream, piece, before, ties: call(
+        functools.partial(state_kernel, pieces[stream][piece], len(before)), state_type, IN_VMEM,
+        [IN_VMEM] * (4 + len(before)) + [ANYWHERE] * len(ties), [], one // 2,
+    )(across[stream], far_end[stream][piece], cut, sums[stream], *before, *ties)
     prefix = parts = query = out = None
+    early = []
     for stream in range(2):
         ties = (sums[1],) if stream == 0 else (parts[0], query)
-        state = call(
-            state_kernel, state_type, IN_VMEM,
-            [IN_VMEM] * 4 + [ANYWHERE] * len(ties), [], one // 2,
-        )(across[stream], far_end[stream], cut, sums[stream], *ties)
+        state = state_of(stream, len(pieces[stream]) - 1, early, ties)
         query = call(
-            query_kernel, query_type, IN_VMEM, [IN_VMEM] * 4 + [ANYWHERE], [], one // 4,
-        )(across[stream], far_end[stream], cut, sums[stream], state)
+            functools.partial(query_kernel, pieces[stream]), query_type, IN_VMEM,
+            [IN_VMEM] * (3 + len(pieces[stream])) + [ANYWHERE], [], one // 4,
+        )(across[stream], *far_end[stream], cut, sums[stream], state)
         parts = [state, *from_others(state, "tok")]
         if stream == 0:
-            query, *parts = lax.optimization_barrier((query, *parts))
+            for piece in range(len(pieces[1]) - 1):
+                early = [state_of(1, piece, early, (query,))]
+            query, parts, early = lax.optimization_barrier((query, parts, early))
             parts = [sum(part.astype(jnp.float32) for part in parts)]
             prefix = entering(parts[0], "group")
         kept = [] if out is None else [out]

time: 89.3 us -> 89.2 us (level)
  waiting for transfers between devices: 27.8 us -> 24.1 us
  starting transfers between devices: 39.9 us -> 42.1 us
  Pallas kernels: 16.1 us -> 17.3 us
    ppermute x6, waiting for transfers between devices: 8.08 us -> 2.87 us  [from_others(): got.append(lax.ppermute(sent, axis, pairs))]
    ppermute x5 -> x6, starting transfers between devices: 30.8 us -> 32.9 us  [partner_swap(): lax.ppermute(value, axis, [(i, i ^ 1) for i in range(lax.axis_size(axis))])]
    ppermute x5 -> x6, waiting for transfers between devices: 18.2 us -> 19.7 us  [partner_swap(): lax.ppermute(value, axis, [(i, i ^ 1) for i in range(lax.axis_size(axis))])]
    pallas_call x4 -> x5, Pallas kernels: 3.67 us -> 4.82 us  [the longest x3 3.37 us: local(): call(functools.partial(state_kernel, pieces[stream][piece], len(before)),...]
  transfers between devices with their start and end apart: 16 -> 17, of which waited for: 10 -> 8; matrix products, arithmetic and copies ran while one was open for 2% -> 2% of each run, Pallas kernels for 17% -> 18%
where the time goes in v20:
time: 89.2 us; the launch traced here: 89 us
  starting transfers between devices  42.1 us (47%)
  waiting for transfers between devices  24.1 us (27%)
  Pallas kernels  17.3 us (19%)
  local copies, waits for them, and re-layouts  5.04 us (6%)
    ppermute x6, starting transfers between devices, partner_swap(): lax.ppermute(value, axis, [(i, i ^ 1) for i in range(lax.axis_size(axis))])  32.9 us
    ppermute x6, waiting for transfers between devices, partner_swap(): lax.ppermute(value, axis, [(i, i ^ 1) for i in range(lax.axis_size(axis))])  19.7 us
    pallas_call x2, Pallas kernels, local(): call(functools.partial(partial_kernel, stream), jax.ShapeDtypeStruct((3,...  9.47 us
    ppermute x6, starting transfers between devices, from_others(): got.append(lax.ppermute(sent, axis, pairs))  7.28 us
    unnamed x12, local copies, waits for them, and re-layouts  3.47 us
    pallas_call x3, Pallas kernels, local(): call(functools.partial(state_kernel, pieces[stream][piece], len(before)),...  3.37 us
    ppermute x6, waiting for transfers between devices, from_others(): got.append(lax.ppermute(sent, axis, pairs))  2.87 us
    pallas_call x2, Pallas kernels, local(): call(functools.partial(read_kernel, stream, len(parts) + 1), out_type, AN...  2.25 us
  transfers between devices with their start and end apart: 17, of which 8 were waited for; matrix products, arithmetic and copies ran while one was open for 2% of the time, Pallas kernels for 18%

profile of v20, /device:TPU:0, one launch (start us, length us, event | category | flops | bytes accessed | tf_op | source)
XLA Modules:
  0.0 89.0 jit_solution(1506455954168125182)
XLA Ops:
  0.0 3.0 %collective-permute-start.1 = (bf16[2,560,512]{2,1,0:T(8,128)(2,1)}, bf16[2,560,512]{2,1,0:T(8,128)(2,1)S(1)}, u32[]{:S(2)}, u32[]{:S(2)}) collective-permute-start(bf16[2,560,512]{2,1,0:T(8,128)(2,1)} %bitcast.22), channel_id=1, source_target_pairs={{0,1},{1,0},{2,3},{3,2},{4,5},{5,4},{6,7},{7,6},{8,9},{9,8},{10,11... | collective-permute-start | bytes 3440648 | tf_op jit(solution)/shard_map/ppermute | solution.py:142
  3.0 1.3 %slice_bitcast_fusion = (bf16[560,512]{1,0:T(8,128)(2,1)S(1)}, bf16[560,512]{1,0:T(8,128)(2,1)S(1)}) fusion(bf16[2,560,512]{2,1,0:T(8,128)(2,1)} %bitcast.23), kind=kLoop, calls=%fused_computation | loop fusion | bytes 2293760 | tf_op jit(solution)/shard_map/squeeze | solution.py:196
  4.9 1.5 %collective-permute-done.5.inner_ref = bf16[560,512]{1,0:T(8,128)(2,1)S(1)} collective-permute-done((bf16[560,512]{1,0:T(8,128)(2,1)S(1)}, bf16[560,512]{1,0:T(8,128)(2,1)S(1)}, u32[]{:S(2)}, u32[]{:S(2)}) %collective-permute-start.5) | collective-permute-done | bytes 573472 | tf_op jit(solution)/shard_map/ppermute | solution.py:154
  6.4 15.0 %collective-permute-start.6 = (bf16[560,512]{1,0:T(8,128)(2,1)S(1)}, bf16[560,512]{1,0:T(8,128)(2,1)S(1)}, u32[]{:S(2)}, u32[]{:S(2)}) collective-permute-start(bf16[560,512]{1,0:T(8,128)(2,1)S(1)} %collective-permute-done.5.inner_ref), channel_id=1, source_target_pairs={{0,1},{1,0},{2,3},{3,2},{4,5},{5,4},{6,7},{7,6},{8,9},{9,8},{10,11... | collective-permute-start | bytes 1720328 | tf_op jit(solution)/shard_map/ppermute | solution.py:142
  21.4 7.9 %collective-permute-done.1.near = bf16[2,560,512]{2,1,0:T(8,128)(2,1)S(1)} collective-permute-done((bf16[2,560,512]{2,1,0:T(8,128)(2,1)}, bf16[2,560,512]{2,1,0:T(8,128)(2,1)S(1)}, u32[]{:S(2)}, u32[]{:S(2)}) %collective-permute-start.1) | collective-permute-done | bytes 1146912 | tf_op jit(solution)/shard_map/ppermute | solution.py:142
  29.5 1.7 %copy-done.1 = bf16[2240,560]{0,1:T(8,128)(2,1)S(1)} copy-done((bf16[2240,560]{0,1:T(8,128)(2,1)S(1)}, bf16[2240,560]{0,1:T(8,128)(2,1)}, u32[]{:S(2)}) %copy-start.1) | copy-done | bytes 2508824
  31.2 1.7 %copy-done.3 = bf16[2240,560]{0,1:T(8,128)(2,1)S(1)} copy-done((bf16[2240,560]{0,1:T(8,128)(2,1)S(1)}, bf16[2240,560]{0,1:T(8,128)(2,1)}, u32[]{:S(2)}) %copy-start.3) | copy-done | bytes 2508824
  33.0 0.7 shard_map.55.tie.cut.rest_1_.rest_2_
  33.7 3.7 %collective-permute-start.3 = (bf16[560,512]{1,0:T(8,128)(2,1)S(1)}, bf16[560,512]{1,0:T(8,128)(2,1)S(1)}, u32[]{:S(2)}, u32[]{:S(2)}) collective-permute-start(bf16[560,512]{1,0:T(8,128)(2,1)S(1)} %collective-permute-done.inner_ref), channel_id=1, source_target_pairs={{0,1},{1,0},{2,3},{3,2},{4,5},{5,4},{6,7},{7,6},{8,9},{9,8},{10,11... | collective-permute-start | bytes 1720328 | tf_op jit(solution)/shard_map/ppermute | solution.py:142
  37.4 4.2 %collective-permute-done.6.b2o = bf16[560,512]{1,0:T(8,128)(2,1)S(1)} collective-permute-done((bf16[560,512]{1,0:T(8,128)(2,1)S(1)}, bf16[560,512]{1,0:T(8,128)(2,1)S(1)}, u32[]{:S(2)}, u32[]{:S(2)}) %collective-permute-start.6) | collective-permute-done | bytes 573472 | tf_op jit(solution)/shard_map/ppermute | solution.py:142
  41.6 5.8 %collective-permute-start.9 = (bf16[560,512]{1,0:T(8,128)(2,1)S(1)}, bf16[560,512]{1,0:T(8,128)(2,1)S(1)}, u32[]{:S(2)}, u32[]{:S(2)}) collective-permute-start(bf16[560,512]{1,0:T(8,128)(2,1)S(1)} %collective-permute-done.4.b2i), channel_id=1, source_target_pairs={{0,1},{1,0},{2,3},{3,2},{4,5},{5,4},{6,7},{7,6},{8,9},{9,8},{10,11... | collective-permute-start | bytes 1720328 | tf_op jit(solution)/shard_map/ppermute | solution.py:142
  47.5 4.7 %shard_map.56.sums.rest_2_ = f32[3,560,512]{2,1,0:T(8,128)S(1)} custom-call(bf16[2,560,512]{2,1,0:T(8,128)(2,1)S(1)} %bitcast.24, bf16[2,560,512]{2,1,0:T(8,128)(2,1)S(1)} %collective-permute-done.1.near, bf16[560,512]{1,0:T(8,128)(2,1)S(1)} %collective-permute-done.4.b2i, bf16[560,512]{1,0:T(8,128)(2,1)S(1)} %collective-permute-done.6.b2o, ...), custom_call_target="tpu_custom_call" | custom-call | flops 60211200 | bytes 1024 | tf_op jit(solution)/shard_map/pallas_call | solution.py:214
  52.2 1.7 %collective-permute-done.3.b2o = bf16[560,512]{1,0:T(8,128)(2,1)S(1)} collective-permute-done((bf16[560,512]{1,0:T(8,128)(2,1)S(1)}, bf16[560,512]{1,0:T(8,128)(2,1)S(1)}, u32[]{:S(2)}, u32[]{:S(2)}) %collective-permute-start.3) | collective-permute-done | bytes 573472 | tf_op jit(solution)/shard_map/ppermute | solution.py:142
  54.0 3.3 %collective-permute-start.7 = (bf16[560,384]{1,0:T(8,128)(2,1)S(1)}, bf16[560,384]{1,0:T(8,128)(2,1)S(1)}, u32[]{:S(2)}, u32[]{:S(2)}) collective-permute-start(bf16[560,384]{1,0:T(8,128)(2,1)S(1)} %slice.22), channel_id=1, source_target_pairs={{0,1},{1,0},{2,3},{3,2},{4,5},{5,4},{6,7},{7,6},{8,9},{9,8},{10,11... | collective-permute-start | bytes 1290248 | tf_op jit(solution)/shard_map/ppermute | solution.py:142
  57.2 4.7 %shard_map.57.rest_0_.sums.rest_3_ = f32[3,560,512]{2,1,0:T(8,128)S(1)} custom-call(bf16[2,560,512]{2,1,0:T(8,128)(2,1)S(1)} %bitcast.25, bf16[2,560,512]{2,1,0:T(8,128)(2,1)S(1)} %collective-permute-done.1.near, bf16[560,512]{1,0:T(8,128)(2,1)S(1)} %collective-permute-done.2.b2i, bf16[560,512]{1,0:T(8,128)(2,1)S(1)} %collective-permute-done.3.b2o, ...), custom_call_target="tpu_custom_call" | custom-call | flops 60211200 | bytes 1024 | tf_op jit(solution)/shard_map/pallas_call | solution.py:214
  62.0 4.2 %collective-permute-done.9.end_ref.rest_0_ = bf16[560,512]{1,0:T(8,128)(2,1)S(1)} collective-permute-done((bf16[560,512]{1,0:T(8,128)(2,1)S(1)}, bf16[560,512]{1,0:T(8,128)(2,1)S(1)}, u32[]{:S(2)}, u32[]{:S(2)}) %collective-permute-start.9) | collective-permute-done | bytes 573472 | tf_op jit(solution)/shard_map/ppermute | solution.py:142
  66.2 1.2 %shard_map.58.rest_3_ = f32[560,112]{1,0:T(8,128)S(1)} custom-call(bf16[560,512]{1,0:T(8,128)(2,1)S(1)} %collective-permute-done.5.inner_ref, bf16[560,512]{1,0:T(8,128)(2,1)S(1)} %collective-permute-done.9.end_ref.rest_0_, bf16[3,560,560]{2,1,0:T(8,128)(2,1)S(1)} %shard_map.55.tie.cut.rest_1_.rest_2_, f32[3,560,512]{2,1,0:T(8,128)S(1)} %shard_map.56.sums.rest_2_, ...), custom_call_target="tpu_custom_call" | custom-call | flops 10035200 | bytes 1024 | tf_op jit(solution)/shard_map/pallas_call | solution.py:218
  67.4 3.0 %collective-permute-start.10 = (bf16[560,112]{1,0:T(8,128)(2,1)S(1)}, bf16[560,112]{1,0:T(8,128)(2,1)S(1)}, u32[]{:S(2)}, u32[]{:S(2)}) collective-permute-start(bf16[560,112]{1,0:T(8,128)(2,1)S(1)} %convert_element_type.15), channel_id=1, source_target_pairs={{0,12},{4,8},{8,4},{12,0},{1,13},{5,9},{9,5},{13,1},{2,14},{6,10},... | collective-permute-start | bytes 376328 | tf_op jit(solution)/shard_map/ppermute | solution.py:165
  70.4 0.5 collective-permute-start.11
  71.1 2.1 %collective-permute-start.8 = (bf16[560,128]{1,0:T(8,128)(2,1)S(1)}, bf16[560,128]{1,0:T(8,128)(2,1)S(1)}, u32[]{:S(2)}, u32[]{:S(2)}) collective-permute-start(bf16[560,128]{1,0:T(8,128)(2,1)S(1)} %slice.23), channel_id=1, source_target_pairs={{0,1},{1,0},{2,3},{3,2},{4,5},{5,4},{6,7},{7,6},{8,9},{9,8},{10,11... | collective-permute-start | bytes 430088 | tf_op jit(solution)/shard_map/ppermute | solution.py:142
  73.2 0.6 shard_map.59.rest_0_.rest_2_.query
  73.8 1.6 %collective-permute-done.7.end_ref.rest_0_ = bf16[560,384]{1,0:T(8,128)(2,1)S(1)} collective-permute-done((bf16[560,384]{1,0:T(8,128)(2,1)S(1)}, bf16[560,384]{1,0:T(8,128)(2,1)S(1)}, u32[]{:S(2)}, u32[]{:S(2)}) %collective-permute-start.7) | collective-permute-done | bytes 430112 | tf_op jit(solution)/shard_map/ppermute | solution.py:142
  75.4 1.2 %shard_map.60.rest_0_ = f32[560,112]{1,0:T(8,128)S(1)} custom-call(bf16[560,512]{1,0:T(8,128)(2,1)S(1)} %collective-permute-done.inner_ref, bf16[560,384]{1,0:T(8,128)(2,1)S(1)} %collective-permute-done.7.end_ref.rest_0_, bf16[3,560,560]{2,1,0:T(8,128)(2,1)S(1)} %shard_map.55.tie.cut.rest_1_.rest_2_, f32[3,560,512]{2,1,0:T(8,128)S(1)} %shard_map.57.rest_0_.sums.rest_3_, ...), custom_call_target="tpu_custom_call" | custom-call | flops 10035200 | bytes 1024 | tf_op jit(solution)/shard_map/pallas_call | solution.py:218
  76.8 1.3 %collective-permute-start.13 = (f32[560,112]{1,0:T(8,128)S(1)}, f32[560,112]{1,0:T(8,128)S(1)}, u32[]{:S(2)}, u32[]{:S(2)}) collective-permute-start(f32[560,112]{1,0:T(8,128)S(1)} %convert_add_fusion.rest_1_), channel_id=1, source_target_pairs={{0,16},{1,17},{2,18},{3,19},{4,20},{5,21},{6,22},{7,23},{8,24},{9,... | collective-permute-start | bytes 752648 | tf_op jit(solution)/shard_map/ppermute | solution.py:171
  78.1 0.9 %shard_map.61.rest_4_.rest_1_ = f32[560,112]{1,0:T(8,128)S(1)} custom-call(bf16[560,512]{1,0:T(8,128)(2,1)S(1)} %collective-permute-done.inner_ref, bf16[560,128]{1,0:T(8,128)(2,1)S(1)} %collective-permute-done.8.end_ref.rest_1_, bf16[3,560,560]{2,1,0:T(8,128)(2,1)S(1)} %shard_map.55.tie.cut.rest_1_.rest_2_, ...), custom_call_target="tpu_custom_call" | custom-call | flops 10035200 | bytes 1024 | tf_op jit(solution)/shard_map/pallas_call | solution.py:218
  79.1 3.0 %collective-permute-start.14 = (bf16[560,112]{1,0:T(8,128)(2,1)S(1)}, bf16[560,112]{1,0:T(8,128)(2,1)S(1)}, u32[]{:S(2)}, u32[]{:S(2)}) collective-permute-start(bf16[560,112]{1,0:T(8,128)(2,1)S(1)} %convert_element_type.19), channel_id=1, source_target_pairs={{0,12},{4,8},{8,4},{12,0},{1,13},{5,9},{9,5},{13,1},{2,14},{6,10},... | collective-permute-start | bytes 376328 | tf_op jit(solution)/shard_map/ppermute | solution.py:165
  82.1 0.5 collective-permute-start.15
  82.8 0.8 shard_map.62.query
  83.7 1.1 %shard_map.63.rest_5_ = bf16[2,560,512]{2,1,0:T(8,128)(2,1)} custom-call(bf16[560,512]{1,0:T(8,128)(2,1)S(1)} %shard_map.59.rest_0_.rest_2_.query, f32[560,1]{1,0:T(8,128)S(1)} %reshape.4.gain, f32[560,112]{1,0:T(8,128)S(1)} %collective-permute-done.13.rest_0_, f32[560,112]{1,0:T(8,128)S(1)} %convert_add_fusion.rest_1_), custom_call_target="tpu_custom_call" | custom-call | flops 1003520 | bytes 1024 | tf_op jit(solution)/shard_map/pallas_call | solution.py:239
  84.8 1.9 %collective-permute-done.14.rest_2_ = bf16[560,112]{1,0:T(8,128)(2,1)S(1)} collective-permute-done((bf16[560,112]{1,0:T(8,128)(2,1)S(1)}, bf16[560,112]{1,0:T(8,128)(2,1)S(1)}, u32[]{:S(2)}, u32[]{:S(2)}) %collective-permute-start.14) | collective-permute-done | bytes 125472 | tf_op jit(solution)/shard_map/ppermute | solution.py:165
  86.7 0.9 %collective-permute-done.15.rest_3_ = bf16[560,112]{1,0:T(8,128)(2,1)S(1)} collective-permute-done((bf16[560,112]{1,0:T(8,128)(2,1)S(1)}, bf16[560,112]{1,0:T(8,128)(2,1)S(1)}, u32[]{:S(2)}, u32[]{:S(2)}) %collective-permute-start.15) | collective-permute-done | bytes 125472 | tf_op jit(solution)/shard_map/ppermute | solution.py:165
  87.7 1.1 %shard_map.64 = bf16[2,560,512]{2,1,0:T(8,128)(2,1)} custom-call(bf16[560,512]{1,0:T(8,128)(2,1)S(1)} %shard_map.62.query, f32[560,1]{1,0:T(8,128)S(1)} %reshape.4.gain, f32[560,112]{1,0:T(8,128)S(1)} %collective-permute-done.13.rest_0_, f32[560,112]{1,0:T(8,128)S(1)} %shard_map.61.rest_4_.rest_1_, ...), custom_call_target="tpu_custom_call", output_to_operand_aliasing={{}: (7, {})} | custom-call | flops 1003520 | bytes 1024 | tf_op jit(solution)/shard_map/pallas_call | solution.py:239
  (32 shorter events, 1.3 us)
Async XLA Ops:
  0.0 29.5 %copy-start = (bf16[2240,560]{0,1:T(8,128)(2,1)S(1)}, bf16[2240,560]{0,1:T(8,128)(2,1)}, u32[]{:S(2)}) copy-start(bf16[2240,560]{0,1:T(8,128)(2,1)} %param.7) | copy-start | bytes 7526404
  0.0 29.3 %collective-permute-start.1 = (bf16[2,560,512]{2,1,0:T(8,128)(2,1)}, bf16[2,560,512]{2,1,0:T(8,128)(2,1)S(1)}, u32[]{:S(2)}, u32[]{:S(2)}) collective-permute-start(bf16[2,560,512]{2,1,0:T(8,128)(2,1)} %bitcast.22), channel_id=1, source_target_pairs={{0,1},{1,0},{2,3},{3,2},{4,5},{5,4},{6,7},{7,6},{8,9},{9,8},{10,11... | collective-permute-start | bytes 3440648 | tf_op jit(solution)/shard_map/ppermute | solution.py:142
  4.3 2.0 %collective-permute-start.5 = (bf16[560,512]{1,0:T(8,128)(2,1)S(1)}, bf16[560,512]{1,0:T(8,128)(2,1)S(1)}, u32[]{:S(2)}, u32[]{:S(2)}) collective-permute-start(bf16[560,512]{1,0:T(8,128)(2,1)S(1)} %get-tuple-element.23), channel_id=1, source_target_pairs={{0,16},{1,2},{2,1},{3,19},{16,0},{17,18},{18,17},{19,3},{4,20},{5,... | collective-permute-start | bytes 1720328 | tf_op jit(solution)/shard_map/ppermute | solution.py:154
  4.4 29.3 %collective-permute-start = (bf16[560,512]{1,0:T(8,128)(2,1)S(1)}, bf16[560,512]{1,0:T(8,128)(2,1)S(1)}, u32[]{:S(2)}, u32[]{:S(2)}) collective-permute-start(bf16[560,512]{1,0:T(8,128)(2,1)S(1)} %get-tuple-element.24), channel_id=1, source_target_pairs={{0,16},{1,2},{2,1},{3,19},{16,0},{17,18},{18,17},{19,3},{4,20},{5,... | collective-permute-start | bytes 1720328 | tf_op jit(solution)/shard_map/ppermute | solution.py:154
  6.4 35.2 %collective-permute-start.6 = (bf16[560,512]{1,0:T(8,128)(2,1)S(1)}, bf16[560,512]{1,0:T(8,128)(2,1)S(1)}, u32[]{:S(2)}, u32[]{:S(2)}) collective-permute-start(bf16[560,512]{1,0:T(8,128)(2,1)S(1)} %collective-permute-done.5.inner_ref), channel_id=1, source_target_pairs={{0,1},{1,0},{2,3},{3,2},{4,5},{5,4},{6,7},{7,6},{8,9},{9,8},{10,11... | collective-permute-start | bytes 1720328 | tf_op jit(solution)/shard_map/ppermute | solution.py:142
  29.4 12.2 %collective-permute-start.4 = (bf16[560,512]{1,0:T(8,128)(2,1)S(1)}, bf16[560,512]{1,0:T(8,128)(2,1)S(1)}, u32[]{:S(2)}, u32[]{:S(2)}) collective-permute-start(bf16[560,512]{1,0:T(8,128)(2,1)S(1)} %get-tuple-element.25), channel_id=1, source_target_pairs={{0,16},{1,2},{2,1},{3,19},{16,0},{17,18},{18,17},{19,3},{4,20},{5,... | collective-permute-start | bytes 1720328 | tf_op jit(solution)/shard_map/ppermute | solution.py:154
  29.5 1.7 %copy-start.1 = (bf16[2240,560]{0,1:T(8,128)(2,1)S(1)}, bf16[2240,560]{0,1:T(8,128)(2,1)}, u32[]{:S(2)}) copy-start(bf16[2240,560]{0,1:T(8,128)(2,1)} %param.8) | copy-start | bytes 7526404
  31.2 1.7 %copy-start.3 = (bf16[2240,560]{0,1:T(8,128)(2,1)S(1)}, bf16[2240,560]{0,1:T(8,128)(2,1)}, u32[]{:S(2)}) copy-start(bf16[2240,560]{0,1:T(8,128)(2,1)} %param.6) | copy-start | bytes 7526404
  33.0 14.5 %copy-start.2 = (bf16[2240,560]{0,1:T(8,128)(2,1)S(1)}, bf16[2240,560]{0,1:T(8,128)(2,1)}, u32[]{:S(2)}) copy-start(bf16[2240,560]{0,1:T(8,128)(2,1)} %param.8) | copy-start | bytes 7526404
  33.0 14.5 %copy-start.4 = (bf16[2,512,560]{1,2,0:T(8,128)(2,1)S(1)}, bf16[2,512,560]{1,2,0:T(8,128)(2,1)}, u32[]{:S(2)}) copy-start(bf16[2,512,560]{1,2,0:T(8,128)(2,1)} %param.5) | copy-start | bytes 3440644
  33.7 20.2 %collective-permute-start.3 = (bf16[560,512]{1,0:T(8,128)(2,1)S(1)}, bf16[560,512]{1,0:T(8,128)(2,1)S(1)}, u32[]{:S(2)}, u32[]{:S(2)}) collective-permute-start(bf16[560,512]{1,0:T(8,128)(2,1)S(1)} %collective-permute-done.inner_ref), channel_id=1, source_target_pairs={{0,1},{1,0},{2,3},{3,2},{4,5},{5,4},{6,7},{7,6},{8,9},{9,8},{10,11... | collective-permute-start | bytes 1720328 | tf_op jit(solution)/shard_map/ppermute | solution.py:142
  37.4 16.5 %collective-permute-start.2 = (bf16[560,512]{1,0:T(8,128)(2,1)S(1)}, bf16[560,512]{1,0:T(8,128)(2,1)S(1)}, u32[]{:S(2)}, u32[]{:S(2)}) collective-permute-start(bf16[560,512]{1,0:T(8,128)(2,1)S(1)} %get-tuple-element.26), channel_id=1, source_target_pairs={{0,16},{1,2},{2,1},{3,19},{16,0},{17,18},{18,17},{19,3},{4,20},{5,... | collective-permute-start | bytes 1720328 | tf_op jit(solution)/shard_map/ppermute | solution.py:154
  41.6 24.6 %collective-permute-start.9 = (bf16[560,512]{1,0:T(8,128)(2,1)S(1)}, bf16[560,512]{1,0:T(8,128)(2,1)S(1)}, u32[]{:S(2)}, u32[]{:S(2)}) collective-permute-start(bf16[560,512]{1,0:T(8,128)(2,1)S(1)} %collective-permute-done.4.b2i), channel_id=1, source_target_pairs={{0,1},{1,0},{2,3},{3,2},{4,5},{5,4},{6,7},{7,6},{8,9},{9,8},{10,11... | collective-permute-start | bytes 1720328 | tf_op jit(solution)/shard_map/ppermute | solution.py:142
  54.0 21.5 %collective-permute-start.7 = (bf16[560,384]{1,0:T(8,128)(2,1)S(1)}, bf16[560,384]{1,0:T(8,128)(2,1)S(1)}, u32[]{:S(2)}, u32[]{:S(2)}) collective-permute-start(bf16[560,384]{1,0:T(8,128)(2,1)S(1)} %slice.22), channel_id=1, source_target_pairs={{0,1},{1,0},{2,3},{3,2},{4,5},{5,4},{6,7},{7,6},{8,9},{9,8},{10,11... | collective-permute-start | bytes 1290248 | tf_op jit(solution)/shard_map/ppermute | solution.py:142
  67.4 9.2 %collective-permute-start.10 = (bf16[560,112]{1,0:T(8,128)(2,1)S(1)}, bf16[560,112]{1,0:T(8,128)(2,1)S(1)}, u32[]{:S(2)}, u32[]{:S(2)}) collective-permute-start(bf16[560,112]{1,0:T(8,128)(2,1)S(1)} %convert_element_type.15), channel_id=1, source_target_pairs={{0,12},{4,8},{8,4},{12,0},{1,13},{5,9},{9,5},{13,1},{2,14},{6,10},... | collective-permute-start | bytes 376328 | tf_op jit(solution)/shard_map/ppermute | solution.py:165
  70.4 6.2 %collective-permute-start.11 = (bf16[560,112]{1,0:T(8,128)(2,1)S(1)}, bf16[560,112]{1,0:T(8,128)(2,1)S(1)}, u32[]{:S(2)}, u32[]{:S(2)}) collective-permute-start(bf16[560,112]{1,0:T(8,128)(2,1)S(1)} %convert_element_type.15), channel_id=1, source_target_pairs={{0,8},{4,12},{8,0},{12,4},{1,9},{5,13},{9,1},{13,5},{2,10},{6,14},... | collective-permute-start | bytes 376328 | tf_op jit(solution)/shard_map/ppermute | solution.py:165
  70.9 5.7 %collective-permute-start.12 = (bf16[560,112]{1,0:T(8,128)(2,1)S(1)}, bf16[560,112]{1,0:T(8,128)(2,1)S(1)}, u32[]{:S(2)}, u32[]{:S(2)}) collective-permute-start(bf16[560,112]{1,0:T(8,128)(2,1)S(1)} %convert_element_type.15), channel_id=1, source_target_pairs={{0,4},{4,0},{8,12},{12,8},{1,5},{5,1},{9,13},{13,9},{2,6},{6,2},{1... | collective-permute-start | bytes 376328 | tf_op jit(solution)/shard_map/ppermute | solution.py:165
  71.1 7.0 %collective-permute-start.8 = (bf16[560,128]{1,0:T(8,128)(2,1)S(1)}, bf16[560,128]{1,0:T(8,128)(2,1)S(1)}, u32[]{:S(2)}, u32[]{:S(2)}) collective-permute-start(bf16[560,128]{1,0:T(8,128)(2,1)S(1)} %slice.23), channel_id=1, source_target_pairs={{0,1},{1,0},{2,3},{3,2},{4,5},{5,4},{6,7},{7,6},{8,9},{9,8},{10,11... | collective-permute-start | bytes 430088 | tf_op jit(solution)/shard_map/ppermute | solution.py:142
  76.8 5.9 %copy-start.5 = (f32[560]{0:T(1024)S(1)}, f32[560]{0:T(1024)}, u32[]{:S(2)}) copy-start(f32[560]{0:T(1024)} %param.9) | copy-start | bytes 6724
  76.8 6.9 %collective-permute-start.13 = (f32[560,112]{1,0:T(8,128)S(1)}, f32[560,112]{1,0:T(8,128)S(1)}, u32[]{:S(2)}, u32[]{:S(2)}) collective-permute-start(f32[560,112]{1,0:T(8,128)S(1)} %convert_add_fusion.rest_1_), channel_id=1, source_target_pairs={{0,16},{1,17},{2,18},{3,19},{4,20},{5,21},{6,22},{7,23},{8,24},{9,... | collective-permute-start | bytes 752648 | tf_op jit(solution)/shard_map/ppermute | solution.py:171
  79.1 7.7 %collective-permute-start.14 = (bf16[560,112]{1,0:T(8,128)(2,1)S(1)}, bf16[560,112]{1,0:T(8,128)(2,1)S(1)}, u32[]{:S(2)}, u32[]{:S(2)}) collective-permute-start(bf16[560,112]{1,0:T(8,128)(2,1)S(1)} %convert_element_type.19), channel_id=1, source_target_pairs={{0,12},{4,8},{8,4},{12,0},{1,13},{5,9},{9,5},{13,1},{2,14},{6,10},... | collective-permute-start | bytes 376328 | tf_op jit(solution)/shard_map/ppermute | solution.py:165
  82.1 5.6 %collective-permute-start.15 = (bf16[560,112]{1,0:T(8,128)(2,1)S(1)}, bf16[560,112]{1,0:T(8,128)(2,1)S(1)}, u32[]{:S(2)}, u32[]{:S(2)}) collective-permute-start(bf16[560,112]{1,0:T(8,128)(2,1)S(1)} %convert_element_type.19), channel_id=1, source_target_pairs={{0,8},{4,12},{8,0},{12,4},{1,9},{5,13},{9,1},{13,5},{2,10},{6,14},... | collective-permute-start | bytes 376328 | tf_op jit(solution)/shard_map/ppermute | solution.py:165
  82.6 5.1 %collective-permute-start.16 = (bf16[560,112]{1,0:T(8,128)(2,1)S(1)}, bf16[560,112]{1,0:T(8,128)(2,1)S(1)}, u32[]{:S(2)}, u32[]{:S(2)}) collective-permute-start(bf16[560,112]{1,0:T(8,128)(2,1)S(1)} %convert_element_type.19), channel_id=1, source_target_pairs={{0,4},{4,0},{8,12},{12,8},{1,5},{5,1},{9,13},{13,9},{2,6},{6,2},{1... | collective-permute-start | bytes 376328 | tf_op jit(solution)/shard_map/ppermute | solution.py:165

commit v21 on v20

--- a/solution.py
+++ b/solution.py
@@ -128,7 +128,10 @@
     copies = []
     for start in range(0, query.shape[0], HEAD_DIM):
         rows = slice(start, start + HEAD_DIM)
-        total = sum(part[rows, :].astype(jnp.float32) for part in rest[:parts])
+        total = 0.0
+        for part in rest[:parts]:
+            terms = [part[rows, :]] if len(part.shape) == 2 else [part[k, rows, :] for k in range(part.shape[0])]
+            total += sum(term.astype(jnp.float32) for term in terms)
         reading = rounded_dot(total.astype(jnp.bfloat16), query[rows, :])
         scale = lax.rsqrt(jnp.mean(reading * reading, axis=0, keepdims=True) + 1e-06)
         held[rows, :] = (reading * scale * gain[rows, :]).astype(jnp.bfloat16)
@@ -228,8 +231,10 @@
             functools.partial(query_kernel, pieces[stream]), query_type, IN_VMEM,
             [IN_VMEM] * (3 + len(pieces[stream])) + [ANYWHERE], [], one // 4,
         )(across[stream], *far_end[stream], cut, sums[stream], state)
-        parts = [state, *from_others(state, "tok")]
-        if stream == 0:
+        if stream == 1:
+            parts = [lax.all_gather(state.astype(jnp.bfloat16), "tok")]
+        else:
+            parts = [state, *from_others(state, "tok")]
             for piece in range(len(pieces[1]) - 1):
                 early = [state_of(1, piece, early, (query,))]
             query, parts, early = lax.optimization_barrier((query, parts, early))

time: 89.2 us -> 98 us (1.099)
  blocking collectives: 0 us -> 11.1 us
  starting transfers between devices: 42.1 us -> 38.3 us
  waiting for transfers between devices: 24.1 us -> 25.8 us
    all_gather x0 -> x1, blocking collectives: none -> 11.1 us  [local(): parts = [lax.all_gather(state.astype(jnp.bfloat16), 'tok')]]
    ppermute x6, waiting for transfers between devices: 19.7 us -> 24.1 us  [partner_swap(): lax.ppermute(value, axis, [(i, i ^ 1) for i in range(lax.axis_size(axis))])]
    ppermute x6 -> x3, starting transfers between devices: 7.28 us -> 3.64 us  [from_others(): got.append(lax.ppermute(sent, axis, pairs))]
    ppermute x6 -> x3, waiting for transfers between devices: 2.87 us -> 0.24 us  [from_others(): got.append(lax.ppermute(sent, axis, pairs))]
  transfers between devices with their start and end apart: 17 -> 14, of which waited for: 8 -> 8; matrix products, arithmetic and copies ran while one was open for 2% -> 2% of each run, Pallas kernels for 18% -> 15%
where the time goes in v21:
time: 98 us; the launch traced here: 97.8 us
  starting transfers between devices  38.3 us (39%)
  waiting for transfers between devices  25.8 us (26%)
  Pallas kernels  17.1 us (17%)
  blocking collectives  11.1 us (11%)
  local copies, waits for them, and re-layouts  5.04 us (5%)
    ppermute x6, starting transfers between devices, partner_swap(): lax.ppermute(value, axis, [(i, i ^ 1) for i in range(lax.axis_size(axis))])  32.7 us
    ppermute x6, waiting for transfers between devices, partner_swap(): lax.ppermute(value, axis, [(i, i ^ 1) for i in range(lax.axis_size(axis))])  24.1 us
    all_gather x1, blocking collectives, local(): parts = [lax.all_gather(state.astype(jnp.bfloat16), 'tok')]  11.1 us
    pallas_call x2, Pallas kernels, local(): call(functools.partial(partial_kernel, stream), jax.ShapeDtypeStruct((3,...  9.47 us
    ppermute x3, starting transfers between devices, from_others(): got.append(lax.ppermute(sent, axis, pairs))  3.64 us
    unnamed x12, local copies, waits for them, and re-layouts  3.47 us
    pallas_call x3, Pallas kernels, local(): call(functools.partial(state_kernel, pieces[stream][piece], len(before)),...  3.17 us
    pallas_call x2, Pallas kernels, local(): call(functools.partial(read_kernel, stream, len(parts) + 1), out_type, AN...  2.24 us
  transfers between devices with their start and end apart: 14, of which 8 were waited for; matrix products, arithmetic and copies ran while one was open for 2% of the time, Pallas kernels for 15%

profile of v21, /device:TPU:0, one launch (start us, length us, event | category | flops | bytes accessed | tf_op | source)
XLA Modules:
  0.0 97.8 jit_solution(15759218238864102634)
XLA Ops:
  0.0 3.0 %collective-permute-start.1 = (bf16[2,560,512]{2,1,0:T(8,128)(2,1)}, bf16[2,560,512]{2,1,0:T(8,128)(2,1)S(1)}, u32[]{:S(2)}, u32[]{:S(2)}) collective-permute-start(bf16[2,560,512]{2,1,0:T(8,128)(2,1)} %bitcast.23), channel_id=1, source_target_pairs={{0,1},{1,0},{2,3},{3,2},{4,5},{5,4},{6,7},{7,6},{8,9},{9,8},{10,11... | collective-permute-start | bytes 3440648 | tf_op jit(solution)/shard_map/ppermute | solution.py:145
  3.0 1.3 %slice_bitcast_fusion = (bf16[560,512]{1,0:T(8,128)(2,1)S(1)}, bf16[560,512]{1,0:T(8,128)(2,1)S(1)}) fusion(bf16[2,560,512]{2,1,0:T(8,128)(2,1)} %bitcast.24), kind=kLoop, calls=%fused_computation | loop fusion | bytes 2293760 | tf_op jit(solution)/shard_map/squeeze | solution.py:199
  4.4 0.5 collective-permute-start
  4.9 1.5 %collective-permute-done.5.inner_ref = bf16[560,512]{1,0:T(8,128)(2,1)S(1)} collective-permute-done((bf16[560,512]{1,0:T(8,128)(2,1)S(1)}, bf16[560,512]{1,0:T(8,128)(2,1)S(1)}, u32[]{:S(2)}, u32[]{:S(2)}) %collective-permute-start.5) | collective-permute-done | bytes 573472 | tf_op jit(solution)/shard_map/ppermute | solution.py:157
  6.4 15.0 %collective-permute-start.6 = (bf16[560,512]{1,0:T(8,128)(2,1)S(1)}, bf16[560,512]{1,0:T(8,128)(2,1)S(1)}, u32[]{:S(2)}, u32[]{:S(2)}) collective-permute-start(bf16[560,512]{1,0:T(8,128)(2,1)S(1)} %collective-permute-done.5.inner_ref), channel_id=1, source_target_pairs={{0,1},{1,0},{2,3},{3,2},{4,5},{5,4},{6,7},{7,6},{8,9},{9,8},{10,11... | collective-permute-start | bytes 1720328 | tf_op jit(solution)/shard_map/ppermute | solution.py:145
  21.4 7.9 %collective-permute-done.1.near = bf16[2,560,512]{2,1,0:T(8,128)(2,1)S(1)} collective-permute-done((bf16[2,560,512]{2,1,0:T(8,128)(2,1)}, bf16[2,560,512]{2,1,0:T(8,128)(2,1)S(1)}, u32[]{:S(2)}, u32[]{:S(2)}) %collective-permute-start.1) | collective-permute-done | bytes 1146912 | tf_op jit(solution)/shard_map/ppermute | solution.py:145
  29.5 1.7 %copy-done.1 = bf16[2240,560]{0,1:T(8,128)(2,1)S(1)} copy-done((bf16[2240,560]{0,1:T(8,128)(2,1)S(1)}, bf16[2240,560]{0,1:T(8,128)(2,1)}, u32[]{:S(2)}) %copy-start.1) | copy-done | bytes 2508824
  31.2 1.7 %copy-done.3 = bf16[2240,560]{0,1:T(8,128)(2,1)S(1)} copy-done((bf16[2240,560]{0,1:T(8,128)(2,1)S(1)}, bf16[2240,560]{0,1:T(8,128)(2,1)}, u32[]{:S(2)}) %copy-start.3) | copy-done | bytes 2508824
  33.0 0.7 shard_map.55.tie.cut.rest_1_.rest_2_
  33.7 3.7 %collective-permute-start.3 = (bf16[560,512]{1,0:T(8,128)(2,1)S(1)}, bf16[560,512]{1,0:T(8,128)(2,1)S(1)}, u32[]{:S(2)}, u32[]{:S(2)}) collective-permute-start(bf16[560,512]{1,0:T(8,128)(2,1)S(1)} %collective-permute-done.inner_ref), channel_id=1, source_target_pairs={{0,1},{1,0},{2,3},{3,2},{4,5},{5,4},{6,7},{7,6},{8,9},{9,8},{10,11... | collective-permute-start | bytes 1720328 | tf_op jit(solution)/shard_map/ppermute | solution.py:145
  37.4 4.2 %collective-permute-done.6.b2o = bf16[560,512]{1,0:T(8,128)(2,1)S(1)} collective-permute-done((bf16[560,512]{1,0:T(8,128)(2,1)S(1)}, bf16[560,512]{1,0:T(8,128)(2,1)S(1)}, u32[]{:S(2)}, u32[]{:S(2)}) %collective-permute-start.6) | collective-permute-done | bytes 573472 | tf_op jit(solution)/shard_map/ppermute | solution.py:145
  41.6 5.8 %collective-permute-start.9 = (bf16[560,512]{1,0:T(8,128)(2,1)S(1)}, bf16[560,512]{1,0:T(8,128)(2,1)S(1)}, u32[]{:S(2)}, u32[]{:S(2)}) collective-permute-start(bf16[560,512]{1,0:T(8,128)(2,1)S(1)} %collective-permute-done.4.b2i), channel_id=1, source_target_pairs={{0,1},{1,0},{2,3},{3,2},{4,5},{5,4},{6,7},{7,6},{8,9},{9,8},{10,11... | collective-permute-start | bytes 1720328 | tf_op jit(solution)/shard_map/ppermute | solution.py:145
  47.5 4.7 %shard_map.56.sums.rest_2_ = f32[3,560,512]{2,1,0:T(8,128)S(1)} custom-call(bf16[2,560,512]{2,1,0:T(8,128)(2,1)S(1)} %bitcast.25, bf16[2,560,512]{2,1,0:T(8,128)(2,1)S(1)} %collective-permute-done.1.near, bf16[560,512]{1,0:T(8,128)(2,1)S(1)} %collective-permute-done.4.b2i, bf16[560,512]{1,0:T(8,128)(2,1)S(1)} %collective-permute-done.6.b2o, ...), custom_call_target="tpu_custom_call" | custom-call | flops 60211200 | bytes 1024 | tf_op jit(solution)/shard_map/pallas_call | solution.py:217
  52.2 1.7 %collective-permute-done.3.b2o = bf16[560,512]{1,0:T(8,128)(2,1)S(1)} collective-permute-done((bf16[560,512]{1,0:T(8,128)(2,1)S(1)}, bf16[560,512]{1,0:T(8,128)(2,1)S(1)}, u32[]{:S(2)}, u32[]{:S(2)}) %collective-permute-start.3) | collective-permute-done | bytes 573472 | tf_op jit(solution)/shard_map/ppermute | solution.py:145
  54.0 3.3 %collective-permute-start.7 = (bf16[560,384]{1,0:T(8,128)(2,1)S(1)}, bf16[560,384]{1,0:T(8,128)(2,1)S(1)}, u32[]{:S(2)}, u32[]{:S(2)}) collective-permute-start(bf16[560,384]{1,0:T(8,128)(2,1)S(1)} %slice.22), channel_id=1, source_target_pairs={{0,1},{1,0},{2,3},{3,2},{4,5},{5,4},{6,7},{7,6},{8,9},{9,8},{10,11... | collective-permute-start | bytes 1290248 | tf_op jit(solution)/shard_map/ppermute | solution.py:145
  57.2 4.7 %shard_map.57.rest_0_.sums.rest_3_ = f32[3,560,512]{2,1,0:T(8,128)S(1)} custom-call(bf16[2,560,512]{2,1,0:T(8,128)(2,1)S(1)} %bitcast.26, bf16[2,560,512]{2,1,0:T(8,128)(2,1)S(1)} %collective-permute-done.1.near, bf16[560,512]{1,0:T(8,128)(2,1)S(1)} %collective-permute-done.2.b2i, bf16[560,512]{1,0:T(8,128)(2,1)S(1)} %collective-permute-done.3.b2o, ...), custom_call_target="tpu_custom_call" | custom-call | flops 60211200 | bytes 1024 | tf_op jit(solution)/shard_map/pallas_call | solution.py:217
  62.0 4.2 %collective-permute-done.9.end_ref.rest_0_ = bf16[560,512]{1,0:T(8,128)(2,1)S(1)} collective-permute-done((bf16[560,512]{1,0:T(8,128)(2,1)S(1)}, bf16[560,512]{1,0:T(8,128)(2,1)S(1)}, u32[]{:S(2)}, u32[]{:S(2)}) %collective-permute-start.9) | collective-permute-done | bytes 573472 | tf_op jit(solution)/shard_map/ppermute | solution.py:145
  66.2 1.2 %shard_map.58.rest_3_ = f32[560,112]{1,0:T(8,128)S(1)} custom-call(bf16[560,512]{1,0:T(8,128)(2,1)S(1)} %collective-permute-done.5.inner_ref, bf16[560,512]{1,0:T(8,128)(2,1)S(1)} %collective-permute-done.9.end_ref.rest_0_, bf16[3,560,560]{2,1,0:T(8,128)(2,1)S(1)} %shard_map.55.tie.cut.rest_1_.rest_2_, f32[3,560,512]{2,1,0:T(8,128)S(1)} %shard_map.56.sums.rest_2_, ...), custom_call_target="tpu_custom_call" | custom-call | flops 10035200 | bytes 1024 | tf_op jit(solution)/shard_map/pallas_call | solution.py:221
  67.4 3.0 %collective-permute-start.10 = (bf16[560,112]{1,0:T(8,128)(2,1)S(1)}, bf16[560,112]{1,0:T(8,128)(2,1)S(1)}, u32[]{:S(2)}, u32[]{:S(2)}) collective-permute-start(bf16[560,112]{1,0:T(8,128)(2,1)S(1)} %convert_element_type.15), channel_id=1, source_target_pairs={{0,12},{4,8},{8,4},{12,0},{1,13},{5,9},{9,5},{13,1},{2,14},{6,10},... | collective-permute-start | bytes 376328 | tf_op jit(solution)/shard_map/ppermute | solution.py:168
  70.4 0.5 collective-permute-start.11
  71.1 0.6 shard_map.59.rest_0_.rest_2_.query
  71.7 2.9 %collective-permute-done.7.end_ref.rest_0_ = bf16[560,384]{1,0:T(8,128)(2,1)S(1)} collective-permute-done((bf16[560,384]{1,0:T(8,128)(2,1)S(1)}, bf16[560,384]{1,0:T(8,128)(2,1)S(1)}, u32[]{:S(2)}, u32[]{:S(2)}) %collective-permute-start.7) | collective-permute-done | bytes 430112 | tf_op jit(solution)/shard_map/ppermute | solution.py:145
  74.6 1.2 %shard_map.60.rest_0_ = f32[560,112]{1,0:T(8,128)S(1)} custom-call(bf16[560,512]{1,0:T(8,128)(2,1)S(1)} %collective-permute-done.inner_ref, bf16[560,384]{1,0:T(8,128)(2,1)S(1)} %collective-permute-done.7.end_ref.rest_0_, bf16[3,560,560]{2,1,0:T(8,128)(2,1)S(1)} %shard_map.55.tie.cut.rest_1_.rest_2_, f32[3,560,512]{2,1,0:T(8,128)S(1)} %shard_map.57.rest_0_.sums.rest_3_, ...), custom_call_target="tpu_custom_call" | custom-call | flops 10035200 | bytes 1024 | tf_op jit(solution)/shard_map/pallas_call | solution.py:221
  75.8 0.2 collective-permute-done.11
  76.1 1.3 %collective-permute-start.13 = (f32[560,112]{1,0:T(8,128)S(1)}, f32[560,112]{1,0:T(8,128)S(1)}, u32[]{:S(2)}, u32[]{:S(2)}) collective-permute-start(f32[560,112]{1,0:T(8,128)S(1)} %convert_add_fusion.rest_1_), channel_id=1, source_target_pairs={{0,16},{1,17},{2,18},{3,19},{4,20},{5,21},{6,22},{7,23},{8,24},{9,... | collective-permute-start | bytes 752648 | tf_op jit(solution)/shard_map/ppermute | solution.py:174
  77.5 1.9 %collective-permute-start.8 = (bf16[560,128]{1,0:T(8,128)(2,1)S(1)}, bf16[560,128]{1,0:T(8,128)(2,1)S(1)}, u32[]{:S(2)}, u32[]{:S(2)}) collective-permute-start(bf16[560,128]{1,0:T(8,128)(2,1)S(1)} %slice.23), channel_id=1, source_target_pairs={{0,1},{1,0},{2,3},{3,2},{4,5},{5,4},{6,7},{7,6},{8,9},{9,8},{10,11... | collective-permute-start | bytes 430088 | tf_op jit(solution)/shard_map/ppermute | solution.py:145
  79.5 3.2 %collective-permute-done.8.end_ref.rest_1_ = bf16[560,128]{1,0:T(8,128)(2,1)S(1)} collective-permute-done((bf16[560,128]{1,0:T(8,128)(2,1)S(1)}, bf16[560,128]{1,0:T(8,128)(2,1)S(1)}, u32[]{:S(2)}, u32[]{:S(2)}) %collective-permute-start.8) | collective-permute-done | bytes 143392 | tf_op jit(solution)/shard_map/ppermute | solution.py:145
  82.6 0.7 shard_map.61.rest_4_
  83.4 0.8 shard_map.62.query
  84.3 11.1 %all-gather = bf16[2240,112]{1,0:T(8,128)(2,1)S(1)} all-gather(bf16[560,112]{1,0:T(8,128)(2,1)S(1)} %convert_element_type.19), channel_id=2, replica_groups=mesh['group'=2,'tok'=4,'head'=4] {'tok'}, dimensions={0}, use_global_device_ids=true | all-gather | bytes 627200 | tf_op jit(solution)/shard_map/all_gather | solution.py:235
  95.4 1.1 %shard_map.63.rest_2_ = bf16[2,560,512]{2,1,0:T(8,128)(2,1)} custom-call(bf16[560,512]{1,0:T(8,128)(2,1)S(1)} %shard_map.59.rest_0_.rest_2_.query, f32[560,1]{1,0:T(8,128)S(1)} %reshape.5.gain, f32[560,112]{1,0:T(8,128)S(1)} %collective-permute-done.13.rest_0_, f32[560,112]{1,0:T(8,128)S(1)} %convert_add_fusion.rest_1_), custom_call_target="tpu_custom_call" | custom-call | flops 1003520 | bytes 1024 | tf_op jit(solution)/shard_map/pallas_call | solution.py:244
  96.5 1.1 %shard_map.64 = bf16[2,560,512]{2,1,0:T(8,128)(2,1)} custom-call(bf16[560,512]{1,0:T(8,128)(2,1)S(1)} %shard_map.62.query, f32[560,1]{1,0:T(8,128)S(1)} %reshape.5.gain, f32[560,112]{1,0:T(8,128)S(1)} %collective-permute-done.13.rest_0_, bf16[4,560,112]{2,1,0:T(8,128)(2,1)S(1)} %bitcast.27, ...), custom_call_target="tpu_custom_call", output_to_operand_aliasing={{}: (4, {})} | custom-call | flops 1003520 | bytes 1024 | tf_op jit(solution)/shard_map/pallas_call | solution.py:244
  (27 shorter events, 0.7 us)
Async XLA Ops:
  0.0 29.5 %copy-start = (bf16[2240,560]{0,1:T(8,128)(2,1)S(1)}, bf16[2240,560]{0,1:T(8,128)(2,1)}, u32[]{:S(2)}) copy-start(bf16[2240,560]{0,1:T(8,128)(2,1)} %param.7) | copy-start | bytes 7526404
  0.0 29.3 %collective-permute-start.1 = (bf16[2,560,512]{2,1,0:T(8,128)(2,1)}, bf16[2,560,512]{2,1,0:T(8,128)(2,1)S(1)}, u32[]{:S(2)}, u32[]{:S(2)}) collective-permute-start(bf16[2,560,512]{2,1,0:T(8,128)(2,1)} %bitcast.23), channel_id=1, source_target_pairs={{0,1},{1,0},{2,3},{3,2},{4,5},{5,4},{6,7},{7,6},{8,9},{9,8},{10,11... | collective-permute-start | bytes 3440648 | tf_op jit(solution)/shard_map/ppermute | solution.py:145
  4.3 2.0 %collective-permute-start.5 = (bf16[560,512]{1,0:T(8,128)(2,1)S(1)}, bf16[560,512]{1,0:T(8,128)(2,1)S(1)}, u32[]{:S(2)}, u32[]{:S(2)}) collective-permute-start(bf16[560,512]{1,0:T(8,128)(2,1)S(1)} %get-tuple-element.23), channel_id=1, source_target_pairs={{0,16},{1,2},{2,1},{3,19},{16,0},{17,18},{18,17},{19,3},{4,20},{5,... | collective-permute-start | bytes 1720328 | tf_op jit(solution)/shard_map/ppermute | solution.py:157
  4.4 29.3 %collective-permute-start = (bf16[560,512]{1,0:T(8,128)(2,1)S(1)}, bf16[560,512]{1,0:T(8,128)(2,1)S(1)}, u32[]{:S(2)}, u32[]{:S(2)}) collective-permute-start(bf16[560,512]{1,0:T(8,128)(2,1)S(1)} %get-tuple-element.24), channel_id=1, source_target_pairs={{0,16},{1,2},{2,1},{3,19},{16,0},{17,18},{18,17},{19,3},{4,20},{5,... | collective-permute-start | bytes 1720328 | tf_op jit(solution)/shard_map/ppermute | solution.py:157
  6.4 35.2 %collective-permute-start.6 = (bf16[560,512]{1,0:T(8,128)(2,1)S(1)}, bf16[560,512]{1,0:T(8,128)(2,1)S(1)}, u32[]{:S(2)}, u32[]{:S(2)}) collective-permute-start(bf16[560,512]{1,0:T(8,128)(2,1)S(1)} %collective-permute-done.5.inner_ref), channel_id=1, source_target_pairs={{0,1},{1,0},{2,3},{3,2},{4,5},{5,4},{6,7},{7,6},{8,9},{9,8},{10,11... | collective-permute-start | bytes 1720328 | tf_op jit(solution)/shard_map/ppermute | solution.py:145
  29.4 12.2 %collective-permute-start.4 = (bf16[560,512]{1,0:T(8,128)(2,1)S(1)}, bf16[560,512]{1,0:T(8,128)(2,1)S(1)}, u32[]{:S(2)}, u32[]{:S(2)}) collective-permute-start(bf16[560,512]{1,0:T(8,128)(2,1)S(1)} %get-tuple-element.25), channel_id=1, source_target_pairs={{0,16},{1,2},{2,1},{3,19},{16,0},{17,18},{18,17},{19,3},{4,20},{5,... | collective-permute-start | bytes 1720328 | tf_op jit(solution)/shard_map/ppermute | solution.py:157
  29.5 1.7 %copy-start.1 = (bf16[2240,560]{0,1:T(8,128)(2,1)S(1)}, bf16[2240,560]{0,1:T(8,128)(2,1)}, u32[]{:S(2)}) copy-start(bf16[2240,560]{0,1:T(8,128)(2,1)} %param.8) | copy-start | bytes 7526404
  31.2 1.7 %copy-start.3 = (bf16[2240,560]{0,1:T(8,128)(2,1)S(1)}, bf16[2240,560]{0,1:T(8,128)(2,1)}, u32[]{:S(2)}) copy-start(bf16[2240,560]{0,1:T(8,128)(2,1)} %param.6) | copy-start | bytes 7526404
  33.0 14.5 %copy-start.2 = (bf16[2240,560]{0,1:T(8,128)(2,1)S(1)}, bf16[2240,560]{0,1:T(8,128)(2,1)}, u32[]{:S(2)}) copy-start(bf16[2240,560]{0,1:T(8,128)(2,1)} %param.8) | copy-start | bytes 7526404
  33.0 14.5 %copy-start.4 = (bf16[2,512,560]{1,2,0:T(8,128)(2,1)S(1)}, bf16[2,512,560]{1,2,0:T(8,128)(2,1)}, u32[]{:S(2)}) copy-start(bf16[2,512,560]{1,2,0:T(8,128)(2,1)} %param.5) | copy-start | bytes 3440644
  33.7 20.2 %collective-permute-start.3 = (bf16[560,512]{1,0:T(8,128)(2,1)S(1)}, bf16[560,512]{1,0:T(8,128)(2,1)S(1)}, u32[]{:S(2)}, u32[]{:S(2)}) collective-permute-start(bf16[560,512]{1,0:T(8,128)(2,1)S(1)} %collective-permute-done.inner_ref), channel_id=1, source_target_pairs={{0,1},{1,0},{2,3},{3,2},{4,5},{5,4},{6,7},{7,6},{8,9},{9,8},{10,11... | collective-permute-start | bytes 1720328 | tf_op jit(solution)/shard_map/ppermute | solution.py:145
  37.4 16.5 %collective-permute-start.2 = (bf16[560,512]{1,0:T(8,128)(2,1)S(1)}, bf16[560,512]{1,0:T(8,128)(2,1)S(1)}, u32[]{:S(2)}, u32[]{:S(2)}) collective-permute-start(bf16[560,512]{1,0:T(8,128)(2,1)S(1)} %get-tuple-element.26), channel_id=1, source_target_pairs={{0,16},{1,2},{2,1},{3,19},{16,0},{17,18},{18,17},{19,3},{4,20},{5,... | collective-permute-start | bytes 1720328 | tf_op jit(solution)/shard_map/ppermute | solution.py:157
  41.6 24.6 %collective-permute-start.9 = (bf16[560,512]{1,0:T(8,128)(2,1)S(1)}, bf16[560,512]{1,0:T(8,128)(2,1)S(1)}, u32[]{:S(2)}, u32[]{:S(2)}) collective-permute-start(bf16[560,512]{1,0:T(8,128)(2,1)S(1)} %collective-permute-done.4.b2i), channel_id=1, source_target_pairs={{0,1},{1,0},{2,3},{3,2},{4,5},{5,4},{6,7},{7,6},{8,9},{9,8},{10,11... | collective-permute-start | bytes 1720328 | tf_op jit(solution)/shard_map/ppermute | solution.py:145
  54.0 20.6 %collective-permute-start.7 = (bf16[560,384]{1,0:T(8,128)(2,1)S(1)}, bf16[560,384]{1,0:T(8,128)(2,1)S(1)}, u32[]{:S(2)}, u32[]{:S(2)}) collective-permute-start(bf16[560,384]{1,0:T(8,128)(2,1)S(1)} %slice.22), channel_id=1, source_target_pairs={{0,1},{1,0},{2,3},{3,2},{4,5},{5,4},{6,7},{7,6},{8,9},{9,8},{10,11... | collective-permute-start | bytes 1290248 | tf_op jit(solution)/shard_map/ppermute | solution.py:145
  67.4 8.4 %collective-permute-start.10 = (bf16[560,112]{1,0:T(8,128)(2,1)S(1)}, bf16[560,112]{1,0:T(8,128)(2,1)S(1)}, u32[]{:S(2)}, u32[]{:S(2)}) collective-permute-start(bf16[560,112]{1,0:T(8,128)(2,1)S(1)} %convert_element_type.15), channel_id=1, source_target_pairs={{0,12},{4,8},{8,4},{12,0},{1,13},{5,9},{9,5},{13,1},{2,14},{6,10},... | collective-permute-start | bytes 376328 | tf_op jit(solution)/shard_map/ppermute | solution.py:168
  70.4 5.6 %collective-permute-start.11 = (bf16[560,112]{1,0:T(8,128)(2,1)S(1)}, bf16[560,112]{1,0:T(8,128)(2,1)S(1)}, u32[]{:S(2)}, u32[]{:S(2)}) collective-permute-start(bf16[560,112]{1,0:T(8,128)(2,1)S(1)} %convert_element_type.15), channel_id=1, source_target_pairs={{0,8},{4,12},{8,0},{12,4},{1,9},{5,13},{9,1},{13,5},{2,10},{6,14},... | collective-permute-start | bytes 376328 | tf_op jit(solution)/shard_map/ppermute | solution.py:168
  70.9 5.1 %collective-permute-start.12 = (bf16[560,112]{1,0:T(8,128)(2,1)S(1)}, bf16[560,112]{1,0:T(8,128)(2,1)S(1)}, u32[]{:S(2)}, u32[]{:S(2)}) collective-permute-start(bf16[560,112]{1,0:T(8,128)(2,1)S(1)} %convert_element_type.15), channel_id=1, source_target_pairs={{0,4},{4,0},{8,12},{12,8},{1,5},{5,1},{9,13},{13,9},{2,6},{6,2},{1... | collective-permute-start | bytes 376328 | tf_op jit(solution)/shard_map/ppermute | solution.py:168
  71.7 7.7 %copy-start.5 = (f32[560]{0:T(1024)S(1)}, f32[560]{0:T(1024)}, u32[]{:S(2)}) copy-start(f32[560]{0:T(1024)} %param.9) | copy-start | bytes 6724
  76.1 19.2 %collective-permute-start.13 = (f32[560,112]{1,0:T(8,128)S(1)}, f32[560,112]{1,0:T(8,128)S(1)}, u32[]{:S(2)}, u32[]{:S(2)}) collective-permute-start(f32[560,112]{1,0:T(8,128)S(1)} %convert_add_fusion.rest_1_), channel_id=1, source_target_pairs={{0,16},{1,17},{2,18},{3,19},{4,20},{5,21},{6,22},{7,23},{8,24},{9,... | collective-permute-start | bytes 752648 | tf_op jit(solution)/shard_map/ppermute | solution.py:174
  77.5 5.2 %collective-permute-start.8 = (bf16[560,128]{1,0:T(8,128)(2,1)S(1)}, bf16[560,128]{1,0:T(8,128)(2,1)S(1)}, u32[]{:S(2)}, u32[]{:S(2)}) collective-permute-start(bf16[560,128]{1,0:T(8,128)(2,1)S(1)} %slice.23), channel_id=1, source_target_pairs={{0,1},{1,0},{2,3},{3,2},{4,5},{5,4},{6,7},{7,6},{8,9},{9,8},{10,11... | collective-permute-start | bytes 430088 | tf_op jit(solution)/shard_map/ppermute | solution.py:145

commit v22 on v20

--- a/solution.py
+++ b/solution.py
@@ -205,7 +205,7 @@
     out_type = jax.ShapeDtypeStruct((2, width, tokens), jnp.bfloat16)
 
     read_scratch = [pltpu.VMEM((width, tokens), jnp.bfloat16), pltpu.SemaphoreType.DMA((width // HEAD_DIM,))]
-    most = tokens - 128 if tokens % 128 == 0 and tokens > 128 else 0
+    most = tokens // 2 if tokens % 256 == 0 else 0
     pieces = ([slice(0, tokens)], [slice(a, b) for a, b in ((0, most), (most, tokens)) if b > a])
     sums = []
     for stream in range(2):

time: 89.2 us -> 88.4 us (level)
  Pallas kernels: 17.3 us -> 16.4 us
    ppermute x6, waiting for transfers between devices: 2.87 us -> 4.66 us  [from_others(): got.append(lax.ppermute(sent, axis, pairs))]
    ppermute x6, waiting for transfers between devices: 19.7 us -> 18.3 us  [partner_swap(): lax.ppermute(value, axis, [(i, i ^ 1) for i in range(lax.axis_size(axis))])]
  transfers between devices with their start and end apart: 17 -> 17, of which waited for: 8 -> 11; matrix products, arithmetic and copies ran while one was open for 2% -> 2% of each run, Pallas kernels for 18% -> 17%
where the time goes in v22:
time: 88.4 us; the launch traced here: 88.1 us
  starting transfers between devices  42 us (48%)
  waiting for transfers between devices  24.5 us (28%)
  Pallas kernels  16.4 us (19%)
  local copies, waits for them, and re-layouts  5.01 us (6%)
    ppermute x6, starting transfers between devices, partner_swap(): lax.ppermute(value, axis, [(i, i ^ 1) for i in range(lax.axis_size(axis))])  32.8 us
    ppermute x6, waiting for transfers between devices, partner_swap(): lax.ppermute(value, axis, [(i, i ^ 1) for i in range(lax.axis_size(axis))])  18.3 us
    pallas_call x2, Pallas kernels, local(): call(functools.partial(partial_kernel, stream), jax.ShapeDtypeStruct((3,...  9.47 us
    ppermute x6, starting transfers between devices, from_others(): got.append(lax.ppermute(sent, axis, pairs))  7.19 us
    ppermute x6, waiting for transfers between devices, from_others(): got.append(lax.ppermute(sent, axis, pairs))  4.66 us
    unnamed x12, local copies, waits for them, and re-layouts  3.47 us
    pallas_call x3, Pallas kernels, local(): call(functools.partial(state_kernel, pieces[stream][piece], len(before)),...  2.7 us
    pallas_call x2, Pallas kernels, local(): call(functools.partial(read_kernel, stream, len(parts) + 1), out_type, AN...  2.25 us
  transfers between devices with their start and end apart: 17, of which 11 were waited for; matrix products, arithmetic and copies ran while one was open for 2% of the time, Pallas kernels for 17%

profile of v22, /device:TPU:0, one launch (start us, length us, event | category | flops | bytes accessed | tf_op | source)
XLA Modules:
  0.0 88.1 jit_solution(8008022330972972015)
XLA Ops:
  0.0 3.0 %collective-permute-start.1 = (bf16[2,560,512]{2,1,0:T(8,128)(2,1)}, bf16[2,560,512]{2,1,0:T(8,128)(2,1)S(1)}, u32[]{:S(2)}, u32[]{:S(2)}) collective-permute-start(bf16[2,560,512]{2,1,0:T(8,128)(2,1)} %bitcast.22), channel_id=1, source_target_pairs={{0,1},{1,0},{2,3},{3,2},{4,5},{5,4},{6,7},{7,6},{8,9},{9,8},{10,11... | collective-permute-start | bytes 3440648 | tf_op jit(solution)/shard_map/ppermute | solution.py:142
  3.0 1.3 %slice_bitcast_fusion = (bf16[560,512]{1,0:T(8,128)(2,1)S(1)}, bf16[560,512]{1,0:T(8,128)(2,1)S(1)}) fusion(bf16[2,560,512]{2,1,0:T(8,128)(2,1)} %bitcast.23), kind=kLoop, calls=%fused_computation | loop fusion | bytes 2293760 | tf_op jit(solution)/shard_map/squeeze | solution.py:196
  4.9 1.5 %collective-permute-done.5.inner_ref = bf16[560,512]{1,0:T(8,128)(2,1)S(1)} collective-permute-done((bf16[560,512]{1,0:T(8,128)(2,1)S(1)}, bf16[560,512]{1,0:T(8,128)(2,1)S(1)}, u32[]{:S(2)}, u32[]{:S(2)}) %collective-permute-start.5) | collective-permute-done | bytes 573472 | tf_op jit(solution)/shard_map/ppermute | solution.py:154
  6.4 15.0 %collective-permute-start.6 = (bf16[560,512]{1,0:T(8,128)(2,1)S(1)}, bf16[560,512]{1,0:T(8,128)(2,1)S(1)}, u32[]{:S(2)}, u32[]{:S(2)}) collective-permute-start(bf16[560,512]{1,0:T(8,128)(2,1)S(1)} %collective-permute-done.5.inner_ref), channel_id=1, source_target_pairs={{0,1},{1,0},{2,3},{3,2},{4,5},{5,4},{6,7},{7,6},{8,9},{9,8},{10,11... | collective-permute-start | bytes 1720328 | tf_op jit(solution)/shard_map/ppermute | solution.py:142
  21.4 7.9 %collective-permute-done.1.near = bf16[2,560,512]{2,1,0:T(8,128)(2,1)S(1)} collective-permute-done((bf16[2,560,512]{2,1,0:T(8,128)(2,1)}, bf16[2,560,512]{2,1,0:T(8,128)(2,1)S(1)}, u32[]{:S(2)}, u32[]{:S(2)}) %collective-permute-start.1) | collective-permute-done | bytes 1146912 | tf_op jit(solution)/shard_map/ppermute | solution.py:142
  29.5 1.7 %copy-done.1 = bf16[2240,560]{0,1:T(8,128)(2,1)S(1)} copy-done((bf16[2240,560]{0,1:T(8,128)(2,1)S(1)}, bf16[2240,560]{0,1:T(8,128)(2,1)}, u32[]{:S(2)}) %copy-start.1) | copy-done | bytes 2508824
  31.2 1.7 %copy-done.3 = bf16[2240,560]{0,1:T(8,128)(2,1)S(1)} copy-done((bf16[2240,560]{0,1:T(8,128)(2,1)S(1)}, bf16[2240,560]{0,1:T(8,128)(2,1)}, u32[]{:S(2)}) %copy-start.3) | copy-done | bytes 2508824
  33.0 0.7 shard_map.55.tie.cut.rest_1_.rest_2_
  33.7 3.7 %collective-permute-start.3 = (bf16[560,512]{1,0:T(8,128)(2,1)S(1)}, bf16[560,512]{1,0:T(8,128)(2,1)S(1)}, u32[]{:S(2)}, u32[]{:S(2)}) collective-permute-start(bf16[560,512]{1,0:T(8,128)(2,1)S(1)} %collective-permute-done.inner_ref), channel_id=1, source_target_pairs={{0,1},{1,0},{2,3},{3,2},{4,5},{5,4},{6,7},{7,6},{8,9},{9,8},{10,11... | collective-permute-start | bytes 1720328 | tf_op jit(solution)/shard_map/ppermute | solution.py:142
  37.4 4.2 %collective-permute-done.6.b2o = bf16[560,512]{1,0:T(8,128)(2,1)S(1)} collective-permute-done((bf16[560,512]{1,0:T(8,128)(2,1)S(1)}, bf16[560,512]{1,0:T(8,128)(2,1)S(1)}, u32[]{:S(2)}, u32[]{:S(2)}) %collective-permute-start.6) | collective-permute-done | bytes 573472 | tf_op jit(solution)/shard_map/ppermute | solution.py:142
  41.6 5.8 %collective-permute-start.9 = (bf16[560,512]{1,0:T(8,128)(2,1)S(1)}, bf16[560,512]{1,0:T(8,128)(2,1)S(1)}, u32[]{:S(2)}, u32[]{:S(2)}) collective-permute-start(bf16[560,512]{1,0:T(8,128)(2,1)S(1)} %collective-permute-done.4.b2i), channel_id=1, source_target_pairs={{0,1},{1,0},{2,3},{3,2},{4,5},{5,4},{6,7},{7,6},{8,9},{9,8},{10,11... | collective-permute-start | bytes 1720328 | tf_op jit(solution)/shard_map/ppermute | solution.py:142
  47.5 4.7 %shard_map.56.sums.rest_2_ = f32[3,560,512]{2,1,0:T(8,128)S(1)} custom-call(bf16[2,560,512]{2,1,0:T(8,128)(2,1)S(1)} %bitcast.24, bf16[2,560,512]{2,1,0:T(8,128)(2,1)S(1)} %collective-permute-done.1.near, bf16[560,512]{1,0:T(8,128)(2,1)S(1)} %collective-permute-done.4.b2i, bf16[560,512]{1,0:T(8,128)(2,1)S(1)} %collective-permute-done.6.b2o, ...), custom_call_target="tpu_custom_call" | custom-call | flops 60211200 | bytes 1024 | tf_op jit(solution)/shard_map/pallas_call | solution.py:214
  52.2 1.7 %collective-permute-done.3.b2o = bf16[560,512]{1,0:T(8,128)(2,1)S(1)} collective-permute-done((bf16[560,512]{1,0:T(8,128)(2,1)S(1)}, bf16[560,512]{1,0:T(8,128)(2,1)S(1)}, u32[]{:S(2)}, u32[]{:S(2)}) %collective-permute-start.3) | collective-permute-done | bytes 573472 | tf_op jit(solution)/shard_map/ppermute | solution.py:142
  54.0 3.3 %collective-permute-start.7 = (bf16[560,256]{1,0:T(8,128)(2,1)S(1)}, bf16[560,256]{1,0:T(8,128)(2,1)S(1)}, u32[]{:S(2)}, u32[]{:S(2)}) collective-permute-start(bf16[560,256]{1,0:T(8,128)(2,1)S(1)} %get-tuple-element.28), channel_id=1, source_target_pairs={{0,1},{1,0},{2,3},{3,2},{4,5},{5,4},{6,7},{7,6},{8,9},{9,8},{10,11... | collective-permute-start | bytes 860168 | tf_op jit(solution)/shard_map/ppermute | solution.py:142
  57.2 4.7 %shard_map.57.rest_0_.sums.rest_3_ = f32[3,560,512]{2,1,0:T(8,128)S(1)} custom-call(bf16[2,560,512]{2,1,0:T(8,128)(2,1)S(1)} %bitcast.25, bf16[2,560,512]{2,1,0:T(8,128)(2,1)S(1)} %collective-permute-done.1.near, bf16[560,512]{1,0:T(8,128)(2,1)S(1)} %collective-permute-done.2.b2i, bf16[560,512]{1,0:T(8,128)(2,1)S(1)} %collective-permute-done.3.b2o, ...), custom_call_target="tpu_custom_call" | custom-call | flops 60211200 | bytes 1024 | tf_op jit(solution)/shard_map/pallas_call | solution.py:214
  62.0 4.2 %collective-permute-done.9.end_ref.rest_0_ = bf16[560,512]{1,0:T(8,128)(2,1)S(1)} collective-permute-done((bf16[560,512]{1,0:T(8,128)(2,1)S(1)}, bf16[560,512]{1,0:T(8,128)(2,1)S(1)}, u32[]{:S(2)}, u32[]{:S(2)}) %collective-permute-start.9) | collective-permute-done | bytes 573472 | tf_op jit(solution)/shard_map/ppermute | solution.py:142
  66.2 1.2 %shard_map.58.rest_3_ = f32[560,112]{1,0:T(8,128)S(1)} custom-call(bf16[560,512]{1,0:T(8,128)(2,1)S(1)} %collective-permute-done.5.inner_ref, bf16[560,512]{1,0:T(8,128)(2,1)S(1)} %collective-permute-done.9.end_ref.rest_0_, bf16[3,560,560]{2,1,0:T(8,128)(2,1)S(1)} %shard_map.55.tie.cut.rest_1_.rest_2_, f32[3,560,512]{2,1,0:T(8,128)S(1)} %shard_map.56.sums.rest_2_, ...), custom_call_target="tpu_custom_call" | custom-call | flops 10035200 | bytes 1024 | tf_op jit(solution)/shard_map/pallas_call | solution.py:218
  67.4 3.0 %collective-permute-start.10 = (bf16[560,112]{1,0:T(8,128)(2,1)S(1)}, bf16[560,112]{1,0:T(8,128)(2,1)S(1)}, u32[]{:S(2)}, u32[]{:S(2)}) collective-permute-start(bf16[560,112]{1,0:T(8,128)(2,1)S(1)} %convert_element_type.15), channel_id=1, source_target_pairs={{0,12},{4,8},{8,4},{12,0},{1,13},{5,9},{9,5},{13,1},{2,14},{6,10},... | collective-permute-start | bytes 376328 | tf_op jit(solution)/shard_map/ppermute | solution.py:165
  70.4 0.5 collective-permute-start.11
  71.1 2.0 %collective-permute-start.8 = (bf16[560,256]{1,0:T(8,128)(2,1)S(1)}, bf16[560,256]{1,0:T(8,128)(2,1)S(1)}, u32[]{:S(2)}, u32[]{:S(2)}) collective-permute-start(bf16[560,256]{1,0:T(8,128)(2,1)S(1)} %get-tuple-element.27), channel_id=1, source_target_pairs={{0,1},{1,0},{2,3},{3,2},{4,5},{5,4},{6,7},{7,6},{8,9},{9,8},{10,11... | collective-permute-start | bytes 860168 | tf_op jit(solution)/shard_map/ppermute | solution.py:142
  73.1 0.6 shard_map.59.rest_0_.rest_2_.query
  73.7 0.7 shard_map.60.rest_0_
  74.9 1.1 %collective-permute-done.11 = bf16[560,112]{1,0:T(8,128)(2,1)S(1)} collective-permute-done((bf16[560,112]{1,0:T(8,128)(2,1)S(1)}, bf16[560,112]{1,0:T(8,128)(2,1)S(1)}, u32[]{:S(2)}, u32[]{:S(2)}) %collective-permute-start.11) | collective-permute-done | bytes 125472 | tf_op jit(solution)/shard_map/ppermute | solution.py:165
  76.2 1.3 %collective-permute-start.13 = (f32[560,112]{1,0:T(8,128)S(1)}, f32[560,112]{1,0:T(8,128)S(1)}, u32[]{:S(2)}, u32[]{:S(2)}) collective-permute-start(f32[560,112]{1,0:T(8,128)S(1)} %convert_add_fusion.rest_1_), channel_id=1, source_target_pairs={{0,16},{1,17},{2,18},{3,19},{4,20},{5,21},{6,22},{7,23},{8,24},{9,... | collective-permute-start | bytes 752648 | tf_op jit(solution)/shard_map/ppermute | solution.py:171
  77.7 0.7 shard_map.61.rest_4_.rest_1_
  78.5 2.9 %collective-permute-start.14 = (bf16[560,112]{1,0:T(8,128)(2,1)S(1)}, bf16[560,112]{1,0:T(8,128)(2,1)S(1)}, u32[]{:S(2)}, u32[]{:S(2)}) collective-permute-start(bf16[560,112]{1,0:T(8,128)(2,1)S(1)} %convert_element_type.19), channel_id=1, source_target_pairs={{0,12},{4,8},{8,4},{12,0},{1,13},{5,9},{9,5},{13,1},{2,14},{6,10},... | collective-permute-start | bytes 376328 | tf_op jit(solution)/shard_map/ppermute | solution.py:165
  81.4 0.5 collective-permute-start.15
  82.2 0.6 shard_map.62.query
  82.8 1.1 %shard_map.63.rest_5_ = bf16[2,560,512]{2,1,0:T(8,128)(2,1)} custom-call(bf16[560,512]{1,0:T(8,128)(2,1)S(1)} %shard_map.59.rest_0_.rest_2_.query, f32[560,1]{1,0:T(8,128)S(1)} %reshape.4.gain, f32[560,112]{1,0:T(8,128)S(1)} %collective-permute-done.13.rest_0_, f32[560,112]{1,0:T(8,128)S(1)} %convert_add_fusion.rest_1_), custom_call_target="tpu_custom_call" | custom-call | flops 1003520 | bytes 1024 | tf_op jit(solution)/shard_map/pallas_call | solution.py:239
  84.0 0.7 collective-permute-done.14.rest_2_
  84.7 1.8 %collective-permute-done.15.rest_3_ = bf16[560,112]{1,0:T(8,128)(2,1)S(1)} collective-permute-done((bf16[560,112]{1,0:T(8,128)(2,1)S(1)}, bf16[560,112]{1,0:T(8,128)(2,1)S(1)}, u32[]{:S(2)}, u32[]{:S(2)}) %collective-permute-start.15) | collective-permute-done | bytes 125472 | tf_op jit(solution)/shard_map/ppermute | solution.py:165
  87.0 1.1 %shard_map.64 = bf16[2,560,512]{2,1,0:T(8,128)(2,1)} custom-call(bf16[560,512]{1,0:T(8,128)(2,1)S(1)} %shard_map.62.query, f32[560,1]{1,0:T(8,128)S(1)} %reshape.4.gain, f32[560,112]{1,0:T(8,128)S(1)} %collective-permute-done.13.rest_0_, f32[560,112]{1,0:T(8,128)S(1)} %shard_map.61.rest_4_.rest_1_, ...), custom_call_target="tpu_custom_call", output_to_operand_aliasing={{}: (7, {})} | custom-call | flops 1003520 | bytes 1024 | tf_op jit(solution)/shard_map/pallas_call | solution.py:239
  (31 shorter events, 2.5 us)
Async XLA Ops:
  0.0 29.5 %copy-start = (bf16[2240,560]{0,1:T(8,128)(2,1)S(1)}, bf16[2240,560]{0,1:T(8,128)(2,1)}, u32[]{:S(2)}) copy-start(bf16[2240,560]{0,1:T(8,128)(2,1)} %param.7) | copy-start | bytes 7526404
  0.0 29.3 %collective-permute-start.1 = (bf16[2,560,512]{2,1,0:T(8,128)(2,1)}, bf16[2,560,512]{2,1,0:T(8,128)(2,1)S(1)}, u32[]{:S(2)}, u32[]{:S(2)}) collective-permute-start(bf16[2,560,512]{2,1,0:T(8,128)(2,1)} %bitcast.22), channel_id=1, source_target_pairs={{0,1},{1,0},{2,3},{3,2},{4,5},{5,4},{6,7},{7,6},{8,9},{9,8},{10,11... | collective-permute-start | bytes 3440648 | tf_op jit(solution)/shard_map/ppermute | solution.py:142
  4.3 2.0 %collective-permute-start.5 = (bf16[560,512]{1,0:T(8,128)(2,1)S(1)}, bf16[560,512]{1,0:T(8,128)(2,1)S(1)}, u32[]{:S(2)}, u32[]{:S(2)}) collective-permute-start(bf16[560,512]{1,0:T(8,128)(2,1)S(1)} %get-tuple-element.23), channel_id=1, source_target_pairs={{0,16},{1,2},{2,1},{3,19},{16,0},{17,18},{18,17},{19,3},{4,20},{5,... | collective-permute-start | bytes 1720328 | tf_op jit(solution)/shard_map/ppermute | solution.py:154
  4.4 29.3 %collective-permute-start = (bf16[560,512]{1,0:T(8,128)(2,1)S(1)}, bf16[560,512]{1,0:T(8,128)(2,1)S(1)}, u32[]{:S(2)}, u32[]{:S(2)}) collective-permute-start(bf16[560,512]{1,0:T(8,128)(2,1)S(1)} %get-tuple-element.24), channel_id=1, source_target_pairs={{0,16},{1,2},{2,1},{3,19},{16,0},{17,18},{18,17},{19,3},{4,20},{5,... | collective-permute-start | bytes 1720328 | tf_op jit(solution)/shard_map/ppermute | solution.py:154
  6.4 35.2 %collective-permute-start.6 = (bf16[560,512]{1,0:T(8,128)(2,1)S(1)}, bf16[560,512]{1,0:T(8,128)(2,1)S(1)}, u32[]{:S(2)}, u32[]{:S(2)}) collective-permute-start(bf16[560,512]{1,0:T(8,128)(2,1)S(1)} %collective-permute-done.5.inner_ref), channel_id=1, source_target_pairs={{0,1},{1,0},{2,3},{3,2},{4,5},{5,4},{6,7},{7,6},{8,9},{9,8},{10,11... | collective-permute-start | bytes 1720328 | tf_op jit(solution)/shard_map/ppermute | solution.py:142
  29.4 12.2 %collective-permute-start.4 = (bf16[560,512]{1,0:T(8,128)(2,1)S(1)}, bf16[560,512]{1,0:T(8,128)(2,1)S(1)}, u32[]{:S(2)}, u32[]{:S(2)}) collective-permute-start(bf16[560,512]{1,0:T(8,128)(2,1)S(1)} %get-tuple-element.25), channel_id=1, source_target_pairs={{0,16},{1,2},{2,1},{3,19},{16,0},{17,18},{18,17},{19,3},{4,20},{5,... | collective-permute-start | bytes 1720328 | tf_op jit(solution)/shard_map/ppermute | solution.py:154
  29.5 1.7 %copy-start.1 = (bf16[2240,560]{0,1:T(8,128)(2,1)S(1)}, bf16[2240,560]{0,1:T(8,128)(2,1)}, u32[]{:S(2)}) copy-start(bf16[2240,560]{0,1:T(8,128)(2,1)} %param.8) | copy-start | bytes 7526404
  31.2 1.7 %copy-start.3 = (bf16[2240,560]{0,1:T(8,128)(2,1)S(1)}, bf16[2240,560]{0,1:T(8,128)(2,1)}, u32[]{:S(2)}) copy-start(bf16[2240,560]{0,1:T(8,128)(2,1)} %param.6) | copy-start | bytes 7526404
  33.0 14.5 %copy-start.2 = (bf16[2240,560]{0,1:T(8,128)(2,1)S(1)}, bf16[2240,560]{0,1:T(8,128)(2,1)}, u32[]{:S(2)}) copy-start(bf16[2240,560]{0,1:T(8,128)(2,1)} %param.8) | copy-start | bytes 7526404
  33.0 14.5 %copy-start.4 = (bf16[2,512,560]{1,2,0:T(8,128)(2,1)S(1)}, bf16[2,512,560]{1,2,0:T(8,128)(2,1)}, u32[]{:S(2)}) copy-start(bf16[2,512,560]{1,2,0:T(8,128)(2,1)} %param.5) | copy-start | bytes 3440644
  33.7 20.2 %collective-permute-start.3 = (bf16[560,512]{1,0:T(8,128)(2,1)S(1)}, bf16[560,512]{1,0:T(8,128)(2,1)S(1)}, u32[]{:S(2)}, u32[]{:S(2)}) collective-permute-start(bf16[560,512]{1,0:T(8,128)(2,1)S(1)} %collective-permute-done.inner_ref), channel_id=1, source_target_pairs={{0,1},{1,0},{2,3},{3,2},{4,5},{5,4},{6,7},{7,6},{8,9},{9,8},{10,11... | collective-permute-start | bytes 1720328 | tf_op jit(solution)/shard_map/ppermute | solution.py:142
  37.4 16.5 %collective-permute-start.2 = (bf16[560,512]{1,0:T(8,128)(2,1)S(1)}, bf16[560,512]{1,0:T(8,128)(2,1)S(1)}, u32[]{:S(2)}, u32[]{:S(2)}) collective-permute-start(bf16[560,512]{1,0:T(8,128)(2,1)S(1)} %get-tuple-element.26), channel_id=1, source_target_pairs={{0,16},{1,2},{2,1},{3,19},{16,0},{17,18},{18,17},{19,3},{4,20},{5,... | collective-permute-start | bytes 1720328 | tf_op jit(solution)/shard_map/ppermute | solution.py:154
  41.6 24.6 %collective-permute-start.9 = (bf16[560,512]{1,0:T(8,128)(2,1)S(1)}, bf16[560,512]{1,0:T(8,128)(2,1)S(1)}, u32[]{:S(2)}, u32[]{:S(2)}) collective-permute-start(bf16[560,512]{1,0:T(8,128)(2,1)S(1)} %collective-permute-done.4.b2i), channel_id=1, source_target_pairs={{0,1},{1,0},{2,3},{3,2},{4,5},{5,4},{6,7},{7,6},{8,9},{9,8},{10,11... | collective-permute-start | bytes 1720328 | tf_op jit(solution)/shard_map/ppermute | solution.py:142
  54.0 19.7 %collective-permute-start.7 = (bf16[560,256]{1,0:T(8,128)(2,1)S(1)}, bf16[560,256]{1,0:T(8,128)(2,1)S(1)}, u32[]{:S(2)}, u32[]{:S(2)}) collective-permute-start(bf16[560,256]{1,0:T(8,128)(2,1)S(1)} %get-tuple-element.28), channel_id=1, source_target_pairs={{0,1},{1,0},{2,3},{3,2},{4,5},{5,4},{6,7},{7,6},{8,9},{9,8},{10,11... | collective-permute-start | bytes 860168 | tf_op jit(solution)/shard_map/ppermute | solution.py:142
  67.4 7.5 %collective-permute-start.10 = (bf16[560,112]{1,0:T(8,128)(2,1)S(1)}, bf16[560,112]{1,0:T(8,128)(2,1)S(1)}, u32[]{:S(2)}, u32[]{:S(2)}) collective-permute-start(bf16[560,112]{1,0:T(8,128)(2,1)S(1)} %convert_element_type.15), channel_id=1, source_target_pairs={{0,12},{4,8},{8,4},{12,0},{1,13},{5,9},{9,5},{13,1},{2,14},{6,10},... | collective-permute-start | bytes 376328 | tf_op jit(solution)/shard_map/ppermute | solution.py:165
  70.4 5.6 %collective-permute-start.11 = (bf16[560,112]{1,0:T(8,128)(2,1)S(1)}, bf16[560,112]{1,0:T(8,128)(2,1)S(1)}, u32[]{:S(2)}, u32[]{:S(2)}) collective-permute-start(bf16[560,112]{1,0:T(8,128)(2,1)S(1)} %convert_element_type.15), channel_id=1, source_target_pairs={{0,8},{4,12},{8,0},{12,4},{1,9},{5,13},{9,1},{13,5},{2,10},{6,14},... | collective-permute-start | bytes 376328 | tf_op jit(solution)/shard_map/ppermute | solution.py:165
  70.9 5.1 %collective-permute-start.12 = (bf16[560,112]{1,0:T(8,128)(2,1)S(1)}, bf16[560,112]{1,0:T(8,128)(2,1)S(1)}, u32[]{:S(2)}, u32[]{:S(2)}) collective-permute-start(bf16[560,112]{1,0:T(8,128)(2,1)S(1)} %convert_element_type.15), channel_id=1, source_target_pairs={{0,4},{4,0},{8,12},{12,8},{1,5},{5,1},{9,13},{13,9},{2,6},{6,2},{1... | collective-permute-start | bytes 376328 | tf_op jit(solution)/shard_map/ppermute | solution.py:165
  71.1 6.6 %collective-permute-start.8 = (bf16[560,256]{1,0:T(8,128)(2,1)S(1)}, bf16[560,256]{1,0:T(8,128)(2,1)S(1)}, u32[]{:S(2)}, u32[]{:S(2)}) collective-permute-start(bf16[560,256]{1,0:T(8,128)(2,1)S(1)} %get-tuple-element.27), channel_id=1, source_target_pairs={{0,1},{1,0},{2,3},{3,2},{4,5},{5,4},{6,7},{7,6},{8,9},{9,8},{10,11... | collective-permute-start | bytes 860168 | tf_op jit(solution)/shard_map/ppermute | solution.py:142
  76.1 5.9 %copy-start.5 = (f32[560]{0:T(1024)S(1)}, f32[560]{0:T(1024)}, u32[]{:S(2)}) copy-start(f32[560]{0:T(1024)} %param.9) | copy-start | bytes 6724
  76.2 6.7 %collective-permute-start.13 = (f32[560,112]{1,0:T(8,128)S(1)}, f32[560,112]{1,0:T(8,128)S(1)}, u32[]{:S(2)}, u32[]{:S(2)}) collective-permute-start(f32[560,112]{1,0:T(8,128)S(1)} %convert_add_fusion.rest_1_), channel_id=1, source_target_pairs={{0,16},{1,17},{2,18},{3,19},{4,20},{5,21},{6,22},{7,23},{8,24},{9,... | collective-permute-start | bytes 752648 | tf_op jit(solution)/shard_map/ppermute | solution.py:171
  78.5 6.2 %collective-permute-start.14 = (bf16[560,112]{1,0:T(8,128)(2,1)S(1)}, bf16[560,112]{1,0:T(8,128)(2,1)S(1)}, u32[]{:S(2)}, u32[]{:S(2)}) collective-permute-start(bf16[560,112]{1,0:T(8,128)(2,1)S(1)} %convert_element_type.19), channel_id=1, source_target_pairs={{0,12},{4,8},{8,4},{12,0},{1,13},{5,9},{9,5},{13,1},{2,14},{6,10},... | collective-permute-start | bytes 376328 | tf_op jit(solution)/shard_map/ppermute | solution.py:165
  81.4 5.1 %collective-permute-start.15 = (bf16[560,112]{1,0:T(8,128)(2,1)S(1)}, bf16[560,112]{1,0:T(8,128)(2,1)S(1)}, u32[]{:S(2)}, u32[]{:S(2)}) collective-permute-start(bf16[560,112]{1,0:T(8,128)(2,1)S(1)} %convert_element_type.19), channel_id=1, source_target_pairs={{0,8},{4,12},{8,0},{12,4},{1,9},{5,13},{9,1},{13,5},{2,10},{6,14},... | collective-permute-start | bytes 376328 | tf_op jit(solution)/shard_map/ppermute | solution.py:165
  81.9 5.1 %collective-permute-start.16 = (bf16[560,112]{1,0:T(8,128)(2,1)S(1)}, bf16[560,112]{1,0:T(8,128)(2,1)S(1)}, u32[]{:S(2)}, u32[]{:S(2)}) collective-permute-start(bf16[560,112]{1,0:T(8,128)(2,1)S(1)} %convert_element_type.19), channel_id=1, source_target_pairs={{0,4},{4,0},{8,12},{12,8},{1,5},{5,1},{9,13},{13,9},{2,6},{6,2},{1... | collective-permute-start | bytes 376328 | tf_op jit(solution)/shard_map/ppermute | solution.py:165

commit v23 on v22

--- a/solution.py
+++ b/solution.py
@@ -206,7 +206,7 @@
 
     read_scratch = [pltpu.VMEM((width, tokens), jnp.bfloat16), pltpu.SemaphoreType.DMA((width // HEAD_DIM,))]
     most = tokens // 2 if tokens % 256 == 0 else 0
-    pieces = ([slice(0, tokens)], [slice(a, b) for a, b in ((0, most), (most, tokens)) if b > a])
+    pieces = [[slice(a, b) for a, b in ((0, most), (most, tokens)) if b > a]] * 2
     sums = []
     for stream in range(2):
         ready, *_ = lax.optimization_barrier((far[stream], across_end[stream], *sums))
@@ -221,6 +221,8 @@
     )(across[stream], far_end[stream][piece], cut, sums[stream], *before, *ties)
     prefix = parts = query = out = None
     early = []
+    for piece in range(len(pieces[0]) - 1):
+        early = [state_of(0, piece, early, (sums[1],))]
     for stream in range(2):
         ties = (sums[1],) if stream == 0 else (parts[0], query)
         state = state_of(stream, len(pieces[stream]) - 1, early, ties)
@@ -230,6 +232,7 @@
         )(across[stream], *far_end[stream], cut, sums[stream], state)
         parts = [state, *from_others(state, "tok")]
         if stream == 0:
+            early = []
             for piece in range(len(pieces[1]) - 1):
                 early = [state_of(1, piece, early, (query,))]
             query, parts, early = lax.optimization_barrier((query, parts, early))

time: 88.4 us -> 88.1 us (level)
    ppermute x6 -> x7, waiting for transfers between devices: 18.3 us -> 17.8 us  [partner_swap(): lax.ppermute(value, axis, [(i, i ^ 1) for i in range(lax.axis_size(axis))])]
    pallas_call x3 -> x4, Pallas kernels: 2.7 us -> 2.98 us  [local(): call(functools.partial(state_kernel, pieces[stream][piece], len(before)),...]
    ppermute x6 -> x7, starting transfers between devices: 32.8 us -> 32.9 us  [partner_swap(): lax.ppermute(value, axis, [(i, i ^ 1) for i in range(lax.axis_size(axis))])]
  transfers between devices with their start and end apart: 17 -> 18, of which waited for: 11 -> 11; matrix products, arithmetic and copies ran while one was open for 2% -> 2% of each run, Pallas kernels for 17% -> 18%
where the time goes in v23:
time: 88.1 us; the launch traced here: 87.8 us
  starting transfers between devices  42.1 us (48%)
  waiting for transfers between devices  23.7 us (27%)
  Pallas kernels  16.7 us (19%)
  local copies, waits for them, and re-layouts  5.05 us (6%)
    ppermute x7, starting transfers between devices, partner_swap(): lax.ppermute(value, axis, [(i, i ^ 1) for i in range(lax.axis_size(axis))])  32.9 us
    ppermute x7, waiting for transfers between devices, partner_swap(): lax.ppermute(value, axis, [(i, i ^ 1) for i in range(lax.axis_size(axis))])  17.8 us
    pallas_call x2, Pallas kernels, local(): call(functools.partial(partial_kernel, stream), jax.ShapeDtypeStruct((3,...  9.47 us
    ppermute x6, starting transfers between devices, from_others(): got.append(lax.ppermute(sent, axis, pairs))  7.19 us
    ppermute x6, waiting for transfers between devices, from_others(): got.append(lax.ppermute(sent, axis, pairs))  4.42 us
    unnamed x12, local copies, waits for them, and re-layouts  3.47 us
    pallas_call x4, Pallas kernels, local(): call(functools.partial(state_kernel, pieces[stream][piece], len(before)),...  2.98 us
    pallas_call x2, Pallas kernels, local(): call(functools.partial(read_kernel, stream, len(parts) + 1), out_type, AN...  2.25 us
  transfers between devices with their start and end apart: 18, of which 11 were waited for; matrix products, arithmetic and copies ran while one was open for 2% of the time, Pallas kernels for 18%

profile of v23, /device:TPU:0, one launch (start us, length us, event | category | flops | bytes accessed | tf_op | source)
XLA Modules:
  0.0 87.8 jit_solution(2228036052917523712)
XLA Ops:
  0.0 3.0 %collective-permute-start.1 = (bf16[2,560,512]{2,1,0:T(8,128)(2,1)}, bf16[2,560,512]{2,1,0:T(8,128)(2,1)S(1)}, u32[]{:S(2)}, u32[]{:S(2)}) collective-permute-start(bf16[2,560,512]{2,1,0:T(8,128)(2,1)} %bitcast.22), channel_id=1, source_target_pairs={{0,1},{1,0},{2,3},{3,2},{4,5},{5,4},{6,7},{7,6},{8,9},{9,8},{10,11... | collective-permute-start | bytes 3440648 | tf_op jit(solution)/shard_map/ppermute | solution.py:142
  3.0 1.3 %slice_bitcast_fusion = (bf16[560,512]{1,0:T(8,128)(2,1)S(1)}, bf16[560,512]{1,0:T(8,128)(2,1)S(1)}) fusion(bf16[2,560,512]{2,1,0:T(8,128)(2,1)} %bitcast.23), kind=kLoop, calls=%fused_computation | loop fusion | bytes 2293760 | tf_op jit(solution)/shard_map/squeeze | solution.py:196
  4.9 1.5 %collective-permute-done.5.inner_ref = bf16[560,512]{1,0:T(8,128)(2,1)S(1)} collective-permute-done((bf16[560,512]{1,0:T(8,128)(2,1)S(1)}, bf16[560,512]{1,0:T(8,128)(2,1)S(1)}, u32[]{:S(2)}, u32[]{:S(2)}) %collective-permute-start.5) | collective-permute-done | bytes 573472 | tf_op jit(solution)/shard_map/ppermute | solution.py:154
  6.4 15.0 %collective-permute-start.6 = (bf16[560,512]{1,0:T(8,128)(2,1)S(1)}, bf16[560,512]{1,0:T(8,128)(2,1)S(1)}, u32[]{:S(2)}, u32[]{:S(2)}) collective-permute-start(bf16[560,512]{1,0:T(8,128)(2,1)S(1)} %collective-permute-done.5.inner_ref), channel_id=1, source_target_pairs={{0,1},{1,0},{2,3},{3,2},{4,5},{5,4},{6,7},{7,6},{8,9},{9,8},{10,11... | collective-permute-start | bytes 1720328 | tf_op jit(solution)/shard_map/ppermute | solution.py:142
  21.4 7.9 %collective-permute-done.1.near = bf16[2,560,512]{2,1,0:T(8,128)(2,1)S(1)} collective-permute-done((bf16[2,560,512]{2,1,0:T(8,128)(2,1)}, bf16[2,560,512]{2,1,0:T(8,128)(2,1)S(1)}, u32[]{:S(2)}, u32[]{:S(2)}) %collective-permute-start.1) | collective-permute-done | bytes 1146912 | tf_op jit(solution)/shard_map/ppermute | solution.py:142
  29.5 1.7 %copy-done.1 = bf16[2240,560]{0,1:T(8,128)(2,1)S(1)} copy-done((bf16[2240,560]{0,1:T(8,128)(2,1)S(1)}, bf16[2240,560]{0,1:T(8,128)(2,1)}, u32[]{:S(2)}) %copy-start.1) | copy-done | bytes 2508824
  31.2 1.7 %copy-done.3 = bf16[2240,560]{0,1:T(8,128)(2,1)S(1)} copy-done((bf16[2240,560]{0,1:T(8,128)(2,1)S(1)}, bf16[2240,560]{0,1:T(8,128)(2,1)}, u32[]{:S(2)}) %copy-start.3) | copy-done | bytes 2508824
  33.0 0.7 shard_map.55.tie.cut.rest_2_
  33.7 3.7 %collective-permute-start.3 = (bf16[560,512]{1,0:T(8,128)(2,1)S(1)}, bf16[560,512]{1,0:T(8,128)(2,1)S(1)}, u32[]{:S(2)}, u32[]{:S(2)}) collective-permute-start(bf16[560,512]{1,0:T(8,128)(2,1)S(1)} %collective-permute-done.inner_ref), channel_id=1, source_target_pairs={{0,1},{1,0},{2,3},{3,2},{4,5},{5,4},{6,7},{7,6},{8,9},{9,8},{10,11... | collective-permute-start | bytes 1720328 | tf_op jit(solution)/shard_map/ppermute | solution.py:142
  37.4 4.2 %collective-permute-done.6.b2o = bf16[560,512]{1,0:T(8,128)(2,1)S(1)} collective-permute-done((bf16[560,512]{1,0:T(8,128)(2,1)S(1)}, bf16[560,512]{1,0:T(8,128)(2,1)S(1)}, u32[]{:S(2)}, u32[]{:S(2)}) %collective-permute-start.6) | collective-permute-done | bytes 573472 | tf_op jit(solution)/shard_map/ppermute | solution.py:142
  41.7 5.9 %collective-permute-start.9 = (bf16[560,256]{1,0:T(8,128)(2,1)S(1)}, bf16[560,256]{1,0:T(8,128)(2,1)S(1)}, u32[]{:S(2)}, u32[]{:S(2)}) collective-permute-start(bf16[560,256]{1,0:T(8,128)(2,1)S(1)} %get-tuple-element.28), channel_id=1, source_target_pairs={{0,1},{1,0},{2,3},{3,2},{4,5},{5,4},{6,7},{7,6},{8,9},{9,8},{10,11... | collective-permute-start | bytes 860168 | tf_op jit(solution)/shard_map/ppermute | solution.py:142
  47.6 4.7 %shard_map.56.sums.rest_3_ = f32[3,560,512]{2,1,0:T(8,128)S(1)} custom-call(bf16[2,560,512]{2,1,0:T(8,128)(2,1)S(1)} %bitcast.24, bf16[2,560,512]{2,1,0:T(8,128)(2,1)S(1)} %collective-permute-done.1.near, bf16[560,512]{1,0:T(8,128)(2,1)S(1)} %collective-permute-done.4.b2i, bf16[560,512]{1,0:T(8,128)(2,1)S(1)} %collective-permute-done.6.b2o, ...), custom_call_target="tpu_custom_call" | custom-call | flops 60211200 | bytes 1024 | tf_op jit(solution)/shard_map/pallas_call | solution.py:214
  52.4 1.5 %collective-permute-done.3.b2o = bf16[560,512]{1,0:T(8,128)(2,1)S(1)} collective-permute-done((bf16[560,512]{1,0:T(8,128)(2,1)S(1)}, bf16[560,512]{1,0:T(8,128)(2,1)S(1)}, u32[]{:S(2)}, u32[]{:S(2)}) %collective-permute-start.3) | collective-permute-done | bytes 573472 | tf_op jit(solution)/shard_map/ppermute | solution.py:142
  54.0 3.3 %collective-permute-start.7 = (bf16[560,256]{1,0:T(8,128)(2,1)S(1)}, bf16[560,256]{1,0:T(8,128)(2,1)S(1)}, u32[]{:S(2)}, u32[]{:S(2)}) collective-permute-start(bf16[560,256]{1,0:T(8,128)(2,1)S(1)} %get-tuple-element.30), channel_id=1, source_target_pairs={{0,1},{1,0},{2,3},{3,2},{4,5},{5,4},{6,7},{7,6},{8,9},{9,8},{10,11... | collective-permute-start | bytes 860168 | tf_op jit(solution)/shard_map/ppermute | solution.py:142
  57.2 4.7 %shard_map.57.rest_0_.rest_1_.sums.rest_3_ = f32[3,560,512]{2,1,0:T(8,128)S(1)} custom-call(bf16[2,560,512]{2,1,0:T(8,128)(2,1)S(1)} %bitcast.25, bf16[2,560,512]{2,1,0:T(8,128)(2,1)S(1)} %collective-permute-done.1.near, bf16[560,512]{1,0:T(8,128)(2,1)S(1)} %collective-permute-done.2.b2i, bf16[560,512]{1,0:T(8,128)(2,1)S(1)} %collective-permute-done.3.b2o, ...), custom_call_target="tpu_custom_call" | custom-call | flops 60211200 | bytes 1024 | tf_op jit(solution)/shard_map/pallas_call | solution.py:214
  62.0 0.7 shard_map.58.rest_0_
  62.7 3.5 %collective-permute-done.10.end_ref.rest_1_ = bf16[560,256]{1,0:T(8,128)(2,1)S(1)} collective-permute-done((bf16[560,256]{1,0:T(8,128)(2,1)S(1)}, bf16[560,256]{1,0:T(8,128)(2,1)S(1)}, u32[]{:S(2)}, u32[]{:S(2)}) %collective-permute-start.10) | collective-permute-done | bytes 286752 | tf_op jit(solution)/shard_map/ppermute | solution.py:142
  66.2 0.7 shard_map.59.rest_4_
  67.0 3.0 %collective-permute-start.11 = (bf16[560,112]{1,0:T(8,128)(2,1)S(1)}, bf16[560,112]{1,0:T(8,128)(2,1)S(1)}, u32[]{:S(2)}, u32[]{:S(2)}) collective-permute-start(bf16[560,112]{1,0:T(8,128)(2,1)S(1)} %convert_element_type.15), channel_id=1, source_target_pairs={{0,12},{4,8},{8,4},{12,0},{1,13},{5,9},{9,5},{13,1},{2,14},{6,10},... | collective-permute-start | bytes 376328 | tf_op jit(solution)/shard_map/ppermute | solution.py:165
  70.6 2.0 %collective-permute-start.8 = (bf16[560,256]{1,0:T(8,128)(2,1)S(1)}, bf16[560,256]{1,0:T(8,128)(2,1)S(1)}, u32[]{:S(2)}, u32[]{:S(2)}) collective-permute-start(bf16[560,256]{1,0:T(8,128)(2,1)S(1)} %get-tuple-element.29), channel_id=1, source_target_pairs={{0,1},{1,0},{2,3},{3,2},{4,5},{5,4},{6,7},{7,6},{8,9},{9,8},{10,11... | collective-permute-start | bytes 860168 | tf_op jit(solution)/shard_map/ppermute | solution.py:142
  72.6 0.6 shard_map.60.rest_0_.rest_2_.query
  73.2 0.7 shard_map.61.rest_0_
  74.5 1.1 %collective-permute-done.12 = bf16[560,112]{1,0:T(8,128)(2,1)S(1)} collective-permute-done((bf16[560,112]{1,0:T(8,128)(2,1)S(1)}, bf16[560,112]{1,0:T(8,128)(2,1)S(1)}, u32[]{:S(2)}, u32[]{:S(2)}) %collective-permute-start.12) | collective-permute-done | bytes 125472 | tf_op jit(solution)/shard_map/ppermute | solution.py:165
  75.7 1.3 %collective-permute-start.14 = (f32[560,112]{1,0:T(8,128)S(1)}, f32[560,112]{1,0:T(8,128)S(1)}, u32[]{:S(2)}, u32[]{:S(2)}) collective-permute-start(f32[560,112]{1,0:T(8,128)S(1)} %convert_add_fusion.rest_1_), channel_id=1, source_target_pairs={{0,16},{1,17},{2,18},{3,19},{4,20},{5,21},{6,22},{7,23},{8,24},{9,... | collective-permute-start | bytes 752648 | tf_op jit(solution)/shard_map/ppermute | solution.py:171
  77.0 0.7 collective-permute-done.8.end_ref.rest_1_
  77.7 0.7 shard_map.62.rest_4_.rest_1_
  78.4 2.7 %collective-permute-start.15 = (bf16[560,112]{1,0:T(8,128)(2,1)S(1)}, bf16[560,112]{1,0:T(8,128)(2,1)S(1)}, u32[]{:S(2)}, u32[]{:S(2)}) collective-permute-start(bf16[560,112]{1,0:T(8,128)(2,1)S(1)} %convert_element_type.19), channel_id=1, source_target_pairs={{0,12},{4,8},{8,4},{12,0},{1,13},{5,9},{9,5},{13,1},{2,14},{6,10},... | collective-permute-start | bytes 376328 | tf_op jit(solution)/shard_map/ppermute | solution.py:165
  82.1 0.6 shard_map.63.query
  82.8 1.1 %shard_map.64.rest_5_ = bf16[2,560,512]{2,1,0:T(8,128)(2,1)} custom-call(bf16[560,512]{1,0:T(8,128)(2,1)S(1)} %shard_map.60.rest_0_.rest_2_.query, f32[560,1]{1,0:T(8,128)S(1)} %reshape.4.gain, f32[560,112]{1,0:T(8,128)S(1)} %collective-permute-done.14.rest_0_, f32[560,112]{1,0:T(8,128)S(1)} %convert_add_fusion.rest_1_), custom_call_target="tpu_custom_call" | custom-call | flops 1003520 | bytes 1024 | tf_op jit(solution)/shard_map/pallas_call | solution.py:242
  83.9 0.9 %collective-permute-done.15.rest_2_ = bf16[560,112]{1,0:T(8,128)(2,1)S(1)} collective-permute-done((bf16[560,112]{1,0:T(8,128)(2,1)S(1)}, bf16[560,112]{1,0:T(8,128)(2,1)S(1)}, u32[]{:S(2)}, u32[]{:S(2)}) %collective-permute-start.15) | collective-permute-done | bytes 125472 | tf_op jit(solution)/shard_map/ppermute | solution.py:165
  84.8 1.5 %collective-permute-done.16.rest_3_ = bf16[560,112]{1,0:T(8,128)(2,1)S(1)} collective-permute-done((bf16[560,112]{1,0:T(8,128)(2,1)S(1)}, bf16[560,112]{1,0:T(8,128)(2,1)S(1)}, u32[]{:S(2)}, u32[]{:S(2)}) %collective-permute-start.16) | collective-permute-done | bytes 125472 | tf_op jit(solution)/shard_map/ppermute | solution.py:165
  86.7 1.1 %shard_map.65 = bf16[2,560,512]{2,1,0:T(8,128)(2,1)} custom-call(bf16[560,512]{1,0:T(8,128)(2,1)S(1)} %shard_map.63.query, f32[560,1]{1,0:T(8,128)S(1)} %reshape.4.gain, f32[560,112]{1,0:T(8,128)S(1)} %collective-permute-done.14.rest_0_, f32[560,112]{1,0:T(8,128)S(1)} %shard_map.62.rest_4_.rest_1_, ...), custom_call_target="tpu_custom_call", output_to_operand_aliasing={{}: (7, {})} | custom-call | flops 1003520 | bytes 1024 | tf_op jit(solution)/shard_map/pallas_call | solution.py:242
  (35 shorter events, 3.5 us)
Async XLA Ops:
  0.0 29.5 %copy-start = (bf16[2240,560]{0,1:T(8,128)(2,1)S(1)}, bf16[2240,560]{0,1:T(8,128)(2,1)}, u32[]{:S(2)}) copy-start(bf16[2240,560]{0,1:T(8,128)(2,1)} %param.7) | copy-start | bytes 7526404
  0.0 29.3 %collective-permute-start.1 = (bf16[2,560,512]{2,1,0:T(8,128)(2,1)}, bf16[2,560,512]{2,1,0:T(8,128)(2,1)S(1)}, u32[]{:S(2)}, u32[]{:S(2)}) collective-permute-start(bf16[2,560,512]{2,1,0:T(8,128)(2,1)} %bitcast.22), channel_id=1, source_target_pairs={{0,1},{1,0},{2,3},{3,2},{4,5},{5,4},{6,7},{7,6},{8,9},{9,8},{10,11... | collective-permute-start | bytes 3440648 | tf_op jit(solution)/shard_map/ppermute | solution.py:142
  4.3 2.0 %collective-permute-start.5 = (bf16[560,512]{1,0:T(8,128)(2,1)S(1)}, bf16[560,512]{1,0:T(8,128)(2,1)S(1)}, u32[]{:S(2)}, u32[]{:S(2)}) collective-permute-start(bf16[560,512]{1,0:T(8,128)(2,1)S(1)} %get-tuple-element.23), channel_id=1, source_target_pairs={{0,16},{1,2},{2,1},{3,19},{16,0},{17,18},{18,17},{19,3},{4,20},{5,... | collective-permute-start | bytes 1720328 | tf_op jit(solution)/shard_map/ppermute | solution.py:154
  4.4 29.3 %collective-permute-start = (bf16[560,512]{1,0:T(8,128)(2,1)S(1)}, bf16[560,512]{1,0:T(8,128)(2,1)S(1)}, u32[]{:S(2)}, u32[]{:S(2)}) collective-permute-start(bf16[560,512]{1,0:T(8,128)(2,1)S(1)} %get-tuple-element.24), channel_id=1, source_target_pairs={{0,16},{1,2},{2,1},{3,19},{16,0},{17,18},{18,17},{19,3},{4,20},{5,... | collective-permute-start | bytes 1720328 | tf_op jit(solution)/shard_map/ppermute | solution.py:154
  6.4 35.2 %collective-permute-start.6 = (bf16[560,512]{1,0:T(8,128)(2,1)S(1)}, bf16[560,512]{1,0:T(8,128)(2,1)S(1)}, u32[]{:S(2)}, u32[]{:S(2)}) collective-permute-start(bf16[560,512]{1,0:T(8,128)(2,1)S(1)} %collective-permute-done.5.inner_ref), channel_id=1, source_target_pairs={{0,1},{1,0},{2,3},{3,2},{4,5},{5,4},{6,7},{7,6},{8,9},{9,8},{10,11... | collective-permute-start | bytes 1720328 | tf_op jit(solution)/shard_map/ppermute | solution.py:142
  29.4 12.2 %collective-permute-start.4 = (bf16[560,512]{1,0:T(8,128)(2,1)S(1)}, bf16[560,512]{1,0:T(8,128)(2,1)S(1)}, u32[]{:S(2)}, u32[]{:S(2)}) collective-permute-start(bf16[560,512]{1,0:T(8,128)(2,1)S(1)} %get-tuple-element.25), channel_id=1, source_target_pairs={{0,16},{1,2},{2,1},{3,19},{16,0},{17,18},{18,17},{19,3},{4,20},{5,... | collective-permute-start | bytes 1720328 | tf_op jit(solution)/shard_map/ppermute | solution.py:154
  29.5 1.7 %copy-start.1 = (bf16[2240,560]{0,1:T(8,128)(2,1)S(1)}, bf16[2240,560]{0,1:T(8,128)(2,1)}, u32[]{:S(2)}) copy-start(bf16[2240,560]{0,1:T(8,128)(2,1)} %param.8) | copy-start | bytes 7526404
  31.2 1.7 %copy-start.3 = (bf16[2240,560]{0,1:T(8,128)(2,1)S(1)}, bf16[2240,560]{0,1:T(8,128)(2,1)}, u32[]{:S(2)}) copy-start(bf16[2240,560]{0,1:T(8,128)(2,1)} %param.6) | copy-start | bytes 7526404
  33.0 14.7 %copy-start.2 = (bf16[2240,560]{0,1:T(8,128)(2,1)S(1)}, bf16[2240,560]{0,1:T(8,128)(2,1)}, u32[]{:S(2)}) copy-start(bf16[2240,560]{0,1:T(8,128)(2,1)} %param.8) | copy-start | bytes 7526404
  33.0 14.7 %copy-start.4 = (bf16[2,512,560]{1,2,0:T(8,128)(2,1)S(1)}, bf16[2,512,560]{1,2,0:T(8,128)(2,1)}, u32[]{:S(2)}) copy-start(bf16[2,512,560]{1,2,0:T(8,128)(2,1)} %param.5) | copy-start | bytes 3440644
  33.7 20.2 %collective-permute-start.3 = (bf16[560,512]{1,0:T(8,128)(2,1)S(1)}, bf16[560,512]{1,0:T(8,128)(2,1)S(1)}, u32[]{:S(2)}, u32[]{:S(2)}) collective-permute-start(bf16[560,512]{1,0:T(8,128)(2,1)S(1)} %collective-permute-done.inner_ref), channel_id=1, source_target_pairs={{0,1},{1,0},{2,3},{3,2},{4,5},{5,4},{6,7},{7,6},{8,9},{9,8},{10,11... | collective-permute-start | bytes 1720328 | tf_op jit(solution)/shard_map/ppermute | solution.py:142
  37.4 16.5 %collective-permute-start.2 = (bf16[560,512]{1,0:T(8,128)(2,1)S(1)}, bf16[560,512]{1,0:T(8,128)(2,1)S(1)}, u32[]{:S(2)}, u32[]{:S(2)}) collective-permute-start(bf16[560,512]{1,0:T(8,128)(2,1)S(1)} %get-tuple-element.26), channel_id=1, source_target_pairs={{0,16},{1,2},{2,1},{3,19},{16,0},{17,18},{18,17},{19,3},{4,20},{5,... | collective-permute-start | bytes 1720328 | tf_op jit(solution)/shard_map/ppermute | solution.py:154
  41.7 20.3 %collective-permute-start.9 = (bf16[560,256]{1,0:T(8,128)(2,1)S(1)}, bf16[560,256]{1,0:T(8,128)(2,1)S(1)}, u32[]{:S(2)}, u32[]{:S(2)}) collective-permute-start(bf16[560,256]{1,0:T(8,128)(2,1)S(1)} %get-tuple-element.28), channel_id=1, source_target_pairs={{0,1},{1,0},{2,3},{3,2},{4,5},{5,4},{6,7},{7,6},{8,9},{9,8},{10,11... | collective-permute-start | bytes 860168 | tf_op jit(solution)/shard_map/ppermute | solution.py:142
  47.6 18.6 %collective-permute-start.10 = (bf16[560,256]{1,0:T(8,128)(2,1)S(1)}, bf16[560,256]{1,0:T(8,128)(2,1)S(1)}, u32[]{:S(2)}, u32[]{:S(2)}) collective-permute-start(bf16[560,256]{1,0:T(8,128)(2,1)S(1)} %get-tuple-element.27), channel_id=1, source_target_pairs={{0,1},{1,0},{2,3},{3,2},{4,5},{5,4},{6,7},{7,6},{8,9},{9,8},{10,11... | collective-permute-start | bytes 860168 | tf_op jit(solution)/shard_map/ppermute | solution.py:142
  54.0 19.3 %collective-permute-start.7 = (bf16[560,256]{1,0:T(8,128)(2,1)S(1)}, bf16[560,256]{1,0:T(8,128)(2,1)S(1)}, u32[]{:S(2)}, u32[]{:S(2)}) collective-permute-start(bf16[560,256]{1,0:T(8,128)(2,1)S(1)} %get-tuple-element.30), channel_id=1, source_target_pairs={{0,1},{1,0},{2,3},{3,2},{4,5},{5,4},{6,7},{7,6},{8,9},{9,8},{10,11... | collective-permute-start | bytes 860168 | tf_op jit(solution)/shard_map/ppermute | solution.py:142
  67.0 7.5 %collective-permute-start.11 = (bf16[560,112]{1,0:T(8,128)(2,1)S(1)}, bf16[560,112]{1,0:T(8,128)(2,1)S(1)}, u32[]{:S(2)}, u32[]{:S(2)}) collective-permute-start(bf16[560,112]{1,0:T(8,128)(2,1)S(1)} %convert_element_type.15), channel_id=1, source_target_pairs={{0,12},{4,8},{8,4},{12,0},{1,13},{5,9},{9,5},{13,1},{2,14},{6,10},... | collective-permute-start | bytes 376328 | tf_op jit(solution)/shard_map/ppermute | solution.py:165
  70.0 5.6 %collective-permute-start.12 = (bf16[560,112]{1,0:T(8,128)(2,1)S(1)}, bf16[560,112]{1,0:T(8,128)(2,1)S(1)}, u32[]{:S(2)}, u32[]{:S(2)}) collective-permute-start(bf16[560,112]{1,0:T(8,128)(2,1)S(1)} %convert_element_type.15), channel_id=1, source_target_pairs={{0,8},{4,12},{8,0},{12,4},{1,9},{5,13},{9,1},{13,5},{2,10},{6,14},... | collective-permute-start | bytes 376328 | tf_op jit(solution)/shard_map/ppermute | solution.py:165
  70.5 5.1 %collective-permute-start.13 = (bf16[560,112]{1,0:T(8,128)(2,1)S(1)}, bf16[560,112]{1,0:T(8,128)(2,1)S(1)}, u32[]{:S(2)}, u32[]{:S(2)}) collective-permute-start(bf16[560,112]{1,0:T(8,128)(2,1)S(1)} %convert_element_type.15), channel_id=1, source_target_pairs={{0,4},{4,0},{8,12},{12,8},{1,5},{5,1},{9,13},{13,9},{2,6},{6,2},{1... | collective-permute-start | bytes 376328 | tf_op jit(solution)/shard_map/ppermute | solution.py:165
  70.6 7.0 %collective-permute-start.8 = (bf16[560,256]{1,0:T(8,128)(2,1)S(1)}, bf16[560,256]{1,0:T(8,128)(2,1)S(1)}, u32[]{:S(2)}, u32[]{:S(2)}) collective-permute-start(bf16[560,256]{1,0:T(8,128)(2,1)S(1)} %get-tuple-element.29), channel_id=1, source_target_pairs={{0,1},{1,0},{2,3},{3,2},{4,5},{5,4},{6,7},{7,6},{8,9},{9,8},{10,11... | collective-permute-start | bytes 860168 | tf_op jit(solution)/shard_map/ppermute | solution.py:142
  75.7 6.3 %copy-start.5 = (f32[560]{0:T(1024)S(1)}, f32[560]{0:T(1024)}, u32[]{:S(2)}) copy-start(f32[560]{0:T(1024)} %param.9) | copy-start | bytes 6724
  75.7 7.1 %collective-permute-start.14 = (f32[560,112]{1,0:T(8,128)S(1)}, f32[560,112]{1,0:T(8,128)S(1)}, u32[]{:S(2)}, u32[]{:S(2)}) collective-permute-start(f32[560,112]{1,0:T(8,128)S(1)} %convert_add_fusion.rest_1_), channel_id=1, source_target_pairs={{0,16},{1,17},{2,18},{3,19},{4,20},{5,21},{6,22},{7,23},{8,24},{9,... | collective-permute-start | bytes 752648 | tf_op jit(solution)/shard_map/ppermute | solution.py:171
  78.4 6.4 %collective-permute-start.15 = (bf16[560,112]{1,0:T(8,128)(2,1)S(1)}, bf16[560,112]{1,0:T(8,128)(2,1)S(1)}, u32[]{:S(2)}, u32[]{:S(2)}) collective-permute-start(bf16[560,112]{1,0:T(8,128)(2,1)S(1)} %convert_element_type.19), channel_id=1, source_target_pairs={{0,12},{4,8},{8,4},{12,0},{1,13},{5,9},{9,5},{13,1},{2,14},{6,10},... | collective-permute-start | bytes 376328 | tf_op jit(solution)/shard_map/ppermute | solution.py:165
  81.1 5.3 %collective-permute-start.16 = (bf16[560,112]{1,0:T(8,128)(2,1)S(1)}, bf16[560,112]{1,0:T(8,128)(2,1)S(1)}, u32[]{:S(2)}, u32[]{:S(2)}) collective-permute-start(bf16[560,112]{1,0:T(8,128)(2,1)S(1)} %convert_element_type.19), channel_id=1, source_target_pairs={{0,8},{4,12},{8,0},{12,4},{1,9},{5,13},{9,1},{13,5},{2,10},{6,14},... | collective-permute-start | bytes 376328 | tf_op jit(solution)/shard_map/ppermute | solution.py:165
  81.6 5.1 %collective-permute-start.17 = (bf16[560,112]{1,0:T(8,128)(2,1)S(1)}, bf16[560,112]{1,0:T(8,128)(2,1)S(1)}, u32[]{:S(2)}, u32[]{:S(2)}) collective-permute-start(bf16[560,112]{1,0:T(8,128)(2,1)S(1)} %convert_element_type.19), channel_id=1, source_target_pairs={{0,4},{4,0},{8,12},{12,8},{1,5},{5,1},{9,13},{13,9},{2,6},{6,2},{1... | collective-permute-start | bytes 376328 | tf_op jit(solution)/shard_map/ppermute | solution.py:165

commit v24 on v23

--- a/solution.py
+++ b/solution.py
@@ -158,7 +158,7 @@
     count = lax.axis_size(axis)
     sent = value.astype(jnp.bfloat16)
     got = []
-    for step in range(count - 1, 0, -1):
+    for step in (count - 1, *range(1, count - 1)):
         pairs = [(i, (i + step) % count) for i in range(count)]
         if count & (count - 1) == 0:
             pairs = [(i, i ^ step) for i in range(count)]

time: 88.1 us -> 88.1 us (level)
  no operation moved by 1% of the time
where the time goes in v24:
time: 88.1 us; the launch traced here: 87.9 us
  starting transfers between devices  42.1 us (48%)
  waiting for transfers between devices  23.7 us (27%)
  Pallas kernels  16.7 us (19%)
  local copies, waits for them, and re-layouts  5.05 us (6%)
    ppermute x7, starting transfers between devices, partner_swap(): lax.ppermute(value, axis, [(i, i ^ 1) for i in range(lax.axis_size(axis))])  32.9 us
    ppermute x7, waiting for transfers between devices, partner_swap(): lax.ppermute(value, axis, [(i, i ^ 1) for i in range(lax.axis_size(axis))])  17.8 us
    pallas_call x2, Pallas kernels, local(): call(functools.partial(partial_kernel, stream), jax.ShapeDtypeStruct((3,...  9.47 us
    ppermute x6, starting transfers between devices, from_others(): got.append(lax.ppermute(sent, axis, pairs))  7.19 us
    ppermute x6, waiting for transfers between devices, from_others(): got.append(lax.ppermute(sent, axis, pairs))  4.44 us
    unnamed x12, local copies, waits for them, and re-layouts  3.47 us
    pallas_call x4, Pallas kernels, local(): call(functools.partial(state_kernel, pieces[stream][piece], len(before)),...  2.98 us
    pallas_call x2, Pallas kernels, local(): call(functools.partial(read_kernel, stream, len(parts) + 1), out_type, AN...  2.25 us
  transfers between devices with their start and end apart: 18, of which 11 were waited for; matrix products, arithmetic and copies ran while one was open for 2% of the time, Pallas kernels for 18%

profile of v24, /device:TPU:0, one launch (start us, length us, event | category | flops | bytes accessed | tf_op | source)
XLA Modules:
  0.0 87.9 jit_solution(13006891582323058267)
XLA Ops:
  0.0 3.0 %collective-permute-start.1 = (bf16[2,560,512]{2,1,0:T(8,128)(2,1)}, bf16[2,560,512]{2,1,0:T(8,128)(2,1)S(1)}, u32[]{:S(2)}, u32[]{:S(2)}) collective-permute-start(bf16[2,560,512]{2,1,0:T(8,128)(2,1)} %bitcast.22), channel_id=1, source_target_pairs={{0,1},{1,0},{2,3},{3,2},{4,5},{5,4},{6,7},{7,6},{8,9},{9,8},{10,11... | collective-permute-start | bytes 3440648 | tf_op jit(solution)/shard_map/ppermute | solution.py:142
  3.0 1.3 %slice_bitcast_fusion = (bf16[560,512]{1,0:T(8,128)(2,1)S(1)}, bf16[560,512]{1,0:T(8,128)(2,1)S(1)}) fusion(bf16[2,560,512]{2,1,0:T(8,128)(2,1)} %bitcast.23), kind=kLoop, calls=%fused_computation | loop fusion | bytes 2293760 | tf_op jit(solution)/shard_map/squeeze | solution.py:196
  4.9 1.5 %collective-permute-done.5.inner_ref = bf16[560,512]{1,0:T(8,128)(2,1)S(1)} collective-permute-done((bf16[560,512]{1,0:T(8,128)(2,1)S(1)}, bf16[560,512]{1,0:T(8,128)(2,1)S(1)}, u32[]{:S(2)}, u32[]{:S(2)}) %collective-permute-start.5) | collective-permute-done | bytes 573472 | tf_op jit(solution)/shard_map/ppermute | solution.py:154
  6.4 15.0 %collective-permute-start.6 = (bf16[560,512]{1,0:T(8,128)(2,1)S(1)}, bf16[560,512]{1,0:T(8,128)(2,1)S(1)}, u32[]{:S(2)}, u32[]{:S(2)}) collective-permute-start(bf16[560,512]{1,0:T(8,128)(2,1)S(1)} %collective-permute-done.5.inner_ref), channel_id=1, source_target_pairs={{0,1},{1,0},{2,3},{3,2},{4,5},{5,4},{6,7},{7,6},{8,9},{9,8},{10,11... | collective-permute-start | bytes 1720328 | tf_op jit(solution)/shard_map/ppermute | solution.py:142
  21.4 7.9 %collective-permute-done.1.near = bf16[2,560,512]{2,1,0:T(8,128)(2,1)S(1)} collective-permute-done((bf16[2,560,512]{2,1,0:T(8,128)(2,1)}, bf16[2,560,512]{2,1,0:T(8,128)(2,1)S(1)}, u32[]{:S(2)}, u32[]{:S(2)}) %collective-permute-start.1) | collective-permute-done | bytes 1146912 | tf_op jit(solution)/shard_map/ppermute | solution.py:142
  29.5 1.7 %copy-done.1 = bf16[2240,560]{0,1:T(8,128)(2,1)S(1)} copy-done((bf16[2240,560]{0,1:T(8,128)(2,1)S(1)}, bf16[2240,560]{0,1:T(8,128)(2,1)}, u32[]{:S(2)}) %copy-start.1) | copy-done | bytes 2508824
  31.2 1.7 %copy-done.3 = bf16[2240,560]{0,1:T(8,128)(2,1)S(1)} copy-done((bf16[2240,560]{0,1:T(8,128)(2,1)S(1)}, bf16[2240,560]{0,1:T(8,128)(2,1)}, u32[]{:S(2)}) %copy-start.3) | copy-done | bytes 2508824
  33.0 0.7 shard_map.55.tie.cut.rest_2_
  33.7 3.7 %collective-permute-start.3 = (bf16[560,512]{1,0:T(8,128)(2,1)S(1)}, bf16[560,512]{1,0:T(8,128)(2,1)S(1)}, u32[]{:S(2)}, u32[]{:S(2)}) collective-permute-start(bf16[560,512]{1,0:T(8,128)(2,1)S(1)} %collective-permute-done.inner_ref), channel_id=1, source_target_pairs={{0,1},{1,0},{2,3},{3,2},{4,5},{5,4},{6,7},{7,6},{8,9},{9,8},{10,11... | collective-permute-start | bytes 1720328 | tf_op jit(solution)/shard_map/ppermute | solution.py:142
  37.4 4.2 %collective-permute-done.6.b2o = bf16[560,512]{1,0:T(8,128)(2,1)S(1)} collective-permute-done((bf16[560,512]{1,0:T(8,128)(2,1)S(1)}, bf16[560,512]{1,0:T(8,128)(2,1)S(1)}, u32[]{:S(2)}, u32[]{:S(2)}) %collective-permute-start.6) | collective-permute-done | bytes 573472 | tf_op jit(solution)/shard_map/ppermute | solution.py:142
  41.7 5.9 %collective-permute-start.9 = (bf16[560,256]{1,0:T(8,128)(2,1)S(1)}, bf16[560,256]{1,0:T(8,128)(2,1)S(1)}, u32[]{:S(2)}, u32[]{:S(2)}) collective-permute-start(bf16[560,256]{1,0:T(8,128)(2,1)S(1)} %get-tuple-element.28), channel_id=1, source_target_pairs={{0,1},{1,0},{2,3},{3,2},{4,5},{5,4},{6,7},{7,6},{8,9},{9,8},{10,11... | collective-permute-start | bytes 860168 | tf_op jit(solution)/shard_map/ppermute | solution.py:142
  47.6 4.7 %shard_map.56.sums.rest_3_ = f32[3,560,512]{2,1,0:T(8,128)S(1)} custom-call(bf16[2,560,512]{2,1,0:T(8,128)(2,1)S(1)} %bitcast.24, bf16[2,560,512]{2,1,0:T(8,128)(2,1)S(1)} %collective-permute-done.1.near, bf16[560,512]{1,0:T(8,128)(2,1)S(1)} %collective-permute-done.4.b2i, bf16[560,512]{1,0:T(8,128)(2,1)S(1)} %collective-permute-done.6.b2o, ...), custom_call_target="tpu_custom_call" | custom-call | flops 60211200 | bytes 1024 | tf_op jit(solution)/shard_map/pallas_call | solution.py:214
  52.4 1.5 %collective-permute-done.3.b2o = bf16[560,512]{1,0:T(8,128)(2,1)S(1)} collective-permute-done((bf16[560,512]{1,0:T(8,128)(2,1)S(1)}, bf16[560,512]{1,0:T(8,128)(2,1)S(1)}, u32[]{:S(2)}, u32[]{:S(2)}) %collective-permute-start.3) | collective-permute-done | bytes 573472 | tf_op jit(solution)/shard_map/ppermute | solution.py:142
  54.0 3.3 %collective-permute-start.7 = (bf16[560,256]{1,0:T(8,128)(2,1)S(1)}, bf16[560,256]{1,0:T(8,128)(2,1)S(1)}, u32[]{:S(2)}, u32[]{:S(2)}) collective-permute-start(bf16[560,256]{1,0:T(8,128)(2,1)S(1)} %get-tuple-element.30), channel_id=1, source_target_pairs={{0,1},{1,0},{2,3},{3,2},{4,5},{5,4},{6,7},{7,6},{8,9},{9,8},{10,11... | collective-permute-start | bytes 860168 | tf_op jit(solution)/shard_map/ppermute | solution.py:142
  57.2 4.7 %shard_map.57.rest_0_.rest_1_.sums.rest_3_ = f32[3,560,512]{2,1,0:T(8,128)S(1)} custom-call(bf16[2,560,512]{2,1,0:T(8,128)(2,1)S(1)} %bitcast.25, bf16[2,560,512]{2,1,0:T(8,128)(2,1)S(1)} %collective-permute-done.1.near, bf16[560,512]{1,0:T(8,128)(2,1)S(1)} %collective-permute-done.2.b2i, bf16[560,512]{1,0:T(8,128)(2,1)S(1)} %collective-permute-done.3.b2o, ...), custom_call_target="tpu_custom_call" | custom-call | flops 60211200 | bytes 1024 | tf_op jit(solution)/shard_map/pallas_call | solution.py:214
  62.0 0.7 shard_map.58.rest_0_
  62.7 3.5 %collective-permute-done.10.end_ref.rest_1_ = bf16[560,256]{1,0:T(8,128)(2,1)S(1)} collective-permute-done((bf16[560,256]{1,0:T(8,128)(2,1)S(1)}, bf16[560,256]{1,0:T(8,128)(2,1)S(1)}, u32[]{:S(2)}, u32[]{:S(2)}) %collective-permute-start.10) | collective-permute-done | bytes 286752 | tf_op jit(solution)/shard_map/ppermute | solution.py:142
  66.2 0.7 shard_map.59.rest_4_
  67.0 3.0 %collective-permute-start.11 = (bf16[560,112]{1,0:T(8,128)(2,1)S(1)}, bf16[560,112]{1,0:T(8,128)(2,1)S(1)}, u32[]{:S(2)}, u32[]{:S(2)}) collective-permute-start(bf16[560,112]{1,0:T(8,128)(2,1)S(1)} %convert_element_type.15), channel_id=1, source_target_pairs={{0,12},{4,8},{8,4},{12,0},{1,13},{5,9},{9,5},{13,1},{2,14},{6,10},... | collective-permute-start | bytes 376328 | tf_op jit(solution)/shard_map/ppermute | solution.py:165
  70.6 2.0 %collective-permute-start.8 = (bf16[560,256]{1,0:T(8,128)(2,1)S(1)}, bf16[560,256]{1,0:T(8,128)(2,1)S(1)}, u32[]{:S(2)}, u32[]{:S(2)}) collective-permute-start(bf16[560,256]{1,0:T(8,128)(2,1)S(1)} %get-tuple-element.29), channel_id=1, source_target_pairs={{0,1},{1,0},{2,3},{3,2},{4,5},{5,4},{6,7},{7,6},{8,9},{9,8},{10,11... | collective-permute-start | bytes 860168 | tf_op jit(solution)/shard_map/ppermute | solution.py:142
  72.6 0.6 shard_map.60.rest_0_.rest_2_.query
  73.2 0.7 shard_map.61.rest_0_
  74.0 1.1 %collective-permute-done.12 = bf16[560,112]{1,0:T(8,128)(2,1)S(1)} collective-permute-done((bf16[560,112]{1,0:T(8,128)(2,1)S(1)}, bf16[560,112]{1,0:T(8,128)(2,1)S(1)}, u32[]{:S(2)}, u32[]{:S(2)}) %collective-permute-start.12) | collective-permute-done | bytes 125472 | tf_op jit(solution)/shard_map/ppermute | solution.py:165
  75.7 1.3 %collective-permute-start.14 = (f32[560,112]{1,0:T(8,128)S(1)}, f32[560,112]{1,0:T(8,128)S(1)}, u32[]{:S(2)}, u32[]{:S(2)}) collective-permute-start(f32[560,112]{1,0:T(8,128)S(1)} %convert_add_fusion.rest_1_), channel_id=1, source_target_pairs={{0,16},{1,17},{2,18},{3,19},{4,20},{5,21},{6,22},{7,23},{8,24},{9,... | collective-permute-start | bytes 752648 | tf_op jit(solution)/shard_map/ppermute | solution.py:171
  77.0 0.7 collective-permute-done.8.end_ref.rest_1_
  77.7 0.7 shard_map.62.rest_4_.rest_1_
  78.4 2.7 %collective-permute-start.15 = (bf16[560,112]{1,0:T(8,128)(2,1)S(1)}, bf16[560,112]{1,0:T(8,128)(2,1)S(1)}, u32[]{:S(2)}, u32[]{:S(2)}) collective-permute-start(bf16[560,112]{1,0:T(8,128)(2,1)S(1)} %convert_element_type.19), channel_id=1, source_target_pairs={{0,12},{4,8},{8,4},{12,0},{1,13},{5,9},{9,5},{13,1},{2,14},{6,10},... | collective-permute-start | bytes 376328 | tf_op jit(solution)/shard_map/ppermute | solution.py:165
  82.1 0.6 shard_map.63.query
  82.8 1.1 %shard_map.64.rest_5_ = bf16[2,560,512]{2,1,0:T(8,128)(2,1)} custom-call(bf16[560,512]{1,0:T(8,128)(2,1)S(1)} %shard_map.60.rest_0_.rest_2_.query, f32[560,1]{1,0:T(8,128)S(1)} %reshape.4.gain, f32[560,112]{1,0:T(8,128)S(1)} %collective-permute-done.14.rest_0_, f32[560,112]{1,0:T(8,128)S(1)} %convert_add_fusion.rest_1_), custom_call_target="tpu_custom_call" | custom-call | flops 1003520 | bytes 1024 | tf_op jit(solution)/shard_map/pallas_call | solution.py:242
  83.9 0.6 collective-permute-done.15.rest_2_
  84.5 1.8 %collective-permute-done.16.rest_3_ = bf16[560,112]{1,0:T(8,128)(2,1)S(1)} collective-permute-done((bf16[560,112]{1,0:T(8,128)(2,1)S(1)}, bf16[560,112]{1,0:T(8,128)(2,1)S(1)}, u32[]{:S(2)}, u32[]{:S(2)}) %collective-permute-start.16) | collective-permute-done | bytes 125472 | tf_op jit(solution)/shard_map/ppermute | solution.py:165
  86.7 1.1 %shard_map.65 = bf16[2,560,512]{2,1,0:T(8,128)(2,1)} custom-call(bf16[560,512]{1,0:T(8,128)(2,1)S(1)} %shard_map.63.query, f32[560,1]{1,0:T(8,128)S(1)} %reshape.4.gain, f32[560,112]{1,0:T(8,128)S(1)} %collective-permute-done.14.rest_0_, f32[560,112]{1,0:T(8,128)S(1)} %shard_map.62.rest_4_.rest_1_, ...), custom_call_target="tpu_custom_call", output_to_operand_aliasing={{}: (7, {})} | custom-call | flops 1003520 | bytes 1024 | tf_op jit(solution)/shard_map/pallas_call | solution.py:242
  (35 shorter events, 3.6 us)
Async XLA Ops:
  0.0 29.5 %copy-start = (bf16[2240,560]{0,1:T(8,128)(2,1)S(1)}, bf16[2240,560]{0,1:T(8,128)(2,1)}, u32[]{:S(2)}) copy-start(bf16[2240,560]{0,1:T(8,128)(2,1)} %param.7) | copy-start | bytes 7526404
  0.0 29.3 %collective-permute-start.1 = (bf16[2,560,512]{2,1,0:T(8,128)(2,1)}, bf16[2,560,512]{2,1,0:T(8,128)(2,1)S(1)}, u32[]{:S(2)}, u32[]{:S(2)}) collective-permute-start(bf16[2,560,512]{2,1,0:T(8,128)(2,1)} %bitcast.22), channel_id=1, source_target_pairs={{0,1},{1,0},{2,3},{3,2},{4,5},{5,4},{6,7},{7,6},{8,9},{9,8},{10,11... | collective-permute-start | bytes 3440648 | tf_op jit(solution)/shard_map/ppermute | solution.py:142
  4.3 2.0 %collective-permute-start.5 = (bf16[560,512]{1,0:T(8,128)(2,1)S(1)}, bf16[560,512]{1,0:T(8,128)(2,1)S(1)}, u32[]{:S(2)}, u32[]{:S(2)}) collective-permute-start(bf16[560,512]{1,0:T(8,128)(2,1)S(1)} %get-tuple-element.23), channel_id=1, source_target_pairs={{0,16},{1,2},{2,1},{3,19},{16,0},{17,18},{18,17},{19,3},{4,20},{5,... | collective-permute-start | bytes 1720328 | tf_op jit(solution)/shard_map/ppermute | solution.py:154
  4.4 29.3 %collective-permute-start = (bf16[560,512]{1,0:T(8,128)(2,1)S(1)}, bf16[560,512]{1,0:T(8,128)(2,1)S(1)}, u32[]{:S(2)}, u32[]{:S(2)}) collective-permute-start(bf16[560,512]{1,0:T(8,128)(2,1)S(1)} %get-tuple-element.24), channel_id=1, source_target_pairs={{0,16},{1,2},{2,1},{3,19},{16,0},{17,18},{18,17},{19,3},{4,20},{5,... | collective-permute-start | bytes 1720328 | tf_op jit(solution)/shard_map/ppermute | solution.py:154
  6.4 35.2 %collective-permute-start.6 = (bf16[560,512]{1,0:T(8,128)(2,1)S(1)}, bf16[560,512]{1,0:T(8,128)(2,1)S(1)}, u32[]{:S(2)}, u32[]{:S(2)}) collective-permute-start(bf16[560,512]{1,0:T(8,128)(2,1)S(1)} %collective-permute-done.5.inner_ref), channel_id=1, source_target_pairs={{0,1},{1,0},{2,3},{3,2},{4,5},{5,4},{6,7},{7,6},{8,9},{9,8},{10,11... | collective-permute-start | bytes 1720328 | tf_op jit(solution)/shard_map/ppermute | solution.py:142
  29.4 12.2 %collective-permute-start.4 = (bf16[560,512]{1,0:T(8,128)(2,1)S(1)}, bf16[560,512]{1,0:T(8,128)(2,1)S(1)}, u32[]{:S(2)}, u32[]{:S(2)}) collective-permute-start(bf16[560,512]{1,0:T(8,128)(2,1)S(1)} %get-tuple-element.25), channel_id=1, source_target_pairs={{0,16},{1,2},{2,1},{3,19},{16,0},{17,18},{18,17},{19,3},{4,20},{5,... | collective-permute-start | bytes 1720328 | tf_op jit(solution)/shard_map/ppermute | solution.py:154
  29.5 1.7 %copy-start.1 = (bf16[2240,560]{0,1:T(8,128)(2,1)S(1)}, bf16[2240,560]{0,1:T(8,128)(2,1)}, u32[]{:S(2)}) copy-start(bf16[2240,560]{0,1:T(8,128)(2,1)} %param.8) | copy-start | bytes 7526404
  31.2 1.7 %copy-start.3 = (bf16[2240,560]{0,1:T(8,128)(2,1)S(1)}, bf16[2240,560]{0,1:T(8,128)(2,1)}, u32[]{:S(2)}) copy-start(bf16[2240,560]{0,1:T(8,128)(2,1)} %param.6) | copy-start | bytes 7526404
  33.0 14.7 %copy-start.2 = (bf16[2240,560]{0,1:T(8,128)(2,1)S(1)}, bf16[2240,560]{0,1:T(8,128)(2,1)}, u32[]{:S(2)}) copy-start(bf16[2240,560]{0,1:T(8,128)(2,1)} %param.8) | copy-start | bytes 7526404
  33.0 14.7 %copy-start.4 = (bf16[2,512,560]{1,2,0:T(8,128)(2,1)S(1)}, bf16[2,512,560]{1,2,0:T(8,128)(2,1)}, u32[]{:S(2)}) copy-start(bf16[2,512,560]{1,2,0:T(8,128)(2,1)} %param.5) | copy-start | bytes 3440644
  33.7 20.2 %collective-permute-start.3 = (bf16[560,512]{1,0:T(8,128)(2,1)S(1)}, bf16[560,512]{1,0:T(8,128)(2,1)S(1)}, u32[]{:S(2)}, u32[]{:S(2)}) collective-permute-start(bf16[560,512]{1,0:T(8,128)(2,1)S(1)} %collective-permute-done.inner_ref), channel_id=1, source_target_pairs={{0,1},{1,0},{2,3},{3,2},{4,5},{5,4},{6,7},{7,6},{8,9},{9,8},{10,11... | collective-permute-start | bytes 1720328 | tf_op jit(solution)/shard_map/ppermute | solution.py:142
  37.4 16.5 %collective-permute-start.2 = (bf16[560,512]{1,0:T(8,128)(2,1)S(1)}, bf16[560,512]{1,0:T(8,128)(2,1)S(1)}, u32[]{:S(2)}, u32[]{:S(2)}) collective-permute-start(bf16[560,512]{1,0:T(8,128)(2,1)S(1)} %get-tuple-element.26), channel_id=1, source_target_pairs={{0,16},{1,2},{2,1},{3,19},{16,0},{17,18},{18,17},{19,3},{4,20},{5,... | collective-permute-start | bytes 1720328 | tf_op jit(solution)/shard_map/ppermute | solution.py:154
  41.7 20.3 %collective-permute-start.9 = (bf16[560,256]{1,0:T(8,128)(2,1)S(1)}, bf16[560,256]{1,0:T(8,128)(2,1)S(1)}, u32[]{:S(2)}, u32[]{:S(2)}) collective-permute-start(bf16[560,256]{1,0:T(8,128)(2,1)S(1)} %get-tuple-element.28), channel_id=1, source_target_pairs={{0,1},{1,0},{2,3},{3,2},{4,5},{5,4},{6,7},{7,6},{8,9},{9,8},{10,11... | collective-permute-start | bytes 860168 | tf_op jit(solution)/shard_map/ppermute | solution.py:142
  47.6 18.6 %collective-permute-start.10 = (bf16[560,256]{1,0:T(8,128)(2,1)S(1)}, bf16[560,256]{1,0:T(8,128)(2,1)S(1)}, u32[]{:S(2)}, u32[]{:S(2)}) collective-permute-start(bf16[560,256]{1,0:T(8,128)(2,1)S(1)} %get-tuple-element.27), channel_id=1, source_target_pairs={{0,1},{1,0},{2,3},{3,2},{4,5},{5,4},{6,7},{7,6},{8,9},{9,8},{10,11... | collective-permute-start | bytes 860168 | tf_op jit(solution)/shard_map/ppermute | solution.py:142
  54.0 19.3 %collective-permute-start.7 = (bf16[560,256]{1,0:T(8,128)(2,1)S(1)}, bf16[560,256]{1,0:T(8,128)(2,1)S(1)}, u32[]{:S(2)}, u32[]{:S(2)}) collective-permute-start(bf16[560,256]{1,0:T(8,128)(2,1)S(1)} %get-tuple-element.30), channel_id=1, source_target_pairs={{0,1},{1,0},{2,3},{3,2},{4,5},{5,4},{6,7},{7,6},{8,9},{9,8},{10,11... | collective-permute-start | bytes 860168 | tf_op jit(solution)/shard_map/ppermute | solution.py:142
  67.0 7.0 %collective-permute-start.11 = (bf16[560,112]{1,0:T(8,128)(2,1)S(1)}, bf16[560,112]{1,0:T(8,128)(2,1)S(1)}, u32[]{:S(2)}, u32[]{:S(2)}) collective-permute-start(bf16[560,112]{1,0:T(8,128)(2,1)S(1)} %convert_element_type.15), channel_id=1, source_target_pairs={{0,12},{4,8},{8,4},{12,0},{1,13},{5,9},{9,5},{13,1},{2,14},{6,10},... | collective-permute-start | bytes 376328 | tf_op jit(solution)/shard_map/ppermute | solution.py:165
  70.0 5.1 %collective-permute-start.12 = (bf16[560,112]{1,0:T(8,128)(2,1)S(1)}, bf16[560,112]{1,0:T(8,128)(2,1)S(1)}, u32[]{:S(2)}, u32[]{:S(2)}) collective-permute-start(bf16[560,112]{1,0:T(8,128)(2,1)S(1)} %convert_element_type.15), channel_id=1, source_target_pairs={{0,4},{4,0},{8,12},{12,8},{1,5},{5,1},{9,13},{13,9},{2,6},{6,2},{1... | collective-permute-start | bytes 376328 | tf_op jit(solution)/shard_map/ppermute | solution.py:165
  70.5 5.1 %collective-permute-start.13 = (bf16[560,112]{1,0:T(8,128)(2,1)S(1)}, bf16[560,112]{1,0:T(8,128)(2,1)S(1)}, u32[]{:S(2)}, u32[]{:S(2)}) collective-permute-start(bf16[560,112]{1,0:T(8,128)(2,1)S(1)} %convert_element_type.15), channel_id=1, source_target_pairs={{0,8},{4,12},{8,0},{12,4},{1,9},{5,13},{9,1},{13,5},{2,10},{6,14},... | collective-permute-start | bytes 376328 | tf_op jit(solution)/shard_map/ppermute | solution.py:165
  70.6 7.0 %collective-permute-start.8 = (bf16[560,256]{1,0:T(8,128)(2,1)S(1)}, bf16[560,256]{1,0:T(8,128)(2,1)S(1)}, u32[]{:S(2)}, u32[]{:S(2)}) collective-permute-start(bf16[560,256]{1,0:T(8,128)(2,1)S(1)} %get-tuple-element.29), channel_id=1, source_target_pairs={{0,1},{1,0},{2,3},{3,2},{4,5},{5,4},{6,7},{7,6},{8,9},{9,8},{10,11... | collective-permute-start | bytes 860168 | tf_op jit(solution)/shard_map/ppermute | solution.py:142
  75.7 6.3 %copy-start.5 = (f32[560]{0:T(1024)S(1)}, f32[560]{0:T(1024)}, u32[]{:S(2)}) copy-start(f32[560]{0:T(1024)} %param.9) | copy-start | bytes 6724
  75.7 7.1 %collective-permute-start.14 = (f32[560,112]{1,0:T(8,128)S(1)}, f32[560,112]{1,0:T(8,128)S(1)}, u32[]{:S(2)}, u32[]{:S(2)}) collective-permute-start(f32[560,112]{1,0:T(8,128)S(1)} %convert_add_fusion.rest_1_), channel_id=1, source_target_pairs={{0,16},{1,17},{2,18},{3,19},{4,20},{5,21},{6,22},{7,23},{8,24},{9,... | collective-permute-start | bytes 752648 | tf_op jit(solution)/shard_map/ppermute | solution.py:171
  78.4 6.1 %collective-permute-start.15 = (bf16[560,112]{1,0:T(8,128)(2,1)S(1)}, bf16[560,112]{1,0:T(8,128)(2,1)S(1)}, u32[]{:S(2)}, u32[]{:S(2)}) collective-permute-start(bf16[560,112]{1,0:T(8,128)(2,1)S(1)} %convert_element_type.19), channel_id=1, source_target_pairs={{0,12},{4,8},{8,4},{12,0},{1,13},{5,9},{9,5},{13,1},{2,14},{6,10},... | collective-permute-start | bytes 376328 | tf_op jit(solution)/shard_map/ppermute | solution.py:165
  81.1 5.1 %collective-permute-start.16 = (bf16[560,112]{1,0:T(8,128)(2,1)S(1)}, bf16[560,112]{1,0:T(8,128)(2,1)S(1)}, u32[]{:S(2)}, u32[]{:S(2)}) collective-permute-start(bf16[560,112]{1,0:T(8,128)(2,1)S(1)} %convert_element_type.19), channel_id=1, source_target_pairs={{0,4},{4,0},{8,12},{12,8},{1,5},{5,1},{9,13},{13,9},{2,6},{6,2},{1... | collective-permute-start | bytes 376328 | tf_op jit(solution)/shard_map/ppermute | solution.py:165
  81.6 5.1 %collective-permute-start.17 = (bf16[560,112]{1,0:T(8,128)(2,1)S(1)}, bf16[560,112]{1,0:T(8,128)(2,1)S(1)}, u32[]{:S(2)}, u32[]{:S(2)}) collective-permute-start(bf16[560,112]{1,0:T(8,128)(2,1)S(1)} %convert_element_type.19), channel_id=1, source_target_pairs={{0,8},{4,12},{8,0},{12,4},{1,9},{5,13},{9,1},{13,5},{2,10},{6,14},... | collective-permute-start | bytes 376328 | tf_op jit(solution)/shard_map/ppermute | solution.py:165
